TPU v7x, 32 devices: a whole 2x2x4 slice. The times are simulated.
32 devices in a mesh: groups: 2 (over y), wide: 4 (over z), narrow: 2 (over x), pair: 2 (over core).
Axes of the slice: x: 2, y: 2, z: 4, core: 2. Of those that a mesh axis runs over, the one named last changes fastest.
Arguments:
- density: float32 [16384], P(('groups', 'wide', 'narrow', 'pair')), parts along dimension 0, may hold values from -4 to 4
- surface_flag: int32 [16384], P(('groups', 'wide', 'narrow', 'pair')), parts along dimension 0, may hold values 0 or 1
- stencil_base: int32 [3, 16384], P(None, ('groups', 'wide', 'narrow', 'pair')), parts along dimension 1, may hold values from 0 to 124, as said below
- sample_weights: float32 [64, 16384], P(None, ('groups', 'wide', 'narrow', 'pair')), parts along dimension 1, may hold values from 0 to 0.125
- dipole_weights: float32 [64, 16384], P(None, ('groups', 'wide', 'narrow', 'pair')), parts along dimension 1, may hold values from -0.5 to 0.5
- near_target: int32 [768], P(('groups', 'wide', 'narrow', 'pair')), parts along dimension 0, may hold values from -1 to 3, as said below
- near_source: int32 [768], P(('groups', 'wide', 'narrow', 'pair')), parts along dimension 0, may hold values from 0 to 35, as said below
- near_tiles: bfloat16 [768, 128, 128], P(('groups', 'wide', 'narrow', 'pair')), parts along dimension 0, may hold values from -0.039794922 to 0.039794922
Outputs:
- krylov: float32 [2, 16384], P(None, ('groups', 'wide', 'narrow', 'pair')), parts along dimension 1
There are 2 independent parts, one for each index of `groups`. A program takes and returns all parts, laid end to end along the dimension named above; each array names one. Nothing has to cross between parts.
Inputs may be any that keep to these rules, and one draw needn't show every extreme that they name: `stencil_base`: for the panels of the device at position w along wide and y along narrow+pair, row 0 lies from w * 32 - 2 to w * 32 + 30 and row 1 from y * 32 - 2 to y * 32 + 30, each clipped to 0 to 124; on every device both ends of both ranges are taken. `near_target`: -1 marks an empty slot; on each device the live slots come first and a live value names one of its 4 blocks; some device has all 24 slots live. The device that near_source names lies within one position of the slot's device along wide and along narrow+pair, and exists.
All inputs are finite; a program needn't handle non-finite values. No bound on the sum of `surface_flag` on one device may be relied on, other than what follows from the above.
Results may differ from a plain program's by a relative error of at most 0.00041.
Values may be sent and summed in bfloat16 or wider, within the bound.
No kernel may reach another device: no remote copies, remote signals or barrier semaphores. Data moves between devices by JAX's collectives and lax.ppermute only.
A program may use at most 128 MiB of HBM per device.

v0:
```python
import jax
import jax.numpy as jnp
from jax import lax
from jax.sharding import PartitionSpec as P

GRID = 256
REGION = 128
BLOCK = 128


KERNEL_GAIN = 4.0
SCREEN = 1.0 / 1024.0
HIGHEST = lax.Precision.HIGHEST


def with_halo(cells, sides, width):
    for axis, dim in sides:
        count = lax.axis_size(axis)
        ends = count - 1
        head = lax.slice_in_dim(cells, 0, width, axis=dim)
        tail = lax.slice_in_dim(cells, cells.shape[dim] - width, cells.shape[dim], axis=dim)
        cells = jnp.concatenate(
            [
                lax.ppermute(tail, axis, [(i, (i + 1) % count) for i in range(ends)]),
                cells,
                lax.ppermute(head, axis, [((i + 1) % count, i) for i in range(ends)]),
            ],
            axis=dim,
        )
    return cells


def symbol(wave_ids, length):
    sine_wave = jnp.sin(jnp.pi * wave_ids.astype(jnp.float32) / length)
    return 4.0 * sine_wave * sine_wave


def cas_table(row_count, col_count, length):
    row_ids = jnp.arange(row_count, dtype=jnp.int32)[:, None]
    col_ids = jnp.arange(col_count, dtype=jnp.int32)[None, :]
    angles = 2.0 * jnp.pi / length * (row_ids * col_ids % length).astype(jnp.float32)
    return jnp.cos(angles) + jnp.sin(angles)


def contract(form, left_side, right_side):
    return jnp.einsum(form, left_side, right_side, precision=HIGHEST)


def brick_rims(field_block):
    return with_halo(field_block, (("wide", 0), (("narrow", "pair"), 1)), 2)


def slab_turn(values):
    return lax.all_to_all(values, "wide", split_axis=2, concat_axis=0, tiled=True)


def pencil_turn(values):
    return lax.all_to_all(values, ("narrow", "pair"), split_axis=2, concat_axis=0, tiled=True)


def fold_rims(padded, span_x, span_y):
    folded = padded[4 : span_x + 4]
    folded = folded + jnp.pad(padded[0:2], ((0, span_x - 2), (0, 0), (0, 0)))
    folded = folded + jnp.pad(padded[span_x + 6 : span_x + 8], ((span_x - 2, 0), (0, 0), (0, 0)))
    result = folded[:, 4 : span_y + 4]
    result = result + jnp.pad(folded[:, 0:2], ((0, 0), (0, span_y - 2), (0, 0)))
    return result + jnp.pad(folded[:, span_y + 6 : span_y + 8], ((0, 0), (span_y - 2, 0), (0, 0)))


def z_lines(coeff, offsets):
    grouped = coeff.reshape(16, 4, -1)
    lines = grouped[:, 0, :, None] * (offsets == 0).astype(jnp.float32)
    for depth in range(1, 4):
        lines = lines + grouped[:, depth, :, None] * (offsets == depth).astype(jnp.float32)
    return lines


def shards(
    density,
    surface_flag,
    stencil_base,
    sample_weights,
    dipole_weights,
    near_target,
    near_source,
    near_tiles,
):
    x_count = lax.axis_size("wide")
    y_count = lax.axis_size(("narrow", "pair"))
    x_index = lax.axis_index("wide")
    y_index = lax.axis_index(("narrow", "pair"))
    span_x = REGION // x_count
    span_y = REGION // y_count
    width_y = span_y + 4
    wide_spec = GRID // x_count
    pencil_spec = GRID // y_count
    forward = cas_table(REGION, GRID, GRID)
    inverse = cas_table(GRID, REGION, GRID) / GRID
    all_waves = symbol(jnp.arange(GRID, dtype=jnp.int32), GRID)
    wide_waves = symbol(x_index * wide_spec + jnp.arange(wide_spec, dtype=jnp.int32), GRID)
    pencil_waves = symbol(y_index * pencil_spec + jnp.arange(pencil_spec, dtype=jnp.int32), GRID)
    column_ids = jnp.arange(16, dtype=jnp.int32)
    local_x = stencil_base[0] - (x_index * span_x - 2)
    local_y = stencil_base[1] - (y_index * span_y - 2)
    line_ids = (
        (local_x[None, :] + (column_ids // 4)[:, None]) * width_y
        + local_y[None, :]
        + (column_ids % 4)[:, None]
    ).reshape(-1)
    offsets = jnp.arange(REGION, dtype=jnp.int32)[None, None, :] - stencil_base[2][None, :, None]
    weight_lines = z_lines(sample_weights, offsets)
    charged = surface_flag == 1
    blocks_dev = density.shape[0] // BLOCK
    owners = (near_target[None, :] == jnp.arange(blocks_dev, dtype=jnp.int32)[:, None]).astype(
        jnp.float32
    )
    line_count = (span_x + 4) * width_y

    def convolve(charge):
        spectrum = contract("xyj,jk->yxk", charge, forward)
        spectrum = pencil_turn(spectrum)
        spectrum = contract("jxz,jk->xzk", spectrum, forward)
        spectrum = slab_turn(spectrum)
        spectrum = contract("jzy,jk->kzy", spectrum, forward)
        kernel = KERNEL_GAIN / (
            SCREEN
            + all_waves[:, None, None]
            + pencil_waves[None, :, None]
            + wide_waves[None, None, :]
        )
        returned = contract("kzy,kj->yzj", spectrum * kernel, inverse)
        returned = slab_turn(returned)
        returned = contract("kzx,kj->zxj", returned, inverse)
        returned = pencil_turn(returned)
        return contract("kxy,kj->xyj", returned, inverse)

    def near_field(vector):
        beside_all = with_halo(
            vector.astype(jnp.bfloat16).reshape(1, 1, -1), (("wide", 0), (("narrow", "pair"), 1)), 1
        )
        blocks = beside_all.reshape(9 * blocks_dev, BLOCK)
        picked = jnp.take(blocks, near_source, axis=0)
        partials = jnp.einsum("tij,tj->ti", near_tiles, picked, preferred_element_type=jnp.float32)
        return jnp.dot(owners, partials, precision=HIGHEST).reshape(-1)

    def apply_operator(vector):
        sources = jnp.where(
            charged[None, :], -sample_weights * vector[None, :], dipole_weights * vector[None, :]
        )
        source_lines = z_lines(sources, offsets).reshape(-1, REGION)
        spread = jnp.zeros((line_count, REGION), jnp.float32).at[line_ids].add(source_lines)
        charge = fold_rims(brick_rims(spread.reshape(span_x + 4, width_y, REGION)), span_x, span_y)
        potential = convolve(charge)
        near_part = near_field(vector)
        padded = brick_rims(potential).reshape(line_count, REGION)
        gathered = jnp.take(padded, line_ids, axis=0).reshape(16, -1, REGION)
        sampled = jnp.sum(jnp.sum(gathered * weight_lines, axis=2), axis=0)
        return 0.5 * jnp.where(charged, 0.0, vector) + sampled + near_part

    first_image = apply_operator(density)
    second = apply_operator(first_image)
    return jnp.stack([first_image, second])


def solution(mesh):
    in_specs = (
        P(("groups", "wide", "narrow", "pair")),
        P(("groups", "wide", "narrow", "pair")),
        P(None, ("groups", "wide", "narrow", "pair")),
        P(None, ("groups", "wide", "narrow", "pair")),
        P(None, ("groups", "wide", "narrow", "pair")),
        P(("groups", "wide", "narrow", "pair")),
        P(("groups", "wide", "narrow", "pair")),
        P(("groups", "wide", "narrow", "pair"), None, None),
    )
    out_specs = P(None, ("groups", "wide", "narrow", "pair"))
    return jax.shard_map(shards, mesh=mesh, in_specs=in_specs, out_specs=out_specs, check_vma=False)
```

profile of v0, /device:TPU:0, one launch (start us, length us, event | category | flops | bytes accessed | tf_op | source)
XLA Modules:
  0.0 767.9 jit_solution(15497132125789858653)
XLA Ops:
  4.1 5.8 fusion.2
  9.9 44.5 %scatter_custom_fusion = f32[1296,128]{1,0:T(8,128)S(1)} fusion(s32[8192]{0:T(1024)S(1)} %bitcast.278, f32[8192,128]{1,0:T(8,128)} %fusion.2, f32[]{:T(128)} %constant.114.clone.1), kind=kCustom, calls=%fused_computation.67 | custom fusion | flops 1048576 | bytes 664064 | tf_op jit(solution)/shard_map/scatter-add | solution.py:151
  54.4 4.9 collective-permute-start
  61.1 4.2 collective-permute-done.1
  73.2 4.4 copy.77
  77.6 3.9 reshape.453
  81.6 18.5 %all_to_all.144 = f32[4,1,65536]{2,1,0:T(1,128)S(1)} all-to-all(f32[4,1,65536]{2,1,0:T(1,128)S(1)} %reshape.453), channel_id=1, replica_groups=mesh['groups'=2,'wide'=4,'narrow'=2,'pair'=2] {'narrow','pair'}, dimensions={0} | all-to-all | bytes 2097152 | tf_op jit(solution)/shard_map/all_to_all | solution.py:58
  100.7 3.7 reduce.6
  111.3 5.3 fusion.64
  116.6 5.5 copy.80
  122.2 5.5 reshape.455
  127.7 5.0 all-to-all-start.1
  132.9 47.9 %all-to-all-done.1 = f32[4,1,131072]{2,1,0:T(1,128)} async-done(((f32[4,1,131072]{2,1,0:T(1,128)}), f32[4,1,131072]{2,1,0:T(1,128)}, u32[]{:S(2)}, u32[]{:S(2)}) %all-to-all-start.1) | async-done | bytes 2097184 | tf_op jit(solution)/shard_map/all_to_all | solution.py:54
  180.8 7.7 %reduce.7 = f32[4,131072]{1,0:T(4,128)S(1)} reduce(f32[4,1,131072]{2,1,0:T(1,128)} %all-to-all-done.1, f32[]{:T(128)} %broadcast.474), dimensions={1}, to_apply=%all_to_all.108.reduce_sub_computation | reduce | bytes 4194308 | tf_op jit(solution)/shard_map/all_to_all | solution.py:54
  188.5 4.0 reshape.456
  192.5 5.9 copy.81
  198.3 4.0 copy.82
  202.3 4.0 fusion.73
  207.3 4.0 fusion.76
  211.3 4.5 copy.83
  215.9 5.6 reshape.457
  221.4 4.4 all-to-all-start.2
  225.9 4.4 collective-permute-start.8
  233.3 40.4 %all-to-all-done.2 = f32[4,1,131072]{2,1,0:T(1,128)} async-done(((f32[4,1,131072]{2,1,0:T(1,128)}), f32[4,1,131072]{2,1,0:T(1,128)}, u32[]{:S(2)}, u32[]{:S(2)}) %all-to-all-start.2) | async-done | bytes 2097184 | tf_op jit(solution)/shard_map/all_to_all | solution.py:54
  273.6 7.7 %reduce.8 = f32[4,131072]{1,0:T(4,128)S(1)} reduce(f32[4,1,131072]{2,1,0:T(1,128)} %all-to-all-done.2, f32[]{:T(128)} %broadcast.474), dimensions={1}, to_apply=%all_to_all.112.reduce_sub_computation | reduce | bytes 4194308 | tf_op jit(solution)/shard_map/all_to_all | solution.py:54
  281.3 4.0 reshape.458
  285.3 6.9 copy.85
  292.2 4.5 all_to_all.115
  319.5 4.0 all-to-all-done.3
  323.5 4.7 reduce.9
  340.2 4.3 collective-permute-done.5
  350.2 27.7 %gather_fusion = f32[8192,128]{1,0:T(8,128)} fusion(f32[1296,128]{1,0:T(8,128)S(1)} %reshape.362, s32[8192]{0:T(1024)S(1)} %copy-done.19), kind=kCustom, calls=%fused_computation.clone | custom fusion | bytes 8421376 | tf_op jit(solution)/shard_map/jit(_take)/gather | solution.py:156
  377.9 8.8 %fusion.11 = f32[8192]{0:T(1024)S(1)} fusion(f32[8192,128]{1,0:T(8,128)} %gather_fusion, f32[8192]{0:T(1024)S(1)} %bitcast.258, f32[8192]{0:T(1024)S(1)} %bitcast.260, f32[8192]{0:T(1024)S(1)} %bitcast.262, f32[8192]{0:T(1024)S(1)} %bitcast.256, f32[512,128]{1,0:T(8,128)S(1)} %get-tuple-element.41, f32[512,128]{1,0:T(8,128)S(1)} %copy-done.2, ...), kind=kLoop, calls=%fused_computation.29 | loop fusion | flops 10477568 | bytes 5414912 | tf_op jit(solution)/shard_map/reduce_sum | solution.py:157
  387.6 5.8 fusion.8
  393.5 44.4 %scatter_custom_fusion.1 = f32[1296,128]{1,0:T(8,128)S(1)} fusion(s32[8192]{0:T(1024)} %bitcast.279, f32[8192,128]{1,0:T(8,128)} %fusion.8, f32[]{:T(128)} %constant.114.clone.1), kind=kCustom, calls=%fused_computation.65 | custom fusion | flops 1048576 | bytes 664064 | tf_op jit(solution)/shard_map/scatter-add | solution.py:151
  442.7 4.3 collective-permute-done.13
  456.0 4.6 copy.89
  460.6 3.9 reshape.461
  464.6 18.2 %all_to_all.145 = f32[4,1,65536]{2,1,0:T(1,128)S(1)} all-to-all(f32[4,1,65536]{2,1,0:T(1,128)S(1)} %reshape.461), channel_id=1, replica_groups=mesh['groups'=2,'wide'=4,'narrow'=2,'pair'=2] {'narrow','pair'}, dimensions={0} | all-to-all | bytes 2097152 | tf_op jit(solution)/shard_map/all_to_all | solution.py:58
  482.8 3.7 reduce.10
  489.9 3.5 copy.110
  493.4 5.3 fusion.61
  498.7 5.5 copy.92
  504.3 4.5 reshape.463
  508.8 51.7 %all_to_all.146 = f32[4,1,131072]{2,1,0:T(1,128)} all-to-all(f32[4,1,131072]{2,1,0:T(1,128)S(1)} %reshape.463), channel_id=1, replica_groups=mesh['groups'=2,'wide'=4,'narrow'=2,'pair'=2] {'wide'}, dimensions={0} | all-to-all | bytes 4194304 | tf_op jit(solution)/shard_map/all_to_all | solution.py:54
  560.6 7.7 %reduce.11 = f32[4,131072]{1,0:T(4,128)S(1)} reduce(f32[4,1,131072]{2,1,0:T(1,128)} %all_to_all.146, f32[]{:T(128)} %broadcast.474), dimensions={1}, to_apply=%all_to_all.124.reduce_sub_computation | reduce | bytes 4194308 | tf_op jit(solution)/shard_map/all_to_all | solution.py:54
  568.2 4.0 reshape.464
  572.2 5.9 copy.93
  578.1 4.0 copy.94
  582.1 4.0 fusion.74
  587.1 4.0 fusion.75
  591.1 4.5 copy.95
  595.6 4.5 reshape.465
  600.1 50.7 %all_to_all.147 = f32[4,1,131072]{2,1,0:T(1,128)} all-to-all(f32[4,1,131072]{2,1,0:T(1,128)S(1)} %reshape.465), channel_id=1, replica_groups=mesh['groups'=2,'wide'=4,'narrow'=2,'pair'=2] {'wide'}, dimensions={0} | all-to-all | bytes 4194304 | tf_op jit(solution)/shard_map/all_to_all | solution.py:54
  650.8 7.7 %reduce.12 = f32[4,131072]{1,0:T(4,128)S(1)} reduce(f32[4,1,131072]{2,1,0:T(1,128)} %all_to_all.147, f32[]{:T(128)} %broadcast.474), dimensions={1}, to_apply=%all_to_all.128.reduce_sub_computation | reduce | bytes 4194308 | tf_op jit(solution)/shard_map/all_to_all | solution.py:54
  658.5 4.0 reshape.466
  662.5 6.9 copy.97
  669.4 4.5 all_to_all.131
  689.7 4.1 collective-permute-done.21
  696.5 4.0 collective-permute-done.23
  701.2 4.7 reduce.13
  719.0 4.2 collective-permute-done.17
  730.4 27.7 %gather_fusion.2 = f32[8192,128]{1,0:T(8,128)} fusion(f32[1296,128]{1,0:T(8,128)S(1)} %reshape.369, s32[8192]{0:T(1024)S(1)} %copy-done.20), kind=kCustom, calls=%fused_computation.2.clone | custom fusion | bytes 8421376 | tf_op jit(solution)/shard_map/jit(_take)/gather | solution.py:156
  758.1 8.7 %fusion.12 = f32[8192]{0:T(1024)S(1)} fusion(f32[8192,128]{1,0:T(8,128)} %gather_fusion.2, f32[8192]{0:T(1024)S(1)} %bitcast.259, f32[8192]{0:T(1024)S(1)} %bitcast.261, f32[8192]{0:T(1024)S(1)} %bitcast.263, f32[8192]{0:T(1024)S(1)} %bitcast.257, f32[512,128]{1,0:T(8,128)S(1)} %get-tuple-element.41, f32[512,128]{1,0:T(8,128)S(1)} %copy-done.3, ...), kind=kLoop, calls=%fused_computation.30 | loop fusion | flops 10477568 | bytes 5414912 | tf_op jit(solution)/shard_map/reduce_sum | solution.py:157
  (220 shorter events, 124.8 us)
Async XLA Ops:
  0.0 347.6 %copy-start = (bf16[24,128,128]{2,1,0:T(8,128)(2,1)S(1)}, bf16[24,128,128]{2,1,0:T(8,128)(2,1)}, u32[]{:S(2)}) copy-start(bf16[24,128,128]{2,1,0:T(8,128)(2,1)} %param.19) | copy-start | bytes 2359300
  1.0 59.8 %copy-start.1 = (f32[512,128]{1,0:T(8,128)}, f32[512,128]{1,0:T(8,128)S(1)}, u32[]{:S(2)}) copy-start(f32[512,128]{1,0:T(8,128)S(1)} %get-tuple-element.42) | copy-start | bytes 786436
  1.0 59.8 %copy-start.4 = (f32[512,128]{1,0:T(8,128)}, f32[512,128]{1,0:T(8,128)S(1)}, u32[]{:S(2)}) copy-start(f32[512,128]{1,0:T(8,128)S(1)} %get-tuple-element.43) | copy-start | bytes 786436
  4.1 5.8 copy-start.22
  9.9 61.6 %copy-start.29 = (pred[32]{0:T(512)(128)(4,1)S(1)}, pred[32]{0:T(512)(128)(4,1)}, u32[]{:S(2)}) copy-start(pred[32]{0:T(512)(128)(4,1)} %constant.132.clone.1) | copy-start | bytes 100
  54.4 6.6 collective-permute-start
  59.4 5.9 collective-permute-start.1
  65.3 2.6 collective-permute-start.2
  66.6 4.8 collective-permute-start.3
  127.7 53.1 %all-to-all-start.1 = ((f32[4,1,131072]{2,1,0:T(1,128)}), f32[4,1,131072]{2,1,0:T(1,128)}, u32[]{:S(2)}, u32[]{:S(2)}) async-start(f32[4,1,131072]{2,1,0:T(1,128)} %reshape.455), calls=%async_computation.1 | async-start | bytes 4194304 | tf_op jit(solution)/shard_map/all_to_all | solution.py:54
  132.7 73.5 %copy-start.31 = (f32[64]{0:T(128)}, f32[64]{0:T(128)S(1)}, u32[]{:S(2)}) copy-start(f32[64]{0:T(128)S(1)} %multiply_multiply_fusion.1) | copy-start | bytes 772
  132.9 73.4 %copy-start.8 = (f32[256,64]{0,1:T(8,128)}, f32[256,64]{0,1:T(8,128)S(1)}, u32[]{:S(2)}) copy-start(f32[256,64]{0,1:T(8,128)S(1)} %broadcast_add_fusion) | copy-start | bytes 196612
  215.8 10.0 %copy-start.23 = (f32[512]{0:T(512)S(1)}, f32[512]{0:T(512)}, u32[]{:S(2)}) copy-start(f32[512]{0:T(512)} %param.12) | copy-start | bytes 6148
  215.8 16.0 %copy-start.7 = (f32[64,512]{1,0:T(8,128)S(1)}, f32[64,512]{1,0:T(8,128)}, u32[]{:S(2)}) copy-start(f32[64,512]{1,0:T(8,128)} %param.15) | copy-start | bytes 393220
  215.8 16.0 %copy-start.21 = (s32[2,4,8,128]{3,2,1,0:T(8,128)S(1)}, s32[2,4,8,128]{3,2,1,0:T(8,128)}, u32[]{:S(2)}) copy-start(s32[2,4,8,128]{3,2,1,0:T(8,128)} %get-tuple-element.38) | copy-start | bytes 98308
  221.4 52.2 %all-to-all-start.2 = ((f32[4,1,131072]{2,1,0:T(1,128)}), f32[4,1,131072]{2,1,0:T(1,128)}, u32[]{:S(2)}, u32[]{:S(2)}) async-start(f32[4,1,131072]{2,1,0:T(1,128)} %reshape.457), calls=%async_computation.2 | async-start | bytes 4194304 | tf_op jit(solution)/shard_map/all_to_all | solution.py:54
  225.9 85.0 %collective-permute-start.8 = (bf16[1,1,512]{2,1,0:T(2,128)(2,1)S(1)}, bf16[1,1,512]{2,1,0:T(2,128)(2,1)}, u32[]{:S(2)}, u32[]{:S(2)}) collective-permute-start(bf16[1,1,512]{2,1,0:T(2,128)(2,1)S(1)} %reshape.364), channel_id=1, source_target_pairs={{0,4},{4,8},{8,12},{1,5},{5,9},{9,13},{2,6},{6,10},{10,14},{3,7},{... | collective-permute-start | bytes 3080 | tf_op jit(solution)/shard_map/ppermute | solution.py:24
  230.3 81.2 %collective-permute-start.9 = (bf16[1,1,512]{2,1,0:T(2,128)(2,1)S(1)}, bf16[1,1,512]{2,1,0:T(2,128)(2,1)}, u32[]{:S(2)}, u32[]{:S(2)}) collective-permute-start(bf16[1,1,512]{2,1,0:T(2,128)(2,1)S(1)} %reshape.364), channel_id=1, source_target_pairs={{4,0},{8,4},{12,8},{5,1},{9,5},{13,9},{6,2},{10,6},{14,10},{7,3},{... | collective-permute-start | bytes 3080 | tf_op jit(solution)/shard_map/ppermute | solution.py:26
  305.5 18.0 %all-to-all-start.3 = ((f32[4,1,65536]{2,1,0:T(1,128)}), f32[4,1,65536]{2,1,0:T(1,128)S(1)}, u32[]{:S(2)}, u32[]{:S(2)}) async-start(f32[4,1,65536]{2,1,0:T(1,128)} %reshape.459), calls=%async_computation.3 | async-start | bytes 2097152 | tf_op jit(solution)/shard_map/all_to_all | solution.py:58
  312.2 3.7 collective-permute-start.10
  314.6 4.2 collective-permute-start.11
  315.9 7.5 copy-start.28
  333.0 6.8 copy-start.35
  333.1 17.1 %copy-start.19 = (s32[8192]{0:T(1024)S(1)}, s32[8192]{0:T(1024)}, u32[]{:S(2)}) copy-start(s32[8192]{0:T(1024)} %fusion.79) | copy-start | bytes 98308
  337.2 3.0 collective-permute-start.4
  338.5 6.0 collective-permute-start.5
  344.5 3.6 collective-permute-start.6
  346.3 3.6 collective-permute-start.7
  350.1 27.7 %copy-start.2 = (f32[512,128]{1,0:T(8,128)S(1)}, f32[512,128]{1,0:T(8,128)}, u32[]{:S(2)}) copy-start(f32[512,128]{1,0:T(8,128)} %copy-done.1) | copy-start | bytes 786436
  350.1 27.7 %copy-start.5 = (f32[512,128]{1,0:T(8,128)S(1)}, f32[512,128]{1,0:T(8,128)}, u32[]{:S(2)}) copy-start(f32[512,128]{1,0:T(8,128)} %copy-done.4) | copy-start | bytes 786436
  350.1 27.7 %copy-start.11 = (f32[16,1,512]{2,1,0:T(1,128)S(1)}, f32[16,1,512]{2,1,0:T(1,128)}, u32[]{:S(2)}) copy-start(f32[16,1,512]{2,1,0:T(1,128)} %get-tuple-element.27) | copy-start | bytes 98308
  350.1 27.7 %copy-start.13 = (f32[16,1,512]{2,1,0:T(1,128)S(1)}, f32[16,1,512]{2,1,0:T(1,128)}, u32[]{:S(2)}) copy-start(f32[16,1,512]{2,1,0:T(1,128)} %get-tuple-element.28) | copy-start | bytes 98308
  350.1 27.7 %copy-start.15 = (f32[16,1,512]{2,1,0:T(1,128)S(1)}, f32[16,1,512]{2,1,0:T(1,128)}, u32[]{:S(2)}) copy-start(f32[16,1,512]{2,1,0:T(1,128)} %get-tuple-element.29) | copy-start | bytes 98308
  350.2 27.7 %copy-start.17 = (f32[16,1,512]{2,1,0:T(1,128)S(1)}, f32[16,1,512]{2,1,0:T(1,128)}, u32[]{:S(2)}) copy-start(f32[16,1,512]{2,1,0:T(1,128)} %get-tuple-element.30) | copy-start | bytes 98308
  377.8 8.9 %copy-start.24 = (f32[512]{0:T(512)S(1)}, f32[512]{0:T(512)}, u32[]{:S(2)}) copy-start(f32[512]{0:T(512)} %param.12) | copy-start | bytes 6148
  377.8 8.9 %copy-start.26 = (pred[512]{0:T(512)(128)(4,1)S(1)}, pred[512]{0:T(512)(128)(4,1)}, u32[]{:S(2)}) copy-start(pred[512]{0:T(512)(128)(4,1)} %copy-done.25) | copy-start | bytes 1540
  377.8 8.9 %copy-start.33 = (s32[24]{0:T(128)S(1)}, s32[24]{0:T(128)}, u32[]{:S(2)}) copy-start(s32[24]{0:T(128)} %param.17) | copy-start | bytes 292
  377.8 9.6 %copy-start.10 = (f32[64,512]{1,0:T(8,128)S(1)}, f32[64,512]{1,0:T(8,128)}, u32[]{:S(2)}) copy-start(f32[64,512]{1,0:T(8,128)} %param.16) | copy-start | bytes 393220
  393.5 60.9 %copy-start.30 = (pred[32]{0:T(512)(128)(4,1)S(1)}, pred[32]{0:T(512)(128)(4,1)}, u32[]{:S(2)}) copy-start(pred[32]{0:T(512)(128)(4,1)} %constant.132.clone.1) | copy-start | bytes 100
  437.9 4.8 collective-permute-start.12
  441.1 5.9 collective-permute-start.13
  447.0 4.7 collective-permute-start.14
  450.5 3.8 collective-permute-start.15
  582.0 4.0 copy-start.9
  582.1 4.0 copy-start.32
  677.3 9.0 %copy-start.27 = (bf16[512]{0:T(512)(128)(2,1)S(1)}, bf16[512]{0:T(512)(128)(2,1)}, u32[]{:S(2)}) copy-start(bf16[512]{0:T(512)(128)(2,1)} %get-tuple-element.44) | copy-start | bytes 3076
  682.7 18.5 %all-to-all-start.7 = ((f32[4,1,65536]{2,1,0:T(1,128)}), f32[4,1,65536]{2,1,0:T(1,128)S(1)}, u32[]{:S(2)}, u32[]{:S(2)}) async-start(f32[4,1,65536]{2,1,0:T(1,128)} %reshape.467), calls=%async_computation.7 | async-start | bytes 2097152 | tf_op jit(solution)/shard_map/all_to_all | solution.py:58
  686.2 3.4 collective-permute-start.20
  688.4 5.5 collective-permute-start.21
  693.9 2.6 collective-permute-start.22
  695.1 5.3 collective-permute-start.23
  708.0 10.7 %copy-start.36 = (pred[24]{0:T(512)(128)(4,1)S(1)}, pred[24]{0:T(512)(128)(4,1)}, u32[]{:S(2)}) copy-start(pred[24]{0:T(512)(128)(4,1)} %compare_and_fusion.1) | copy-start | bytes 76
  710.8 19.6 %copy-start.20 = (s32[8192]{0:T(1024)S(1)}, s32[8192]{0:T(1024)}, u32[]{:S(2)}) copy-start(s32[8192]{0:T(1024)} %fusion.79) | copy-start | bytes 98308
  714.9 4.1 collective-permute-start.16
  717.4 5.8 collective-permute-start.17
  723.3 4.8 collective-permute-start.18
  726.2 4.0 collective-permute-start.19
  730.4 27.7 %copy-start.3 = (f32[512,128]{1,0:T(8,128)S(1)}, f32[512,128]{1,0:T(8,128)}, u32[]{:S(2)}) copy-start(f32[512,128]{1,0:T(8,128)} %copy-done.1) | copy-start | bytes 786436
  730.4 27.7 %copy-start.6 = (f32[512,128]{1,0:T(8,128)S(1)}, f32[512,128]{1,0:T(8,128)}, u32[]{:S(2)}) copy-start(f32[512,128]{1,0:T(8,128)} %copy-done.4) | copy-start | bytes 786436
  730.4 27.7 %copy-start.12 = (f32[16,1,512]{2,1,0:T(1,128)S(1)}, f32[16,1,512]{2,1,0:T(1,128)}, u32[]{:S(2)}) copy-start(f32[16,1,512]{2,1,0:T(1,128)} %get-tuple-element.27) | copy-start | bytes 98308
  730.4 27.7 %copy-start.14 = (f32[16,1,512]{2,1,0:T(1,128)S(1)}, f32[16,1,512]{2,1,0:T(1,128)}, u32[]{:S(2)}) copy-start(f32[16,1,512]{2,1,0:T(1,128)} %get-tuple-element.28) | copy-start | bytes 98308
  730.4 27.7 %copy-start.16 = (f32[16,1,512]{2,1,0:T(1,128)S(1)}, f32[16,1,512]{2,1,0:T(1,128)}, u32[]{:S(2)}) copy-start(f32[16,1,512]{2,1,0:T(1,128)} %get-tuple-element.29) | copy-start | bytes 98308
  730.4 27.7 %copy-start.18 = (f32[16,1,512]{2,1,0:T(1,128)S(1)}, f32[16,1,512]{2,1,0:T(1,128)}, u32[]{:S(2)}) copy-start(f32[16,1,512]{2,1,0:T(1,128)} %get-tuple-element.30) | copy-start | bytes 98308
  758.1 8.8 %copy-start.34 = (s32[24]{0:T(128)S(1)}, s32[24]{0:T(128)}, u32[]{:S(2)}) copy-start(s32[24]{0:T(128)} %param.17) | copy-start | bytes 292
  (1 other events, 0.5 us)
where the time goes:
time: 779 us; the launch traced here: 768 us
  local copies, waits for them, and re-layouts  216 us (28%)
  other arithmetic  175 us (22%)
  blocking collectives  139 us (18%)
  waiting for transfers between devices  131 us (17%)
  starting transfers between devices  63.6 us (8%)
  matrix products  41 us (5%)
    all_to_all x2, blocking collectives, slab_turn(): lax.all_to_all(values, 'wide', split_axis=2, concat_axis=0, tiled=True)  102 us
    scatter-add x2, other arithmetic, apply_operator(): jnp.zeros((line_count, REGION), jnp.float32).at[line_ids].add(source_lines)  88.9 us
    all_to_all x2, waiting for transfers between devices, slab_turn(): lax.all_to_all(values, 'wide', split_axis=2, concat_axis=0, tiled=True)  88.3 us
    unnamed x100, local copies, waits for them, and re-layouts  61.4 us
    gather x2, local copies, waits for them, and re-layouts, apply_operator(): gathered = jnp.take(padded, line_ids, axis=0).reshape(16, -1, REGION)  55.3 us
    all_to_all x8, local copies, waits for them, and re-layouts, slab_turn(): lax.all_to_all(values, 'wide', split_axis=2, concat_axis=0, tiled=True)  42.6 us
    ppermute x12, waiting for transfers between devices, with_halo(): lax.ppermute(head, axis, [((i + 1) % count, i) for i in range(ends)])  37.9 us
    all_to_all x2, blocking collectives, pencil_turn(): lax.all_to_all(values, ('narrow', 'pair'), split_axis=2, concat_axis=0, t...  36.8 us
  transfers between devices with their start and end apart: 28, of which 18 were waited for; matrix products, arithmetic and copies ran while one was open for 5% of the time, Pallas kernels for 0%

commit v1 on v0

v1 whole, which is shorter than its diff:
```python
import functools

import jax
import jax.numpy as jnp
import numpy as np
from jax import lax
from jax.experimental import pallas as pl
from jax.experimental.pallas import tpu as pltpu
from jax.sharding import PartitionSpec as P

GRID = 256
REGION = 128
BLOCK = 128
HALF = 64
KERNEL_GAIN = 4.0
SCREEN = 1.0 / 1024.0
HIGHEST = lax.Precision.HIGHEST
Y_AXES = ("narrow", "pair")
ALL_AXES = ("wide", "narrow", "pair")
F32 = jnp.float32
VMEM_LIMIT = 24 * 1024 * 1024


def cas(angles):
    return np.cos(angles) + np.sin(angles)


def low_lanes(rows):
    return lax.broadcasted_iota(jnp.int32, (rows, 2 * HALF), 1) < HALF


def swap(values):
    return pltpu.roll(values, HALF, 1)


def dot(left, right):
    return jnp.dot(left, right, precision=HIGHEST, preferred_element_type=F32)


def params():
    return pltpu.CompilerParams(vmem_limit_bytes=VMEM_LIMIT)


def whole_vmem():
    return pl.BlockSpec(memory_space=pltpu.VMEM)


def in_smem():
    return pl.BlockSpec(memory_space=pltpu.SMEM)


def cost(flops, moved):
    return pl.CostEstimate(flops=flops, bytes_accessed=moved, transcendentals=0)


def tables(y_count, span_y):
    depth = GRID // y_count
    reach = span_y + 4
    waves = np.arange(GRID)
    step = 2.0 * np.pi / GRID
    z_table = cas(step * np.outer(np.arange(REGION), waves))
    z_forward = np.zeros((y_count, 2 * REGION, 2 * HALF))
    z_inverse = np.zeros((y_count, 2 * HALF, 2 * REGION))
    symbols = 4.0 * np.sin(np.pi * waves / GRID) ** 2
    shift = np.full((y_count, GRID, 2 * HALF), 1.0)
    y_forward = np.zeros((y_count, GRID, reach))
    for block in range(y_count):
        mine = z_table[:, block * depth : (block + 1) * depth]
        for half in range(2):
            rows = slice(half * REGION, (half + 1) * REGION)
            lanes = slice(half * HALF, half * HALF + depth)
            z_forward[block, rows, lanes] = mine
            z_inverse[block, lanes, rows] = mine.T / GRID
            shift[block, :, lanes] = (
                SCREEN + symbols[:, None] + symbols[None, block * depth : (block + 1) * depth]
            )
        cells = block * span_y - 2 + np.arange(reach)
        y_forward[block] = cas(step * np.outer(waves, cells))
    root = np.sqrt(shift * (shift + 4.0))
    decay = 2.0 / (2.0 + shift + root)
    log_decay = np.log(decay)
    ring = 1.0 / (1.0 - np.exp(GRID * log_decay))
    gain = KERNEL_GAIN / root
    modes = np.stack([decay, log_decay, ring, gain], axis=1)
    single = lambda values: values.astype(np.float32)
    return single(z_forward), single(z_inverse), single(y_forward), single(modes)


def lines_kernel(depth_ref, flag_ref, sample_ref, dipole_ref, source_out, sample_out):
    first = pl.program_id(0) * BLOCK
    sample = sample_ref[...]
    source = jnp.where(flag_ref[...] == 1, -sample, dipole_ref[...])
    lanes = lax.broadcasted_iota(jnp.int32, (16, REGION), 1)
    for panel in range(BLOCK):
        offset = lanes - depth_ref[first + panel]
        rows = slice(panel * 16, panel * 16 + 16)
        for coeff, out in ((source, source_out), (sample, sample_out)):
            line = jnp.zeros((16, REGION), F32)
            for depth in range(4):
                column = coeff[depth * 16 : depth * 16 + 16, panel : panel + 1]
                line = jnp.where(offset == depth, column, line)
            out[rows, :] = line


def panel_lines(base_z, flag, sample, dipole):
    count = base_z.shape[0]
    by_depth = lambda w: w.reshape(16, 4, count).transpose(1, 0, 2).reshape(64, count)
    wide_block = pl.BlockSpec((64, BLOCK), lambda i: (0, i))
    out_block = pl.BlockSpec((16 * BLOCK, REGION), lambda i: (i, 0))
    shape = jax.ShapeDtypeStruct((16 * count, REGION), F32)
    return pl.pallas_call(
        lines_kernel,
        grid=(count // BLOCK,),
        in_specs=[in_smem(), pl.BlockSpec((1, BLOCK), lambda i: (0, i)), wide_block, wide_block],
        out_specs=[out_block, out_block],
        out_shape=[shape, shape],
        compiler_params=params(),
        name="panel_lines",
    )(base_z, flag.reshape(1, -1), by_depth(sample), by_depth(dipole))


def spread_kernel(reach, pieces, vector_ref, row_ref, line_ref, table_ref, *refs):
    outs, grids = refs[:pieces], refs[pieces:]
    step = pl.program_id(0)

    @pl.when(step == 0)
    def _():
        for grid in grids:
            grid[...] = jnp.zeros_like(grid)

    chains = len(grids)

    def body(group, carry):
        for chain in range(chains):
            local = group * chains + chain
            panel = step * BLOCK + local
            value = vector_ref[panel]
            row = row_ref[panel]
            places = [pl.ds(row + a * reach, 4) for a in range(4)]
            held = [grids[chain][place, :] for place in places]
            added = [line_ref[pl.ds(local * 16 + 4 * a, 4), :] * value for a in range(4)]
            for a in range(4):
                grids[chain][places[a], :] = held[a] + added[a]
        return carry

    lax.fori_loop(0, BLOCK // chains, body, 0, unroll=4)

    @pl.when(step == pl.num_programs(0) - 1)
    def _():
        total = grids[0][...]
        for grid in grids[1:]:
            total = total + grid[...]
        half = total.shape[0] // 2
        both = jnp.concatenate([total[:half], total[half:]], axis=1)
        for piece in range(pieces):
            outs[piece][...] = dot(both, table_ref[piece])


def spread(vector, rows, lines, table, reach_x, reach_y):
    count = vector.shape[0]
    pieces = table.shape[0]
    line_count = reach_x * reach_y
    half = line_count // 2
    return pl.pallas_call(
        functools.partial(spread_kernel, reach_y, pieces),
        grid=(count // BLOCK,),
        in_specs=[
            in_smem(),
            in_smem(),
            pl.BlockSpec((16 * BLOCK, REGION), lambda i: (i, 0)),
            pl.BlockSpec(table.shape, lambda i: (0, 0, 0)),
        ],
        out_specs=[pl.BlockSpec((half, 2 * HALF), lambda i: (0, 0))] * pieces,
        out_shape=[jax.ShapeDtypeStruct((half, 2 * HALF), F32)] * pieces,
        scratch_shapes=[pltpu.VMEM((line_count, REGION), F32)] * 4,
        compiler_params=params(),
        cost_estimate=cost(2 * half * 256 * 512, 4 * 16 * count * REGION),
        name="spread",
    )(vector, rows, lines, table)


def forward_kernel(reach_x, reach_y, pieces, *refs):
    parts = refs[:pieces]
    table_ref, modes_ref, spectrum, right_out, left_out, own_out, stacked = refs[pieces:]
    half = reach_x // 2
    tall = pieces * reach_y
    for i in range(half):
        for piece in range(pieces):
            stacked[i * tall + piece * reach_y : i * tall + (piece + 1) * reach_y, :] = parts[
                piece
            ][i * reach_y : (i + 1) * reach_y, :]
    table = table_ref[...]
    for i in range(0, half, 2):
        if i + 1 < half:
            pair = jnp.concatenate(
                [stacked[i * tall : (i + 1) * tall, :], stacked[(i + 1) * tall : (i + 2) * tall, :]],
                axis=1,
            )
            both = dot(table, pair)
            spectrum[i] = both[:, : 2 * HALF]
            spectrum[i + 1] = both[:, 2 * HALF :]
        else:
            spectrum[i] = dot(table, stacked[i * tall : (i + 1) * tall, :])

    chunk = 32

    def body(index, carry):
        rows = pl.ds(pl.multiple_of(index * chunk, chunk), chunk)
        low = low_lanes(chunk)
        decay = modes_ref[0, rows, :]
        log_decay = modes_ref[1, rows, :]
        across_half = jnp.exp(half * log_decay)
        across_cut = jnp.exp((half - 4) * log_decay)
        layers = [spectrum[i, rows, :] for i in range(half)]
        run = layers[0]
        cut_right = run
        for i in range(1, half):
            run = decay * run + layers[i]
            if i == half - 5:
                cut_right = run
        right = run
        run = layers[half - 1]
        cut_left = run
        for i in range(half - 2, -1, -1):
            run = decay * run + layers[i]
            if i == 4:
                cut_left = run
        left = run
        swapped_right, swapped_left = swap(right), swap(left)
        own = jnp.where(low, left + across_half * swapped_left, right + across_half * swapped_right)
        own_out[rows, :] = own
        right_out[0, rows, :] = jnp.where(low, swap(layers[half - 4]), layers[half - 3])
        right_out[1, rows, :] = jnp.where(low, swap(layers[half - 2]), layers[half - 1])
        right_out[2, rows, :] = jnp.where(low, own, cut_right + across_cut * swapped_right)
        left_out[0, rows, :] = jnp.where(low, layers[0], swap(layers[1]))
        left_out[1, rows, :] = jnp.where(low, layers[2], swap(layers[3]))
        left_out[2, rows, :] = jnp.where(low, cut_left + across_cut * swapped_left, own)
        return carry

    lax.fori_loop(0, GRID // chunk, body, 0)


def forward(parts, table, modes, reach_x, reach_y):
    pieces = len(parts)
    half = reach_x // 2
    lanes = 2 * HALF
    struct = lambda *shape: jax.ShapeDtypeStruct(shape, F32)
    return pl.pallas_call(
        functools.partial(forward_kernel, reach_x, reach_y, pieces),
        in_specs=[whole_vmem()] * (pieces + 2),
        out_specs=[whole_vmem()] * 4,
        out_shape=[
            struct(half, GRID, lanes),
            struct(3, GRID, lanes),
            struct(3, GRID, lanes),
            struct(GRID, lanes),
        ],
        scratch_shapes=[pltpu.VMEM((half * pieces * reach_y, lanes), F32)],
        compiler_params=params(),
        cost_estimate=cost(2 * half * 256 * 256 * 128, 4 * half * GRID * lanes * 2),
        name="forward",
    )(*parts, table, modes)


def inverse_kernel(reach_x, reach_y, pieces, fars, *refs):
    power_ref, spectrum, from_left, from_right, own_ref = refs[:5]
    far_refs = refs[5 : 5 + fars]
    table_ref, modes_ref = refs[5 + fars : 7 + fars]
    outs = refs[7 + fars : 7 + fars + pieces]
    field = refs[7 + fars + pieces]
    half = reach_x // 2
    span = reach_x - 4
    chunk = 16

    def body(index, carry):
        rows = pl.ds(pl.multiple_of(index * chunk, chunk), chunk)
        low = low_lanes(chunk)
        decay = modes_ref[0, rows, :]
        log_decay = modes_ref[1, rows, :]
        ring = modes_ref[2, rows, :]
        gain = modes_ref[3, rows, :]
        across_half = jnp.exp(half * log_decay)
        around = jnp.exp((GRID - 4) * log_decay)
        beside = jnp.exp((GRID - reach_x - span) * log_decay)
        layers = [spectrum[i, rows, :] for i in range(half)]
        head = from_left[0, rows, :], from_left[1, rows, :]
        tail = from_right[0, rows, :], from_right[1, rows, :]
        zero = jnp.zeros_like(decay)
        from_head = [head[0], swap(head[0]), head[1], swap(head[1])]
        from_tail = [swap(tail[0]), tail[0], swap(tail[1]), tail[1]]
        head_sum = from_head[0]
        for i in range(1, 4):
            head_sum = decay * head_sum + from_head[i]
        tail_sum = from_tail[3]
        for i in range(2, -1, -1):
            tail_sum = decay * tail_sum + from_tail[i]
        for i in range(4):
            layers[i] = layers[i] + jnp.where(low, from_head[i], zero)
        for i in range(4):
            place = half - 4 + i
            layers[place] = layers[place] + jnp.where(low, zero, from_tail[i])
        total = own_ref[rows, :] * jnp.exp((GRID - reach_x) * log_decay)
        one = jnp.ones_like(decay)
        total = total + from_left[2, rows, :] * jnp.where(low, beside, one)
        total = total + from_right[2, rows, :] * jnp.where(low, one, beside)
        for far in range(fars):
            power = jnp.where(low, power_ref[2 * far], power_ref[2 * far + 1])
            total = total + far_refs[far][rows, :] * jnp.exp(power * log_decay)
        entering = (swap(total) + around * jnp.where(low, head_sum, tail_sum)) * ring
        run = layers[0]
        for i in range(1, half):
            run = decay * run + layers[i]
        right_start = jnp.where(low, entering, swap(across_half * entering + run))
        run = layers[half - 1]
        for i in range(half - 2, -1, -1):
            run = decay * run + layers[i]
        left_start = jnp.where(low, swap(across_half * entering + run), entering)
        run = right_start
        forward_runs = []
        for i in range(half):
            run = decay * run + layers[i]
            forward_runs.append(run)
        run = left_start
        for i in range(half - 1, -1, -1):
            ahead = decay * run
            field[i, rows, :] = gain * (forward_runs[i] + ahead)
            run = ahead + layers[i]
        return carry

    lax.fori_loop(0, GRID // chunk, body, 0)
    table = table_ref[...]
    for i in range(0, half, 2):
        if i + 1 < half:
            pair = dot(table, jnp.concatenate([field[i], field[i + 1]], axis=1))
            results = [pair[:, : 2 * HALF], pair[:, 2 * HALF :]]
        else:
            results = [dot(table, field[i])]
        for j, result in enumerate(results):
            place = slice((i + j) * reach_y, (i + j + 1) * reach_y)
            for piece in range(pieces):
                outs[piece][place, :] = result[piece * reach_y : (piece + 1) * reach_y]


def inverse(powers, spectrum, from_left, from_right, own, fars, table, modes, reach_x, reach_y):
    pieces = table.shape[0] // reach_y
    half = reach_x // 2
    shape = jax.ShapeDtypeStruct((half * reach_y, 2 * HALF), F32)
    return pl.pallas_call(
        functools.partial(inverse_kernel, reach_x, reach_y, pieces, len(fars)),
        in_specs=[in_smem()] + [whole_vmem()] * (6 + len(fars)),
        out_specs=[whole_vmem()] * pieces,
        out_shape=[shape] * pieces,
        scratch_shapes=[pltpu.VMEM((half, GRID, 2 * HALF), F32)],
        compiler_params=params(),
        cost_estimate=cost(2 * half * 256 * 256 * 128, 4 * half * GRID * 2 * HALF * 2),
        name="inverse",
    )(powers, spectrum, from_left, from_right, own, *fars, table, modes)


def sample_kernel(reach, pieces, row_ref, *refs):
    parts = refs[:pieces]
    table_ref, line_ref, base_ref, near_ref, out_ref, field, sums = refs[pieces:]
    step = pl.program_id(0)

    @pl.when(step == 0)
    def _():
        both = dot(jnp.concatenate([part[...] for part in parts], axis=1), table_ref[...])
        half = both.shape[0]
        field[:half, :] = both[:, :REGION]
        field[half:, :] = both[:, REGION:]

    def body(local, carry):
        row = row_ref[step * BLOCK + local]
        total = field[pl.ds(row, 4), :] * line_ref[pl.ds(local * 16, 4), :]
        for a in range(1, 4):
            total = total + field[pl.ds(row + a * reach, 4), :] * line_ref[
                pl.ds(local * 16 + 4 * a, 4), :
            ]
        sums[pl.ds(local, 1), :] = jnp.sum(total, axis=0, keepdims=True)
        return carry

    lax.fori_loop(0, BLOCK, body, 0, unroll=8)
    sampled = lax.dot_general(
        jnp.ones((8, REGION), F32),
        sums[...],
        (((1,), (1,)), ((), ())),
        precision=HIGHEST,
        preferred_element_type=F32,
    )
    out_ref[...] = base_ref[...] + sampled[:1] + near_ref[pl.ds(step, 1), :]


def sample(rows, parts, table, lines, base, near, reach):
    count = rows.shape[0]
    pieces = len(parts)
    half = parts[0].shape[0]
    constant = lambda shape: pl.BlockSpec(shape, lambda i: (0,) * len(shape))
    panel_row = pl.BlockSpec((1, BLOCK), lambda i: (0, i))
    return pl.pallas_call(
        functools.partial(sample_kernel, reach, pieces),
        grid=(count // BLOCK,),
        in_specs=[in_smem()]
        + [constant(part.shape) for part in parts]
        + [
            constant(table.shape),
            pl.BlockSpec((16 * BLOCK, REGION), lambda i: (i, 0)),
            panel_row,
            constant(near.shape),
        ],
        out_specs=panel_row,
        out_shape=jax.ShapeDtypeStruct((1, count), F32),
        scratch_shapes=[
            pltpu.VMEM((2 * half, REGION), F32),
            pltpu.VMEM((BLOCK, REGION), F32),
        ],
        compiler_params=params(),
        cost_estimate=cost(2 * half * 256 * 512, 4 * 16 * count * REGION),
        name="sample",
    )(rows, *parts, table, lines, base, near)


def near_kernel(slots, place_ref, target_ref, vector_ref, tile_ref, out_ref):
    out_ref[...] = jnp.zeros_like(out_ref)
    for slot in range(slots):
        picked = vector_ref[pl.ds(place_ref[slot], 1), :]
        picked = jnp.broadcast_to(picked, (16, BLOCK)).astype(jnp.bfloat16)
        product = lax.dot_general(
            picked,
            tile_ref[slot],
            (((1,), (1,)), ((), ())),
            preferred_element_type=F32,
        )
        target = pl.ds(target_ref[slot], 1)
        out_ref[target, :] = out_ref[target, :] + product[:1]


def near_field(places, targets, blocks, tiles, out_rows):
    slots = tiles.shape[0]
    return pl.pallas_call(
        functools.partial(near_kernel, slots),
        in_specs=[in_smem(), in_smem(), whole_vmem(), whole_vmem()],
        out_specs=whole_vmem(),
        out_shape=jax.ShapeDtypeStruct((out_rows, BLOCK), F32),
        compiler_params=params(),
        cost_estimate=cost(2 * slots * 16 * BLOCK * BLOCK, 2 * slots * BLOCK * BLOCK),
        name="near_field",
    )(places, targets, blocks, tiles)


def shards(
    density,
    surface_flag,
    stencil_base,
    sample_weights,
    dipole_weights,
    near_target,
    near_source,
    near_tiles,
):
    x_count = lax.axis_size("wide")
    y_count = lax.axis_size(Y_AXES)
    x_index = lax.axis_index("wide")
    y_index = lax.axis_index(Y_AXES)
    span_x = REGION // x_count
    span_y = REGION // y_count
    reach_x = span_x + 4
    reach_y = span_y + 4
    count = density.shape[0]
    blocks_dev = count // BLOCK

    z_forward, z_inverse, y_forward, modes = (jnp.asarray(t) for t in tables(y_count, span_y))
    order = y_index ^ jnp.arange(y_count, dtype=jnp.int32)
    z_forward = jnp.take(z_forward, order, axis=0)
    z_inverse = jnp.take(z_inverse, order, axis=0).reshape(y_count * 2 * HALF, 2 * REGION)
    y_picked = jnp.take(y_forward, order, axis=0)
    y_inverse = y_picked.transpose(0, 2, 1).reshape(y_count * reach_y, GRID)
    y_forward = y_inverse.T
    y_inverse = y_inverse / GRID
    modes = lax.dynamic_index_in_dim(modes, y_index, 0, keepdims=False)

    local_x = stencil_base[0] - (x_index * span_x - 2)
    local_y = stencil_base[1] - (y_index * span_y - 2)
    rows = local_x * reach_y + local_y
    source_lines, sample_lines = panel_lines(
        stencil_base[2], surface_flag, sample_weights, dipole_weights
    )
    own_share = jnp.where(surface_flag == 1, 0.0, 0.5).astype(F32)

    neighbour = near_source // blocks_dev
    source_x = x_index + neighbour // 3 - 1
    source_y = y_index + neighbour % 3 - 1
    places = (source_x * y_count + source_y) * blocks_dev + near_source % blocks_dev
    out_rows = 8 * ((blocks_dev + 8) // 8)
    live = near_target >= 0
    places = jnp.where(live, places, 0)
    targets = jnp.where(live, near_target, out_rows - 1)

    far_moves = []
    powers = []

    def add_far(pairs, behind):
        far_moves.append(pairs)
        for distance in (-behind, behind):
            ahead = span_x * distance - reach_x
            powers.append(jnp.where(distance >= 2, ahead, ahead + GRID))

    for shift in range(2, x_count - 1):
        pairs = [(i, (i + shift) % x_count) for i in range(x_count)]
        add_far(pairs, jnp.where(x_index >= shift, shift, shift - x_count))
    if x_count > 2:
        last = x_count - 1
        behind = jnp.where(x_index == 0, -last, jnp.where(x_index == last, last, 0))
        add_far([(0, last), (last, 0)], behind)
    powers = jnp.stack(powers).astype(F32) if powers else jnp.zeros((2,), F32)
    to_right = [(i, i + 1) for i in range(x_count - 1)]
    to_left = [(i + 1, i) for i in range(x_count - 1)]

    def turn(parts):
        return [
            part
            if flip == 0
            else lax.ppermute(part, Y_AXES, [(i, i ^ flip) for i in range(y_count)])
            for flip, part in enumerate(parts)
        ]

    def apply_operator(vector):
        beside = lax.all_gather(
            vector.astype(jnp.bfloat16).reshape(blocks_dev, BLOCK), ALL_AXES, axis=0, tiled=True
        ).astype(F32)
        near_part = near_field(places, targets, beside, near_tiles, out_rows)
        parts = turn(spread(vector, rows, source_lines, z_forward, reach_x, reach_y))
        spectrum, right_going, left_going, own = forward(parts, y_forward, modes, reach_x, reach_y)
        from_left = lax.ppermute(right_going, "wide", to_right)
        from_right = lax.ppermute(left_going, "wide", to_left)
        fars = [lax.ppermute(own, "wide", pairs) for pairs in far_moves]
        parts = turn(
            inverse(
                powers,
                spectrum,
                from_left,
                from_right,
                own,
                fars,
                y_inverse,
                modes,
                reach_x,
                reach_y,
            )
        )
        base = (own_share * vector).reshape(1, -1)
        return sample(rows, parts, z_inverse, sample_lines, base, near_part, reach_y)[0]

    first_image = apply_operator(density)
    second = apply_operator(first_image)
    return jnp.stack([first_image, second])


def solution(mesh):
    panels = P(("groups",) + ALL_AXES)
    columns = P(None, ("groups",) + ALL_AXES)
    in_specs = (
        panels,
        panels,
        columns,
        columns,
        columns,
        panels,
        panels,
        P(("groups",) + ALL_AXES, None, None),
    )
    return jax.shard_map(
        shards, mesh=mesh, in_specs=in_specs, out_specs=columns, check_vma=False
    )
```

time: 779 us -> 212 us (0.27); the launches traced: 768 us -> 211 us
  local copies, waits for them, and re-layouts: 216 us -> 18.3 us
  other arithmetic: 175 us -> 2.21 us
  blocking collectives: 139 us -> 53.3 us
  waiting for transfers between devices: 131 us -> 55.6 us
  Pallas kernels: 0 us -> 51.2 us
  matrix products: 41 us -> 0 us
  starting transfers between devices: 63.6 us -> 30.5 us
    all_to_all x4 -> x0, blocking collectives: 139 us -> none  [the longest x2 102 us: slab_turn(): lax.all_to_all(values, 'wide', split_axis=2, concat_axis=0, tiled=True)]
    all_to_all x4 -> x0, waiting for transfers between devices: 92.3 us -> none  [the longest x2 88.3 us: slab_turn(): lax.all_to_all(values, 'wide', split_axis=2, concat_axis=0, tiled=True)]
    scatter-add x2 -> x0, other arithmetic: 88.9 us -> none  [apply_operator(): jnp.zeros((line_count, REGION), jnp.float32).at[line_ids].add(source_lines)]
    all_to_all x15 -> x0, local copies, waits for them, and re-layouts: 61 us -> none  [the longest x8 42.6 us: slab_turn(): lax.all_to_all(values, 'wide', split_axis=2, concat_axis=0, tiled=True)]
    all_gather x0 -> x2, blocking collectives: none -> 53.3 us  [apply_operator(): lax.all_gather(vector.astype(jnp.bfloat16).reshape(blocks_dev, BLOCK), AL...]
    gather x4 -> x3, local copies, waits for them, and re-layouts: 56.6 us -> 4.63 us  [the longest x1 2.45 us: shards(): jnp.take(z_inverse, order, axis=0).reshape(y_count * 2 * HALF, 2 * REGION)]
    pallas_call x0 -> x11, Pallas kernels: none -> 51.2 us  [the longest x2 11.7 us: inverse(): pl.pallas_call(functools.partial(inverse_kernel, reach_x, reach_y, pieces...]
    unnamed x100 -> x36, local copies, waits for them, and re-layouts: 61.4 us -> 10.4 us
  transfers between devices with their start and end apart: 28 -> 20, of which waited for: 18 -> 6; matrix products, arithmetic and copies ran while one was open for 5% -> 3% of each run, Pallas kernels for 0% -> 1%
where the time goes in v1:
time: 212 us; the launch traced here: 211 us
  waiting for transfers between devices  55.6 us (26%)
  blocking collectives  53.3 us (25%)
  Pallas kernels  51.2 us (24%)
  starting transfers between devices  30.5 us (14%)
  local copies, waits for them, and re-layouts  18.3 us (9%)
  other arithmetic  2.21 us (1%)
    all_gather x2, blocking collectives, apply_operator(): lax.all_gather(vector.astype(jnp.bfloat16).reshape(blocks_dev, BLOCK), AL...  53.3 us
    ppermute x12, waiting for transfers between devices, turn(): lax.ppermute(part, Y_AXES, [(i, i ^ flip) for i in range(y_count)])  28.2 us
    ppermute x4, waiting for transfers between devices, apply_operator(): fars = [lax.ppermute(own, 'wide', pairs) for pairs in far_moves]  27.4 us
    ppermute x4, starting transfers between devices, apply_operator(): fars = [lax.ppermute(own, 'wide', pairs) for pairs in far_moves]  13.9 us
    pallas_call x2, Pallas kernels, inverse(): pl.pallas_call(functools.partial(inverse_kernel, reach_x, reach_y, pieces...  11.7 us
    pallas_call x1, Pallas kernels, panel_lines(): pl.pallas_call(lines_kernel, grid=(count // BLOCK,), in_specs=[in_smem(),...  10.4 us
    unnamed x36, local copies, waits for them, and re-layouts  10.4 us
    pallas_call x2, Pallas kernels, sample(): pl.pallas_call(functools.partial(sample_kernel, reach, pieces), grid=(cou...  9.97 us
  transfers between devices with their start and end apart: 20, of which 6 were waited for; matrix products, arithmetic and copies ran while one was open for 3% of the time, Pallas kernels for 1%

profile of v1, /device:TPU:0, one launch (start us, length us, event | category | flops | bytes accessed | tf_op | source)
XLA Modules:
  0.0 211.5 jit_solution(16083020264902422614)
XLA Ops:
  0.1 0.9 reshape.64
  1.1 0.9 reshape.62
  2.1 1.6 gather_fusion
  3.7 0.1 broadcast_select_fusion.table_ref
  3.8 10.4 %panel_lines.1 = (f32[8192,128]{1,0:T(8,128)S(1)}, f32[8192,128]{1,0:T(8,128)S(1)}) custom-call(s32[512]{0:T(512)S(1)} %bitcast.47, s32[1,512]{1,0:T(1,128)S(1)} %bitcast.45, f32[64,512]{1,0:T(8,128)S(1)} %bitcast.37, f32[64,512]{1,0:T(8,128)S(1)} %bitcast.36), custom_call_target="tpu_custom_call" | custom-call | tf_op jit(solution)/shard_map/panel_lines/pallas_call | solution.py:111
  14.3 2.0 copy-done
  16.2 5.4 %spread.2 = (f32[648,128]{1,0:T(8,128)S(1)}, f32[648,128]{1,0:T(8,128)}, f32[648,128]{1,0:T(8,128)}, f32[648,128]{1,0:T(8,128)S(1)}) custom-call(f32[512]{0:T(512)S(1)} %copy-done.12, s32[512]{0:T(512)S(1)} %bitcast.38, f32[8192,128]{1,0:T(8,128)S(1)} %get-tuple-element.31.line_ref, f32[4,256,128]{2,1,0:T(8,128)S(1)} %broadcast_select_fusion.table_ref), custom_call_target="tpu_custom_call" | custom-call | flops 169869312 | bytes 4194304 | tf_op jit(solution)/shard_map/spread/pallas_call | solution.py:164
  21.6 0.5 collective-permute-start
  22.1 2.5 %collective-permute-start.1 = (f32[648,128]{1,0:T(8,128)}, f32[648,128]{1,0:T(8,128)S(1)}, u32[]{:S(2)}, u32[]{:S(2)}) collective-permute-start(f32[648,128]{1,0:T(8,128)} %get-tuple-element.34), channel_id=1, source_target_pairs={{0,2},{1,3},{2,0},{3,1},{4,6},{5,7},{6,4},{7,5},{8,10},{9,11},{10,... | collective-permute-start | bytes 995336 | tf_op jit(solution)/shard_map/ppermute | solution.py:522
  24.6 0.1 collective-permute-start.2
  24.7 0.6 gather_fusion.1
  25.3 0.0 copy-start.16
  25.3 0.0 copy-start.17
  25.3 0.1 select_bitcast_fusion
  25.4 0.1 copy.22
  25.6 1.1 dynamic-slice_bitcast_fusion.refs_5_.refs_8_
  26.7 0.0 collective-permute-done.refs_1_
  26.7 6.8 %collective-permute-done.1.refs_2_ = f32[648,128]{1,0:T(8,128)S(1)} collective-permute-done((f32[648,128]{1,0:T(8,128)}, f32[648,128]{1,0:T(8,128)S(1)}, u32[]{:S(2)}, u32[]{:S(2)}) %collective-permute-start.1) | collective-permute-done | bytes 331808 | tf_op jit(solution)/shard_map/ppermute | solution.py:522
  33.5 6.7 %collective-permute-done.2.refs_3_ = f32[648,128]{1,0:T(8,128)S(1)} collective-permute-done((f32[648,128]{1,0:T(8,128)S(1)}, f32[648,128]{1,0:T(8,128)S(1)}, u32[]{:S(2)}, u32[]{:S(2)}) %collective-permute-start.2) | collective-permute-done | bytes 331808 | tf_op jit(solution)/shard_map/ppermute | solution.py:522
  40.1 4.0 %forward.2 = (f32[18,256,128]{2,1,0:T(8,128)S(1)}, f32[3,256,128]{2,1,0:T(8,128)}, f32[3,256,128]{2,1,0:T(8,128)}, f32[256,128]{1,0:T(8,128)S(1)}) custom-call(f32[648,128]{1,0:T(8,128)S(1)} %get-tuple-element.32.refs_0_, f32[648,128]{1,0:T(8,128)S(1)} %collective-permute-done.refs_1_, f32[648,128]{1,0:T(8,128)S(1)} %collective-permute-done.1.refs_2_, ...), custom_call_target="tpu_custom_call" | custom-call | flops 301989888 | bytes 4718592 | tf_op jit(solution)/shard_map/forward/pallas_call | solution.py:248
  44.1 1.4 copy-done.6
  45.5 3.5 %collective-permute-start.3 = (f32[3,256,128]{2,1,0:T(8,128)}, f32[3,256,128]{2,1,0:T(8,128)S(1)}, u32[]{:S(2)}, u32[]{:S(2)}) collective-permute-start(f32[3,256,128]{2,1,0:T(8,128)} %get-tuple-element.37), channel_id=1, source_target_pairs={{0,4},{4,8},{8,12},{1,5},{5,9},{9,13},{2,6},{6,10},{10,14},{3,7},{... | collective-permute-start | bytes 1179656 | tf_op jit(solution)/shard_map/ppermute | solution.py:533
  49.1 1.3 collective-permute-start.4
  50.4 3.7 %collective-permute-start.5 = (f32[256,128]{1,0:T(8,128)S(1)}, f32[256,128]{1,0:T(8,128)S(1)}, u32[]{:S(2)}, u32[]{:S(2)}) collective-permute-start(f32[256,128]{1,0:T(8,128)S(1)} %get-tuple-element.39.refs_4_), channel_id=1, source_target_pairs={{0,8},{4,12},{8,0},{12,4},{1,9},{5,13},{9,1},{13,5},{2,10},{6,14},... | collective-permute-start | bytes 393224 | tf_op jit(solution)/shard_map/ppermute | solution.py:535
  54.1 3.3 %collective-permute-start.6 = (f32[256,128]{1,0:T(8,128)S(1)}, f32[256,128]{1,0:T(8,128)S(1)}, u32[]{:S(2)}, u32[]{:S(2)}) collective-permute-start(f32[256,128]{1,0:T(8,128)S(1)} %get-tuple-element.39.refs_4_), channel_id=1, source_target_pairs={{0,12},{12,0},{1,13},{13,1},{2,14},{14,2},{3,15},{15,3},{16,28},{2... | collective-permute-start | bytes 393224 | tf_op jit(solution)/shard_map/ppermute | solution.py:535
  57.4 0.1 add_convert_fusion.refs_0_
  57.5 14.1 %collective-permute-done.5.refs_5_ = f32[256,128]{1,0:T(8,128)S(1)} collective-permute-done((f32[256,128]{1,0:T(8,128)S(1)}, f32[256,128]{1,0:T(8,128)S(1)}, u32[]{:S(2)}, u32[]{:S(2)}) %collective-permute-start.5) | collective-permute-done | bytes 131104 | tf_op jit(solution)/shard_map/ppermute | solution.py:535
  71.6 0.7 copy-done.8
  72.2 0.0 collective-permute-done.6.refs_6_
  72.2 0.7 copy-done.10
  72.9 1.7 copy-done.7
  74.6 0.9 copy-done.9
  75.5 0.9 copy-done.11
  76.4 6.3 %inverse.2 = (f32[648,128]{1,0:T(8,128)S(1)}, f32[648,128]{1,0:T(8,128)}, f32[648,128]{1,0:T(8,128)}, f32[648,128]{1,0:T(8,128)}) custom-call(f32[4]{0:T(128)S(1)} %add_convert_fusion.refs_0_, f32[18,256,128]{2,1,0:T(8,128)S(1)} %copy-done.7, f32[3,256,128]{2,1,0:T(8,128)S(1)} %collective-permute-done.3.refs_2_, ...), custom_call_target="tpu_custom_call" | custom-call | flops 301989888 | bytes 4718592 | tf_op jit(solution)/shard_map/inverse/pallas_call | solution.py:348
  82.7 1.5 collective-permute-start.8
  84.2 0.4 collective-permute-start.9
  84.6 0.1 broadcast_bitcast_fusion
  84.6 27.3 %all-gather = bf16[16,4,128]{2,1,0:T(4,128)(2,1)S(1)} all-gather(bf16[1,4,128]{2,1,0:T(4,128)(2,1)S(1)} %get-tuple-element.61), channel_id=1, replica_groups=mesh['groups'=2,'wide'=4,'narrow'=2,'pair'=2] {'wide','narrow','pair'}, dimensions={0}, use_global_device_ids=true | all-gather | bytes 17408 | tf_op jit(solution)/shard_map/all_gather | solution.py:527
  112.0 2.4 %gather_fusion.2 = f32[4,128,256]{2,1,0:T(8,128)} fusion(f32[4,128,256]{2,1,0:T(8,128)} %constant.139.clone, s32[1024]{0:T(1024)S(1)} %pad_clamp_fusion), kind=kCustom, calls=%fused_computation.2 | custom fusion | bytes 1048592 | tf_op jit(solution)/shard_map/jit(_take)/gather | solution.py:474
  114.4 1.0 near_field.2.refs_7_
  115.5 1.2 bitcast_select_fusion.refs_4_
  116.7 2.2 %copy-done.1 = f32[8192,128]{1,0:T(8,128)S(1)} copy-done((f32[8192,128]{1,0:T(8,128)S(1)}, f32[8192,128]{1,0:T(8,128)}, u32[]{:S(2)}) %copy-start.1) | copy-done | bytes 4194328
  118.9 5.3 %sample.2 = f32[1,512]{1,0:T(1,128)S(1)} custom-call(s32[512]{0:T(512)S(1)} %bitcast.39, f32[648,128]{1,0:T(8,128)S(1)} %get-tuple-element.40.refs_0_, f32[648,128]{1,0:T(8,128)S(1)} %collective-permute-done.7.refs_1_, f32[648,128]{1,0:T(8,128)S(1)} %collective-permute-done.8.refs_2_, f32[648,128]{1,0:T(8,128)} %collective-permute-done.9.refs_3_, ...), custom_call_target="tpu_custom_call" | custom-call | flops 169869312 | bytes 4194304 | tf_op jit(solution)/shard_map/sample/pallas_call | solution.py:399
  124.2 4.6 %spread.3 = (f32[648,128]{1,0:T(8,128)S(1)}, f32[648,128]{1,0:T(8,128)S(1)}, f32[648,128]{1,0:T(8,128)S(1)}, f32[648,128]{1,0:T(8,128)S(1)}) custom-call(f32[512]{0:T(512)S(1)} %bitcast.42, s32[512]{0:T(512)S(1)} %bitcast.40, f32[8192,128]{1,0:T(8,128)S(1)} %copy-done.4, f32[4,256,128]{2,1,0:T(8,128)S(1)} %broadcast_select_fusion.table_ref), custom_call_target="tpu_custom_call" | custom-call | flops 169869312 | bytes 4194304 | tf_op jit(solution)/shard_map/spread/pallas_call | solution.py:164
  128.7 0.4 collective-permute-start.10
  129.1 0.5 collective-permute-start.11
  129.6 1.0 collective-permute-start.12
  130.7 9.1 %collective-permute-done.11.refs_2_ = f32[648,128]{1,0:T(8,128)S(1)} collective-permute-done((f32[648,128]{1,0:T(8,128)S(1)}, f32[648,128]{1,0:T(8,128)S(1)}, u32[]{:S(2)}, u32[]{:S(2)}) %collective-permute-start.11) | collective-permute-done | bytes 331808 | tf_op jit(solution)/shard_map/ppermute | solution.py:522
  139.8 5.6 %collective-permute-done.12.refs_3_ = f32[648,128]{1,0:T(8,128)S(1)} collective-permute-done((f32[648,128]{1,0:T(8,128)S(1)}, f32[648,128]{1,0:T(8,128)S(1)}, u32[]{:S(2)}, u32[]{:S(2)}) %collective-permute-start.12) | collective-permute-done | bytes 331808 | tf_op jit(solution)/shard_map/ppermute | solution.py:522
  145.4 3.1 %forward.3 = (f32[18,256,128]{2,1,0:T(8,128)S(1)}, f32[3,256,128]{2,1,0:T(8,128)S(1)}, f32[3,256,128]{2,1,0:T(8,128)S(1)}, f32[256,128]{1,0:T(8,128)S(1)}) custom-call(f32[648,128]{1,0:T(8,128)S(1)} %get-tuple-element.45.refs_0_, f32[648,128]{1,0:T(8,128)S(1)} %collective-permute-done.10.refs_1_, f32[648,128]{1,0:T(8,128)S(1)} %collective-permute-done.11.refs_2_, ...), custom_call_target="tpu_custom_call" | custom-call | flops 301989888 | bytes 4718592 | tf_op jit(solution)/shard_map/forward/pallas_call | solution.py:248
  148.4 1.6 collective-permute-start.13
  150.1 1.3 collective-permute-start.14
  151.4 2.7 %collective-permute-start.15 = (f32[256,128]{1,0:T(8,128)S(1)}, f32[256,128]{1,0:T(8,128)S(1)}, u32[]{:S(2)}, u32[]{:S(2)}) collective-permute-start(f32[256,128]{1,0:T(8,128)S(1)} %get-tuple-element.52.refs_4_), channel_id=1, source_target_pairs={{0,8},{4,12},{8,0},{12,4},{1,9},{5,13},{9,1},{13,5},{2,10},{6,14},... | collective-permute-start | bytes 393224 | tf_op jit(solution)/shard_map/ppermute | solution.py:535
  154.1 4.3 %collective-permute-start.16 = (f32[256,128]{1,0:T(8,128)S(1)}, f32[256,128]{1,0:T(8,128)S(1)}, u32[]{:S(2)}, u32[]{:S(2)}) collective-permute-start(f32[256,128]{1,0:T(8,128)S(1)} %get-tuple-element.52.refs_4_), channel_id=1, source_target_pairs={{0,12},{12,0},{1,13},{13,1},{2,14},{14,2},{3,15},{15,3},{16,28},{2... | collective-permute-start | bytes 393224 | tf_op jit(solution)/shard_map/ppermute | solution.py:535
  158.3 13.3 %collective-permute-done.15.refs_5_ = f32[256,128]{1,0:T(8,128)S(1)} collective-permute-done((f32[256,128]{1,0:T(8,128)S(1)}, f32[256,128]{1,0:T(8,128)S(1)}, u32[]{:S(2)}, u32[]{:S(2)}) %collective-permute-start.15) | collective-permute-done | bytes 131104 | tf_op jit(solution)/shard_map/ppermute | solution.py:535
  171.7 5.4 %inverse.3 = (f32[648,128]{1,0:T(8,128)S(1)}, f32[648,128]{1,0:T(8,128)S(1)}, f32[648,128]{1,0:T(8,128)S(1)}, f32[648,128]{1,0:T(8,128)S(1)}) custom-call(f32[4]{0:T(128)S(1)} %add_convert_fusion.refs_0_, f32[18,256,128]{2,1,0:T(8,128)S(1)} %get-tuple-element.49.refs_1_, f32[3,256,128]{2,1,0:T(8,128)S(1)} %collective-permute-done.13.refs_2_, ...), custom_call_target="tpu_custom_call" | custom-call | flops 301989888 | bytes 4718592 | tf_op jit(solution)/shard_map/inverse/pallas_call | solution.py:348
  177.1 0.1 collective-permute-start.17
  177.2 0.3 collective-permute-start.18
  177.5 1.5 collective-permute-start.19
  179.1 25.9 %all-gather.1 = bf16[16,4,128]{2,1,0:T(4,128)(2,1)S(1)} all-gather(bf16[1,4,128]{2,1,0:T(4,128)(2,1)S(1)} %bitcast.50), channel_id=1, replica_groups=mesh['groups'=2,'wide'=4,'narrow'=2,'pair'=2] {'wide','narrow','pair'}, dimensions={0}, use_global_device_ids=true | all-gather | bytes 17408 | tf_op jit(solution)/shard_map/all_gather | solution.py:527
  205.0 1.0 near_field.3.refs_7_
  206.1 0.0 collective-permute-done.17.refs_1_
  206.1 4.7 %sample.3 = f32[1,512]{1,0:T(1,128)S(1)} custom-call(s32[512]{0:T(512)S(1)} %bitcast.41, f32[648,128]{1,0:T(8,128)S(1)} %get-tuple-element.53.refs_0_, f32[648,128]{1,0:T(8,128)S(1)} %collective-permute-done.17.refs_1_, f32[648,128]{1,0:T(8,128)S(1)} %collective-permute-done.18.refs_2_, f32[648,128]{1,0:T(8,128)S(1)} %collective-permute-done.19.refs_3_, ...), custom_call_target="tpu_custom_call" | custom-call | flops 169869312 | bytes 4194304 | tf_op jit(solution)/shard_map/sample/pallas_call | solution.py:399
  210.8 0.6 pad_maximum_fusion
  (52 shorter events, 0.3 us)
Async XLA Ops:
  0.0 3.8 %copy-start.15 = (s32[3,512]{1,0:T(4,128)S(1)}, s32[3,512]{1,0:T(4,128)}, u32[]{:S(2)}) copy-start(s32[3,512]{1,0:T(4,128)} %param.14) | copy-start | bytes 18436
  0.0 3.8 %copy-start.13 = (s32[512]{0:T(512)S(1)}, s32[512]{0:T(512)}, u32[]{:S(2)}) copy-start(s32[512]{0:T(512)} %param.13) | copy-start | bytes 6148
  0.0 16.2 %copy-start.12 = (f32[512]{0:T(512)S(1)}, f32[512]{0:T(512)}, u32[]{:S(2)}) copy-start(f32[512]{0:T(512)} %vector_ref.1) | copy-start | bytes 6148
  14.2 2.0 copy-start
  16.2 5.4 %copy-start.3 = (f32[8192,128]{1,0:T(8,128)}, f32[8192,128]{1,0:T(8,128)S(1)}, u32[]{:S(2)}) copy-start(f32[8192,128]{1,0:T(8,128)S(1)} %get-tuple-element.31.line_ref) | copy-start | bytes 12582916
  16.2 8.5 %copy-start.14 = (f32[4,256,36]{1,2,0:T(8,128)S(1)}, f32[4,256,36]{1,2,0:T(8,128)}, u32[]{:S(2)}) copy-start(f32[4,256,36]{1,2,0:T(8,128)} %constant.140.clone) | copy-start | bytes 442372
  21.6 5.1 %collective-permute-start = (f32[648,128]{1,0:T(8,128)}, f32[648,128]{1,0:T(8,128)S(1)}, u32[]{:S(2)}, u32[]{:S(2)}) collective-permute-start(f32[648,128]{1,0:T(8,128)} %get-tuple-element.33), channel_id=1, source_target_pairs={{0,1},{1,0},{2,3},{3,2},{4,5},{5,4},{6,7},{7,6},{8,9},{9,8},{10,11... | collective-permute-start | bytes 995336 | tf_op jit(solution)/shard_map/ppermute | solution.py:522
  22.1 11.4 %collective-permute-start.1 = (f32[648,128]{1,0:T(8,128)}, f32[648,128]{1,0:T(8,128)S(1)}, u32[]{:S(2)}, u32[]{:S(2)}) collective-permute-start(f32[648,128]{1,0:T(8,128)} %get-tuple-element.34), channel_id=1, source_target_pairs={{0,2},{1,3},{2,0},{3,1},{4,6},{5,7},{6,4},{7,5},{8,10},{9,11},{10,... | collective-permute-start | bytes 995336 | tf_op jit(solution)/shard_map/ppermute | solution.py:522
  24.6 15.5 %collective-permute-start.2 = (f32[648,128]{1,0:T(8,128)S(1)}, f32[648,128]{1,0:T(8,128)S(1)}, u32[]{:S(2)}, u32[]{:S(2)}) collective-permute-start(f32[648,128]{1,0:T(8,128)S(1)} %get-tuple-element.35), channel_id=1, source_target_pairs={{0,3},{1,2},{2,1},{3,0},{4,7},{5,6},{6,5},{7,4},{8,11},{9,10},{10,... | collective-permute-start | bytes 995336 | tf_op jit(solution)/shard_map/ppermute | solution.py:522
  25.3 32.1 %copy-start.16 = (s32[24]{0:T(128)S(1)}, s32[24]{0:T(128)}, u32[]{:S(2)}) copy-start(s32[24]{0:T(128)} %param.17) | copy-start | bytes 292
  25.3 32.1 %copy-start.17 = (s32[24]{0:T(128)S(1)}, s32[24]{0:T(128)}, u32[]{:S(2)}) copy-start(s32[24]{0:T(128)} %param.18) | copy-start | bytes 292
  44.1 1.4 copy-start.6
  45.5 27.4 %collective-permute-start.3 = (f32[3,256,128]{2,1,0:T(8,128)}, f32[3,256,128]{2,1,0:T(8,128)S(1)}, u32[]{:S(2)}, u32[]{:S(2)}) collective-permute-start(f32[3,256,128]{2,1,0:T(8,128)} %get-tuple-element.37), channel_id=1, source_target_pairs={{0,4},{4,8},{8,12},{1,5},{5,9},{9,13},{2,6},{6,10},{10,14},{3,7},{... | collective-permute-start | bytes 1179656 | tf_op jit(solution)/shard_map/ppermute | solution.py:533
  49.1 23.8 %collective-permute-start.4 = (f32[3,256,128]{2,1,0:T(8,128)}, f32[3,256,128]{2,1,0:T(8,128)S(1)}, u32[]{:S(2)}, u32[]{:S(2)}) collective-permute-start(f32[3,256,128]{2,1,0:T(8,128)} %get-tuple-element.38), channel_id=1, source_target_pairs={{4,0},{8,4},{12,8},{5,1},{9,5},{13,9},{6,2},{10,6},{14,10},{7,3},{... | collective-permute-start | bytes 1179656 | tf_op jit(solution)/shard_map/ppermute | solution.py:534
  50.4 21.2 %collective-permute-start.5 = (f32[256,128]{1,0:T(8,128)S(1)}, f32[256,128]{1,0:T(8,128)S(1)}, u32[]{:S(2)}, u32[]{:S(2)}) collective-permute-start(f32[256,128]{1,0:T(8,128)S(1)} %get-tuple-element.39.refs_4_), channel_id=1, source_target_pairs={{0,8},{4,12},{8,0},{12,4},{1,9},{5,13},{9,1},{13,5},{2,10},{6,14},... | collective-permute-start | bytes 393224 | tf_op jit(solution)/shard_map/ppermute | solution.py:535
  54.1 18.2 %collective-permute-start.6 = (f32[256,128]{1,0:T(8,128)S(1)}, f32[256,128]{1,0:T(8,128)S(1)}, u32[]{:S(2)}, u32[]{:S(2)}) collective-permute-start(f32[256,128]{1,0:T(8,128)S(1)} %get-tuple-element.39.refs_4_), channel_id=1, source_target_pairs={{0,12},{12,0},{1,13},{13,1},{2,14},{14,2},{3,15},{15,3},{16,28},{2... | collective-permute-start | bytes 393224 | tf_op jit(solution)/shard_map/ppermute | solution.py:535
  71.6 0.7 copy-start.8
  72.2 0.7 copy-start.10
  72.9 1.7 copy-start.7
  74.6 0.9 copy-start.9
  75.5 0.9 copy-start.11
  76.4 38.0 %copy-start.5 = (bf16[24,128,128]{2,1,0:T(8,128)(2,1)S(1)}, bf16[24,128,128]{2,1,0:T(8,128)(2,1)}, u32[]{:S(2)}) copy-start(bf16[24,128,128]{2,1,0:T(8,128)(2,1)} %tile_ref.3) | copy-start | bytes 2359300
  82.7 34.0 %collective-permute-start.7 = (f32[648,128]{1,0:T(8,128)}, f32[648,128]{1,0:T(8,128)S(1)}, u32[]{:S(2)}, u32[]{:S(2)}) collective-permute-start(f32[648,128]{1,0:T(8,128)} %get-tuple-element.41), channel_id=1, source_target_pairs={{0,1},{1,0},{2,3},{3,2},{4,5},{5,4},{6,7},{7,6},{8,9},{9,8},{10,11... | collective-permute-start | bytes 995336 | tf_op jit(solution)/shard_map/ppermute | solution.py:522
  82.7 34.0 %collective-permute-start.8 = (f32[648,128]{1,0:T(8,128)}, f32[648,128]{1,0:T(8,128)S(1)}, u32[]{:S(2)}, u32[]{:S(2)}) collective-permute-start(f32[648,128]{1,0:T(8,128)} %get-tuple-element.42), channel_id=1, source_target_pairs={{0,2},{1,3},{2,0},{3,1},{4,6},{5,7},{6,4},{7,5},{8,10},{9,11},{10,... | collective-permute-start | bytes 995336 | tf_op jit(solution)/shard_map/ppermute | solution.py:522
  84.2 32.5 %collective-permute-start.9 = (f32[648,128]{1,0:T(8,128)}, f32[648,128]{1,0:T(8,128)}, u32[]{:S(2)}, u32[]{:S(2)}) collective-permute-start(f32[648,128]{1,0:T(8,128)} %get-tuple-element.43), channel_id=1, source_target_pairs={{0,3},{1,2},{2,1},{3,0},{4,7},{5,6},{6,5},{7,4},{8,11},{9,10},{10,... | collective-permute-start | bytes 995336 | tf_op jit(solution)/shard_map/ppermute | solution.py:522
  116.7 2.2 %copy-start.1 = (f32[8192,128]{1,0:T(8,128)S(1)}, f32[8192,128]{1,0:T(8,128)}, u32[]{:S(2)}) copy-start(f32[8192,128]{1,0:T(8,128)} %copy-done) | copy-start | bytes 12582916
  118.9 5.3 %copy-start.4 = (f32[8192,128]{1,0:T(8,128)S(1)}, f32[8192,128]{1,0:T(8,128)}, u32[]{:S(2)}) copy-start(f32[8192,128]{1,0:T(8,128)} %copy-done.3) | copy-start | bytes 12582916
  128.7 1.9 collective-permute-start.10
  129.1 10.6 %collective-permute-start.11 = (f32[648,128]{1,0:T(8,128)S(1)}, f32[648,128]{1,0:T(8,128)S(1)}, u32[]{:S(2)}, u32[]{:S(2)}) collective-permute-start(f32[648,128]{1,0:T(8,128)S(1)} %get-tuple-element.47), channel_id=1, source_target_pairs={{0,2},{1,3},{2,0},{3,1},{4,6},{5,7},{6,4},{7,5},{8,10},{9,11},{10,... | collective-permute-start | bytes 995336 | tf_op jit(solution)/shard_map/ppermute | solution.py:522
  129.6 15.7 %collective-permute-start.12 = (f32[648,128]{1,0:T(8,128)S(1)}, f32[648,128]{1,0:T(8,128)S(1)}, u32[]{:S(2)}, u32[]{:S(2)}) collective-permute-start(f32[648,128]{1,0:T(8,128)S(1)} %get-tuple-element.48), channel_id=1, source_target_pairs={{0,3},{1,2},{2,1},{3,0},{4,7},{5,6},{6,5},{7,4},{8,11},{9,10},{10,... | collective-permute-start | bytes 995336 | tf_op jit(solution)/shard_map/ppermute | solution.py:522
  148.4 23.2 %collective-permute-start.13 = (f32[3,256,128]{2,1,0:T(8,128)S(1)}, f32[3,256,128]{2,1,0:T(8,128)S(1)}, u32[]{:S(2)}, u32[]{:S(2)}) collective-permute-start(f32[3,256,128]{2,1,0:T(8,128)S(1)} %get-tuple-element.50), channel_id=1, source_target_pairs={{0,4},{4,8},{8,12},{1,5},{5,9},{9,13},{2,6},{6,10},{10,14},{3,7},{... | collective-permute-start | bytes 1179656 | tf_op jit(solution)/shard_map/ppermute | solution.py:533
  150.1 21.6 %collective-permute-start.14 = (f32[3,256,128]{2,1,0:T(8,128)S(1)}, f32[3,256,128]{2,1,0:T(8,128)S(1)}, u32[]{:S(2)}, u32[]{:S(2)}) collective-permute-start(f32[3,256,128]{2,1,0:T(8,128)S(1)} %get-tuple-element.51), channel_id=1, source_target_pairs={{4,0},{8,4},{12,8},{5,1},{9,5},{13,9},{6,2},{10,6},{14,10},{7,3},{... | collective-permute-start | bytes 1179656 | tf_op jit(solution)/shard_map/ppermute | solution.py:534
  151.4 20.3 %collective-permute-start.15 = (f32[256,128]{1,0:T(8,128)S(1)}, f32[256,128]{1,0:T(8,128)S(1)}, u32[]{:S(2)}, u32[]{:S(2)}) collective-permute-start(f32[256,128]{1,0:T(8,128)S(1)} %get-tuple-element.52.refs_4_), channel_id=1, source_target_pairs={{0,8},{4,12},{8,0},{12,4},{1,9},{5,13},{9,1},{13,5},{2,10},{6,14},... | collective-permute-start | bytes 393224 | tf_op jit(solution)/shard_map/ppermute | solution.py:535
  154.1 17.6 %collective-permute-start.16 = (f32[256,128]{1,0:T(8,128)S(1)}, f32[256,128]{1,0:T(8,128)S(1)}, u32[]{:S(2)}, u32[]{:S(2)}) collective-permute-start(f32[256,128]{1,0:T(8,128)S(1)} %get-tuple-element.52.refs_4_), channel_id=1, source_target_pairs={{0,12},{12,0},{1,13},{13,1},{2,14},{14,2},{3,15},{15,3},{16,28},{2... | collective-permute-start | bytes 393224 | tf_op jit(solution)/shard_map/ppermute | solution.py:535
  171.7 34.4 %copy-start.2 = (f32[8192,128]{1,0:T(8,128)S(1)}, f32[8192,128]{1,0:T(8,128)}, u32[]{:S(2)}) copy-start(f32[8192,128]{1,0:T(8,128)} %copy-done) | copy-start | bytes 12582916
  177.1 29.0 %collective-permute-start.17 = (f32[648,128]{1,0:T(8,128)S(1)}, f32[648,128]{1,0:T(8,128)S(1)}, u32[]{:S(2)}, u32[]{:S(2)}) collective-permute-start(f32[648,128]{1,0:T(8,128)S(1)} %get-tuple-element.54), channel_id=1, source_target_pairs={{0,1},{1,0},{2,3},{3,2},{4,5},{5,4},{6,7},{7,6},{8,9},{9,8},{10,11... | collective-permute-start | bytes 995336 | tf_op jit(solution)/shard_map/ppermute | solution.py:522
  177.2 28.9 %collective-permute-start.18 = (f32[648,128]{1,0:T(8,128)S(1)}, f32[648,128]{1,0:T(8,128)S(1)}, u32[]{:S(2)}, u32[]{:S(2)}) collective-permute-start(f32[648,128]{1,0:T(8,128)S(1)} %get-tuple-element.55), channel_id=1, source_target_pairs={{0,2},{1,3},{2,0},{3,1},{4,6},{5,7},{6,4},{7,5},{8,10},{9,11},{10,... | collective-permute-start | bytes 995336 | tf_op jit(solution)/shard_map/ppermute | solution.py:522
  177.5 28.6 %collective-permute-start.19 = (f32[648,128]{1,0:T(8,128)S(1)}, f32[648,128]{1,0:T(8,128)S(1)}, u32[]{:S(2)}, u32[]{:S(2)}) collective-permute-start(f32[648,128]{1,0:T(8,128)S(1)} %get-tuple-element.56), channel_id=1, source_target_pairs={{0,3},{1,2},{2,1},{3,0},{4,7},{5,6},{6,5},{7,4},{8,11},{9,10},{10,... | collective-permute-start | bytes 995336 | tf_op jit(solution)/shard_map/ppermute | solution.py:522

commit v2 on v1

v2 whole, which is shorter than its diff:
```python
import functools
import math

import jax
import jax.numpy as jnp
import numpy as np
from jax import lax
from jax.experimental import pallas as pl
from jax.experimental.pallas import tpu as pltpu
from jax.sharding import PartitionSpec as P

GRID = 256
REGION = 128
BLOCK = 128
HALF = 64
KERNEL_GAIN = 4.0
SCREEN = 1.0 / 1024.0
LN2 = math.log(2.0)
Y_AXES = ("narrow", "pair")
ALL_AXES = ("wide", "narrow", "pair")
F32 = jnp.float32
BF16 = jnp.bfloat16
VMEM_LIMIT = 24 * 1024 * 1024
GROUP = 32
CHAINS = 4


def cas(angles):
    return np.cos(angles) + np.sin(angles)


def up_to(count, multiple):
    return -(-count // multiple) * multiple


def low_lanes(rows):
    return lax.broadcasted_iota(jnp.int32, (rows, 2 * HALF), 1) < HALF


def swap(values):
    return pltpu.roll(values, HALF, 1)


def split(values):
    high = values.astype(BF16)
    return high, (values - high.astype(F32)).astype(BF16)


def dot(left, right):
    return jnp.dot(left, right, preferred_element_type=F32)


def dot_three(left, right):
    return dot(left[0], right[0]) + (dot(left[0], right[1]) + dot(left[1], right[0]))


def params():
    return pltpu.CompilerParams(vmem_limit_bytes=VMEM_LIMIT)


def whole_vmem():
    return pl.BlockSpec(memory_space=pltpu.VMEM)


def in_smem():
    return pl.BlockSpec(memory_space=pltpu.SMEM)


def cost(flops, moved):
    return pl.CostEstimate(flops=flops, bytes_accessed=moved, transcendentals=0)


def full_scale(exponent, fraction):
    return fraction * jnp.exp(exponent * LN2) * (1.0 / 1024.0)


def fit_scale(largest):
    largest = jnp.maximum(largest, 1e-30)
    exponent = jnp.floor(jnp.log(largest) * (1.0 / LN2))
    fraction = jnp.ceil(largest * jnp.exp(-exponent * LN2) * 1024.0) + 1.0
    return exponent, fraction


def to_short(values):
    return values.astype(jnp.int32).astype(jnp.int16)


def from_short(values):
    return values.astype(jnp.int32).astype(F32)


def quantize(values, exponent, fraction):
    return to_short(jnp.round(values * (32767.0 / full_scale(exponent, fraction))))


def unit(exponent, fraction):
    return full_scale(exponent, fraction) * (1.0 / 32767.0)


def encode_rounded(values):
    rounded = values.astype(BF16).astype(F32)
    size = jnp.maximum(jnp.abs(rounded), 1e-30)
    exponent = jnp.floor(jnp.log(size) * (1.0 / LN2))
    return jnp.round(rounded * jnp.exp((10.0 - exponent) * LN2)), exponent


def decode_rounded(mantissa, exponent):
    return (mantissa * jnp.exp((exponent - 10.0) * LN2)).astype(BF16).astype(F32)


def send_piece(out, head, values):
    exponent, fraction = fit_scale(jnp.max(jnp.abs(values), axis=0, keepdims=True))
    head[0:1, :] = exponent
    head[1:2, :] = fraction
    top = head.shape[0]
    out[:top, :] = to_short(head[...])
    out[top:, :] = quantize(values, exponent, fraction)


def y_position():
    return lax.axis_index("narrow") * lax.axis_size("pair") + lax.axis_index("pair")


def halves(table):
    high = table.astype(jnp.bfloat16)
    return high, (table - high.astype(np.float64)).astype(jnp.bfloat16)


def tables(y_count, span_y):
    depth = GRID // y_count
    reach = span_y + 4
    waves = np.arange(GRID)
    step = 2.0 * np.pi / GRID
    z_table = cas(step * np.outer(np.arange(REGION), waves))
    z_forward = np.zeros((y_count, 2 * REGION, 2 * HALF))
    z_inverse = np.zeros((y_count, 2 * HALF, 2 * REGION))
    symbols = 4.0 * np.sin(np.pi * waves / GRID) ** 2
    shift = np.full((y_count, GRID, 2 * HALF), 1.0)
    y_forward = np.zeros((GRID, y_count, up_to(reach, 8)))
    y_inverse = np.zeros((y_count, up_to(reach, 16), GRID))
    for block in range(y_count):
        mine = z_table[:, block * depth : (block + 1) * depth]
        for half in range(2):
            rows = slice(half * REGION, (half + 1) * REGION)
            lanes = slice(half * HALF, half * HALF + depth)
            z_forward[block, rows, lanes] = mine
            z_inverse[block, lanes, rows] = mine.T / GRID
            shift[block, :, lanes] = (
                SCREEN + symbols[:, None] + symbols[None, block * depth : (block + 1) * depth]
            )
        cells = block * span_y - 2 + np.arange(reach)
        y_table = cas(step * np.outer(waves, cells))
        y_forward[:, block, :reach] = y_table
        y_inverse[block, :reach] = y_table.T / GRID
    y_forward = halves(y_forward.reshape(GRID, -1))
    y_forward = np.concatenate([y_forward[0], y_forward[0], y_forward[1]], axis=1)
    root = np.sqrt(shift * (shift + 4.0))
    decay = 2.0 / (2.0 + shift + root)
    log_decay = np.log(decay)
    ring = 1.0 / (1.0 - np.exp(GRID * log_decay))
    gain = KERNEL_GAIN / root
    modes = np.stack([decay, log_decay, ring, gain], axis=1).astype(np.float32)
    return (
        halves(z_forward),
        halves(z_inverse),
        y_forward,
        halves(y_inverse.reshape(-1, GRID)),
        modes,
    )


def weave_kernel(flag_ref, sample_ref, dipole_ref, source_out, sample_out):
    charged = flag_ref[...] == 1
    rows = []
    for depth in range(4):
        sample = sample_ref[pl.ds(depth, 16, stride=4), :]
        dipole = dipole_ref[pl.ds(depth, 16, stride=4), :]
        rows.append(jnp.concatenate([jnp.where(charged, -sample, dipole), sample], axis=0))
    weights = jnp.concatenate(rows, axis=1)
    first, rest = split(weights)
    second, third = split(weights - first.astype(F32))
    place = lax.broadcasted_iota(jnp.int32, (4 * BLOCK, 4 * BLOCK), 0)
    lane = lax.broadcasted_iota(jnp.int32, (4 * BLOCK, 4 * BLOCK), 1)
    wanted = 4 * (place % BLOCK) + place // BLOCK
    weave = jnp.where(lane == wanted, 1.0, 0.0).astype(BF16)
    woven = dot(first, weave) + (dot(second, weave) + dot(third, weave))
    for part in range(4):
        source_out[part] = woven[:16, part * BLOCK : (part + 1) * BLOCK]
        sample_out[part] = woven[16:, part * BLOCK : (part + 1) * BLOCK]


def weave(flag, sample, dipole):
    count = sample.shape[1]
    shape = jax.ShapeDtypeStruct((count // GROUP, 16, BLOCK), F32)
    columns = lambda rows: pl.BlockSpec((rows, BLOCK), lambda i: (0, i))
    out_block = pl.BlockSpec((BLOCK // GROUP, 16, BLOCK), lambda i: (i, 0, 0))
    return pl.pallas_call(
        weave_kernel,
        grid=(count // BLOCK,),
        in_specs=[columns(1), columns(64), columns(64)],
        out_specs=[out_block] * 2,
        out_shape=[shape, shape],
        compiler_params=params(),
        name="weave",
    )(flag.reshape(1, -1), sample, dipole)


def placed_weights(coeff_ref, panel, depth):
    held = coeff_ref[panel // GROUP]
    return pltpu.roll(held, (depth - (panel % GROUP) * 4) & (REGION - 1), 1)


def spread_kernel(reach, pieces, *refs):
    vector_ref, row_ref, depth_ref, rounded_ref, coeff_ref, high_ref, low_ref = refs[:7]
    outs = refs[7 : 7 + pieces]
    head = refs[7 + pieces]
    grids = refs[8 + pieces :]
    for grid in grids:
        grid[...] = jnp.zeros_like(grid)
    lanes = lax.broadcasted_iota(jnp.int32, (4, REGION), 1)
    chains = len(grids)

    def body(group, carry):
        for chain in range(chains):
            panel = group * chains + chain
            row = row_ref[panel]
            depth = depth_ref[panel]
            line = placed_weights(coeff_ref, panel, depth)
            offset = lanes - depth
            value = jnp.where((offset >= 0) & (offset < 4), vector_ref[panel], 0.0)
            places = [pl.ds(row + a * reach, 4) for a in range(4)]
            held = [grids[chain][place, :] for place in places]
            added = [line[4 * a : 4 * a + 4] * value for a in range(4)]
            for a in range(4):
                grids[chain][places[a], :] = held[a] + added[a]
        return carry

    lax.fori_loop(0, vector_ref.shape[0] // chains, body, 0, unroll=2)

    total = grids[0][...]
    for grid in grids[1:]:
        total = total + grid[...]
    half = total.shape[0] // 2
    both = jnp.concatenate([total[:half], total[half:]], axis=1)
    extra = outs[0].shape[0] - head.shape[0] - half
    if extra:
        both = jnp.concatenate([both, jnp.zeros((extra, 2 * REGION), F32)], axis=0)
    both = split(both)
    blocks = rounded_ref.shape[0]
    mantissa, exponent = encode_rounded(rounded_ref[...])
    head[...] = jnp.zeros_like(head)
    head[2 : 2 + blocks, :] = mantissa
    head[2 + blocks : 2 + 2 * blocks, :] = exponent
    mine = y_position()
    for piece in range(0, pieces, 2):
        pick = lambda ref: jnp.concatenate([ref[mine ^ piece], ref[mine ^ (piece + 1)]], axis=1)
        result = dot_three(both, (pick(high_ref), pick(low_ref)))
        send_piece(outs[piece], head, result[:, : 2 * HALF])
        send_piece(outs[piece + 1], head, result[:, 2 * HALF :])


def spread(vector, rows, depths, coeff, table, reach_x, reach_y):
    pieces = table[0].shape[0]
    line_count = reach_x * reach_y
    half = line_count // 2
    blocks = vector.shape[0] // BLOCK
    top = up_to(2 + 2 * blocks, 16)
    lanes = 2 * HALF
    return pl.pallas_call(
        functools.partial(spread_kernel, reach_y, pieces),
        in_specs=[in_smem()] * 3 + [whole_vmem()] * 4,
        out_specs=[whole_vmem()] * pieces,
        out_shape=[jax.ShapeDtypeStruct((top + up_to(half, 16), lanes), jnp.int16)] * pieces,
        scratch_shapes=[pltpu.VMEM((top, lanes), F32)]
        + [pltpu.VMEM((line_count, REGION), F32)] * CHAINS,
        compiler_params=params(),
        cost_estimate=cost(2 * half * 256 * 512, 4 * 16 * vector.shape[0] * REGION),
        name="spread",
    )(vector, rows, depths, vector.reshape(blocks, BLOCK), coeff, *table)


def forward_kernel(reach_x, reach_y, blocks, pieces, *refs):
    parts = refs[:pieces]
    table_ref, modes_ref = refs[pieces : pieces + 2]
    spectrum, right_out, left_out, own_out, peers_out = refs[pieces + 2 : pieces + 7]
    opened, stacked, slabs, head = refs[pieces + 7 :]
    half = reach_x // 2
    pitch = up_to(reach_y, 8)
    tall = pieces * pitch
    top = parts[0].shape[0] - opened.shape[0]
    mine = y_position()
    if pitch > reach_y:
        stacked[...] = jnp.zeros_like(stacked)
    head[...] = jnp.zeros_like(head)
    for piece in range(pieces):
        first = from_short(parts[piece][:top, :])
        mantissa, exponent = first[2 : 2 + blocks], first[2 + blocks : 2 + 2 * blocks]
        peers_out[piece * blocks : (piece + 1) * blocks, :] = decode_rounded(mantissa, exponent)
        at = 6 + 2 * piece * blocks
        head[at : at + blocks, :] = mantissa
        head[at + blocks : at + 2 * blocks, :] = exponent
        opened[...] = from_short(parts[piece][top:, :]) * unit(first[0:1], first[1:2])
        place = (mine ^ piece) * pitch
        for i in range(half):
            stacked[pl.ds(pl.multiple_of(i * tall + place, 8), reach_y), :] = opened[
                i * reach_y : (i + 1) * reach_y, :
            ]
    table = table_ref[...]

    def tripled(values):
        high, low = split(values)
        return jnp.concatenate([high, low, high], axis=0)

    for i in range(0, half, 2):
        if i + 1 < half:
            pair = jnp.concatenate(
                [stacked[i * tall : (i + 1) * tall, :], stacked[(i + 1) * tall : (i + 2) * tall, :]],
                axis=1,
            )
            both = dot(table, tripled(pair))
            spectrum[i] = both[:, : 2 * HALF]
            spectrum[i + 1] = both[:, 2 * HALF :]
        else:
            spectrum[i] = dot(table, tripled(stacked[i * tall : (i + 1) * tall, :]))

    chunk = 32

    def body(index, largest):
        rows = pl.ds(pl.multiple_of(index * chunk, chunk), chunk)
        low = low_lanes(chunk)
        decay = modes_ref[0, rows, :]
        log_decay = modes_ref[1, rows, :]
        across_half = jnp.exp(half * log_decay)
        across_cut = jnp.exp((half - 4) * log_decay)
        layers = [spectrum[i, rows, :] for i in range(half)]
        run = layers[0]
        cut_right = run
        for i in range(1, half):
            run = decay * run + layers[i]
            if i == half - 5:
                cut_right = run
        right = run
        run = layers[half - 1]
        cut_left = run
        for i in range(half - 2, -1, -1):
            run = decay * run + layers[i]
            if i == 4:
                cut_left = run
        left = run
        swapped_right, swapped_left = swap(right), swap(left)
        own = jnp.where(low, left + across_half * swapped_left, right + across_half * swapped_right)
        made = [
            jnp.where(low, swap(layers[half - 4]), layers[half - 3]),
            jnp.where(low, swap(layers[half - 2]), layers[half - 1]),
            jnp.where(low, own, cut_right + across_cut * swapped_right),
            jnp.where(low, layers[0], swap(layers[1])),
            jnp.where(low, layers[2], swap(layers[3])),
            jnp.where(low, cut_left + across_cut * swapped_left, own),
            own,
        ]
        for slab, values in enumerate(made):
            slabs[slab, rows, :] = values
        return tuple(
            jnp.maximum(old, jnp.max(jnp.abs(values).reshape(chunk // 8, 8, 2 * HALF), axis=0))
            for old, values in zip(largest, made)
        )

    zero = jnp.zeros((8, 2 * HALF), F32)
    largest = lax.fori_loop(0, GRID // chunk, body, (zero,) * 7)
    scales = [fit_scale(jnp.max(value, axis=0, keepdims=True)) for value in largest]
    head_rows = head.shape[0]
    for out, first in ((right_out, 0), (left_out, 3)):
        for slab in range(3):
            exponent, fraction = scales[first + slab]
            head[2 * slab : 2 * slab + 1, :] = exponent
            head[2 * slab + 1 : 2 * slab + 2, :] = fraction
            at = head_rows + slab * GRID
            out[at : at + GRID, :] = quantize(slabs[first + slab], exponent, fraction)
        out[:head_rows, :] = to_short(head[...])
    exponent, fraction = scales[6]
    head[0:1, :] = exponent
    head[1:2, :] = fraction
    own_out[:16, :] = to_short(head[:16, :])
    own_out[16:, :] = quantize(slabs[6], exponent, fraction)


def forward(parts, table, modes, reach_x, reach_y, blocks):
    pieces = len(parts)
    half = reach_x // 2
    lanes = 2 * HALF
    head = up_to(6 + 2 * pieces * blocks, 16)
    body = up_to(half * reach_y, 16)
    short = lambda rows: jax.ShapeDtypeStruct((rows, lanes), jnp.int16)
    return pl.pallas_call(
        functools.partial(forward_kernel, reach_x, reach_y, blocks, pieces),
        in_specs=[whole_vmem()] * (pieces + 2),
        out_specs=[whole_vmem()] * 5,
        out_shape=[
            jax.ShapeDtypeStruct((half, GRID, lanes), F32),
            short(head + 3 * GRID),
            short(head + 3 * GRID),
            short(16 + GRID),
            jax.ShapeDtypeStruct((pieces * blocks, BLOCK), F32),
        ],
        scratch_shapes=[
            pltpu.VMEM((body, lanes), F32),
            pltpu.VMEM((half * pieces * up_to(reach_y, 8), lanes), F32),
            pltpu.VMEM((7, GRID, lanes), F32),
            pltpu.VMEM((head, lanes), F32),
        ],
        compiler_params=params(),
        cost_estimate=cost(2 * half * 256 * 256 * 128, 4 * half * GRID * lanes * 2),
        name="forward",
    )(*parts, table, modes)


def inverse_kernel(reach_x, reach_y, pieces, fars, *refs):
    spectrum, from_left, from_right, own_ref = refs[:4]
    far_refs = refs[4 : 4 + fars]
    high_ref, low_ref, modes_ref = refs[4 + fars : 7 + fars]
    outs = refs[7 + fars : 7 + fars + pieces]
    field, blocks_out, ready, head = refs[7 + fars + pieces :]
    half = reach_x // 2
    span = reach_x - 4
    chunk = 16
    head_rows = from_left.shape[0] - 3 * GRID
    x_count = lax.axis_size("wide")
    x_index = lax.axis_index("wide")

    left_head = from_short(from_left[:16, :])
    right_head = from_short(from_right[:16, :])
    left_units = [unit(left_head[2 * s : 2 * s + 1], left_head[2 * s + 1 : 2 * s + 2]) for s in range(3)]
    right_units = [
        unit(right_head[2 * s : 2 * s + 1], right_head[2 * s + 1 : 2 * s + 2]) for s in range(3)
    ]
    far_units = []
    own_head = from_short(own_ref[:16, :])
    own_unit = unit(own_head[0:1], own_head[1:2])
    for far in far_refs:
        first = from_short(far[:16, :])
        far_units.append(unit(first[0:1], first[1:2]))
    powers = []
    for far, shift in enumerate(list(range(2, x_count - 1)) + [x_count - 1][: int(x_count > 2)]):
        if shift < x_count - 1:
            behind = jnp.where(x_index >= shift, shift, shift - x_count)
        else:
            behind = jnp.where(x_index == 0, -shift, jnp.where(x_index == shift, shift, 0))
        both = []
        for distance in (-behind, behind):
            ahead = span * distance - reach_x
            both.append(jnp.where(distance >= 2, ahead, ahead + GRID).astype(F32))
        powers.append(both)

    def body(index, carry):
        first = pl.multiple_of(index * chunk, chunk)
        rows = pl.ds(first, chunk)
        low = low_lanes(chunk)
        decay = modes_ref[0, rows, :]
        log_decay = modes_ref[1, rows, :]
        ring = modes_ref[2, rows, :]
        gain = modes_ref[3, rows, :]
        across_half = jnp.exp(half * log_decay)
        around = jnp.exp((GRID - 4) * log_decay)
        beside = jnp.exp((GRID - reach_x - span) * log_decay)
        layers = [spectrum[i, rows, :] for i in range(half)]

        def slab(ref, which, units):
            at = pl.ds(pl.multiple_of(head_rows + which * GRID + index * chunk, chunk), chunk)
            return from_short(ref[at, :]) * units[which]

        def moment(ref, scale):
            at = pl.ds(pl.multiple_of(16 + index * chunk, chunk), chunk)
            return from_short(ref[at, :]) * scale

        head_layers = [slab(from_left, 0, left_units), slab(from_left, 1, left_units)]
        tail_layers = [slab(from_right, 0, right_units), slab(from_right, 1, right_units)]
        zero = jnp.zeros_like(decay)
        from_head = [head_layers[0], swap(head_layers[0]), head_layers[1], swap(head_layers[1])]
        from_tail = [swap(tail_layers[0]), tail_layers[0], swap(tail_layers[1]), tail_layers[1]]
        head_sum = from_head[0]
        for i in range(1, 4):
            head_sum = decay * head_sum + from_head[i]
        tail_sum = from_tail[3]
        for i in range(2, -1, -1):
            tail_sum = decay * tail_sum + from_tail[i]
        for i in range(4):
            layers[i] = layers[i] + jnp.where(low, from_head[i], zero)
        for i in range(4):
            place = half - 4 + i
            layers[place] = layers[place] + jnp.where(low, zero, from_tail[i])
        total = moment(own_ref, own_unit) * jnp.exp((GRID - reach_x) * log_decay)
        one = jnp.ones_like(decay)
        total = total + slab(from_left, 2, left_units) * jnp.where(low, beside, one)
        total = total + slab(from_right, 2, right_units) * jnp.where(low, one, beside)
        for far in range(fars):
            power = jnp.where(low, powers[far][0], powers[far][1])
            total = total + moment(far_refs[far], far_units[far]) * jnp.exp(power * log_decay)
        entering = (swap(total) + around * jnp.where(low, head_sum, tail_sum)) * ring
        run = layers[0]
        for i in range(1, half):
            run = decay * run + layers[i]
        right_start = jnp.where(low, entering, swap(across_half * entering + run))
        run = layers[half - 1]
        for i in range(half - 2, -1, -1):
            run = decay * run + layers[i]
        left_start = jnp.where(low, swap(across_half * entering + run), entering)
        run = right_start
        forward_runs = []
        for i in range(half):
            run = decay * run + layers[i]
            forward_runs.append(run)
        run = left_start
        for i in range(half - 1, -1, -1):
            ahead = decay * run
            field[i, rows, :] = gain * (forward_runs[i] + ahead)
            run = ahead + layers[i]
        return carry

    lax.fori_loop(0, GRID // chunk, body, 0)
    table = (high_ref[...], low_ref[...])
    pitch = up_to(reach_y, 16)
    for i in range(0, half, 2):
        if i + 1 < half:
            pair = dot_three(table, split(jnp.concatenate([field[i], field[i + 1]], axis=1)))
            blocks_out[i] = pair[:, : 2 * HALF]
            blocks_out[i + 1] = pair[:, 2 * HALF :]
        else:
            blocks_out[i] = dot_three(table, split(field[i]))
    mine = y_position()
    if ready.shape[0] > half * reach_y:
        ready[half * reach_y :, :] = jnp.zeros_like(ready[half * reach_y :, :])
    head[...] = jnp.zeros_like(head)
    for piece in range(pieces):
        place = pl.ds(pl.multiple_of((mine ^ piece) * pitch, 16), reach_y)
        for i in range(half):
            ready[i * reach_y : (i + 1) * reach_y, :] = blocks_out[i, place, :]
        send_piece(outs[piece], head, ready[...])


def inverse(spectrum, from_left, from_right, own, fars, table, modes, reach_x, reach_y, pieces):
    half = reach_x // 2
    lanes = 2 * HALF
    body = up_to(half * reach_y, 16)
    return pl.pallas_call(
        functools.partial(inverse_kernel, reach_x, reach_y, pieces, len(fars)),
        in_specs=[whole_vmem()] * (7 + len(fars)),
        out_specs=[whole_vmem()] * pieces,
        out_shape=[jax.ShapeDtypeStruct((16 + body, lanes), jnp.int16)] * pieces,
        scratch_shapes=[
            pltpu.VMEM((half, GRID, lanes), F32),
            pltpu.VMEM((half, pieces * up_to(reach_y, 16), lanes), F32),
            pltpu.VMEM((body, lanes), F32),
            pltpu.VMEM((16, lanes), F32),
        ],
        compiler_params=params(),
        cost_estimate=cost(2 * half * 256 * 256 * 128, 4 * half * GRID * lanes * 2),
        name="inverse",
    )(spectrum, from_left, from_right, own, *fars, *table, modes)


def sample_kernel(reach, half_rows, pieces, row_ref, depth_ref, *refs):
    parts = refs[:pieces]
    high_ref, low_ref, coeff_ref, base_ref, near_ref, out_ref, field, sums = refs[pieces:]
    mine = y_position()
    opened = []
    for part in parts:
        first = from_short(part[:16, :])
        opened.append(from_short(part[16:, :]) * unit(first[0:1], first[1:2]))
    values = split(jnp.concatenate(opened, axis=1))
    pick = lambda ref: jnp.concatenate([ref[mine ^ piece] for piece in range(pieces)], axis=0)
    both = dot_three(values, (pick(high_ref), pick(low_ref)))
    field[:half_rows, :] = both[:half_rows, :REGION]
    field[half_rows:, :] = both[:half_rows, REGION:]
    lanes = lax.broadcasted_iota(jnp.int32, (1, REGION), 1)

    def body(panel, carry):
        row = row_ref[panel]
        depth = depth_ref[panel]
        line = placed_weights(coeff_ref, panel, depth)
        total = field[pl.ds(row, 4), :] * line[:4]
        for a in range(1, 4):
            total = total + field[pl.ds(row + a * reach, 4), :] * line[4 * a : 4 * a + 4]
        offset = lanes - depth
        total = jnp.sum(total, axis=0, keepdims=True)
        sums[pl.ds(panel, 1), :] = jnp.where((offset >= 0) & (offset < 4), total, 0.0)
        return carry

    count = row_ref.shape[0]
    lax.fori_loop(0, count, body, 0, unroll=8)
    sampled = lax.dot_general(
        jnp.ones((8, REGION), F32),
        sums[...],
        (((1,), (1,)), ((), ())),
        precision=lax.Precision.HIGHEST,
        preferred_element_type=F32,
    )
    for block in range(count // BLOCK):
        lane = slice(block * BLOCK, (block + 1) * BLOCK)
        out_ref[block : block + 1, :] = (
            base_ref[block : block + 1, :] + sampled[:1, lane] + near_ref[block : block + 1, :]
        )


def sample(rows, depths, parts, table, coeff, base, near, reach_x, reach_y):
    count = rows.shape[0]
    pieces = len(parts)
    half_rows = reach_x * reach_y // 2
    return pl.pallas_call(
        functools.partial(sample_kernel, reach_y, half_rows, pieces),
        in_specs=[in_smem()] * 2 + [whole_vmem()] * (pieces + 5),
        out_specs=whole_vmem(),
        out_shape=jax.ShapeDtypeStruct((count // BLOCK, BLOCK), F32),
        scratch_shapes=[
            pltpu.VMEM((2 * half_rows, REGION), F32),
            pltpu.VMEM((count, REGION), F32),
        ],
        compiler_params=params(),
        cost_estimate=cost(2 * half_rows * 256 * 512, 4 * 16 * count * REGION),
        name="sample",
    )(rows, depths, *parts, *table, coeff, base, near)


def near_kernel(slots, blocks, place_ref, target_ref, *refs):
    left_ref, right_ref, peers_ref, tile_ref, out_ref, held = refs
    count = peers_ref.shape[0]
    held[count : 2 * count, :] = peers_ref[...]
    for first, ref in ((0, left_ref), (2 * count, right_ref)):
        top = from_short(ref[...])
        for piece in range(count // blocks):
            at = 6 + 2 * piece * blocks
            held[first + piece * blocks : first + (piece + 1) * blocks, :] = decode_rounded(
                top[at : at + blocks], top[at + blocks : at + 2 * blocks]
            )
    out_ref[...] = jnp.zeros_like(out_ref)
    for slot in range(slots):
        picked = held[pl.ds(place_ref[slot], 1), :]
        picked = jnp.broadcast_to(picked, (16, BLOCK)).astype(BF16)
        product = lax.dot_general(
            picked,
            tile_ref[slot],
            (((1,), (1,)), ((), ())),
            preferred_element_type=F32,
        )
        target = pl.ds(target_ref[slot], 1)
        out_ref[target, :] = out_ref[target, :] + product[:1]


def near_field(places, targets, from_left, from_right, peers, tiles, blocks, out_rows):
    slots = tiles.shape[0]
    head = from_left.shape[0] - 3 * GRID
    constant = lambda shape: pl.BlockSpec(shape, lambda i: (0,) * len(shape))
    return pl.pallas_call(
        functools.partial(near_kernel, slots, blocks),
        grid=(1,),
        in_specs=[
            in_smem(),
            in_smem(),
            constant((head, BLOCK)),
            constant((head, BLOCK)),
            constant(peers.shape),
            constant(tiles.shape),
        ],
        out_specs=constant((out_rows, BLOCK)),
        out_shape=jax.ShapeDtypeStruct((out_rows, BLOCK), F32),
        scratch_shapes=[pltpu.VMEM((3 * peers.shape[0], BLOCK), F32)],
        compiler_params=params(),
        cost_estimate=cost(2 * slots * 16 * BLOCK * BLOCK, 2 * slots * BLOCK * BLOCK),
        name="near_field",
    )(places, targets, from_left, from_right, peers, tiles)


def shards(
    density,
    surface_flag,
    stencil_base,
    sample_weights,
    dipole_weights,
    near_target,
    near_source,
    near_tiles,
):
    x_count = lax.axis_size("wide")
    y_count = lax.axis_size(Y_AXES)
    x_index = lax.axis_index("wide")
    y_index = lax.axis_index(Y_AXES)
    span_x = REGION // x_count
    span_y = REGION // y_count
    reach_x = span_x + 4
    reach_y = span_y + 4
    count = density.shape[0]
    blocks = count // BLOCK

    z_forward, z_inverse, y_forward, y_inverse, modes = tables(y_count, span_y)
    modes = lax.dynamic_index_in_dim(jnp.asarray(modes), y_index, 0, keepdims=False)

    rows = (stencil_base[0] - (x_index * span_x - 2)) * reach_y + (
        stencil_base[1] - (y_index * span_y - 2)
    )
    depths = stencil_base[2]
    source_coeff, sample_coeff = weave(surface_flag, sample_weights, dipole_weights)
    own_share = jnp.where(surface_flag == 1, 0.0, 0.5).astype(F32)

    neighbour = near_source // blocks
    flip = (y_index + neighbour % 3 - 1) ^ y_index
    places = ((neighbour // 3) * y_count + flip) * blocks + near_source % blocks
    out_rows = up_to(blocks + 1, 8)
    live = near_target >= 0
    places = jnp.where(live, places, 0)
    targets = jnp.where(live, near_target, out_rows - 1)

    far_moves = [
        [(i, (i + shift) % x_count) for i in range(x_count)] for shift in range(2, x_count - 1)
    ]
    if x_count > 2:
        far_moves.append([(0, x_count - 1), (x_count - 1, 0)])
    to_right = [(i, i + 1) for i in range(x_count - 1)]
    to_left = [(i + 1, i) for i in range(x_count - 1)]

    def turn(parts):
        return [
            part
            if flip == 0
            else lax.ppermute(part, Y_AXES, [(i, i ^ flip) for i in range(y_count)])
            for flip, part in enumerate(parts)
        ]

    def apply_operator(vector):
        parts = turn(spread(vector, rows, depths, source_coeff, z_forward, reach_x, reach_y))
        spectrum, right_going, left_going, own, peers = forward(
            parts, y_forward, modes, reach_x, reach_y, blocks
        )
        from_left = lax.ppermute(right_going, "wide", to_right)
        from_right = lax.ppermute(left_going, "wide", to_left)
        fars = [lax.ppermute(own, "wide", pairs) for pairs in far_moves]
        near_part = near_field(
            places, targets, from_left, from_right, peers, near_tiles, blocks, out_rows
        )
        parts = turn(
            inverse(
                spectrum,
                from_left,
                from_right,
                own,
                fars,
                y_inverse,
                modes,
                reach_x,
                reach_y,
                y_count,
            )
        )
        base = (own_share * vector).reshape(blocks, BLOCK)
        return sample(
            rows, depths, parts, z_inverse, sample_coeff, base, near_part, reach_x, reach_y
        ).reshape(-1)

    first_image = apply_operator(density)
    second = apply_operator(first_image)
    return jnp.stack([first_image, second])


def solution(mesh):
    panels = P(("groups",) + ALL_AXES)
    columns = P(None, ("groups",) + ALL_AXES)
    in_specs = (
        panels,
        panels,
        columns,
        columns,
        columns,
        panels,
        panels,
        P(("groups",) + ALL_AXES, None, None),
    )
    return jax.shard_map(
        shards, mesh=mesh, in_specs=in_specs, out_specs=columns, check_vma=False
    )
```

time: 212 us -> 141 us (0.67)
  blocking collectives: 53.3 us -> 0 us
  waiting for transfers between devices: 55.6 us -> 43.1 us
  local copies, waits for them, and re-layouts: 18.3 us -> 7.19 us
  Pallas kernels: 51.2 us -> 58.5 us
    all_gather x2 -> x0, blocking collectives: 53.3 us -> none  [apply_operator(): lax.all_gather(vector.astype(jnp.bfloat16).reshape(blocks_dev, BLOCK), AL...]
    ppermute x4, waiting for transfers between devices: 27.4 us -> 8.5 us  [apply_operator(): fars = [lax.ppermute(own, 'wide', pairs) for pairs in far_moves]]
    pallas_call x9, Pallas kernels: 39.4 us -> 48.6 us  [the longest x2 21.9 us: sample(): pl.pallas_call(functools.partial(sample_kernel, reach_y, half_rows, piece...]
    gather x3 -> x0, local copies, waits for them, and re-layouts: 4.63 us -> none  [the longest x1 2.45 us: shards(): jnp.take(z_inverse, order, axis=0).reshape(y_count * 2 * HALF, 2 * REGION)]
    unnamed x36 -> x38, local copies, waits for them, and re-layouts: 10.4 us -> 6.11 us
    ppermute x2, waiting for transfers between devices: 0.01 us -> 3.71 us  [apply_operator(): from_right = lax.ppermute(left_going, 'wide', to_left)]
    reshape x6 -> x0, local copies, waits for them, and re-layouts: 2.12 us -> none  [the longest x4 1.98 us: panel_lines(): w.reshape(16, 4, count).transpose(1, 0, 2).reshape(64, count)]
  transfers between devices with their start and end apart: 20 -> 20, of which waited for: 6 -> 12; matrix products, arithmetic and copies ran while one was open for 3% -> 1% of each run, Pallas kernels for 1% -> 1%
where the time goes in v2:
time: 141 us
  Pallas kernels  58.5 us (41%)
  waiting for transfers between devices  43.1 us (31%)
  starting transfers between devices  30.1 us (21%)
  local copies, waits for them, and re-layouts  7.19 us (5%)
  other arithmetic  1.49 us (1%)
    ppermute x12, waiting for transfers between devices, turn(): lax.ppermute(part, Y_AXES, [(i, i ^ flip) for i in range(y_count)])  29.3 us
    pallas_call x2, Pallas kernels, sample(): pl.pallas_call(functools.partial(sample_kernel, reach_y, half_rows, piece...  21.9 us
    pallas_call x2, Pallas kernels, spread(): pl.pallas_call(functools.partial(spread_kernel, reach_y, pieces), in_spec...  18 us
    ppermute x4, starting transfers between devices, apply_operator(): fars = [lax.ppermute(own, 'wide', pairs) for pairs in far_moves]  13.1 us
    pallas_call x2, Pallas kernels, inverse(): pl.pallas_call(functools.partial(inverse_kernel, reach_x, reach_y, pieces...  9.96 us
    ppermute x12, starting transfers between devices, turn(): lax.ppermute(part, Y_AXES, [(i, i ^ flip) for i in range(y_count)])  8.95 us
    ppermute x4, waiting for transfers between devices, apply_operator(): fars = [lax.ppermute(own, 'wide', pairs) for pairs in far_moves]  8.5 us
    unnamed x38, local copies, waits for them, and re-layouts  6.11 us
  transfers between devices with their start and end apart: 20, of which 12 were waited for; matrix products, arithmetic and copies ran while one was open for 1% of the time, Pallas kernels for 1%

profile of v2, /device:TPU:0, one launch (start us, length us, event | category | flops | bytes accessed | tf_op | source)
XLA Modules:
  0.0 140.6 jit_solution(17264706993157612967)
XLA Ops:
  0.0 0.8 fusion.7
  0.8 0.0 copy-start.11
  0.8 0.9 copy-done.11
  1.7 0.9 copy-done.12
  2.6 0.7 copy-done.15
  3.3 1.8 %weave.1 = (f32[16,16,128]{2,1,0:T(8,128)S(1)}, f32[16,16,128]{2,1,0:T(8,128)S(1)}) custom-call(s32[1,512]{1,0:T(1,128)S(1)} %bitcast.25, f32[64,512]{1,0:T(8,128)S(1)} %copy-done.11, f32[64,512]{1,0:T(8,128)S(1)} %copy-done.12), custom_call_target="tpu_custom_call" | custom-call | tf_op jit(solution)/shard_map/weave/pallas_call | solution.py:197
  5.1 1.0 copy-done.5
  6.1 0.9 copy-done.7
  7.0 0.7 copy-done.13
  7.7 9.0 %spread.2 = (s16[672,128]{1,0:T(8,128)(2,1)S(1)}, s16[672,128]{1,0:T(8,128)(2,1)S(1)}, s16[672,128]{1,0:T(8,128)(2,1)S(1)}, s16[672,128]{1,0:T(8,128)(2,1)S(1)}) custom-call(f32[512]{0:T(512)S(1)} %copy-done.13, s32[512]{0:T(512)S(1)} %bitcast.18, s32[512]{0:T(512)S(1)} %bitcast.14, f32[4,128]{1,0:T(4,128)S(1)} %bitcast.24, ...), custom_call_target="tpu_custom_call" | custom-call | flops 169869312 | bytes 4194304 | tf_op jit(solution)/shard_map/spread/pallas_call | solution.py:269
  16.7 0.5 collective-permute-start
  17.3 2.6 %collective-permute-start.1 = (s16[672,128]{1,0:T(8,128)(2,1)S(1)}, s16[672,128]{1,0:T(8,128)(2,1)S(1)}, u32[]{:S(2)}, u32[]{:S(2)}) collective-permute-start(s16[672,128]{1,0:T(8,128)(2,1)S(1)} %get-tuple-element.36), channel_id=1, source_target_pairs={{0,2},{1,3},{2,0},{3,1},{4,6},{5,7},{6,4},{7,5},{8,10},{9,11},{10,... | collective-permute-start | bytes 516104 | tf_op jit(solution)/shard_map/ppermute | solution.py:723
  19.8 0.1 collective-permute-start.2
  19.9 1.1 dynamic-slice_bitcast_fusion.refs_5_.refs_8_
  21.0 0.0 collective-permute-done.refs_1_
  21.0 4.1 %collective-permute-done.1.refs_2_ = s16[672,128]{1,0:T(8,128)(2,1)S(1)} collective-permute-done((s16[672,128]{1,0:T(8,128)(2,1)S(1)}, s16[672,128]{1,0:T(8,128)(2,1)S(1)}, u32[]{:S(2)}, u32[]{:S(2)}) %collective-permute-start.1) | collective-permute-done | bytes 172064 | tf_op jit(solution)/shard_map/ppermute | solution.py:723
  25.0 3.2 %collective-permute-done.2.refs_3_ = s16[672,128]{1,0:T(8,128)(2,1)S(1)} collective-permute-done((s16[672,128]{1,0:T(8,128)(2,1)S(1)}, s16[672,128]{1,0:T(8,128)(2,1)S(1)}, u32[]{:S(2)}, u32[]{:S(2)}) %collective-permute-start.2) | collective-permute-done | bytes 172064 | tf_op jit(solution)/shard_map/ppermute | solution.py:723
  28.2 0.9 copy-done.3
  29.2 2.3 %forward.2 = (f32[18,256,128]{2,1,0:T(8,128)S(1)}, s16[816,128]{1,0:T(8,128)(2,1)S(1)}, s16[816,128]{1,0:T(8,128)(2,1)S(1)}, s16[272,128]{1,0:T(8,128)(2,1)S(1)}, f32[16,128]{1,0:T(8,128)S(1)}) custom-call(s16[672,128]{1,0:T(8,128)(2,1)S(1)} %get-tuple-element.34.refs_0_, s16[672,128]{1,0:T(8,128)(2,1)S(1)} %collective-permute-done.refs_1_, ...), custom_call_target="tpu_custom_call" | custom-call | flops 301989888 | bytes 4718592 | tf_op jit(solution)/shard_map/forward/pallas_call | solution.py:394
  31.5 2.7 %collective-permute-start.5 = (s16[272,128]{1,0:T(8,128)(2,1)S(1)}, s16[272,128]{1,0:T(8,128)(2,1)S(1)}, u32[]{:S(2)}, u32[]{:S(2)}) collective-permute-start(s16[272,128]{1,0:T(8,128)(2,1)S(1)} %get-tuple-element.41.refs_3_), channel_id=1, source_target_pairs={{0,8},{4,12},{8,0},{12,4},{1,9},{5,13},{9,1},{13,5},{2,10},{6,14},... | collective-permute-start | bytes 208904 | tf_op jit(solution)/shard_map/ppermute | solution.py:734
  34.3 3.2 %collective-permute-start.6 = (s16[272,128]{1,0:T(8,128)(2,1)S(1)}, s16[272,128]{1,0:T(8,128)(2,1)S(1)}, u32[]{:S(2)}, u32[]{:S(2)}) collective-permute-start(s16[272,128]{1,0:T(8,128)(2,1)S(1)} %get-tuple-element.41.refs_3_), channel_id=1, source_target_pairs={{0,12},{12,0},{1,13},{13,1},{2,14},{14,2},{3,15},{15,3},{16,28},{2... | collective-permute-start | bytes 208904 | tf_op jit(solution)/shard_map/ppermute | solution.py:734
  37.5 1.3 collective-permute-start.3
  38.8 1.3 collective-permute-start.4
  40.2 0.0 collective-permute-done.5.refs_4_
  40.2 2.1 %collective-permute-done.6.refs_5_ = s16[272,128]{1,0:T(8,128)(2,1)S(1)} collective-permute-done((s16[272,128]{1,0:T(8,128)(2,1)S(1)}, s16[272,128]{1,0:T(8,128)(2,1)S(1)}, u32[]{:S(2)}, u32[]{:S(2)}) %collective-permute-start.6) | collective-permute-done | bytes 69664 | tf_op jit(solution)/shard_map/ppermute | solution.py:734
  42.3 1.5 %collective-permute-done.3.refs_1_.refs_0_ = s16[816,128]{1,0:T(8,128)(2,1)S(1)} collective-permute-done((s16[816,128]{1,0:T(8,128)(2,1)S(1)}, s16[816,128]{1,0:T(8,128)(2,1)S(1)}, u32[]{:S(2)}, u32[]{:S(2)}) %collective-permute-start.3) | collective-permute-done | bytes 208928 | tf_op jit(solution)/shard_map/ppermute | solution.py:732
  43.8 3.7 %collective-permute-done.4.refs_2_.refs_1_ = s16[816,128]{1,0:T(8,128)(2,1)S(1)} collective-permute-done((s16[816,128]{1,0:T(8,128)(2,1)S(1)}, s16[816,128]{1,0:T(8,128)(2,1)S(1)}, u32[]{:S(2)}, u32[]{:S(2)}) %collective-permute-start.4) | collective-permute-done | bytes 208928 | tf_op jit(solution)/shard_map/ppermute | solution.py:733
  47.5 0.0 copy-start.6
  47.5 0.0 copy-start.8
  47.5 5.0 %inverse.2 = (s16[672,128]{1,0:T(8,128)(2,1)S(1)}, s16[672,128]{1,0:T(8,128)(2,1)S(1)}, s16[672,128]{1,0:T(8,128)(2,1)S(1)}, s16[672,128]{1,0:T(8,128)(2,1)S(1)}) custom-call(f32[18,256,128]{2,1,0:T(8,128)S(1)} %get-tuple-element.38.refs_0_, s16[816,128]{1,0:T(8,128)(2,1)S(1)} %collective-permute-done.3.refs_1_.refs_0_, ...), custom_call_target="tpu_custom_call" | custom-call | flops 301989888 | bytes 4718592 | tf_op jit(solution)/shard_map/inverse/pallas_call | solution.py:544
  52.5 0.0 copy-start.4
  52.5 0.1 collective-permute-start.7
  52.6 1.6 %collective-permute-start.8 = (s16[672,128]{1,0:T(8,128)(2,1)S(1)}, s16[672,128]{1,0:T(8,128)(2,1)S(1)}, u32[]{:S(2)}, u32[]{:S(2)}) collective-permute-start(s16[672,128]{1,0:T(8,128)(2,1)S(1)} %get-tuple-element.44), channel_id=1, source_target_pairs={{0,2},{1,3},{2,0},{3,1},{4,6},{5,7},{6,4},{7,5},{8,10},{9,11},{10,... | collective-permute-start | bytes 516104 | tf_op jit(solution)/shard_map/ppermute | solution.py:723
  54.2 0.3 collective-permute-start.9
  54.5 1.1 near_field.2.refs_8_
  55.6 4.3 %collective-permute-done.8.refs_2_ = s16[672,128]{1,0:T(8,128)(2,1)S(1)} collective-permute-done((s16[672,128]{1,0:T(8,128)(2,1)S(1)}, s16[672,128]{1,0:T(8,128)(2,1)S(1)}, u32[]{:S(2)}, u32[]{:S(2)}) %collective-permute-start.8) | collective-permute-done | bytes 172064 | tf_op jit(solution)/shard_map/ppermute | solution.py:723
  59.9 2.8 %collective-permute-done.9.refs_3_ = s16[672,128]{1,0:T(8,128)(2,1)S(1)} collective-permute-done((s16[672,128]{1,0:T(8,128)(2,1)S(1)}, s16[672,128]{1,0:T(8,128)(2,1)S(1)}, u32[]{:S(2)}, u32[]{:S(2)}) %collective-permute-start.9) | collective-permute-done | bytes 172064 | tf_op jit(solution)/shard_map/ppermute | solution.py:723
  62.6 11.0 %sample.2.refs_3_ = f32[4,128]{1,0:T(4,128)S(1)} custom-call(s32[512]{0:T(512)S(1)} %bitcast.19, s32[512]{0:T(512)S(1)} %bitcast.15, s16[672,128]{1,0:T(8,128)(2,1)S(1)} %get-tuple-element.42.refs_0_, s16[672,128]{1,0:T(8,128)(2,1)S(1)} %collective-permute-done.7.refs_1_, s16[672,128]{1,0:T(8,128)(2,1)S(1)} %collective-permute-done.8.refs_2_, ...), custom_call_target="tpu_custom_call" | custom-call | flops 169869312 | bytes 4194304 | tf_op jit(solution)/shard_map/sample/pallas_call | solution.py:608
  73.6 0.0 copy-done.8
  73.6 9.0 %spread.3 = (s16[672,128]{1,0:T(8,128)(2,1)S(1)}, s16[672,128]{1,0:T(8,128)(2,1)S(1)}, s16[672,128]{1,0:T(8,128)(2,1)S(1)}, s16[672,128]{1,0:T(8,128)(2,1)S(1)}) custom-call(f32[512]{0:T(512)S(1)} %bitcast.22, s32[512]{0:T(512)S(1)} %bitcast.20, s32[512]{0:T(512)S(1)} %bitcast.16, f32[4,128]{1,0:T(4,128)S(1)} %sample.2.refs_3_, ...), custom_call_target="tpu_custom_call" | custom-call | flops 169869312 | bytes 4194304 | tf_op jit(solution)/shard_map/spread/pallas_call | solution.py:269
  82.7 0.3 collective-permute-start.10
  83.0 1.5 %collective-permute-start.11 = (s16[672,128]{1,0:T(8,128)(2,1)S(1)}, s16[672,128]{1,0:T(8,128)(2,1)S(1)}, u32[]{:S(2)}, u32[]{:S(2)}) collective-permute-start(s16[672,128]{1,0:T(8,128)(2,1)S(1)} %get-tuple-element.50), channel_id=1, source_target_pairs={{0,2},{1,3},{2,0},{3,1},{4,6},{5,7},{6,4},{7,5},{8,10},{9,11},{10,... | collective-permute-start | bytes 516104 | tf_op jit(solution)/shard_map/ppermute | solution.py:723
  84.5 0.1 collective-permute-start.12
  84.6 0.0 collective-permute-done.10.refs_1_
  84.6 5.6 %collective-permute-done.11.refs_2_ = s16[672,128]{1,0:T(8,128)(2,1)S(1)} collective-permute-done((s16[672,128]{1,0:T(8,128)(2,1)S(1)}, s16[672,128]{1,0:T(8,128)(2,1)S(1)}, u32[]{:S(2)}, u32[]{:S(2)}) %collective-permute-start.11) | collective-permute-done | bytes 172064 | tf_op jit(solution)/shard_map/ppermute | solution.py:723
  90.2 2.3 %collective-permute-done.12.refs_3_ = s16[672,128]{1,0:T(8,128)(2,1)S(1)} collective-permute-done((s16[672,128]{1,0:T(8,128)(2,1)S(1)}, s16[672,128]{1,0:T(8,128)(2,1)S(1)}, u32[]{:S(2)}, u32[]{:S(2)}) %collective-permute-start.12) | collective-permute-done | bytes 172064 | tf_op jit(solution)/shard_map/ppermute | solution.py:723
  92.5 2.4 %forward.3 = (f32[18,256,128]{2,1,0:T(8,128)S(1)}, s16[816,128]{1,0:T(8,128)(2,1)S(1)}, s16[816,128]{1,0:T(8,128)(2,1)S(1)}, s16[272,128]{1,0:T(8,128)(2,1)S(1)}, f32[16,128]{1,0:T(8,128)S(1)}) custom-call(s16[672,128]{1,0:T(8,128)(2,1)S(1)} %get-tuple-element.48.refs_0_, s16[672,128]{1,0:T(8,128)(2,1)S(1)} %collective-permute-done.10.refs_1_, ...), custom_call_target="tpu_custom_call" | custom-call | flops 301989888 | bytes 4718592 | tf_op jit(solution)/shard_map/forward/pallas_call | solution.py:394
  94.9 4.1 %collective-permute-start.13 = (s16[816,128]{1,0:T(8,128)(2,1)S(1)}, s16[816,128]{1,0:T(8,128)(2,1)S(1)}, u32[]{:S(2)}, u32[]{:S(2)}) collective-permute-start(s16[816,128]{1,0:T(8,128)(2,1)S(1)} %get-tuple-element.53), channel_id=1, source_target_pairs={{0,4},{4,8},{8,12},{1,5},{5,9},{9,13},{2,6},{6,10},{10,14},{3,7},{... | collective-permute-start | bytes 626696 | tf_op jit(solution)/shard_map/ppermute | solution.py:732
  99.0 1.3 collective-permute-start.14
  100.3 3.9 %collective-permute-start.15 = (s16[272,128]{1,0:T(8,128)(2,1)S(1)}, s16[272,128]{1,0:T(8,128)(2,1)S(1)}, u32[]{:S(2)}, u32[]{:S(2)}) collective-permute-start(s16[272,128]{1,0:T(8,128)(2,1)S(1)} %get-tuple-element.55.refs_3_), channel_id=1, source_target_pairs={{0,8},{4,12},{8,0},{12,4},{1,9},{5,13},{9,1},{13,5},{2,10},{6,14},... | collective-permute-start | bytes 208904 | tf_op jit(solution)/shard_map/ppermute | solution.py:734
  104.2 3.3 %collective-permute-start.16 = (s16[272,128]{1,0:T(8,128)(2,1)S(1)}, s16[272,128]{1,0:T(8,128)(2,1)S(1)}, u32[]{:S(2)}, u32[]{:S(2)}) collective-permute-start(s16[272,128]{1,0:T(8,128)(2,1)S(1)} %get-tuple-element.55.refs_3_), channel_id=1, source_target_pairs={{0,12},{12,0},{1,13},{13,1},{2,14},{14,2},{3,15},{15,3},{16,28},{2... | collective-permute-start | bytes 208904 | tf_op jit(solution)/shard_map/ppermute | solution.py:734
  107.5 6.4 %collective-permute-done.15.refs_4_ = s16[272,128]{1,0:T(8,128)(2,1)S(1)} collective-permute-done((s16[272,128]{1,0:T(8,128)(2,1)S(1)}, s16[272,128]{1,0:T(8,128)(2,1)S(1)}, u32[]{:S(2)}, u32[]{:S(2)}) %collective-permute-start.15) | collective-permute-done | bytes 69664 | tf_op jit(solution)/shard_map/ppermute | solution.py:734
  113.9 0.0 collective-permute-done.16.refs_5_
  113.9 0.0 collective-permute-done.13.refs_1_.refs_0_
  113.9 0.0 collective-permute-done.14.refs_2_.refs_1_
  113.9 5.0 %inverse.3 = (s16[672,128]{1,0:T(8,128)(2,1)S(1)}, s16[672,128]{1,0:T(8,128)(2,1)S(1)}, s16[672,128]{1,0:T(8,128)(2,1)S(1)}, s16[672,128]{1,0:T(8,128)(2,1)S(1)}) custom-call(f32[18,256,128]{2,1,0:T(8,128)S(1)} %get-tuple-element.52.refs_0_, s16[816,128]{1,0:T(8,128)(2,1)S(1)} %collective-permute-done.13.refs_1_.refs_0_, ...), custom_call_target="tpu_custom_call" | custom-call | flops 301989888 | bytes 4718592 | tf_op jit(solution)/shard_map/inverse/pallas_call | solution.py:544
  118.9 0.1 collective-permute-start.17
  119.0 1.5 %collective-permute-start.18 = (s16[672,128]{1,0:T(8,128)(2,1)S(1)}, s16[672,128]{1,0:T(8,128)(2,1)S(1)}, u32[]{:S(2)}, u32[]{:S(2)}) collective-permute-start(s16[672,128]{1,0:T(8,128)(2,1)S(1)} %get-tuple-element.58), channel_id=1, source_target_pairs={{0,2},{1,3},{2,0},{3,1},{4,6},{5,7},{6,4},{7,5},{8,10},{9,11},{10,... | collective-permute-start | bytes 516104 | tf_op jit(solution)/shard_map/ppermute | solution.py:723
  120.5 0.3 collective-permute-start.19
  120.8 1.1 near_field.3.refs_8_
  121.9 4.3 %collective-permute-done.18.refs_2_ = s16[672,128]{1,0:T(8,128)(2,1)S(1)} collective-permute-done((s16[672,128]{1,0:T(8,128)(2,1)S(1)}, s16[672,128]{1,0:T(8,128)(2,1)S(1)}, u32[]{:S(2)}, u32[]{:S(2)}) %collective-permute-start.18) | collective-permute-done | bytes 172064 | tf_op jit(solution)/shard_map/ppermute | solution.py:723
  126.2 2.8 %collective-permute-done.19.refs_3_ = s16[672,128]{1,0:T(8,128)(2,1)S(1)} collective-permute-done((s16[672,128]{1,0:T(8,128)(2,1)S(1)}, s16[672,128]{1,0:T(8,128)(2,1)S(1)}, u32[]{:S(2)}, u32[]{:S(2)}) %collective-permute-start.19) | collective-permute-done | bytes 172064 | tf_op jit(solution)/shard_map/ppermute | solution.py:723
  129.0 11.0 %sample.3 = f32[4,128]{1,0:T(4,128)S(1)} custom-call(s32[512]{0:T(512)S(1)} %bitcast.21, s32[512]{0:T(512)S(1)} %bitcast.17, s16[672,128]{1,0:T(8,128)(2,1)S(1)} %get-tuple-element.56.refs_0_, s16[672,128]{1,0:T(8,128)(2,1)S(1)} %collective-permute-done.17.refs_1_, s16[672,128]{1,0:T(8,128)(2,1)S(1)} %collective-permute-done.18.refs_2_, ...), custom_call_target="tpu_custom_call" | custom-call | flops 169869312 | bytes 4194304 | tf_op jit(solution)/shard_map/sample/pallas_call | solution.py:608
  140.0 0.6 pad_maximum_fusion
  (31 shorter events, 0.1 us)
Async XLA Ops:
  0.0 47.5 %copy-start.9 = (bf16[192,256]{1,0:T(8,128)(2,1)S(1)}, bf16[192,256]{1,0:T(8,128)(2,1)}, u32[]{:S(2)}) copy-start(bf16[192,256]{1,0:T(8,128)(2,1)} %constant.94.clone.refs_6_) | copy-start | bytes 294916
  0.0 47.5 %copy-start.10 = (bf16[192,256]{1,0:T(8,128)(2,1)S(1)}, bf16[192,256]{1,0:T(8,128)(2,1)}, u32[]{:S(2)}) copy-start(bf16[192,256]{1,0:T(8,128)(2,1)} %constant.95.clone.refs_7_) | copy-start | bytes 294916
  0.8 0.9 copy-start.11
  1.7 0.9 copy-start.12
  2.6 0.7 copy-start.15
  3.3 36.8 %copy-start.14 = (f32[512]{0:T(512)S(1)}, f32[512]{0:T(512)}, u32[]{:S(2)}) copy-start(f32[512]{0:T(512)} %refs_0_.1) | copy-start | bytes 6148
  3.3 36.8 %copy-start.16 = (s32[512]{0:T(512)S(1)}, s32[512]{0:T(512)}, u32[]{:S(2)}) copy-start(s32[512]{0:T(512)} %param.17) | copy-start | bytes 6148
  5.1 1.0 copy-start.5
  6.1 0.9 copy-start.7
  7.0 0.7 copy-start.13
  16.7 4.2 %collective-permute-start = (s16[672,128]{1,0:T(8,128)(2,1)S(1)}, s16[672,128]{1,0:T(8,128)(2,1)S(1)}, u32[]{:S(2)}, u32[]{:S(2)}) collective-permute-start(s16[672,128]{1,0:T(8,128)(2,1)S(1)} %get-tuple-element.35), channel_id=1, source_target_pairs={{0,1},{1,0},{2,3},{3,2},{4,5},{5,4},{6,7},{7,6},{8,9},{9,8},{10,11... | collective-permute-start | bytes 516104 | tf_op jit(solution)/shard_map/ppermute | solution.py:723
  17.3 7.8 %collective-permute-start.1 = (s16[672,128]{1,0:T(8,128)(2,1)S(1)}, s16[672,128]{1,0:T(8,128)(2,1)S(1)}, u32[]{:S(2)}, u32[]{:S(2)}) collective-permute-start(s16[672,128]{1,0:T(8,128)(2,1)S(1)} %get-tuple-element.36), channel_id=1, source_target_pairs={{0,2},{1,3},{2,0},{3,1},{4,6},{5,7},{6,4},{7,5},{8,10},{9,11},{10,... | collective-permute-start | bytes 516104 | tf_op jit(solution)/shard_map/ppermute | solution.py:723
  19.8 8.4 %collective-permute-start.2 = (s16[672,128]{1,0:T(8,128)(2,1)S(1)}, s16[672,128]{1,0:T(8,128)(2,1)S(1)}, u32[]{:S(2)}, u32[]{:S(2)}) collective-permute-start(s16[672,128]{1,0:T(8,128)(2,1)S(1)} %get-tuple-element.37), channel_id=1, source_target_pairs={{0,3},{1,2},{2,1},{3,0},{4,7},{5,6},{6,5},{7,4},{8,11},{9,10},{10,... | collective-permute-start | bytes 516104 | tf_op jit(solution)/shard_map/ppermute | solution.py:723
  28.2 1.0 copy-start.3
  29.2 25.3 %copy-start.17 = (s32[24]{0:T(128)S(1)}, s32[24]{0:T(128)}, u32[]{:S(2)}) copy-start(s32[24]{0:T(128)} %param.21) | copy-start | bytes 292
  29.2 25.3 %copy-start.18 = (s32[24]{0:T(128)S(1)}, s32[24]{0:T(128)}, u32[]{:S(2)}) copy-start(s32[24]{0:T(128)} %param.22) | copy-start | bytes 292
  29.2 25.4 %copy-start = (bf16[24,128,128]{2,1,0:T(8,128)(2,1)S(1)}, bf16[24,128,128]{2,1,0:T(8,128)(2,1)}, u32[]{:S(2)}) copy-start(bf16[24,128,128]{2,1,0:T(8,128)(2,1)} %refs_3_.3) | copy-start | bytes 2359300
  31.5 8.6 %collective-permute-start.5 = (s16[272,128]{1,0:T(8,128)(2,1)S(1)}, s16[272,128]{1,0:T(8,128)(2,1)S(1)}, u32[]{:S(2)}, u32[]{:S(2)}) collective-permute-start(s16[272,128]{1,0:T(8,128)(2,1)S(1)} %get-tuple-element.41.refs_3_), channel_id=1, source_target_pairs={{0,8},{4,12},{8,0},{12,4},{1,9},{5,13},{9,1},{13,5},{2,10},{6,14},... | collective-permute-start | bytes 208904 | tf_op jit(solution)/shard_map/ppermute | solution.py:734
  34.3 8.0 %collective-permute-start.6 = (s16[272,128]{1,0:T(8,128)(2,1)S(1)}, s16[272,128]{1,0:T(8,128)(2,1)S(1)}, u32[]{:S(2)}, u32[]{:S(2)}) collective-permute-start(s16[272,128]{1,0:T(8,128)(2,1)S(1)} %get-tuple-element.41.refs_3_), channel_id=1, source_target_pairs={{0,12},{12,0},{1,13},{13,1},{2,14},{14,2},{3,15},{15,3},{16,28},{2... | collective-permute-start | bytes 208904 | tf_op jit(solution)/shard_map/ppermute | solution.py:734
  37.5 6.3 %collective-permute-start.3 = (s16[816,128]{1,0:T(8,128)(2,1)S(1)}, s16[816,128]{1,0:T(8,128)(2,1)S(1)}, u32[]{:S(2)}, u32[]{:S(2)}) collective-permute-start(s16[816,128]{1,0:T(8,128)(2,1)S(1)} %get-tuple-element.39), channel_id=1, source_target_pairs={{0,4},{4,8},{8,12},{1,5},{5,9},{9,13},{2,6},{6,10},{10,14},{3,7},{... | collective-permute-start | bytes 626696 | tf_op jit(solution)/shard_map/ppermute | solution.py:732
  38.8 8.7 %collective-permute-start.4 = (s16[816,128]{1,0:T(8,128)(2,1)S(1)}, s16[816,128]{1,0:T(8,128)(2,1)S(1)}, u32[]{:S(2)}, u32[]{:S(2)}) collective-permute-start(s16[816,128]{1,0:T(8,128)(2,1)S(1)} %get-tuple-element.40), channel_id=1, source_target_pairs={{4,0},{8,4},{12,8},{5,1},{9,5},{13,9},{6,2},{10,6},{14,10},{7,3},{... | collective-permute-start | bytes 626696 | tf_op jit(solution)/shard_map/ppermute | solution.py:733
  47.5 15.1 %copy-start.1 = (bf16[4,128,256]{2,1,0:T(8,128)(2,1)S(1)}, bf16[4,128,256]{2,1,0:T(8,128)(2,1)}, u32[]{:S(2)}) copy-start(bf16[4,128,256]{2,1,0:T(8,128)(2,1)} %constant.96.clone.refs_4_) | copy-start | bytes 786436
  47.5 15.1 %copy-start.2 = (bf16[4,128,256]{2,1,0:T(8,128)(2,1)S(1)}, bf16[4,128,256]{2,1,0:T(8,128)(2,1)}, u32[]{:S(2)}) copy-start(bf16[4,128,256]{2,1,0:T(8,128)(2,1)} %constant.97.clone.refs_5_) | copy-start | bytes 786436
  47.5 26.1 %copy-start.6 = (bf16[4,256,128]{2,1,0:T(8,128)(2,1)S(1)}, bf16[4,256,128]{2,1,0:T(8,128)(2,1)}, u32[]{:S(2)}) copy-start(bf16[4,256,128]{2,1,0:T(8,128)(2,1)} %constant.91.clone.refs_5_) | copy-start | bytes 786436
  47.5 26.1 %copy-start.8 = (bf16[4,256,128]{2,1,0:T(8,128)(2,1)S(1)}, bf16[4,256,128]{2,1,0:T(8,128)(2,1)}, u32[]{:S(2)}) copy-start(bf16[4,256,128]{2,1,0:T(8,128)(2,1)} %constant.92.clone.refs_6_) | copy-start | bytes 786436
  52.5 40.0 %copy-start.4 = (bf16[256,480]{1,0:T(8,128)(2,1)S(1)}, bf16[256,480]{1,0:T(8,128)(2,1)}, u32[]{:S(2)}) copy-start(bf16[256,480]{1,0:T(8,128)(2,1)} %constant.93.clone.refs_4_) | copy-start | bytes 737284
  52.5 3.0 %collective-permute-start.7 = (s16[672,128]{1,0:T(8,128)(2,1)S(1)}, s16[672,128]{1,0:T(8,128)(2,1)S(1)}, u32[]{:S(2)}, u32[]{:S(2)}) collective-permute-start(s16[672,128]{1,0:T(8,128)(2,1)S(1)} %get-tuple-element.43), channel_id=1, source_target_pairs={{0,1},{1,0},{2,3},{3,2},{4,5},{5,4},{6,7},{7,6},{8,9},{9,8},{10,11... | collective-permute-start | bytes 516104 | tf_op jit(solution)/shard_map/ppermute | solution.py:723
  52.6 7.2 %collective-permute-start.8 = (s16[672,128]{1,0:T(8,128)(2,1)S(1)}, s16[672,128]{1,0:T(8,128)(2,1)S(1)}, u32[]{:S(2)}, u32[]{:S(2)}) collective-permute-start(s16[672,128]{1,0:T(8,128)(2,1)S(1)} %get-tuple-element.44), channel_id=1, source_target_pairs={{0,2},{1,3},{2,0},{3,1},{4,6},{5,7},{6,4},{7,5},{8,10},{9,11},{10,... | collective-permute-start | bytes 516104 | tf_op jit(solution)/shard_map/ppermute | solution.py:723
  54.2 8.5 %collective-permute-start.9 = (s16[672,128]{1,0:T(8,128)(2,1)S(1)}, s16[672,128]{1,0:T(8,128)(2,1)S(1)}, u32[]{:S(2)}, u32[]{:S(2)}) collective-permute-start(s16[672,128]{1,0:T(8,128)(2,1)S(1)} %get-tuple-element.45), channel_id=1, source_target_pairs={{0,3},{1,2},{2,1},{3,0},{4,7},{5,6},{6,5},{7,4},{8,11},{9,10},{10,... | collective-permute-start | bytes 516104 | tf_op jit(solution)/shard_map/ppermute | solution.py:723
  82.7 1.9 %collective-permute-start.10 = (s16[672,128]{1,0:T(8,128)(2,1)S(1)}, s16[672,128]{1,0:T(8,128)(2,1)S(1)}, u32[]{:S(2)}, u32[]{:S(2)}) collective-permute-start(s16[672,128]{1,0:T(8,128)(2,1)S(1)} %get-tuple-element.49), channel_id=1, source_target_pairs={{0,1},{1,0},{2,3},{3,2},{4,5},{5,4},{6,7},{7,6},{8,9},{9,8},{10,11... | collective-permute-start | bytes 516104 | tf_op jit(solution)/shard_map/ppermute | solution.py:723
  83.0 7.2 %collective-permute-start.11 = (s16[672,128]{1,0:T(8,128)(2,1)S(1)}, s16[672,128]{1,0:T(8,128)(2,1)S(1)}, u32[]{:S(2)}, u32[]{:S(2)}) collective-permute-start(s16[672,128]{1,0:T(8,128)(2,1)S(1)} %get-tuple-element.50), channel_id=1, source_target_pairs={{0,2},{1,3},{2,0},{3,1},{4,6},{5,7},{6,4},{7,5},{8,10},{9,11},{10,... | collective-permute-start | bytes 516104 | tf_op jit(solution)/shard_map/ppermute | solution.py:723
  84.5 8.0 %collective-permute-start.12 = (s16[672,128]{1,0:T(8,128)(2,1)S(1)}, s16[672,128]{1,0:T(8,128)(2,1)S(1)}, u32[]{:S(2)}, u32[]{:S(2)}) collective-permute-start(s16[672,128]{1,0:T(8,128)(2,1)S(1)} %get-tuple-element.51), channel_id=1, source_target_pairs={{0,3},{1,2},{2,1},{3,0},{4,7},{5,6},{6,5},{7,4},{8,11},{9,10},{10,... | collective-permute-start | bytes 516104 | tf_op jit(solution)/shard_map/ppermute | solution.py:723
  94.9 19.0 %collective-permute-start.13 = (s16[816,128]{1,0:T(8,128)(2,1)S(1)}, s16[816,128]{1,0:T(8,128)(2,1)S(1)}, u32[]{:S(2)}, u32[]{:S(2)}) collective-permute-start(s16[816,128]{1,0:T(8,128)(2,1)S(1)} %get-tuple-element.53), channel_id=1, source_target_pairs={{0,4},{4,8},{8,12},{1,5},{5,9},{9,13},{2,6},{6,10},{10,14},{3,7},{... | collective-permute-start | bytes 626696 | tf_op jit(solution)/shard_map/ppermute | solution.py:732
  99.0 14.9 %collective-permute-start.14 = (s16[816,128]{1,0:T(8,128)(2,1)S(1)}, s16[816,128]{1,0:T(8,128)(2,1)S(1)}, u32[]{:S(2)}, u32[]{:S(2)}) collective-permute-start(s16[816,128]{1,0:T(8,128)(2,1)S(1)} %get-tuple-element.54), channel_id=1, source_target_pairs={{4,0},{8,4},{12,8},{5,1},{9,5},{13,9},{6,2},{10,6},{14,10},{7,3},{... | collective-permute-start | bytes 626696 | tf_op jit(solution)/shard_map/ppermute | solution.py:733
  100.3 13.6 %collective-permute-start.15 = (s16[272,128]{1,0:T(8,128)(2,1)S(1)}, s16[272,128]{1,0:T(8,128)(2,1)S(1)}, u32[]{:S(2)}, u32[]{:S(2)}) collective-permute-start(s16[272,128]{1,0:T(8,128)(2,1)S(1)} %get-tuple-element.55.refs_3_), channel_id=1, source_target_pairs={{0,8},{4,12},{8,0},{12,4},{1,9},{5,13},{9,1},{13,5},{2,10},{6,14},... | collective-permute-start | bytes 208904 | tf_op jit(solution)/shard_map/ppermute | solution.py:734
  104.2 9.7 %collective-permute-start.16 = (s16[272,128]{1,0:T(8,128)(2,1)S(1)}, s16[272,128]{1,0:T(8,128)(2,1)S(1)}, u32[]{:S(2)}, u32[]{:S(2)}) collective-permute-start(s16[272,128]{1,0:T(8,128)(2,1)S(1)} %get-tuple-element.55.refs_3_), channel_id=1, source_target_pairs={{0,12},{12,0},{1,13},{13,1},{2,14},{14,2},{3,15},{15,3},{16,28},{2... | collective-permute-start | bytes 208904 | tf_op jit(solution)/shard_map/ppermute | solution.py:734
  118.9 3.0 %collective-permute-start.17 = (s16[672,128]{1,0:T(8,128)(2,1)S(1)}, s16[672,128]{1,0:T(8,128)(2,1)S(1)}, u32[]{:S(2)}, u32[]{:S(2)}) collective-permute-start(s16[672,128]{1,0:T(8,128)(2,1)S(1)} %get-tuple-element.57), channel_id=1, source_target_pairs={{0,1},{1,0},{2,3},{3,2},{4,5},{5,4},{6,7},{7,6},{8,9},{9,8},{10,11... | collective-permute-start | bytes 516104 | tf_op jit(solution)/shard_map/ppermute | solution.py:723
  119.0 7.2 %collective-permute-start.18 = (s16[672,128]{1,0:T(8,128)(2,1)S(1)}, s16[672,128]{1,0:T(8,128)(2,1)S(1)}, u32[]{:S(2)}, u32[]{:S(2)}) collective-permute-start(s16[672,128]{1,0:T(8,128)(2,1)S(1)} %get-tuple-element.58), channel_id=1, source_target_pairs={{0,2},{1,3},{2,0},{3,1},{4,6},{5,7},{6,4},{7,5},{8,10},{9,11},{10,... | collective-permute-start | bytes 516104 | tf_op jit(solution)/shard_map/ppermute | solution.py:723
  120.5 8.5 %collective-permute-start.19 = (s16[672,128]{1,0:T(8,128)(2,1)S(1)}, s16[672,128]{1,0:T(8,128)(2,1)S(1)}, u32[]{:S(2)}, u32[]{:S(2)}) collective-permute-start(s16[672,128]{1,0:T(8,128)(2,1)S(1)} %get-tuple-element.59), channel_id=1, source_target_pairs={{0,3},{1,2},{2,1},{3,0},{4,7},{5,6},{6,5},{7,4},{8,11},{9,10},{10,... | collective-permute-start | bytes 516104 | tf_op jit(solution)/shard_map/ppermute | solution.py:723

commit v3 on v2

--- a/solution.py
+++ b/solution.py
@@ -21,8 +21,9 @@
 F32 = jnp.float32
 BF16 = jnp.bfloat16
 VMEM_LIMIT = 24 * 1024 * 1024
+START_LIMIT = 56 * 1024 * 1024
 GROUP = 32
-CHAINS = 4
+CHAINS = 2
 
 
 def cas(angles):
@@ -169,79 +170,97 @@
     )
 
 
-def weave_kernel(flag_ref, sample_ref, dipole_ref, source_out, sample_out):
-    charged = flag_ref[...] == 1
-    rows = []
-    for depth in range(4):
-        sample = sample_ref[pl.ds(depth, 16, stride=4), :]
-        dipole = dipole_ref[pl.ds(depth, 16, stride=4), :]
-        rows.append(jnp.concatenate([jnp.where(charged, -sample, dipole), sample], axis=0))
-    weights = jnp.concatenate(rows, axis=1)
-    first, rest = split(weights)
-    second, third = split(weights - first.astype(F32))
+def weave(flag, sample_refs, dipole_refs, source_out, sample_out):
     place = lax.broadcasted_iota(jnp.int32, (4 * BLOCK, 4 * BLOCK), 0)
     lane = lax.broadcasted_iota(jnp.int32, (4 * BLOCK, 4 * BLOCK), 1)
     wanted = 4 * (place % BLOCK) + place // BLOCK
-    weave = jnp.where(lane == wanted, 1.0, 0.0).astype(BF16)
-    woven = dot(first, weave) + (dot(second, weave) + dot(third, weave))
-    for part in range(4):
-        source_out[part] = woven[:16, part * BLOCK : (part + 1) * BLOCK]
-        sample_out[part] = woven[16:, part * BLOCK : (part + 1) * BLOCK]
-
-
-def weave(flag, sample, dipole):
-    count = sample.shape[1]
-    shape = jax.ShapeDtypeStruct((count // GROUP, 16, BLOCK), F32)
-    columns = lambda rows: pl.BlockSpec((rows, BLOCK), lambda i: (0, i))
-    out_block = pl.BlockSpec((BLOCK // GROUP, 16, BLOCK), lambda i: (i, 0, 0))
-    return pl.pallas_call(
-        weave_kernel,
-        grid=(count // BLOCK,),
-        in_specs=[columns(1), columns(64), columns(64)],
-        out_specs=[out_block] * 2,
-        out_shape=[shape, shape],
-        compiler_params=params(),
-        name="weave",
-    )(flag.reshape(1, -1), sample, dipole)
-
-
-def placed_weights(coeff_ref, panel, depth):
-    held = coeff_ref[panel // GROUP]
-    return pltpu.roll(held, (depth - (panel % GROUP) * 4) & (REGION - 1), 1)
-
-
-def spread_kernel(reach, pieces, *refs):
-    vector_ref, row_ref, depth_ref, rounded_ref, coeff_ref, high_ref, low_ref = refs[:7]
-    outs = refs[7 : 7 + pieces]
-    head = refs[7 + pieces]
-    grids = refs[8 + pieces :]
+    mixing = jnp.where(lane == wanted, 1.0, 0.0).astype(BF16)
+    stacked = []
+    for tile, (sample_ref, dipole_ref) in enumerate(zip(sample_refs, dipole_refs)):
+        charged = flag[:, tile * BLOCK : (tile + 1) * BLOCK] == 1
+        rows = []
+        for depth in range(4):
+            sample = sample_ref[pl.ds(depth, 16, stride=4), :]
+            dipole = dipole_ref[pl.ds(depth, 16, stride=4), :]
+            rows.append(jnp.concatenate([jnp.where(charged, -sample, dipole), sample], axis=0))
+        stacked.append(jnp.concatenate(rows, axis=1))
+    weights = jnp.concatenate(stacked, axis=0)
+    first, rest = split(weights)
+    second, third = split(weights - first.astype(F32))
+    woven = dot(first, mixing) + (dot(second, mixing) + dot(third, mixing))
+    for tile in range(len(sample_refs)):
+        for which, out in enumerate((source_out, sample_out)):
+            for part in range(BLOCK // GROUP):
+                at = (tile * (BLOCK // GROUP) + part) * 16
+                lanes = slice(part * BLOCK, (part + 1) * BLOCK)
+                for a in range(4):
+                    row = tile * 32 + which * 16 + 4 * a
+                    out[pl.ds(at + 8 * (a // 2) + a % 2, 4, stride=2), :] = woven[
+                        row : row + 4, lanes
+                    ]
+
+
+def pair_rows(x, reach_x, reach_y):
+    even = (x // 2) * 2 * reach_y + x % 2
+    if x == 0 or x == reach_x - 1:
+        return [even]
+    return [even, reach_x * reach_y + ((x - 1) // 2) * 2 * reach_y + (x - 1) % 2]
+
+
+def pair_count(reach_x, reach_y):
+    return (2 * reach_x - 2) * reach_y
+
+
+def add_panels(reach, vector_ref, row_ref, depth_ref, coeff_ref, grids):
+    lanes = lax.broadcasted_iota(jnp.int32, (8, REGION), 1)
+
+    def body(group, carry):
+        at = pl.multiple_of(group * 16, 16)
+        coeff = [coeff_ref[pl.ds(at, 8), :], coeff_ref[pl.ds(at + 8, 8), :]]
+        for local in range(GROUP):
+            panel = group * GROUP + local
+            grid = grids[local % len(grids)]
+            row = row_ref[panel]
+            depth = depth_ref[panel]
+            shift = (depth - 4 * local) & (REGION - 1)
+            value = jnp.where(((lanes - depth) & -4) == 0, vector_ref[panel], 0.0)
+            places = [pl.ds(row, 8), pl.ds(row + 2 * reach, 8)]
+            held = [grid[place, :] for place in places]
+            for q in range(2):
+                grid[places[q], :] = held[q] + pltpu.roll(coeff[q], shift, 1) * value
+        return carry
+
+    lax.fori_loop(0, vector_ref.shape[0] // GROUP, body, 0)
+
+
+def spread_kernel(first, reach_x, reach_y, pieces, tiles, *refs):
+    vector_ref, row_ref, depth_ref, rounded_ref, high_ref, low_ref = refs[:6]
+    refs = refs[6:]
+    if first:
+        flag_ref, sample_refs, dipole_refs = refs[0], refs[1 : 1 + tiles], refs[1 + tiles : 1 + 2 * tiles]
+        refs = refs[1 + 2 * tiles :]
+    else:
+        coeff_ref = refs[0]
+        refs = refs[1:]
+    outs, refs = refs[:pieces], refs[pieces:]
+    if first:
+        coeff_ref, sample_coeff_ref = refs[:2]
+        refs = refs[2:]
+        weave(flag_ref[...], sample_refs, dipole_refs, coeff_ref, sample_coeff_ref)
+    head, total = refs[:2]
+    grids = refs[2:]
     for grid in grids:
         grid[...] = jnp.zeros_like(grid)
-    lanes = lax.broadcasted_iota(jnp.int32, (4, REGION), 1)
-    chains = len(grids)
-
-    def body(group, carry):
-        for chain in range(chains):
-            panel = group * chains + chain
-            row = row_ref[panel]
-            depth = depth_ref[panel]
-            line = placed_weights(coeff_ref, panel, depth)
-            offset = lanes - depth
-            value = jnp.where((offset >= 0) & (offset < 4), vector_ref[panel], 0.0)
-            places = [pl.ds(row + a * reach, 4) for a in range(4)]
-            held = [grids[chain][place, :] for place in places]
-            added = [line[4 * a : 4 * a + 4] * value for a in range(4)]
-            for a in range(4):
-                grids[chain][places[a], :] = held[a] + added[a]
-        return carry
-
-    lax.fori_loop(0, vector_ref.shape[0] // chains, body, 0, unroll=2)
-
-    total = grids[0][...]
-    for grid in grids[1:]:
-        total = total + grid[...]
-    half = total.shape[0] // 2
-    both = jnp.concatenate([total[:half], total[half:]], axis=1)
+    add_panels(reach_y, vector_ref, row_ref, depth_ref, coeff_ref, grids)
+    for x in range(reach_x):
+        parts = [
+            grid[pl.ds(row, reach_y, stride=2), :]
+            for row in pair_rows(x, reach_x, reach_y)
+            for grid in grids
+        ]
+        total[x * reach_y : (x + 1) * reach_y, :] = sum(parts[1:], parts[0])
+    half = reach_x * reach_y // 2
+    both = jnp.concatenate([total[:half, :], total[half:, :]], axis=1)
     extra = outs[0].shape[0] - head.shape[0] - half
     if extra:
         both = jnp.concatenate([both, jnp.zeros((extra, 2 * REGION), F32)], axis=0)
@@ -259,24 +278,46 @@
         send_piece(outs[piece + 1], head, result[:, 2 * HALF :])
 
 
-def spread(vector, rows, depths, coeff, table, reach_x, reach_y):
+def spread(vector, rows, depths, table, coeff, raw, reach_x, reach_y):
     pieces = table[0].shape[0]
-    line_count = reach_x * reach_y
-    half = line_count // 2
-    blocks = vector.shape[0] // BLOCK
+    count = vector.shape[0]
+    half = reach_x * reach_y // 2
+    blocks = count // BLOCK
     top = up_to(2 + 2 * blocks, 16)
     lanes = 2 * HALF
+    constant = lambda shape: pl.BlockSpec(shape, lambda i: (0,) * len(shape))
+    piece = (top + up_to(half, 16), lanes)
+    woven = (count // GROUP * 16, BLOCK)
+    out_shapes = [jax.ShapeDtypeStruct(piece, jnp.int16)] * pieces
+    operands = [vector, rows, depths, vector.reshape(blocks, BLOCK), *table]
+    in_specs = [in_smem()] * 3 + [constant(value.shape) for value in operands[3:]]
+    first = coeff is None
+    if first:
+        flag, sample, dipole = raw
+        tile = lambda t: pl.BlockSpec((64, BLOCK), lambda i: (0, t))
+        operands += [flag.reshape(1, -1)] + [sample] * blocks + [dipole] * blocks
+        in_specs += [constant((1, count))] + [tile(t) for t in range(blocks)] * 2
+        out_shapes += [jax.ShapeDtypeStruct(woven, F32)] * 2
+    else:
+        operands.append(coeff)
+        in_specs.append(constant(woven))
     return pl.pallas_call(
-        functools.partial(spread_kernel, reach_y, pieces),
-        in_specs=[in_smem()] * 3 + [whole_vmem()] * 4,
-        out_specs=[whole_vmem()] * pieces,
-        out_shape=[jax.ShapeDtypeStruct((top + up_to(half, 16), lanes), jnp.int16)] * pieces,
-        scratch_shapes=[pltpu.VMEM((top, lanes), F32)]
-        + [pltpu.VMEM((line_count, REGION), F32)] * CHAINS,
-        compiler_params=params(),
-        cost_estimate=cost(2 * half * 256 * 512, 4 * 16 * vector.shape[0] * REGION),
-        name="spread",
-    )(vector, rows, depths, vector.reshape(blocks, BLOCK), coeff, *table)
+        functools.partial(spread_kernel, first, reach_x, reach_y, pieces, blocks),
+        grid=(1,),
+        in_specs=in_specs,
+        out_specs=[constant(out.shape) for out in out_shapes],
+        out_shape=out_shapes,
+        scratch_shapes=[
+            pltpu.VMEM((top, lanes), F32),
+            pltpu.VMEM((reach_x * reach_y, REGION), F32),
+        ]
+        + [pltpu.VMEM((pair_count(reach_x, reach_y), REGION), F32)] * CHAINS,
+        compiler_params=pltpu.CompilerParams(
+            vmem_limit_bytes=START_LIMIT if first else VMEM_LIMIT
+        ),
+        cost_estimate=cost(2 * half * 256 * 512, 4 * 16 * count * REGION),
+        name="start" if first else "spread",
+    )(*operands)
 
 
 def forward_kernel(reach_x, reach_y, blocks, pieces, *refs):
@@ -558,10 +599,30 @@
     )(spectrum, from_left, from_right, own, *fars, *table, modes)
 
 
-def sample_kernel(reach, half_rows, pieces, row_ref, depth_ref, *refs):
+def sum_rows(values):
+    row = lax.broadcasted_iota(jnp.int32, values[0].shape, 0)
+    for step in (4, 2, 1):
+        low = (row & step) == 0
+        paired = []
+        for one, other in zip(values[: len(values) // 2], values[len(values) // 2 :]):
+            kept = jnp.where(low, one, other)
+            moved = jnp.where(low, other, one)
+            if step == 4:
+                moved = pltpu.roll(moved, 4, 0)
+            else:
+                moved = jnp.where(low, pltpu.roll(moved, 8 - step, 0), pltpu.roll(moved, step, 0))
+            paired.append(kept + moved)
+        values = paired
+    return values[0]
+
+
+def sample_kernel(last, reach_x, reach_y, pieces, row_ref, depth_ref, *refs):
     parts = refs[:pieces]
-    high_ref, low_ref, coeff_ref, base_ref, near_ref, out_ref, field, sums = refs[pieces:]
+    high_ref, low_ref, coeff_ref, own_ref, vector_ref, near_ref, out_ref, flat, field, sums = refs[
+        pieces:
+    ]
     mine = y_position()
+    half_rows = reach_x * reach_y // 2
     opened = []
     for part in parts:
         first = from_short(part[:16, :])
@@ -569,24 +630,34 @@
     values = split(jnp.concatenate(opened, axis=1))
     pick = lambda ref: jnp.concatenate([ref[mine ^ piece] for piece in range(pieces)], axis=0)
     both = dot_three(values, (pick(high_ref), pick(low_ref)))
-    field[:half_rows, :] = both[:half_rows, :REGION]
-    field[half_rows:, :] = both[:half_rows, REGION:]
-    lanes = lax.broadcasted_iota(jnp.int32, (1, REGION), 1)
-
-    def body(panel, carry):
-        row = row_ref[panel]
-        depth = depth_ref[panel]
-        line = placed_weights(coeff_ref, panel, depth)
-        total = field[pl.ds(row, 4), :] * line[:4]
-        for a in range(1, 4):
-            total = total + field[pl.ds(row + a * reach, 4), :] * line[4 * a : 4 * a + 4]
-        offset = lanes - depth
-        total = jnp.sum(total, axis=0, keepdims=True)
-        sums[pl.ds(panel, 1), :] = jnp.where((offset >= 0) & (offset < 4), total, 0.0)
+    flat[:half_rows, :] = both[:half_rows, :REGION]
+    flat[half_rows:, :] = both[:half_rows, REGION:]
+    for x in range(reach_x):
+        layer = flat[x * reach_y : (x + 1) * reach_y, :]
+        for row in pair_rows(x, reach_x, reach_y):
+            field[pl.ds(row, reach_y, stride=2), :] = layer
+    lanes = lax.broadcasted_iota(jnp.int32, (8, REGION), 1)
+
+    def body(group, carry):
+        at = pl.multiple_of(group * 16, 16)
+        coeff = [coeff_ref[pl.ds(at, 8), :], coeff_ref[pl.ds(at + 8, 8), :]]
+        for eight in range(0, GROUP, 8):
+            totals = []
+            for local in range(eight, eight + 8):
+                panel = group * GROUP + local
+                row = row_ref[panel]
+                depth = depth_ref[panel]
+                shift = (depth - 4 * local) & (REGION - 1)
+                total = field[pl.ds(row, 8), :] * pltpu.roll(coeff[0], shift, 1)
+                total = total + field[pl.ds(row + 2 * reach_y, 8), :] * pltpu.roll(
+                    coeff[1], shift, 1
+                )
+                totals.append(jnp.where(((lanes - depth) & -4) == 0, total, 0.0))
+            sums[pl.ds(pl.multiple_of(group * GROUP + eight, 8), 8), :] = sum_rows(totals)
         return carry
 
     count = row_ref.shape[0]
-    lax.fori_loop(0, count, body, 0, unroll=8)
+    lax.fori_loop(0, count // GROUP, body, 0)
     sampled = lax.dot_general(
         jnp.ones((8, REGION), F32),
         sums[...],
@@ -596,28 +667,45 @@
     )
     for block in range(count // BLOCK):
         lane = slice(block * BLOCK, (block + 1) * BLOCK)
-        out_ref[block : block + 1, :] = (
-            base_ref[block : block + 1, :] + sampled[:1, lane] + near_ref[block : block + 1, :]
-        )
-
-
-def sample(rows, depths, parts, table, coeff, base, near, reach_x, reach_y):
+        row = slice(block, block + 1)
+        vector = vector_ref[row, :]
+        image = jnp.where(own_ref[row, :] == 1, 0.0, 0.5 * vector) + sampled[:1, lane]
+        image = image + near_ref[row, :]
+        if last:
+            out_ref[0:1, lane] = vector
+            out_ref[1:2, lane] = image
+        else:
+            out_ref[row, :] = image
+
+
+def sample(last, rows, depths, parts, table, coeff, flag, vector, near, reach_x, reach_y):
     count = rows.shape[0]
+    blocks = count // BLOCK
     pieces = len(parts)
-    half_rows = reach_x * reach_y // 2
+    shape = (2, count) if last else (blocks, BLOCK)
     return pl.pallas_call(
-        functools.partial(sample_kernel, reach_y, half_rows, pieces),
-        in_specs=[in_smem()] * 2 + [whole_vmem()] * (pieces + 5),
+        functools.partial(sample_kernel, last, reach_x, reach_y, pieces),
+        in_specs=[in_smem()] * 2 + [whole_vmem()] * (pieces + 6),
         out_specs=whole_vmem(),
-        out_shape=jax.ShapeDtypeStruct((count // BLOCK, BLOCK), F32),
+        out_shape=jax.ShapeDtypeStruct(shape, F32),
         scratch_shapes=[
-            pltpu.VMEM((2 * half_rows, REGION), F32),
+            pltpu.VMEM((reach_x * reach_y, REGION), F32),
+            pltpu.VMEM((pair_count(reach_x, reach_y), REGION), F32),
             pltpu.VMEM((count, REGION), F32),
         ],
         compiler_params=params(),
-        cost_estimate=cost(2 * half_rows * 256 * 512, 4 * 16 * count * REGION),
+        cost_estimate=cost(reach_x * reach_y * 256 * 512, 4 * 16 * count * REGION),
         name="sample",
-    )(rows, depths, *parts, *table, coeff, base, near)
+    )(
+        rows,
+        depths,
+        *parts,
+        *table,
+        coeff,
+        flag.reshape(blocks, BLOCK),
+        vector.reshape(blocks, BLOCK),
+        near,
+    )
 
 
 def near_kernel(slots, blocks, place_ref, target_ref, *refs):
@@ -693,12 +781,12 @@
     z_forward, z_inverse, y_forward, y_inverse, modes = tables(y_count, span_y)
     modes = lax.dynamic_index_in_dim(jnp.asarray(modes), y_index, 0, keepdims=False)
 
-    rows = (stencil_base[0] - (x_index * span_x - 2)) * reach_y + (
-        stencil_base[1] - (y_index * span_y - 2)
+    local_x = stencil_base[0] - (x_index * span_x - 2)
+    local_y = stencil_base[1] - (y_index * span_y - 2)
+    rows = (
+        (local_x % 2) * (reach_x * reach_y) + (local_x // 2) * (2 * reach_y) + 2 * local_y
     )
     depths = stencil_base[2]
-    source_coeff, sample_coeff = weave(surface_flag, sample_weights, dipole_weights)
-    own_share = jnp.where(surface_flag == 1, 0.0, 0.5).astype(F32)
 
     neighbour = near_source // blocks
     flip = (y_index + neighbour % 3 - 1) ^ y_index
@@ -724,10 +812,9 @@
             for flip, part in enumerate(parts)
         ]
 
-    def apply_operator(vector):
-        parts = turn(spread(vector, rows, depths, source_coeff, z_forward, reach_x, reach_y))
+    def convolve_and_sample(last, vector, sent, sample_coeff):
         spectrum, right_going, left_going, own, peers = forward(
-            parts, y_forward, modes, reach_x, reach_y, blocks
+            turn(sent), y_forward, modes, reach_x, reach_y, blocks
         )
         from_left = lax.ppermute(right_going, "wide", to_right)
         from_right = lax.ppermute(left_going, "wide", to_left)
@@ -735,28 +822,39 @@
         near_part = near_field(
             places, targets, from_left, from_right, peers, near_tiles, blocks, out_rows
         )
-        parts = turn(
-            inverse(
-                spectrum,
-                from_left,
-                from_right,
-                own,
-                fars,
-                y_inverse,
-                modes,
-                reach_x,
-                reach_y,
-                y_count,
-            )
+        parts = inverse(
+            spectrum,
+            from_left,
+            from_right,
+            own,
+            fars,
+            y_inverse,
+            modes,
+            reach_x,
+            reach_y,
+            y_count,
         )
-        base = (own_share * vector).reshape(blocks, BLOCK)
         return sample(
-            rows, depths, parts, z_inverse, sample_coeff, base, near_part, reach_x, reach_y
-        ).reshape(-1)
-
-    first_image = apply_operator(density)
-    second = apply_operator(first_image)
-    return jnp.stack([first_image, second])
+            last,
+            rows,
+            depths,
+            turn(parts),
+            z_inverse,
+            sample_coeff,
+            surface_flag,
+            vector,
+            near_part,
+            reach_x,
+            reach_y,
+        )
+
+    raw = (surface_flag, sample_weights, dipole_weights)
+    *sent, source_coeff, sample_coeff = spread(
+        density, rows, depths, z_forward, None, raw, reach_x, reach_y
+    )
+    first_image = convolve_and_sample(False, density, sent, sample_coeff).reshape(-1)
+    sent = spread(first_image, rows, depths, z_forward, source_coeff, None, reach_x, reach_y)
+    return convolve_and_sample(True, first_image, sent, sample_coeff)
 
 
 def solution(mesh):

time: 141 us -> 113 us (0.80)
  Pallas kernels: 58.5 us -> 36.4 us
  local copies, waits for them, and re-layouts: 7.19 us -> 2.1 us
  waiting for transfers between devices: 43.1 us -> 41.1 us
    pallas_call x5 -> x4, Pallas kernels: 41.7 us -> 19.7 us  [the longest x2 10.2 us: spread(): pl.pallas_call(functools.partial(spread_kernel, first, reach_x, reach_y,...]
    unnamed x38 -> x34, local copies, waits for them, and re-layouts: 6.11 us -> 1.03 us
    ppermute x8, waiting for transfers between devices: 13.8 us -> 11.6 us  [the longest x4 11.6 us: convolve_and_sample(): fars = [lax.ppermute(own, 'wide', pairs) for pairs in far_moves]]
  transfers between devices with their start and end apart: 20 -> 20, of which waited for: 12 -> 10; matrix products, arithmetic and copies ran while one was open for 1% -> 1% of each run, Pallas kernels for 1% -> 2%
where the time goes in v3:
time: 113 us; the launch traced here: 112 us
  waiting for transfers between devices  41.1 us (36%)
  Pallas kernels  36.4 us (32%)
  starting transfers between devices  30.5 us (27%)
  local copies, waits for them, and re-layouts  2.1 us (2%)
  other arithmetic  2.01 us (2%)
    ppermute x12, waiting for transfers between devices, turn(): lax.ppermute(part, Y_AXES, [(i, i ^ flip) for i in range(y_count)])  29.5 us
    ppermute x4, starting transfers between devices, convolve_and_sample(): fars = [lax.ppermute(own, 'wide', pairs) for pairs in far_moves]  14.1 us
    ppermute x4, waiting for transfers between devices, convolve_and_sample(): fars = [lax.ppermute(own, 'wide', pairs) for pairs in far_moves]  11.6 us
    pallas_call x2, Pallas kernels, spread(): pl.pallas_call(functools.partial(spread_kernel, first, reach_x, reach_y,...  10.2 us
    pallas_call x2, Pallas kernels, inverse(): pl.pallas_call(functools.partial(inverse_kernel, reach_x, reach_y, pieces...  9.92 us
    pallas_call x2, Pallas kernels, sample(): pl.pallas_call(functools.partial(sample_kernel, last, reach_x, reach_y, p...  9.47 us
    ppermute x12, starting transfers between devices, turn(): lax.ppermute(part, Y_AXES, [(i, i ^ flip) for i in range(y_count)])  8.92 us
    ppermute x2, starting transfers between devices, convolve_and_sample(): from_left = lax.ppermute(right_going, 'wide', to_right)  4.89 us
  transfers between devices with their start and end apart: 20, of which 10 were waited for; matrix products, arithmetic and copies ran while one was open for 1% of the time, Pallas kernels for 2%

profile of v3, /device:TPU:0, one launch (start us, length us, event | category | flops | bytes accessed | tf_op | source)
XLA Modules:
  0.0 112.4 jit_solution(12543411482042818405)
XLA Ops:
  0.0 1.4 %fusion.11 = (s32[1,512]{1,0:T(1,128)}, s32[1,512]{1,0:T(1,128)S(1)}, s32[1,512]{1,0:T(1,128)S(1)}) fusion(s32[3,512]{1,0:T(4,128)} %param.18, s32[]{:T(128)S(6)} %sub.38, s32[]{:T(128)S(6)} %sub.43), kind=kLoop, calls=%fused_computation.29 | loop fusion | flops 1536 | bytes 12296 | tf_op jit(solution)/shard_map/slice | solution.py:789
  1.4 0.6 fusion.2.refs_1_.row_ref
  2.0 5.9 %start.1 = (s16[672,128]{1,0:T(8,128)(2,1)}, s16[672,128]{1,0:T(8,128)(2,1)}, s16[672,128]{1,0:T(8,128)(2,1)}, s16[672,128]{1,0:T(8,128)(2,1)}, f32[256,128]{1,0:T(8,128)}, /*index=5*/f32[256,128]{1,0:T(8,128)}) custom-call(f32[512]{0:T(512)} %refs_0_.1, s32[512]{0:T(512)} %fusion.2.refs_1_.row_ref, s32[512]{0:T(512)} %bitcast.9, f32[4,128]{1,0:T(4,128)} %bitcast.14, ...), custom_call_target="tpu_custom_call" | custom-call | flops 169869312 | bytes 4194304 | tf_op jit(solution)/shard_map/start/pallas_call | solution.py:304
  7.9 0.5 collective-permute-start
  8.4 2.6 %collective-permute-start.1 = (s16[672,128]{1,0:T(8,128)(2,1)}, s16[672,128]{1,0:T(8,128)(2,1)S(1)}, u32[]{:S(2)}, u32[]{:S(2)}) collective-permute-start(s16[672,128]{1,0:T(8,128)(2,1)} %get-tuple-element.35), channel_id=1, source_target_pairs={{0,2},{1,3},{2,0},{3,1},{4,6},{5,7},{6,4},{7,5},{8,10},{9,11},{10,... | collective-permute-start | bytes 516104 | tf_op jit(solution)/shard_map/ppermute | solution.py:811
  11.0 0.1 collective-permute-start.2
  11.0 1.1 dynamic-slice_bitcast_fusion.refs_5_.refs_8_
  12.1 0.0 collective-permute-done.refs_1_
  12.1 4.3 %collective-permute-done.1.refs_2_ = s16[672,128]{1,0:T(8,128)(2,1)S(1)} collective-permute-done((s16[672,128]{1,0:T(8,128)(2,1)}, s16[672,128]{1,0:T(8,128)(2,1)S(1)}, u32[]{:S(2)}, u32[]{:S(2)}) %collective-permute-start.1) | collective-permute-done | bytes 172064 | tf_op jit(solution)/shard_map/ppermute | solution.py:811
  16.4 3.2 %collective-permute-done.2.refs_3_ = s16[672,128]{1,0:T(8,128)(2,1)S(1)} collective-permute-done((s16[672,128]{1,0:T(8,128)(2,1)}, s16[672,128]{1,0:T(8,128)(2,1)S(1)}, u32[]{:S(2)}, u32[]{:S(2)}) %collective-permute-start.2) | collective-permute-done | bytes 172064 | tf_op jit(solution)/shard_map/ppermute | solution.py:811
  19.6 0.0 copy-done.3
  19.6 0.9 copy-done.9
  20.5 2.3 %forward.2 = (f32[18,256,128]{2,1,0:T(8,128)S(1)}, s16[816,128]{1,0:T(8,128)(2,1)S(1)}, s16[816,128]{1,0:T(8,128)(2,1)S(1)}, s16[272,128]{1,0:T(8,128)(2,1)S(1)}, f32[16,128]{1,0:T(8,128)S(1)}) custom-call(s16[672,128]{1,0:T(8,128)(2,1)S(1)} %copy-done.9, s16[672,128]{1,0:T(8,128)(2,1)S(1)} %collective-permute-done.refs_1_, ...), custom_call_target="tpu_custom_call" | custom-call | flops 301989888 | bytes 4718592 | tf_op jit(solution)/shard_map/forward/pallas_call | solution.py:435
  22.8 3.6 %collective-permute-start.3 = (s16[816,128]{1,0:T(8,128)(2,1)S(1)}, s16[816,128]{1,0:T(8,128)(2,1)S(1)}, u32[]{:S(2)}, u32[]{:S(2)}) collective-permute-start(s16[816,128]{1,0:T(8,128)(2,1)S(1)} %get-tuple-element.38), channel_id=1, source_target_pairs={{0,4},{4,8},{8,12},{1,5},{5,9},{9,13},{2,6},{6,10},{10,14},{3,7},{... | collective-permute-start | bytes 626696 | tf_op jit(solution)/shard_map/ppermute | solution.py:819
  26.4 1.3 %collective-permute-start.4 = (s16[816,128]{1,0:T(8,128)(2,1)S(1)}, s16[816,128]{1,0:T(8,128)(2,1)S(1)}, u32[]{:S(2)}, u32[]{:S(2)}) collective-permute-start(s16[816,128]{1,0:T(8,128)(2,1)S(1)} %get-tuple-element.39), channel_id=1, source_target_pairs={{4,0},{8,4},{12,8},{5,1},{9,5},{13,9},{6,2},{10,6},{14,10},{7,3},{... | collective-permute-start | bytes 626696 | tf_op jit(solution)/shard_map/ppermute | solution.py:820
  27.7 3.7 %collective-permute-start.5 = (s16[272,128]{1,0:T(8,128)(2,1)S(1)}, s16[272,128]{1,0:T(8,128)(2,1)S(1)}, u32[]{:S(2)}, u32[]{:S(2)}) collective-permute-start(s16[272,128]{1,0:T(8,128)(2,1)S(1)} %get-tuple-element.40.refs_3_), channel_id=1, source_target_pairs={{0,8},{4,12},{8,0},{12,4},{1,9},{5,13},{9,1},{13,5},{2,10},{6,14},... | collective-permute-start | bytes 208904 | tf_op jit(solution)/shard_map/ppermute | solution.py:821
  31.4 3.3 %collective-permute-start.6 = (s16[272,128]{1,0:T(8,128)(2,1)S(1)}, s16[272,128]{1,0:T(8,128)(2,1)S(1)}, u32[]{:S(2)}, u32[]{:S(2)}) collective-permute-start(s16[272,128]{1,0:T(8,128)(2,1)S(1)} %get-tuple-element.40.refs_3_), channel_id=1, source_target_pairs={{0,12},{12,0},{1,13},{13,1},{2,14},{14,2},{3,15},{15,3},{16,28},{2... | collective-permute-start | bytes 208904 | tf_op jit(solution)/shard_map/ppermute | solution.py:821
  34.7 6.2 %collective-permute-done.5.refs_4_ = s16[272,128]{1,0:T(8,128)(2,1)S(1)} collective-permute-done((s16[272,128]{1,0:T(8,128)(2,1)S(1)}, s16[272,128]{1,0:T(8,128)(2,1)S(1)}, u32[]{:S(2)}, u32[]{:S(2)}) %collective-permute-start.5) | collective-permute-done | bytes 69664 | tf_op jit(solution)/shard_map/ppermute | solution.py:821
  40.9 0.0 collective-permute-done.6.refs_5_
  40.9 0.0 collective-permute-done.3.refs_1_.refs_0_
  40.9 0.0 collective-permute-done.4.refs_2_.refs_1_
  40.9 0.0 copy-start.1
  40.9 0.0 copy-start.2
  40.9 0.0 copy-start.12
  41.0 0.0 copy-start.13
  41.0 0.0 copy-start.14
  41.0 0.0 copy-start.4
  41.0 0.0 copy-start.5
  41.0 5.0 %inverse.2 = (s16[672,128]{1,0:T(8,128)(2,1)S(1)}, s16[672,128]{1,0:T(8,128)(2,1)S(1)}, s16[672,128]{1,0:T(8,128)(2,1)S(1)}, s16[672,128]{1,0:T(8,128)(2,1)S(1)}) custom-call(f32[18,256,128]{2,1,0:T(8,128)S(1)} %get-tuple-element.37.refs_0_, s16[816,128]{1,0:T(8,128)(2,1)S(1)} %collective-permute-done.3.refs_1_.refs_0_, ...), custom_call_target="tpu_custom_call" | custom-call | flops 301989888 | bytes 4718592 | tf_op jit(solution)/shard_map/inverse/pallas_call | solution.py:585
  46.0 0.1 collective-permute-start.7
  46.1 1.5 %collective-permute-start.8 = (s16[672,128]{1,0:T(8,128)(2,1)S(1)}, s16[672,128]{1,0:T(8,128)(2,1)S(1)}, u32[]{:S(2)}, u32[]{:S(2)}) collective-permute-start(s16[672,128]{1,0:T(8,128)(2,1)S(1)} %get-tuple-element.43), channel_id=1, source_target_pairs={{0,2},{1,3},{2,0},{3,1},{4,6},{5,7},{6,4},{7,5},{8,10},{9,11},{10,... | collective-permute-start | bytes 516104 | tf_op jit(solution)/shard_map/ppermute | solution.py:811
  47.6 0.3 collective-permute-start.9
  48.0 1.1 near_field.2.refs_9_
  49.0 0.0 collective-permute-done.7.refs_1_
  49.0 4.3 %collective-permute-done.8.refs_2_ = s16[672,128]{1,0:T(8,128)(2,1)S(1)} collective-permute-done((s16[672,128]{1,0:T(8,128)(2,1)S(1)}, s16[672,128]{1,0:T(8,128)(2,1)S(1)}, u32[]{:S(2)}, u32[]{:S(2)}) %collective-permute-start.8) | collective-permute-done | bytes 172064 | tf_op jit(solution)/shard_map/ppermute | solution.py:811
  53.3 2.8 %collective-permute-done.9.refs_3_ = s16[672,128]{1,0:T(8,128)(2,1)S(1)} collective-permute-done((s16[672,128]{1,0:T(8,128)(2,1)S(1)}, s16[672,128]{1,0:T(8,128)(2,1)S(1)}, u32[]{:S(2)}, u32[]{:S(2)}) %collective-permute-start.9) | collective-permute-done | bytes 172064 | tf_op jit(solution)/shard_map/ppermute | solution.py:811
  56.1 0.0 copy-done.6
  56.1 4.4 %sample.2.refs_3_.refs_8_ = f32[4,128]{1,0:T(4,128)S(1)} custom-call(s32[512]{0:T(512)S(1)} %copy-done.11, s32[512]{0:T(512)S(1)} %bitcast.10, s16[672,128]{1,0:T(8,128)(2,1)S(1)} %get-tuple-element.41.refs_0_, s16[672,128]{1,0:T(8,128)(2,1)S(1)} %collective-permute-done.7.refs_1_, s16[672,128]{1,0:T(8,128)(2,1)S(1)} %collective-permute-done.8.refs_2_, ...), custom_call_target="tpu_custom_call" | custom-call | flops 169869312 | bytes 4194304 | tf_op jit(solution)/shard_map/sample/pallas_call | solution.py:686
  60.6 0.0 copy-done.5
  60.6 4.3 %spread.1 = (s16[672,128]{1,0:T(8,128)(2,1)S(1)}, s16[672,128]{1,0:T(8,128)(2,1)S(1)}, s16[672,128]{1,0:T(8,128)(2,1)S(1)}, s16[672,128]{1,0:T(8,128)(2,1)S(1)}) custom-call(f32[512]{0:T(512)S(1)} %bitcast.13, s32[512]{0:T(512)S(1)} %copy-done.11, s32[512]{0:T(512)S(1)} %bitcast.11, f32[4,128]{1,0:T(4,128)S(1)} %sample.2.refs_3_.refs_8_, ...), custom_call_target="tpu_custom_call" | custom-call | flops 169869312 | bytes 4194304 | tf_op jit(solution)/shard_map/spread/pallas_call | solution.py:304
  64.9 0.3 collective-permute-start.10
  65.2 1.5 %collective-permute-start.11 = (s16[672,128]{1,0:T(8,128)(2,1)S(1)}, s16[672,128]{1,0:T(8,128)(2,1)S(1)}, u32[]{:S(2)}, u32[]{:S(2)}) collective-permute-start(s16[672,128]{1,0:T(8,128)(2,1)S(1)} %get-tuple-element.50), channel_id=1, source_target_pairs={{0,2},{1,3},{2,0},{3,1},{4,6},{5,7},{6,4},{7,5},{8,10},{9,11},{10,... | collective-permute-start | bytes 516104 | tf_op jit(solution)/shard_map/ppermute | solution.py:811
  66.7 0.1 collective-permute-start.12
  66.8 0.0 collective-permute-done.10.refs_1_
  66.8 5.6 %collective-permute-done.11.refs_2_ = s16[672,128]{1,0:T(8,128)(2,1)S(1)} collective-permute-done((s16[672,128]{1,0:T(8,128)(2,1)S(1)}, s16[672,128]{1,0:T(8,128)(2,1)S(1)}, u32[]{:S(2)}, u32[]{:S(2)}) %collective-permute-start.11) | collective-permute-done | bytes 172064 | tf_op jit(solution)/shard_map/ppermute | solution.py:811
  72.4 2.3 %collective-permute-done.12.refs_3_ = s16[672,128]{1,0:T(8,128)(2,1)S(1)} collective-permute-done((s16[672,128]{1,0:T(8,128)(2,1)S(1)}, s16[672,128]{1,0:T(8,128)(2,1)S(1)}, u32[]{:S(2)}, u32[]{:S(2)}) %collective-permute-start.12) | collective-permute-done | bytes 172064 | tf_op jit(solution)/shard_map/ppermute | solution.py:811
  74.7 2.4 %forward.3 = (f32[18,256,128]{2,1,0:T(8,128)S(1)}, s16[816,128]{1,0:T(8,128)(2,1)S(1)}, s16[816,128]{1,0:T(8,128)(2,1)S(1)}, s16[272,128]{1,0:T(8,128)(2,1)S(1)}, f32[16,128]{1,0:T(8,128)S(1)}) custom-call(s16[672,128]{1,0:T(8,128)(2,1)S(1)} %get-tuple-element.48.refs_0_, s16[672,128]{1,0:T(8,128)(2,1)S(1)} %collective-permute-done.10.refs_1_, ...), custom_call_target="tpu_custom_call" | custom-call | flops 301989888 | bytes 4718592 | tf_op jit(solution)/shard_map/forward/pallas_call | solution.py:435
  77.1 1.3 %collective-permute-start.13 = (s16[816,128]{1,0:T(8,128)(2,1)S(1)}, s16[816,128]{1,0:T(8,128)(2,1)S(1)}, u32[]{:S(2)}, u32[]{:S(2)}) collective-permute-start(s16[816,128]{1,0:T(8,128)(2,1)S(1)} %get-tuple-element.53), channel_id=1, source_target_pairs={{0,4},{4,8},{8,12},{1,5},{5,9},{9,13},{2,6},{6,10},{10,14},{3,7},{... | collective-permute-start | bytes 626696 | tf_op jit(solution)/shard_map/ppermute | solution.py:819
  78.4 1.3 %collective-permute-start.14 = (s16[816,128]{1,0:T(8,128)(2,1)S(1)}, s16[816,128]{1,0:T(8,128)(2,1)S(1)}, u32[]{:S(2)}, u32[]{:S(2)}) collective-permute-start(s16[816,128]{1,0:T(8,128)(2,1)S(1)} %get-tuple-element.54), channel_id=1, source_target_pairs={{4,0},{8,4},{12,8},{5,1},{9,5},{13,9},{6,2},{10,6},{14,10},{7,3},{... | collective-permute-start | bytes 626696 | tf_op jit(solution)/shard_map/ppermute | solution.py:820
  79.7 2.9 %collective-permute-start.15 = (s16[272,128]{1,0:T(8,128)(2,1)S(1)}, s16[272,128]{1,0:T(8,128)(2,1)S(1)}, u32[]{:S(2)}, u32[]{:S(2)}) collective-permute-start(s16[272,128]{1,0:T(8,128)(2,1)S(1)} %get-tuple-element.55.refs_3_), channel_id=1, source_target_pairs={{0,8},{4,12},{8,0},{12,4},{1,9},{5,13},{9,1},{13,5},{2,10},{6,14},... | collective-permute-start | bytes 208904 | tf_op jit(solution)/shard_map/ppermute | solution.py:821
  82.6 4.3 %collective-permute-start.16 = (s16[272,128]{1,0:T(8,128)(2,1)S(1)}, s16[272,128]{1,0:T(8,128)(2,1)S(1)}, u32[]{:S(2)}, u32[]{:S(2)}) collective-permute-start(s16[272,128]{1,0:T(8,128)(2,1)S(1)} %get-tuple-element.55.refs_3_), channel_id=1, source_target_pairs={{0,12},{12,0},{1,13},{13,1},{2,14},{14,2},{3,15},{15,3},{16,28},{2... | collective-permute-start | bytes 208904 | tf_op jit(solution)/shard_map/ppermute | solution.py:821
  86.9 5.4 %collective-permute-done.15.refs_4_ = s16[272,128]{1,0:T(8,128)(2,1)S(1)} collective-permute-done((s16[272,128]{1,0:T(8,128)(2,1)S(1)}, s16[272,128]{1,0:T(8,128)(2,1)S(1)}, u32[]{:S(2)}, u32[]{:S(2)}) %collective-permute-start.15) | collective-permute-done | bytes 69664 | tf_op jit(solution)/shard_map/ppermute | solution.py:821
  92.3 0.0 collective-permute-done.16.refs_5_
  92.3 0.0 collective-permute-done.13.refs_1_.refs_0_
  92.3 0.0 collective-permute-done.14.refs_2_.refs_1_
  92.3 5.0 %inverse.3 = (s16[672,128]{1,0:T(8,128)(2,1)S(1)}, s16[672,128]{1,0:T(8,128)(2,1)S(1)}, s16[672,128]{1,0:T(8,128)(2,1)S(1)}, s16[672,128]{1,0:T(8,128)(2,1)S(1)}) custom-call(f32[18,256,128]{2,1,0:T(8,128)S(1)} %get-tuple-element.52.refs_0_, s16[816,128]{1,0:T(8,128)(2,1)S(1)} %collective-permute-done.13.refs_1_.refs_0_, ...), custom_call_target="tpu_custom_call" | custom-call | flops 301989888 | bytes 4718592 | tf_op jit(solution)/shard_map/inverse/pallas_call | solution.py:585
  97.3 0.1 collective-permute-start.17
  97.3 1.5 %collective-permute-start.18 = (s16[672,128]{1,0:T(8,128)(2,1)S(1)}, s16[672,128]{1,0:T(8,128)(2,1)S(1)}, u32[]{:S(2)}, u32[]{:S(2)}) collective-permute-start(s16[672,128]{1,0:T(8,128)(2,1)S(1)} %get-tuple-element.58), channel_id=1, source_target_pairs={{0,2},{1,3},{2,0},{3,1},{4,6},{5,7},{6,4},{7,5},{8,10},{9,11},{10,... | collective-permute-start | bytes 516104 | tf_op jit(solution)/shard_map/ppermute | solution.py:811
  98.9 0.3 collective-permute-start.19
  99.2 1.0 near_field.3.refs_9_
  100.2 0.0 collective-permute-done.17.refs_1_
  100.2 4.3 %collective-permute-done.18.refs_2_ = s16[672,128]{1,0:T(8,128)(2,1)S(1)} collective-permute-done((s16[672,128]{1,0:T(8,128)(2,1)S(1)}, s16[672,128]{1,0:T(8,128)(2,1)S(1)}, u32[]{:S(2)}, u32[]{:S(2)}) %collective-permute-start.18) | collective-permute-done | bytes 172064 | tf_op jit(solution)/shard_map/ppermute | solution.py:811
  104.6 2.8 %collective-permute-done.19.refs_3_ = s16[672,128]{1,0:T(8,128)(2,1)S(1)} collective-permute-done((s16[672,128]{1,0:T(8,128)(2,1)S(1)}, s16[672,128]{1,0:T(8,128)(2,1)S(1)}, u32[]{:S(2)}, u32[]{:S(2)}) %collective-permute-start.19) | collective-permute-done | bytes 172064 | tf_op jit(solution)/shard_map/ppermute | solution.py:811
  107.4 5.0 %sample.3 = f32[2,512]{1,0:T(2,128)} custom-call(s32[512]{0:T(512)S(1)} %copy-done.11, s32[512]{0:T(512)S(1)} %bitcast.12, s16[672,128]{1,0:T(8,128)(2,1)S(1)} %get-tuple-element.56.refs_0_, s16[672,128]{1,0:T(8,128)(2,1)S(1)} %collective-permute-done.17.refs_1_, s16[672,128]{1,0:T(8,128)(2,1)S(1)} %collective-permute-done.18.refs_2_, ...), custom_call_target="tpu_custom_call" | custom-call | flops 169869312 | bytes 4194304 | tf_op jit(solution)/shard_map/sample/pallas_call | solution.py:686
  (24 shorter events, 0.1 us)
Async XLA Ops:
  0.0 19.6 %copy-start.3 = (bf16[256,480]{1,0:T(8,128)(2,1)S(1)}, bf16[256,480]{1,0:T(8,128)(2,1)}, u32[]{:S(2)}) copy-start(bf16[256,480]{1,0:T(8,128)(2,1)} %constant.112.clone.refs_4_) | copy-start | bytes 737284
  0.0 40.9 %copy-start.7 = (bf16[192,256]{1,0:T(8,128)(2,1)S(1)}, bf16[192,256]{1,0:T(8,128)(2,1)}, u32[]{:S(2)}) copy-start(bf16[192,256]{1,0:T(8,128)(2,1)} %constant.113.clone.refs_6_) | copy-start | bytes 294916
  0.0 40.9 %copy-start.8 = (bf16[192,256]{1,0:T(8,128)(2,1)S(1)}, bf16[192,256]{1,0:T(8,128)(2,1)}, u32[]{:S(2)}) copy-start(bf16[192,256]{1,0:T(8,128)(2,1)} %constant.114.clone.refs_7_) | copy-start | bytes 294916
  7.9 4.2 %collective-permute-start = (s16[672,128]{1,0:T(8,128)(2,1)}, s16[672,128]{1,0:T(8,128)(2,1)S(1)}, u32[]{:S(2)}, u32[]{:S(2)}) collective-permute-start(s16[672,128]{1,0:T(8,128)(2,1)} %get-tuple-element.34), channel_id=1, source_target_pairs={{0,1},{1,0},{2,3},{3,2},{4,5},{5,4},{6,7},{7,6},{8,9},{9,8},{10,11... | collective-permute-start | bytes 516104 | tf_op jit(solution)/shard_map/ppermute | solution.py:811
  8.4 8.0 %collective-permute-start.1 = (s16[672,128]{1,0:T(8,128)(2,1)}, s16[672,128]{1,0:T(8,128)(2,1)S(1)}, u32[]{:S(2)}, u32[]{:S(2)}) collective-permute-start(s16[672,128]{1,0:T(8,128)(2,1)} %get-tuple-element.35), channel_id=1, source_target_pairs={{0,2},{1,3},{2,0},{3,1},{4,6},{5,7},{6,4},{7,5},{8,10},{9,11},{10,... | collective-permute-start | bytes 516104 | tf_op jit(solution)/shard_map/ppermute | solution.py:811
  11.0 8.6 %collective-permute-start.2 = (s16[672,128]{1,0:T(8,128)(2,1)}, s16[672,128]{1,0:T(8,128)(2,1)S(1)}, u32[]{:S(2)}, u32[]{:S(2)}) collective-permute-start(s16[672,128]{1,0:T(8,128)(2,1)} %get-tuple-element.36), channel_id=1, source_target_pairs={{0,3},{1,2},{2,1},{3,0},{4,7},{5,6},{6,5},{7,4},{8,11},{9,10},{10,... | collective-permute-start | bytes 516104 | tf_op jit(solution)/shard_map/ppermute | solution.py:811
  19.6 0.9 copy-start.9
  20.5 27.4 %copy-start.15 = (s32[24]{0:T(128)S(1)}, s32[24]{0:T(128)}, u32[]{:S(2)}) copy-start(s32[24]{0:T(128)} %param.21) | copy-start | bytes 292
  20.5 27.4 %copy-start.16 = (s32[24]{0:T(128)S(1)}, s32[24]{0:T(128)}, u32[]{:S(2)}) copy-start(s32[24]{0:T(128)} %param.22) | copy-start | bytes 292
  20.5 27.5 %copy-start = (bf16[24,128,128]{2,1,0:T(8,128)(2,1)S(1)}, bf16[24,128,128]{2,1,0:T(8,128)(2,1)}, u32[]{:S(2)}) copy-start(bf16[24,128,128]{2,1,0:T(8,128)(2,1)} %refs_3_.3) | copy-start | bytes 2359300
  22.8 18.0 %collective-permute-start.3 = (s16[816,128]{1,0:T(8,128)(2,1)S(1)}, s16[816,128]{1,0:T(8,128)(2,1)S(1)}, u32[]{:S(2)}, u32[]{:S(2)}) collective-permute-start(s16[816,128]{1,0:T(8,128)(2,1)S(1)} %get-tuple-element.38), channel_id=1, source_target_pairs={{0,4},{4,8},{8,12},{1,5},{5,9},{9,13},{2,6},{6,10},{10,14},{3,7},{... | collective-permute-start | bytes 626696 | tf_op jit(solution)/shard_map/ppermute | solution.py:819
  26.4 14.5 %collective-permute-start.4 = (s16[816,128]{1,0:T(8,128)(2,1)S(1)}, s16[816,128]{1,0:T(8,128)(2,1)S(1)}, u32[]{:S(2)}, u32[]{:S(2)}) collective-permute-start(s16[816,128]{1,0:T(8,128)(2,1)S(1)} %get-tuple-element.39), channel_id=1, source_target_pairs={{4,0},{8,4},{12,8},{5,1},{9,5},{13,9},{6,2},{10,6},{14,10},{7,3},{... | collective-permute-start | bytes 626696 | tf_op jit(solution)/shard_map/ppermute | solution.py:820
  27.7 13.1 %collective-permute-start.5 = (s16[272,128]{1,0:T(8,128)(2,1)S(1)}, s16[272,128]{1,0:T(8,128)(2,1)S(1)}, u32[]{:S(2)}, u32[]{:S(2)}) collective-permute-start(s16[272,128]{1,0:T(8,128)(2,1)S(1)} %get-tuple-element.40.refs_3_), channel_id=1, source_target_pairs={{0,8},{4,12},{8,0},{12,4},{1,9},{5,13},{9,1},{13,5},{2,10},{6,14},... | collective-permute-start | bytes 208904 | tf_op jit(solution)/shard_map/ppermute | solution.py:821
  31.4 9.4 %collective-permute-start.6 = (s16[272,128]{1,0:T(8,128)(2,1)S(1)}, s16[272,128]{1,0:T(8,128)(2,1)S(1)}, u32[]{:S(2)}, u32[]{:S(2)}) collective-permute-start(s16[272,128]{1,0:T(8,128)(2,1)S(1)} %get-tuple-element.40.refs_3_), channel_id=1, source_target_pairs={{0,12},{12,0},{1,13},{13,1},{2,14},{14,2},{3,15},{15,3},{16,28},{2... | collective-permute-start | bytes 208904 | tf_op jit(solution)/shard_map/ppermute | solution.py:821
  40.9 15.2 %copy-start.1 = (bf16[4,128,256]{2,1,0:T(8,128)(2,1)S(1)}, bf16[4,128,256]{2,1,0:T(8,128)(2,1)}, u32[]{:S(2)}) copy-start(bf16[4,128,256]{2,1,0:T(8,128)(2,1)} %constant.115.clone.refs_4_) | copy-start | bytes 786436
  40.9 15.2 %copy-start.2 = (bf16[4,128,256]{2,1,0:T(8,128)(2,1)S(1)}, bf16[4,128,256]{2,1,0:T(8,128)(2,1)}, u32[]{:S(2)}) copy-start(bf16[4,128,256]{2,1,0:T(8,128)(2,1)} %constant.116.clone.refs_5_) | copy-start | bytes 786436
  40.9 15.2 %copy-start.6 = (f32[256,128]{1,0:T(8,128)S(1)}, f32[256,128]{1,0:T(8,128)}, u32[]{:S(2)}) copy-start(f32[256,128]{1,0:T(8,128)} %get-tuple-element.45.refs_6_) | copy-start | bytes 393220
  40.9 15.2 %copy-start.11 = (s32[512]{0:T(512)S(1)}, s32[512]{0:T(512)}, u32[]{:S(2)}) copy-start(s32[512]{0:T(512)} %fusion.2.refs_1_.row_ref) | copy-start | bytes 6148
  40.9 15.2 %copy-start.12 = (s32[1,512]{1,0:T(1,128)S(1)}, s32[1,512]{1,0:T(1,128)}, u32[]{:S(2)}) copy-start(s32[1,512]{1,0:T(1,128)} %get-tuple-element.61) | copy-start | bytes 6148
  41.0 15.2 %copy-start.13 = (f32[512]{0:T(512)S(1)}, f32[512]{0:T(512)}, u32[]{:S(2)}) copy-start(f32[512]{0:T(512)} %refs_0_.1) | copy-start | bytes 6148
  41.0 15.2 %copy-start.14 = (s32[512]{0:T(512)S(1)}, s32[512]{0:T(512)}, u32[]{:S(2)}) copy-start(s32[512]{0:T(512)} %param.17) | copy-start | bytes 6148
  41.0 19.6 %copy-start.4 = (bf16[4,256,128]{2,1,0:T(8,128)(2,1)S(1)}, bf16[4,256,128]{2,1,0:T(8,128)(2,1)}, u32[]{:S(2)}) copy-start(bf16[4,256,128]{2,1,0:T(8,128)(2,1)} %constant.110.clone.refs_4_) | copy-start | bytes 786436
  41.0 19.6 %copy-start.5 = (bf16[4,256,128]{2,1,0:T(8,128)(2,1)S(1)}, bf16[4,256,128]{2,1,0:T(8,128)(2,1)}, u32[]{:S(2)}) copy-start(bf16[4,256,128]{2,1,0:T(8,128)(2,1)} %constant.111.clone.refs_5_) | copy-start | bytes 786436
  41.0 19.6 %copy-start.10 = (f32[256,128]{1,0:T(8,128)S(1)}, f32[256,128]{1,0:T(8,128)}, u32[]{:S(2)}) copy-start(f32[256,128]{1,0:T(8,128)} %get-tuple-element.47.refs_6_) | copy-start | bytes 393220
  46.0 3.0 %collective-permute-start.7 = (s16[672,128]{1,0:T(8,128)(2,1)S(1)}, s16[672,128]{1,0:T(8,128)(2,1)S(1)}, u32[]{:S(2)}, u32[]{:S(2)}) collective-permute-start(s16[672,128]{1,0:T(8,128)(2,1)S(1)} %get-tuple-element.42), channel_id=1, source_target_pairs={{0,1},{1,0},{2,3},{3,2},{4,5},{5,4},{6,7},{7,6},{8,9},{9,8},{10,11... | collective-permute-start | bytes 516104 | tf_op jit(solution)/shard_map/ppermute | solution.py:811
  46.1 7.2 %collective-permute-start.8 = (s16[672,128]{1,0:T(8,128)(2,1)S(1)}, s16[672,128]{1,0:T(8,128)(2,1)S(1)}, u32[]{:S(2)}, u32[]{:S(2)}) collective-permute-start(s16[672,128]{1,0:T(8,128)(2,1)S(1)} %get-tuple-element.43), channel_id=1, source_target_pairs={{0,2},{1,3},{2,0},{3,1},{4,6},{5,7},{6,4},{7,5},{8,10},{9,11},{10,... | collective-permute-start | bytes 516104 | tf_op jit(solution)/shard_map/ppermute | solution.py:811
  47.6 8.5 %collective-permute-start.9 = (s16[672,128]{1,0:T(8,128)(2,1)S(1)}, s16[672,128]{1,0:T(8,128)(2,1)S(1)}, u32[]{:S(2)}, u32[]{:S(2)}) collective-permute-start(s16[672,128]{1,0:T(8,128)(2,1)S(1)} %get-tuple-element.44), channel_id=1, source_target_pairs={{0,3},{1,2},{2,1},{3,0},{4,7},{5,6},{6,5},{7,4},{8,11},{9,10},{10,... | collective-permute-start | bytes 516104 | tf_op jit(solution)/shard_map/ppermute | solution.py:811
  64.9 1.9 %collective-permute-start.10 = (s16[672,128]{1,0:T(8,128)(2,1)S(1)}, s16[672,128]{1,0:T(8,128)(2,1)S(1)}, u32[]{:S(2)}, u32[]{:S(2)}) collective-permute-start(s16[672,128]{1,0:T(8,128)(2,1)S(1)} %get-tuple-element.49), channel_id=1, source_target_pairs={{0,1},{1,0},{2,3},{3,2},{4,5},{5,4},{6,7},{7,6},{8,9},{9,8},{10,11... | collective-permute-start | bytes 516104 | tf_op jit(solution)/shard_map/ppermute | solution.py:811
  65.2 7.2 %collective-permute-start.11 = (s16[672,128]{1,0:T(8,128)(2,1)S(1)}, s16[672,128]{1,0:T(8,128)(2,1)S(1)}, u32[]{:S(2)}, u32[]{:S(2)}) collective-permute-start(s16[672,128]{1,0:T(8,128)(2,1)S(1)} %get-tuple-element.50), channel_id=1, source_target_pairs={{0,2},{1,3},{2,0},{3,1},{4,6},{5,7},{6,4},{7,5},{8,10},{9,11},{10,... | collective-permute-start | bytes 516104 | tf_op jit(solution)/shard_map/ppermute | solution.py:811
  66.7 8.0 %collective-permute-start.12 = (s16[672,128]{1,0:T(8,128)(2,1)S(1)}, s16[672,128]{1,0:T(8,128)(2,1)S(1)}, u32[]{:S(2)}, u32[]{:S(2)}) collective-permute-start(s16[672,128]{1,0:T(8,128)(2,1)S(1)} %get-tuple-element.51), channel_id=1, source_target_pairs={{0,3},{1,2},{2,1},{3,0},{4,7},{5,6},{6,5},{7,4},{8,11},{9,10},{10,... | collective-permute-start | bytes 516104 | tf_op jit(solution)/shard_map/ppermute | solution.py:811
  77.1 15.2 %collective-permute-start.13 = (s16[816,128]{1,0:T(8,128)(2,1)S(1)}, s16[816,128]{1,0:T(8,128)(2,1)S(1)}, u32[]{:S(2)}, u32[]{:S(2)}) collective-permute-start(s16[816,128]{1,0:T(8,128)(2,1)S(1)} %get-tuple-element.53), channel_id=1, source_target_pairs={{0,4},{4,8},{8,12},{1,5},{5,9},{9,13},{2,6},{6,10},{10,14},{3,7},{... | collective-permute-start | bytes 626696 | tf_op jit(solution)/shard_map/ppermute | solution.py:819
  78.4 13.8 %collective-permute-start.14 = (s16[816,128]{1,0:T(8,128)(2,1)S(1)}, s16[816,128]{1,0:T(8,128)(2,1)S(1)}, u32[]{:S(2)}, u32[]{:S(2)}) collective-permute-start(s16[816,128]{1,0:T(8,128)(2,1)S(1)} %get-tuple-element.54), channel_id=1, source_target_pairs={{4,0},{8,4},{12,8},{5,1},{9,5},{13,9},{6,2},{10,6},{14,10},{7,3},{... | collective-permute-start | bytes 626696 | tf_op jit(solution)/shard_map/ppermute | solution.py:820
  79.7 12.5 %collective-permute-start.15 = (s16[272,128]{1,0:T(8,128)(2,1)S(1)}, s16[272,128]{1,0:T(8,128)(2,1)S(1)}, u32[]{:S(2)}, u32[]{:S(2)}) collective-permute-start(s16[272,128]{1,0:T(8,128)(2,1)S(1)} %get-tuple-element.55.refs_3_), channel_id=1, source_target_pairs={{0,8},{4,12},{8,0},{12,4},{1,9},{5,13},{9,1},{13,5},{2,10},{6,14},... | collective-permute-start | bytes 208904 | tf_op jit(solution)/shard_map/ppermute | solution.py:821
  82.6 9.7 %collective-permute-start.16 = (s16[272,128]{1,0:T(8,128)(2,1)S(1)}, s16[272,128]{1,0:T(8,128)(2,1)S(1)}, u32[]{:S(2)}, u32[]{:S(2)}) collective-permute-start(s16[272,128]{1,0:T(8,128)(2,1)S(1)} %get-tuple-element.55.refs_3_), channel_id=1, source_target_pairs={{0,12},{12,0},{1,13},{13,1},{2,14},{14,2},{3,15},{15,3},{16,28},{2... | collective-permute-start | bytes 208904 | tf_op jit(solution)/shard_map/ppermute | solution.py:821
  97.3 3.0 %collective-permute-start.17 = (s16[672,128]{1,0:T(8,128)(2,1)S(1)}, s16[672,128]{1,0:T(8,128)(2,1)S(1)}, u32[]{:S(2)}, u32[]{:S(2)}) collective-permute-start(s16[672,128]{1,0:T(8,128)(2,1)S(1)} %get-tuple-element.57), channel_id=1, source_target_pairs={{0,1},{1,0},{2,3},{3,2},{4,5},{5,4},{6,7},{7,6},{8,9},{9,8},{10,11... | collective-permute-start | bytes 516104 | tf_op jit(solution)/shard_map/ppermute | solution.py:811
  97.3 7.2 %collective-permute-start.18 = (s16[672,128]{1,0:T(8,128)(2,1)S(1)}, s16[672,128]{1,0:T(8,128)(2,1)S(1)}, u32[]{:S(2)}, u32[]{:S(2)}) collective-permute-start(s16[672,128]{1,0:T(8,128)(2,1)S(1)} %get-tuple-element.58), channel_id=1, source_target_pairs={{0,2},{1,3},{2,0},{3,1},{4,6},{5,7},{6,4},{7,5},{8,10},{9,11},{10,... | collective-permute-start | bytes 516104 | tf_op jit(solution)/shard_map/ppermute | solution.py:811
  98.9 8.5 %collective-permute-start.19 = (s16[672,128]{1,0:T(8,128)(2,1)S(1)}, s16[672,128]{1,0:T(8,128)(2,1)S(1)}, u32[]{:S(2)}, u32[]{:S(2)}) collective-permute-start(s16[672,128]{1,0:T(8,128)(2,1)S(1)} %get-tuple-element.59), channel_id=1, source_target_pairs={{0,3},{1,2},{2,1},{3,0},{4,7},{5,6},{6,5},{7,4},{8,11},{9,10},{10,... | collective-permute-start | bytes 516104 | tf_op jit(solution)/shard_map/ppermute | solution.py:811

commit v4 on v3

--- a/solution.py
+++ b/solution.py
@@ -165,7 +165,7 @@
         halves(z_forward),
         halves(z_inverse),
         y_forward,
-        halves(y_inverse.reshape(-1, GRID)),
+        halves(y_inverse),
         modes,
     )
 
@@ -211,47 +211,85 @@
     return (2 * reach_x - 2) * reach_y
 
 
-def add_panels(reach, vector_ref, row_ref, depth_ref, coeff_ref, grids):
+def in_window(lanes, depth):
+    return ((lanes - depth) & -4) == 0
+
+
+def add_panels(reach, woven, vector_ref, place_ref, weight_ref, grids):
     lanes = lax.broadcasted_iota(jnp.int32, (8, REGION), 1)
 
     def body(group, carry):
         at = pl.multiple_of(group * 16, 16)
-        coeff = [coeff_ref[pl.ds(at, 8), :], coeff_ref[pl.ds(at + 8, 8), :]]
+        coeff = [weight_ref[pl.ds(at + 8 * q, 8), :] for q in range(2)] if woven else None
         for local in range(GROUP):
             panel = group * GROUP + local
             grid = grids[local % len(grids)]
-            row = row_ref[panel]
-            depth = depth_ref[panel]
-            shift = (depth - 4 * local) & (REGION - 1)
-            value = jnp.where(((lanes - depth) & -4) == 0, vector_ref[panel], 0.0)
+            row = place_ref[0, panel]
+            value = vector_ref[panel]
+            if woven:
+                depth = place_ref[1, panel]
+                shift = (depth - 4 * local) & (REGION - 1)
+                value = jnp.where(in_window(lanes, depth), value, 0.0)
+                lines = [pltpu.roll(coeff[q], shift, 1) for q in range(2)]
+            else:
+                first = pl.multiple_of(panel * 16, 16)
+                lines = [weight_ref[pl.ds(first + 8 * q, 8), :] for q in range(2)]
             places = [pl.ds(row, 8), pl.ds(row + 2 * reach, 8)]
             held = [grid[place, :] for place in places]
             for q in range(2):
-                grid[places[q], :] = held[q] + pltpu.roll(coeff[q], shift, 1) * value
+                grid[places[q], :] = held[q] + lines[q] * value
         return carry
 
     lax.fori_loop(0, vector_ref.shape[0] // GROUP, body, 0)
 
 
-def spread_kernel(first, reach_x, reach_y, pieces, tiles, *refs):
-    vector_ref, row_ref, depth_ref, rounded_ref, high_ref, low_ref = refs[:6]
-    refs = refs[6:]
+def send_pieces(outs, flips, head, rounded, both, high_ref, low_ref):
+    blocks = rounded.shape[0]
+    mantissa, exponent = encode_rounded(rounded)
+    head[...] = jnp.zeros_like(head)
+    head[2 : 2 + blocks, :] = mantissa
+    head[2 + blocks : 2 + 2 * blocks, :] = exponent
+    mine = y_position()
+    for at in range(0, len(flips), 2):
+        pick = lambda ref: jnp.concatenate([ref[mine ^ flip] for flip in flips[at : at + 2]], axis=1)
+        result = dot_three(both, (pick(high_ref), pick(low_ref)))
+        for i, out in enumerate(outs[at : at + 2]):
+            send_piece(out, head, result[:, i * 2 * HALF : (i + 1) * 2 * HALF])
+
+
+def spread_kernel(first, reach_x, reach_y, flips, tiles, *refs):
+    vector_ref, rounded_ref, high_ref, low_ref = refs[:4]
+    refs = refs[4:]
     if first:
-        flag_ref, sample_refs, dipole_refs = refs[0], refs[1 : 1 + tiles], refs[1 + tiles : 1 + 2 * tiles]
-        refs = refs[1 + 2 * tiles :]
+        stencil_ref, flag_ref = refs[:2]
+        sample_refs, dipole_refs = refs[2 : 2 + tiles], refs[2 + tiles : 2 + 2 * tiles]
+        refs = refs[2 + 2 * tiles :]
     else:
-        coeff_ref = refs[0]
-        refs = refs[1:]
-    outs, refs = refs[:pieces], refs[pieces:]
+        place_ref, weight_ref = refs[:2]
+        refs = refs[2:]
+    outs, (wide_high, wide_low), refs = refs[: len(flips)], refs[len(flips) :][:2], refs[len(flips) + 2 :]
     if first:
-        coeff_ref, sample_coeff_ref = refs[:2]
-        refs = refs[2:]
-        weave(flag_ref[...], sample_refs, dipole_refs, coeff_ref, sample_coeff_ref)
+        weight_ref, sample_coeff_ref, places_out = refs[:3]
+        place_ref, sem = refs[-2:]
+        refs = refs[3:-2]
+        span_x, span_y = reach_x - 4, reach_y - 4
+        local_x = stencil_ref[0:1, :] - (lax.axis_index("wide") * span_x - 2)
+        local_y = stencil_ref[1:2, :] - (y_position() * span_y - 2)
+        odd = local_x & 1
+        places_out[0:1, :] = (
+            odd * (reach_x * reach_y) + (local_x >> 1) * (2 * reach_y) + 2 * local_y
+        )
+        places_out[1:2, :] = stencil_ref[2:3, :]
+        copy = pltpu.make_async_copy(places_out, place_ref, sem)
+        copy.start()
     head, total = refs[:2]
     grids = refs[2:]
     for grid in grids:
         grid[...] = jnp.zeros_like(grid)
-    add_panels(reach_y, vector_ref, row_ref, depth_ref, coeff_ref, grids)
+    if first:
+        weave(flag_ref[...], sample_refs, dipole_refs, weight_ref, sample_coeff_ref)
+        copy.wait()
+    add_panels(reach_y, first, vector_ref, place_ref, weight_ref, grids)
     for x in range(reach_x):
         parts = [
             grid[pl.ds(row, reach_y, stride=2), :]
@@ -261,57 +299,52 @@
         total[x * reach_y : (x + 1) * reach_y, :] = sum(parts[1:], parts[0])
     half = reach_x * reach_y // 2
     both = jnp.concatenate([total[:half, :], total[half:, :]], axis=1)
-    extra = outs[0].shape[0] - head.shape[0] - half
+    extra = wide_high.shape[0] - half
     if extra:
         both = jnp.concatenate([both, jnp.zeros((extra, 2 * REGION), F32)], axis=0)
-    both = split(both)
-    blocks = rounded_ref.shape[0]
-    mantissa, exponent = encode_rounded(rounded_ref[...])
-    head[...] = jnp.zeros_like(head)
-    head[2 : 2 + blocks, :] = mantissa
-    head[2 + blocks : 2 + 2 * blocks, :] = exponent
-    mine = y_position()
-    for piece in range(0, pieces, 2):
-        pick = lambda ref: jnp.concatenate([ref[mine ^ piece], ref[mine ^ (piece + 1)]], axis=1)
-        result = dot_three(both, (pick(high_ref), pick(low_ref)))
-        send_piece(outs[piece], head, result[:, : 2 * HALF])
-        send_piece(outs[piece + 1], head, result[:, 2 * HALF :])
-
-
-def spread(vector, rows, depths, table, coeff, raw, reach_x, reach_y):
-    pieces = table[0].shape[0]
+    high, low = split(both)
+    wide_high[...] = high
+    wide_low[...] = low
+    send_pieces(outs, flips, head, rounded_ref[...], (high, low), high_ref, low_ref)
+
+
+def spread(vector, places, table, lines, raw, reach_x, reach_y, flips):
     count = vector.shape[0]
     half = reach_x * reach_y // 2
     blocks = count // BLOCK
     top = up_to(2 + 2 * blocks, 16)
     lanes = 2 * HALF
     constant = lambda shape: pl.BlockSpec(shape, lambda i: (0,) * len(shape))
-    piece = (top + up_to(half, 16), lanes)
+    body = up_to(half, 16)
     woven = (count // GROUP * 16, BLOCK)
-    out_shapes = [jax.ShapeDtypeStruct(piece, jnp.int16)] * pieces
-    operands = [vector, rows, depths, vector.reshape(blocks, BLOCK), *table]
-    in_specs = [in_smem()] * 3 + [constant(value.shape) for value in operands[3:]]
-    first = coeff is None
+    out_shapes = [jax.ShapeDtypeStruct((top + body, lanes), jnp.int16)] * len(flips)
+    out_shapes += [jax.ShapeDtypeStruct((body, 2 * REGION), BF16)] * 2
+    operands = [vector, vector.reshape(blocks, BLOCK), *table]
+    in_specs = [in_smem()] + [constant(value.shape) for value in operands[1:]]
+    scratch = [
+        pltpu.VMEM((top, lanes), F32),
+        pltpu.VMEM((reach_x * reach_y, REGION), F32),
+    ] + [pltpu.VMEM((pair_count(reach_x, reach_y), REGION), F32)] * CHAINS
+    first = lines is None
     if first:
-        flag, sample, dipole = raw
+        stencil, flag, sample, dipole = raw
         tile = lambda t: pl.BlockSpec((64, BLOCK), lambda i: (0, t))
-        operands += [flag.reshape(1, -1)] + [sample] * blocks + [dipole] * blocks
-        in_specs += [constant((1, count))] + [tile(t) for t in range(blocks)] * 2
+        operands += [stencil, flag.reshape(1, -1)] + [sample] * blocks + [dipole] * blocks
+        in_specs += [constant(stencil.shape), constant((1, count))]
+        in_specs += [tile(t) for t in range(blocks)] * 2
         out_shapes += [jax.ShapeDtypeStruct(woven, F32)] * 2
+        out_shapes += [jax.ShapeDtypeStruct((2, count), jnp.int32)]
+        scratch += [pltpu.SMEM((2, count), jnp.int32), pltpu.SemaphoreType.DMA]
     else:
-        operands.append(coeff)
-        in_specs.append(constant(woven))
+        operands += [places, lines]
+        in_specs += [in_smem(), whole_vmem()]
     return pl.pallas_call(
-        functools.partial(spread_kernel, first, reach_x, reach_y, pieces, blocks),
+        functools.partial(spread_kernel, first, reach_x, reach_y, flips, blocks),
         grid=(1,),
         in_specs=in_specs,
         out_specs=[constant(out.shape) for out in out_shapes],
         out_shape=out_shapes,
-        scratch_shapes=[
-            pltpu.VMEM((top, lanes), F32),
-            pltpu.VMEM((reach_x * reach_y, REGION), F32),
-        ]
-        + [pltpu.VMEM((pair_count(reach_x, reach_y), REGION), F32)] * CHAINS,
+        scratch_shapes=scratch,
         compiler_params=pltpu.CompilerParams(
             vmem_limit_bytes=START_LIMIT if first else VMEM_LIMIT
         ),
@@ -320,11 +353,66 @@
     )(*operands)
 
 
+def spread_rest_kernel(flips, rounded_ref, wide_high, wide_low, high_ref, low_ref, *refs):
+    outs, head = refs[:-1], refs[-1]
+    both = (wide_high[...], wide_low[...])
+    send_pieces(outs, flips, head, rounded_ref[...], both, high_ref, low_ref)
+
+
+def spread_rest(vector, both, table, flips):
+    blocks = vector.shape[0] // BLOCK
+    top = up_to(2 + 2 * blocks, 16)
+    shape = (top + both[0].shape[0], 2 * HALF)
+    return pl.pallas_call(
+        functools.partial(spread_rest_kernel, flips),
+        in_specs=[whole_vmem()] * 5,
+        out_specs=[whole_vmem()] * len(flips),
+        out_shape=[jax.ShapeDtypeStruct(shape, jnp.int16)] * len(flips),
+        scratch_shapes=[pltpu.VMEM((top, 2 * HALF), F32)],
+        compiler_params=params(),
+        cost_estimate=cost(2 * shape[0] * 256 * 256 * 3, 4 * shape[0] * 512),
+        name="spread_rest",
+    )(vector.reshape(blocks, BLOCK), *both, *table)
+
+
+def lines_kernel(place_ref, coeff_ref, out_ref):
+    lanes = lax.broadcasted_iota(jnp.int32, (8, REGION), 1)
+
+    def body(group, carry):
+        at = pl.multiple_of(group * 16, 16)
+        coeff = [coeff_ref[pl.ds(at + 8 * q, 8), :] for q in range(2)]
+        for local in range(GROUP):
+            panel = group * GROUP + local
+            depth = place_ref[1, panel]
+            shift = (depth - 4 * local) & (REGION - 1)
+            inside = in_window(lanes, depth)
+            for q in range(2):
+                first = pl.multiple_of(panel * 16 + 8 * q, 8)
+                out_ref[pl.ds(first, 8), :] = jnp.where(inside, pltpu.roll(coeff[q], shift, 1), 0.0)
+        return carry
+
+    lax.fori_loop(0, place_ref.shape[1] // GROUP, body, 0)
+
+
+def place_lines(places, coeff):
+    count = places.shape[1]
+    shape = (count * 16, REGION)
+    return pl.pallas_call(
+        lines_kernel,
+        in_specs=[in_smem(), whole_vmem()],
+        out_specs=whole_vmem(),
+        out_shape=jax.ShapeDtypeStruct(shape, F32),
+        compiler_params=params(),
+        cost_estimate=cost(16 * count * REGION, 4 * 16 * count * REGION),
+        name="place_lines",
+    )(places, coeff)
+
+
 def forward_kernel(reach_x, reach_y, blocks, pieces, *refs):
     parts = refs[:pieces]
     table_ref, modes_ref = refs[pieces : pieces + 2]
-    spectrum, right_out, left_out, own_out, peers_out = refs[pieces + 2 : pieces + 7]
-    opened, stacked, slabs, head = refs[pieces + 7 :]
+    spectrum, right_out, left_out, own_out, peers_out, inner_out = refs[pieces + 2 : pieces + 8]
+    opened, stacked, slabs, head = refs[pieces + 8 :]
     half = reach_x // 2
     pitch = up_to(reach_y, 8)
     tall = pieces * pitch
@@ -388,6 +476,7 @@
             if i == 4:
                 cut_left = run
         left = run
+        inner_out[rows, :] = jnp.where(low, right, left)
         swapped_right, swapped_left = swap(right), swap(left)
         own = jnp.where(low, left + across_half * swapped_left, right + across_half * swapped_right)
         made = [
@@ -435,13 +524,14 @@
     return pl.pallas_call(
         functools.partial(forward_kernel, reach_x, reach_y, blocks, pieces),
         in_specs=[whole_vmem()] * (pieces + 2),
-        out_specs=[whole_vmem()] * 5,
+        out_specs=[whole_vmem()] * 6,
         out_shape=[
             jax.ShapeDtypeStruct((half, GRID, lanes), F32),
             short(head + 3 * GRID),
             short(head + 3 * GRID),
             short(16 + GRID),
             jax.ShapeDtypeStruct((pieces * blocks, BLOCK), F32),
+            jax.ShapeDtypeStruct((GRID, lanes), F32),
         ],
         scratch_shapes=[
             pltpu.VMEM((body, lanes), F32),
@@ -455,15 +545,37 @@
     )(*parts, table, modes)
 
 
-def inverse_kernel(reach_x, reach_y, pieces, fars, *refs):
-    spectrum, from_left, from_right, own_ref = refs[:4]
-    far_refs = refs[4 : 4 + fars]
-    high_ref, low_ref, modes_ref = refs[4 + fars : 7 + fars]
-    outs = refs[7 + fars : 7 + fars + pieces]
-    field, blocks_out, ready, head = refs[7 + fars + pieces :]
+def send_fields(outs, flips, reach_y, field_high, field_low, high_ref, low_ref, ready, head):
+    half = field_high.shape[0]
+    mine = y_position()
+    pitch = up_to(reach_y, 16)
+    pick = lambda ref: jnp.concatenate([ref[mine ^ flip] for flip in flips], axis=0)
+    table = (pick(high_ref), pick(low_ref))
+    for i in range(0, half, 2):
+        many = min(2, half - i)
+        join = lambda ref: jnp.concatenate([ref[i + j] for j in range(many)], axis=1)
+        result = dot_three(table, (join(field_high), join(field_low)))
+        for j in range(many):
+            for piece in range(len(flips)):
+                ready[piece, (i + j) * reach_y : (i + j + 1) * reach_y, :] = result[
+                    piece * pitch : piece * pitch + reach_y, j * 2 * HALF : (j + 1) * 2 * HALF
+                ]
+    head[...] = jnp.zeros_like(head)
+    for piece, out in enumerate(outs):
+        if ready.shape[1] > half * reach_y:
+            ready[piece, half * reach_y :, :] = jnp.zeros_like(ready[piece, half * reach_y :, :])
+        send_piece(out, head, ready[piece])
+
+
+def inverse_kernel(reach_x, reach_y, flips, fars, *refs):
+    spectrum, from_left, from_right, own_ref, inner_ref = refs[:5]
+    far_refs = refs[5 : 5 + fars]
+    high_ref, low_ref, modes_ref = refs[5 + fars : 8 + fars]
+    outs = refs[8 + fars : 8 + fars + len(flips)]
+    field_high, field_low, ready, head = refs[8 + fars + len(flips) :]
     half = reach_x // 2
     span = reach_x - 4
-    chunk = 16
+    chunk = 32
     head_rows = from_left.shape[0] - 3 * GRID
     x_count = lax.axis_size("wide")
     x_index = lax.axis_index("wide")
@@ -501,6 +613,7 @@
         ring = modes_ref[2, rows, :]
         gain = modes_ref[3, rows, :]
         across_half = jnp.exp(half * log_decay)
+        across_cut = jnp.exp((half - 4) * log_decay)
         around = jnp.exp((GRID - 4) * log_decay)
         beside = jnp.exp((GRID - reach_x - span) * log_decay)
         layers = [spectrum[i, rows, :] for i in range(half)]
@@ -536,67 +649,72 @@
         for far in range(fars):
             power = jnp.where(low, powers[far][0], powers[far][1])
             total = total + moment(far_refs[far], far_units[far]) * jnp.exp(power * log_decay)
-        entering = (swap(total) + around * jnp.where(low, head_sum, tail_sum)) * ring
-        run = layers[0]
-        for i in range(1, half):
-            run = decay * run + layers[i]
-        right_start = jnp.where(low, entering, swap(across_half * entering + run))
-        run = layers[half - 1]
-        for i in range(half - 2, -1, -1):
-            run = decay * run + layers[i]
-        left_start = jnp.where(low, swap(across_half * entering + run), entering)
-        run = right_start
+        shared = jnp.where(low, head_sum, tail_sum)
+        entering = (swap(total) + around * shared) * ring
+        leaving = swap(across_half * entering + across_cut * shared + inner_ref[rows, :])
+        run = jnp.where(low, entering, leaving)
         forward_runs = []
         for i in range(half):
             run = decay * run + layers[i]
             forward_runs.append(run)
-        run = left_start
+        run = jnp.where(low, leaving, entering)
         for i in range(half - 1, -1, -1):
             ahead = decay * run
-            field[i, rows, :] = gain * (forward_runs[i] + ahead)
+            high, rest = split(gain * (forward_runs[i] + ahead))
+            field_high[i, rows, :] = high
+            field_low[i, rows, :] = rest
             run = ahead + layers[i]
         return carry
 
     lax.fori_loop(0, GRID // chunk, body, 0)
-    table = (high_ref[...], low_ref[...])
-    pitch = up_to(reach_y, 16)
-    for i in range(0, half, 2):
-        if i + 1 < half:
-            pair = dot_three(table, split(jnp.concatenate([field[i], field[i + 1]], axis=1)))
-            blocks_out[i] = pair[:, : 2 * HALF]
-            blocks_out[i + 1] = pair[:, 2 * HALF :]
-        else:
-            blocks_out[i] = dot_three(table, split(field[i]))
-    mine = y_position()
-    if ready.shape[0] > half * reach_y:
-        ready[half * reach_y :, :] = jnp.zeros_like(ready[half * reach_y :, :])
-    head[...] = jnp.zeros_like(head)
-    for piece in range(pieces):
-        place = pl.ds(pl.multiple_of((mine ^ piece) * pitch, 16), reach_y)
-        for i in range(half):
-            ready[i * reach_y : (i + 1) * reach_y, :] = blocks_out[i, place, :]
-        send_piece(outs[piece], head, ready[...])
-
-
-def inverse(spectrum, from_left, from_right, own, fars, table, modes, reach_x, reach_y, pieces):
+    send_fields(outs, flips, reach_y, field_high, field_low, high_ref, low_ref, ready, head)
+
+
+def inverse(
+    spectrum, from_left, from_right, own, inner, fars, table, modes, reach_x, reach_y, flips
+):
     half = reach_x // 2
     lanes = 2 * HALF
     body = up_to(half * reach_y, 16)
+    shapes = [jax.ShapeDtypeStruct((16 + body, lanes), jnp.int16)] * len(flips)
+    shapes += [jax.ShapeDtypeStruct((half, GRID, lanes), BF16)] * 2
     return pl.pallas_call(
-        functools.partial(inverse_kernel, reach_x, reach_y, pieces, len(fars)),
-        in_specs=[whole_vmem()] * (7 + len(fars)),
-        out_specs=[whole_vmem()] * pieces,
-        out_shape=[jax.ShapeDtypeStruct((16 + body, lanes), jnp.int16)] * pieces,
+        functools.partial(inverse_kernel, reach_x, reach_y, flips, len(fars)),
+        in_specs=[whole_vmem()] * (8 + len(fars)),
+        out_specs=[whole_vmem()] * len(shapes),
+        out_shape=shapes,
         scratch_shapes=[
-            pltpu.VMEM((half, GRID, lanes), F32),
-            pltpu.VMEM((half, pieces * up_to(reach_y, 16), lanes), F32),
-            pltpu.VMEM((body, lanes), F32),
+            pltpu.VMEM((len(flips), body, lanes), F32),
             pltpu.VMEM((16, lanes), F32),
         ],
         compiler_params=params(),
         cost_estimate=cost(2 * half * 256 * 256 * 128, 4 * half * GRID * lanes * 2),
         name="inverse",
-    )(spectrum, from_left, from_right, own, *fars, *table, modes)
+    )(spectrum, from_left, from_right, own, inner, *fars, *table, modes)
+
+
+def inverse_rest_kernel(reach_y, flips, field_high, field_low, high_ref, low_ref, *refs):
+    outs, (ready, head) = refs[: len(flips)], refs[len(flips) :]
+    send_fields(outs, flips, reach_y, field_high, field_low, high_ref, low_ref, ready, head)
+
+
+def inverse_rest(field, table, reach_y, flips):
+    half = field[0].shape[0]
+    lanes = 2 * HALF
+    body = up_to(half * reach_y, 16)
+    return pl.pallas_call(
+        functools.partial(inverse_rest_kernel, reach_y, flips),
+        in_specs=[whole_vmem()] * 4,
+        out_specs=[whole_vmem()] * len(flips),
+        out_shape=[jax.ShapeDtypeStruct((16 + body, lanes), jnp.int16)] * len(flips),
+        scratch_shapes=[
+            pltpu.VMEM((len(flips), body, lanes), F32),
+            pltpu.VMEM((16, lanes), F32),
+        ],
+        compiler_params=params(),
+        cost_estimate=cost(2 * half * 256 * 256 * 128, 4 * half * GRID * lanes * 2),
+        name="inverse_rest",
+    )(*field, *table)
 
 
 def sum_rows(values):
@@ -616,9 +734,9 @@
     return values[0]
 
 
-def sample_kernel(last, reach_x, reach_y, pieces, row_ref, depth_ref, *refs):
+def sample_kernel(last, reach_x, reach_y, pieces, place_ref, *refs):
     parts = refs[:pieces]
-    high_ref, low_ref, coeff_ref, own_ref, vector_ref, near_ref, out_ref, flat, field, sums = refs[
+    high_ref, low_ref, line_ref, own_ref, vector_ref, near_ref, out_ref, flat, field, sums = refs[
         pieces:
     ]
     mine = y_position()
@@ -636,27 +754,22 @@
         layer = flat[x * reach_y : (x + 1) * reach_y, :]
         for row in pair_rows(x, reach_x, reach_y):
             field[pl.ds(row, reach_y, stride=2), :] = layer
-    lanes = lax.broadcasted_iota(jnp.int32, (8, REGION), 1)
+    count = place_ref.shape[1]
 
     def body(group, carry):
-        at = pl.multiple_of(group * 16, 16)
-        coeff = [coeff_ref[pl.ds(at, 8), :], coeff_ref[pl.ds(at + 8, 8), :]]
         for eight in range(0, GROUP, 8):
             totals = []
             for local in range(eight, eight + 8):
                 panel = group * GROUP + local
-                row = row_ref[panel]
-                depth = depth_ref[panel]
-                shift = (depth - 4 * local) & (REGION - 1)
-                total = field[pl.ds(row, 8), :] * pltpu.roll(coeff[0], shift, 1)
-                total = total + field[pl.ds(row + 2 * reach_y, 8), :] * pltpu.roll(
-                    coeff[1], shift, 1
+                row = place_ref[0, panel]
+                first = pl.multiple_of(panel * 16, 16)
+                totals.append(
+                    field[pl.ds(row, 8), :] * line_ref[pl.ds(first, 8), :]
+                    + field[pl.ds(row + 2 * reach_y, 8), :] * line_ref[pl.ds(first + 8, 8), :]
                 )
-                totals.append(jnp.where(((lanes - depth) & -4) == 0, total, 0.0))
             sums[pl.ds(pl.multiple_of(group * GROUP + eight, 8), 8), :] = sum_rows(totals)
         return carry
 
-    count = row_ref.shape[0]
     lax.fori_loop(0, count // GROUP, body, 0)
     sampled = lax.dot_general(
         jnp.ones((8, REGION), F32),
@@ -678,14 +791,14 @@
             out_ref[row, :] = image
 
 
-def sample(last, rows, depths, parts, table, coeff, flag, vector, near, reach_x, reach_y):
-    count = rows.shape[0]
+def sample(last, places, parts, table, lines, flag, vector, near, reach_x, reach_y):
+    count = places.shape[1]
     blocks = count // BLOCK
     pieces = len(parts)
     shape = (2, count) if last else (blocks, BLOCK)
     return pl.pallas_call(
         functools.partial(sample_kernel, last, reach_x, reach_y, pieces),
-        in_specs=[in_smem()] * 2 + [whole_vmem()] * (pieces + 6),
+        in_specs=[in_smem()] + [whole_vmem()] * (pieces + 6),
         out_specs=whole_vmem(),
         out_shape=jax.ShapeDtypeStruct(shape, F32),
         scratch_shapes=[
@@ -697,11 +810,10 @@
         cost_estimate=cost(reach_x * reach_y * 256 * 512, 4 * 16 * count * REGION),
         name="sample",
     )(
-        rows,
-        depths,
+        places,
         *parts,
         *table,
-        coeff,
+        lines,
         flag.reshape(blocks, BLOCK),
         vector.reshape(blocks, BLOCK),
         near,
@@ -769,7 +881,6 @@
 ):
     x_count = lax.axis_size("wide")
     y_count = lax.axis_size(Y_AXES)
-    x_index = lax.axis_index("wide")
     y_index = lax.axis_index(Y_AXES)
     span_x = REGION // x_count
     span_y = REGION // y_count
@@ -781,19 +892,12 @@
     z_forward, z_inverse, y_forward, y_inverse, modes = tables(y_count, span_y)
     modes = lax.dynamic_index_in_dim(jnp.asarray(modes), y_index, 0, keepdims=False)
 
-    local_x = stencil_base[0] - (x_index * span_x - 2)
-    local_y = stencil_base[1] - (y_index * span_y - 2)
-    rows = (
-        (local_x % 2) * (reach_x * reach_y) + (local_x // 2) * (2 * reach_y) + 2 * local_y
-    )
-    depths = stencil_base[2]
-
     neighbour = near_source // blocks
     flip = (y_index + neighbour % 3 - 1) ^ y_index
-    places = ((neighbour // 3) * y_count + flip) * blocks + near_source % blocks
+    sources = ((neighbour // 3) * y_count + flip) * blocks + near_source % blocks
     out_rows = up_to(blocks + 1, 8)
     live = near_target >= 0
-    places = jnp.where(live, places, 0)
+    sources = jnp.where(live, sources, 0)
     targets = jnp.where(live, near_target, out_rows - 1)
 
     far_moves = [
@@ -804,43 +908,50 @@
     to_right = [(i, i + 1) for i in range(x_count - 1)]
     to_left = [(i + 1, i) for i in range(x_count - 1)]
 
-    def turn(parts):
+    pair = lax.axis_size("pair")
+    inside, outside = list(range(pair)), list(range(pair, y_count))
+
+    def flipped(parts, flips):
         return [
             part
             if flip == 0
             else lax.ppermute(part, Y_AXES, [(i, i ^ flip) for i in range(y_count)])
-            for flip, part in enumerate(parts)
+            for flip, part in zip(flips, parts)
         ]
 
-    def convolve_and_sample(last, vector, sent, sample_coeff):
-        spectrum, right_going, left_going, own, peers = forward(
-            turn(sent), y_forward, modes, reach_x, reach_y, blocks
+    def convolve_and_sample(last, vector, sent, both, places, sample_lines):
+        arrived = flipped(sent, outside)
+        arrived = flipped(spread_rest(vector, both, z_forward, inside), inside) + arrived
+        spectrum, right_going, left_going, own, peers, inner = forward(
+            arrived, y_forward, modes, reach_x, reach_y, blocks
         )
         from_left = lax.ppermute(right_going, "wide", to_right)
         from_right = lax.ppermute(left_going, "wide", to_left)
         fars = [lax.ppermute(own, "wide", pairs) for pairs in far_moves]
         near_part = near_field(
-            places, targets, from_left, from_right, peers, near_tiles, blocks, out_rows
+            sources, targets, from_left, from_right, peers, near_tiles, blocks, out_rows
         )
-        parts = inverse(
+        *sent, high, low = inverse(
             spectrum,
             from_left,
             from_right,
             own,
+            inner,
             fars,
             y_inverse,
             modes,
             reach_x,
             reach_y,
-            y_count,
+            outside,
         )
+        arrived = flipped(sent, outside)
+        arrived = flipped(inverse_rest((high, low), y_inverse, reach_y, inside), inside) + arrived
         return sample(
             last,
-            rows,
-            depths,
-            turn(parts),
+            places,
+            arrived,
             z_inverse,
-            sample_coeff,
+            sample_lines,
             surface_flag,
             vector,
             near_part,
@@ -848,13 +959,19 @@
             reach_y,
         )
 
-    raw = (surface_flag, sample_weights, dipole_weights)
-    *sent, source_coeff, sample_coeff = spread(
-        density, rows, depths, z_forward, None, raw, reach_x, reach_y
+    raw = (stencil_base, surface_flag, sample_weights, dipole_weights)
+    *sent, high, low, source_coeff, sample_coeff, places = spread(
+        density, None, z_forward, None, raw, reach_x, reach_y, outside
     )
-    first_image = convolve_and_sample(False, density, sent, sample_coeff).reshape(-1)
-    sent = spread(first_image, rows, depths, z_forward, source_coeff, None, reach_x, reach_y)
-    return convolve_and_sample(True, first_image, sent, sample_coeff)
+    sample_lines = place_lines(places, sample_coeff)
+    source_lines = place_lines(places, source_coeff)
+    first_image = convolve_and_sample(
+        False, density, sent, (high, low), places, sample_lines
+    ).reshape(-1)
+    *sent, high, low = spread(
+        first_image, places, z_forward, source_lines, None, reach_x, reach_y, outside
+    )
+    return convolve_and_sample(True, first_image, sent, (high, low), places, sample_lines)
 
 
 def solution(mesh):

time: 113 us -> 112 us (level)
  waiting for transfers between devices: 41.1 us -> 36.2 us
  local copies, waits for them, and re-layouts: 2.1 us -> 5.69 us
  other arithmetic: 2.01 us -> 0.03 us
  Pallas kernels: 36.4 us -> 38.3 us
    pallas_call x2 -> x8, Pallas kernels: 9.92 us -> 14.9 us  [the longest x2 6.14 us: inverse(): pl.pallas_call(functools.partial(inverse_kernel, reach_x, reach_y, flips,...]
    ppermute x4, waiting for transfers between devices: 11.6 us -> 6.63 us  [convolve_and_sample(): fars = [lax.ppermute(own, 'wide', pairs) for pairs in far_moves]]
    unnamed x34 -> x40, local copies, waits for them, and re-layouts: 1.03 us -> 4.61 us
    pallas_call x2, Pallas kernels: 9.47 us -> 7.04 us  [sample(): pl.pallas_call(functools.partial(sample_kernel, last, reach_x, reach_y, p...]
    slice x1 -> x0, other arithmetic: 1.39 us -> none  [shards(): depths = stencil_base[2]]
  transfers between devices with their start and end apart: 20 -> 20, of which waited for: 10 -> 10; matrix products, arithmetic and copies ran while one was open for 1% -> 1% of each run, Pallas kernels for 2% -> 7%
where the time goes in v4:
time: 112 us
  Pallas kernels  38.3 us (34%)
  waiting for transfers between devices  36.2 us (32%)
  starting transfers between devices  31.1 us (28%)
  local copies, waits for them, and re-layouts  5.69 us (5%)
    ppermute x12, waiting for transfers between devices, flipped(): lax.ppermute(part, Y_AXES, [(i, i ^ flip) for i in range(y_count)])  29.5 us
    ppermute x4, starting transfers between devices, convolve_and_sample(): fars = [lax.ppermute(own, 'wide', pairs) for pairs in far_moves]  14.6 us
    pallas_call x2, Pallas kernels, spread(): pl.pallas_call(functools.partial(spread_kernel, first, reach_x, reach_y,...  9.56 us
    ppermute x12, starting transfers between devices, flipped(): lax.ppermute(part, Y_AXES, [(i, i ^ flip) for i in range(y_count)])  8.95 us
    pallas_call x2, Pallas kernels, sample(): pl.pallas_call(functools.partial(sample_kernel, last, reach_x, reach_y, p...  7.04 us
    ppermute x4, waiting for transfers between devices, convolve_and_sample(): fars = [lax.ppermute(own, 'wide', pairs) for pairs in far_moves]  6.63 us
    pallas_call x2, Pallas kernels, inverse(): pl.pallas_call(functools.partial(inverse_kernel, reach_x, reach_y, flips,...  6.14 us
    pallas_call x2, Pallas kernels, place_lines(): pl.pallas_call(lines_kernel, in_specs=[in_smem(), whole_vmem()], out_spec...  5.88 us
  transfers between devices with their start and end apart: 20, of which 10 were waited for; matrix products, arithmetic and copies ran while one was open for 1% of the time, Pallas kernels for 7%

profile of v4, /device:TPU:0, one launch (start us, length us, event | category | flops | bytes accessed | tf_op | source)
XLA Modules:
  0.0 111.6 jit_solution(3721903112529334848)
XLA Ops:
  0.0 6.8 %start.1 = (s16[672,128]{1,0:T(8,128)(2,1)}, s16[672,128]{1,0:T(8,128)(2,1)}, bf16[656,256]{1,0:T(8,128)(2,1)}, bf16[656,256]{1,0:T(8,128)(2,1)}, f32[256,128]{1...) custom-call(f32[512]{0:T(512)} %refs_0_.1, f32[4,128]{1,0:T(4,128)} %bitcast.7, ...), custom_call_target="tpu_custom_call" | custom-call | flops 169869312 | bytes 4194304 | tf_op jit(solution)/shard_map/start/pallas_call | solution.py:341
  6.8 0.0 copy-start
  6.8 0.9 copy-done
  7.7 0.9 copy-done.2
  8.7 1.0 copy-done.10
  9.6 1.0 copy-done.11
  10.6 0.7 copy-done.15
  11.3 0.6 spread_rest.2
  11.9 0.5 collective-permute-start
  12.4 2.6 %collective-permute-start.1 = (s16[672,128]{1,0:T(8,128)(2,1)}, s16[672,128]{1,0:T(8,128)(2,1)S(1)}, u32[]{:S(2)}, u32[]{:S(2)}) collective-permute-start(s16[672,128]{1,0:T(8,128)(2,1)} %get-tuple-element.49), channel_id=1, source_target_pairs={{0,2},{1,3},{2,0},{3,1},{4,6},{5,7},{6,4},{7,5},{8,10},{9,11},{10,... | collective-permute-start | bytes 516104 | tf_op jit(solution)/shard_map/ppermute | solution.py:918
  15.0 0.1 collective-permute-start.2
  15.0 1.1 dynamic-slice_bitcast_fusion.refs_5_.refs_9_
  16.1 4.3 %collective-permute-done.1.refs_2_ = s16[672,128]{1,0:T(8,128)(2,1)S(1)} collective-permute-done((s16[672,128]{1,0:T(8,128)(2,1)}, s16[672,128]{1,0:T(8,128)(2,1)S(1)}, u32[]{:S(2)}, u32[]{:S(2)}) %collective-permute-start.1) | collective-permute-done | bytes 172064 | tf_op jit(solution)/shard_map/ppermute | solution.py:918
  20.4 3.2 %collective-permute-done.2.refs_3_ = s16[672,128]{1,0:T(8,128)(2,1)S(1)} collective-permute-done((s16[672,128]{1,0:T(8,128)(2,1)}, s16[672,128]{1,0:T(8,128)(2,1)S(1)}, u32[]{:S(2)}, u32[]{:S(2)}) %collective-permute-start.2) | collective-permute-done | bytes 172064 | tf_op jit(solution)/shard_map/ppermute | solution.py:918
  23.6 2.3 %forward.2 = (f32[18,256,128]{2,1,0:T(8,128)S(1)}, s16[816,128]{1,0:T(8,128)(2,1)S(1)}, s16[816,128]{1,0:T(8,128)(2,1)S(1)}, s16[272,128]{1,0:T(8,128)(2,1)S(1)}...) custom-call(s16[672,128]{1,0:T(8,128)(2,1)S(1)} %get-tuple-element.47.refs_0_, ...), custom_call_target="tpu_custom_call" | custom-call | flops 301989888 | bytes 4718592 | tf_op jit(solution)/shard_map/forward/pallas_call | solution.py:524
  25.9 3.6 %collective-permute-start.3 = (s16[816,128]{1,0:T(8,128)(2,1)S(1)}, s16[816,128]{1,0:T(8,128)(2,1)S(1)}, u32[]{:S(2)}, u32[]{:S(2)}) collective-permute-start(s16[816,128]{1,0:T(8,128)(2,1)S(1)} %get-tuple-element.52), channel_id=1, source_target_pairs={{0,4},{4,8},{8,12},{1,5},{5,9},{9,13},{2,6},{6,10},{10,14},{3,7},{... | collective-permute-start | bytes 626696 | tf_op jit(solution)/shard_map/ppermute | solution.py:928
  29.5 1.3 %collective-permute-start.4 = (s16[816,128]{1,0:T(8,128)(2,1)S(1)}, s16[816,128]{1,0:T(8,128)(2,1)S(1)}, u32[]{:S(2)}, u32[]{:S(2)}) collective-permute-start(s16[816,128]{1,0:T(8,128)(2,1)S(1)} %get-tuple-element.53), channel_id=1, source_target_pairs={{4,0},{8,4},{12,8},{5,1},{9,5},{13,9},{6,2},{10,6},{14,10},{7,3},{... | collective-permute-start | bytes 626696 | tf_op jit(solution)/shard_map/ppermute | solution.py:929
  30.8 3.7 %collective-permute-start.5 = (s16[272,128]{1,0:T(8,128)(2,1)S(1)}, s16[272,128]{1,0:T(8,128)(2,1)S(1)}, u32[]{:S(2)}, u32[]{:S(2)}) collective-permute-start(s16[272,128]{1,0:T(8,128)(2,1)S(1)} %get-tuple-element.54.refs_3_), channel_id=1, source_target_pairs={{0,8},{4,12},{8,0},{12,4},{1,9},{5,13},{9,1},{13,5},{2,10},{6,14},... | collective-permute-start | bytes 208904 | tf_op jit(solution)/shard_map/ppermute | solution.py:930
  34.5 3.2 %collective-permute-start.6 = (s16[272,128]{1,0:T(8,128)(2,1)S(1)}, s16[272,128]{1,0:T(8,128)(2,1)S(1)}, u32[]{:S(2)}, u32[]{:S(2)}) collective-permute-start(s16[272,128]{1,0:T(8,128)(2,1)S(1)} %get-tuple-element.54.refs_3_), channel_id=1, source_target_pairs={{0,12},{12,0},{1,13},{13,1},{2,14},{14,2},{3,15},{15,3},{16,28},{2... | collective-permute-start | bytes 208904 | tf_op jit(solution)/shard_map/ppermute | solution.py:930
  37.8 2.9 %place_lines.2.refs_6_ = f32[8192,128]{1,0:T(8,128)S(1)} custom-call(s32[2,512]{1,0:T(2,128)S(1)} %copy-done.14, f32[256,128]{1,0:T(8,128)S(1)} %copy-done.13), custom_call_target="tpu_custom_call" | custom-call | flops 1048576 | bytes 4194304 | tf_op jit(solution)/shard_map/place_lines/pallas_call | solution.py:400
  40.8 0.0 copy-start.5
  40.8 0.0 copy-start.6
  40.8 2.9 %place_lines.3.refs_5_ = f32[8192,128]{1,0:T(8,128)S(1)} custom-call(s32[2,512]{1,0:T(2,128)S(1)} %copy-done.14, f32[256,128]{1,0:T(8,128)S(1)} %copy-done.12), custom_call_target="tpu_custom_call" | custom-call | flops 1048576 | bytes 4194304 | tf_op jit(solution)/shard_map/place_lines/pallas_call | solution.py:400
  43.7 0.2 collective-permute-done.5.refs_5_
  44.0 3.1 %inverse.2 = (s16[672,128]{1,0:T(8,128)(2,1)S(1)}, s16[672,128]{1,0:T(8,128)(2,1)S(1)}, bf16[18,256,128]{2,1,0:T(8,128)(2,1)S(1)}, bf16[18,256,128]{2,1,0:T(8,128)(2,1)S(1)}) custom-call(f32[18,256,128]{2,1,0:T(8,128)S(1)} %get-tuple-element.51.refs_0_, s16[816,128]{1,0:T(8,128)(2,1)S(1)} %collective-permute-done.3.refs_1_.refs_0_, ...), custom_call_target="tpu_custom_call" | custom-call | flops 301989888 | bytes 4718592 | tf_op jit(solution)/shard_map/inverse/pallas_call | solution.py:681
  47.1 0.0 copy-start.18
  47.1 0.0 copy-start.19
  47.1 0.0 copy-start.4
  47.1 0.0 copy-start.8
  47.1 0.0 copy-start.9
  47.1 0.0 copy-start.16
  47.1 0.0 copy-start.17
  47.1 0.9 inverse_rest.2
  48.0 0.1 collective-permute-start.7
  48.1 1.6 %collective-permute-start.8 = (s16[672,128]{1,0:T(8,128)(2,1)S(1)}, s16[672,128]{1,0:T(8,128)(2,1)S(1)}, u32[]{:S(2)}, u32[]{:S(2)}) collective-permute-start(s16[672,128]{1,0:T(8,128)(2,1)S(1)} %get-tuple-element.60), channel_id=1, source_target_pairs={{0,2},{1,3},{2,0},{3,1},{4,6},{5,7},{6,4},{7,5},{8,10},{9,11},{10,... | collective-permute-start | bytes 516104 | tf_op jit(solution)/shard_map/ppermute | solution.py:918
  49.7 0.3 collective-permute-start.9
  50.0 1.1 near_field.2.refs_9_
  51.1 4.3 %collective-permute-done.8.refs_2_ = s16[672,128]{1,0:T(8,128)(2,1)S(1)} collective-permute-done((s16[672,128]{1,0:T(8,128)(2,1)S(1)}, s16[672,128]{1,0:T(8,128)(2,1)S(1)}, u32[]{:S(2)}, u32[]{:S(2)}) %collective-permute-start.8) | collective-permute-done | bytes 172064 | tf_op jit(solution)/shard_map/ppermute | solution.py:918
  55.4 2.8 %collective-permute-done.9.refs_3_ = s16[672,128]{1,0:T(8,128)(2,1)S(1)} collective-permute-done((s16[672,128]{1,0:T(8,128)(2,1)S(1)}, s16[672,128]{1,0:T(8,128)(2,1)S(1)}, u32[]{:S(2)}, u32[]{:S(2)}) %collective-permute-start.9) | collective-permute-done | bytes 172064 | tf_op jit(solution)/shard_map/ppermute | solution.py:918
  58.2 0.0 copy-start.1
  58.2 0.0 copy-start.3
  58.2 3.2 %sample.2.refs_1_.rounded_ref.refs_8_ = f32[4,128]{1,0:T(4,128)S(1)} custom-call(s32[2,512]{1,0:T(2,128)S(1)} %copy-done.14, s16[672,128]{1,0:T(8,128)(2,1)S(1)} %get-tuple-element.58.refs_0_, s16[672,128]{1,0:T(8,128)(2,1)S(1)} %collective-permute-done.7.refs_1_, s16[672,128]{1,0:T(8,128)(2,1)S(1)} %collective-permute-done.8.refs_2_, ...), custom_call_target="tpu_custom_call" | custom-call | flops 169869312 | bytes 4194304 | tf_op jit(solution)/shard_map/sample/pallas_call | solution.py:799
  61.4 2.8 %spread.1 = (s16[672,128]{1,0:T(8,128)(2,1)S(1)}, s16[672,128]{1,0:T(8,128)(2,1)S(1)}, bf16[656,256]{1,0:T(8,128)(2,1)S(1)}, bf16[656,256]{1,0:T(8,128)(2,1)S(1)}) custom-call(f32[512]{0:T(512)S(1)} %bitcast.6, f32[4,128]{1,0:T(4,128)S(1)} %sample.2.refs_1_.rounded_ref.refs_8_, bf16[4,256,128]{2,1,0:T(8,128)(2,1)S(1)} %copy-done.1, ...), custom_call_target="tpu_custom_call" | custom-call | flops 169869312 | bytes 4194304 | tf_op jit(solution)/shard_map/spread/pallas_call | solution.py:341
  64.2 0.6 spread_rest.3
  64.8 0.3 collective-permute-start.10
  65.2 1.5 %collective-permute-start.11 = (s16[672,128]{1,0:T(8,128)(2,1)S(1)}, s16[672,128]{1,0:T(8,128)(2,1)S(1)}, u32[]{:S(2)}, u32[]{:S(2)}) collective-permute-start(s16[672,128]{1,0:T(8,128)(2,1)S(1)} %get-tuple-element.69), channel_id=1, source_target_pairs={{0,2},{1,3},{2,0},{3,1},{4,6},{5,7},{6,4},{7,5},{8,10},{9,11},{10,... | collective-permute-start | bytes 516104 | tf_op jit(solution)/shard_map/ppermute | solution.py:918
  66.7 0.1 collective-permute-start.12
  66.7 5.6 %collective-permute-done.11.refs_2_ = s16[672,128]{1,0:T(8,128)(2,1)S(1)} collective-permute-done((s16[672,128]{1,0:T(8,128)(2,1)S(1)}, s16[672,128]{1,0:T(8,128)(2,1)S(1)}, u32[]{:S(2)}, u32[]{:S(2)}) %collective-permute-start.11) | collective-permute-done | bytes 172064 | tf_op jit(solution)/shard_map/ppermute | solution.py:918
  72.4 2.3 %collective-permute-done.12.refs_3_ = s16[672,128]{1,0:T(8,128)(2,1)S(1)} collective-permute-done((s16[672,128]{1,0:T(8,128)(2,1)S(1)}, s16[672,128]{1,0:T(8,128)(2,1)S(1)}, u32[]{:S(2)}, u32[]{:S(2)}) %collective-permute-start.12) | collective-permute-done | bytes 172064 | tf_op jit(solution)/shard_map/ppermute | solution.py:918
  74.7 2.3 %forward.3 = (f32[18,256,128]{2,1,0:T(8,128)S(1)}, s16[816,128]{1,0:T(8,128)(2,1)S(1)}, s16[816,128]{1,0:T(8,128)(2,1)S(1)}, s16[272,128]{1,0:T(8,128)(2,1)S(1)}...) custom-call(s16[672,128]{1,0:T(8,128)(2,1)S(1)} %get-tuple-element.67.refs_0_, ...), custom_call_target="tpu_custom_call" | custom-call | flops 301989888 | bytes 4718592 | tf_op jit(solution)/shard_map/forward/pallas_call | solution.py:524
  77.0 1.4 %collective-permute-start.13 = (s16[816,128]{1,0:T(8,128)(2,1)S(1)}, s16[816,128]{1,0:T(8,128)(2,1)S(1)}, u32[]{:S(2)}, u32[]{:S(2)}) collective-permute-start(s16[816,128]{1,0:T(8,128)(2,1)S(1)} %get-tuple-element.72), channel_id=1, source_target_pairs={{0,4},{4,8},{8,12},{1,5},{5,9},{9,13},{2,6},{6,10},{10,14},{3,7},{... | collective-permute-start | bytes 626696 | tf_op jit(solution)/shard_map/ppermute | solution.py:928
  78.4 1.3 %collective-permute-start.14 = (s16[816,128]{1,0:T(8,128)(2,1)S(1)}, s16[816,128]{1,0:T(8,128)(2,1)S(1)}, u32[]{:S(2)}, u32[]{:S(2)}) collective-permute-start(s16[816,128]{1,0:T(8,128)(2,1)S(1)} %get-tuple-element.73), channel_id=1, source_target_pairs={{4,0},{8,4},{12,8},{5,1},{9,5},{13,9},{6,2},{10,6},{14,10},{7,3},{... | collective-permute-start | bytes 626696 | tf_op jit(solution)/shard_map/ppermute | solution.py:929
  79.7 4.1 %collective-permute-start.15 = (s16[272,128]{1,0:T(8,128)(2,1)S(1)}, s16[272,128]{1,0:T(8,128)(2,1)S(1)}, u32[]{:S(2)}, u32[]{:S(2)}) collective-permute-start(s16[272,128]{1,0:T(8,128)(2,1)S(1)} %get-tuple-element.74.refs_3_), channel_id=1, source_target_pairs={{0,8},{4,12},{8,0},{12,4},{1,9},{5,13},{9,1},{13,5},{2,10},{6,14},... | collective-permute-start | bytes 208904 | tf_op jit(solution)/shard_map/ppermute | solution.py:930
  83.8 3.6 %collective-permute-start.16 = (s16[272,128]{1,0:T(8,128)(2,1)S(1)}, s16[272,128]{1,0:T(8,128)(2,1)S(1)}, u32[]{:S(2)}, u32[]{:S(2)}) collective-permute-start(s16[272,128]{1,0:T(8,128)(2,1)S(1)} %get-tuple-element.74.refs_3_), channel_id=1, source_target_pairs={{0,12},{12,0},{1,13},{13,1},{2,14},{14,2},{3,15},{15,3},{16,28},{2... | collective-permute-start | bytes 208904 | tf_op jit(solution)/shard_map/ppermute | solution.py:930
  87.3 6.4 %collective-permute-done.15.refs_5_ = s16[272,128]{1,0:T(8,128)(2,1)S(1)} collective-permute-done((s16[272,128]{1,0:T(8,128)(2,1)S(1)}, s16[272,128]{1,0:T(8,128)(2,1)S(1)}, u32[]{:S(2)}, u32[]{:S(2)}) %collective-permute-start.15) | collective-permute-done | bytes 69664 | tf_op jit(solution)/shard_map/ppermute | solution.py:930
  93.7 3.1 %inverse.3 = (s16[672,128]{1,0:T(8,128)(2,1)S(1)}, s16[672,128]{1,0:T(8,128)(2,1)S(1)}, bf16[18,256,128]{2,1,0:T(8,128)(2,1)S(1)}, bf16[18,256,128]{2,1,0:T(8,128)(2,1)S(1)}) custom-call(f32[18,256,128]{2,1,0:T(8,128)S(1)} %get-tuple-element.71.refs_0_, s16[816,128]{1,0:T(8,128)(2,1)S(1)} %collective-permute-done.13.refs_1_.refs_0_, ...), custom_call_target="tpu_custom_call" | custom-call | flops 301989888 | bytes 4718592 | tf_op jit(solution)/shard_map/inverse/pallas_call | solution.py:681
  96.8 0.9 inverse_rest.3
  97.7 0.1 collective-permute-start.17
  97.8 1.6 %collective-permute-start.18 = (s16[672,128]{1,0:T(8,128)(2,1)S(1)}, s16[672,128]{1,0:T(8,128)(2,1)S(1)}, u32[]{:S(2)}, u32[]{:S(2)}) collective-permute-start(s16[672,128]{1,0:T(8,128)(2,1)S(1)} %get-tuple-element.80), channel_id=1, source_target_pairs={{0,2},{1,3},{2,0},{3,1},{4,6},{5,7},{6,4},{7,5},{8,10},{9,11},{10,... | collective-permute-start | bytes 516104 | tf_op jit(solution)/shard_map/ppermute | solution.py:918
  99.3 0.3 collective-permute-start.19
  99.6 1.1 near_field.3.refs_9_
  100.7 4.3 %collective-permute-done.18.refs_2_ = s16[672,128]{1,0:T(8,128)(2,1)S(1)} collective-permute-done((s16[672,128]{1,0:T(8,128)(2,1)S(1)}, s16[672,128]{1,0:T(8,128)(2,1)S(1)}, u32[]{:S(2)}, u32[]{:S(2)}) %collective-permute-start.18) | collective-permute-done | bytes 172064 | tf_op jit(solution)/shard_map/ppermute | solution.py:918
  105.0 2.8 %collective-permute-done.19.refs_3_ = s16[672,128]{1,0:T(8,128)(2,1)S(1)} collective-permute-done((s16[672,128]{1,0:T(8,128)(2,1)S(1)}, s16[672,128]{1,0:T(8,128)(2,1)S(1)}, u32[]{:S(2)}, u32[]{:S(2)}) %collective-permute-start.19) | collective-permute-done | bytes 172064 | tf_op jit(solution)/shard_map/ppermute | solution.py:918
  107.8 3.8 %sample.3 = f32[2,512]{1,0:T(2,128)} custom-call(s32[2,512]{1,0:T(2,128)S(1)} %copy-done.14, s16[672,128]{1,0:T(8,128)(2,1)S(1)} %get-tuple-element.78.refs_0_, s16[672,128]{1,0:T(8,128)(2,1)S(1)} %collective-permute-done.17.refs_1_, s16[672,128]{1,0:T(8,128)(2,1)S(1)} %collective-permute-done.18.refs_2_, ...), custom_call_target="tpu_custom_call" | custom-call | flops 169869312 | bytes 4194304 | tf_op jit(solution)/shard_map/sample/pallas_call | solution.py:799
  (34 shorter events, 0.1 us)
Async XLA Ops:
  0.0 23.6 %copy-start.7 = (bf16[256,480]{1,0:T(8,128)(2,1)S(1)}, bf16[256,480]{1,0:T(8,128)(2,1)}, u32[]{:S(2)}) copy-start(bf16[256,480]{1,0:T(8,128)(2,1)} %constant.76.clone.refs_4_) | copy-start | bytes 737284
  6.8 1.0 copy-start
  7.7 0.9 copy-start.2
  8.7 1.0 copy-start.10
  9.6 1.0 copy-start.11
  10.6 0.7 copy-start.15
  11.3 26.5 %copy-start.13 = (f32[256,128]{1,0:T(8,128)S(1)}, f32[256,128]{1,0:T(8,128)}, u32[]{:S(2)}) copy-start(f32[256,128]{1,0:T(8,128)} %get-tuple-element.62.coeff_ref) | copy-start | bytes 393220
  11.3 26.5 %copy-start.14 = (s32[2,512]{1,0:T(2,128)S(1)}, s32[2,512]{1,0:T(2,128)}, u32[]{:S(2)}) copy-start(s32[2,512]{1,0:T(2,128)} %get-tuple-element.44.place_ref.refs_4_) | copy-start | bytes 12292
  11.9 4.2 %collective-permute-start = (s16[672,128]{1,0:T(8,128)(2,1)S(1)}, s16[672,128]{1,0:T(8,128)(2,1)S(1)}, u32[]{:S(2)}, u32[]{:S(2)}) collective-permute-start(s16[672,128]{1,0:T(8,128)(2,1)S(1)} %get-tuple-element.48), channel_id=1, source_target_pairs={{0,1},{1,0},{2,3},{3,2},{4,5},{5,4},{6,7},{7,6},{8,9},{9,8},{10,11... | collective-permute-start | bytes 516104 | tf_op jit(solution)/shard_map/ppermute | solution.py:918
  12.4 8.0 %collective-permute-start.1 = (s16[672,128]{1,0:T(8,128)(2,1)}, s16[672,128]{1,0:T(8,128)(2,1)S(1)}, u32[]{:S(2)}, u32[]{:S(2)}) collective-permute-start(s16[672,128]{1,0:T(8,128)(2,1)} %get-tuple-element.49), channel_id=1, source_target_pairs={{0,2},{1,3},{2,0},{3,1},{4,6},{5,7},{6,4},{7,5},{8,10},{9,11},{10,... | collective-permute-start | bytes 516104 | tf_op jit(solution)/shard_map/ppermute | solution.py:918
  15.0 8.6 %collective-permute-start.2 = (s16[672,128]{1,0:T(8,128)(2,1)}, s16[672,128]{1,0:T(8,128)(2,1)S(1)}, u32[]{:S(2)}, u32[]{:S(2)}) collective-permute-start(s16[672,128]{1,0:T(8,128)(2,1)} %get-tuple-element.50), channel_id=1, source_target_pairs={{0,3},{1,2},{2,1},{3,0},{4,7},{5,6},{6,5},{7,4},{8,11},{9,10},{10,... | collective-permute-start | bytes 516104 | tf_op jit(solution)/shard_map/ppermute | solution.py:918
  25.9 18.0 %collective-permute-start.3 = (s16[816,128]{1,0:T(8,128)(2,1)S(1)}, s16[816,128]{1,0:T(8,128)(2,1)S(1)}, u32[]{:S(2)}, u32[]{:S(2)}) collective-permute-start(s16[816,128]{1,0:T(8,128)(2,1)S(1)} %get-tuple-element.52), channel_id=1, source_target_pairs={{0,4},{4,8},{8,12},{1,5},{5,9},{9,13},{2,6},{6,10},{10,14},{3,7},{... | collective-permute-start | bytes 626696 | tf_op jit(solution)/shard_map/ppermute | solution.py:928
  29.5 14.5 %collective-permute-start.4 = (s16[816,128]{1,0:T(8,128)(2,1)S(1)}, s16[816,128]{1,0:T(8,128)(2,1)S(1)}, u32[]{:S(2)}, u32[]{:S(2)}) collective-permute-start(s16[816,128]{1,0:T(8,128)(2,1)S(1)} %get-tuple-element.53), channel_id=1, source_target_pairs={{4,0},{8,4},{12,8},{5,1},{9,5},{13,9},{6,2},{10,6},{14,10},{7,3},{... | collective-permute-start | bytes 626696 | tf_op jit(solution)/shard_map/ppermute | solution.py:929
  30.8 13.2 %collective-permute-start.5 = (s16[272,128]{1,0:T(8,128)(2,1)S(1)}, s16[272,128]{1,0:T(8,128)(2,1)S(1)}, u32[]{:S(2)}, u32[]{:S(2)}) collective-permute-start(s16[272,128]{1,0:T(8,128)(2,1)S(1)} %get-tuple-element.54.refs_3_), channel_id=1, source_target_pairs={{0,8},{4,12},{8,0},{12,4},{1,9},{5,13},{9,1},{13,5},{2,10},{6,14},... | collective-permute-start | bytes 208904 | tf_op jit(solution)/shard_map/ppermute | solution.py:930
  34.5 9.4 %collective-permute-start.6 = (s16[272,128]{1,0:T(8,128)(2,1)S(1)}, s16[272,128]{1,0:T(8,128)(2,1)S(1)}, u32[]{:S(2)}, u32[]{:S(2)}) collective-permute-start(s16[272,128]{1,0:T(8,128)(2,1)S(1)} %get-tuple-element.54.refs_3_), channel_id=1, source_target_pairs={{0,12},{12,0},{1,13},{13,1},{2,14},{14,2},{3,15},{15,3},{16,28},{2... | collective-permute-start | bytes 208904 | tf_op jit(solution)/shard_map/ppermute | solution.py:930
  37.8 3.0 %copy-start.12 = (f32[256,128]{1,0:T(8,128)S(1)}, f32[256,128]{1,0:T(8,128)}, u32[]{:S(2)}) copy-start(f32[256,128]{1,0:T(8,128)} %get-tuple-element.64.coeff_ref) | copy-start | bytes 393220
  40.8 3.2 %copy-start.5 = (bf16[4,48,256]{2,1,0:T(8,128)(2,1)S(1)}, bf16[4,48,256]{2,1,0:T(8,128)(2,1)}, u32[]{:S(2)}) copy-start(bf16[4,48,256]{2,1,0:T(8,128)(2,1)} %constant.77.clone.refs_7_.high_ref) | copy-start | bytes 294916
  40.8 3.2 %copy-start.6 = (bf16[4,48,256]{2,1,0:T(8,128)(2,1)S(1)}, bf16[4,48,256]{2,1,0:T(8,128)(2,1)}, u32[]{:S(2)}) copy-start(bf16[4,48,256]{2,1,0:T(8,128)(2,1)} %constant.78.clone.refs_8_.low_ref) | copy-start | bytes 294916
  47.1 2.9 %copy-start.18 = (s32[24]{0:T(128)S(1)}, s32[24]{0:T(128)}, u32[]{:S(2)}) copy-start(s32[24]{0:T(128)} %param.21) | copy-start | bytes 292
  47.1 2.9 %copy-start.19 = (s32[24]{0:T(128)S(1)}, s32[24]{0:T(128)}, u32[]{:S(2)}) copy-start(s32[24]{0:T(128)} %param.22) | copy-start | bytes 292
  47.1 2.9 %copy-start.4 = (bf16[24,128,128]{2,1,0:T(8,128)(2,1)S(1)}, bf16[24,128,128]{2,1,0:T(8,128)(2,1)}, u32[]{:S(2)}) copy-start(bf16[24,128,128]{2,1,0:T(8,128)(2,1)} %refs_3_.5) | copy-start | bytes 2359300
  47.1 11.0 %copy-start.8 = (bf16[4,128,256]{2,1,0:T(8,128)(2,1)S(1)}, bf16[4,128,256]{2,1,0:T(8,128)(2,1)}, u32[]{:S(2)}) copy-start(bf16[4,128,256]{2,1,0:T(8,128)(2,1)} %constant.79.clone.refs_4_) | copy-start | bytes 786436
  47.1 11.0 %copy-start.9 = (bf16[4,128,256]{2,1,0:T(8,128)(2,1)S(1)}, bf16[4,128,256]{2,1,0:T(8,128)(2,1)}, u32[]{:S(2)}) copy-start(bf16[4,128,256]{2,1,0:T(8,128)(2,1)} %constant.80.clone.refs_5_) | copy-start | bytes 786436
  47.1 11.0 %copy-start.16 = (f32[512]{0:T(512)S(1)}, f32[512]{0:T(512)}, u32[]{:S(2)}) copy-start(f32[512]{0:T(512)} %refs_0_.1) | copy-start | bytes 6148
  47.1 11.0 %copy-start.17 = (s32[512]{0:T(512)S(1)}, s32[512]{0:T(512)}, u32[]{:S(2)}) copy-start(s32[512]{0:T(512)} %param.17) | copy-start | bytes 6148
  48.0 3.0 %collective-permute-start.7 = (s16[672,128]{1,0:T(8,128)(2,1)S(1)}, s16[672,128]{1,0:T(8,128)(2,1)S(1)}, u32[]{:S(2)}, u32[]{:S(2)}) collective-permute-start(s16[672,128]{1,0:T(8,128)(2,1)S(1)} %get-tuple-element.59), channel_id=1, source_target_pairs={{0,1},{1,0},{2,3},{3,2},{4,5},{5,4},{6,7},{7,6},{8,9},{9,8},{10,11... | collective-permute-start | bytes 516104 | tf_op jit(solution)/shard_map/ppermute | solution.py:918
  48.1 7.2 %collective-permute-start.8 = (s16[672,128]{1,0:T(8,128)(2,1)S(1)}, s16[672,128]{1,0:T(8,128)(2,1)S(1)}, u32[]{:S(2)}, u32[]{:S(2)}) collective-permute-start(s16[672,128]{1,0:T(8,128)(2,1)S(1)} %get-tuple-element.60), channel_id=1, source_target_pairs={{0,2},{1,3},{2,0},{3,1},{4,6},{5,7},{6,4},{7,5},{8,10},{9,11},{10,... | collective-permute-start | bytes 516104 | tf_op jit(solution)/shard_map/ppermute | solution.py:918
  49.7 8.5 %collective-permute-start.9 = (s16[672,128]{1,0:T(8,128)(2,1)S(1)}, s16[672,128]{1,0:T(8,128)(2,1)S(1)}, u32[]{:S(2)}, u32[]{:S(2)}) collective-permute-start(s16[672,128]{1,0:T(8,128)(2,1)S(1)} %get-tuple-element.61), channel_id=1, source_target_pairs={{0,3},{1,2},{2,1},{3,0},{4,7},{5,6},{6,5},{7,4},{8,11},{9,10},{10,... | collective-permute-start | bytes 516104 | tf_op jit(solution)/shard_map/ppermute | solution.py:918
  58.2 3.2 %copy-start.1 = (bf16[4,256,128]{2,1,0:T(8,128)(2,1)S(1)}, bf16[4,256,128]{2,1,0:T(8,128)(2,1)}, u32[]{:S(2)}) copy-start(bf16[4,256,128]{2,1,0:T(8,128)(2,1)} %constant.74.clone.refs_2_.high_ref) | copy-start | bytes 786436
  58.2 3.2 %copy-start.3 = (bf16[4,256,128]{2,1,0:T(8,128)(2,1)S(1)}, bf16[4,256,128]{2,1,0:T(8,128)(2,1)}, u32[]{:S(2)}) copy-start(bf16[4,256,128]{2,1,0:T(8,128)(2,1)} %constant.75.clone.refs_3_.low_ref) | copy-start | bytes 786436
  64.8 1.9 %collective-permute-start.10 = (s16[672,128]{1,0:T(8,128)(2,1)S(1)}, s16[672,128]{1,0:T(8,128)(2,1)S(1)}, u32[]{:S(2)}, u32[]{:S(2)}) collective-permute-start(s16[672,128]{1,0:T(8,128)(2,1)S(1)} %get-tuple-element.68), channel_id=1, source_target_pairs={{0,1},{1,0},{2,3},{3,2},{4,5},{5,4},{6,7},{7,6},{8,9},{9,8},{10,11... | collective-permute-start | bytes 516104 | tf_op jit(solution)/shard_map/ppermute | solution.py:918
  65.2 7.2 %collective-permute-start.11 = (s16[672,128]{1,0:T(8,128)(2,1)S(1)}, s16[672,128]{1,0:T(8,128)(2,1)S(1)}, u32[]{:S(2)}, u32[]{:S(2)}) collective-permute-start(s16[672,128]{1,0:T(8,128)(2,1)S(1)} %get-tuple-element.69), channel_id=1, source_target_pairs={{0,2},{1,3},{2,0},{3,1},{4,6},{5,7},{6,4},{7,5},{8,10},{9,11},{10,... | collective-permute-start | bytes 516104 | tf_op jit(solution)/shard_map/ppermute | solution.py:918
  66.7 8.0 %collective-permute-start.12 = (s16[672,128]{1,0:T(8,128)(2,1)S(1)}, s16[672,128]{1,0:T(8,128)(2,1)S(1)}, u32[]{:S(2)}, u32[]{:S(2)}) collective-permute-start(s16[672,128]{1,0:T(8,128)(2,1)S(1)} %get-tuple-element.70), channel_id=1, source_target_pairs={{0,3},{1,2},{2,1},{3,0},{4,7},{5,6},{6,5},{7,4},{8,11},{9,10},{10,... | collective-permute-start | bytes 516104 | tf_op jit(solution)/shard_map/ppermute | solution.py:918
  77.0 16.7 %collective-permute-start.13 = (s16[816,128]{1,0:T(8,128)(2,1)S(1)}, s16[816,128]{1,0:T(8,128)(2,1)S(1)}, u32[]{:S(2)}, u32[]{:S(2)}) collective-permute-start(s16[816,128]{1,0:T(8,128)(2,1)S(1)} %get-tuple-element.72), channel_id=1, source_target_pairs={{0,4},{4,8},{8,12},{1,5},{5,9},{9,13},{2,6},{6,10},{10,14},{3,7},{... | collective-permute-start | bytes 626696 | tf_op jit(solution)/shard_map/ppermute | solution.py:928
  78.4 15.3 %collective-permute-start.14 = (s16[816,128]{1,0:T(8,128)(2,1)S(1)}, s16[816,128]{1,0:T(8,128)(2,1)S(1)}, u32[]{:S(2)}, u32[]{:S(2)}) collective-permute-start(s16[816,128]{1,0:T(8,128)(2,1)S(1)} %get-tuple-element.73), channel_id=1, source_target_pairs={{4,0},{8,4},{12,8},{5,1},{9,5},{13,9},{6,2},{10,6},{14,10},{7,3},{... | collective-permute-start | bytes 626696 | tf_op jit(solution)/shard_map/ppermute | solution.py:929
  79.7 14.0 %collective-permute-start.15 = (s16[272,128]{1,0:T(8,128)(2,1)S(1)}, s16[272,128]{1,0:T(8,128)(2,1)S(1)}, u32[]{:S(2)}, u32[]{:S(2)}) collective-permute-start(s16[272,128]{1,0:T(8,128)(2,1)S(1)} %get-tuple-element.74.refs_3_), channel_id=1, source_target_pairs={{0,8},{4,12},{8,0},{12,4},{1,9},{5,13},{9,1},{13,5},{2,10},{6,14},... | collective-permute-start | bytes 208904 | tf_op jit(solution)/shard_map/ppermute | solution.py:930
  83.8 10.0 %collective-permute-start.16 = (s16[272,128]{1,0:T(8,128)(2,1)S(1)}, s16[272,128]{1,0:T(8,128)(2,1)S(1)}, u32[]{:S(2)}, u32[]{:S(2)}) collective-permute-start(s16[272,128]{1,0:T(8,128)(2,1)S(1)} %get-tuple-element.74.refs_3_), channel_id=1, source_target_pairs={{0,12},{12,0},{1,13},{13,1},{2,14},{14,2},{3,15},{15,3},{16,28},{2... | collective-permute-start | bytes 208904 | tf_op jit(solution)/shard_map/ppermute | solution.py:930
  97.7 3.0 %collective-permute-start.17 = (s16[672,128]{1,0:T(8,128)(2,1)S(1)}, s16[672,128]{1,0:T(8,128)(2,1)S(1)}, u32[]{:S(2)}, u32[]{:S(2)}) collective-permute-start(s16[672,128]{1,0:T(8,128)(2,1)S(1)} %get-tuple-element.79), channel_id=1, source_target_pairs={{0,1},{1,0},{2,3},{3,2},{4,5},{5,4},{6,7},{7,6},{8,9},{9,8},{10,11... | collective-permute-start | bytes 516104 | tf_op jit(solution)/shard_map/ppermute | solution.py:918
  97.8 7.2 %collective-permute-start.18 = (s16[672,128]{1,0:T(8,128)(2,1)S(1)}, s16[672,128]{1,0:T(8,128)(2,1)S(1)}, u32[]{:S(2)}, u32[]{:S(2)}) collective-permute-start(s16[672,128]{1,0:T(8,128)(2,1)S(1)} %get-tuple-element.80), channel_id=1, source_target_pairs={{0,2},{1,3},{2,0},{3,1},{4,6},{5,7},{6,4},{7,5},{8,10},{9,11},{10,... | collective-permute-start | bytes 516104 | tf_op jit(solution)/shard_map/ppermute | solution.py:918
  99.3 8.5 %collective-permute-start.19 = (s16[672,128]{1,0:T(8,128)(2,1)S(1)}, s16[672,128]{1,0:T(8,128)(2,1)S(1)}, u32[]{:S(2)}, u32[]{:S(2)}) collective-permute-start(s16[672,128]{1,0:T(8,128)(2,1)S(1)} %get-tuple-element.81), channel_id=1, source_target_pairs={{0,3},{1,2},{2,1},{3,0},{4,7},{5,6},{6,5},{7,4},{8,11},{9,10},{10,... | collective-permute-start | bytes 516104 | tf_op jit(solution)/shard_map/ppermute | solution.py:918

commit v5 on v4

--- a/solution.py
+++ b/solution.py
@@ -21,7 +21,6 @@
 F32 = jnp.float32
 BF16 = jnp.bfloat16
 VMEM_LIMIT = 24 * 1024 * 1024
-START_LIMIT = 56 * 1024 * 1024
 GROUP = 32
 CHAINS = 2
 
@@ -257,39 +256,7 @@
             send_piece(out, head, result[:, i * 2 * HALF : (i + 1) * 2 * HALF])
 
 
-def spread_kernel(first, reach_x, reach_y, flips, tiles, *refs):
-    vector_ref, rounded_ref, high_ref, low_ref = refs[:4]
-    refs = refs[4:]
-    if first:
-        stencil_ref, flag_ref = refs[:2]
-        sample_refs, dipole_refs = refs[2 : 2 + tiles], refs[2 + tiles : 2 + 2 * tiles]
-        refs = refs[2 + 2 * tiles :]
-    else:
-        place_ref, weight_ref = refs[:2]
-        refs = refs[2:]
-    outs, (wide_high, wide_low), refs = refs[: len(flips)], refs[len(flips) :][:2], refs[len(flips) + 2 :]
-    if first:
-        weight_ref, sample_coeff_ref, places_out = refs[:3]
-        place_ref, sem = refs[-2:]
-        refs = refs[3:-2]
-        span_x, span_y = reach_x - 4, reach_y - 4
-        local_x = stencil_ref[0:1, :] - (lax.axis_index("wide") * span_x - 2)
-        local_y = stencil_ref[1:2, :] - (y_position() * span_y - 2)
-        odd = local_x & 1
-        places_out[0:1, :] = (
-            odd * (reach_x * reach_y) + (local_x >> 1) * (2 * reach_y) + 2 * local_y
-        )
-        places_out[1:2, :] = stencil_ref[2:3, :]
-        copy = pltpu.make_async_copy(places_out, place_ref, sem)
-        copy.start()
-    head, total = refs[:2]
-    grids = refs[2:]
-    for grid in grids:
-        grid[...] = jnp.zeros_like(grid)
-    if first:
-        weave(flag_ref[...], sample_refs, dipole_refs, weight_ref, sample_coeff_ref)
-        copy.wait()
-    add_panels(reach_y, first, vector_ref, place_ref, weight_ref, grids)
+def spread_grid(reach_x, reach_y, rounded, tables, outs, flips, wides, head, total, grids):
     for x in range(reach_x):
         parts = [
             grid[pl.ds(row, reach_y, stride=2), :]
@@ -299,57 +266,138 @@
         total[x * reach_y : (x + 1) * reach_y, :] = sum(parts[1:], parts[0])
     half = reach_x * reach_y // 2
     both = jnp.concatenate([total[:half, :], total[half:, :]], axis=1)
-    extra = wide_high.shape[0] - half
+    extra = wides[0].shape[0] - half
     if extra:
         both = jnp.concatenate([both, jnp.zeros((extra, 2 * REGION), F32)], axis=0)
-    high, low = split(both)
-    wide_high[...] = high
-    wide_low[...] = low
-    send_pieces(outs, flips, head, rounded_ref[...], (high, low), high_ref, low_ref)
-
-
-def spread(vector, places, table, lines, raw, reach_x, reach_y, flips):
+    both = split(both)
+    for wide, values in zip(wides, both):
+        wide[...] = values
+    send_pieces(outs, flips, head, rounded, both, *tables)
+
+
+def start_kernel(reach_x, reach_y, flips, *refs):
+    vector_ref, *remote = refs[:8]
+    refs = refs[8:]
+    outs, refs = refs[: len(flips)], refs[len(flips) :]
+    wides, (weight_ref, sample_coeff_ref, places_out), refs = refs[:2], refs[2:5], refs[5:]
+    rounded, high, low, stencil, flag, samples, dipoles = refs[:7]
+    place_ref, sems, head, total = refs[7:11]
+    grids = refs[11:]
+    tiles = samples.shape[0]
+    copies = []
+    fetch = lambda source, target: copies.append(
+        pltpu.make_async_copy(source, target, sems.at[len(copies)])
+    )
+    rounded_in, high_in, low_in, stencil_in, flag_in, sample_in, dipole_in = remote
+    fetch(stencil_in, stencil)
+    fetch(flag_in, flag)
+    for tile in range(tiles):
+        lanes = pl.ds(tile * BLOCK, BLOCK)
+        fetch(sample_in.at[:, lanes], samples.at[tile])
+        fetch(dipole_in.at[:, lanes], dipoles.at[tile])
+    needed_first = len(copies)
+    fetch(rounded_in, rounded)
+    fetch(high_in, high)
+    fetch(low_in, low)
+    for copy in copies:
+        copy.start()
+    for grid in grids:
+        grid[...] = jnp.zeros_like(grid)
+    copies[0].wait()
+    span_x, span_y = reach_x - 4, reach_y - 4
+    local_x = stencil[0:1, :] - (lax.axis_index("wide") * span_x - 2)
+    local_y = stencil[1:2, :] - (y_position() * span_y - 2)
+    odd = local_x & 1
+    places_out[0:1, :] = odd * (reach_x * reach_y) + (local_x >> 1) * (2 * reach_y) + 2 * local_y
+    places_out[1:2, :] = stencil[2:3, :]
+    to_scalar = pltpu.make_async_copy(places_out, place_ref, sems.at[len(copies)])
+    to_scalar.start()
+    for copy in copies[1:needed_first]:
+        copy.wait()
+    each = lambda values: [values.at[tile] for tile in range(tiles)]
+    weave(flag[...], each(samples), each(dipoles), weight_ref, sample_coeff_ref)
+    to_scalar.wait()
+    add_panels(reach_y, True, vector_ref, place_ref, weight_ref, grids)
+    for copy in copies[needed_first:]:
+        copy.wait()
+    spread_grid(
+        reach_x, reach_y, rounded[...], (high, low), outs, flips, wides, head, total, grids
+    )
+
+
+def spread_kernel(reach_x, reach_y, flips, *refs):
+    vector_ref, place_ref, rounded_ref, high_ref, low_ref, line_ref = refs[:6]
+    refs = refs[6:]
+    outs, wides, (head, total), grids = (
+        refs[: len(flips)],
+        refs[len(flips) : len(flips) + 2],
+        refs[len(flips) + 2 : len(flips) + 4],
+        refs[len(flips) + 4 :],
+    )
+    for grid in grids:
+        grid[...] = jnp.zeros_like(grid)
+    add_panels(reach_y, False, vector_ref, place_ref, line_ref, grids)
+    spread_grid(
+        reach_x,
+        reach_y,
+        rounded_ref[...],
+        (high_ref, low_ref),
+        outs,
+        flips,
+        wides,
+        head,
+        total,
+        grids,
+    )
+
+
+def spread(vector, table, placed, raw, reach_x, reach_y, flips):
     count = vector.shape[0]
     half = reach_x * reach_y // 2
     blocks = count // BLOCK
     top = up_to(2 + 2 * blocks, 16)
     lanes = 2 * HALF
-    constant = lambda shape: pl.BlockSpec(shape, lambda i: (0,) * len(shape))
     body = up_to(half, 16)
     woven = (count // GROUP * 16, BLOCK)
     out_shapes = [jax.ShapeDtypeStruct((top + body, lanes), jnp.int16)] * len(flips)
     out_shapes += [jax.ShapeDtypeStruct((body, 2 * REGION), BF16)] * 2
-    operands = [vector, vector.reshape(blocks, BLOCK), *table]
-    in_specs = [in_smem()] + [constant(value.shape) for value in operands[1:]]
-    scratch = [
+    rounded = vector.reshape(blocks, BLOCK)
+    work = [
         pltpu.VMEM((top, lanes), F32),
         pltpu.VMEM((reach_x * reach_y, REGION), F32),
     ] + [pltpu.VMEM((pair_count(reach_x, reach_y), REGION), F32)] * CHAINS
-    first = lines is None
-    if first:
+    if placed is None:
         stencil, flag, sample, dipole = raw
-        tile = lambda t: pl.BlockSpec((64, BLOCK), lambda i: (0, t))
-        operands += [stencil, flag.reshape(1, -1)] + [sample] * blocks + [dipole] * blocks
-        in_specs += [constant(stencil.shape), constant((1, count))]
-        in_specs += [tile(t) for t in range(blocks)] * 2
+        operands = [vector, rounded, *table, stencil, flag.reshape(1, -1), sample, dipole]
+        in_specs = [in_smem()] + [pl.BlockSpec(memory_space=pltpu.HBM)] * 7
         out_shapes += [jax.ShapeDtypeStruct(woven, F32)] * 2
         out_shapes += [jax.ShapeDtypeStruct((2, count), jnp.int32)]
-        scratch += [pltpu.SMEM((2, count), jnp.int32), pltpu.SemaphoreType.DMA]
+        tiled = pltpu.VMEM((blocks, 64, BLOCK), F32)
+        work = [
+            pltpu.VMEM(rounded.shape, F32),
+            pltpu.VMEM(table[0].shape, BF16),
+            pltpu.VMEM(table[1].shape, BF16),
+            pltpu.VMEM(stencil.shape, jnp.int32),
+            pltpu.VMEM((1, count), jnp.int32),
+            tiled,
+            tiled,
+            pltpu.SMEM((2, count), jnp.int32),
+            pltpu.SemaphoreType.DMA((6 + 2 * blocks,)),
+        ] + work
     else:
-        operands += [places, lines]
-        in_specs += [in_smem(), whole_vmem()]
+        operands = [vector, placed[0], rounded, *table, placed[1]]
+        in_specs = [in_smem()] * 2 + [whole_vmem()] * 4
     return pl.pallas_call(
-        functools.partial(spread_kernel, first, reach_x, reach_y, flips, blocks),
-        grid=(1,),
+        functools.partial(
+            start_kernel if placed is None else spread_kernel, reach_x, reach_y, flips
+        ),
         in_specs=in_specs,
-        out_specs=[constant(out.shape) for out in out_shapes],
+        out_specs=[whole_vmem()] * len(out_shapes),
         out_shape=out_shapes,
-        scratch_shapes=scratch,
-        compiler_params=pltpu.CompilerParams(
-            vmem_limit_bytes=START_LIMIT if first else VMEM_LIMIT
-        ),
+        scratch_shapes=work,
+        compiler_params=params(),
         cost_estimate=cost(2 * half * 256 * 512, 4 * 16 * count * REGION),
-        name="start" if first else "spread",
+        name="start" if placed is None else "spread",
     )(*operands)
 
 
@@ -411,7 +459,7 @@
 def forward_kernel(reach_x, reach_y, blocks, pieces, *refs):
     parts = refs[:pieces]
     table_ref, modes_ref = refs[pieces : pieces + 2]
-    spectrum, right_out, left_out, own_out, peers_out, inner_out = refs[pieces + 2 : pieces + 8]
+    spectrum, even_out, odd_out, own_out, peers_out, inner_out = refs[pieces + 2 : pieces + 8]
     opened, stacked, slabs, head = refs[pieces + 8 :]
     half = reach_x // 2
     pitch = up_to(reach_y, 8)
@@ -499,7 +547,8 @@
     largest = lax.fori_loop(0, GRID // chunk, body, (zero,) * 7)
     scales = [fit_scale(jnp.max(value, axis=0, keepdims=True)) for value in largest]
     head_rows = head.shape[0]
-    for out, first in ((right_out, 0), (left_out, 3)):
+
+    def send(out, first):
         for slab in range(3):
             exponent, fraction = scales[first + slab]
             head[2 * slab : 2 * slab + 1, :] = exponent
@@ -507,6 +556,19 @@
             at = head_rows + slab * GRID
             out[at : at + GRID, :] = quantize(slabs[first + slab], exponent, fraction)
         out[:head_rows, :] = to_short(head[...])
+
+    on_left = lax.axis_index("wide") & 1
+
+    @pl.when(on_left == 0)
+    def _():
+        send(even_out, 0)
+        send(odd_out, 3)
+
+    @pl.when(on_left == 1)
+    def _():
+        send(even_out, 3)
+        send(odd_out, 0)
+
     exponent, fraction = scales[6]
     head[0:1, :] = exponent
     head[1:2, :] = fraction
@@ -568,7 +630,7 @@
 
 
 def inverse_kernel(reach_x, reach_y, flips, fars, *refs):
-    spectrum, from_left, from_right, own_ref, inner_ref = refs[:5]
+    spectrum, from_even, from_odd, own_ref, inner_ref = refs[:5]
     far_refs = refs[5 : 5 + fars]
     high_ref, low_ref, modes_ref = refs[5 + fars : 8 + fars]
     outs = refs[8 + fars : 8 + fars + len(flips)]
@@ -576,16 +638,20 @@
     half = reach_x // 2
     span = reach_x - 4
     chunk = 32
-    head_rows = from_left.shape[0] - 3 * GRID
+    head_rows = from_even.shape[0] - 3 * GRID
     x_count = lax.axis_size("wide")
     x_index = lax.axis_index("wide")
 
-    left_head = from_short(from_left[:16, :])
-    right_head = from_short(from_right[:16, :])
-    left_units = [unit(left_head[2 * s : 2 * s + 1], left_head[2 * s + 1 : 2 * s + 2]) for s in range(3)]
-    right_units = [
-        unit(right_head[2 * s : 2 * s + 1], right_head[2 * s + 1 : 2 * s + 2]) for s in range(3)
+    on_left = (x_index & 1) == 1
+    both_heads = from_short(from_even[:16, :]), from_short(from_odd[:16, :])
+    both_units = [
+        [unit(first[2 * slab : 2 * slab + 1], first[2 * slab + 1 : 2 * slab + 2]) for slab in range(3)]
+        for first in both_heads
     ]
+
+    def sided(even, odd):
+        return jnp.where(on_left, even, odd), jnp.where(on_left, odd, even)
+
     far_units = []
     own_head = from_short(own_ref[:16, :])
     own_unit = unit(own_head[0:1], own_head[1:2])
@@ -593,11 +659,8 @@
         first = from_short(far[:16, :])
         far_units.append(unit(first[0:1], first[1:2]))
     powers = []
-    for far, shift in enumerate(list(range(2, x_count - 1)) + [x_count - 1][: int(x_count > 2)]):
-        if shift < x_count - 1:
-            behind = jnp.where(x_index >= shift, shift, shift - x_count)
-        else:
-            behind = jnp.where(x_index == 0, -shift, jnp.where(x_index == shift, shift, 0))
+    for flip in range(2, x_count):
+        behind = x_index - (x_index ^ flip)
         both = []
         for distance in (-behind, behind):
             ahead = span * distance - reach_x
@@ -618,16 +681,17 @@
         beside = jnp.exp((GRID - reach_x - span) * log_decay)
         layers = [spectrum[i, rows, :] for i in range(half)]
 
-        def slab(ref, which, units):
+        def slab(which):
             at = pl.ds(pl.multiple_of(head_rows + which * GRID + index * chunk, chunk), chunk)
-            return from_short(ref[at, :]) * units[which]
+            even = from_short(from_even[at, :]) * both_units[0][which]
+            return sided(even, from_short(from_odd[at, :]) * both_units[1][which])
 
         def moment(ref, scale):
             at = pl.ds(pl.multiple_of(16 + index * chunk, chunk), chunk)
             return from_short(ref[at, :]) * scale
 
-        head_layers = [slab(from_left, 0, left_units), slab(from_left, 1, left_units)]
-        tail_layers = [slab(from_right, 0, right_units), slab(from_right, 1, right_units)]
+        head_layers, tail_layers = zip(slab(0), slab(1))
+        left_moments, right_moments = slab(2)
         zero = jnp.zeros_like(decay)
         from_head = [head_layers[0], swap(head_layers[0]), head_layers[1], swap(head_layers[1])]
         from_tail = [swap(tail_layers[0]), tail_layers[0], swap(tail_layers[1]), tail_layers[1]]
@@ -644,8 +708,8 @@
             layers[place] = layers[place] + jnp.where(low, zero, from_tail[i])
         total = moment(own_ref, own_unit) * jnp.exp((GRID - reach_x) * log_decay)
         one = jnp.ones_like(decay)
-        total = total + slab(from_left, 2, left_units) * jnp.where(low, beside, one)
-        total = total + slab(from_right, 2, right_units) * jnp.where(low, one, beside)
+        total = total + left_moments * jnp.where(low, beside, one)
+        total = total + right_moments * jnp.where(low, one, beside)
         for far in range(fars):
             power = jnp.where(low, powers[far][0], powers[far][1])
             total = total + moment(far_refs[far], far_units[far]) * jnp.exp(power * log_decay)
@@ -671,7 +735,7 @@
 
 
 def inverse(
-    spectrum, from_left, from_right, own, inner, fars, table, modes, reach_x, reach_y, flips
+    spectrum, from_even, from_odd, own, inner, fars, table, modes, reach_x, reach_y, flips
 ):
     half = reach_x // 2
     lanes = 2 * HALF
@@ -690,7 +754,7 @@
         compiler_params=params(),
         cost_estimate=cost(2 * half * 256 * 256 * 128, 4 * half * GRID * lanes * 2),
         name="inverse",
-    )(spectrum, from_left, from_right, own, inner, *fars, *table, modes)
+    )(spectrum, from_even, from_odd, own, inner, *fars, *table, modes)
 
 
 def inverse_rest_kernel(reach_y, flips, field_high, field_low, high_ref, low_ref, *refs):
@@ -821,14 +885,15 @@
 
 
 def near_kernel(slots, blocks, place_ref, target_ref, *refs):
-    left_ref, right_ref, peers_ref, tile_ref, out_ref, held = refs
+    even_ref, odd_ref, peers_ref, tile_ref, out_ref, held = refs
     count = peers_ref.shape[0]
     held[count : 2 * count, :] = peers_ref[...]
-    for first, ref in ((0, left_ref), (2 * count, right_ref)):
+    on_left = lax.axis_index("wide") & 1
+    for side, ref in ((1 - on_left, even_ref), (on_left, odd_ref)):
         top = from_short(ref[...])
         for piece in range(count // blocks):
             at = 6 + 2 * piece * blocks
-            held[first + piece * blocks : first + (piece + 1) * blocks, :] = decode_rounded(
+            held[pl.ds(side * (2 * count) + piece * blocks, blocks), :] = decode_rounded(
                 top[at : at + blocks], top[at + blocks : at + 2 * blocks]
             )
     out_ref[...] = jnp.zeros_like(out_ref)
@@ -845,9 +910,9 @@
         out_ref[target, :] = out_ref[target, :] + product[:1]
 
 
-def near_field(places, targets, from_left, from_right, peers, tiles, blocks, out_rows):
+def near_field(places, targets, from_even, from_odd, peers, tiles, blocks, out_rows):
     slots = tiles.shape[0]
-    head = from_left.shape[0] - 3 * GRID
+    head = from_even.shape[0] - 3 * GRID
     constant = lambda shape: pl.BlockSpec(shape, lambda i: (0,) * len(shape))
     return pl.pallas_call(
         functools.partial(near_kernel, slots, blocks),
@@ -866,7 +931,7 @@
         compiler_params=params(),
         cost_estimate=cost(2 * slots * 16 * BLOCK * BLOCK, 2 * slots * BLOCK * BLOCK),
         name="near_field",
-    )(places, targets, from_left, from_right, peers, tiles)
+    )(places, targets, from_even, from_odd, peers, tiles)
 
 
 def shards(
@@ -900,41 +965,38 @@
     sources = jnp.where(live, sources, 0)
     targets = jnp.where(live, near_target, out_rows - 1)
 
-    far_moves = [
-        [(i, (i + shift) % x_count) for i in range(x_count)] for shift in range(2, x_count - 1)
+    swaps = lambda pairs: [(i, j) for i, j in pairs] + [(j, i) for i, j in pairs]
+    even_swap = swaps([(i, i + 1) for i in range(0, x_count - 1, 2)])
+    odd_swap = swaps([(i, i + 1) for i in range(1, x_count - 1, 2)])
+    far_swaps = [
+        swaps([(i, i ^ flip) for i in range(x_count) if (i ^ flip) > i + 1])
+        for flip in range(2, x_count)
     ]
-    if x_count > 2:
-        far_moves.append([(0, x_count - 1), (x_count - 1, 0)])
-    to_right = [(i, i + 1) for i in range(x_count - 1)]
-    to_left = [(i + 1, i) for i in range(x_count - 1)]
-
-    pair = lax.axis_size("pair")
-    inside, outside = list(range(pair)), list(range(pair, y_count))
+
+    local, moving = [0], list(range(1, y_count))
 
     def flipped(parts, flips):
         return [
-            part
-            if flip == 0
-            else lax.ppermute(part, Y_AXES, [(i, i ^ flip) for i in range(y_count)])
+            lax.ppermute(part, Y_AXES, [(i, i ^ flip) for i in range(y_count)])
             for flip, part in zip(flips, parts)
         ]
 
     def convolve_and_sample(last, vector, sent, both, places, sample_lines):
-        arrived = flipped(sent, outside)
-        arrived = flipped(spread_rest(vector, both, z_forward, inside), inside) + arrived
-        spectrum, right_going, left_going, own, peers, inner = forward(
+        arrived = flipped(sent, moving)
+        arrived = list(spread_rest(vector, both, z_forward, local)) + arrived
+        spectrum, even_message, odd_message, own, peers, inner = forward(
             arrived, y_forward, modes, reach_x, reach_y, blocks
         )
-        from_left = lax.ppermute(right_going, "wide", to_right)
-        from_right = lax.ppermute(left_going, "wide", to_left)
-        fars = [lax.ppermute(own, "wide", pairs) for pairs in far_moves]
+        from_even = lax.ppermute(even_message, "wide", even_swap)
+        from_odd = lax.ppermute(odd_message, "wide", odd_swap)
+        fars = [lax.ppermute(own, "wide", pairs) for pairs in far_swaps]
         near_part = near_field(
-            sources, targets, from_left, from_right, peers, near_tiles, blocks, out_rows
+            sources, targets, from_even, from_odd, peers, near_tiles, blocks, out_rows
         )
         *sent, high, low = inverse(
             spectrum,
-            from_left,
-            from_right,
+            from_even,
+            from_odd,
             own,
             inner,
             fars,
@@ -942,10 +1004,10 @@
             modes,
             reach_x,
             reach_y,
-            outside,
+            moving,
         )
-        arrived = flipped(sent, outside)
-        arrived = flipped(inverse_rest((high, low), y_inverse, reach_y, inside), inside) + arrived
+        arrived = flipped(sent, moving)
+        arrived = list(inverse_rest((high, low), y_inverse, reach_y, local)) + arrived
         return sample(
             last,
             places,
@@ -961,7 +1023,7 @@
 
     raw = (stencil_base, surface_flag, sample_weights, dipole_weights)
     *sent, high, low, source_coeff, sample_coeff, places = spread(
-        density, None, z_forward, None, raw, reach_x, reach_y, outside
+        density, z_forward, None, raw, reach_x, reach_y, moving
     )
     sample_lines = place_lines(places, sample_coeff)
     source_lines = place_lines(places, source_coeff)
@@ -969,7 +1031,7 @@
         False, density, sent, (high, low), places, sample_lines
     ).reshape(-1)
     *sent, high, low = spread(
-        first_image, places, z_forward, source_lines, None, reach_x, reach_y, outside
+        first_image, z_forward, (places, source_lines), None, reach_x, reach_y, moving
     )
     return convolve_and_sample(True, first_image, sent, (high, low), places, sample_lines)
 

time: 112 us -> 107 us (0.955)
  waiting for transfers between devices: 36.2 us -> 30 us
  local copies, waits for them, and re-layouts: 5.69 us -> 9.5 us
  starting transfers between devices: 31.1 us -> 29.2 us
    ppermute x12, waiting for transfers between devices: 29.5 us -> 23.9 us  [flipped(): lax.ppermute(part, Y_AXES, [(i, i ^ flip) for i in range(y_count)])]
    unnamed x40 -> x44, local copies, waits for them, and re-layouts: 4.61 us -> 8.42 us
    ppermute x8, starting transfers between devices: 22.1 us -> 20.2 us  [the longest x4 17.1 us: convolve_and_sample(): fars = [lax.ppermute(own, 'wide', pairs) for pairs in far_swaps]]
  transfers between devices with their start and end apart: 20 -> 20, of which waited for: 10 -> 9; matrix products, arithmetic and copies ran while one was open for 1% -> 1% of each run, Pallas kernels for 7% -> 10%
where the time goes in v5:
time: 107 us
  Pallas kernels  37.5 us (35%)
  waiting for transfers between devices  30 us (28%)
  starting transfers between devices  29.2 us (27%)
  local copies, waits for them, and re-layouts  9.5 us (9%)
    ppermute x12, waiting for transfers between devices, flipped(): lax.ppermute(part, Y_AXES, [(i, i ^ flip) for i in range(y_count)])  23.9 us
    ppermute x4, starting transfers between devices, convolve_and_sample(): fars = [lax.ppermute(own, 'wide', pairs) for pairs in far_swaps]  17.1 us
    ppermute x12, starting transfers between devices, flipped(): lax.ppermute(part, Y_AXES, [(i, i ^ flip) for i in range(y_count)])  8.94 us
    pallas_call x2, Pallas kernels, spread(): pl.pallas_call(functools.partial(start_kernel if placed is None else spre...  8.53 us
    unnamed x44, local copies, waits for them, and re-layouts  8.42 us
    pallas_call x2, Pallas kernels, sample(): pl.pallas_call(functools.partial(sample_kernel, last, reach_x, reach_y, p...  7.03 us
    pallas_call x2, Pallas kernels, inverse(): pl.pallas_call(functools.partial(inverse_kernel, reach_x, reach_y, flips,...  6.37 us
    ppermute x4, waiting for transfers between devices, convolve_and_sample(): fars = [lax.ppermute(own, 'wide', pairs) for pairs in far_swaps]  6.04 us
  transfers between devices with their start and end apart: 20, of which 9 were waited for; matrix products, arithmetic and copies ran while one was open for 1% of the time, Pallas kernels for 10%

profile of v5, /device:TPU:0, one launch (start us, length us, event | category | flops | bytes accessed | tf_op | source)
XLA Modules:
  0.0 106.5 jit_solution(9246776135296109620)
XLA Ops:
  0.0 0.9 copy-done
  1.0 0.9 copy-done.3
  1.9 0.9 copy-done.12
  2.8 0.9 copy-done.13
  3.7 0.7 copy-done.14
  4.4 0.7 copy-done.17
  5.1 0.7 copy-done.19
  5.8 5.4 %start.1 = (s16[672,128]{1,0:T(8,128)(2,1)S(1)}, s16[672,128]{1,0:T(8,128)(2,1)S(1)}, s16[672,128]{1,0:T(8,128)(2,1)S(1)}, bf16[656,256]{1,0:T(8,128)(2,1)S(1)},...) custom-call(f32[512]{0:T(512)S(1)} %copy-done.14, ...), custom_call_target="tpu_custom_call" | custom-call | flops 169869312 | bytes 4194304 | tf_op jit(solution)/shard_map/start/pallas_call | solution.py:390
  11.2 0.5 collective-permute-start
  11.7 2.6 %collective-permute-start.1 = (s16[672,128]{1,0:T(8,128)(2,1)S(1)}, s16[672,128]{1,0:T(8,128)(2,1)S(1)}, u32[]{:S(2)}, u32[]{:S(2)}) collective-permute-start(s16[672,128]{1,0:T(8,128)(2,1)S(1)} %get-tuple-element.44), channel_id=1, source_target_pairs={{0,2},{1,3},{2,0},{3,1},{4,6},{5,7},{6,4},{7,5},{8,10},{9,11},{10,... | collective-permute-start | bytes 516104 | tf_op jit(solution)/shard_map/ppermute | solution.py:980
  14.3 0.1 collective-permute-start.2
  14.4 0.9 copy-done.1
  15.3 0.9 copy-done.4
  16.3 0.7 copy-done.15
  17.0 0.5 spread_rest.2.refs_0_
  17.5 1.1 %dynamic-slice_bitcast_fusion.refs_5_.refs_9_ = f32[4,256,128]{2,1,0:T(8,128)S(1)} fusion(f32[4,4,256,128]{3,2,1,0:T(8,128)} %constant.73.clone, s32[]{:T(128)S(6)} %select_n.30), kind=kLoop, calls=%fused_computation | loop fusion | bytes 1048580 | tf_op jit(solution)/shard_map/jit(dynamic_index_in_dim)/squeeze | solution.py:958
  18.6 0.9 collective-permute-done.1.refs_2_
  19.5 3.2 %collective-permute-done.2.refs_3_ = s16[672,128]{1,0:T(8,128)(2,1)S(1)} collective-permute-done((s16[672,128]{1,0:T(8,128)(2,1)S(1)}, s16[672,128]{1,0:T(8,128)(2,1)S(1)}, u32[]{:S(2)}, u32[]{:S(2)}) %collective-permute-start.2) | collective-permute-done | bytes 172064 | tf_op jit(solution)/shard_map/ppermute | solution.py:980
  22.7 2.4 %forward.2 = (f32[18,256,128]{2,1,0:T(8,128)S(1)}, s16[816,128]{1,0:T(8,128)(2,1)S(1)}, s16[816,128]{1,0:T(8,128)(2,1)S(1)}, s16[272,128]{1,0:T(8,128)(2,1)S(1)}...) custom-call(s16[672,128]{1,0:T(8,128)(2,1)S(1)} %spread_rest.2.refs_0_, ...), custom_call_target="tpu_custom_call" | custom-call | flops 301989888 | bytes 4718592 | tf_op jit(solution)/shard_map/forward/pallas_call | solution.py:586
  25.1 1.7 %collective-permute-start.3 = (s16[816,128]{1,0:T(8,128)(2,1)S(1)}, s16[816,128]{1,0:T(8,128)(2,1)S(1)}, u32[]{:S(2)}, u32[]{:S(2)}) collective-permute-start(s16[816,128]{1,0:T(8,128)(2,1)S(1)} %get-tuple-element.47), channel_id=1, source_target_pairs={{0,4},{8,12},{4,0},{12,8},{1,5},{9,13},{5,1},{13,9},{2,6},{10,14},... | collective-permute-start | bytes 626696 | tf_op jit(solution)/shard_map/ppermute | solution.py:990
  26.8 0.7 collective-permute-start.4
  27.5 3.9 %collective-permute-start.5 = (s16[272,128]{1,0:T(8,128)(2,1)S(1)}, s16[272,128]{1,0:T(8,128)(2,1)S(1)}, u32[]{:S(2)}, u32[]{:S(2)}) collective-permute-start(s16[272,128]{1,0:T(8,128)(2,1)S(1)} %get-tuple-element.49.refs_3_), channel_id=1, source_target_pairs={{0,8},{4,12},{8,0},{12,4},{1,9},{5,13},{9,1},{13,5},{2,10},{6,14},... | collective-permute-start | bytes 208904 | tf_op jit(solution)/shard_map/ppermute | solution.py:992
  31.4 4.8 %collective-permute-start.6 = (s16[272,128]{1,0:T(8,128)(2,1)S(1)}, s16[272,128]{1,0:T(8,128)(2,1)S(1)}, u32[]{:S(2)}, u32[]{:S(2)}) collective-permute-start(s16[272,128]{1,0:T(8,128)(2,1)S(1)} %get-tuple-element.49.refs_3_), channel_id=1, source_target_pairs={{0,12},{12,0},{1,13},{13,1},{2,14},{14,2},{3,15},{15,3},{16,28},{2... | collective-permute-start | bytes 208904 | tf_op jit(solution)/shard_map/ppermute | solution.py:992
  36.2 2.9 %place_lines.2.refs_6_ = f32[8192,128]{1,0:T(8,128)S(1)} custom-call(s32[2,512]{1,0:T(2,128)S(1)} %get-tuple-element.40.place_ref.refs_1_, f32[256,128]{1,0:T(8,128)S(1)} %get-tuple-element.56.coeff_ref), custom_call_target="tpu_custom_call" | custom-call | flops 1048576 | bytes 4194304 | tf_op jit(solution)/shard_map/place_lines/pallas_call | solution.py:448
  39.2 0.0 copy-start.8
  39.2 2.9 %place_lines.3.refs_5_ = f32[8192,128]{1,0:T(8,128)S(1)} custom-call(s32[2,512]{1,0:T(2,128)S(1)} %get-tuple-element.40.place_ref.refs_1_, f32[256,128]{1,0:T(8,128)S(1)} %get-tuple-element.58.coeff_ref), custom_call_target="tpu_custom_call" | custom-call | flops 1048576 | bytes 4194304 | tf_op jit(solution)/shard_map/place_lines/pallas_call | solution.py:448
  42.1 0.0 copy-start.21
  42.1 0.0 copy-start.6
  42.2 3.2 %inverse.2 = (s16[672,128]{1,0:T(8,128)(2,1)S(1)}, s16[672,128]{1,0:T(8,128)(2,1)S(1)}, s16[672,128]{1,0:T(8,128)(2,1)S(1)}, bf16[18,256,128]{2,1,0:T(8,128)(2,1)S(1)}, bf16[18,256,128]{2,1,0:T(8,128)(2,1)S(1)}) custom-call(f32[18,256,128]{2,1,0:T(8,128)S(1)} %get-tuple-element.46.refs_0_, s16[816,128]{1,0:T(8,128)(2,1)S(1)} %collective-permute-done.3.refs_1_.refs_0_, ...), custom_call_target="tpu_custom_call" | custom-call | flops 301989888 | bytes 4718592 | tf_op jit(solution)/shard_map/inverse/pallas_call | solution.py:745
  45.4 0.0 copy-start.10
  45.4 0.0 copy-start.11
  45.4 0.0 copy-start.18
  45.4 0.1 collective-permute-start.7
  45.5 1.5 %collective-permute-start.8 = (s16[672,128]{1,0:T(8,128)(2,1)S(1)}, s16[672,128]{1,0:T(8,128)(2,1)S(1)}, u32[]{:S(2)}, u32[]{:S(2)}) collective-permute-start(s16[672,128]{1,0:T(8,128)(2,1)S(1)} %get-tuple-element.54), channel_id=1, source_target_pairs={{0,2},{1,3},{2,0},{3,1},{4,6},{5,7},{6,4},{7,5},{8,10},{9,11},{10,... | collective-permute-start | bytes 516104 | tf_op jit(solution)/shard_map/ppermute | solution.py:980
  47.1 0.3 collective-permute-start.9
  47.4 1.0 near_field.2.refs_9_
  48.5 0.9 inverse_rest.2.refs_0_
  49.4 3.4 %collective-permute-done.8.refs_2_ = s16[672,128]{1,0:T(8,128)(2,1)S(1)} collective-permute-done((s16[672,128]{1,0:T(8,128)(2,1)S(1)}, s16[672,128]{1,0:T(8,128)(2,1)S(1)}, u32[]{:S(2)}, u32[]{:S(2)}) %collective-permute-start.8) | collective-permute-done | bytes 172064 | tf_op jit(solution)/shard_map/ppermute | solution.py:980
  52.8 2.8 %collective-permute-done.9.refs_3_ = s16[672,128]{1,0:T(8,128)(2,1)S(1)} collective-permute-done((s16[672,128]{1,0:T(8,128)(2,1)S(1)}, s16[672,128]{1,0:T(8,128)(2,1)S(1)}, u32[]{:S(2)}, u32[]{:S(2)}) %collective-permute-start.9) | collective-permute-done | bytes 172064 | tf_op jit(solution)/shard_map/ppermute | solution.py:980
  55.6 0.0 copy-start.2
  55.6 0.0 copy-start.5
  55.6 3.2 %sample.2.refs_2_.rounded_ref.refs_8_ = f32[4,128]{1,0:T(4,128)S(1)} custom-call(s32[2,512]{1,0:T(2,128)S(1)} %get-tuple-element.40.place_ref.refs_1_, s16[672,128]{1,0:T(8,128)(2,1)S(1)} %inverse_rest.2.refs_0_, s16[672,128]{1,0:T(8,128)(2,1)S(1)} %collective-permute-done.7.refs_1_, s16[672,128]{1,0:T(8,128)(2,1)S(1)} %collective-permute-done.8.refs_2_, ...), custom_call_target="tpu_custom_call" | custom-call | flops 169869312 | bytes 4194304 | tf_op jit(solution)/shard_map/sample/pallas_call | solution.py:863
  58.8 3.1 %spread.1 = (s16[672,128]{1,0:T(8,128)(2,1)S(1)}, s16[672,128]{1,0:T(8,128)(2,1)S(1)}, s16[672,128]{1,0:T(8,128)(2,1)S(1)}, bf16[656,256]{1,0:T(8,128)(2,1)S(1)}, bf16[656,256]{1,0:T(8,128)(2,1)S(1)}) custom-call(f32[512]{0:T(512)S(1)} %bitcast.6, s32[2,512]{1,0:T(2,128)S(1)} %get-tuple-element.40.place_ref.refs_1_, ...), custom_call_target="tpu_custom_call" | custom-call | flops 169869312 | bytes 4194304 | tf_op jit(solution)/shard_map/spread/pallas_call | solution.py:390
  61.9 0.3 collective-permute-start.10
  62.3 1.5 %collective-permute-start.11 = (s16[672,128]{1,0:T(8,128)(2,1)S(1)}, s16[672,128]{1,0:T(8,128)(2,1)S(1)}, u32[]{:S(2)}, u32[]{:S(2)}) collective-permute-start(s16[672,128]{1,0:T(8,128)(2,1)S(1)} %get-tuple-element.62), channel_id=1, source_target_pairs={{0,2},{1,3},{2,0},{3,1},{4,6},{5,7},{6,4},{7,5},{8,10},{9,11},{10,... | collective-permute-start | bytes 516104 | tf_op jit(solution)/shard_map/ppermute | solution.py:980
  63.8 0.1 collective-permute-start.12
  63.9 0.5 spread_rest.3.refs_0_
  64.4 5.1 %collective-permute-done.11.refs_2_ = s16[672,128]{1,0:T(8,128)(2,1)S(1)} collective-permute-done((s16[672,128]{1,0:T(8,128)(2,1)S(1)}, s16[672,128]{1,0:T(8,128)(2,1)S(1)}, u32[]{:S(2)}, u32[]{:S(2)}) %collective-permute-start.11) | collective-permute-done | bytes 172064 | tf_op jit(solution)/shard_map/ppermute | solution.py:980
  69.5 2.3 %collective-permute-done.12.refs_3_ = s16[672,128]{1,0:T(8,128)(2,1)S(1)} collective-permute-done((s16[672,128]{1,0:T(8,128)(2,1)S(1)}, s16[672,128]{1,0:T(8,128)(2,1)S(1)}, u32[]{:S(2)}, u32[]{:S(2)}) %collective-permute-start.12) | collective-permute-done | bytes 172064 | tf_op jit(solution)/shard_map/ppermute | solution.py:980
  71.8 2.4 %forward.3 = (f32[18,256,128]{2,1,0:T(8,128)S(1)}, s16[816,128]{1,0:T(8,128)(2,1)S(1)}, s16[816,128]{1,0:T(8,128)(2,1)S(1)}, s16[272,128]{1,0:T(8,128)(2,1)S(1)}...) custom-call(s16[672,128]{1,0:T(8,128)(2,1)S(1)} %spread_rest.3.refs_0_, ...), custom_call_target="tpu_custom_call" | custom-call | flops 301989888 | bytes 4718592 | tf_op jit(solution)/shard_map/forward/pallas_call | solution.py:586
  74.2 0.1 collective-permute-start.13
  74.3 0.7 collective-permute-start.14
  75.0 4.8 %collective-permute-start.15 = (s16[272,128]{1,0:T(8,128)(2,1)S(1)}, s16[272,128]{1,0:T(8,128)(2,1)S(1)}, u32[]{:S(2)}, u32[]{:S(2)}) collective-permute-start(s16[272,128]{1,0:T(8,128)(2,1)S(1)} %get-tuple-element.67.refs_3_), channel_id=1, source_target_pairs={{0,8},{4,12},{8,0},{12,4},{1,9},{5,13},{9,1},{13,5},{2,10},{6,14},... | collective-permute-start | bytes 208904 | tf_op jit(solution)/shard_map/ppermute | solution.py:992
  79.7 3.6 %collective-permute-start.16 = (s16[272,128]{1,0:T(8,128)(2,1)S(1)}, s16[272,128]{1,0:T(8,128)(2,1)S(1)}, u32[]{:S(2)}, u32[]{:S(2)}) collective-permute-start(s16[272,128]{1,0:T(8,128)(2,1)S(1)} %get-tuple-element.67.refs_3_), channel_id=1, source_target_pairs={{0,12},{12,0},{1,13},{13,1},{2,14},{14,2},{3,15},{15,3},{16,28},{2... | collective-permute-start | bytes 208904 | tf_op jit(solution)/shard_map/ppermute | solution.py:992
  83.4 6.0 %collective-permute-done.15.refs_5_ = s16[272,128]{1,0:T(8,128)(2,1)S(1)} collective-permute-done((s16[272,128]{1,0:T(8,128)(2,1)S(1)}, s16[272,128]{1,0:T(8,128)(2,1)S(1)}, u32[]{:S(2)}, u32[]{:S(2)}) %collective-permute-start.15) | collective-permute-done | bytes 69664 | tf_op jit(solution)/shard_map/ppermute | solution.py:992
  89.4 3.2 %inverse.3 = (s16[672,128]{1,0:T(8,128)(2,1)S(1)}, s16[672,128]{1,0:T(8,128)(2,1)S(1)}, s16[672,128]{1,0:T(8,128)(2,1)S(1)}, bf16[18,256,128]{2,1,0:T(8,128)(2,1)S(1)}, bf16[18,256,128]{2,1,0:T(8,128)(2,1)S(1)}) custom-call(f32[18,256,128]{2,1,0:T(8,128)S(1)} %get-tuple-element.64.refs_0_, s16[816,128]{1,0:T(8,128)(2,1)S(1)} %collective-permute-done.13.refs_1_.refs_0_, ...), custom_call_target="tpu_custom_call" | custom-call | flops 301989888 | bytes 4718592 | tf_op jit(solution)/shard_map/inverse/pallas_call | solution.py:745
  92.6 0.1 collective-permute-start.17
  92.7 1.5 %collective-permute-start.18 = (s16[672,128]{1,0:T(8,128)(2,1)S(1)}, s16[672,128]{1,0:T(8,128)(2,1)S(1)}, u32[]{:S(2)}, u32[]{:S(2)}) collective-permute-start(s16[672,128]{1,0:T(8,128)(2,1)S(1)} %get-tuple-element.72), channel_id=1, source_target_pairs={{0,2},{1,3},{2,0},{3,1},{4,6},{5,7},{6,4},{7,5},{8,10},{9,11},{10,... | collective-permute-start | bytes 516104 | tf_op jit(solution)/shard_map/ppermute | solution.py:980
  94.2 0.3 collective-permute-start.19
  94.6 1.0 near_field.3.refs_9_
  95.6 0.9 inverse_rest.3.refs_0_
  96.5 3.4 %collective-permute-done.18.refs_2_ = s16[672,128]{1,0:T(8,128)(2,1)S(1)} collective-permute-done((s16[672,128]{1,0:T(8,128)(2,1)S(1)}, s16[672,128]{1,0:T(8,128)(2,1)S(1)}, u32[]{:S(2)}, u32[]{:S(2)}) %collective-permute-start.18) | collective-permute-done | bytes 172064 | tf_op jit(solution)/shard_map/ppermute | solution.py:980
  99.9 2.8 %collective-permute-done.19.refs_3_ = s16[672,128]{1,0:T(8,128)(2,1)S(1)} collective-permute-done((s16[672,128]{1,0:T(8,128)(2,1)S(1)}, s16[672,128]{1,0:T(8,128)(2,1)S(1)}, u32[]{:S(2)}, u32[]{:S(2)}) %collective-permute-start.19) | collective-permute-done | bytes 172064 | tf_op jit(solution)/shard_map/ppermute | solution.py:980
  102.7 3.8 %sample.3 = f32[2,512]{1,0:T(2,128)} custom-call(s32[2,512]{1,0:T(2,128)S(1)} %get-tuple-element.40.place_ref.refs_1_, s16[672,128]{1,0:T(8,128)(2,1)S(1)} %inverse_rest.3.refs_0_, s16[672,128]{1,0:T(8,128)(2,1)S(1)} %collective-permute-done.17.refs_1_, s16[672,128]{1,0:T(8,128)(2,1)S(1)} %collective-permute-done.18.refs_2_, ...), custom_call_target="tpu_custom_call" | custom-call | flops 169869312 | bytes 4194304 | tf_op jit(solution)/shard_map/sample/pallas_call | solution.py:863
  (38 shorter events, 0.1 us)
Async XLA Ops:
  0.0 0.9 copy-start
  1.0 0.9 copy-start.3
  1.9 0.9 copy-start.12
  2.8 0.9 copy-start.13
  3.7 0.7 copy-start.14
  4.4 0.7 copy-start.17
  5.1 0.7 copy-start.19
  5.8 16.9 %copy-start.9 = (bf16[256,480]{1,0:T(8,128)(2,1)S(1)}, bf16[256,480]{1,0:T(8,128)(2,1)}, u32[]{:S(2)}) copy-start(bf16[256,480]{1,0:T(8,128)(2,1)} %constant.76.clone.refs_4_) | copy-start | bytes 737284
  11.2 7.3 %collective-permute-start = (s16[672,128]{1,0:T(8,128)(2,1)S(1)}, s16[672,128]{1,0:T(8,128)(2,1)S(1)}, u32[]{:S(2)}, u32[]{:S(2)}) collective-permute-start(s16[672,128]{1,0:T(8,128)(2,1)S(1)} %get-tuple-element.43), channel_id=1, source_target_pairs={{0,1},{1,0},{2,3},{3,2},{4,5},{5,4},{6,7},{7,6},{8,9},{9,8},{10,11... | collective-permute-start | bytes 516104 | tf_op jit(solution)/shard_map/ppermute | solution.py:980
  11.7 7.8 %collective-permute-start.1 = (s16[672,128]{1,0:T(8,128)(2,1)S(1)}, s16[672,128]{1,0:T(8,128)(2,1)S(1)}, u32[]{:S(2)}, u32[]{:S(2)}) collective-permute-start(s16[672,128]{1,0:T(8,128)(2,1)S(1)} %get-tuple-element.44), channel_id=1, source_target_pairs={{0,2},{1,3},{2,0},{3,1},{4,6},{5,7},{6,4},{7,5},{8,10},{9,11},{10,... | collective-permute-start | bytes 516104 | tf_op jit(solution)/shard_map/ppermute | solution.py:980
  14.3 8.4 %collective-permute-start.2 = (s16[672,128]{1,0:T(8,128)(2,1)S(1)}, s16[672,128]{1,0:T(8,128)(2,1)S(1)}, u32[]{:S(2)}, u32[]{:S(2)}) collective-permute-start(s16[672,128]{1,0:T(8,128)(2,1)S(1)} %get-tuple-element.45), channel_id=1, source_target_pairs={{0,3},{1,2},{2,1},{3,0},{4,7},{5,6},{6,5},{7,4},{8,11},{9,10},{10,... | collective-permute-start | bytes 516104 | tf_op jit(solution)/shard_map/ppermute | solution.py:980
  14.4 0.9 copy-start.1
  15.3 0.9 copy-start.4
  16.3 0.7 copy-start.15
  25.1 17.1 %collective-permute-start.3 = (s16[816,128]{1,0:T(8,128)(2,1)S(1)}, s16[816,128]{1,0:T(8,128)(2,1)S(1)}, u32[]{:S(2)}, u32[]{:S(2)}) collective-permute-start(s16[816,128]{1,0:T(8,128)(2,1)S(1)} %get-tuple-element.47), channel_id=1, source_target_pairs={{0,4},{8,12},{4,0},{12,8},{1,5},{9,13},{5,1},{13,9},{2,6},{10,14},... | collective-permute-start | bytes 626696 | tf_op jit(solution)/shard_map/ppermute | solution.py:990
  26.8 15.4 %collective-permute-start.4 = (s16[816,128]{1,0:T(8,128)(2,1)S(1)}, s16[816,128]{1,0:T(8,128)(2,1)S(1)}, u32[]{:S(2)}, u32[]{:S(2)}) collective-permute-start(s16[816,128]{1,0:T(8,128)(2,1)S(1)} %get-tuple-element.48), channel_id=1, source_target_pairs={{4,8},{8,4},{5,9},{9,5},{6,10},{10,6},{7,11},{11,7},{20,24},{24,20... | collective-permute-start | bytes 626696 | tf_op jit(solution)/shard_map/ppermute | solution.py:991
  27.5 14.7 %collective-permute-start.5 = (s16[272,128]{1,0:T(8,128)(2,1)S(1)}, s16[272,128]{1,0:T(8,128)(2,1)S(1)}, u32[]{:S(2)}, u32[]{:S(2)}) collective-permute-start(s16[272,128]{1,0:T(8,128)(2,1)S(1)} %get-tuple-element.49.refs_3_), channel_id=1, source_target_pairs={{0,8},{4,12},{8,0},{12,4},{1,9},{5,13},{9,1},{13,5},{2,10},{6,14},... | collective-permute-start | bytes 208904 | tf_op jit(solution)/shard_map/ppermute | solution.py:992
  31.4 10.8 %collective-permute-start.6 = (s16[272,128]{1,0:T(8,128)(2,1)S(1)}, s16[272,128]{1,0:T(8,128)(2,1)S(1)}, u32[]{:S(2)}, u32[]{:S(2)}) collective-permute-start(s16[272,128]{1,0:T(8,128)(2,1)S(1)} %get-tuple-element.49.refs_3_), channel_id=1, source_target_pairs={{0,12},{12,0},{1,13},{13,1},{2,14},{14,2},{3,15},{15,3},{16,28},{2... | collective-permute-start | bytes 208904 | tf_op jit(solution)/shard_map/ppermute | solution.py:992
  39.2 3.0 %copy-start.7 = (bf16[4,48,256]{2,1,0:T(8,128)(2,1)S(1)}, bf16[4,48,256]{2,1,0:T(8,128)(2,1)}, u32[]{:S(2)}) copy-start(bf16[4,48,256]{2,1,0:T(8,128)(2,1)} %constant.77.clone.refs_7_.high_ref) | copy-start | bytes 294916
  39.2 3.0 %copy-start.8 = (bf16[4,48,256]{2,1,0:T(8,128)(2,1)S(1)}, bf16[4,48,256]{2,1,0:T(8,128)(2,1)}, u32[]{:S(2)}) copy-start(bf16[4,48,256]{2,1,0:T(8,128)(2,1)} %constant.78.clone.refs_8_.low_ref) | copy-start | bytes 294916
  42.1 5.3 %copy-start.20 = (s32[24]{0:T(128)S(1)}, s32[24]{0:T(128)}, u32[]{:S(2)}) copy-start(s32[24]{0:T(128)} %param.21) | copy-start | bytes 292
  42.1 5.3 %copy-start.21 = (s32[24]{0:T(128)S(1)}, s32[24]{0:T(128)}, u32[]{:S(2)}) copy-start(s32[24]{0:T(128)} %param.22) | copy-start | bytes 292
  42.1 5.3 %copy-start.6 = (bf16[24,128,128]{2,1,0:T(8,128)(2,1)S(1)}, bf16[24,128,128]{2,1,0:T(8,128)(2,1)}, u32[]{:S(2)}) copy-start(bf16[24,128,128]{2,1,0:T(8,128)(2,1)} %refs_3_.5) | copy-start | bytes 2359300
  45.4 10.2 %copy-start.10 = (bf16[4,128,256]{2,1,0:T(8,128)(2,1)S(1)}, bf16[4,128,256]{2,1,0:T(8,128)(2,1)}, u32[]{:S(2)}) copy-start(bf16[4,128,256]{2,1,0:T(8,128)(2,1)} %constant.79.clone.refs_4_) | copy-start | bytes 786436
  45.4 10.1 %copy-start.11 = (bf16[4,128,256]{2,1,0:T(8,128)(2,1)S(1)}, bf16[4,128,256]{2,1,0:T(8,128)(2,1)}, u32[]{:S(2)}) copy-start(bf16[4,128,256]{2,1,0:T(8,128)(2,1)} %constant.80.clone.refs_5_) | copy-start | bytes 786436
  45.4 10.1 %copy-start.16 = (f32[512]{0:T(512)S(1)}, f32[512]{0:T(512)}, u32[]{:S(2)}) copy-start(f32[512]{0:T(512)} %refs_0_.1) | copy-start | bytes 6148
  45.4 10.1 %copy-start.18 = (s32[512]{0:T(512)S(1)}, s32[512]{0:T(512)}, u32[]{:S(2)}) copy-start(s32[512]{0:T(512)} %param.17) | copy-start | bytes 6148
  45.4 3.9 %collective-permute-start.7 = (s16[672,128]{1,0:T(8,128)(2,1)S(1)}, s16[672,128]{1,0:T(8,128)(2,1)S(1)}, u32[]{:S(2)}, u32[]{:S(2)}) collective-permute-start(s16[672,128]{1,0:T(8,128)(2,1)S(1)} %get-tuple-element.53), channel_id=1, source_target_pairs={{0,1},{1,0},{2,3},{3,2},{4,5},{5,4},{6,7},{7,6},{8,9},{9,8},{10,11... | collective-permute-start | bytes 516104 | tf_op jit(solution)/shard_map/ppermute | solution.py:980
  45.5 7.2 %collective-permute-start.8 = (s16[672,128]{1,0:T(8,128)(2,1)S(1)}, s16[672,128]{1,0:T(8,128)(2,1)S(1)}, u32[]{:S(2)}, u32[]{:S(2)}) collective-permute-start(s16[672,128]{1,0:T(8,128)(2,1)S(1)} %get-tuple-element.54), channel_id=1, source_target_pairs={{0,2},{1,3},{2,0},{3,1},{4,6},{5,7},{6,4},{7,5},{8,10},{9,11},{10,... | collective-permute-start | bytes 516104 | tf_op jit(solution)/shard_map/ppermute | solution.py:980
  47.1 8.5 %collective-permute-start.9 = (s16[672,128]{1,0:T(8,128)(2,1)S(1)}, s16[672,128]{1,0:T(8,128)(2,1)S(1)}, u32[]{:S(2)}, u32[]{:S(2)}) collective-permute-start(s16[672,128]{1,0:T(8,128)(2,1)S(1)} %get-tuple-element.55), channel_id=1, source_target_pairs={{0,3},{1,2},{2,1},{3,0},{4,7},{5,6},{6,5},{7,4},{8,11},{9,10},{10,... | collective-permute-start | bytes 516104 | tf_op jit(solution)/shard_map/ppermute | solution.py:980
  55.6 3.2 %copy-start.2 = (bf16[4,256,128]{2,1,0:T(8,128)(2,1)S(1)}, bf16[4,256,128]{2,1,0:T(8,128)(2,1)}, u32[]{:S(2)}) copy-start(bf16[4,256,128]{2,1,0:T(8,128)(2,1)} %constant.74.clone.refs_2_.high_ref.refs_3_) | copy-start | bytes 786436
  55.6 3.2 %copy-start.5 = (bf16[4,256,128]{2,1,0:T(8,128)(2,1)S(1)}, bf16[4,256,128]{2,1,0:T(8,128)(2,1)}, u32[]{:S(2)}) copy-start(bf16[4,256,128]{2,1,0:T(8,128)(2,1)} %constant.75.clone.refs_3_.low_ref.refs_4_) | copy-start | bytes 786436
  61.9 2.5 %collective-permute-start.10 = (s16[672,128]{1,0:T(8,128)(2,1)S(1)}, s16[672,128]{1,0:T(8,128)(2,1)S(1)}, u32[]{:S(2)}, u32[]{:S(2)}) collective-permute-start(s16[672,128]{1,0:T(8,128)(2,1)S(1)} %get-tuple-element.61), channel_id=1, source_target_pairs={{0,1},{1,0},{2,3},{3,2},{4,5},{5,4},{6,7},{7,6},{8,9},{9,8},{10,11... | collective-permute-start | bytes 516104 | tf_op jit(solution)/shard_map/ppermute | solution.py:980
  62.3 7.2 %collective-permute-start.11 = (s16[672,128]{1,0:T(8,128)(2,1)S(1)}, s16[672,128]{1,0:T(8,128)(2,1)S(1)}, u32[]{:S(2)}, u32[]{:S(2)}) collective-permute-start(s16[672,128]{1,0:T(8,128)(2,1)S(1)} %get-tuple-element.62), channel_id=1, source_target_pairs={{0,2},{1,3},{2,0},{3,1},{4,6},{5,7},{6,4},{7,5},{8,10},{9,11},{10,... | collective-permute-start | bytes 516104 | tf_op jit(solution)/shard_map/ppermute | solution.py:980
  63.8 8.0 %collective-permute-start.12 = (s16[672,128]{1,0:T(8,128)(2,1)S(1)}, s16[672,128]{1,0:T(8,128)(2,1)S(1)}, u32[]{:S(2)}, u32[]{:S(2)}) collective-permute-start(s16[672,128]{1,0:T(8,128)(2,1)S(1)} %get-tuple-element.63), channel_id=1, source_target_pairs={{0,3},{1,2},{2,1},{3,0},{4,7},{5,6},{6,5},{7,4},{8,11},{9,10},{10,... | collective-permute-start | bytes 516104 | tf_op jit(solution)/shard_map/ppermute | solution.py:980
  74.2 15.2 %collective-permute-start.13 = (s16[816,128]{1,0:T(8,128)(2,1)S(1)}, s16[816,128]{1,0:T(8,128)(2,1)S(1)}, u32[]{:S(2)}, u32[]{:S(2)}) collective-permute-start(s16[816,128]{1,0:T(8,128)(2,1)S(1)} %get-tuple-element.65), channel_id=1, source_target_pairs={{0,4},{8,12},{4,0},{12,8},{1,5},{9,13},{5,1},{13,9},{2,6},{10,14},... | collective-permute-start | bytes 626696 | tf_op jit(solution)/shard_map/ppermute | solution.py:990
  74.3 15.1 %collective-permute-start.14 = (s16[816,128]{1,0:T(8,128)(2,1)S(1)}, s16[816,128]{1,0:T(8,128)(2,1)S(1)}, u32[]{:S(2)}, u32[]{:S(2)}) collective-permute-start(s16[816,128]{1,0:T(8,128)(2,1)S(1)} %get-tuple-element.66), channel_id=1, source_target_pairs={{4,8},{8,4},{5,9},{9,5},{6,10},{10,6},{7,11},{11,7},{20,24},{24,20... | collective-permute-start | bytes 626696 | tf_op jit(solution)/shard_map/ppermute | solution.py:991
  75.0 14.4 %collective-permute-start.15 = (s16[272,128]{1,0:T(8,128)(2,1)S(1)}, s16[272,128]{1,0:T(8,128)(2,1)S(1)}, u32[]{:S(2)}, u32[]{:S(2)}) collective-permute-start(s16[272,128]{1,0:T(8,128)(2,1)S(1)} %get-tuple-element.67.refs_3_), channel_id=1, source_target_pairs={{0,8},{4,12},{8,0},{12,4},{1,9},{5,13},{9,1},{13,5},{2,10},{6,14},... | collective-permute-start | bytes 208904 | tf_op jit(solution)/shard_map/ppermute | solution.py:992
  79.7 9.7 %collective-permute-start.16 = (s16[272,128]{1,0:T(8,128)(2,1)S(1)}, s16[272,128]{1,0:T(8,128)(2,1)S(1)}, u32[]{:S(2)}, u32[]{:S(2)}) collective-permute-start(s16[272,128]{1,0:T(8,128)(2,1)S(1)} %get-tuple-element.67.refs_3_), channel_id=1, source_target_pairs={{0,12},{12,0},{1,13},{13,1},{2,14},{14,2},{3,15},{15,3},{16,28},{2... | collective-permute-start | bytes 208904 | tf_op jit(solution)/shard_map/ppermute | solution.py:992
  92.6 3.9 %collective-permute-start.17 = (s16[672,128]{1,0:T(8,128)(2,1)S(1)}, s16[672,128]{1,0:T(8,128)(2,1)S(1)}, u32[]{:S(2)}, u32[]{:S(2)}) collective-permute-start(s16[672,128]{1,0:T(8,128)(2,1)S(1)} %get-tuple-element.71), channel_id=1, source_target_pairs={{0,1},{1,0},{2,3},{3,2},{4,5},{5,4},{6,7},{7,6},{8,9},{9,8},{10,11... | collective-permute-start | bytes 516104 | tf_op jit(solution)/shard_map/ppermute | solution.py:980
  92.7 7.2 %collective-permute-start.18 = (s16[672,128]{1,0:T(8,128)(2,1)S(1)}, s16[672,128]{1,0:T(8,128)(2,1)S(1)}, u32[]{:S(2)}, u32[]{:S(2)}) collective-permute-start(s16[672,128]{1,0:T(8,128)(2,1)S(1)} %get-tuple-element.72), channel_id=1, source_target_pairs={{0,2},{1,3},{2,0},{3,1},{4,6},{5,7},{6,4},{7,5},{8,10},{9,11},{10,... | collective-permute-start | bytes 516104 | tf_op jit(solution)/shard_map/ppermute | solution.py:980
  94.2 8.5 %collective-permute-start.19 = (s16[672,128]{1,0:T(8,128)(2,1)S(1)}, s16[672,128]{1,0:T(8,128)(2,1)S(1)}, u32[]{:S(2)}, u32[]{:S(2)}) collective-permute-start(s16[672,128]{1,0:T(8,128)(2,1)S(1)} %get-tuple-element.73), channel_id=1, source_target_pairs={{0,3},{1,2},{2,1},{3,0},{4,7},{5,6},{6,5},{7,4},{8,11},{9,10},{10,... | collective-permute-start | bytes 516104 | tf_op jit(solution)/shard_map/ppermute | solution.py:980

commit v6 on v5

--- a/solution.py
+++ b/solution.py
@@ -21,6 +21,8 @@
 F32 = jnp.float32
 BF16 = jnp.bfloat16
 VMEM_LIMIT = 24 * 1024 * 1024
+START_LIMIT = 60 * 1024 * 1024
+FAR_FLOPS = 8 * 10**9
 GROUP = 32
 CHAINS = 2
 
@@ -60,6 +62,10 @@
 
 def whole_vmem():
     return pl.BlockSpec(memory_space=pltpu.VMEM)
+
+
+def anywhere():
+    return pl.BlockSpec(memory_space=pl.ANY)
 
 
 def in_smem():
@@ -126,7 +132,7 @@
     return high, (table - high.astype(np.float64)).astype(jnp.bfloat16)
 
 
-def tables(y_count, span_y):
+def tables(y_count, pair, span_y):
     depth = GRID // y_count
     reach = span_y + 4
     waves = np.arange(GRID)
@@ -152,8 +158,9 @@
         y_table = cas(step * np.outer(waves, cells))
         y_forward[:, block, :reach] = y_table
         y_inverse[block, :reach] = y_table.T / GRID
-    y_forward = halves(y_forward.reshape(GRID, -1))
-    y_forward = np.concatenate([y_forward[0], y_forward[0], y_forward[1]], axis=1)
+    y_forward = y_forward.reshape(GRID, y_count // pair, -1).transpose(1, 0, 2)
+    y_forward = halves(y_forward)
+    y_forward = np.concatenate([y_forward[0], y_forward[0], y_forward[1]], axis=2)
     root = np.sqrt(shift * (shift + 4.0))
     decay = 2.0 / (2.0 + shift + root)
     log_decay = np.log(decay)
@@ -395,7 +402,9 @@
         out_specs=[whole_vmem()] * len(out_shapes),
         out_shape=out_shapes,
         scratch_shapes=work,
-        compiler_params=params(),
+        compiler_params=pltpu.CompilerParams(
+            vmem_limit_bytes=START_LIMIT if placed is None else VMEM_LIMIT
+        ),
         cost_estimate=cost(2 * half * 256 * 512, 4 * 16 * count * REGION),
         name="start" if placed is None else "spread",
     )(*operands)
@@ -423,7 +432,8 @@
     )(vector.reshape(blocks, BLOCK), *both, *table)
 
 
-def lines_kernel(place_ref, coeff_ref, out_ref):
+def lines_kernel(place_ref, coeff_ref, *refs):
+    out_ref = refs[-1]
     lanes = lax.broadcasted_iota(jnp.int32, (8, REGION), 1)
 
     def body(group, carry):
@@ -442,32 +452,94 @@
     lax.fori_loop(0, place_ref.shape[1] // GROUP, body, 0)
 
 
-def place_lines(places, coeff):
+def place_lines(places, coeff, awaited):
     count = places.shape[1]
     shape = (count * 16, REGION)
     return pl.pallas_call(
         lines_kernel,
-        in_specs=[in_smem(), whole_vmem()],
+        in_specs=[in_smem(), whole_vmem()] + [anywhere()] * len(awaited),
         out_specs=whole_vmem(),
         out_shape=jax.ShapeDtypeStruct(shape, F32),
         compiler_params=params(),
         cost_estimate=cost(16 * count * REGION, 4 * 16 * count * REGION),
         name="place_lines",
-    )(places, coeff)
-
-
-def forward_kernel(reach_x, reach_y, blocks, pieces, *refs):
-    parts = refs[:pieces]
-    table_ref, modes_ref = refs[pieces : pieces + 2]
-    spectrum, even_out, odd_out, own_out, peers_out, inner_out = refs[pieces + 2 : pieces + 8]
-    opened, stacked, slabs, head = refs[pieces + 8 :]
+    )(places, coeff, *awaited)
+
+
+def stack_pieces(parts, reach_x, reach_y, top, opened, stacked):
     half = reach_x // 2
     pitch = up_to(reach_y, 8)
-    tall = pieces * pitch
+    tall = len(parts) * pitch
+    core = lax.axis_index("pair")
+    for bit, part in enumerate(parts):
+        first = from_short(part[:top, :])
+        opened[...] = from_short(part[top:, :]) * unit(first[0:1], first[1:2])
+        place = (core ^ bit) * pitch
+        for i in range(half):
+            stacked[pl.ds(pl.multiple_of(i * tall + place, 8), reach_y), :] = opened[
+                i * reach_y : (i + 1) * reach_y, :
+            ]
+
+
+def transform_pieces(table, stacked, before, spectrum):
+    half = spectrum.shape[0]
+    tall = stacked.shape[0] // half
+
+    def tripled(values):
+        high, low = split(values)
+        return jnp.concatenate([high, low, high], axis=0)
+
+    for i in range(0, half, 2):
+        places = range(i, min(i + 2, half))
+        held = jnp.concatenate([stacked[j * tall : (j + 1) * tall, :] for j in places], axis=1)
+        result = dot(table, tripled(held))
+        for j in places:
+            made = result[:, (j - i) * 2 * HALF : (j - i + 1) * 2 * HALF]
+            spectrum[j] = made if before is None else before[j] + made
+
+
+def forward_early_kernel(reach_x, reach_y, pair, *refs):
+    parts = refs[:pair]
+    table_ref, spectrum, opened, stacked = refs[pair:]
     top = parts[0].shape[0] - opened.shape[0]
-    mine = y_position()
-    if pitch > reach_y:
-        stacked[...] = jnp.zeros_like(stacked)
+    stacked[...] = jnp.zeros_like(stacked)
+    stack_pieces(parts, reach_x, reach_y, top, opened, stacked)
+    transform_pieces(table_ref[lax.axis_index("narrow")], stacked, None, spectrum)
+
+
+def stacking_scratch(pair, reach_x, reach_y):
+    half = reach_x // 2
+    return [
+        pltpu.VMEM((up_to(half * reach_y, 16), 2 * HALF), F32),
+        pltpu.VMEM((half * pair * up_to(reach_y, 8), 2 * HALF), F32),
+    ]
+
+
+def forward_early(parts, table, reach_x, reach_y):
+    half = reach_x // 2
+    pair = len(parts)
+    return pl.pallas_call(
+        functools.partial(forward_early_kernel, reach_x, reach_y, pair),
+        in_specs=[whole_vmem()] * (pair + 1),
+        out_specs=whole_vmem(),
+        out_shape=jax.ShapeDtypeStruct((half, GRID, 2 * HALF), F32),
+        scratch_shapes=stacking_scratch(pair, reach_x, reach_y),
+        compiler_params=params(),
+        cost_estimate=cost(2 * half * 256 * 256 * 128, 4 * half * GRID * 2 * HALF * 2),
+        name="forward_early",
+    )(*parts, table)
+
+
+def forward_kernel(reach_x, reach_y, blocks, pieces, awaited, *refs):
+    parts = refs[:pieces]
+    early_ref, table_ref, modes_ref = refs[pieces : pieces + 3]
+    refs = refs[: pieces + 3] + refs[pieces + 3 + awaited :]
+    spectrum, even_out, odd_out, own_out, peers_out, inner_out = refs[pieces + 3 : pieces + 9]
+    opened, stacked, slabs, head = refs[pieces + 9 :]
+    half = reach_x // 2
+    pair = lax.axis_size("pair")
+    top = parts[0].shape[0] - opened.shape[0]
+    stacked[...] = jnp.zeros_like(stacked)
     head[...] = jnp.zeros_like(head)
     for piece in range(pieces):
         first = from_short(parts[piece][:top, :])
@@ -476,29 +548,11 @@
         at = 6 + 2 * piece * blocks
         head[at : at + blocks, :] = mantissa
         head[at + blocks : at + 2 * blocks, :] = exponent
-        opened[...] = from_short(parts[piece][top:, :]) * unit(first[0:1], first[1:2])
-        place = (mine ^ piece) * pitch
-        for i in range(half):
-            stacked[pl.ds(pl.multiple_of(i * tall + place, 8), reach_y), :] = opened[
-                i * reach_y : (i + 1) * reach_y, :
-            ]
-    table = table_ref[...]
-
-    def tripled(values):
-        high, low = split(values)
-        return jnp.concatenate([high, low, high], axis=0)
-
-    for i in range(0, half, 2):
-        if i + 1 < half:
-            pair = jnp.concatenate(
-                [stacked[i * tall : (i + 1) * tall, :], stacked[(i + 1) * tall : (i + 2) * tall, :]],
-                axis=1,
-            )
-            both = dot(table, tripled(pair))
-            spectrum[i] = both[:, : 2 * HALF]
-            spectrum[i + 1] = both[:, 2 * HALF :]
-        else:
-            spectrum[i] = dot(table, tripled(stacked[i * tall : (i + 1) * tall, :]))
+    before = early_ref
+    for chip in range(1, pieces // pair):
+        stack_pieces(parts[chip * pair : (chip + 1) * pair], reach_x, reach_y, top, opened, stacked)
+        transform_pieces(table_ref[lax.axis_index("narrow") ^ chip], stacked, before, spectrum)
+        before = spectrum
 
     chunk = 32
 
@@ -576,16 +630,17 @@
     own_out[16:, :] = quantize(slabs[6], exponent, fraction)
 
 
-def forward(parts, table, modes, reach_x, reach_y, blocks):
+def forward(parts, early, table, modes, reach_x, reach_y, blocks, awaited):
     pieces = len(parts)
     half = reach_x // 2
     lanes = 2 * HALF
     head = up_to(6 + 2 * pieces * blocks, 16)
-    body = up_to(half * reach_y, 16)
     short = lambda rows: jax.ShapeDtypeStruct((rows, lanes), jnp.int16)
     return pl.pallas_call(
-        functools.partial(forward_kernel, reach_x, reach_y, blocks, pieces),
-        in_specs=[whole_vmem()] * (pieces + 2),
+        functools.partial(
+            forward_kernel, reach_x, reach_y, blocks, pieces, len(awaited)
+        ),
+        in_specs=[whole_vmem()] * (pieces + 3) + [anywhere()] * len(awaited),
         out_specs=[whole_vmem()] * 6,
         out_shape=[
             jax.ShapeDtypeStruct((half, GRID, lanes), F32),
@@ -595,16 +650,50 @@
             jax.ShapeDtypeStruct((pieces * blocks, BLOCK), F32),
             jax.ShapeDtypeStruct((GRID, lanes), F32),
         ],
-        scratch_shapes=[
-            pltpu.VMEM((body, lanes), F32),
-            pltpu.VMEM((half * pieces * up_to(reach_y, 8), lanes), F32),
+        scratch_shapes=stacking_scratch(pieces // table.shape[0], reach_x, reach_y)
+        + [
             pltpu.VMEM((7, GRID, lanes), F32),
             pltpu.VMEM((head, lanes), F32),
         ],
         compiler_params=params(),
         cost_estimate=cost(2 * half * 256 * 256 * 128, 4 * half * GRID * lanes * 2),
         name="forward",
-    )(*parts, table, modes)
+    )(*parts, early, table, modes, *awaited)
+
+
+def far_kernel(reach_x, *refs):
+    own_ref, *far_refs = refs[:-2]
+    modes_ref, out_ref = refs[-2:]
+    span = reach_x - 4
+    x_index = lax.axis_index("wide")
+    low = low_lanes(GRID)
+    log_decay = modes_ref[1]
+
+    def moment(ref):
+        first = from_short(ref[:16, :])
+        return from_short(ref[16:, :]) * unit(first[0:1], first[1:2])
+
+    total = moment(own_ref) * jnp.exp((GRID - reach_x) * log_decay)
+    for flip, ref in enumerate(far_refs, 2):
+        behind = x_index - (x_index ^ flip)
+        powers = []
+        for distance in (-behind, behind):
+            ahead = span * distance - reach_x
+            powers.append(jnp.where(distance >= 2, ahead, ahead + GRID).astype(F32))
+        total = total + moment(ref) * jnp.exp(jnp.where(low, *powers) * log_decay)
+    out_ref[...] = total
+
+
+def far_moments(own, fars, modes, reach_x):
+    return pl.pallas_call(
+        functools.partial(far_kernel, reach_x),
+        in_specs=[whole_vmem()] * (2 + len(fars)),
+        out_specs=whole_vmem(),
+        out_shape=jax.ShapeDtypeStruct((GRID, 2 * HALF), F32),
+        compiler_params=params(),
+        cost_estimate=cost(FAR_FLOPS, 4 * GRID * 2 * HALF * (3 + len(fars))),
+        name="far_moments",
+    )(own, *fars, modes)
 
 
 def send_fields(outs, flips, reach_y, field_high, field_low, high_ref, low_ref, ready, head):
@@ -629,20 +718,16 @@
         send_piece(out, head, ready[piece])
 
 
-def inverse_kernel(reach_x, reach_y, flips, fars, *refs):
-    spectrum, from_even, from_odd, own_ref, inner_ref = refs[:5]
-    far_refs = refs[5 : 5 + fars]
-    high_ref, low_ref, modes_ref = refs[5 + fars : 8 + fars]
-    outs = refs[8 + fars : 8 + fars + len(flips)]
-    field_high, field_low, ready, head = refs[8 + fars + len(flips) :]
+def inverse_kernel(reach_x, reach_y, flips, *refs):
+    spectrum, from_even, from_odd, far_ref, inner_ref = refs[:5]
+    high_ref, low_ref, modes_ref = refs[5:8]
+    outs = refs[8 : 8 + len(flips)]
+    field_high, field_low, ready, head = refs[8 + len(flips) :]
     half = reach_x // 2
     span = reach_x - 4
     chunk = 32
     head_rows = from_even.shape[0] - 3 * GRID
-    x_count = lax.axis_size("wide")
-    x_index = lax.axis_index("wide")
-
-    on_left = (x_index & 1) == 1
+    on_left = (lax.axis_index("wide") & 1) == 1
     both_heads = from_short(from_even[:16, :]), from_short(from_odd[:16, :])
     both_units = [
         [unit(first[2 * slab : 2 * slab + 1], first[2 * slab + 1 : 2 * slab + 2]) for slab in range(3)]
@@ -651,21 +736,6 @@
 
     def sided(even, odd):
         return jnp.where(on_left, even, odd), jnp.where(on_left, odd, even)
-
-    far_units = []
-    own_head = from_short(own_ref[:16, :])
-    own_unit = unit(own_head[0:1], own_head[1:2])
-    for far in far_refs:
-        first = from_short(far[:16, :])
-        far_units.append(unit(first[0:1], first[1:2]))
-    powers = []
-    for flip in range(2, x_count):
-        behind = x_index - (x_index ^ flip)
-        both = []
-        for distance in (-behind, behind):
-            ahead = span * distance - reach_x
-            both.append(jnp.where(distance >= 2, ahead, ahead + GRID).astype(F32))
-        powers.append(both)
 
     def body(index, carry):
         first = pl.multiple_of(index * chunk, chunk)
@@ -685,10 +755,6 @@
             at = pl.ds(pl.multiple_of(head_rows + which * GRID + index * chunk, chunk), chunk)
             even = from_short(from_even[at, :]) * both_units[0][which]
             return sided(even, from_short(from_odd[at, :]) * both_units[1][which])
-
-        def moment(ref, scale):
-            at = pl.ds(pl.multiple_of(16 + index * chunk, chunk), chunk)
-            return from_short(ref[at, :]) * scale
 
         head_layers, tail_layers = zip(slab(0), slab(1))
         left_moments, right_moments = slab(2)
@@ -706,13 +772,10 @@
         for i in range(4):
             place = half - 4 + i
             layers[place] = layers[place] + jnp.where(low, zero, from_tail[i])
-        total = moment(own_ref, own_unit) * jnp.exp((GRID - reach_x) * log_decay)
+        total = far_ref[rows, :]
         one = jnp.ones_like(decay)
         total = total + left_moments * jnp.where(low, beside, one)
         total = total + right_moments * jnp.where(low, one, beside)
-        for far in range(fars):
-            power = jnp.where(low, powers[far][0], powers[far][1])
-            total = total + moment(far_refs[far], far_units[far]) * jnp.exp(power * log_decay)
         shared = jnp.where(low, head_sum, tail_sum)
         entering = (swap(total) + around * shared) * ring
         leaving = swap(across_half * entering + across_cut * shared + inner_ref[rows, :])
@@ -734,17 +797,15 @@
     send_fields(outs, flips, reach_y, field_high, field_low, high_ref, low_ref, ready, head)
 
 
-def inverse(
-    spectrum, from_even, from_odd, own, inner, fars, table, modes, reach_x, reach_y, flips
-):
+def inverse(spectrum, from_even, from_odd, far, inner, table, modes, reach_x, reach_y, flips):
     half = reach_x // 2
     lanes = 2 * HALF
     body = up_to(half * reach_y, 16)
     shapes = [jax.ShapeDtypeStruct((16 + body, lanes), jnp.int16)] * len(flips)
     shapes += [jax.ShapeDtypeStruct((half, GRID, lanes), BF16)] * 2
     return pl.pallas_call(
-        functools.partial(inverse_kernel, reach_x, reach_y, flips, len(fars)),
-        in_specs=[whole_vmem()] * (8 + len(fars)),
+        functools.partial(inverse_kernel, reach_x, reach_y, flips),
+        in_specs=[whole_vmem()] * 8,
         out_specs=[whole_vmem()] * len(shapes),
         out_shape=shapes,
         scratch_shapes=[
@@ -754,7 +815,7 @@
         compiler_params=params(),
         cost_estimate=cost(2 * half * 256 * 256 * 128, 4 * half * GRID * lanes * 2),
         name="inverse",
-    )(spectrum, from_even, from_odd, own, inner, *fars, *table, modes)
+    )(spectrum, from_even, from_odd, far, inner, *table, modes)
 
 
 def inverse_rest_kernel(reach_y, flips, field_high, field_low, high_ref, low_ref, *refs):
@@ -798,20 +859,43 @@
     return values[0]
 
 
-def sample_kernel(last, reach_x, reach_y, pieces, place_ref, *refs):
-    parts = refs[:pieces]
-    high_ref, low_ref, line_ref, own_ref, vector_ref, near_ref, out_ref, flat, field, sums = refs[
-        pieces:
-    ]
+def z_lines(parts, flips, high_ref, low_ref):
     mine = y_position()
-    half_rows = reach_x * reach_y // 2
     opened = []
     for part in parts:
         first = from_short(part[:16, :])
         opened.append(from_short(part[16:, :]) * unit(first[0:1], first[1:2]))
     values = split(jnp.concatenate(opened, axis=1))
-    pick = lambda ref: jnp.concatenate([ref[mine ^ piece] for piece in range(pieces)], axis=0)
-    both = dot_three(values, (pick(high_ref), pick(low_ref)))
+    pick = lambda ref: jnp.concatenate([ref[mine ^ flip] for flip in flips], axis=0)
+    return dot_three(values, (pick(high_ref), pick(low_ref)))
+
+
+def sample_early_kernel(*refs):
+    *parts, high_ref, low_ref, out_ref = refs
+    out_ref[...] = z_lines(parts, range(len(parts)), high_ref, low_ref)
+
+
+def sample_early(parts, table):
+    rows = parts[0].shape[0] - 16
+    return pl.pallas_call(
+        sample_early_kernel,
+        in_specs=[whole_vmem()] * (len(parts) + 2),
+        out_specs=whole_vmem(),
+        out_shape=jax.ShapeDtypeStruct((rows, 2 * REGION), F32),
+        compiler_params=params(),
+        cost_estimate=cost(2 * rows * 256 * 256 * 3, 4 * rows * 512),
+        name="sample_early",
+    )(*parts, *table)
+
+
+def sample_kernel(last, reach_x, reach_y, flips, place_ref, *refs):
+    parts = refs[: len(flips)]
+    early_ref, high_ref, low_ref, line_ref, own_ref, vector_ref, near_ref, out_ref = refs[
+        len(flips) : len(flips) + 8
+    ]
+    flat, field, sums = refs[len(flips) + 8 :]
+    half_rows = reach_x * reach_y // 2
+    both = early_ref[...] + z_lines(parts, flips, high_ref, low_ref)
     flat[:half_rows, :] = both[:half_rows, :REGION]
     flat[half_rows:, :] = both[:half_rows, REGION:]
     for x in range(reach_x):
@@ -855,14 +939,13 @@
             out_ref[row, :] = image
 
 
-def sample(last, places, parts, table, lines, flag, vector, near, reach_x, reach_y):
+def sample(last, places, parts, flips, early, table, lines, flag, vector, near, reach_x, reach_y):
     count = places.shape[1]
     blocks = count // BLOCK
-    pieces = len(parts)
     shape = (2, count) if last else (blocks, BLOCK)
     return pl.pallas_call(
-        functools.partial(sample_kernel, last, reach_x, reach_y, pieces),
-        in_specs=[in_smem()] + [whole_vmem()] * (pieces + 6),
+        functools.partial(sample_kernel, last, reach_x, reach_y, flips),
+        in_specs=[in_smem()] + [whole_vmem()] * (len(parts) + 7),
         out_specs=whole_vmem(),
         out_shape=jax.ShapeDtypeStruct(shape, F32),
         scratch_shapes=[
@@ -876,6 +959,7 @@
     )(
         places,
         *parts,
+        early,
         *table,
         lines,
         flag.reshape(blocks, BLOCK),
@@ -947,6 +1031,7 @@
     x_count = lax.axis_size("wide")
     y_count = lax.axis_size(Y_AXES)
     y_index = lax.axis_index(Y_AXES)
+    pair = lax.axis_size("pair")
     span_x = REGION // x_count
     span_y = REGION // y_count
     reach_x = span_x + 4
@@ -954,7 +1039,7 @@
     count = density.shape[0]
     blocks = count // BLOCK
 
-    z_forward, z_inverse, y_forward, y_inverse, modes = tables(y_count, span_y)
+    z_forward, z_inverse, y_forward, y_inverse, modes = tables(y_count, pair, span_y)
     modes = lax.dynamic_index_in_dim(jnp.asarray(modes), y_index, 0, keepdims=False)
 
     neighbour = near_source // blocks
@@ -981,15 +1066,16 @@
             for flip, part in zip(flips, parts)
         ]
 
-    def convolve_and_sample(last, vector, sent, both, places, sample_lines):
+    def convolve_and_sample(last, vector, sent, both, places, sample_lines, awaited):
         arrived = flipped(sent, moving)
         arrived = list(spread_rest(vector, both, z_forward, local)) + arrived
+        early = forward_early(arrived[:pair], y_forward, reach_x, reach_y)
         spectrum, even_message, odd_message, own, peers, inner = forward(
-            arrived, y_forward, modes, reach_x, reach_y, blocks
+            arrived, early, y_forward, modes, reach_x, reach_y, blocks, awaited
         )
+        fars = [lax.ppermute(own, "wide", pairs) for pairs in far_swaps]
         from_even = lax.ppermute(even_message, "wide", even_swap)
         from_odd = lax.ppermute(odd_message, "wide", odd_swap)
-        fars = [lax.ppermute(own, "wide", pairs) for pairs in far_swaps]
         near_part = near_field(
             sources, targets, from_even, from_odd, peers, near_tiles, blocks, out_rows
         )
@@ -997,9 +1083,8 @@
             spectrum,
             from_even,
             from_odd,
-            own,
+            far_moments(own, fars, modes, reach_x),
             inner,
-            fars,
             y_inverse,
             modes,
             reach_x,
@@ -1008,10 +1093,12 @@
         )
         arrived = flipped(sent, moving)
         arrived = list(inverse_rest((high, low), y_inverse, reach_y, local)) + arrived
-        return sample(
+        image = sample(
             last,
             places,
-            arrived,
+            arrived[pair:],
+            list(range(pair, y_count)),
+            sample_early(arrived[:pair], z_inverse),
             z_inverse,
             sample_lines,
             surface_flag,
@@ -1020,20 +1107,25 @@
             reach_x,
             reach_y,
         )
+        return image, near_part
 
     raw = (stencil_base, surface_flag, sample_weights, dipole_weights)
     *sent, high, low, source_coeff, sample_coeff, places = spread(
         density, z_forward, None, raw, reach_x, reach_y, moving
     )
-    sample_lines = place_lines(places, sample_coeff)
-    source_lines = place_lines(places, source_coeff)
-    first_image = convolve_and_sample(
-        False, density, sent, (high, low), places, sample_lines
-    ).reshape(-1)
+    sample_lines = place_lines(places, sample_coeff, [])
+    first_image, near_part = convolve_and_sample(
+        False, density, sent, (high, low), places, sample_lines, [sample_lines]
+    )
+    first_image = first_image.reshape(-1)
+    source_lines = place_lines(places, source_coeff, [near_part])
     *sent, high, low = spread(
         first_image, z_forward, (places, source_lines), None, reach_x, reach_y, moving
     )
-    return convolve_and_sample(True, first_image, sent, (high, low), places, sample_lines)
+    both_images, _ = convolve_and_sample(
+        True, first_image, sent, (high, low), places, sample_lines, []
+    )
+    return both_images
 
 
 def solution(mesh):

time: 107 us -> 97 us (0.907)
  local copies, waits for them, and re-layouts: 9.5 us -> 2.9 us
  starting transfers between devices: 29.2 us -> 23.8 us
  Pallas kernels: 37.5 us -> 40 us
    ppermute x12, waiting for transfers between devices: 23.9 us -> 14.5 us  [flipped(): lax.ppermute(part, Y_AXES, [(i, i ^ flip) for i in range(y_count)])]
    unnamed x44 -> x36, local copies, waits for them, and re-layouts: 8.42 us -> 1.82 us
    ppermute x2, waiting for transfers between devices: 0.01 us -> 5.96 us  [convolve_and_sample(): from_even = lax.ppermute(even_message, 'wide', even_swap)]
    ppermute x4, starting transfers between devices: 17.1 us -> 12.3 us  [convolve_and_sample(): fars = [lax.ppermute(own, 'wide', pairs) for pairs in far_swaps]]
    ppermute x4, waiting for transfers between devices: 6.04 us -> 9.03 us  [convolve_and_sample(): fars = [lax.ppermute(own, 'wide', pairs) for pairs in far_swaps]]
    pallas_call x2, Pallas kernels: 8.53 us -> 10.3 us  [spread(): pl.pallas_call(functools.partial(start_kernel if placed is None else spre...]
    pallas_call x6 -> x12, Pallas kernels: 19.3 us -> 21 us  [the longest x2 6.48 us: sample(): pl.pallas_call(functools.partial(sample_kernel, last, reach_x, reach_y, f...]
    ppermute x2, starting transfers between devices: 1.78 us -> 0.14 us  [convolve_and_sample(): from_even = lax.ppermute(even_message, 'wide', even_swap)]
  transfers between devices with their start and end apart: 20 -> 20, of which waited for: 9 -> 11; matrix products, arithmetic and copies ran while one was open for 1% -> 1% of each run, Pallas kernels for 10% -> 14%
where the time goes in v6:
time: 97 us; the launch traced here: 96.6 us
  Pallas kernels  40 us (41%)
  waiting for transfers between devices  29.5 us (30%)
  starting transfers between devices  23.8 us (25%)
  local copies, waits for them, and re-layouts  2.9 us (3%)
    ppermute x12, waiting for transfers between devices, flipped(): lax.ppermute(part, Y_AXES, [(i, i ^ flip) for i in range(y_count)])  14.5 us
    ppermute x4, starting transfers between devices, convolve_and_sample(): fars = [lax.ppermute(own, 'wide', pairs) for pairs in far_swaps]  12.3 us
    pallas_call x2, Pallas kernels, spread(): pl.pallas_call(functools.partial(start_kernel if placed is None else spre...  10.3 us
    ppermute x12, starting transfers between devices, flipped(): lax.ppermute(part, Y_AXES, [(i, i ^ flip) for i in range(y_count)])  9.66 us
    ppermute x4, waiting for transfers between devices, convolve_and_sample(): fars = [lax.ppermute(own, 'wide', pairs) for pairs in far_swaps]  9.03 us
    pallas_call x2, Pallas kernels, sample(): pl.pallas_call(functools.partial(sample_kernel, last, reach_x, reach_y, f...  6.48 us
    pallas_call x2, Pallas kernels, inverse(): pl.pallas_call(functools.partial(inverse_kernel, reach_x, reach_y, flips)...  6.21 us
    ppermute x2, waiting for transfers between devices, convolve_and_sample(): from_even = lax.ppermute(even_message, 'wide', even_swap)  5.96 us
  transfers between devices with their start and end apart: 20, of which 11 were waited for; matrix products, arithmetic and copies ran while one was open for 1% of the time, Pallas kernels for 14%

profile of v6, /device:TPU:0, one launch (start us, length us, event | category | flops | bytes accessed | tf_op | source)
XLA Modules:
  0.0 96.6 jit_solution(517764790365204773)
XLA Ops:
  0.0 7.2 %start.1 = (s16[672,128]{1,0:T(8,128)(2,1)}, s16[672,128]{1,0:T(8,128)(2,1)}, s16[672,128]{1,0:T(8,128)(2,1)}, bf16[656,256]{1,0:T(8,128)(2,1)}, bf16[656,256]{1...) custom-call(f32[512]{0:T(512)} %refs_0_.1, f32[4,128]{1,0:T(4,128)} %bitcast.7, ...), custom_call_target="tpu_custom_call" | custom-call | flops 169869312 | bytes 4194304 | tf_op jit(solution)/shard_map/start/pallas_call | solution.py:397
  7.2 0.0 copy-start.2
  7.3 0.0 copy-start.3
  7.3 0.5 collective-permute-start
  7.8 2.6 %collective-permute-start.1 = (s16[672,128]{1,0:T(8,128)(2,1)}, s16[672,128]{1,0:T(8,128)(2,1)S(1)}, u32[]{:S(2)}, u32[]{:S(2)}) collective-permute-start(s16[672,128]{1,0:T(8,128)(2,1)} %get-tuple-element.44), channel_id=1, source_target_pairs={{0,2},{1,3},{2,0},{3,1},{4,6},{5,7},{6,4},{7,5},{8,10},{9,11},{10,... | collective-permute-start | bytes 516104 | tf_op jit(solution)/shard_map/ppermute | solution.py:1065
  10.4 0.1 collective-permute-start.2
  10.4 0.9 copy-done.11
  11.3 0.7 copy-done.12
  12.0 2.9 %place_lines.2.refs_7_.refs_5_ = f32[8192,128]{1,0:T(8,128)S(1)} custom-call(s32[2,512]{1,0:T(2,128)S(1)} %copy-done.12, f32[256,128]{1,0:T(8,128)S(1)} %copy-done.11), custom_call_target="tpu_custom_call" | custom-call | flops 1048576 | bytes 4194304 | tf_op jit(solution)/shard_map/place_lines/pallas_call | solution.py:458
  15.0 0.5 spread_rest.2.refs_0_
  15.5 1.1 %dynamic-slice_bitcast_fusion.refs_6_.refs_3_.refs_7_ = f32[4,256,128]{2,1,0:T(8,128)S(1)} fusion(f32[4,4,256,128]{3,2,1,0:T(8,128)} %constant.73.clone, s32[]{:T(128)S(6)} %select_n.30), kind=kLoop, calls=%fused_computation | loop fusion | bytes 1048580 | tf_op jit(solution)/shard_map/jit(dynamic_index_in_dim)/squeeze | solution.py:1043
  16.7 0.6 forward_early.2.refs_4_
  17.3 1.7 %collective-permute-done.2.refs_3_ = s16[672,128]{1,0:T(8,128)(2,1)S(1)} collective-permute-done((s16[672,128]{1,0:T(8,128)(2,1)}, s16[672,128]{1,0:T(8,128)(2,1)S(1)}, u32[]{:S(2)}, u32[]{:S(2)}) %collective-permute-start.2) | collective-permute-done | bytes 172064 | tf_op jit(solution)/shard_map/ppermute | solution.py:1065
  19.0 1.9 %forward.2 = (f32[18,256,128]{2,1,0:T(8,128)S(1)}, s16[816,128]{1,0:T(8,128)(2,1)S(1)}, s16[816,128]{1,0:T(8,128)(2,1)S(1)}, s16[272,128]{1,0:T(8,128)(2,1)S(1)}...) custom-call(s16[672,128]{1,0:T(8,128)(2,1)S(1)} %spread_rest.2.refs_0_, ...), custom_call_target="tpu_custom_call" | custom-call | flops 301989888 | bytes 4718592 | tf_op jit(solution)/shard_map/forward/pallas_call | solution.py:639
  20.9 2.7 %collective-permute-start.5 = (s16[272,128]{1,0:T(8,128)(2,1)S(1)}, s16[272,128]{1,0:T(8,128)(2,1)S(1)}, u32[]{:S(2)}, u32[]{:S(2)}) collective-permute-start(s16[272,128]{1,0:T(8,128)(2,1)S(1)} %get-tuple-element.50.refs_0_), channel_id=1, source_target_pairs={{0,8},{4,12},{8,0},{12,4},{1,9},{5,13},{9,1},{13,5},{2,10},{6,14},... | collective-permute-start | bytes 208904 | tf_op jit(solution)/shard_map/ppermute | solution.py:1076
  23.6 3.2 %collective-permute-start.6 = (s16[272,128]{1,0:T(8,128)(2,1)S(1)}, s16[272,128]{1,0:T(8,128)(2,1)S(1)}, u32[]{:S(2)}, u32[]{:S(2)}) collective-permute-start(s16[272,128]{1,0:T(8,128)(2,1)S(1)} %get-tuple-element.50.refs_0_), channel_id=1, source_target_pairs={{0,12},{12,0},{1,13},{13,1},{2,14},{14,2},{3,15},{15,3},{16,28},{2... | collective-permute-start | bytes 208904 | tf_op jit(solution)/shard_map/ppermute | solution.py:1076
  26.8 0.1 collective-permute-start.3
  26.9 0.0 copy-start.6
  26.9 0.0 copy-start.7
  26.9 0.8 collective-permute-start.4
  27.8 4.6 %collective-permute-done.6.refs_2_ = s16[272,128]{1,0:T(8,128)(2,1)S(1)} collective-permute-done((s16[272,128]{1,0:T(8,128)(2,1)S(1)}, s16[272,128]{1,0:T(8,128)(2,1)S(1)}, u32[]{:S(2)}, u32[]{:S(2)}) %collective-permute-start.6) | collective-permute-done | bytes 69664 | tf_op jit(solution)/shard_map/ppermute | solution.py:1076
  32.3 0.1 far_moments.2.refs_3_
  32.4 0.0 copy-start.16
  32.4 0.0 copy-start.17
  32.5 2.7 %collective-permute-done.3.refs_1_.refs_0_ = s16[816,128]{1,0:T(8,128)(2,1)S(1)} collective-permute-done((s16[816,128]{1,0:T(8,128)(2,1)S(1)}, s16[816,128]{1,0:T(8,128)(2,1)S(1)}, u32[]{:S(2)}, u32[]{:S(2)}) %collective-permute-start.3) | collective-permute-done | bytes 208928 | tf_op jit(solution)/shard_map/ppermute | solution.py:1077
  35.2 3.1 %inverse.2 = (s16[672,128]{1,0:T(8,128)(2,1)S(1)}, s16[672,128]{1,0:T(8,128)(2,1)S(1)}, s16[672,128]{1,0:T(8,128)(2,1)S(1)}, bf16[18,256,128]{2,1,0:T(8,128)(2,1)S(1)}, bf16[18,256,128]{2,1,0:T(8,128)(2,1)S(1)}) custom-call(f32[18,256,128]{2,1,0:T(8,128)S(1)} %get-tuple-element.47.refs_0_, s16[816,128]{1,0:T(8,128)(2,1)S(1)} %collective-permute-done.3.refs_1_.refs_0_, ...), custom_call_target="tpu_custom_call" | custom-call | flops 301989888 | bytes 4718592 | tf_op jit(solution)/shard_map/inverse/pallas_call | solution.py:806
  38.3 1.6 %collective-permute-start.7 = (s16[672,128]{1,0:T(8,128)(2,1)S(1)}, s16[672,128]{1,0:T(8,128)(2,1)S(1)}, u32[]{:S(2)}, u32[]{:S(2)}) collective-permute-start(s16[672,128]{1,0:T(8,128)(2,1)S(1)} %get-tuple-element.52), channel_id=1, source_target_pairs={{0,2},{1,3},{2,0},{3,1},{4,6},{5,7},{6,4},{7,5},{8,10},{9,11},{10,... | collective-permute-start | bytes 516104 | tf_op jit(solution)/shard_map/ppermute | solution.py:1065
  39.9 0.6 collective-permute-start.9
  40.6 1.1 %near_field.2.refs_8_.refs_0_ = f32[8,128]{1,0:T(8,128)S(1)} custom-call(s32[24]{0:T(128)S(1)} %get-tuple-element.76.place_ref, s32[24]{0:T(128)S(1)} %get-tuple-element.75.target_ref, s16[816,128]{1,0:T(8,128)(2,1)S(1)} %collective-permute-done.3.refs_1_.refs_0_, s16[816,128]{1,0:T(8,128)(2,1)S(1)} %collective-permute-done.4.refs_2_.refs_1_, ...), custom_call_target="tpu_custom_call" | custom-call | flops 12582912 | bytes 786432 | tf_op jit(solution)/shard_map/near_field/pallas_call | solution.py:1001
  41.6 0.0 copy-done.13
  41.6 2.9 %place_lines.3.refs_5_ = f32[8192,128]{1,0:T(8,128)S(1)} custom-call(s32[2,512]{1,0:T(2,128)S(1)} %copy-done.13, f32[256,128]{1,0:T(8,128)S(1)} %copy-done.10, f32[8,128]{1,0:T(8,128)S(1)} %near_field.2.refs_8_.refs_0_), custom_call_target="tpu_custom_call" | custom-call | flops 1048576 | bytes 4194304 | tf_op jit(solution)/shard_map/place_lines/pallas_call | solution.py:458
  44.6 0.0 copy-start.1
  44.6 0.8 inverse_rest.2.refs_0_
  45.5 0.1 copy-done
  45.5 0.1 copy-done.1
  45.6 0.4 sample_early.2.refs_2_
  46.1 0.6 collective-permute-done.8.refs_1_
  46.7 2.9 %sample.2.refs_2_.rounded_ref.refs_7_ = f32[4,128]{1,0:T(4,128)S(1)} custom-call(s32[2,512]{1,0:T(2,128)S(1)} %copy-done.13, s16[672,128]{1,0:T(8,128)(2,1)S(1)} %collective-permute-done.7.refs_0_, s16[672,128]{1,0:T(8,128)(2,1)S(1)} %collective-permute-done.8.refs_1_, f32[656,256]{1,0:T(8,128)S(1)} %sample_early.2.refs_2_, ...), custom_call_target="tpu_custom_call" | custom-call | flops 169869312 | bytes 4194304 | tf_op jit(solution)/shard_map/sample/pallas_call | solution.py:946
  49.7 3.1 %spread.1 = (s16[672,128]{1,0:T(8,128)(2,1)S(1)}, s16[672,128]{1,0:T(8,128)(2,1)S(1)}, s16[672,128]{1,0:T(8,128)(2,1)S(1)}, bf16[656,256]{1,0:T(8,128)(2,1)S(1)}, bf16[656,256]{1,0:T(8,128)(2,1)S(1)}) custom-call(f32[512]{0:T(512)S(1)} %bitcast.6, s32[2,512]{1,0:T(2,128)S(1)} %copy-done.13, f32[4,128]{1,0:T(4,128)S(1)} %sample.2.refs_2_.rounded_ref.refs_7_, ...), custom_call_target="tpu_custom_call" | custom-call | flops 169869312 | bytes 4194304 | tf_op jit(solution)/shard_map/spread/pallas_call | solution.py:397
  52.8 0.8 collective-permute-start.10
  53.6 1.5 %collective-permute-start.11 = (s16[672,128]{1,0:T(8,128)(2,1)S(1)}, s16[672,128]{1,0:T(8,128)(2,1)S(1)}, u32[]{:S(2)}, u32[]{:S(2)}) collective-permute-start(s16[672,128]{1,0:T(8,128)(2,1)S(1)} %get-tuple-element.62), channel_id=1, source_target_pairs={{0,2},{1,3},{2,0},{3,1},{4,6},{5,7},{6,4},{7,5},{8,10},{9,11},{10,... | collective-permute-start | bytes 516104 | tf_op jit(solution)/shard_map/ppermute | solution.py:1065
  55.1 0.5 spread_rest.3.refs_0_
  55.7 0.6 forward_early.3.refs_4_
  56.3 4.5 %collective-permute-done.11.refs_2_ = s16[672,128]{1,0:T(8,128)(2,1)S(1)} collective-permute-done((s16[672,128]{1,0:T(8,128)(2,1)S(1)}, s16[672,128]{1,0:T(8,128)(2,1)S(1)}, u32[]{:S(2)}, u32[]{:S(2)}) %collective-permute-start.11) | collective-permute-done | bytes 172064 | tf_op jit(solution)/shard_map/ppermute | solution.py:1065
  60.8 1.9 %collective-permute-done.12.refs_3_ = s16[672,128]{1,0:T(8,128)(2,1)S(1)} collective-permute-done((s16[672,128]{1,0:T(8,128)(2,1)S(1)}, s16[672,128]{1,0:T(8,128)(2,1)S(1)}, u32[]{:S(2)}, u32[]{:S(2)}) %collective-permute-start.12) | collective-permute-done | bytes 172064 | tf_op jit(solution)/shard_map/ppermute | solution.py:1065
  62.8 1.9 %forward.3 = (f32[18,256,128]{2,1,0:T(8,128)S(1)}, s16[816,128]{1,0:T(8,128)(2,1)S(1)}, s16[816,128]{1,0:T(8,128)(2,1)S(1)}, s16[272,128]{1,0:T(8,128)(2,1)S(1)}...) custom-call(s16[672,128]{1,0:T(8,128)(2,1)S(1)} %spread_rest.3.refs_0_, ...), custom_call_target="tpu_custom_call" | custom-call | flops 301989888 | bytes 4718592 | tf_op jit(solution)/shard_map/forward/pallas_call | solution.py:639
  64.7 3.1 %collective-permute-start.15 = (s16[272,128]{1,0:T(8,128)(2,1)S(1)}, s16[272,128]{1,0:T(8,128)(2,1)S(1)}, u32[]{:S(2)}, u32[]{:S(2)}) collective-permute-start(s16[272,128]{1,0:T(8,128)(2,1)S(1)} %get-tuple-element.67.refs_0_), channel_id=1, source_target_pairs={{0,8},{4,12},{8,0},{12,4},{1,9},{5,13},{9,1},{13,5},{2,10},{6,14},... | collective-permute-start | bytes 208904 | tf_op jit(solution)/shard_map/ppermute | solution.py:1076
  67.8 3.2 %collective-permute-start.16 = (s16[272,128]{1,0:T(8,128)(2,1)S(1)}, s16[272,128]{1,0:T(8,128)(2,1)S(1)}, u32[]{:S(2)}, u32[]{:S(2)}) collective-permute-start(s16[272,128]{1,0:T(8,128)(2,1)S(1)} %get-tuple-element.67.refs_0_), channel_id=1, source_target_pairs={{0,12},{12,0},{1,13},{13,1},{2,14},{14,2},{3,15},{15,3},{16,28},{2... | collective-permute-start | bytes 208904 | tf_op jit(solution)/shard_map/ppermute | solution.py:1076
  71.1 0.1 collective-permute-start.13
  71.1 0.9 collective-permute-start.14
  72.0 0.3 collective-permute-done.15.refs_1_
  72.3 4.2 %collective-permute-done.16.refs_2_ = s16[272,128]{1,0:T(8,128)(2,1)S(1)} collective-permute-done((s16[272,128]{1,0:T(8,128)(2,1)S(1)}, s16[272,128]{1,0:T(8,128)(2,1)S(1)}, u32[]{:S(2)}, u32[]{:S(2)}) %collective-permute-start.16) | collective-permute-done | bytes 69664 | tf_op jit(solution)/shard_map/ppermute | solution.py:1076
  76.5 0.1 far_moments.3.refs_3_
  76.6 3.2 %collective-permute-done.13.refs_1_.refs_0_ = s16[816,128]{1,0:T(8,128)(2,1)S(1)} collective-permute-done((s16[816,128]{1,0:T(8,128)(2,1)S(1)}, s16[816,128]{1,0:T(8,128)(2,1)S(1)}, u32[]{:S(2)}, u32[]{:S(2)}) %collective-permute-start.13) | collective-permute-done | bytes 208928 | tf_op jit(solution)/shard_map/ppermute | solution.py:1077
  79.8 3.1 %inverse.3 = (s16[672,128]{1,0:T(8,128)(2,1)S(1)}, s16[672,128]{1,0:T(8,128)(2,1)S(1)}, s16[672,128]{1,0:T(8,128)(2,1)S(1)}, bf16[18,256,128]{2,1,0:T(8,128)(2,1)S(1)}, bf16[18,256,128]{2,1,0:T(8,128)(2,1)S(1)}) custom-call(f32[18,256,128]{2,1,0:T(8,128)S(1)} %get-tuple-element.64.refs_0_, s16[816,128]{1,0:T(8,128)(2,1)S(1)} %collective-permute-done.13.refs_1_.refs_0_, ...), custom_call_target="tpu_custom_call" | custom-call | flops 301989888 | bytes 4718592 | tf_op jit(solution)/shard_map/inverse/pallas_call | solution.py:806
  83.0 0.1 collective-permute-start.19
  83.0 1.5 %collective-permute-start.17 = (s16[672,128]{1,0:T(8,128)(2,1)S(1)}, s16[672,128]{1,0:T(8,128)(2,1)S(1)}, u32[]{:S(2)}, u32[]{:S(2)}) collective-permute-start(s16[672,128]{1,0:T(8,128)(2,1)S(1)} %get-tuple-element.69), channel_id=1, source_target_pairs={{0,2},{1,3},{2,0},{3,1},{4,6},{5,7},{6,4},{7,5},{8,10},{9,11},{10,... | collective-permute-start | bytes 516104 | tf_op jit(solution)/shard_map/ppermute | solution.py:1065
  84.5 0.4 collective-permute-start.18
  84.9 1.1 %near_field.3.refs_8_ = f32[8,128]{1,0:T(8,128)S(1)} custom-call(s32[24]{0:T(128)S(1)} %get-tuple-element.76.place_ref, s32[24]{0:T(128)S(1)} %get-tuple-element.75.target_ref, s16[816,128]{1,0:T(8,128)(2,1)S(1)} %collective-permute-done.13.refs_1_.refs_0_, s16[816,128]{1,0:T(8,128)(2,1)S(1)} %collective-permute-done.14.refs_2_.refs_1_, ...), custom_call_target="tpu_custom_call" | custom-call | flops 12582912 | bytes 786432 | tf_op jit(solution)/shard_map/near_field/pallas_call | solution.py:1001
  86.0 0.9 inverse_rest.3.refs_0_
  86.8 0.4 sample_early.3.refs_2_
  87.3 3.0 %collective-permute-done.17.refs_0_ = s16[672,128]{1,0:T(8,128)(2,1)S(1)} collective-permute-done((s16[672,128]{1,0:T(8,128)(2,1)S(1)}, s16[672,128]{1,0:T(8,128)(2,1)S(1)}, u32[]{:S(2)}, u32[]{:S(2)}) %collective-permute-start.17) | collective-permute-done | bytes 172064 | tf_op jit(solution)/shard_map/ppermute | solution.py:1065
  90.3 2.8 %collective-permute-done.18.refs_1_ = s16[672,128]{1,0:T(8,128)(2,1)S(1)} collective-permute-done((s16[672,128]{1,0:T(8,128)(2,1)S(1)}, s16[672,128]{1,0:T(8,128)(2,1)S(1)}, u32[]{:S(2)}, u32[]{:S(2)}) %collective-permute-start.18) | collective-permute-done | bytes 172064 | tf_op jit(solution)/shard_map/ppermute | solution.py:1065
  93.1 3.6 %sample.3 = f32[2,512]{1,0:T(2,128)} custom-call(s32[2,512]{1,0:T(2,128)S(1)} %copy-done.13, s16[672,128]{1,0:T(8,128)(2,1)S(1)} %collective-permute-done.17.refs_0_, s16[672,128]{1,0:T(8,128)(2,1)S(1)} %collective-permute-done.18.refs_1_, f32[656,256]{1,0:T(8,128)S(1)} %sample_early.3.refs_2_, bf16[4,128,256]{2,1,0:T(8,128)(2,1)S(1)} %copy-done, ...), custom_call_target="tpu_custom_call" | custom-call | flops 169869312 | bytes 4194304 | tf_op jit(solution)/shard_map/sample/pallas_call | solution.py:946
  (36 shorter events, 0.1 us)
Async XLA Ops:
  0.0 15.0 %copy-start.14 = (f32[512]{0:T(512)S(1)}, f32[512]{0:T(512)}, u32[]{:S(2)}) copy-start(f32[512]{0:T(512)} %refs_0_.1) | copy-start | bytes 6148
  7.2 7.7 %copy-start.2 = (bf16[4,256,128]{2,1,0:T(8,128)(2,1)S(1)}, bf16[4,256,128]{2,1,0:T(8,128)(2,1)}, u32[]{:S(2)}) copy-start(bf16[4,256,128]{2,1,0:T(8,128)(2,1)} %constant.74.clone.refs_2_.high_ref.refs_3_) | copy-start | bytes 786436
  7.3 7.7 %copy-start.3 = (bf16[4,256,128]{2,1,0:T(8,128)(2,1)S(1)}, bf16[4,256,128]{2,1,0:T(8,128)(2,1)}, u32[]{:S(2)}) copy-start(bf16[4,256,128]{2,1,0:T(8,128)(2,1)} %constant.75.clone.refs_3_.low_ref.refs_4_) | copy-start | bytes 786436
  7.3 7.7 %copy-start.8 = (bf16[656,256]{1,0:T(8,128)(2,1)S(1)}, bf16[656,256]{1,0:T(8,128)(2,1)}, u32[]{:S(2)}) copy-start(bf16[656,256]{1,0:T(8,128)(2,1)} %get-tuple-element.41.wide_high) | copy-start | bytes 1007620
  7.3 7.7 %copy-start.9 = (bf16[656,256]{1,0:T(8,128)(2,1)S(1)}, bf16[656,256]{1,0:T(8,128)(2,1)}, u32[]{:S(2)}) copy-start(bf16[656,256]{1,0:T(8,128)(2,1)} %get-tuple-element.42.wide_low) | copy-start | bytes 1007620
  7.3 9.4 %collective-permute-start = (s16[672,128]{1,0:T(8,128)(2,1)}, s16[672,128]{1,0:T(8,128)(2,1)S(1)}, u32[]{:S(2)}, u32[]{:S(2)}) collective-permute-start(s16[672,128]{1,0:T(8,128)(2,1)} %get-tuple-element.43), channel_id=1, source_target_pairs={{0,1},{1,0},{2,3},{3,2},{4,5},{5,4},{6,7},{7,6},{8,9},{9,8},{10,11... | collective-permute-start | bytes 516104 | tf_op jit(solution)/shard_map/ppermute | solution.py:1065
  7.8 9.5 %collective-permute-start.1 = (s16[672,128]{1,0:T(8,128)(2,1)}, s16[672,128]{1,0:T(8,128)(2,1)S(1)}, u32[]{:S(2)}, u32[]{:S(2)}) collective-permute-start(s16[672,128]{1,0:T(8,128)(2,1)} %get-tuple-element.44), channel_id=1, source_target_pairs={{0,2},{1,3},{2,0},{3,1},{4,6},{5,7},{6,4},{7,5},{8,10},{9,11},{10,... | collective-permute-start | bytes 516104 | tf_op jit(solution)/shard_map/ppermute | solution.py:1065
  10.4 8.6 %collective-permute-start.2 = (s16[672,128]{1,0:T(8,128)(2,1)}, s16[672,128]{1,0:T(8,128)(2,1)S(1)}, u32[]{:S(2)}, u32[]{:S(2)}) collective-permute-start(s16[672,128]{1,0:T(8,128)(2,1)} %get-tuple-element.45), channel_id=1, source_target_pairs={{0,3},{1,2},{2,1},{3,0},{4,7},{5,6},{6,5},{7,4},{8,11},{9,10},{10,... | collective-permute-start | bytes 516104 | tf_op jit(solution)/shard_map/ppermute | solution.py:1065
  10.4 0.9 copy-start.11
  11.3 0.7 copy-start.12
  12.0 4.6 %copy-start.4 = (bf16[2,256,240]{2,1,0:T(8,128)(2,1)S(1)}, bf16[2,256,240]{2,1,0:T(8,128)(2,1)}, u32[]{:S(2)}) copy-start(bf16[2,256,240]{2,1,0:T(8,128)(2,1)} %constant.76.clone.refs_2_.refs_5_) | copy-start | bytes 737284
  20.9 6.9 %collective-permute-start.5 = (s16[272,128]{1,0:T(8,128)(2,1)S(1)}, s16[272,128]{1,0:T(8,128)(2,1)S(1)}, u32[]{:S(2)}, u32[]{:S(2)}) collective-permute-start(s16[272,128]{1,0:T(8,128)(2,1)S(1)} %get-tuple-element.50.refs_0_), channel_id=1, source_target_pairs={{0,8},{4,12},{8,0},{12,4},{1,9},{5,13},{9,1},{13,5},{2,10},{6,14},... | collective-permute-start | bytes 208904 | tf_op jit(solution)/shard_map/ppermute | solution.py:1076
  23.6 8.7 %collective-permute-start.6 = (s16[272,128]{1,0:T(8,128)(2,1)S(1)}, s16[272,128]{1,0:T(8,128)(2,1)S(1)}, u32[]{:S(2)}, u32[]{:S(2)}) collective-permute-start(s16[272,128]{1,0:T(8,128)(2,1)S(1)} %get-tuple-element.50.refs_0_), channel_id=1, source_target_pairs={{0,12},{12,0},{1,13},{13,1},{2,14},{14,2},{3,15},{15,3},{16,28},{2... | collective-permute-start | bytes 208904 | tf_op jit(solution)/shard_map/ppermute | solution.py:1076
  26.8 8.3 %collective-permute-start.3 = (s16[816,128]{1,0:T(8,128)(2,1)S(1)}, s16[816,128]{1,0:T(8,128)(2,1)S(1)}, u32[]{:S(2)}, u32[]{:S(2)}) collective-permute-start(s16[816,128]{1,0:T(8,128)(2,1)S(1)} %get-tuple-element.48), channel_id=1, source_target_pairs={{0,4},{8,12},{4,0},{12,8},{1,5},{9,13},{5,1},{13,9},{2,6},{10,14},... | collective-permute-start | bytes 626696 | tf_op jit(solution)/shard_map/ppermute | solution.py:1077
  26.9 8.3 %copy-start.6 = (bf16[4,48,256]{2,1,0:T(8,128)(2,1)S(1)}, bf16[4,48,256]{2,1,0:T(8,128)(2,1)}, u32[]{:S(2)}) copy-start(bf16[4,48,256]{2,1,0:T(8,128)(2,1)} %constant.77.clone.refs_5_.high_ref) | copy-start | bytes 294916
  26.9 8.3 %copy-start.7 = (bf16[4,48,256]{2,1,0:T(8,128)(2,1)S(1)}, bf16[4,48,256]{2,1,0:T(8,128)(2,1)}, u32[]{:S(2)}) copy-start(bf16[4,48,256]{2,1,0:T(8,128)(2,1)} %constant.78.clone.refs_6_.low_ref) | copy-start | bytes 294916
  26.9 8.2 %collective-permute-start.4 = (s16[816,128]{1,0:T(8,128)(2,1)S(1)}, s16[816,128]{1,0:T(8,128)(2,1)S(1)}, u32[]{:S(2)}, u32[]{:S(2)}) collective-permute-start(s16[816,128]{1,0:T(8,128)(2,1)S(1)} %get-tuple-element.49), channel_id=1, source_target_pairs={{4,8},{8,4},{5,9},{9,5},{6,10},{10,6},{7,11},{11,7},{20,24},{24,20... | collective-permute-start | bytes 626696 | tf_op jit(solution)/shard_map/ppermute | solution.py:1078
  32.4 8.1 %copy-start.16 = (s32[24]{0:T(128)S(1)}, s32[24]{0:T(128)}, u32[]{:S(2)}) copy-start(s32[24]{0:T(128)} %param.21) | copy-start | bytes 292
  32.4 8.1 %copy-start.17 = (s32[24]{0:T(128)S(1)}, s32[24]{0:T(128)}, u32[]{:S(2)}) copy-start(s32[24]{0:T(128)} %param.22) | copy-start | bytes 292
  32.4 8.1 %copy-start.5 = (bf16[24,128,128]{2,1,0:T(8,128)(2,1)S(1)}, bf16[24,128,128]{2,1,0:T(8,128)(2,1)}, u32[]{:S(2)}) copy-start(bf16[24,128,128]{2,1,0:T(8,128)(2,1)} %refs_3_.9) | copy-start | bytes 2359300
  35.2 6.4 %copy-start.10 = (f32[256,128]{1,0:T(8,128)S(1)}, f32[256,128]{1,0:T(8,128)}, u32[]{:S(2)}) copy-start(f32[256,128]{1,0:T(8,128)} %get-tuple-element.58.coeff_ref) | copy-start | bytes 393220
  35.2 6.4 %copy-start.13 = (s32[2,512]{1,0:T(2,128)S(1)}, s32[2,512]{1,0:T(2,128)}, u32[]{:S(2)}) copy-start(s32[2,512]{1,0:T(2,128)} %get-tuple-element.40.place_ref.refs_1_) | copy-start | bytes 12292
  38.3 7.8 %collective-permute-start.7 = (s16[672,128]{1,0:T(8,128)(2,1)S(1)}, s16[672,128]{1,0:T(8,128)(2,1)S(1)}, u32[]{:S(2)}, u32[]{:S(2)}) collective-permute-start(s16[672,128]{1,0:T(8,128)(2,1)S(1)} %get-tuple-element.52), channel_id=1, source_target_pairs={{0,2},{1,3},{2,0},{3,1},{4,6},{5,7},{6,4},{7,5},{8,10},{9,11},{10,... | collective-permute-start | bytes 516104 | tf_op jit(solution)/shard_map/ppermute | solution.py:1065
  39.9 6.8 %collective-permute-start.8 = (s16[672,128]{1,0:T(8,128)(2,1)S(1)}, s16[672,128]{1,0:T(8,128)(2,1)S(1)}, u32[]{:S(2)}, u32[]{:S(2)}) collective-permute-start(s16[672,128]{1,0:T(8,128)(2,1)S(1)} %get-tuple-element.53), channel_id=1, source_target_pairs={{0,3},{1,2},{2,1},{3,0},{4,7},{5,6},{6,5},{7,4},{8,11},{9,10},{10,... | collective-permute-start | bytes 516104 | tf_op jit(solution)/shard_map/ppermute | solution.py:1065
  39.9 5.6 %collective-permute-start.9 = (s16[672,128]{1,0:T(8,128)(2,1)S(1)}, s16[672,128]{1,0:T(8,128)(2,1)S(1)}, u32[]{:S(2)}, u32[]{:S(2)}) collective-permute-start(s16[672,128]{1,0:T(8,128)(2,1)S(1)} %get-tuple-element.56), channel_id=1, source_target_pairs={{0,1},{1,0},{2,3},{3,2},{4,5},{5,4},{6,7},{7,6},{8,9},{9,8},{10,11... | collective-permute-start | bytes 516104 | tf_op jit(solution)/shard_map/ppermute | solution.py:1065
  44.6 1.0 copy-start
  44.6 1.0 %copy-start.1 = (bf16[4,128,256]{2,1,0:T(8,128)(2,1)S(1)}, bf16[4,128,256]{2,1,0:T(8,128)(2,1)}, u32[]{:S(2)}) copy-start(bf16[4,128,256]{2,1,0:T(8,128)(2,1)} %constant.80.clone.refs_3_.refs_4_) | copy-start | bytes 786436
  44.6 2.1 %copy-start.15 = (s32[512]{0:T(512)S(1)}, s32[512]{0:T(512)}, u32[]{:S(2)}) copy-start(s32[512]{0:T(512)} %param.17) | copy-start | bytes 6148
  52.8 2.9 %collective-permute-start.10 = (s16[672,128]{1,0:T(8,128)(2,1)S(1)}, s16[672,128]{1,0:T(8,128)(2,1)S(1)}, u32[]{:S(2)}, u32[]{:S(2)}) collective-permute-start(s16[672,128]{1,0:T(8,128)(2,1)S(1)} %get-tuple-element.61), channel_id=1, source_target_pairs={{0,1},{1,0},{2,3},{3,2},{4,5},{5,4},{6,7},{7,6},{8,9},{9,8},{10,11... | collective-permute-start | bytes 516104 | tf_op jit(solution)/shard_map/ppermute | solution.py:1065
  53.6 7.2 %collective-permute-start.11 = (s16[672,128]{1,0:T(8,128)(2,1)S(1)}, s16[672,128]{1,0:T(8,128)(2,1)S(1)}, u32[]{:S(2)}, u32[]{:S(2)}) collective-permute-start(s16[672,128]{1,0:T(8,128)(2,1)S(1)} %get-tuple-element.62), channel_id=1, source_target_pairs={{0,2},{1,3},{2,0},{3,1},{4,6},{5,7},{6,4},{7,5},{8,10},{9,11},{10,... | collective-permute-start | bytes 516104 | tf_op jit(solution)/shard_map/ppermute | solution.py:1065
  55.1 7.6 %collective-permute-start.12 = (s16[672,128]{1,0:T(8,128)(2,1)S(1)}, s16[672,128]{1,0:T(8,128)(2,1)S(1)}, u32[]{:S(2)}, u32[]{:S(2)}) collective-permute-start(s16[672,128]{1,0:T(8,128)(2,1)S(1)} %get-tuple-element.63), channel_id=1, source_target_pairs={{0,3},{1,2},{2,1},{3,0},{4,7},{5,6},{6,5},{7,4},{8,11},{9,10},{10,... | collective-permute-start | bytes 516104 | tf_op jit(solution)/shard_map/ppermute | solution.py:1065
  64.7 7.6 %collective-permute-start.15 = (s16[272,128]{1,0:T(8,128)(2,1)S(1)}, s16[272,128]{1,0:T(8,128)(2,1)S(1)}, u32[]{:S(2)}, u32[]{:S(2)}) collective-permute-start(s16[272,128]{1,0:T(8,128)(2,1)S(1)} %get-tuple-element.67.refs_0_), channel_id=1, source_target_pairs={{0,8},{4,12},{8,0},{12,4},{1,9},{5,13},{9,1},{13,5},{2,10},{6,14},... | collective-permute-start | bytes 208904 | tf_op jit(solution)/shard_map/ppermute | solution.py:1076
  67.8 8.7 %collective-permute-start.16 = (s16[272,128]{1,0:T(8,128)(2,1)S(1)}, s16[272,128]{1,0:T(8,128)(2,1)S(1)}, u32[]{:S(2)}, u32[]{:S(2)}) collective-permute-start(s16[272,128]{1,0:T(8,128)(2,1)S(1)} %get-tuple-element.67.refs_0_), channel_id=1, source_target_pairs={{0,12},{12,0},{1,13},{13,1},{2,14},{14,2},{3,15},{15,3},{16,28},{2... | collective-permute-start | bytes 208904 | tf_op jit(solution)/shard_map/ppermute | solution.py:1076
  71.1 8.8 %collective-permute-start.13 = (s16[816,128]{1,0:T(8,128)(2,1)S(1)}, s16[816,128]{1,0:T(8,128)(2,1)S(1)}, u32[]{:S(2)}, u32[]{:S(2)}) collective-permute-start(s16[816,128]{1,0:T(8,128)(2,1)S(1)} %get-tuple-element.65), channel_id=1, source_target_pairs={{0,4},{8,12},{4,0},{12,8},{1,5},{9,13},{5,1},{13,9},{2,6},{10,14},... | collective-permute-start | bytes 626696 | tf_op jit(solution)/shard_map/ppermute | solution.py:1077
  71.1 8.7 %collective-permute-start.14 = (s16[816,128]{1,0:T(8,128)(2,1)S(1)}, s16[816,128]{1,0:T(8,128)(2,1)S(1)}, u32[]{:S(2)}, u32[]{:S(2)}) collective-permute-start(s16[816,128]{1,0:T(8,128)(2,1)S(1)} %get-tuple-element.66), channel_id=1, source_target_pairs={{4,8},{8,4},{5,9},{9,5},{6,10},{10,6},{7,11},{11,7},{20,24},{24,20... | collective-permute-start | bytes 626696 | tf_op jit(solution)/shard_map/ppermute | solution.py:1078
  83.0 3.9 %collective-permute-start.19 = (s16[672,128]{1,0:T(8,128)(2,1)S(1)}, s16[672,128]{1,0:T(8,128)(2,1)S(1)}, u32[]{:S(2)}, u32[]{:S(2)}) collective-permute-start(s16[672,128]{1,0:T(8,128)(2,1)S(1)} %get-tuple-element.73), channel_id=1, source_target_pairs={{0,1},{1,0},{2,3},{3,2},{4,5},{5,4},{6,7},{7,6},{8,9},{9,8},{10,11... | collective-permute-start | bytes 516104 | tf_op jit(solution)/shard_map/ppermute | solution.py:1065
  83.0 7.2 %collective-permute-start.17 = (s16[672,128]{1,0:T(8,128)(2,1)S(1)}, s16[672,128]{1,0:T(8,128)(2,1)S(1)}, u32[]{:S(2)}, u32[]{:S(2)}) collective-permute-start(s16[672,128]{1,0:T(8,128)(2,1)S(1)} %get-tuple-element.69), channel_id=1, source_target_pairs={{0,2},{1,3},{2,0},{3,1},{4,6},{5,7},{6,4},{7,5},{8,10},{9,11},{10,... | collective-permute-start | bytes 516104 | tf_op jit(solution)/shard_map/ppermute | solution.py:1065
  84.5 8.5 %collective-permute-start.18 = (s16[672,128]{1,0:T(8,128)(2,1)S(1)}, s16[672,128]{1,0:T(8,128)(2,1)S(1)}, u32[]{:S(2)}, u32[]{:S(2)}) collective-permute-start(s16[672,128]{1,0:T(8,128)(2,1)S(1)} %get-tuple-element.70), channel_id=1, source_target_pairs={{0,3},{1,2},{2,1},{3,0},{4,7},{5,6},{6,5},{7,4},{8,11},{9,10},{10,... | collective-permute-start | bytes 516104 | tf_op jit(solution)/shard_map/ppermute | solution.py:1065

commit v7 on v6

--- a/solution.py
+++ b/solution.py
@@ -22,7 +22,6 @@
 BF16 = jnp.bfloat16
 VMEM_LIMIT = 24 * 1024 * 1024
 START_LIMIT = 60 * 1024 * 1024
-FAR_FLOPS = 8 * 10**9
 GROUP = 32
 CHAINS = 2
 
@@ -588,8 +587,8 @@
             jnp.where(low, layers[0], swap(layers[1])),
             jnp.where(low, layers[2], swap(layers[3])),
             jnp.where(low, cut_left + across_cut * swapped_left, own),
-            own,
         ]
+        own_out[rows, :] = own
         for slab, values in enumerate(made):
             slabs[slab, rows, :] = values
         return tuple(
@@ -598,7 +597,7 @@
         )
 
     zero = jnp.zeros((8, 2 * HALF), F32)
-    largest = lax.fori_loop(0, GRID // chunk, body, (zero,) * 7)
+    largest = lax.fori_loop(0, GRID // chunk, body, (zero,) * 6)
     scales = [fit_scale(jnp.max(value, axis=0, keepdims=True)) for value in largest]
     head_rows = head.shape[0]
 
@@ -622,12 +621,6 @@
     def _():
         send(even_out, 3)
         send(odd_out, 0)
-
-    exponent, fraction = scales[6]
-    head[0:1, :] = exponent
-    head[1:2, :] = fraction
-    own_out[:16, :] = to_short(head[:16, :])
-    own_out[16:, :] = quantize(slabs[6], exponent, fraction)
 
 
 def forward(parts, early, table, modes, reach_x, reach_y, blocks, awaited):
@@ -646,13 +639,13 @@
             jax.ShapeDtypeStruct((half, GRID, lanes), F32),
             short(head + 3 * GRID),
             short(head + 3 * GRID),
-            short(16 + GRID),
+            jax.ShapeDtypeStruct((GRID, lanes), F32),
             jax.ShapeDtypeStruct((pieces * blocks, BLOCK), F32),
             jax.ShapeDtypeStruct((GRID, lanes), F32),
         ],
         scratch_shapes=stacking_scratch(pieces // table.shape[0], reach_x, reach_y)
         + [
-            pltpu.VMEM((7, GRID, lanes), F32),
+            pltpu.VMEM((6, GRID, lanes), F32),
             pltpu.VMEM((head, lanes), F32),
         ],
         compiler_params=params(),
@@ -661,39 +654,55 @@
     )(*parts, early, table, modes, *awaited)
 
 
-def far_kernel(reach_x, *refs):
-    own_ref, *far_refs = refs[:-2]
-    modes_ref, out_ref = refs[-2:]
+def opened_slabs(ref, count, head_rows):
+    first = from_short(ref[:16, :])
+    for slab in range(count):
+        scale = unit(first[2 * slab : 2 * slab + 1], first[2 * slab + 1 : 2 * slab + 2])
+        at = head_rows + slab * GRID
+        yield from_short(ref[at : at + GRID, :]) * scale
+
+
+def pair_kernel(reach_x, flips, own_ref, even_ref, modes_ref, *refs):
+    outs, head = refs[:-1], refs[-1]
     span = reach_x - 4
-    x_index = lax.axis_index("wide")
+    here = lax.axis_index("wide")
     low = low_lanes(GRID)
-    log_decay = modes_ref[1]
-
-    def moment(ref):
-        first = from_short(ref[:16, :])
-        return from_short(ref[16:, :]) * unit(first[0:1], first[1:2])
-
-    total = moment(own_ref) * jnp.exp((GRID - reach_x) * log_decay)
-    for flip, ref in enumerate(far_refs, 2):
-        behind = x_index - (x_index ^ flip)
+    decay, log_decay = modes_ref[0], modes_ref[1]
+    own = own_ref[...]
+    one, two, cut = opened_slabs(even_ref, 3, even_ref.shape[0] - 3 * GRID)
+    left = ((decay * cut + swap(one)) * decay + one) * decay + swap(two)
+    left = jnp.where(low, cut, left * decay + two)
+    right = ((decay * cut + swap(two)) * decay + two) * decay + swap(one)
+    right = jnp.where(low, right * decay + one, cut)
+    partner = jnp.where((here & 1) == 1, left, right)
+
+    def weight(distances):
         powers = []
-        for distance in (-behind, behind):
+        for distance in distances:
             ahead = span * distance - reach_x
             powers.append(jnp.where(distance >= 2, ahead, ahead + GRID).astype(F32))
-        total = total + moment(ref) * jnp.exp(jnp.where(low, *powers) * log_decay)
-    out_ref[...] = total
-
-
-def far_moments(own, fars, modes, reach_x):
+        return jnp.exp(jnp.where(low, *powers) * log_decay)
+
+    head[...] = jnp.zeros_like(head)
+    for flip, out in zip(flips, outs):
+        behind = (here ^ flip) - here
+        message = own * weight((-behind, behind))
+        behind = (here ^ flip) - (here ^ 1)
+        beside = jnp.where(jnp.abs(behind) == 1, 0.0, 1.0)
+        send_piece(out, head, message + partner * (weight((-behind, behind)) * beside))
+
+
+def pair_messages(own, from_even, modes, reach_x, flips):
     return pl.pallas_call(
-        functools.partial(far_kernel, reach_x),
-        in_specs=[whole_vmem()] * (2 + len(fars)),
-        out_specs=whole_vmem(),
-        out_shape=jax.ShapeDtypeStruct((GRID, 2 * HALF), F32),
+        functools.partial(pair_kernel, reach_x, flips),
+        in_specs=[whole_vmem()] * 3,
+        out_specs=[whole_vmem()] * len(flips),
+        out_shape=[jax.ShapeDtypeStruct((16 + GRID, 2 * HALF), jnp.int16)] * len(flips),
+        scratch_shapes=[pltpu.VMEM((16, 2 * HALF), F32)],
         compiler_params=params(),
-        cost_estimate=cost(FAR_FLOPS, 4 * GRID * 2 * HALF * (3 + len(fars))),
-        name="far_moments",
-    )(own, *fars, modes)
+        cost_estimate=cost(16 * GRID * 2 * HALF, 4 * GRID * 2 * HALF * (6 + len(flips))),
+        name="pair_messages",
+    )(own, from_even, modes)
 
 
 def send_fields(outs, flips, reach_y, field_high, field_low, high_ref, low_ref, ready, head):
@@ -718,11 +727,12 @@
         send_piece(out, head, ready[piece])
 
 
-def inverse_kernel(reach_x, reach_y, flips, *refs):
-    spectrum, from_even, from_odd, far_ref, inner_ref = refs[:5]
-    high_ref, low_ref, modes_ref = refs[5:8]
-    outs = refs[8 : 8 + len(flips)]
-    field_high, field_low, ready, head = refs[8 + len(flips) :]
+def inverse_kernel(reach_x, reach_y, flips, fars, *refs):
+    spectrum, from_even, from_odd, own_ref, inner_ref, *far_refs = refs[: 5 + fars]
+    refs = refs[5 + fars :]
+    high_ref, low_ref, modes_ref = refs[:3]
+    outs = refs[3 : 3 + len(flips)]
+    field_high, field_low, ready, head = refs[3 + len(flips) :]
     half = reach_x // 2
     span = reach_x - 4
     chunk = 32
@@ -736,6 +746,11 @@
 
     def sided(even, odd):
         return jnp.where(on_left, even, odd), jnp.where(on_left, odd, even)
+
+    far_units = []
+    for ref in far_refs:
+        first = from_short(ref[:16, :])
+        far_units.append(unit(first[0:1], first[1:2]))
 
     def body(index, carry):
         first = pl.multiple_of(index * chunk, chunk)
@@ -772,7 +787,10 @@
         for i in range(4):
             place = half - 4 + i
             layers[place] = layers[place] + jnp.where(low, zero, from_tail[i])
-        total = far_ref[rows, :]
+        total = own_ref[rows, :] * jnp.exp((GRID - reach_x) * log_decay)
+        at = pl.ds(pl.multiple_of(16 + index * chunk, 16), chunk)
+        for ref, scale in zip(far_refs, far_units):
+            total = total + from_short(ref[at, :]) * scale
         one = jnp.ones_like(decay)
         total = total + left_moments * jnp.where(low, beside, one)
         total = total + right_moments * jnp.where(low, one, beside)
@@ -797,15 +815,17 @@
     send_fields(outs, flips, reach_y, field_high, field_low, high_ref, low_ref, ready, head)
 
 
-def inverse(spectrum, from_even, from_odd, far, inner, table, modes, reach_x, reach_y, flips):
+def inverse(
+    spectrum, from_even, from_odd, own, inner, fars, table, modes, reach_x, reach_y, flips
+):
     half = reach_x // 2
     lanes = 2 * HALF
     body = up_to(half * reach_y, 16)
     shapes = [jax.ShapeDtypeStruct((16 + body, lanes), jnp.int16)] * len(flips)
     shapes += [jax.ShapeDtypeStruct((half, GRID, lanes), BF16)] * 2
     return pl.pallas_call(
-        functools.partial(inverse_kernel, reach_x, reach_y, flips),
-        in_specs=[whole_vmem()] * 8,
+        functools.partial(inverse_kernel, reach_x, reach_y, flips, len(fars)),
+        in_specs=[whole_vmem()] * (8 + len(fars)),
         out_specs=[whole_vmem()] * len(shapes),
         out_shape=shapes,
         scratch_shapes=[
@@ -815,7 +835,7 @@
         compiler_params=params(),
         cost_estimate=cost(2 * half * 256 * 256 * 128, 4 * half * GRID * lanes * 2),
         name="inverse",
-    )(spectrum, from_even, from_odd, far, inner, *table, modes)
+    )(spectrum, from_even, from_odd, own, inner, *fars, *table, modes)
 
 
 def inverse_rest_kernel(reach_y, flips, field_high, field_low, high_ref, low_ref, *refs):
@@ -1053,10 +1073,7 @@
     swaps = lambda pairs: [(i, j) for i, j in pairs] + [(j, i) for i, j in pairs]
     even_swap = swaps([(i, i + 1) for i in range(0, x_count - 1, 2)])
     odd_swap = swaps([(i, i + 1) for i in range(1, x_count - 1, 2)])
-    far_swaps = [
-        swaps([(i, i ^ flip) for i in range(x_count) if (i ^ flip) > i + 1])
-        for flip in range(2, x_count)
-    ]
+    far_flips = list(range(2, x_count, 2))
 
     local, moving = [0], list(range(1, y_count))
 
@@ -1073,9 +1090,14 @@
         spectrum, even_message, odd_message, own, peers, inner = forward(
             arrived, early, y_forward, modes, reach_x, reach_y, blocks, awaited
         )
-        fars = [lax.ppermute(own, "wide", pairs) for pairs in far_swaps]
         from_even = lax.ppermute(even_message, "wide", even_swap)
         from_odd = lax.ppermute(odd_message, "wide", odd_swap)
+        fars = [
+            lax.ppermute(message, "wide", [(i, i ^ flip) for i in range(x_count)])
+            for flip, message in zip(
+                far_flips, pair_messages(own, from_even, modes, reach_x, far_flips)
+            )
+        ]
         near_part = near_field(
             sources, targets, from_even, from_odd, peers, near_tiles, blocks, out_rows
         )
@@ -1083,8 +1105,9 @@
             spectrum,
             from_even,
             from_odd,
-            far_moments(own, fars, modes, reach_x),
+            own,
             inner,
+            fars,
             y_inverse,
             modes,
             reach_x,

time: 97 us -> 96 us (0.990)
  starting transfers between devices: 23.8 us -> 17.5 us
  waiting for transfers between devices: 29.5 us -> 34.9 us
    ppermute x4 -> x2, starting transfers between devices: 12.3 us -> 4.43 us  [convolve_and_sample(): lax.ppermute(message, 'wide', [(i, i ^ flip) for i in range(x_count)])]
    ppermute x2, waiting for transfers between devices: 5.96 us -> 11.7 us  [convolve_and_sample(): from_even = lax.ppermute(even_message, 'wide', even_swap)]
    ppermute x2, starting transfers between devices: 0.14 us -> 1.93 us  [convolve_and_sample(): from_even = lax.ppermute(even_message, 'wide', even_swap)]
    ppermute x4 -> x2, waiting for transfers between devices: 9.03 us -> 8.88 us  [convolve_and_sample(): lax.ppermute(message, 'wide', [(i, i ^ flip) for i in range(x_count)])]
  transfers between devices with their start and end apart: 20 -> 18, of which waited for: 11 -> 10; matrix products, arithmetic and copies ran while one was open for 1% -> 1% of each run, Pallas kernels for 14% -> 14%
where the time goes in v7:
time: 96 us; the launch traced here: 95.7 us
  Pallas kernels  40 us (42%)
  waiting for transfers between devices  34.9 us (36%)
  starting transfers between devices  17.5 us (18%)
  local copies, waits for them, and re-layouts  2.9 us (3%)
    ppermute x12, waiting for transfers between devices, flipped(): lax.ppermute(part, Y_AXES, [(i, i ^ flip) for i in range(y_count)])  14.4 us
    ppermute x2, waiting for transfers between devices, convolve_and_sample(): from_even = lax.ppermute(even_message, 'wide', even_swap)  11.7 us
    pallas_call x2, Pallas kernels, spread(): pl.pallas_call(functools.partial(start_kernel if placed is None else spre...  10.3 us
    ppermute x12, starting transfers between devices, flipped(): lax.ppermute(part, Y_AXES, [(i, i ^ flip) for i in range(y_count)])  9.6 us
    ppermute x2, waiting for transfers between devices, convolve_and_sample(): lax.ppermute(message, 'wide', [(i, i ^ flip) for i in range(x_count)])  8.88 us
    pallas_call x2, Pallas kernels, sample(): pl.pallas_call(functools.partial(sample_kernel, last, reach_x, reach_y, f...  6.49 us
    pallas_call x2, Pallas kernels, inverse(): pl.pallas_call(functools.partial(inverse_kernel, reach_x, reach_y, flips,...  6.17 us
    pallas_call x2, Pallas kernels, place_lines(): pl.pallas_call(lines_kernel, in_specs=[in_smem(), whole_vmem()] + [anywhe...  5.88 us
  transfers between devices with their start and end apart: 18, of which 10 were waited for; matrix products, arithmetic and copies ran while one was open for 1% of the time, Pallas kernels for 14%

profile of v7, /device:TPU:0, one launch (start us, length us, event | category | flops | bytes accessed | tf_op | source)
XLA Modules:
  0.0 95.7 jit_solution(8235287631402357782)
XLA Ops:
  0.0 7.2 %start.1 = (s16[672,128]{1,0:T(8,128)(2,1)}, s16[672,128]{1,0:T(8,128)(2,1)}, s16[672,128]{1,0:T(8,128)(2,1)}, bf16[656,256]{1,0:T(8,128)(2,1)}, bf16[656,256]{1...) custom-call(f32[512]{0:T(512)} %refs_0_.1, f32[4,128]{1,0:T(4,128)} %bitcast.7, ...), custom_call_target="tpu_custom_call" | custom-call | flops 169869312 | bytes 4194304 | tf_op jit(solution)/shard_map/start/pallas_call | solution.py:396
  7.2 0.0 copy-start.2
  7.3 0.0 copy-start.3
  7.3 0.5 collective-permute-start
  7.8 2.6 %collective-permute-start.1 = (s16[672,128]{1,0:T(8,128)(2,1)}, s16[672,128]{1,0:T(8,128)(2,1)S(1)}, u32[]{:S(2)}, u32[]{:S(2)}) collective-permute-start(s16[672,128]{1,0:T(8,128)(2,1)} %get-tuple-element.44), channel_id=1, source_target_pairs={{0,2},{1,3},{2,0},{3,1},{4,6},{5,7},{6,4},{7,5},{8,10},{9,11},{10,... | collective-permute-start | bytes 516104 | tf_op jit(solution)/shard_map/ppermute | solution.py:1082
  10.4 0.1 collective-permute-start.2
  10.4 0.9 copy-done.11
  11.3 0.7 copy-done.12
  12.0 2.9 %place_lines.2.refs_7_.refs_5_ = f32[8192,128]{1,0:T(8,128)S(1)} custom-call(s32[2,512]{1,0:T(2,128)S(1)} %copy-done.12, f32[256,128]{1,0:T(8,128)S(1)} %copy-done.11), custom_call_target="tpu_custom_call" | custom-call | flops 1048576 | bytes 4194304 | tf_op jit(solution)/shard_map/place_lines/pallas_call | solution.py:457
  15.0 0.5 spread_rest.2.refs_0_
  15.5 1.1 %dynamic-slice_bitcast_fusion.refs_6_.modes_ref.refs_8_ = f32[4,256,128]{2,1,0:T(8,128)S(1)} fusion(f32[4,4,256,128]{3,2,1,0:T(8,128)} %constant.73.clone, s32[]{:T(128)S(6)} %select_n.30), kind=kLoop, calls=%fused_computation | loop fusion | bytes 1048580 | tf_op jit(solution)/shard_map/jit(dynamic_index_in_dim)/squeeze | solution.py:1063
  16.6 0.0 collective-permute-done.refs_1_
  16.7 0.6 forward_early.2.refs_4_
  17.3 0.0 copy-start.6
  17.3 0.0 copy-start.7
  17.3 1.6 %collective-permute-done.2.refs_3_ = s16[672,128]{1,0:T(8,128)(2,1)S(1)} collective-permute-done((s16[672,128]{1,0:T(8,128)(2,1)}, s16[672,128]{1,0:T(8,128)(2,1)S(1)}, u32[]{:S(2)}, u32[]{:S(2)}) %collective-permute-start.2) | collective-permute-done | bytes 172064 | tf_op jit(solution)/shard_map/ppermute | solution.py:1082
  19.0 1.8 %forward.2 = (f32[18,256,128]{2,1,0:T(8,128)S(1)}, s16[816,128]{1,0:T(8,128)(2,1)S(1)}, s16[816,128]{1,0:T(8,128)(2,1)S(1)}, f32[256,128]{1,0:T(8,128)S(1)}, f32...) custom-call(s16[672,128]{1,0:T(8,128)(2,1)S(1)} %spread_rest.2.refs_0_, s16[672,128]{1,0:T(8,128)(2,1)S(1)} %collective-permute-done.refs_1_, ...), custom_call_target="tpu_custom_call" | custom-call | flops 301989888 | bytes 4718592 | tf_op jit(solution)/shard_map/forward/pallas_call | solution.py:632
  20.8 1.7 %collective-permute-start.3 = (s16[816,128]{1,0:T(8,128)(2,1)S(1)}, s16[816,128]{1,0:T(8,128)(2,1)S(1)}, u32[]{:S(2)}, u32[]{:S(2)}) collective-permute-start(s16[816,128]{1,0:T(8,128)(2,1)S(1)} %get-tuple-element.48), channel_id=1, source_target_pairs={{0,4},{8,12},{4,0},{12,8},{1,5},{9,13},{5,1},{13,9},{2,6},{10,14},... | collective-permute-start | bytes 626696 | tf_op jit(solution)/shard_map/ppermute | solution.py:1093
  22.5 0.7 collective-permute-start.4
  23.2 4.9 %collective-permute-done.3.even_ref.refs_1_.refs_0_ = s16[816,128]{1,0:T(8,128)(2,1)S(1)} collective-permute-done((s16[816,128]{1,0:T(8,128)(2,1)S(1)}, s16[816,128]{1,0:T(8,128)(2,1)S(1)}, u32[]{:S(2)}, u32[]{:S(2)}) %collective-permute-start.3) | collective-permute-done | bytes 208928 | tf_op jit(solution)/shard_map/ppermute | solution.py:1093
  28.1 0.2 pair_messages.2
  28.4 2.8 %collective-permute-start.5 = (s16[272,128]{1,0:T(8,128)(2,1)S(1)}, s16[272,128]{1,0:T(8,128)(2,1)S(1)}, u32[]{:S(2)}, u32[]{:S(2)}) collective-permute-start(s16[272,128]{1,0:T(8,128)(2,1)S(1)} %pair_messages.2), channel_id=1, source_target_pairs={{0,8},{4,12},{8,0},{12,4},{1,9},{5,13},{9,1},{13,5},{2,10},{6,14},... | collective-permute-start | bytes 208904 | tf_op jit(solution)/shard_map/ppermute | solution.py:1096
  31.2 0.0 collective-permute-done.4.refs_2_.refs_1_
  31.2 4.1 %collective-permute-done.5.refs_5_ = s16[272,128]{1,0:T(8,128)(2,1)S(1)} collective-permute-done((s16[272,128]{1,0:T(8,128)(2,1)S(1)}, s16[272,128]{1,0:T(8,128)(2,1)S(1)}, u32[]{:S(2)}, u32[]{:S(2)}) %collective-permute-start.5) | collective-permute-done | bytes 69664 | tf_op jit(solution)/shard_map/ppermute | solution.py:1096
  35.3 3.1 %inverse.2 = (s16[672,128]{1,0:T(8,128)(2,1)S(1)}, s16[672,128]{1,0:T(8,128)(2,1)S(1)}, s16[672,128]{1,0:T(8,128)(2,1)S(1)}, bf16[18,256,128]{2,1,0:T(8,128)(2,1)S(1)}, bf16[18,256,128]{2,1,0:T(8,128)(2,1)S(1)}) custom-call(f32[18,256,128]{2,1,0:T(8,128)S(1)} %get-tuple-element.47.refs_0_, ...), custom_call_target="tpu_custom_call" | custom-call | flops 301989888 | bytes 4718592 | tf_op jit(solution)/shard_map/inverse/pallas_call | solution.py:826
  38.4 1.5 %collective-permute-start.6 = (s16[672,128]{1,0:T(8,128)(2,1)S(1)}, s16[672,128]{1,0:T(8,128)(2,1)S(1)}, u32[]{:S(2)}, u32[]{:S(2)}) collective-permute-start(s16[672,128]{1,0:T(8,128)(2,1)S(1)} %get-tuple-element.52), channel_id=1, source_target_pairs={{0,2},{1,3},{2,0},{3,1},{4,6},{5,7},{6,4},{7,5},{8,10},{9,11},{10,... | collective-permute-start | bytes 516104 | tf_op jit(solution)/shard_map/ppermute | solution.py:1082
  39.9 0.0 collective-permute-start.7
  39.9 0.7 collective-permute-start.8
  40.6 1.1 %near_field.2.refs_8_.refs_0_ = f32[8,128]{1,0:T(8,128)S(1)} custom-call(s32[24]{0:T(128)S(1)} %get-tuple-element.76.place_ref, s32[24]{0:T(128)S(1)} %get-tuple-element.75.target_ref, s16[816,128]{1,0:T(8,128)(2,1)S(1)} %collective-permute-done.3.even_ref.refs_1_.refs_0_, s16[816,128]{1,0:T(8,128)(2,1)S(1)} %collective-permute-done.4.refs_2_.refs_1_, ...), custom_call_target="tpu_custom_call" | custom-call | flops 12582912 | bytes 786432 | tf_op jit(solution)/shard_map/near_field/pallas_call | solution.py:1021
  41.7 0.0 copy-done.13
  41.7 2.9 %place_lines.3.refs_5_ = f32[8192,128]{1,0:T(8,128)S(1)} custom-call(s32[2,512]{1,0:T(2,128)S(1)} %copy-done.13, f32[256,128]{1,0:T(8,128)S(1)} %copy-done.10, f32[8,128]{1,0:T(8,128)S(1)} %near_field.2.refs_8_.refs_0_), custom_call_target="tpu_custom_call" | custom-call | flops 1048576 | bytes 4194304 | tf_op jit(solution)/shard_map/place_lines/pallas_call | solution.py:457
  44.7 0.0 copy-start.1
  44.7 0.0 copy-start.15
  44.7 0.9 inverse_rest.2.refs_0_
  45.6 0.0 copy-done
  45.6 0.1 copy-done.1
  45.7 0.4 sample_early.2.refs_2_
  46.2 0.4 collective-permute-done.7.refs_1_
  46.6 2.9 %sample.2.refs_2_.rounded_ref.refs_7_ = f32[4,128]{1,0:T(4,128)S(1)} custom-call(s32[2,512]{1,0:T(2,128)S(1)} %copy-done.13, s16[672,128]{1,0:T(8,128)(2,1)S(1)} %collective-permute-done.6.refs_0_, s16[672,128]{1,0:T(8,128)(2,1)S(1)} %collective-permute-done.7.refs_1_, f32[656,256]{1,0:T(8,128)S(1)} %sample_early.2.refs_2_, ...), custom_call_target="tpu_custom_call" | custom-call | flops 169869312 | bytes 4194304 | tf_op jit(solution)/shard_map/sample/pallas_call | solution.py:966
  49.5 3.1 %spread.1 = (s16[672,128]{1,0:T(8,128)(2,1)S(1)}, s16[672,128]{1,0:T(8,128)(2,1)S(1)}, s16[672,128]{1,0:T(8,128)(2,1)S(1)}, bf16[656,256]{1,0:T(8,128)(2,1)S(1)}, bf16[656,256]{1,0:T(8,128)(2,1)S(1)}) custom-call(f32[512]{0:T(512)S(1)} %bitcast.6, s32[2,512]{1,0:T(2,128)S(1)} %copy-done.13, f32[4,128]{1,0:T(4,128)S(1)} %sample.2.refs_2_.rounded_ref.refs_7_, ...), custom_call_target="tpu_custom_call" | custom-call | flops 169869312 | bytes 4194304 | tf_op jit(solution)/shard_map/spread/pallas_call | solution.py:396
  52.7 0.8 collective-permute-start.9
  53.5 1.5 %collective-permute-start.10 = (s16[672,128]{1,0:T(8,128)(2,1)S(1)}, s16[672,128]{1,0:T(8,128)(2,1)S(1)}, u32[]{:S(2)}, u32[]{:S(2)}) collective-permute-start(s16[672,128]{1,0:T(8,128)(2,1)S(1)} %get-tuple-element.62), channel_id=1, source_target_pairs={{0,2},{1,3},{2,0},{3,1},{4,6},{5,7},{6,4},{7,5},{8,10},{9,11},{10,... | collective-permute-start | bytes 516104 | tf_op jit(solution)/shard_map/ppermute | solution.py:1082
  55.0 0.5 spread_rest.3.refs_0_
  55.5 0.6 forward_early.3.refs_4_
  56.1 4.6 %collective-permute-done.10.refs_2_ = s16[672,128]{1,0:T(8,128)(2,1)S(1)} collective-permute-done((s16[672,128]{1,0:T(8,128)(2,1)S(1)}, s16[672,128]{1,0:T(8,128)(2,1)S(1)}, u32[]{:S(2)}, u32[]{:S(2)}) %collective-permute-start.10) | collective-permute-done | bytes 172064 | tf_op jit(solution)/shard_map/ppermute | solution.py:1082
  60.7 1.9 %collective-permute-done.11.refs_3_ = s16[672,128]{1,0:T(8,128)(2,1)S(1)} collective-permute-done((s16[672,128]{1,0:T(8,128)(2,1)S(1)}, s16[672,128]{1,0:T(8,128)(2,1)S(1)}, u32[]{:S(2)}, u32[]{:S(2)}) %collective-permute-start.11) | collective-permute-done | bytes 172064 | tf_op jit(solution)/shard_map/ppermute | solution.py:1082
  62.7 1.8 %forward.3 = (f32[18,256,128]{2,1,0:T(8,128)S(1)}, s16[816,128]{1,0:T(8,128)(2,1)S(1)}, s16[816,128]{1,0:T(8,128)(2,1)S(1)}, f32[256,128]{1,0:T(8,128)S(1)}, f32...) custom-call(s16[672,128]{1,0:T(8,128)(2,1)S(1)} %spread_rest.3.refs_0_, s16[672,128]{1,0:T(8,128)(2,1)S(1)} %collective-permute-done.9.refs_1_, ...), custom_call_target="tpu_custom_call" | custom-call | flops 301989888 | bytes 4718592 | tf_op jit(solution)/shard_map/forward/pallas_call | solution.py:632
  64.5 0.2 collective-permute-start.12
  64.7 0.8 collective-permute-start.13
  65.6 6.7 %collective-permute-done.12.even_ref.refs_1_.refs_0_ = s16[816,128]{1,0:T(8,128)(2,1)S(1)} collective-permute-done((s16[816,128]{1,0:T(8,128)(2,1)S(1)}, s16[816,128]{1,0:T(8,128)(2,1)S(1)}, u32[]{:S(2)}, u32[]{:S(2)}) %collective-permute-start.12) | collective-permute-done | bytes 208928 | tf_op jit(solution)/shard_map/ppermute | solution.py:1093
  72.3 0.2 pair_messages.3
  72.6 1.6 %collective-permute-start.14 = (s16[272,128]{1,0:T(8,128)(2,1)S(1)}, s16[272,128]{1,0:T(8,128)(2,1)S(1)}, u32[]{:S(2)}, u32[]{:S(2)}) collective-permute-start(s16[272,128]{1,0:T(8,128)(2,1)S(1)} %pair_messages.3), channel_id=1, source_target_pairs={{0,8},{4,12},{8,0},{12,4},{1,9},{5,13},{9,1},{13,5},{2,10},{6,14},... | collective-permute-start | bytes 208904 | tf_op jit(solution)/shard_map/ppermute | solution.py:1096
  74.2 0.0 collective-permute-done.13.refs_2_.refs_1_
  74.2 4.8 %collective-permute-done.14.refs_5_ = s16[272,128]{1,0:T(8,128)(2,1)S(1)} collective-permute-done((s16[272,128]{1,0:T(8,128)(2,1)S(1)}, s16[272,128]{1,0:T(8,128)(2,1)S(1)}, u32[]{:S(2)}, u32[]{:S(2)}) %collective-permute-start.14) | collective-permute-done | bytes 69664 | tf_op jit(solution)/shard_map/ppermute | solution.py:1096
  79.0 3.1 %inverse.3 = (s16[672,128]{1,0:T(8,128)(2,1)S(1)}, s16[672,128]{1,0:T(8,128)(2,1)S(1)}, s16[672,128]{1,0:T(8,128)(2,1)S(1)}, bf16[18,256,128]{2,1,0:T(8,128)(2,1)S(1)}, bf16[18,256,128]{2,1,0:T(8,128)(2,1)S(1)}) custom-call(f32[18,256,128]{2,1,0:T(8,128)S(1)} %get-tuple-element.64.refs_0_, ...), custom_call_target="tpu_custom_call" | custom-call | flops 301989888 | bytes 4718592 | tf_op jit(solution)/shard_map/inverse/pallas_call | solution.py:826
  82.0 0.1 collective-permute-start.17
  82.1 1.5 %collective-permute-start.15 = (s16[672,128]{1,0:T(8,128)(2,1)S(1)}, s16[672,128]{1,0:T(8,128)(2,1)S(1)}, u32[]{:S(2)}, u32[]{:S(2)}) collective-permute-start(s16[672,128]{1,0:T(8,128)(2,1)S(1)} %get-tuple-element.69), channel_id=1, source_target_pairs={{0,2},{1,3},{2,0},{3,1},{4,6},{5,7},{6,4},{7,5},{8,10},{9,11},{10,... | collective-permute-start | bytes 516104 | tf_op jit(solution)/shard_map/ppermute | solution.py:1082
  83.7 0.3 collective-permute-start.16
  84.0 1.0 %near_field.3.refs_8_ = f32[8,128]{1,0:T(8,128)S(1)} custom-call(s32[24]{0:T(128)S(1)} %get-tuple-element.76.place_ref, s32[24]{0:T(128)S(1)} %get-tuple-element.75.target_ref, s16[816,128]{1,0:T(8,128)(2,1)S(1)} %collective-permute-done.12.even_ref.refs_1_.refs_0_, s16[816,128]{1,0:T(8,128)(2,1)S(1)} %collective-permute-done.13.refs_2_.refs_1_, ...), custom_call_target="tpu_custom_call" | custom-call | flops 12582912 | bytes 786432 | tf_op jit(solution)/shard_map/near_field/pallas_call | solution.py:1021
  85.0 0.9 inverse_rest.3.refs_0_
  85.9 0.4 sample_early.3.refs_2_
  86.4 3.0 %collective-permute-done.15.refs_0_ = s16[672,128]{1,0:T(8,128)(2,1)S(1)} collective-permute-done((s16[672,128]{1,0:T(8,128)(2,1)S(1)}, s16[672,128]{1,0:T(8,128)(2,1)S(1)}, u32[]{:S(2)}, u32[]{:S(2)}) %collective-permute-start.15) | collective-permute-done | bytes 172064 | tf_op jit(solution)/shard_map/ppermute | solution.py:1082
  89.4 2.8 %collective-permute-done.16.refs_1_ = s16[672,128]{1,0:T(8,128)(2,1)S(1)} collective-permute-done((s16[672,128]{1,0:T(8,128)(2,1)S(1)}, s16[672,128]{1,0:T(8,128)(2,1)S(1)}, u32[]{:S(2)}, u32[]{:S(2)}) %collective-permute-start.16) | collective-permute-done | bytes 172064 | tf_op jit(solution)/shard_map/ppermute | solution.py:1082
  92.1 3.6 %sample.3 = f32[2,512]{1,0:T(2,128)} custom-call(s32[2,512]{1,0:T(2,128)S(1)} %copy-done.13, s16[672,128]{1,0:T(8,128)(2,1)S(1)} %collective-permute-done.15.refs_0_, s16[672,128]{1,0:T(8,128)(2,1)S(1)} %collective-permute-done.16.refs_1_, f32[656,256]{1,0:T(8,128)S(1)} %sample_early.3.refs_2_, bf16[4,128,256]{2,1,0:T(8,128)(2,1)S(1)} %copy-done, ...), custom_call_target="tpu_custom_call" | custom-call | flops 169869312 | bytes 4194304 | tf_op jit(solution)/shard_map/sample/pallas_call | solution.py:966
  (32 shorter events, 0.1 us)
Async XLA Ops:
  0.0 15.0 %copy-start.14 = (f32[512]{0:T(512)S(1)}, f32[512]{0:T(512)}, u32[]{:S(2)}) copy-start(f32[512]{0:T(512)} %refs_0_.1) | copy-start | bytes 6148
  7.2 7.7 %copy-start.2 = (bf16[4,256,128]{2,1,0:T(8,128)(2,1)S(1)}, bf16[4,256,128]{2,1,0:T(8,128)(2,1)}, u32[]{:S(2)}) copy-start(bf16[4,256,128]{2,1,0:T(8,128)(2,1)} %constant.74.clone.refs_2_.high_ref.refs_3_) | copy-start | bytes 786436
  7.3 7.7 %copy-start.3 = (bf16[4,256,128]{2,1,0:T(8,128)(2,1)S(1)}, bf16[4,256,128]{2,1,0:T(8,128)(2,1)}, u32[]{:S(2)}) copy-start(bf16[4,256,128]{2,1,0:T(8,128)(2,1)} %constant.75.clone.refs_3_.low_ref.refs_4_) | copy-start | bytes 786436
  7.3 7.7 %copy-start.8 = (bf16[656,256]{1,0:T(8,128)(2,1)S(1)}, bf16[656,256]{1,0:T(8,128)(2,1)}, u32[]{:S(2)}) copy-start(bf16[656,256]{1,0:T(8,128)(2,1)} %get-tuple-element.41.wide_high) | copy-start | bytes 1007620
  7.3 7.7 %copy-start.9 = (bf16[656,256]{1,0:T(8,128)(2,1)S(1)}, bf16[656,256]{1,0:T(8,128)(2,1)}, u32[]{:S(2)}) copy-start(bf16[656,256]{1,0:T(8,128)(2,1)} %get-tuple-element.42.wide_low) | copy-start | bytes 1007620
  7.3 9.4 %collective-permute-start = (s16[672,128]{1,0:T(8,128)(2,1)}, s16[672,128]{1,0:T(8,128)(2,1)S(1)}, u32[]{:S(2)}, u32[]{:S(2)}) collective-permute-start(s16[672,128]{1,0:T(8,128)(2,1)} %get-tuple-element.43), channel_id=1, source_target_pairs={{0,1},{1,0},{2,3},{3,2},{4,5},{5,4},{6,7},{7,6},{8,9},{9,8},{10,11... | collective-permute-start | bytes 516104 | tf_op jit(solution)/shard_map/ppermute | solution.py:1082
  7.8 9.5 %collective-permute-start.1 = (s16[672,128]{1,0:T(8,128)(2,1)}, s16[672,128]{1,0:T(8,128)(2,1)S(1)}, u32[]{:S(2)}, u32[]{:S(2)}) collective-permute-start(s16[672,128]{1,0:T(8,128)(2,1)} %get-tuple-element.44), channel_id=1, source_target_pairs={{0,2},{1,3},{2,0},{3,1},{4,6},{5,7},{6,4},{7,5},{8,10},{9,11},{10,... | collective-permute-start | bytes 516104 | tf_op jit(solution)/shard_map/ppermute | solution.py:1082
  10.4 8.6 %collective-permute-start.2 = (s16[672,128]{1,0:T(8,128)(2,1)}, s16[672,128]{1,0:T(8,128)(2,1)S(1)}, u32[]{:S(2)}, u32[]{:S(2)}) collective-permute-start(s16[672,128]{1,0:T(8,128)(2,1)} %get-tuple-element.45), channel_id=1, source_target_pairs={{0,3},{1,2},{2,1},{3,0},{4,7},{5,6},{6,5},{7,4},{8,11},{9,10},{10,... | collective-permute-start | bytes 516104 | tf_op jit(solution)/shard_map/ppermute | solution.py:1082
  10.4 0.9 copy-start.11
  11.3 0.7 copy-start.12
  12.0 4.6 %copy-start.4 = (bf16[2,256,240]{2,1,0:T(8,128)(2,1)S(1)}, bf16[2,256,240]{2,1,0:T(8,128)(2,1)}, u32[]{:S(2)}) copy-start(bf16[2,256,240]{2,1,0:T(8,128)(2,1)} %constant.76.clone.refs_2_.refs_5_) | copy-start | bytes 737284
  17.3 18.0 %copy-start.6 = (bf16[4,48,256]{2,1,0:T(8,128)(2,1)S(1)}, bf16[4,48,256]{2,1,0:T(8,128)(2,1)}, u32[]{:S(2)}) copy-start(bf16[4,48,256]{2,1,0:T(8,128)(2,1)} %constant.77.clone.refs_6_.high_ref) | copy-start | bytes 294916
  17.3 18.0 %copy-start.7 = (bf16[4,48,256]{2,1,0:T(8,128)(2,1)S(1)}, bf16[4,48,256]{2,1,0:T(8,128)(2,1)}, u32[]{:S(2)}) copy-start(bf16[4,48,256]{2,1,0:T(8,128)(2,1)} %constant.78.clone.refs_7_.low_ref) | copy-start | bytes 294916
  20.8 7.3 %collective-permute-start.3 = (s16[816,128]{1,0:T(8,128)(2,1)S(1)}, s16[816,128]{1,0:T(8,128)(2,1)S(1)}, u32[]{:S(2)}, u32[]{:S(2)}) collective-permute-start(s16[816,128]{1,0:T(8,128)(2,1)S(1)} %get-tuple-element.48), channel_id=1, source_target_pairs={{0,4},{8,12},{4,0},{12,8},{1,5},{9,13},{5,1},{13,9},{2,6},{10,14},... | collective-permute-start | bytes 626696 | tf_op jit(solution)/shard_map/ppermute | solution.py:1093
  22.5 8.7 %collective-permute-start.4 = (s16[816,128]{1,0:T(8,128)(2,1)S(1)}, s16[816,128]{1,0:T(8,128)(2,1)S(1)}, u32[]{:S(2)}, u32[]{:S(2)}) collective-permute-start(s16[816,128]{1,0:T(8,128)(2,1)S(1)} %get-tuple-element.49), channel_id=1, source_target_pairs={{4,8},{8,4},{5,9},{9,5},{6,10},{10,6},{7,11},{11,7},{20,24},{24,20... | collective-permute-start | bytes 626696 | tf_op jit(solution)/shard_map/ppermute | solution.py:1094
  28.1 12.5 %copy-start.16 = (s32[24]{0:T(128)S(1)}, s32[24]{0:T(128)}, u32[]{:S(2)}) copy-start(s32[24]{0:T(128)} %param.21) | copy-start | bytes 292
  28.1 12.5 %copy-start.17 = (s32[24]{0:T(128)S(1)}, s32[24]{0:T(128)}, u32[]{:S(2)}) copy-start(s32[24]{0:T(128)} %param.22) | copy-start | bytes 292
  28.1 12.5 %copy-start.5 = (bf16[24,128,128]{2,1,0:T(8,128)(2,1)S(1)}, bf16[24,128,128]{2,1,0:T(8,128)(2,1)}, u32[]{:S(2)}) copy-start(bf16[24,128,128]{2,1,0:T(8,128)(2,1)} %refs_3_.9) | copy-start | bytes 2359300
  28.4 6.9 %collective-permute-start.5 = (s16[272,128]{1,0:T(8,128)(2,1)S(1)}, s16[272,128]{1,0:T(8,128)(2,1)S(1)}, u32[]{:S(2)}, u32[]{:S(2)}) collective-permute-start(s16[272,128]{1,0:T(8,128)(2,1)S(1)} %pair_messages.2), channel_id=1, source_target_pairs={{0,8},{4,12},{8,0},{12,4},{1,9},{5,13},{9,1},{13,5},{2,10},{6,14},... | collective-permute-start | bytes 208904 | tf_op jit(solution)/shard_map/ppermute | solution.py:1096
  35.3 6.4 %copy-start.10 = (f32[256,128]{1,0:T(8,128)S(1)}, f32[256,128]{1,0:T(8,128)}, u32[]{:S(2)}) copy-start(f32[256,128]{1,0:T(8,128)} %get-tuple-element.58.coeff_ref) | copy-start | bytes 393220
  35.3 6.4 %copy-start.13 = (s32[2,512]{1,0:T(2,128)S(1)}, s32[2,512]{1,0:T(2,128)}, u32[]{:S(2)}) copy-start(s32[2,512]{1,0:T(2,128)} %get-tuple-element.40.place_ref.refs_1_) | copy-start | bytes 12292
  38.4 7.8 %collective-permute-start.6 = (s16[672,128]{1,0:T(8,128)(2,1)S(1)}, s16[672,128]{1,0:T(8,128)(2,1)S(1)}, u32[]{:S(2)}, u32[]{:S(2)}) collective-permute-start(s16[672,128]{1,0:T(8,128)(2,1)S(1)} %get-tuple-element.52), channel_id=1, source_target_pairs={{0,2},{1,3},{2,0},{3,1},{4,6},{5,7},{6,4},{7,5},{8,10},{9,11},{10,... | collective-permute-start | bytes 516104 | tf_op jit(solution)/shard_map/ppermute | solution.py:1082
  39.9 6.7 %collective-permute-start.7 = (s16[672,128]{1,0:T(8,128)(2,1)S(1)}, s16[672,128]{1,0:T(8,128)(2,1)S(1)}, u32[]{:S(2)}, u32[]{:S(2)}) collective-permute-start(s16[672,128]{1,0:T(8,128)(2,1)S(1)} %get-tuple-element.53), channel_id=1, source_target_pairs={{0,3},{1,2},{2,1},{3,0},{4,7},{5,6},{6,5},{7,4},{8,11},{9,10},{10,... | collective-permute-start | bytes 516104 | tf_op jit(solution)/shard_map/ppermute | solution.py:1082
  39.9 5.6 %collective-permute-start.8 = (s16[672,128]{1,0:T(8,128)(2,1)S(1)}, s16[672,128]{1,0:T(8,128)(2,1)S(1)}, u32[]{:S(2)}, u32[]{:S(2)}) collective-permute-start(s16[672,128]{1,0:T(8,128)(2,1)S(1)} %get-tuple-element.56), channel_id=1, source_target_pairs={{0,1},{1,0},{2,3},{3,2},{4,5},{5,4},{6,7},{7,6},{8,9},{9,8},{10,11... | collective-permute-start | bytes 516104 | tf_op jit(solution)/shard_map/ppermute | solution.py:1082
  44.7 1.0 copy-start
  44.7 1.0 %copy-start.1 = (bf16[4,128,256]{2,1,0:T(8,128)(2,1)S(1)}, bf16[4,128,256]{2,1,0:T(8,128)(2,1)}, u32[]{:S(2)}) copy-start(bf16[4,128,256]{2,1,0:T(8,128)(2,1)} %constant.80.clone.refs_3_.refs_4_) | copy-start | bytes 786436
  44.7 1.9 %copy-start.15 = (s32[512]{0:T(512)S(1)}, s32[512]{0:T(512)}, u32[]{:S(2)}) copy-start(s32[512]{0:T(512)} %param.17) | copy-start | bytes 6148
  52.7 2.8 %collective-permute-start.9 = (s16[672,128]{1,0:T(8,128)(2,1)S(1)}, s16[672,128]{1,0:T(8,128)(2,1)S(1)}, u32[]{:S(2)}, u32[]{:S(2)}) collective-permute-start(s16[672,128]{1,0:T(8,128)(2,1)S(1)} %get-tuple-element.61), channel_id=1, source_target_pairs={{0,1},{1,0},{2,3},{3,2},{4,5},{5,4},{6,7},{7,6},{8,9},{9,8},{10,11... | collective-permute-start | bytes 516104 | tf_op jit(solution)/shard_map/ppermute | solution.py:1082
  53.5 7.2 %collective-permute-start.10 = (s16[672,128]{1,0:T(8,128)(2,1)S(1)}, s16[672,128]{1,0:T(8,128)(2,1)S(1)}, u32[]{:S(2)}, u32[]{:S(2)}) collective-permute-start(s16[672,128]{1,0:T(8,128)(2,1)S(1)} %get-tuple-element.62), channel_id=1, source_target_pairs={{0,2},{1,3},{2,0},{3,1},{4,6},{5,7},{6,4},{7,5},{8,10},{9,11},{10,... | collective-permute-start | bytes 516104 | tf_op jit(solution)/shard_map/ppermute | solution.py:1082
  55.0 7.7 %collective-permute-start.11 = (s16[672,128]{1,0:T(8,128)(2,1)S(1)}, s16[672,128]{1,0:T(8,128)(2,1)S(1)}, u32[]{:S(2)}, u32[]{:S(2)}) collective-permute-start(s16[672,128]{1,0:T(8,128)(2,1)S(1)} %get-tuple-element.63), channel_id=1, source_target_pairs={{0,3},{1,2},{2,1},{3,0},{4,7},{5,6},{6,5},{7,4},{8,11},{9,10},{10,... | collective-permute-start | bytes 516104 | tf_op jit(solution)/shard_map/ppermute | solution.py:1082
  64.5 7.8 %collective-permute-start.12 = (s16[816,128]{1,0:T(8,128)(2,1)S(1)}, s16[816,128]{1,0:T(8,128)(2,1)S(1)}, u32[]{:S(2)}, u32[]{:S(2)}) collective-permute-start(s16[816,128]{1,0:T(8,128)(2,1)S(1)} %get-tuple-element.65), channel_id=1, source_target_pairs={{0,4},{8,12},{4,0},{12,8},{1,5},{9,13},{5,1},{13,9},{2,6},{10,14},... | collective-permute-start | bytes 626696 | tf_op jit(solution)/shard_map/ppermute | solution.py:1093
  64.7 9.5 %collective-permute-start.13 = (s16[816,128]{1,0:T(8,128)(2,1)S(1)}, s16[816,128]{1,0:T(8,128)(2,1)S(1)}, u32[]{:S(2)}, u32[]{:S(2)}) collective-permute-start(s16[816,128]{1,0:T(8,128)(2,1)S(1)} %get-tuple-element.66), channel_id=1, source_target_pairs={{4,8},{8,4},{5,9},{9,5},{6,10},{10,6},{7,11},{11,7},{20,24},{24,20... | collective-permute-start | bytes 626696 | tf_op jit(solution)/shard_map/ppermute | solution.py:1094
  72.6 6.4 %collective-permute-start.14 = (s16[272,128]{1,0:T(8,128)(2,1)S(1)}, s16[272,128]{1,0:T(8,128)(2,1)S(1)}, u32[]{:S(2)}, u32[]{:S(2)}) collective-permute-start(s16[272,128]{1,0:T(8,128)(2,1)S(1)} %pair_messages.3), channel_id=1, source_target_pairs={{0,8},{4,12},{8,0},{12,4},{1,9},{5,13},{9,1},{13,5},{2,10},{6,14},... | collective-permute-start | bytes 208904 | tf_op jit(solution)/shard_map/ppermute | solution.py:1096
  82.0 3.9 %collective-permute-start.17 = (s16[672,128]{1,0:T(8,128)(2,1)S(1)}, s16[672,128]{1,0:T(8,128)(2,1)S(1)}, u32[]{:S(2)}, u32[]{:S(2)}) collective-permute-start(s16[672,128]{1,0:T(8,128)(2,1)S(1)} %get-tuple-element.73), channel_id=1, source_target_pairs={{0,1},{1,0},{2,3},{3,2},{4,5},{5,4},{6,7},{7,6},{8,9},{9,8},{10,11... | collective-permute-start | bytes 516104 | tf_op jit(solution)/shard_map/ppermute | solution.py:1082
  82.1 7.2 %collective-permute-start.15 = (s16[672,128]{1,0:T(8,128)(2,1)S(1)}, s16[672,128]{1,0:T(8,128)(2,1)S(1)}, u32[]{:S(2)}, u32[]{:S(2)}) collective-permute-start(s16[672,128]{1,0:T(8,128)(2,1)S(1)} %get-tuple-element.69), channel_id=1, source_target_pairs={{0,2},{1,3},{2,0},{3,1},{4,6},{5,7},{6,4},{7,5},{8,10},{9,11},{10,... | collective-permute-start | bytes 516104 | tf_op jit(solution)/shard_map/ppermute | solution.py:1082
  83.7 8.5 %collective-permute-start.16 = (s16[672,128]{1,0:T(8,128)(2,1)S(1)}, s16[672,128]{1,0:T(8,128)(2,1)S(1)}, u32[]{:S(2)}, u32[]{:S(2)}) collective-permute-start(s16[672,128]{1,0:T(8,128)(2,1)S(1)} %get-tuple-element.70), channel_id=1, source_target_pairs={{0,3},{1,2},{2,1},{3,0},{4,7},{5,6},{6,5},{7,4},{8,11},{9,10},{10,... | collective-permute-start | bytes 516104 | tf_op jit(solution)/shard_map/ppermute | solution.py:1082

commit v8 on v7

--- a/solution.py
+++ b/solution.py
@@ -21,9 +21,9 @@
 F32 = jnp.float32
 BF16 = jnp.bfloat16
 VMEM_LIMIT = 24 * 1024 * 1024
-START_LIMIT = 60 * 1024 * 1024
+START_LIMIT = VMEM_LIMIT
 GROUP = 32
-CHAINS = 2
+CHAINS = 4
 
 
 def cas(angles):
@@ -375,6 +375,8 @@
     if placed is None:
         stencil, flag, sample, dipole = raw
         operands = [vector, rounded, *table, stencil, flag.reshape(1, -1), sample, dipole]
+        pinned = [pltpu.with_memory_space_constraint(value, pltpu.HBM) for value in operands[1:]]
+        operands = [vector] + pinned
         in_specs = [in_smem()] + [pl.BlockSpec(memory_space=pltpu.HBM)] * 7
         out_shapes += [jax.ShapeDtypeStruct(woven, F32)] * 2
         out_shapes += [jax.ShapeDtypeStruct((2, count), jnp.int32)]

time: 96 us -> 94.9 us (0.989)
  local copies, waits for them, and re-layouts: 2.9 us -> 1.27 us
  waiting for transfers between devices: 34.9 us -> 36.3 us
    unnamed x36 -> x24, local copies, waits for them, and re-layouts: 1.81 us -> 0.19 us
    ppermute x12, waiting for transfers between devices: 14.4 us -> 15.8 us  [flipped(): lax.ppermute(part, Y_AXES, [(i, i ^ flip) for i in range(y_count)])]
where the time goes in v8:
time: 94.9 us; the launch traced here: 94.6 us
  Pallas kernels  39.2 us (41%)
  waiting for transfers between devices  36.3 us (38%)
  starting transfers between devices  17.5 us (18%)
  local copies, waits for them, and re-layouts  1.27 us (1%)
    ppermute x12, waiting for transfers between devices, flipped(): lax.ppermute(part, Y_AXES, [(i, i ^ flip) for i in range(y_count)])  15.8 us
    ppermute x2, waiting for transfers between devices, convolve_and_sample(): from_even = lax.ppermute(even_message, 'wide', even_swap)  11.7 us
    ppermute x12, starting transfers between devices, flipped(): lax.ppermute(part, Y_AXES, [(i, i ^ flip) for i in range(y_count)])  9.61 us
    pallas_call x2, Pallas kernels, spread(): pl.pallas_call(functools.partial(start_kernel if placed is None else spre...  9.5 us
    ppermute x2, waiting for transfers between devices, convolve_and_sample(): lax.ppermute(message, 'wide', [(i, i ^ flip) for i in range(x_count)])  8.86 us
    pallas_call x2, Pallas kernels, sample(): pl.pallas_call(functools.partial(sample_kernel, last, reach_x, reach_y, f...  6.49 us
    pallas_call x2, Pallas kernels, inverse(): pl.pallas_call(functools.partial(inverse_kernel, reach_x, reach_y, flips,...  6.16 us
    pallas_call x2, Pallas kernels, place_lines(): pl.pallas_call(lines_kernel, in_specs=[in_smem(), whole_vmem()] + [anywhe...  5.9 us
  transfers between devices with their start and end apart: 18, of which 10 were waited for; matrix products, arithmetic and copies ran while one was open for 1% of the time, Pallas kernels for 14%

profile of v8, /device:TPU:0, one launch (start us, length us, event | category | flops | bytes accessed | tf_op | source)
XLA Modules:
  0.0 94.6 jit_solution(12489302543801885482)
XLA Ops:
  0.0 6.2 %start.1 = (s16[672,128]{1,0:T(8,128)(2,1)S(1)}, s16[672,128]{1,0:T(8,128)(2,1)S(1)}, s16[672,128]{1,0:T(8,128)(2,1)S(1)}, bf16[656,256]{1,0:T(8,128)(2,1)S(1)},...) custom-call(f32[512]{0:T(512)} %refs_0_.1, ...), custom_call_target="tpu_custom_call" | custom-call | flops 169869312 | bytes 4194304 | tf_op jit(solution)/shard_map/start/pallas_call | solution.py:398
  6.2 0.0 copy-start.2
  6.2 0.0 copy-start.3
  6.2 0.0 copy-start.8
  6.2 0.5 collective-permute-start
  6.8 2.6 %collective-permute-start.1 = (s16[672,128]{1,0:T(8,128)(2,1)S(1)}, s16[672,128]{1,0:T(8,128)(2,1)S(1)}, u32[]{:S(2)}, u32[]{:S(2)}) collective-permute-start(s16[672,128]{1,0:T(8,128)(2,1)S(1)} %get-tuple-element.44), channel_id=1, source_target_pairs={{0,2},{1,3},{2,0},{3,1},{4,6},{5,7},{6,4},{7,5},{8,10},{9,11},{10,... | collective-permute-start | bytes 516104 | tf_op jit(solution)/shard_map/ppermute | solution.py:1084
  9.3 0.1 collective-permute-start.2
  9.4 2.9 %place_lines.2.refs_7_.refs_5_ = f32[8192,128]{1,0:T(8,128)S(1)} custom-call(s32[2,512]{1,0:T(2,128)S(1)} %get-tuple-element.40.place_ref.refs_1_, f32[256,128]{1,0:T(8,128)S(1)} %get-tuple-element.46.coeff_ref), custom_call_target="tpu_custom_call" | custom-call | flops 1048576 | bytes 4194304 | tf_op jit(solution)/shard_map/place_lines/pallas_call | solution.py:459
  12.4 0.5 spread_rest.2.refs_0_
  12.9 1.1 %dynamic-slice_bitcast_fusion.refs_6_.modes_ref.refs_8_ = f32[4,256,128]{2,1,0:T(8,128)S(1)} fusion(f32[4,4,256,128]{3,2,1,0:T(8,128)} %constant.73.clone, s32[]{:T(128)S(6)} %select_n.30), kind=kLoop, calls=%fused_computation | loop fusion | bytes 1048580 | tf_op jit(solution)/shard_map/jit(dynamic_index_in_dim)/squeeze | solution.py:1065
  14.0 0.6 forward_early.2.refs_4_
  14.6 0.0 copy-start.6
  14.7 0.0 copy-start.7
  14.7 0.0 collective-permute-done.1.refs_2_
  14.7 3.0 %collective-permute-done.2.refs_3_ = s16[672,128]{1,0:T(8,128)(2,1)S(1)} collective-permute-done((s16[672,128]{1,0:T(8,128)(2,1)S(1)}, s16[672,128]{1,0:T(8,128)(2,1)S(1)}, u32[]{:S(2)}, u32[]{:S(2)}) %collective-permute-start.2) | collective-permute-done | bytes 172064 | tf_op jit(solution)/shard_map/ppermute | solution.py:1084
  17.7 1.8 %forward.2 = (f32[18,256,128]{2,1,0:T(8,128)S(1)}, s16[816,128]{1,0:T(8,128)(2,1)S(1)}, s16[816,128]{1,0:T(8,128)(2,1)S(1)}, f32[256,128]{1,0:T(8,128)S(1)}, f32...) custom-call(s16[672,128]{1,0:T(8,128)(2,1)S(1)} %spread_rest.2.refs_0_, s16[672,128]{1,0:T(8,128)(2,1)S(1)} %collective-permute-done.refs_1_, ...), custom_call_target="tpu_custom_call" | custom-call | flops 301989888 | bytes 4718592 | tf_op jit(solution)/shard_map/forward/pallas_call | solution.py:634
  19.5 1.7 %collective-permute-start.3 = (s16[816,128]{1,0:T(8,128)(2,1)S(1)}, s16[816,128]{1,0:T(8,128)(2,1)S(1)}, u32[]{:S(2)}, u32[]{:S(2)}) collective-permute-start(s16[816,128]{1,0:T(8,128)(2,1)S(1)} %get-tuple-element.48), channel_id=1, source_target_pairs={{0,4},{8,12},{4,0},{12,8},{1,5},{9,13},{5,1},{13,9},{2,6},{10,14},... | collective-permute-start | bytes 626696 | tf_op jit(solution)/shard_map/ppermute | solution.py:1095
  21.2 0.7 collective-permute-start.4
  21.9 4.9 %collective-permute-done.3.even_ref.refs_1_.refs_0_ = s16[816,128]{1,0:T(8,128)(2,1)S(1)} collective-permute-done((s16[816,128]{1,0:T(8,128)(2,1)S(1)}, s16[816,128]{1,0:T(8,128)(2,1)S(1)}, u32[]{:S(2)}, u32[]{:S(2)}) %collective-permute-start.3) | collective-permute-done | bytes 208928 | tf_op jit(solution)/shard_map/ppermute | solution.py:1095
  26.8 0.2 pair_messages.2
  27.1 2.8 %collective-permute-start.5 = (s16[272,128]{1,0:T(8,128)(2,1)S(1)}, s16[272,128]{1,0:T(8,128)(2,1)S(1)}, u32[]{:S(2)}, u32[]{:S(2)}) collective-permute-start(s16[272,128]{1,0:T(8,128)(2,1)S(1)} %pair_messages.2), channel_id=1, source_target_pairs={{0,8},{4,12},{8,0},{12,4},{1,9},{5,13},{9,1},{13,5},{2,10},{6,14},... | collective-permute-start | bytes 208904 | tf_op jit(solution)/shard_map/ppermute | solution.py:1098
  29.9 0.0 collective-permute-done.4.refs_2_.refs_1_
  29.9 4.1 %collective-permute-done.5.refs_5_ = s16[272,128]{1,0:T(8,128)(2,1)S(1)} collective-permute-done((s16[272,128]{1,0:T(8,128)(2,1)S(1)}, s16[272,128]{1,0:T(8,128)(2,1)S(1)}, u32[]{:S(2)}, u32[]{:S(2)}) %collective-permute-start.5) | collective-permute-done | bytes 69664 | tf_op jit(solution)/shard_map/ppermute | solution.py:1098
  34.0 3.1 %inverse.2 = (s16[672,128]{1,0:T(8,128)(2,1)S(1)}, s16[672,128]{1,0:T(8,128)(2,1)S(1)}, s16[672,128]{1,0:T(8,128)(2,1)S(1)}, bf16[18,256,128]{2,1,0:T(8,128)(2,1)S(1)}, bf16[18,256,128]{2,1,0:T(8,128)(2,1)S(1)}) custom-call(f32[18,256,128]{2,1,0:T(8,128)S(1)} %get-tuple-element.47.refs_0_, ...), custom_call_target="tpu_custom_call" | custom-call | flops 301989888 | bytes 4718592 | tf_op jit(solution)/shard_map/inverse/pallas_call | solution.py:828
  37.1 1.5 %collective-permute-start.6 = (s16[672,128]{1,0:T(8,128)(2,1)S(1)}, s16[672,128]{1,0:T(8,128)(2,1)S(1)}, u32[]{:S(2)}, u32[]{:S(2)}) collective-permute-start(s16[672,128]{1,0:T(8,128)(2,1)S(1)} %get-tuple-element.52), channel_id=1, source_target_pairs={{0,2},{1,3},{2,0},{3,1},{4,6},{5,7},{6,4},{7,5},{8,10},{9,11},{10,... | collective-permute-start | bytes 516104 | tf_op jit(solution)/shard_map/ppermute | solution.py:1084
  38.7 0.7 collective-permute-start.8
  39.4 1.1 %near_field.2.refs_8_.refs_0_ = f32[8,128]{1,0:T(8,128)S(1)} custom-call(s32[24]{0:T(128)S(1)} %get-tuple-element.76.place_ref, s32[24]{0:T(128)S(1)} %get-tuple-element.75.target_ref, s16[816,128]{1,0:T(8,128)(2,1)S(1)} %collective-permute-done.3.even_ref.refs_1_.refs_0_, s16[816,128]{1,0:T(8,128)(2,1)S(1)} %collective-permute-done.4.refs_2_.refs_1_, ...), custom_call_target="tpu_custom_call" | custom-call | flops 12582912 | bytes 786432 | tf_op jit(solution)/shard_map/near_field/pallas_call | solution.py:1023
  40.4 3.0 %place_lines.3.refs_5_ = f32[8192,128]{1,0:T(8,128)S(1)} custom-call(s32[2,512]{1,0:T(2,128)S(1)} %get-tuple-element.40.place_ref.refs_1_, f32[256,128]{1,0:T(8,128)S(1)} %get-tuple-element.58.coeff_ref, f32[8,128]{1,0:T(8,128)S(1)} %near_field.2.refs_8_.refs_0_), custom_call_target="tpu_custom_call" | custom-call | flops 1048576 | bytes 4194304 | tf_op jit(solution)/shard_map/place_lines/pallas_call | solution.py:459
  43.4 0.0 copy-start.1
  43.4 0.0 copy-start.9
  43.4 0.9 inverse_rest.2.refs_0_
  44.3 0.0 collective-permute-done.8.refs_1_
  44.3 0.0 copy-done
  44.3 0.1 copy-done.1
  44.4 0.4 sample_early.2.refs_2_
  44.9 0.0 collective-permute-done.6.refs_0_
  44.9 0.4 collective-permute-done.7.refs_1_
  45.3 2.9 %sample.2.refs_2_.rounded_ref.refs_7_ = f32[4,128]{1,0:T(4,128)S(1)} custom-call(s32[2,512]{1,0:T(2,128)S(1)} %get-tuple-element.40.place_ref.refs_1_, s16[672,128]{1,0:T(8,128)(2,1)S(1)} %collective-permute-done.6.refs_0_, s16[672,128]{1,0:T(8,128)(2,1)S(1)} %collective-permute-done.7.refs_1_, f32[656,256]{1,0:T(8,128)S(1)} %sample_early.2.refs_2_, ...), custom_call_target="tpu_custom_call" | custom-call | flops 169869312 | bytes 4194304 | tf_op jit(solution)/shard_map/sample/pallas_call | solution.py:968
  48.3 3.3 %spread.1 = (s16[672,128]{1,0:T(8,128)(2,1)S(1)}, s16[672,128]{1,0:T(8,128)(2,1)S(1)}, s16[672,128]{1,0:T(8,128)(2,1)S(1)}, bf16[656,256]{1,0:T(8,128)(2,1)S(1)}, bf16[656,256]{1,0:T(8,128)(2,1)S(1)}) custom-call(f32[512]{0:T(512)S(1)} %bitcast.6, s32[2,512]{1,0:T(2,128)S(1)} %get-tuple-element.40.place_ref.refs_1_, ...), custom_call_target="tpu_custom_call" | custom-call | flops 169869312 | bytes 4194304 | tf_op jit(solution)/shard_map/spread/pallas_call | solution.py:398
  51.6 0.8 collective-permute-start.9
  52.4 1.5 %collective-permute-start.10 = (s16[672,128]{1,0:T(8,128)(2,1)S(1)}, s16[672,128]{1,0:T(8,128)(2,1)S(1)}, u32[]{:S(2)}, u32[]{:S(2)}) collective-permute-start(s16[672,128]{1,0:T(8,128)(2,1)S(1)} %get-tuple-element.62), channel_id=1, source_target_pairs={{0,2},{1,3},{2,0},{3,1},{4,6},{5,7},{6,4},{7,5},{8,10},{9,11},{10,... | collective-permute-start | bytes 516104 | tf_op jit(solution)/shard_map/ppermute | solution.py:1084
  53.9 0.0 collective-permute-start.11
  53.9 0.5 spread_rest.3.refs_0_
  54.4 0.6 forward_early.3.refs_4_
  55.1 4.6 %collective-permute-done.10.refs_2_ = s16[672,128]{1,0:T(8,128)(2,1)S(1)} collective-permute-done((s16[672,128]{1,0:T(8,128)(2,1)S(1)}, s16[672,128]{1,0:T(8,128)(2,1)S(1)}, u32[]{:S(2)}, u32[]{:S(2)}) %collective-permute-start.10) | collective-permute-done | bytes 172064 | tf_op jit(solution)/shard_map/ppermute | solution.py:1084
  59.7 1.9 %collective-permute-done.11.refs_3_ = s16[672,128]{1,0:T(8,128)(2,1)S(1)} collective-permute-done((s16[672,128]{1,0:T(8,128)(2,1)S(1)}, s16[672,128]{1,0:T(8,128)(2,1)S(1)}, u32[]{:S(2)}, u32[]{:S(2)}) %collective-permute-start.11) | collective-permute-done | bytes 172064 | tf_op jit(solution)/shard_map/ppermute | solution.py:1084
  61.6 1.8 %forward.3 = (f32[18,256,128]{2,1,0:T(8,128)S(1)}, s16[816,128]{1,0:T(8,128)(2,1)S(1)}, s16[816,128]{1,0:T(8,128)(2,1)S(1)}, f32[256,128]{1,0:T(8,128)S(1)}, f32...) custom-call(s16[672,128]{1,0:T(8,128)(2,1)S(1)} %spread_rest.3.refs_0_, s16[672,128]{1,0:T(8,128)(2,1)S(1)} %collective-permute-done.9.refs_1_, ...), custom_call_target="tpu_custom_call" | custom-call | flops 301989888 | bytes 4718592 | tf_op jit(solution)/shard_map/forward/pallas_call | solution.py:634
  63.4 0.2 collective-permute-start.12
  63.7 0.8 collective-permute-start.13
  64.5 6.7 %collective-permute-done.12.even_ref.refs_1_.refs_0_ = s16[816,128]{1,0:T(8,128)(2,1)S(1)} collective-permute-done((s16[816,128]{1,0:T(8,128)(2,1)S(1)}, s16[816,128]{1,0:T(8,128)(2,1)S(1)}, u32[]{:S(2)}, u32[]{:S(2)}) %collective-permute-start.12) | collective-permute-done | bytes 208928 | tf_op jit(solution)/shard_map/ppermute | solution.py:1095
  71.3 0.2 pair_messages.3
  71.5 1.6 %collective-permute-start.14 = (s16[272,128]{1,0:T(8,128)(2,1)S(1)}, s16[272,128]{1,0:T(8,128)(2,1)S(1)}, u32[]{:S(2)}, u32[]{:S(2)}) collective-permute-start(s16[272,128]{1,0:T(8,128)(2,1)S(1)} %pair_messages.3), channel_id=1, source_target_pairs={{0,8},{4,12},{8,0},{12,4},{1,9},{5,13},{9,1},{13,5},{2,10},{6,14},... | collective-permute-start | bytes 208904 | tf_op jit(solution)/shard_map/ppermute | solution.py:1098
  73.1 0.0 collective-permute-done.13.refs_2_.refs_1_
  73.1 4.8 %collective-permute-done.14.refs_5_ = s16[272,128]{1,0:T(8,128)(2,1)S(1)} collective-permute-done((s16[272,128]{1,0:T(8,128)(2,1)S(1)}, s16[272,128]{1,0:T(8,128)(2,1)S(1)}, u32[]{:S(2)}, u32[]{:S(2)}) %collective-permute-start.14) | collective-permute-done | bytes 69664 | tf_op jit(solution)/shard_map/ppermute | solution.py:1098
  77.9 3.1 %inverse.3 = (s16[672,128]{1,0:T(8,128)(2,1)S(1)}, s16[672,128]{1,0:T(8,128)(2,1)S(1)}, s16[672,128]{1,0:T(8,128)(2,1)S(1)}, bf16[18,256,128]{2,1,0:T(8,128)(2,1)S(1)}, bf16[18,256,128]{2,1,0:T(8,128)(2,1)S(1)}) custom-call(f32[18,256,128]{2,1,0:T(8,128)S(1)} %get-tuple-element.64.refs_0_, ...), custom_call_target="tpu_custom_call" | custom-call | flops 301989888 | bytes 4718592 | tf_op jit(solution)/shard_map/inverse/pallas_call | solution.py:828
  81.0 0.1 collective-permute-start.17
  81.1 1.5 %collective-permute-start.15 = (s16[672,128]{1,0:T(8,128)(2,1)S(1)}, s16[672,128]{1,0:T(8,128)(2,1)S(1)}, u32[]{:S(2)}, u32[]{:S(2)}) collective-permute-start(s16[672,128]{1,0:T(8,128)(2,1)S(1)} %get-tuple-element.69), channel_id=1, source_target_pairs={{0,2},{1,3},{2,0},{3,1},{4,6},{5,7},{6,4},{7,5},{8,10},{9,11},{10,... | collective-permute-start | bytes 516104 | tf_op jit(solution)/shard_map/ppermute | solution.py:1084
  82.6 0.3 collective-permute-start.16
  82.9 1.0 %near_field.3.refs_8_ = f32[8,128]{1,0:T(8,128)S(1)} custom-call(s32[24]{0:T(128)S(1)} %get-tuple-element.76.place_ref, s32[24]{0:T(128)S(1)} %get-tuple-element.75.target_ref, s16[816,128]{1,0:T(8,128)(2,1)S(1)} %collective-permute-done.12.even_ref.refs_1_.refs_0_, s16[816,128]{1,0:T(8,128)(2,1)S(1)} %collective-permute-done.13.refs_2_.refs_1_, ...), custom_call_target="tpu_custom_call" | custom-call | flops 12582912 | bytes 786432 | tf_op jit(solution)/shard_map/near_field/pallas_call | solution.py:1023
  84.0 0.9 inverse_rest.3.refs_0_
  84.9 0.4 sample_early.3.refs_2_
  85.3 3.0 %collective-permute-done.15.refs_0_ = s16[672,128]{1,0:T(8,128)(2,1)S(1)} collective-permute-done((s16[672,128]{1,0:T(8,128)(2,1)S(1)}, s16[672,128]{1,0:T(8,128)(2,1)S(1)}, u32[]{:S(2)}, u32[]{:S(2)}) %collective-permute-start.15) | collective-permute-done | bytes 172064 | tf_op jit(solution)/shard_map/ppermute | solution.py:1084
  88.3 2.8 %collective-permute-done.16.refs_1_ = s16[672,128]{1,0:T(8,128)(2,1)S(1)} collective-permute-done((s16[672,128]{1,0:T(8,128)(2,1)S(1)}, s16[672,128]{1,0:T(8,128)(2,1)S(1)}, u32[]{:S(2)}, u32[]{:S(2)}) %collective-permute-start.16) | collective-permute-done | bytes 172064 | tf_op jit(solution)/shard_map/ppermute | solution.py:1084
  91.1 3.6 %sample.3 = f32[2,512]{1,0:T(2,128)} custom-call(s32[2,512]{1,0:T(2,128)S(1)} %get-tuple-element.40.place_ref.refs_1_, s16[672,128]{1,0:T(8,128)(2,1)S(1)} %collective-permute-done.15.refs_0_, s16[672,128]{1,0:T(8,128)(2,1)S(1)} %collective-permute-done.16.refs_1_, f32[656,256]{1,0:T(8,128)S(1)} %sample_early.3.refs_2_, bf16[4,128,256]{2,1,0:T(8,128)(2,1)S(1)} %copy-done, ...), custom_call_target="tpu_custom_call" | custom-call | flops 169869312 | bytes 4194304 | tf_op jit(solution)/shard_map/sample/pallas_call | solution.py:968
  (20 shorter events, 0.1 us)
Async XLA Ops:
  6.2 6.1 %copy-start.2 = (bf16[4,256,128]{2,1,0:T(8,128)(2,1)S(1)}, bf16[4,256,128]{2,1,0:T(8,128)(2,1)}, u32[]{:S(2)}) copy-start(bf16[4,256,128]{2,1,0:T(8,128)(2,1)} %constant.74.clone.refs_2_.high_ref.refs_3_) | copy-start | bytes 786436
  6.2 6.1 %copy-start.3 = (bf16[4,256,128]{2,1,0:T(8,128)(2,1)S(1)}, bf16[4,256,128]{2,1,0:T(8,128)(2,1)}, u32[]{:S(2)}) copy-start(bf16[4,256,128]{2,1,0:T(8,128)(2,1)} %constant.75.clone.refs_3_.low_ref.refs_4_) | copy-start | bytes 786436
  6.2 6.1 %copy-start.8 = (f32[512]{0:T(512)S(1)}, f32[512]{0:T(512)}, u32[]{:S(2)}) copy-start(f32[512]{0:T(512)} %refs_0_.1) | copy-start | bytes 6148
  6.2 7.7 %collective-permute-start = (s16[672,128]{1,0:T(8,128)(2,1)S(1)}, s16[672,128]{1,0:T(8,128)(2,1)S(1)}, u32[]{:S(2)}, u32[]{:S(2)}) collective-permute-start(s16[672,128]{1,0:T(8,128)(2,1)S(1)} %get-tuple-element.43), channel_id=1, source_target_pairs={{0,1},{1,0},{2,3},{3,2},{4,5},{5,4},{6,7},{7,6},{8,9},{9,8},{10,11... | collective-permute-start | bytes 516104 | tf_op jit(solution)/shard_map/ppermute | solution.py:1084
  6.8 7.9 %collective-permute-start.1 = (s16[672,128]{1,0:T(8,128)(2,1)S(1)}, s16[672,128]{1,0:T(8,128)(2,1)S(1)}, u32[]{:S(2)}, u32[]{:S(2)}) collective-permute-start(s16[672,128]{1,0:T(8,128)(2,1)S(1)} %get-tuple-element.44), channel_id=1, source_target_pairs={{0,2},{1,3},{2,0},{3,1},{4,6},{5,7},{6,4},{7,5},{8,10},{9,11},{10,... | collective-permute-start | bytes 516104 | tf_op jit(solution)/shard_map/ppermute | solution.py:1084
  9.3 8.4 %collective-permute-start.2 = (s16[672,128]{1,0:T(8,128)(2,1)S(1)}, s16[672,128]{1,0:T(8,128)(2,1)S(1)}, u32[]{:S(2)}, u32[]{:S(2)}) collective-permute-start(s16[672,128]{1,0:T(8,128)(2,1)S(1)} %get-tuple-element.45), channel_id=1, source_target_pairs={{0,3},{1,2},{2,1},{3,0},{4,7},{5,6},{6,5},{7,4},{8,11},{9,10},{10,... | collective-permute-start | bytes 516104 | tf_op jit(solution)/shard_map/ppermute | solution.py:1084
  9.4 4.6 %copy-start.4 = (bf16[2,256,240]{2,1,0:T(8,128)(2,1)S(1)}, bf16[2,256,240]{2,1,0:T(8,128)(2,1)}, u32[]{:S(2)}) copy-start(bf16[2,256,240]{2,1,0:T(8,128)(2,1)} %constant.76.clone.refs_2_.refs_5_) | copy-start | bytes 737284
  14.6 19.4 %copy-start.6 = (bf16[4,48,256]{2,1,0:T(8,128)(2,1)S(1)}, bf16[4,48,256]{2,1,0:T(8,128)(2,1)}, u32[]{:S(2)}) copy-start(bf16[4,48,256]{2,1,0:T(8,128)(2,1)} %constant.77.clone.refs_6_.high_ref) | copy-start | bytes 294916
  14.7 19.4 %copy-start.7 = (bf16[4,48,256]{2,1,0:T(8,128)(2,1)S(1)}, bf16[4,48,256]{2,1,0:T(8,128)(2,1)}, u32[]{:S(2)}) copy-start(bf16[4,48,256]{2,1,0:T(8,128)(2,1)} %constant.78.clone.refs_7_.low_ref) | copy-start | bytes 294916
  19.5 7.3 %collective-permute-start.3 = (s16[816,128]{1,0:T(8,128)(2,1)S(1)}, s16[816,128]{1,0:T(8,128)(2,1)S(1)}, u32[]{:S(2)}, u32[]{:S(2)}) collective-permute-start(s16[816,128]{1,0:T(8,128)(2,1)S(1)} %get-tuple-element.48), channel_id=1, source_target_pairs={{0,4},{8,12},{4,0},{12,8},{1,5},{9,13},{5,1},{13,9},{2,6},{10,14},... | collective-permute-start | bytes 626696 | tf_op jit(solution)/shard_map/ppermute | solution.py:1095
  21.2 8.7 %collective-permute-start.4 = (s16[816,128]{1,0:T(8,128)(2,1)S(1)}, s16[816,128]{1,0:T(8,128)(2,1)S(1)}, u32[]{:S(2)}, u32[]{:S(2)}) collective-permute-start(s16[816,128]{1,0:T(8,128)(2,1)S(1)} %get-tuple-element.49), channel_id=1, source_target_pairs={{4,8},{8,4},{5,9},{9,5},{6,10},{10,6},{7,11},{11,7},{20,24},{24,20... | collective-permute-start | bytes 626696 | tf_op jit(solution)/shard_map/ppermute | solution.py:1096
  26.8 12.5 %copy-start.10 = (s32[24]{0:T(128)S(1)}, s32[24]{0:T(128)}, u32[]{:S(2)}) copy-start(s32[24]{0:T(128)} %param.21) | copy-start | bytes 292
  26.8 12.5 %copy-start.11 = (s32[24]{0:T(128)S(1)}, s32[24]{0:T(128)}, u32[]{:S(2)}) copy-start(s32[24]{0:T(128)} %param.22) | copy-start | bytes 292
  26.8 12.5 %copy-start.5 = (bf16[24,128,128]{2,1,0:T(8,128)(2,1)S(1)}, bf16[24,128,128]{2,1,0:T(8,128)(2,1)}, u32[]{:S(2)}) copy-start(bf16[24,128,128]{2,1,0:T(8,128)(2,1)} %refs_3_.9) | copy-start | bytes 2359300
  27.1 6.9 %collective-permute-start.5 = (s16[272,128]{1,0:T(8,128)(2,1)S(1)}, s16[272,128]{1,0:T(8,128)(2,1)S(1)}, u32[]{:S(2)}, u32[]{:S(2)}) collective-permute-start(s16[272,128]{1,0:T(8,128)(2,1)S(1)} %pair_messages.2), channel_id=1, source_target_pairs={{0,8},{4,12},{8,0},{12,4},{1,9},{5,13},{9,1},{13,5},{2,10},{6,14},... | collective-permute-start | bytes 208904 | tf_op jit(solution)/shard_map/ppermute | solution.py:1098
  37.1 7.8 %collective-permute-start.6 = (s16[672,128]{1,0:T(8,128)(2,1)S(1)}, s16[672,128]{1,0:T(8,128)(2,1)S(1)}, u32[]{:S(2)}, u32[]{:S(2)}) collective-permute-start(s16[672,128]{1,0:T(8,128)(2,1)S(1)} %get-tuple-element.52), channel_id=1, source_target_pairs={{0,2},{1,3},{2,0},{3,1},{4,6},{5,7},{6,4},{7,5},{8,10},{9,11},{10,... | collective-permute-start | bytes 516104 | tf_op jit(solution)/shard_map/ppermute | solution.py:1084
  38.7 6.7 %collective-permute-start.7 = (s16[672,128]{1,0:T(8,128)(2,1)S(1)}, s16[672,128]{1,0:T(8,128)(2,1)S(1)}, u32[]{:S(2)}, u32[]{:S(2)}) collective-permute-start(s16[672,128]{1,0:T(8,128)(2,1)S(1)} %get-tuple-element.53), channel_id=1, source_target_pairs={{0,3},{1,2},{2,1},{3,0},{4,7},{5,6},{6,5},{7,4},{8,11},{9,10},{10,... | collective-permute-start | bytes 516104 | tf_op jit(solution)/shard_map/ppermute | solution.py:1084
  38.7 5.6 %collective-permute-start.8 = (s16[672,128]{1,0:T(8,128)(2,1)S(1)}, s16[672,128]{1,0:T(8,128)(2,1)S(1)}, u32[]{:S(2)}, u32[]{:S(2)}) collective-permute-start(s16[672,128]{1,0:T(8,128)(2,1)S(1)} %get-tuple-element.56), channel_id=1, source_target_pairs={{0,1},{1,0},{2,3},{3,2},{4,5},{5,4},{6,7},{7,6},{8,9},{9,8},{10,11... | collective-permute-start | bytes 516104 | tf_op jit(solution)/shard_map/ppermute | solution.py:1084
  43.4 1.0 %copy-start = (bf16[4,128,256]{2,1,0:T(8,128)(2,1)S(1)}, bf16[4,128,256]{2,1,0:T(8,128)(2,1)}, u32[]{:S(2)}) copy-start(bf16[4,128,256]{2,1,0:T(8,128)(2,1)} %constant.79.clone.refs_2_.refs_3_) | copy-start | bytes 786436
  43.4 1.0 %copy-start.1 = (bf16[4,128,256]{2,1,0:T(8,128)(2,1)S(1)}, bf16[4,128,256]{2,1,0:T(8,128)(2,1)}, u32[]{:S(2)}) copy-start(bf16[4,128,256]{2,1,0:T(8,128)(2,1)} %constant.80.clone.refs_3_.refs_4_) | copy-start | bytes 786436
  43.4 1.9 %copy-start.9 = (s32[512]{0:T(512)S(1)}, s32[512]{0:T(512)}, u32[]{:S(2)}) copy-start(s32[512]{0:T(512)} %param.17) | copy-start | bytes 6148
  51.6 2.8 %collective-permute-start.9 = (s16[672,128]{1,0:T(8,128)(2,1)S(1)}, s16[672,128]{1,0:T(8,128)(2,1)S(1)}, u32[]{:S(2)}, u32[]{:S(2)}) collective-permute-start(s16[672,128]{1,0:T(8,128)(2,1)S(1)} %get-tuple-element.61), channel_id=1, source_target_pairs={{0,1},{1,0},{2,3},{3,2},{4,5},{5,4},{6,7},{7,6},{8,9},{9,8},{10,11... | collective-permute-start | bytes 516104 | tf_op jit(solution)/shard_map/ppermute | solution.py:1084
  52.4 7.2 %collective-permute-start.10 = (s16[672,128]{1,0:T(8,128)(2,1)S(1)}, s16[672,128]{1,0:T(8,128)(2,1)S(1)}, u32[]{:S(2)}, u32[]{:S(2)}) collective-permute-start(s16[672,128]{1,0:T(8,128)(2,1)S(1)} %get-tuple-element.62), channel_id=1, source_target_pairs={{0,2},{1,3},{2,0},{3,1},{4,6},{5,7},{6,4},{7,5},{8,10},{9,11},{10,... | collective-permute-start | bytes 516104 | tf_op jit(solution)/shard_map/ppermute | solution.py:1084
  53.9 7.7 %collective-permute-start.11 = (s16[672,128]{1,0:T(8,128)(2,1)S(1)}, s16[672,128]{1,0:T(8,128)(2,1)S(1)}, u32[]{:S(2)}, u32[]{:S(2)}) collective-permute-start(s16[672,128]{1,0:T(8,128)(2,1)S(1)} %get-tuple-element.63), channel_id=1, source_target_pairs={{0,3},{1,2},{2,1},{3,0},{4,7},{5,6},{6,5},{7,4},{8,11},{9,10},{10,... | collective-permute-start | bytes 516104 | tf_op jit(solution)/shard_map/ppermute | solution.py:1084
  63.4 7.8 %collective-permute-start.12 = (s16[816,128]{1,0:T(8,128)(2,1)S(1)}, s16[816,128]{1,0:T(8,128)(2,1)S(1)}, u32[]{:S(2)}, u32[]{:S(2)}) collective-permute-start(s16[816,128]{1,0:T(8,128)(2,1)S(1)} %get-tuple-element.65), channel_id=1, source_target_pairs={{0,4},{8,12},{4,0},{12,8},{1,5},{9,13},{5,1},{13,9},{2,6},{10,14},... | collective-permute-start | bytes 626696 | tf_op jit(solution)/shard_map/ppermute | solution.py:1095
  63.7 9.5 %collective-permute-start.13 = (s16[816,128]{1,0:T(8,128)(2,1)S(1)}, s16[816,128]{1,0:T(8,128)(2,1)S(1)}, u32[]{:S(2)}, u32[]{:S(2)}) collective-permute-start(s16[816,128]{1,0:T(8,128)(2,1)S(1)} %get-tuple-element.66), channel_id=1, source_target_pairs={{4,8},{8,4},{5,9},{9,5},{6,10},{10,6},{7,11},{11,7},{20,24},{24,20... | collective-permute-start | bytes 626696 | tf_op jit(solution)/shard_map/ppermute | solution.py:1096
  71.5 6.4 %collective-permute-start.14 = (s16[272,128]{1,0:T(8,128)(2,1)S(1)}, s16[272,128]{1,0:T(8,128)(2,1)S(1)}, u32[]{:S(2)}, u32[]{:S(2)}) collective-permute-start(s16[272,128]{1,0:T(8,128)(2,1)S(1)} %pair_messages.3), channel_id=1, source_target_pairs={{0,8},{4,12},{8,0},{12,4},{1,9},{5,13},{9,1},{13,5},{2,10},{6,14},... | collective-permute-start | bytes 208904 | tf_op jit(solution)/shard_map/ppermute | solution.py:1098
  81.0 3.9 %collective-permute-start.17 = (s16[672,128]{1,0:T(8,128)(2,1)S(1)}, s16[672,128]{1,0:T(8,128)(2,1)S(1)}, u32[]{:S(2)}, u32[]{:S(2)}) collective-permute-start(s16[672,128]{1,0:T(8,128)(2,1)S(1)} %get-tuple-element.73), channel_id=1, source_target_pairs={{0,1},{1,0},{2,3},{3,2},{4,5},{5,4},{6,7},{7,6},{8,9},{9,8},{10,11... | collective-permute-start | bytes 516104 | tf_op jit(solution)/shard_map/ppermute | solution.py:1084
  81.1 7.2 %collective-permute-start.15 = (s16[672,128]{1,0:T(8,128)(2,1)S(1)}, s16[672,128]{1,0:T(8,128)(2,1)S(1)}, u32[]{:S(2)}, u32[]{:S(2)}) collective-permute-start(s16[672,128]{1,0:T(8,128)(2,1)S(1)} %get-tuple-element.69), channel_id=1, source_target_pairs={{0,2},{1,3},{2,0},{3,1},{4,6},{5,7},{6,4},{7,5},{8,10},{9,11},{10,... | collective-permute-start | bytes 516104 | tf_op jit(solution)/shard_map/ppermute | solution.py:1084
  82.6 8.5 %collective-permute-start.16 = (s16[672,128]{1,0:T(8,128)(2,1)S(1)}, s16[672,128]{1,0:T(8,128)(2,1)S(1)}, u32[]{:S(2)}, u32[]{:S(2)}) collective-permute-start(s16[672,128]{1,0:T(8,128)(2,1)S(1)} %get-tuple-element.70), channel_id=1, source_target_pairs={{0,3},{1,2},{2,1},{3,0},{4,7},{5,6},{6,5},{7,4},{8,11},{9,10},{10,... | collective-permute-start | bytes 516104 | tf_op jit(solution)/shard_map/ppermute | solution.py:1084

commit v9 on v8

--- a/solution.py
+++ b/solution.py
@@ -23,7 +23,7 @@
 VMEM_LIMIT = 24 * 1024 * 1024
 START_LIMIT = VMEM_LIMIT
 GROUP = 32
-CHAINS = 4
+CHAINS = 2
 
 
 def cas(angles):
@@ -535,8 +535,8 @@
     parts = refs[:pieces]
     early_ref, table_ref, modes_ref = refs[pieces : pieces + 3]
     refs = refs[: pieces + 3] + refs[pieces + 3 + awaited :]
-    spectrum, even_out, odd_out, own_out, peers_out, inner_out = refs[pieces + 3 : pieces + 9]
-    opened, stacked, slabs, head = refs[pieces + 9 :]
+    spectrum, even_out, layers_out, odd_out, own_out, peers_out, inner_out, *refs = refs[pieces + 3 :]
+    opened, stacked, slabs, head = refs
     half = reach_x // 2
     pair = lax.axis_size("pair")
     top = parts[0].shape[0] - opened.shape[0]
@@ -589,6 +589,7 @@
             jnp.where(low, layers[0], swap(layers[1])),
             jnp.where(low, layers[2], swap(layers[3])),
             jnp.where(low, cut_left + across_cut * swapped_left, own),
+            own,
         ]
         own_out[rows, :] = own
         for slab, values in enumerate(made):
@@ -599,30 +600,27 @@
         )
 
     zero = jnp.zeros((8, 2 * HALF), F32)
-    largest = lax.fori_loop(0, GRID // chunk, body, (zero,) * 6)
+    largest = lax.fori_loop(0, GRID // chunk, body, (zero,) * 7)
     scales = [fit_scale(jnp.max(value, axis=0, keepdims=True)) for value in largest]
     head_rows = head.shape[0]
 
-    def send(out, first):
-        for slab in range(3):
-            exponent, fraction = scales[first + slab]
-            head[2 * slab : 2 * slab + 1, :] = exponent
-            head[2 * slab + 1 : 2 * slab + 2, :] = fraction
-            at = head_rows + slab * GRID
-            out[at : at + GRID, :] = quantize(slabs[first + slab], exponent, fraction)
-        out[:head_rows, :] = to_short(head[...])
+    def send(out, top, which):
+        for place, slab in enumerate(which):
+            exponent, fraction = scales[slab]
+            head[2 * place : 2 * place + 1, :] = exponent
+            head[2 * place + 1 : 2 * place + 2, :] = fraction
+            at = top + place * GRID
+            out[at : at + GRID, :] = quantize(slabs[slab], exponent, fraction)
+        out[:top, :] = to_short(head[:top, :])
 
     on_left = lax.axis_index("wide") & 1
-
-    @pl.when(on_left == 0)
-    def _():
-        send(even_out, 0)
-        send(odd_out, 3)
-
-    @pl.when(on_left == 1)
-    def _():
-        send(even_out, 3)
-        send(odd_out, 0)
+    for side, (even, odd) in enumerate(((0, 3), (3, 0))):
+
+        @pl.when(on_left == side)
+        def _():
+            send(even_out, head_rows, (even + 2, 6))
+            send(layers_out, 16, (even, even + 1))
+            send(odd_out, head_rows, (odd + 2, odd, odd + 1))
 
 
 def forward(parts, early, table, modes, reach_x, reach_y, blocks, awaited):
@@ -636,10 +634,11 @@
             forward_kernel, reach_x, reach_y, blocks, pieces, len(awaited)
         ),
         in_specs=[whole_vmem()] * (pieces + 3) + [anywhere()] * len(awaited),
-        out_specs=[whole_vmem()] * 6,
+        out_specs=[whole_vmem()] * 7,
         out_shape=[
             jax.ShapeDtypeStruct((half, GRID, lanes), F32),
-            short(head + 3 * GRID),
+            short(head + 2 * GRID),
+            short(16 + 2 * GRID),
             short(head + 3 * GRID),
             jax.ShapeDtypeStruct((GRID, lanes), F32),
             jax.ShapeDtypeStruct((pieces * blocks, BLOCK), F32),
@@ -647,7 +646,7 @@
         ],
         scratch_shapes=stacking_scratch(pieces // table.shape[0], reach_x, reach_y)
         + [
-            pltpu.VMEM((6, GRID, lanes), F32),
+            pltpu.VMEM((7, GRID, lanes), F32),
             pltpu.VMEM((head, lanes), F32),
         ],
         compiler_params=params(),
@@ -669,14 +668,9 @@
     span = reach_x - 4
     here = lax.axis_index("wide")
     low = low_lanes(GRID)
-    decay, log_decay = modes_ref[0], modes_ref[1]
+    log_decay = modes_ref[1]
     own = own_ref[...]
-    one, two, cut = opened_slabs(even_ref, 3, even_ref.shape[0] - 3 * GRID)
-    left = ((decay * cut + swap(one)) * decay + one) * decay + swap(two)
-    left = jnp.where(low, cut, left * decay + two)
-    right = ((decay * cut + swap(two)) * decay + two) * decay + swap(one)
-    right = jnp.where(low, right * decay + one, cut)
-    partner = jnp.where((here & 1) == 1, left, right)
+    _, partner = opened_slabs(even_ref, 2, even_ref.shape[0] - 2 * GRID)
 
     def weight(distances):
         powers = []
@@ -730,21 +724,25 @@
 
 
 def inverse_kernel(reach_x, reach_y, flips, fars, *refs):
-    spectrum, from_even, from_odd, own_ref, inner_ref, *far_refs = refs[: 5 + fars]
-    refs = refs[5 + fars :]
+    spectrum, from_even, even_layers, from_odd, own_ref, inner_ref, *far_refs = refs[: 6 + fars]
+    refs = refs[6 + fars :]
     high_ref, low_ref, modes_ref = refs[:3]
     outs = refs[3 : 3 + len(flips)]
     field_high, field_low, ready, head = refs[3 + len(flips) :]
     half = reach_x // 2
     span = reach_x - 4
     chunk = 32
-    head_rows = from_even.shape[0] - 3 * GRID
+    head_rows = from_even.shape[0] - 2 * GRID
     on_left = (lax.axis_index("wide") & 1) == 1
-    both_heads = from_short(from_even[:16, :]), from_short(from_odd[:16, :])
-    both_units = [
-        [unit(first[2 * slab : 2 * slab + 1], first[2 * slab + 1 : 2 * slab + 2]) for slab in range(3)]
-        for first in both_heads
-    ]
+    even_places = (from_even, head_rows, 0), (even_layers, 16, 0), (even_layers, 16, 1)
+    odd_places = tuple((from_odd, head_rows, place) for place in range(3))
+
+    def slab_unit(place):
+        ref, _, at = place
+        first = from_short(ref[:16, :])
+        return unit(first[2 * at : 2 * at + 1], first[2 * at + 1 : 2 * at + 2])
+
+    both_units = [[slab_unit(place) for place in places] for places in (even_places, odd_places)]
 
     def sided(even, odd):
         return jnp.where(on_left, even, odd), jnp.where(on_left, odd, even)
@@ -769,12 +767,15 @@
         layers = [spectrum[i, rows, :] for i in range(half)]
 
         def slab(which):
-            at = pl.ds(pl.multiple_of(head_rows + which * GRID + index * chunk, chunk), chunk)
-            even = from_short(from_even[at, :]) * both_units[0][which]
-            return sided(even, from_short(from_odd[at, :]) * both_units[1][which])
-
-        head_layers, tail_layers = zip(slab(0), slab(1))
-        left_moments, right_moments = slab(2)
+            found = []
+            for places, units in zip((even_places, odd_places), both_units):
+                ref, top, place = places[which]
+                at = pl.multiple_of(top + place * GRID + index * chunk, 16)
+                found.append(from_short(ref[pl.ds(at, chunk), :]) * units[which])
+            return sided(*found)
+
+        left_moments, right_moments = slab(0)
+        head_layers, tail_layers = zip(slab(1), slab(2))
         zero = jnp.zeros_like(decay)
         from_head = [head_layers[0], swap(head_layers[0]), head_layers[1], swap(head_layers[1])]
         from_tail = [swap(tail_layers[0]), tail_layers[0], swap(tail_layers[1]), tail_layers[1]]
@@ -818,7 +819,18 @@
 
 
 def inverse(
-    spectrum, from_even, from_odd, own, inner, fars, table, modes, reach_x, reach_y, flips
+    spectrum,
+    from_even,
+    even_layers,
+    from_odd,
+    own,
+    inner,
+    fars,
+    table,
+    modes,
+    reach_x,
+    reach_y,
+    flips,
 ):
     half = reach_x // 2
     lanes = 2 * HALF
@@ -827,7 +839,7 @@
     shapes += [jax.ShapeDtypeStruct((half, GRID, lanes), BF16)] * 2
     return pl.pallas_call(
         functools.partial(inverse_kernel, reach_x, reach_y, flips, len(fars)),
-        in_specs=[whole_vmem()] * (8 + len(fars)),
+        in_specs=[whole_vmem()] * (9 + len(fars)),
         out_specs=[whole_vmem()] * len(shapes),
         out_shape=shapes,
         scratch_shapes=[
@@ -837,7 +849,7 @@
         compiler_params=params(),
         cost_estimate=cost(2 * half * 256 * 256 * 128, 4 * half * GRID * lanes * 2),
         name="inverse",
-    )(spectrum, from_even, from_odd, own, inner, *fars, *table, modes)
+    )(spectrum, from_even, even_layers, from_odd, own, inner, *fars, *table, modes)
 
 
 def inverse_rest_kernel(reach_y, flips, field_high, field_low, high_ref, low_ref, *refs):
@@ -1018,7 +1030,7 @@
 
 def near_field(places, targets, from_even, from_odd, peers, tiles, blocks, out_rows):
     slots = tiles.shape[0]
-    head = from_even.shape[0] - 3 * GRID
+    head = from_even.shape[0] - 2 * GRID
     constant = lambda shape: pl.BlockSpec(shape, lambda i: (0,) * len(shape))
     return pl.pallas_call(
         functools.partial(near_kernel, slots, blocks),
@@ -1089,11 +1101,12 @@
         arrived = flipped(sent, moving)
         arrived = list(spread_rest(vector, both, z_forward, local)) + arrived
         early = forward_early(arrived[:pair], y_forward, reach_x, reach_y)
-        spectrum, even_message, odd_message, own, peers, inner = forward(
+        spectrum, even_message, layers, odd_message, own, peers, inner = forward(
             arrived, early, y_forward, modes, reach_x, reach_y, blocks, awaited
         )
         from_even = lax.ppermute(even_message, "wide", even_swap)
         from_odd = lax.ppermute(odd_message, "wide", odd_swap)
+        even_layers = lax.ppermute(layers, "wide", even_swap)
         fars = [
             lax.ppermute(message, "wide", [(i, i ^ flip) for i in range(x_count)])
             for flip, message in zip(
@@ -1106,6 +1119,7 @@
         *sent, high, low = inverse(
             spectrum,
             from_even,
+            even_layers,
             from_odd,
             own,
             inner,

time: 94.9 us -> 94.5 us (level)
  starting transfers between devices: 17.5 us -> 25.2 us
  waiting for transfers between devices: 36.3 us -> 28.6 us
    ppermute x2, waiting for transfers between devices: 11.7 us -> 0.8 us  [convolve_and_sample(): from_even = lax.ppermute(even_message, 'wide', even_swap)]
    ppermute x0 -> x2, starting transfers between devices: none -> 9.15 us  [convolve_and_sample(): even_layers = lax.ppermute(layers, 'wide', even_swap)]
    ppermute x0 -> x2, waiting for transfers between devices: none -> 3.25 us  [convolve_and_sample(): even_layers = lax.ppermute(layers, 'wide', even_swap)]
    ppermute x2, starting transfers between devices: 4.44 us -> 3.06 us  [convolve_and_sample(): lax.ppermute(message, 'wide', [(i, i ^ flip) for i in range(x_count)])]
  transfers between devices with their start and end apart: 18 -> 20, of which waited for: 10 -> 11; matrix products, arithmetic and copies ran while one was open for 1% -> 1% of each run, Pallas kernels for 14% -> 14%
where the time goes in v9:
time: 94.5 us; the launch traced here: 94.2 us
  Pallas kernels  38.8 us (41%)
  waiting for transfers between devices  28.6 us (30%)
  starting transfers between devices  25.2 us (27%)
  local copies, waits for them, and re-layouts  1.28 us (1%)
    ppermute x12, waiting for transfers between devices, flipped(): lax.ppermute(part, Y_AXES, [(i, i ^ flip) for i in range(y_count)])  16 us
    ppermute x12, starting transfers between devices, flipped(): lax.ppermute(part, Y_AXES, [(i, i ^ flip) for i in range(y_count)])  9.67 us
    pallas_call x2, Pallas kernels, spread(): pl.pallas_call(functools.partial(start_kernel if placed is None else spre...  9.17 us
    ppermute x2, starting transfers between devices, convolve_and_sample(): even_layers = lax.ppermute(layers, 'wide', even_swap)  9.15 us
    ppermute x2, waiting for transfers between devices, convolve_and_sample(): lax.ppermute(message, 'wide', [(i, i ^ flip) for i in range(x_count)])  8.53 us
    pallas_call x2, Pallas kernels, sample(): pl.pallas_call(functools.partial(sample_kernel, last, reach_x, reach_y, f...  6.49 us
    pallas_call x2, Pallas kernels, inverse(): pl.pallas_call(functools.partial(inverse_kernel, reach_x, reach_y, flips,...  6.18 us
    pallas_call x2, Pallas kernels, place_lines(): pl.pallas_call(lines_kernel, in_specs=[in_smem(), whole_vmem()] + [anywhe...  5.9 us
  transfers between devices with their start and end apart: 20, of which 11 were waited for; matrix products, arithmetic and copies ran while one was open for 1% of the time, Pallas kernels for 14%

profile of v9, /device:TPU:0, one launch (start us, length us, event | category | flops | bytes accessed | tf_op | source)
XLA Modules:
  0.0 94.2 jit_solution(9660296608930203349)
XLA Ops:
  0.0 6.1 %start.1 = (s16[672,128]{1,0:T(8,128)(2,1)S(1)}, s16[672,128]{1,0:T(8,128)(2,1)S(1)}, s16[672,128]{1,0:T(8,128)(2,1)S(1)}, bf16[656,256]{1,0:T(8,128)(2,1)S(1)},...) custom-call(f32[512]{0:T(512)} %refs_0_.1, ...), custom_call_target="tpu_custom_call" | custom-call | flops 169869312 | bytes 4194304 | tf_op jit(solution)/shard_map/start/pallas_call | solution.py:398
  6.1 0.0 copy-start.2
  6.1 0.0 copy-start.3
  6.1 0.0 copy-start.8
  6.1 0.5 collective-permute-start
  6.6 2.6 %collective-permute-start.1 = (s16[672,128]{1,0:T(8,128)(2,1)S(1)}, s16[672,128]{1,0:T(8,128)(2,1)S(1)}, u32[]{:S(2)}, u32[]{:S(2)}) collective-permute-start(s16[672,128]{1,0:T(8,128)(2,1)S(1)} %get-tuple-element.46), channel_id=1, source_target_pairs={{0,2},{1,3},{2,0},{3,1},{4,6},{5,7},{6,4},{7,5},{8,10},{9,11},{10,... | collective-permute-start | bytes 516104 | tf_op jit(solution)/shard_map/ppermute | solution.py:1096
  9.2 0.1 collective-permute-start.2
  9.3 2.9 %place_lines.2.refs_7_.refs_5_ = f32[8192,128]{1,0:T(8,128)S(1)} custom-call(s32[2,512]{1,0:T(2,128)S(1)} %get-tuple-element.42.place_ref.refs_1_, f32[256,128]{1,0:T(8,128)S(1)} %get-tuple-element.48.coeff_ref), custom_call_target="tpu_custom_call" | custom-call | flops 1048576 | bytes 4194304 | tf_op jit(solution)/shard_map/place_lines/pallas_call | solution.py:459
  12.2 0.5 spread_rest.2.refs_0_
  12.8 1.1 %dynamic-slice_bitcast_fusion.refs_6_.modes_ref.refs_9_ = f32[4,256,128]{2,1,0:T(8,128)S(1)} fusion(f32[4,4,256,128]{3,2,1,0:T(8,128)} %constant.73.clone, s32[]{:T(128)S(6)} %select_n.30), kind=kLoop, calls=%fused_computation | loop fusion | bytes 1048580 | tf_op jit(solution)/shard_map/jit(dynamic_index_in_dim)/squeeze | solution.py:1077
  13.8 0.0 collective-permute-done.refs_1_
  13.9 0.6 forward_early.2.refs_4_
  14.5 0.0 copy-start.6
  14.5 0.0 copy-start.7
  14.5 0.0 collective-permute-done.1.refs_2_
  14.6 3.0 %collective-permute-done.2.refs_3_ = s16[672,128]{1,0:T(8,128)(2,1)S(1)} collective-permute-done((s16[672,128]{1,0:T(8,128)(2,1)S(1)}, s16[672,128]{1,0:T(8,128)(2,1)S(1)}, u32[]{:S(2)}, u32[]{:S(2)}) %collective-permute-start.2) | collective-permute-done | bytes 172064 | tf_op jit(solution)/shard_map/ppermute | solution.py:1096
  17.6 1.9 %forward.2 = (f32[18,256,128]{2,1,0:T(8,128)S(1)}, s16[560,128]{1,0:T(8,128)(2,1)S(1)}, s16[528,128]{1,0:T(8,128)(2,1)S(1)}, s16[816,128]{1,0:T(8,128)(2,1)S(1)}...) custom-call(s16[672,128]{1,0:T(8,128)(2,1)S(1)} %spread_rest.2.refs_0_, ...), custom_call_target="tpu_custom_call" | custom-call | flops 301989888 | bytes 4718592 | tf_op jit(solution)/shard_map/forward/pallas_call | solution.py:632
  19.5 1.7 %collective-permute-start.3 = (s16[560,128]{1,0:T(8,128)(2,1)S(1)}, s16[560,128]{1,0:T(8,128)(2,1)S(1)}, u32[]{:S(2)}, u32[]{:S(2)}) collective-permute-start(s16[560,128]{1,0:T(8,128)(2,1)S(1)} %get-tuple-element.50), channel_id=1, source_target_pairs={{0,4},{8,12},{4,0},{12,8},{1,5},{9,13},{5,1},{13,9},{2,6},{10,14},... | collective-permute-start | bytes 430088 | tf_op jit(solution)/shard_map/ppermute | solution.py:1107
  21.2 0.7 collective-permute-start.5
  21.8 4.5 %collective-permute-start.4 = (s16[528,128]{1,0:T(8,128)(2,1)S(1)}, s16[528,128]{1,0:T(8,128)(2,1)S(1)}, u32[]{:S(2)}, u32[]{:S(2)}) collective-permute-start(s16[528,128]{1,0:T(8,128)(2,1)S(1)} %get-tuple-element.51), channel_id=1, source_target_pairs={{0,4},{8,12},{4,0},{12,8},{1,5},{9,13},{5,1},{13,9},{2,6},{10,14},... | collective-permute-start | bytes 405512 | tf_op jit(solution)/shard_map/ppermute | solution.py:1109
  26.3 0.0 collective-permute-done.3.even_ref.refs_1_.refs_0_
  26.3 0.1 pair_messages.2
  26.4 1.9 %collective-permute-start.6 = (s16[272,128]{1,0:T(8,128)(2,1)S(1)}, s16[272,128]{1,0:T(8,128)(2,1)S(1)}, u32[]{:S(2)}, u32[]{:S(2)}) collective-permute-start(s16[272,128]{1,0:T(8,128)(2,1)S(1)} %pair_messages.2), channel_id=1, source_target_pairs={{0,8},{4,12},{8,0},{12,4},{1,9},{5,13},{9,1},{13,5},{2,10},{6,14},... | collective-permute-start | bytes 208904 | tf_op jit(solution)/shard_map/ppermute | solution.py:1111
  28.4 1.4 %collective-permute-done.4.refs_2_ = s16[528,128]{1,0:T(8,128)(2,1)S(1)} collective-permute-done((s16[528,128]{1,0:T(8,128)(2,1)S(1)}, s16[528,128]{1,0:T(8,128)(2,1)S(1)}, u32[]{:S(2)}, u32[]{:S(2)}) %collective-permute-start.4) | collective-permute-done | bytes 135200 | tf_op jit(solution)/shard_map/ppermute | solution.py:1109
  29.8 4.2 %collective-permute-done.6.refs_6_ = s16[272,128]{1,0:T(8,128)(2,1)S(1)} collective-permute-done((s16[272,128]{1,0:T(8,128)(2,1)S(1)}, s16[272,128]{1,0:T(8,128)(2,1)S(1)}, u32[]{:S(2)}, u32[]{:S(2)}) %collective-permute-start.6) | collective-permute-done | bytes 69664 | tf_op jit(solution)/shard_map/ppermute | solution.py:1111
  34.0 3.1 %inverse.2 = (s16[672,128]{1,0:T(8,128)(2,1)S(1)}, s16[672,128]{1,0:T(8,128)(2,1)S(1)}, s16[672,128]{1,0:T(8,128)(2,1)S(1)}, bf16[18,256,128]{2,1,0:T(8,128)(2,1)S(1)}, bf16[18,256,128]{2,1,0:T(8,128)(2,1)S(1)}) custom-call(f32[18,256,128]{2,1,0:T(8,128)S(1)} %get-tuple-element.49.refs_0_, ...), custom_call_target="tpu_custom_call" | custom-call | flops 301989888 | bytes 4718592 | tf_op jit(solution)/shard_map/inverse/pallas_call | solution.py:840
  37.1 1.6 %collective-permute-start.7 = (s16[672,128]{1,0:T(8,128)(2,1)S(1)}, s16[672,128]{1,0:T(8,128)(2,1)S(1)}, u32[]{:S(2)}, u32[]{:S(2)}) collective-permute-start(s16[672,128]{1,0:T(8,128)(2,1)S(1)} %get-tuple-element.55), channel_id=1, source_target_pairs={{0,2},{1,3},{2,0},{3,1},{4,6},{5,7},{6,4},{7,5},{8,10},{9,11},{10,... | collective-permute-start | bytes 516104 | tf_op jit(solution)/shard_map/ppermute | solution.py:1096
  38.6 0.7 collective-permute-start.9
  39.3 1.1 %near_field.2.refs_8_.refs_0_ = f32[8,128]{1,0:T(8,128)S(1)} custom-call(s32[24]{0:T(128)S(1)} %get-tuple-element.80.place_ref, s32[24]{0:T(128)S(1)} %get-tuple-element.79.target_ref, s16[560,128]{1,0:T(8,128)(2,1)S(1)} %collective-permute-done.3.even_ref.refs_1_.refs_0_, s16[816,128]{1,0:T(8,128)(2,1)S(1)} %collective-permute-done.5.refs_3_.refs_1_, ...), custom_call_target="tpu_custom_call" | custom-call | flops 12582912 | bytes 786432 | tf_op jit(solution)/shard_map/near_field/pallas_call | solution.py:1035
  40.4 3.0 %place_lines.3.refs_5_ = f32[8192,128]{1,0:T(8,128)S(1)} custom-call(s32[2,512]{1,0:T(2,128)S(1)} %get-tuple-element.42.place_ref.refs_1_, f32[256,128]{1,0:T(8,128)S(1)} %get-tuple-element.61.coeff_ref, f32[8,128]{1,0:T(8,128)S(1)} %near_field.2.refs_8_.refs_0_), custom_call_target="tpu_custom_call" | custom-call | flops 1048576 | bytes 4194304 | tf_op jit(solution)/shard_map/place_lines/pallas_call | solution.py:459
  43.3 0.0 copy-start.1
  43.4 0.0 copy-start.9
  43.4 0.8 inverse_rest.2.refs_0_
  44.2 0.1 copy-done
  44.3 0.1 copy-done.1
  44.4 0.4 sample_early.2.refs_2_
  44.8 0.7 collective-permute-done.8.refs_1_
  45.6 2.9 %sample.2.refs_2_.rounded_ref.refs_7_ = f32[4,128]{1,0:T(4,128)S(1)} custom-call(s32[2,512]{1,0:T(2,128)S(1)} %get-tuple-element.42.place_ref.refs_1_, s16[672,128]{1,0:T(8,128)(2,1)S(1)} %collective-permute-done.7.refs_0_, s16[672,128]{1,0:T(8,128)(2,1)S(1)} %collective-permute-done.8.refs_1_, f32[656,256]{1,0:T(8,128)S(1)} %sample_early.2.refs_2_, ...), custom_call_target="tpu_custom_call" | custom-call | flops 169869312 | bytes 4194304 | tf_op jit(solution)/shard_map/sample/pallas_call | solution.py:980
  48.5 3.1 %spread.1 = (s16[672,128]{1,0:T(8,128)(2,1)S(1)}, s16[672,128]{1,0:T(8,128)(2,1)S(1)}, s16[672,128]{1,0:T(8,128)(2,1)S(1)}, bf16[656,256]{1,0:T(8,128)(2,1)S(1)}, bf16[656,256]{1,0:T(8,128)(2,1)S(1)}) custom-call(f32[512]{0:T(512)S(1)} %bitcast.6, s32[2,512]{1,0:T(2,128)S(1)} %get-tuple-element.42.place_ref.refs_1_, ...), custom_call_target="tpu_custom_call" | custom-call | flops 169869312 | bytes 4194304 | tf_op jit(solution)/shard_map/spread/pallas_call | solution.py:398
  51.6 0.9 collective-permute-start.10
  52.5 1.5 %collective-permute-start.11 = (s16[672,128]{1,0:T(8,128)(2,1)S(1)}, s16[672,128]{1,0:T(8,128)(2,1)S(1)}, u32[]{:S(2)}, u32[]{:S(2)}) collective-permute-start(s16[672,128]{1,0:T(8,128)(2,1)S(1)} %get-tuple-element.65), channel_id=1, source_target_pairs={{0,2},{1,3},{2,0},{3,1},{4,6},{5,7},{6,4},{7,5},{8,10},{9,11},{10,... | collective-permute-start | bytes 516104 | tf_op jit(solution)/shard_map/ppermute | solution.py:1096
  54.0 0.5 spread_rest.3.refs_0_
  54.5 0.7 forward_early.3.refs_4_
  55.2 4.5 %collective-permute-done.11.refs_2_ = s16[672,128]{1,0:T(8,128)(2,1)S(1)} collective-permute-done((s16[672,128]{1,0:T(8,128)(2,1)S(1)}, s16[672,128]{1,0:T(8,128)(2,1)S(1)}, u32[]{:S(2)}, u32[]{:S(2)}) %collective-permute-start.11) | collective-permute-done | bytes 172064 | tf_op jit(solution)/shard_map/ppermute | solution.py:1096
  59.7 1.9 %collective-permute-done.12.refs_3_ = s16[672,128]{1,0:T(8,128)(2,1)S(1)} collective-permute-done((s16[672,128]{1,0:T(8,128)(2,1)S(1)}, s16[672,128]{1,0:T(8,128)(2,1)S(1)}, u32[]{:S(2)}, u32[]{:S(2)}) %collective-permute-start.12) | collective-permute-done | bytes 172064 | tf_op jit(solution)/shard_map/ppermute | solution.py:1096
  61.7 1.9 %forward.3 = (f32[18,256,128]{2,1,0:T(8,128)S(1)}, s16[560,128]{1,0:T(8,128)(2,1)S(1)}, s16[528,128]{1,0:T(8,128)(2,1)S(1)}, s16[816,128]{1,0:T(8,128)(2,1)S(1)}...) custom-call(s16[672,128]{1,0:T(8,128)(2,1)S(1)} %spread_rest.3.refs_0_, ...), custom_call_target="tpu_custom_call" | custom-call | flops 301989888 | bytes 4718592 | tf_op jit(solution)/shard_map/forward/pallas_call | solution.py:632
  63.6 0.1 collective-permute-start.13
  63.6 0.9 collective-permute-start.15
  64.5 4.7 %collective-permute-start.14 = (s16[528,128]{1,0:T(8,128)(2,1)S(1)}, s16[528,128]{1,0:T(8,128)(2,1)S(1)}, u32[]{:S(2)}, u32[]{:S(2)}) collective-permute-start(s16[528,128]{1,0:T(8,128)(2,1)S(1)} %get-tuple-element.69), channel_id=1, source_target_pairs={{0,4},{8,12},{4,0},{12,8},{1,5},{9,13},{5,1},{13,9},{2,6},{10,14},... | collective-permute-start | bytes 405512 | tf_op jit(solution)/shard_map/ppermute | solution.py:1109
  69.2 0.8 collective-permute-done.13.even_ref.refs_1_.refs_0_
  70.0 0.1 pair_messages.3
  70.1 1.2 %collective-permute-start.16 = (s16[272,128]{1,0:T(8,128)(2,1)S(1)}, s16[272,128]{1,0:T(8,128)(2,1)S(1)}, u32[]{:S(2)}, u32[]{:S(2)}) collective-permute-start(s16[272,128]{1,0:T(8,128)(2,1)S(1)} %pair_messages.3), channel_id=1, source_target_pairs={{0,8},{4,12},{8,0},{12,4},{1,9},{5,13},{9,1},{13,5},{2,10},{6,14},... | collective-permute-start | bytes 208904 | tf_op jit(solution)/shard_map/ppermute | solution.py:1111
  71.3 1.8 %collective-permute-done.14.refs_2_ = s16[528,128]{1,0:T(8,128)(2,1)S(1)} collective-permute-done((s16[528,128]{1,0:T(8,128)(2,1)S(1)}, s16[528,128]{1,0:T(8,128)(2,1)S(1)}, u32[]{:S(2)}, u32[]{:S(2)}) %collective-permute-start.14) | collective-permute-done | bytes 135200 | tf_op jit(solution)/shard_map/ppermute | solution.py:1109
  73.1 4.3 %collective-permute-done.16.refs_6_ = s16[272,128]{1,0:T(8,128)(2,1)S(1)} collective-permute-done((s16[272,128]{1,0:T(8,128)(2,1)S(1)}, s16[272,128]{1,0:T(8,128)(2,1)S(1)}, u32[]{:S(2)}, u32[]{:S(2)}) %collective-permute-start.16) | collective-permute-done | bytes 69664 | tf_op jit(solution)/shard_map/ppermute | solution.py:1111
  77.5 3.1 %inverse.3 = (s16[672,128]{1,0:T(8,128)(2,1)S(1)}, s16[672,128]{1,0:T(8,128)(2,1)S(1)}, s16[672,128]{1,0:T(8,128)(2,1)S(1)}, bf16[18,256,128]{2,1,0:T(8,128)(2,1)S(1)}, bf16[18,256,128]{2,1,0:T(8,128)(2,1)S(1)}) custom-call(f32[18,256,128]{2,1,0:T(8,128)S(1)} %get-tuple-element.67.refs_0_, ...), custom_call_target="tpu_custom_call" | custom-call | flops 301989888 | bytes 4718592 | tf_op jit(solution)/shard_map/inverse/pallas_call | solution.py:840
  80.5 0.1 collective-permute-start.19
  80.6 1.6 %collective-permute-start.17 = (s16[672,128]{1,0:T(8,128)(2,1)S(1)}, s16[672,128]{1,0:T(8,128)(2,1)S(1)}, u32[]{:S(2)}, u32[]{:S(2)}) collective-permute-start(s16[672,128]{1,0:T(8,128)(2,1)S(1)} %get-tuple-element.73), channel_id=1, source_target_pairs={{0,2},{1,3},{2,0},{3,1},{4,6},{5,7},{6,4},{7,5},{8,10},{9,11},{10,... | collective-permute-start | bytes 516104 | tf_op jit(solution)/shard_map/ppermute | solution.py:1096
  82.2 0.3 collective-permute-start.18
  82.5 1.1 %near_field.3.refs_8_ = f32[8,128]{1,0:T(8,128)S(1)} custom-call(s32[24]{0:T(128)S(1)} %get-tuple-element.80.place_ref, s32[24]{0:T(128)S(1)} %get-tuple-element.79.target_ref, s16[560,128]{1,0:T(8,128)(2,1)S(1)} %collective-permute-done.13.even_ref.refs_1_.refs_0_, s16[816,128]{1,0:T(8,128)(2,1)S(1)} %collective-permute-done.15.refs_3_.refs_1_, ...), custom_call_target="tpu_custom_call" | custom-call | flops 12582912 | bytes 786432 | tf_op jit(solution)/shard_map/near_field/pallas_call | solution.py:1035
  83.5 0.9 inverse_rest.3.refs_0_
  84.4 0.4 sample_early.3.refs_2_
  84.9 3.0 %collective-permute-done.17.refs_0_ = s16[672,128]{1,0:T(8,128)(2,1)S(1)} collective-permute-done((s16[672,128]{1,0:T(8,128)(2,1)S(1)}, s16[672,128]{1,0:T(8,128)(2,1)S(1)}, u32[]{:S(2)}, u32[]{:S(2)}) %collective-permute-start.17) | collective-permute-done | bytes 172064 | tf_op jit(solution)/shard_map/ppermute | solution.py:1096
  87.9 2.8 %collective-permute-done.18.refs_1_ = s16[672,128]{1,0:T(8,128)(2,1)S(1)} collective-permute-done((s16[672,128]{1,0:T(8,128)(2,1)S(1)}, s16[672,128]{1,0:T(8,128)(2,1)S(1)}, u32[]{:S(2)}, u32[]{:S(2)}) %collective-permute-start.18) | collective-permute-done | bytes 172064 | tf_op jit(solution)/shard_map/ppermute | solution.py:1096
  90.7 3.6 %sample.3 = f32[2,512]{1,0:T(2,128)} custom-call(s32[2,512]{1,0:T(2,128)S(1)} %get-tuple-element.42.place_ref.refs_1_, s16[672,128]{1,0:T(8,128)(2,1)S(1)} %collective-permute-done.17.refs_0_, s16[672,128]{1,0:T(8,128)(2,1)S(1)} %collective-permute-done.18.refs_1_, f32[656,256]{1,0:T(8,128)S(1)} %sample_early.3.refs_2_, bf16[4,128,256]{2,1,0:T(8,128)(2,1)S(1)} %copy-done, ...), custom_call_target="tpu_custom_call" | custom-call | flops 169869312 | bytes 4194304 | tf_op jit(solution)/shard_map/sample/pallas_call | solution.py:980
  (24 shorter events, 0.1 us)
Async XLA Ops:
  6.1 6.1 %copy-start.2 = (bf16[4,256,128]{2,1,0:T(8,128)(2,1)S(1)}, bf16[4,256,128]{2,1,0:T(8,128)(2,1)}, u32[]{:S(2)}) copy-start(bf16[4,256,128]{2,1,0:T(8,128)(2,1)} %constant.74.clone.refs_2_.high_ref.refs_3_) | copy-start | bytes 786436
  6.1 6.1 %copy-start.3 = (bf16[4,256,128]{2,1,0:T(8,128)(2,1)S(1)}, bf16[4,256,128]{2,1,0:T(8,128)(2,1)}, u32[]{:S(2)}) copy-start(bf16[4,256,128]{2,1,0:T(8,128)(2,1)} %constant.75.clone.refs_3_.low_ref.refs_4_) | copy-start | bytes 786436
  6.1 6.1 %copy-start.8 = (f32[512]{0:T(512)S(1)}, f32[512]{0:T(512)}, u32[]{:S(2)}) copy-start(f32[512]{0:T(512)} %refs_0_.1) | copy-start | bytes 6148
  6.1 7.7 %collective-permute-start = (s16[672,128]{1,0:T(8,128)(2,1)S(1)}, s16[672,128]{1,0:T(8,128)(2,1)S(1)}, u32[]{:S(2)}, u32[]{:S(2)}) collective-permute-start(s16[672,128]{1,0:T(8,128)(2,1)S(1)} %get-tuple-element.45), channel_id=1, source_target_pairs={{0,1},{1,0},{2,3},{3,2},{4,5},{5,4},{6,7},{7,6},{8,9},{9,8},{10,11... | collective-permute-start | bytes 516104 | tf_op jit(solution)/shard_map/ppermute | solution.py:1096
  6.6 7.9 %collective-permute-start.1 = (s16[672,128]{1,0:T(8,128)(2,1)S(1)}, s16[672,128]{1,0:T(8,128)(2,1)S(1)}, u32[]{:S(2)}, u32[]{:S(2)}) collective-permute-start(s16[672,128]{1,0:T(8,128)(2,1)S(1)} %get-tuple-element.46), channel_id=1, source_target_pairs={{0,2},{1,3},{2,0},{3,1},{4,6},{5,7},{6,4},{7,5},{8,10},{9,11},{10,... | collective-permute-start | bytes 516104 | tf_op jit(solution)/shard_map/ppermute | solution.py:1096
  9.2 8.4 %collective-permute-start.2 = (s16[672,128]{1,0:T(8,128)(2,1)S(1)}, s16[672,128]{1,0:T(8,128)(2,1)S(1)}, u32[]{:S(2)}, u32[]{:S(2)}) collective-permute-start(s16[672,128]{1,0:T(8,128)(2,1)S(1)} %get-tuple-element.47), channel_id=1, source_target_pairs={{0,3},{1,2},{2,1},{3,0},{4,7},{5,6},{6,5},{7,4},{8,11},{9,10},{10,... | collective-permute-start | bytes 516104 | tf_op jit(solution)/shard_map/ppermute | solution.py:1096
  9.3 4.6 %copy-start.4 = (bf16[2,256,240]{2,1,0:T(8,128)(2,1)S(1)}, bf16[2,256,240]{2,1,0:T(8,128)(2,1)}, u32[]{:S(2)}) copy-start(bf16[2,256,240]{2,1,0:T(8,128)(2,1)} %constant.76.clone.refs_2_.refs_5_) | copy-start | bytes 737284
  14.5 19.4 %copy-start.6 = (bf16[4,48,256]{2,1,0:T(8,128)(2,1)S(1)}, bf16[4,48,256]{2,1,0:T(8,128)(2,1)}, u32[]{:S(2)}) copy-start(bf16[4,48,256]{2,1,0:T(8,128)(2,1)} %constant.77.clone.refs_7_.high_ref) | copy-start | bytes 294916
  14.5 19.4 %copy-start.7 = (bf16[4,48,256]{2,1,0:T(8,128)(2,1)S(1)}, bf16[4,48,256]{2,1,0:T(8,128)(2,1)}, u32[]{:S(2)}) copy-start(bf16[4,48,256]{2,1,0:T(8,128)(2,1)} %constant.78.clone.refs_8_.low_ref) | copy-start | bytes 294916
  19.5 6.8 %collective-permute-start.3 = (s16[560,128]{1,0:T(8,128)(2,1)S(1)}, s16[560,128]{1,0:T(8,128)(2,1)S(1)}, u32[]{:S(2)}, u32[]{:S(2)}) collective-permute-start(s16[560,128]{1,0:T(8,128)(2,1)S(1)} %get-tuple-element.50), channel_id=1, source_target_pairs={{0,4},{8,12},{4,0},{12,8},{1,5},{9,13},{5,1},{13,9},{2,6},{10,14},... | collective-permute-start | bytes 430088 | tf_op jit(solution)/shard_map/ppermute | solution.py:1107
  21.2 8.6 %collective-permute-start.5 = (s16[816,128]{1,0:T(8,128)(2,1)S(1)}, s16[816,128]{1,0:T(8,128)(2,1)S(1)}, u32[]{:S(2)}, u32[]{:S(2)}) collective-permute-start(s16[816,128]{1,0:T(8,128)(2,1)S(1)} %get-tuple-element.52), channel_id=1, source_target_pairs={{4,8},{8,4},{5,9},{9,5},{6,10},{10,6},{7,11},{11,7},{20,24},{24,20... | collective-permute-start | bytes 626696 | tf_op jit(solution)/shard_map/ppermute | solution.py:1108
  21.8 7.9 %collective-permute-start.4 = (s16[528,128]{1,0:T(8,128)(2,1)S(1)}, s16[528,128]{1,0:T(8,128)(2,1)S(1)}, u32[]{:S(2)}, u32[]{:S(2)}) collective-permute-start(s16[528,128]{1,0:T(8,128)(2,1)S(1)} %get-tuple-element.51), channel_id=1, source_target_pairs={{0,4},{8,12},{4,0},{12,8},{1,5},{9,13},{5,1},{13,9},{2,6},{10,14},... | collective-permute-start | bytes 405512 | tf_op jit(solution)/shard_map/ppermute | solution.py:1109
  26.3 13.0 %copy-start.10 = (s32[24]{0:T(128)S(1)}, s32[24]{0:T(128)}, u32[]{:S(2)}) copy-start(s32[24]{0:T(128)} %param.21) | copy-start | bytes 292
  26.3 13.0 %copy-start.11 = (s32[24]{0:T(128)S(1)}, s32[24]{0:T(128)}, u32[]{:S(2)}) copy-start(s32[24]{0:T(128)} %param.22) | copy-start | bytes 292
  26.3 13.0 %copy-start.5 = (bf16[24,128,128]{2,1,0:T(8,128)(2,1)S(1)}, bf16[24,128,128]{2,1,0:T(8,128)(2,1)}, u32[]{:S(2)}) copy-start(bf16[24,128,128]{2,1,0:T(8,128)(2,1)} %refs_3_.9) | copy-start | bytes 2359300
  26.4 7.5 %collective-permute-start.6 = (s16[272,128]{1,0:T(8,128)(2,1)S(1)}, s16[272,128]{1,0:T(8,128)(2,1)S(1)}, u32[]{:S(2)}, u32[]{:S(2)}) collective-permute-start(s16[272,128]{1,0:T(8,128)(2,1)S(1)} %pair_messages.2), channel_id=1, source_target_pairs={{0,8},{4,12},{8,0},{12,4},{1,9},{5,13},{9,1},{13,5},{2,10},{6,14},... | collective-permute-start | bytes 208904 | tf_op jit(solution)/shard_map/ppermute | solution.py:1111
  37.1 7.8 %collective-permute-start.7 = (s16[672,128]{1,0:T(8,128)(2,1)S(1)}, s16[672,128]{1,0:T(8,128)(2,1)S(1)}, u32[]{:S(2)}, u32[]{:S(2)}) collective-permute-start(s16[672,128]{1,0:T(8,128)(2,1)S(1)} %get-tuple-element.55), channel_id=1, source_target_pairs={{0,2},{1,3},{2,0},{3,1},{4,6},{5,7},{6,4},{7,5},{8,10},{9,11},{10,... | collective-permute-start | bytes 516104 | tf_op jit(solution)/shard_map/ppermute | solution.py:1096
  38.6 6.9 %collective-permute-start.8 = (s16[672,128]{1,0:T(8,128)(2,1)S(1)}, s16[672,128]{1,0:T(8,128)(2,1)S(1)}, u32[]{:S(2)}, u32[]{:S(2)}) collective-permute-start(s16[672,128]{1,0:T(8,128)(2,1)S(1)} %get-tuple-element.56), channel_id=1, source_target_pairs={{0,3},{1,2},{2,1},{3,0},{4,7},{5,6},{6,5},{7,4},{8,11},{9,10},{10,... | collective-permute-start | bytes 516104 | tf_op jit(solution)/shard_map/ppermute | solution.py:1096
  38.6 5.6 %collective-permute-start.9 = (s16[672,128]{1,0:T(8,128)(2,1)S(1)}, s16[672,128]{1,0:T(8,128)(2,1)S(1)}, u32[]{:S(2)}, u32[]{:S(2)}) collective-permute-start(s16[672,128]{1,0:T(8,128)(2,1)S(1)} %get-tuple-element.59), channel_id=1, source_target_pairs={{0,1},{1,0},{2,3},{3,2},{4,5},{5,4},{6,7},{7,6},{8,9},{9,8},{10,11... | collective-permute-start | bytes 516104 | tf_op jit(solution)/shard_map/ppermute | solution.py:1096
  43.3 1.0 %copy-start = (bf16[4,128,256]{2,1,0:T(8,128)(2,1)S(1)}, bf16[4,128,256]{2,1,0:T(8,128)(2,1)}, u32[]{:S(2)}) copy-start(bf16[4,128,256]{2,1,0:T(8,128)(2,1)} %constant.79.clone.refs_2_.refs_3_) | copy-start | bytes 786436
  43.3 1.0 %copy-start.1 = (bf16[4,128,256]{2,1,0:T(8,128)(2,1)S(1)}, bf16[4,128,256]{2,1,0:T(8,128)(2,1)}, u32[]{:S(2)}) copy-start(bf16[4,128,256]{2,1,0:T(8,128)(2,1)} %constant.80.clone.refs_3_.refs_4_) | copy-start | bytes 786436
  43.4 2.2 %copy-start.9 = (s32[512]{0:T(512)S(1)}, s32[512]{0:T(512)}, u32[]{:S(2)}) copy-start(s32[512]{0:T(512)} %param.17) | copy-start | bytes 6148
  51.6 2.9 %collective-permute-start.10 = (s16[672,128]{1,0:T(8,128)(2,1)S(1)}, s16[672,128]{1,0:T(8,128)(2,1)S(1)}, u32[]{:S(2)}, u32[]{:S(2)}) collective-permute-start(s16[672,128]{1,0:T(8,128)(2,1)S(1)} %get-tuple-element.64), channel_id=1, source_target_pairs={{0,1},{1,0},{2,3},{3,2},{4,5},{5,4},{6,7},{7,6},{8,9},{9,8},{10,11... | collective-permute-start | bytes 516104 | tf_op jit(solution)/shard_map/ppermute | solution.py:1096
  52.5 7.2 %collective-permute-start.11 = (s16[672,128]{1,0:T(8,128)(2,1)S(1)}, s16[672,128]{1,0:T(8,128)(2,1)S(1)}, u32[]{:S(2)}, u32[]{:S(2)}) collective-permute-start(s16[672,128]{1,0:T(8,128)(2,1)S(1)} %get-tuple-element.65), channel_id=1, source_target_pairs={{0,2},{1,3},{2,0},{3,1},{4,6},{5,7},{6,4},{7,5},{8,10},{9,11},{10,... | collective-permute-start | bytes 516104 | tf_op jit(solution)/shard_map/ppermute | solution.py:1096
  54.0 7.7 %collective-permute-start.12 = (s16[672,128]{1,0:T(8,128)(2,1)S(1)}, s16[672,128]{1,0:T(8,128)(2,1)S(1)}, u32[]{:S(2)}, u32[]{:S(2)}) collective-permute-start(s16[672,128]{1,0:T(8,128)(2,1)S(1)} %get-tuple-element.66), channel_id=1, source_target_pairs={{0,3},{1,2},{2,1},{3,0},{4,7},{5,6},{6,5},{7,4},{8,11},{9,10},{10,... | collective-permute-start | bytes 516104 | tf_op jit(solution)/shard_map/ppermute | solution.py:1096
  63.6 6.4 %collective-permute-start.13 = (s16[560,128]{1,0:T(8,128)(2,1)S(1)}, s16[560,128]{1,0:T(8,128)(2,1)S(1)}, u32[]{:S(2)}, u32[]{:S(2)}) collective-permute-start(s16[560,128]{1,0:T(8,128)(2,1)S(1)} %get-tuple-element.68), channel_id=1, source_target_pairs={{0,4},{8,12},{4,0},{12,8},{1,5},{9,13},{5,1},{13,9},{2,6},{10,14},... | collective-permute-start | bytes 430088 | tf_op jit(solution)/shard_map/ppermute | solution.py:1107
  63.6 9.5 %collective-permute-start.15 = (s16[816,128]{1,0:T(8,128)(2,1)S(1)}, s16[816,128]{1,0:T(8,128)(2,1)S(1)}, u32[]{:S(2)}, u32[]{:S(2)}) collective-permute-start(s16[816,128]{1,0:T(8,128)(2,1)S(1)} %get-tuple-element.70), channel_id=1, source_target_pairs={{4,8},{8,4},{5,9},{9,5},{6,10},{10,6},{7,11},{11,7},{20,24},{24,20... | collective-permute-start | bytes 626696 | tf_op jit(solution)/shard_map/ppermute | solution.py:1108
  64.5 8.6 %collective-permute-start.14 = (s16[528,128]{1,0:T(8,128)(2,1)S(1)}, s16[528,128]{1,0:T(8,128)(2,1)S(1)}, u32[]{:S(2)}, u32[]{:S(2)}) collective-permute-start(s16[528,128]{1,0:T(8,128)(2,1)S(1)} %get-tuple-element.69), channel_id=1, source_target_pairs={{0,4},{8,12},{4,0},{12,8},{1,5},{9,13},{5,1},{13,9},{2,6},{10,14},... | collective-permute-start | bytes 405512 | tf_op jit(solution)/shard_map/ppermute | solution.py:1109
  70.1 7.3 %collective-permute-start.16 = (s16[272,128]{1,0:T(8,128)(2,1)S(1)}, s16[272,128]{1,0:T(8,128)(2,1)S(1)}, u32[]{:S(2)}, u32[]{:S(2)}) collective-permute-start(s16[272,128]{1,0:T(8,128)(2,1)S(1)} %pair_messages.3), channel_id=1, source_target_pairs={{0,8},{4,12},{8,0},{12,4},{1,9},{5,13},{9,1},{13,5},{2,10},{6,14},... | collective-permute-start | bytes 208904 | tf_op jit(solution)/shard_map/ppermute | solution.py:1111
  80.5 3.9 %collective-permute-start.19 = (s16[672,128]{1,0:T(8,128)(2,1)S(1)}, s16[672,128]{1,0:T(8,128)(2,1)S(1)}, u32[]{:S(2)}, u32[]{:S(2)}) collective-permute-start(s16[672,128]{1,0:T(8,128)(2,1)S(1)} %get-tuple-element.77), channel_id=1, source_target_pairs={{0,1},{1,0},{2,3},{3,2},{4,5},{5,4},{6,7},{7,6},{8,9},{9,8},{10,11... | collective-permute-start | bytes 516104 | tf_op jit(solution)/shard_map/ppermute | solution.py:1096
  80.6 7.2 %collective-permute-start.17 = (s16[672,128]{1,0:T(8,128)(2,1)S(1)}, s16[672,128]{1,0:T(8,128)(2,1)S(1)}, u32[]{:S(2)}, u32[]{:S(2)}) collective-permute-start(s16[672,128]{1,0:T(8,128)(2,1)S(1)} %get-tuple-element.73), channel_id=1, source_target_pairs={{0,2},{1,3},{2,0},{3,1},{4,6},{5,7},{6,4},{7,5},{8,10},{9,11},{10,... | collective-permute-start | bytes 516104 | tf_op jit(solution)/shard_map/ppermute | solution.py:1096
  82.2 8.5 %collective-permute-start.18 = (s16[672,128]{1,0:T(8,128)(2,1)S(1)}, s16[672,128]{1,0:T(8,128)(2,1)S(1)}, u32[]{:S(2)}, u32[]{:S(2)}) collective-permute-start(s16[672,128]{1,0:T(8,128)(2,1)S(1)} %get-tuple-element.74), channel_id=1, source_target_pairs={{0,3},{1,2},{2,1},{3,0},{4,7},{5,6},{6,5},{7,4},{8,11},{9,10},{10,... | collective-permute-start | bytes 516104 | tf_op jit(solution)/shard_map/ppermute | solution.py:1096

commit v10 on v9

--- a/solution.py
+++ b/solution.py
@@ -22,6 +22,7 @@
 BF16 = jnp.bfloat16
 VMEM_LIMIT = 24 * 1024 * 1024
 START_LIMIT = VMEM_LIMIT
+EARLY_FLOPS = 5 * 10**9
 GROUP = 32
 CHAINS = 2
 
@@ -157,8 +158,8 @@
         y_table = cas(step * np.outer(waves, cells))
         y_forward[:, block, :reach] = y_table
         y_inverse[block, :reach] = y_table.T / GRID
-    y_forward = y_forward.reshape(GRID, y_count // pair, -1).transpose(1, 0, 2)
-    y_forward = halves(y_forward)
+    y_forward = y_forward.reshape(GRID, y_count // pair, pair, -1).transpose(2, 0, 1, 3)
+    y_forward = halves(y_forward.reshape(pair, GRID, -1))
     y_forward = np.concatenate([y_forward[0], y_forward[0], y_forward[1]], axis=2)
     root = np.sqrt(shift * (shift + 4.0))
     decay = 2.0 / (2.0 + shift + root)
@@ -471,11 +472,11 @@
     half = reach_x // 2
     pitch = up_to(reach_y, 8)
     tall = len(parts) * pitch
-    core = lax.axis_index("pair")
-    for bit, part in enumerate(parts):
+    chip = lax.axis_index("narrow")
+    for flip, part in enumerate(parts):
         first = from_short(part[:top, :])
         opened[...] = from_short(part[top:, :]) * unit(first[0:1], first[1:2])
-        place = (core ^ bit) * pitch
+        place = (chip ^ flip) * pitch
         for i in range(half):
             stacked[pl.ds(pl.multiple_of(i * tall + place, 8), reach_y), :] = opened[
                 i * reach_y : (i + 1) * reach_y, :
@@ -499,34 +500,34 @@
             spectrum[j] = made if before is None else before[j] + made
 
 
-def forward_early_kernel(reach_x, reach_y, pair, *refs):
-    parts = refs[:pair]
-    table_ref, spectrum, opened, stacked = refs[pair:]
+def forward_early_kernel(reach_x, reach_y, chips, *refs):
+    parts = refs[:chips]
+    table_ref, spectrum, opened, stacked = refs[chips:]
     top = parts[0].shape[0] - opened.shape[0]
     stacked[...] = jnp.zeros_like(stacked)
     stack_pieces(parts, reach_x, reach_y, top, opened, stacked)
-    transform_pieces(table_ref[lax.axis_index("narrow")], stacked, None, spectrum)
-
-
-def stacking_scratch(pair, reach_x, reach_y):
+    transform_pieces(table_ref[lax.axis_index("pair")], stacked, None, spectrum)
+
+
+def stacking_scratch(chips, reach_x, reach_y):
     half = reach_x // 2
     return [
         pltpu.VMEM((up_to(half * reach_y, 16), 2 * HALF), F32),
-        pltpu.VMEM((half * pair * up_to(reach_y, 8), 2 * HALF), F32),
+        pltpu.VMEM((half * chips * up_to(reach_y, 8), 2 * HALF), F32),
     ]
 
 
 def forward_early(parts, table, reach_x, reach_y):
     half = reach_x // 2
-    pair = len(parts)
+    chips = len(parts)
     return pl.pallas_call(
-        functools.partial(forward_early_kernel, reach_x, reach_y, pair),
-        in_specs=[whole_vmem()] * (pair + 1),
+        functools.partial(forward_early_kernel, reach_x, reach_y, chips),
+        in_specs=[whole_vmem()] * (chips + 1),
         out_specs=whole_vmem(),
         out_shape=jax.ShapeDtypeStruct((half, GRID, 2 * HALF), F32),
-        scratch_shapes=stacking_scratch(pair, reach_x, reach_y),
+        scratch_shapes=stacking_scratch(chips, reach_x, reach_y),
         compiler_params=params(),
-        cost_estimate=cost(2 * half * 256 * 256 * 128, 4 * half * GRID * 2 * HALF * 2),
+        cost_estimate=cost(EARLY_FLOPS, 4 * half * GRID * 2 * HALF * 2),
         name="forward_early",
     )(*parts, table)
 
@@ -550,9 +551,9 @@
         head[at : at + blocks, :] = mantissa
         head[at + blocks : at + 2 * blocks, :] = exponent
     before = early_ref
-    for chip in range(1, pieces // pair):
-        stack_pieces(parts[chip * pair : (chip + 1) * pair], reach_x, reach_y, top, opened, stacked)
-        transform_pieces(table_ref[lax.axis_index("narrow") ^ chip], stacked, before, spectrum)
+    for core in range(1, pair):
+        stack_pieces(parts[core::pair], reach_x, reach_y, top, opened, stacked)
+        transform_pieces(table_ref[lax.axis_index("pair") ^ core], stacked, before, spectrum)
         before = spectrum
 
     chunk = 32
@@ -904,20 +905,20 @@
     return dot_three(values, (pick(high_ref), pick(low_ref)))
 
 
-def sample_early_kernel(*refs):
+def sample_early_kernel(flips, *refs):
     *parts, high_ref, low_ref, out_ref = refs
-    out_ref[...] = z_lines(parts, range(len(parts)), high_ref, low_ref)
-
-
-def sample_early(parts, table):
+    out_ref[...] = z_lines(parts, flips, high_ref, low_ref)
+
+
+def sample_early(parts, flips, table):
     rows = parts[0].shape[0] - 16
     return pl.pallas_call(
-        sample_early_kernel,
+        functools.partial(sample_early_kernel, flips),
         in_specs=[whole_vmem()] * (len(parts) + 2),
         out_specs=whole_vmem(),
         out_shape=jax.ShapeDtypeStruct((rows, 2 * REGION), F32),
         compiler_params=params(),
-        cost_estimate=cost(2 * rows * 256 * 256 * 3, 4 * rows * 512),
+        cost_estimate=cost(EARLY_FLOPS, 4 * rows * 512),
         name="sample_early",
     )(*parts, *table)
 
@@ -1003,7 +1004,8 @@
 
 
 def near_kernel(slots, blocks, place_ref, target_ref, *refs):
-    even_ref, odd_ref, peers_ref, tile_ref, out_ref, held = refs
+    even_ref, odd_ref, peers_ref, tile_ref = refs[:4]
+    out_ref, held = refs[-2:]
     count = peers_ref.shape[0]
     held[count : 2 * count, :] = peers_ref[...]
     on_left = lax.axis_index("wide") & 1
@@ -1028,7 +1030,7 @@
         out_ref[target, :] = out_ref[target, :] + product[:1]
 
 
-def near_field(places, targets, from_even, from_odd, peers, tiles, blocks, out_rows):
+def near_field(places, targets, from_even, from_odd, peers, tiles, blocks, out_rows, awaited):
     slots = tiles.shape[0]
     head = from_even.shape[0] - 2 * GRID
     constant = lambda shape: pl.BlockSpec(shape, lambda i: (0,) * len(shape))
@@ -1042,14 +1044,15 @@
             constant((head, BLOCK)),
             constant(peers.shape),
             constant(tiles.shape),
-        ],
+        ]
+        + [anywhere()] * len(awaited),
         out_specs=constant((out_rows, BLOCK)),
         out_shape=jax.ShapeDtypeStruct((out_rows, BLOCK), F32),
         scratch_shapes=[pltpu.VMEM((3 * peers.shape[0], BLOCK), F32)],
         compiler_params=params(),
         cost_estimate=cost(2 * slots * 16 * BLOCK * BLOCK, 2 * slots * BLOCK * BLOCK),
         name="near_field",
-    )(places, targets, from_even, from_odd, peers, tiles)
+    )(places, targets, from_even, from_odd, peers, tiles, *awaited)
 
 
 def shards(
@@ -1089,18 +1092,24 @@
     odd_swap = swaps([(i, i + 1) for i in range(1, x_count - 1, 2)])
     far_flips = list(range(2, x_count, 2))
 
-    local, moving = [0], list(range(1, y_count))
-
-    def flipped(parts, flips):
-        return [
-            lax.ppermute(part, Y_AXES, [(i, i ^ flip) for i in range(y_count)])
-            for flip, part in zip(flips, parts)
-        ]
+    first = list(range(pair, y_count, pair))
+    rest = [flip for flip in range(y_count) if flip not in first]
+    same_core = list(range(0, y_count, pair))
+    other_core = [flip for flip in range(y_count) if flip not in same_core]
+
+    def turned(sent, then):
+        arrived = [None] * y_count
+        for flip, part in zip(first + rest, list(sent) + list(then)):
+            swap_pairs = [(i, i ^ flip) for i in range(y_count)]
+            arrived[flip] = part if flip == 0 else lax.ppermute(part, Y_AXES, swap_pairs)
+        return arrived
+
+    def chosen(parts, flips):
+        return [parts[flip] for flip in flips]
 
     def convolve_and_sample(last, vector, sent, both, places, sample_lines, awaited):
-        arrived = flipped(sent, moving)
-        arrived = list(spread_rest(vector, both, z_forward, local)) + arrived
-        early = forward_early(arrived[:pair], y_forward, reach_x, reach_y)
+        arrived = turned(sent, spread_rest(vector, both, z_forward, rest))
+        early = forward_early(chosen(arrived, same_core), y_forward, reach_x, reach_y)
         spectrum, even_message, layers, odd_message, own, peers, inner = forward(
             arrived, early, y_forward, modes, reach_x, reach_y, blocks, awaited
         )
@@ -1113,9 +1122,6 @@
                 far_flips, pair_messages(own, from_even, modes, reach_x, far_flips)
             )
         ]
-        near_part = near_field(
-            sources, targets, from_even, from_odd, peers, near_tiles, blocks, out_rows
-        )
         *sent, high, low = inverse(
             spectrum,
             from_even,
@@ -1128,16 +1134,19 @@
             modes,
             reach_x,
             reach_y,
-            moving,
+            first,
         )
-        arrived = flipped(sent, moving)
-        arrived = list(inverse_rest((high, low), y_inverse, reach_y, local)) + arrived
+        then = inverse_rest((high, low), y_inverse, reach_y, rest)
+        near_part = near_field(
+            sources, targets, from_even, from_odd, peers, near_tiles, blocks, out_rows, then[:1]
+        )
+        arrived = turned(sent, then)
         image = sample(
             last,
             places,
-            arrived[pair:],
-            list(range(pair, y_count)),
-            sample_early(arrived[:pair], z_inverse),
+            chosen(arrived, other_core),
+            other_core,
+            sample_early(chosen(arrived, same_core), same_core, z_inverse),
             z_inverse,
             sample_lines,
             surface_flag,
@@ -1150,7 +1159,7 @@
 
     raw = (stencil_base, surface_flag, sample_weights, dipole_weights)
     *sent, high, low, source_coeff, sample_coeff, places = spread(
-        density, z_forward, None, raw, reach_x, reach_y, moving
+        density, z_forward, None, raw, reach_x, reach_y, first
     )
     sample_lines = place_lines(places, sample_coeff, [])
     first_image, near_part = convolve_and_sample(
@@ -1159,7 +1168,7 @@
     first_image = first_image.reshape(-1)
     source_lines = place_lines(places, source_coeff, [near_part])
     *sent, high, low = spread(
-        first_image, z_forward, (places, source_lines), None, reach_x, reach_y, moving
+        first_image, z_forward, (places, source_lines), None, reach_x, reach_y, first
     )
     both_images, _ = convolve_and_sample(
         True, first_image, sent, (high, low), places, sample_lines, []

time: 94.5 us -> 93.5 us (0.989)
  waiting for transfers between devices: 28.6 us -> 24.8 us
  local copies, waits for them, and re-layouts: 1.28 us -> 3.71 us
    ppermute x12, waiting for transfers between devices: 16 us -> 12.2 us  [turned(): lax.ppermute(part, Y_AXES, swap_pairs)]
    unnamed x24 -> x30, local copies, waits for them, and re-layouts: 0.19 us -> 2.63 us
  transfers between devices with their start and end apart: 20 -> 20, of which waited for: 11 -> 11; matrix products, arithmetic and copies ran while one was open for 1% -> 1% of each run, Pallas kernels for 14% -> 15%
where the time goes in v10:
time: 93.5 us; the launch traced here: 92.8 us
  Pallas kernels  38.7 us (41%)
  starting transfers between devices  25.2 us (27%)
  waiting for transfers between devices  24.8 us (27%)
  local copies, waits for them, and re-layouts  3.71 us (4%)
    ppermute x12, waiting for transfers between devices, turned(): lax.ppermute(part, Y_AXES, swap_pairs)  12.2 us
    ppermute x12, starting transfers between devices, turned(): lax.ppermute(part, Y_AXES, swap_pairs)  10.3 us
    ppermute x2, starting transfers between devices, convolve_and_sample(): even_layers = lax.ppermute(layers, 'wide', even_swap)  8.78 us
    ppermute x2, waiting for transfers between devices, convolve_and_sample(): lax.ppermute(message, 'wide', [(i, i ^ flip) for i in range(x_count)])  8.74 us
    pallas_call x2, Pallas kernels, spread(): pl.pallas_call(functools.partial(start_kernel if placed is None else spre...  8.4 us
    pallas_call x2, Pallas kernels, sample(): pl.pallas_call(functools.partial(sample_kernel, last, reach_x, reach_y, f...  6.49 us
    pallas_call x2, Pallas kernels, inverse(): pl.pallas_call(functools.partial(inverse_kernel, reach_x, reach_y, flips,...  6 us
    pallas_call x2, Pallas kernels, place_lines(): pl.pallas_call(lines_kernel, in_specs=[in_smem(), whole_vmem()] + [anywhe...  5.89 us
  transfers between devices with their start and end apart: 20, of which 11 were waited for; matrix products, arithmetic and copies ran while one was open for 1% of the time, Pallas kernels for 15%

profile of v10, /device:TPU:0, one launch (start us, length us, event | category | flops | bytes accessed | tf_op | source)
XLA Modules:
  0.0 92.8 jit_solution(14522956302146687428)
XLA Ops:
  0.0 5.7 %start.1 = (s16[672,128]{1,0:T(8,128)(2,1)S(1)}, bf16[656,256]{1,0:T(8,128)(2,1)S(1)}, bf16[656,256]{1,0:T(8,128)(2,1)S(1)}, f32[256,128]{1,0:T(8,128)S(1)}, f32...) custom-call(f32[512]{0:T(512)} %refs_0_.1, f32[4,128]{1,0:T(4,128)} %bitcast.7, ...), custom_call_target="tpu_custom_call" | custom-call | flops 169869312 | bytes 4194304 | tf_op jit(solution)/shard_map/start/pallas_call | solution.py:399
  5.7 3.0 %collective-permute-start.1 = (s16[672,128]{1,0:T(8,128)(2,1)S(1)}, s16[672,128]{1,0:T(8,128)(2,1)S(1)}, u32[]{:S(2)}, u32[]{:S(2)}) collective-permute-start(s16[672,128]{1,0:T(8,128)(2,1)S(1)} %get-tuple-element.51), channel_id=1, source_target_pairs={{0,2},{1,3},{2,0},{3,1},{4,6},{5,7},{6,4},{7,5},{8,10},{9,11},{10,... | collective-permute-start | bytes 516104 | tf_op jit(solution)/shard_map/ppermute | solution.py:1104
  8.7 0.9 %copy-done = bf16[4,256,128]{2,1,0:T(8,128)(2,1)S(1)} copy-done((bf16[4,256,128]{2,1,0:T(8,128)(2,1)S(1)}, bf16[4,256,128]{2,1,0:T(8,128)(2,1)}, u32[]{:S(2)}) %copy-start) | copy-done | bytes 262168
  9.6 0.9 %copy-done.2 = bf16[4,256,128]{2,1,0:T(8,128)(2,1)S(1)} copy-done((bf16[4,256,128]{2,1,0:T(8,128)(2,1)S(1)}, bf16[4,256,128]{2,1,0:T(8,128)(2,1)}, u32[]{:S(2)}) %copy-start.2) | copy-done | bytes 262168
  10.6 0.7 copy-done.10
  11.3 0.9 spread_rest.2
  12.1 0.1 collective-permute-start
  12.2 0.1 collective-permute-start.2
  12.4 2.9 %place_lines.2.refs_7_.refs_5_ = f32[8192,128]{1,0:T(8,128)S(1)} custom-call(s32[2,512]{1,0:T(2,128)S(1)} %get-tuple-element.46.place_ref.refs_1_, f32[256,128]{1,0:T(8,128)S(1)} %get-tuple-element.53.coeff_ref), custom_call_target="tpu_custom_call" | custom-call | flops 1048576 | bytes 4194304 | tf_op jit(solution)/shard_map/place_lines/pallas_call | solution.py:460
  15.3 1.1 %dynamic-slice_bitcast_fusion.refs_6_.modes_ref.refs_9_ = f32[4,256,128]{2,1,0:T(8,128)S(1)} fusion(f32[4,4,256,128]{3,2,1,0:T(8,128)} %constant.73.clone, s32[]{:T(128)S(6)} %select_n.30), kind=kLoop, calls=%fused_computation | loop fusion | bytes 1048580 | tf_op jit(solution)/shard_map/jit(dynamic_index_in_dim)/squeeze | solution.py:1080
  16.4 0.0 collective-permute-done.1.refs_1_.refs_2_
  16.4 0.6 forward_early.2.refs_4_
  17.1 0.0 copy-start.5
  17.1 0.0 copy-start.6
  17.1 1.3 %collective-permute-done.2.refs_3_ = s16[672,128]{1,0:T(8,128)(2,1)S(1)} collective-permute-done((s16[672,128]{1,0:T(8,128)(2,1)S(1)}, s16[672,128]{1,0:T(8,128)(2,1)S(1)}, u32[]{:S(2)}, u32[]{:S(2)}) %collective-permute-start.2) | collective-permute-done | bytes 172064 | tf_op jit(solution)/shard_map/ppermute | solution.py:1104
  18.4 1.9 %forward.2 = (f32[18,256,128]{2,1,0:T(8,128)S(1)}, s16[560,128]{1,0:T(8,128)(2,1)S(1)}, s16[528,128]{1,0:T(8,128)(2,1)S(1)}, s16[816,128]{1,0:T(8,128)(2,1)S(1)}...) custom-call(s16[672,128]{1,0:T(8,128)(2,1)S(1)} %get-tuple-element.49.refs_0_, ...), custom_call_target="tpu_custom_call" | custom-call | flops 301989888 | bytes 4718592 | tf_op jit(solution)/shard_map/forward/pallas_call | solution.py:633
  20.3 1.6 %collective-permute-start.3 = (s16[560,128]{1,0:T(8,128)(2,1)S(1)}, s16[560,128]{1,0:T(8,128)(2,1)S(1)}, u32[]{:S(2)}, u32[]{:S(2)}) collective-permute-start(s16[560,128]{1,0:T(8,128)(2,1)S(1)} %get-tuple-element.55), channel_id=1, source_target_pairs={{0,4},{8,12},{4,0},{12,8},{1,5},{9,13},{5,1},{13,9},{2,6},{10,14},... | collective-permute-start | bytes 430088 | tf_op jit(solution)/shard_map/ppermute | solution.py:1116
  21.9 0.7 collective-permute-start.5
  22.6 4.5 %collective-permute-start.4 = (s16[528,128]{1,0:T(8,128)(2,1)S(1)}, s16[528,128]{1,0:T(8,128)(2,1)S(1)}, u32[]{:S(2)}, u32[]{:S(2)}) collective-permute-start(s16[528,128]{1,0:T(8,128)(2,1)S(1)} %get-tuple-element.56), channel_id=1, source_target_pairs={{0,4},{8,12},{4,0},{12,8},{1,5},{9,13},{5,1},{13,9},{2,6},{10,14},... | collective-permute-start | bytes 405512 | tf_op jit(solution)/shard_map/ppermute | solution.py:1118
  27.1 0.1 pair_messages.2
  27.2 2.0 %collective-permute-start.6 = (s16[272,128]{1,0:T(8,128)(2,1)S(1)}, s16[272,128]{1,0:T(8,128)(2,1)S(1)}, u32[]{:S(2)}, u32[]{:S(2)}) collective-permute-start(s16[272,128]{1,0:T(8,128)(2,1)S(1)} %pair_messages.2), channel_id=1, source_target_pairs={{0,8},{4,12},{8,0},{12,4},{1,9},{5,13},{9,1},{13,5},{2,10},{6,14},... | collective-permute-start | bytes 208904 | tf_op jit(solution)/shard_map/ppermute | solution.py:1120
  29.2 1.4 %collective-permute-done.4.refs_2_ = s16[528,128]{1,0:T(8,128)(2,1)S(1)} collective-permute-done((s16[528,128]{1,0:T(8,128)(2,1)S(1)}, s16[528,128]{1,0:T(8,128)(2,1)S(1)}, u32[]{:S(2)}, u32[]{:S(2)}) %collective-permute-start.4) | collective-permute-done | bytes 135200 | tf_op jit(solution)/shard_map/ppermute | solution.py:1118
  30.6 4.2 %collective-permute-done.6.refs_6_ = s16[272,128]{1,0:T(8,128)(2,1)S(1)} collective-permute-done((s16[272,128]{1,0:T(8,128)(2,1)S(1)}, s16[272,128]{1,0:T(8,128)(2,1)S(1)}, u32[]{:S(2)}, u32[]{:S(2)}) %collective-permute-start.6) | collective-permute-done | bytes 69664 | tf_op jit(solution)/shard_map/ppermute | solution.py:1120
  34.8 3.0 %inverse.2 = (s16[672,128]{1,0:T(8,128)(2,1)S(1)}, bf16[18,256,128]{2,1,0:T(8,128)(2,1)S(1)}, bf16[18,256,128]{2,1,0:T(8,128)(2,1)S(1)}) custom-call(f32[18,256,128]{2,1,0:T(8,128)S(1)} %get-tuple-element.54.refs_0_, s16[560,128]{1,0:T(8,128)(2,1)S(1)} %collective-permute-done.3.even_ref.refs_1_.refs_0_, s16[528,128]{1,0:T(8,128)(2,1)S(1)} %collective-permute-done.4.refs_2_, ...), custom_call_target="tpu_custom_call" | custom-call | flops 301989888 | bytes 4718592 | tf_op jit(solution)/shard_map/inverse/pallas_call | solution.py:841
  37.8 0.6 collective-permute-start.9
  38.5 0.9 %inverse_rest.2 = (s16[672,128]{1,0:T(8,128)(2,1)S(1)}, s16[672,128]{1,0:T(8,128)(2,1)S(1)}, s16[672,128]{1,0:T(8,128)(2,1)S(1)}) custom-call(bf16[18,256,128]{2,1,0:T(8,128)(2,1)S(1)} %get-tuple-element.60.field_high, bf16[18,256,128]{2,1,0:T(8,128)(2,1)S(1)} %get-tuple-element.61.field_low, bf16[4,48,256]{2,1,0:T(8,128)(2,1)S(1)} %copy-done.5, ...), custom_call_target="tpu_custom_call" | custom-call | flops 301989888 | bytes 4718592 | tf_op jit(solution)/shard_map/inverse_rest/pallas_call | solution.py:865
  39.4 0.1 collective-permute-start.7
  39.5 1.6 %collective-permute-start.8 = (s16[672,128]{1,0:T(8,128)(2,1)S(1)}, s16[672,128]{1,0:T(8,128)(2,1)S(1)}, u32[]{:S(2)}, u32[]{:S(2)}) collective-permute-start(s16[672,128]{1,0:T(8,128)(2,1)S(1)} %get-tuple-element.63), channel_id=1, source_target_pairs={{0,3},{1,2},{2,1},{3,0},{4,7},{5,6},{6,5},{7,4},{8,11},{9,10},{10,... | collective-permute-start | bytes 516104 | tf_op jit(solution)/shard_map/ppermute | solution.py:1104
  41.1 1.0 %near_field.2.refs_8_.refs_0_ = f32[8,128]{1,0:T(8,128)S(1)} custom-call(s32[24]{0:T(128)S(1)} %get-tuple-element.88.place_ref, s32[24]{0:T(128)S(1)} %get-tuple-element.87.target_ref, s16[560,128]{1,0:T(8,128)(2,1)S(1)} %collective-permute-done.3.even_ref.refs_1_.refs_0_, s16[816,128]{1,0:T(8,128)(2,1)S(1)} %collective-permute-done.5.refs_3_.refs_1_, ...), custom_call_target="tpu_custom_call" | custom-call | flops 12582912 | bytes 786432 | tf_op jit(solution)/shard_map/near_field/pallas_call | solution.py:1037
  42.2 0.0 copy-start.8
  42.2 3.0 %place_lines.3.refs_5_ = f32[8192,128]{1,0:T(8,128)S(1)} custom-call(s32[2,512]{1,0:T(2,128)S(1)} %get-tuple-element.46.place_ref.refs_1_, f32[256,128]{1,0:T(8,128)S(1)} %get-tuple-element.67.coeff_ref, f32[8,128]{1,0:T(8,128)S(1)} %near_field.2.refs_8_.refs_0_), custom_call_target="tpu_custom_call" | custom-call | flops 1048576 | bytes 4194304 | tf_op jit(solution)/shard_map/place_lines/pallas_call | solution.py:460
  45.1 0.0 copy-start.12
  45.1 0.0 collective-permute-done.9.refs_1_
  45.2 0.5 sample_early.2.refs_2_
  45.6 0.0 collective-permute-done.7.refs_0_
  45.6 0.6 collective-permute-done.8.refs_1_
  46.3 2.9 %sample.2.refs_2_.rounded_ref.refs_7_ = f32[4,128]{1,0:T(4,128)S(1)} custom-call(s32[2,512]{1,0:T(2,128)S(1)} %get-tuple-element.46.place_ref.refs_1_, s16[672,128]{1,0:T(8,128)(2,1)S(1)} %collective-permute-done.7.refs_0_, s16[672,128]{1,0:T(8,128)(2,1)S(1)} %collective-permute-done.8.refs_1_, f32[656,256]{1,0:T(8,128)S(1)} %sample_early.2.refs_2_, ...), custom_call_target="tpu_custom_call" | custom-call | flops 169869312 | bytes 4194304 | tf_op jit(solution)/shard_map/sample/pallas_call | solution.py:981
  49.2 2.7 %spread.1 = (s16[672,128]{1,0:T(8,128)(2,1)S(1)}, bf16[656,256]{1,0:T(8,128)(2,1)S(1)}, bf16[656,256]{1,0:T(8,128)(2,1)S(1)}) custom-call(f32[512]{0:T(512)S(1)} %bitcast.6, s32[2,512]{1,0:T(2,128)S(1)} %get-tuple-element.46.place_ref.refs_1_, f32[4,128]{1,0:T(4,128)S(1)} %sample.2.refs_2_.rounded_ref.refs_7_, bf16[4,256,128]{2,1,0:T(8,128)(2,1)S(1)} %copy-done.1, ...), custom_call_target="tpu_custom_call" | custom-call | flops 169869312 | bytes 4194304 | tf_op jit(solution)/shard_map/spread/pallas_call | solution.py:399
  52.0 1.1 %collective-permute-start.11 = (s16[672,128]{1,0:T(8,128)(2,1)S(1)}, s16[672,128]{1,0:T(8,128)(2,1)S(1)}, u32[]{:S(2)}, u32[]{:S(2)}) collective-permute-start(s16[672,128]{1,0:T(8,128)(2,1)S(1)} %get-tuple-element.72), channel_id=1, source_target_pairs={{0,2},{1,3},{2,0},{3,1},{4,6},{5,7},{6,4},{7,5},{8,10},{9,11},{10,... | collective-permute-start | bytes 516104 | tf_op jit(solution)/shard_map/ppermute | solution.py:1104
  53.0 0.9 spread_rest.3
  53.9 0.1 collective-permute-start.10
  54.1 1.4 %collective-permute-start.12 = (s16[672,128]{1,0:T(8,128)(2,1)S(1)}, s16[672,128]{1,0:T(8,128)(2,1)S(1)}, u32[]{:S(2)}, u32[]{:S(2)}) collective-permute-start(s16[672,128]{1,0:T(8,128)(2,1)S(1)} %get-tuple-element.73), channel_id=1, source_target_pairs={{0,3},{1,2},{2,1},{3,0},{4,7},{5,6},{6,5},{7,4},{8,11},{9,10},{10,... | collective-permute-start | bytes 516104 | tf_op jit(solution)/shard_map/ppermute | solution.py:1104
  55.4 3.8 %collective-permute-done.11.refs_1_.refs_2_ = s16[672,128]{1,0:T(8,128)(2,1)S(1)} collective-permute-done((s16[672,128]{1,0:T(8,128)(2,1)S(1)}, s16[672,128]{1,0:T(8,128)(2,1)S(1)}, u32[]{:S(2)}, u32[]{:S(2)}) %collective-permute-start.11) | collective-permute-done | bytes 172064 | tf_op jit(solution)/shard_map/ppermute | solution.py:1104
  59.2 0.7 forward_early.3.refs_4_
  59.9 3.1 %collective-permute-done.12.refs_3_ = s16[672,128]{1,0:T(8,128)(2,1)S(1)} collective-permute-done((s16[672,128]{1,0:T(8,128)(2,1)S(1)}, s16[672,128]{1,0:T(8,128)(2,1)S(1)}, u32[]{:S(2)}, u32[]{:S(2)}) %collective-permute-start.12) | collective-permute-done | bytes 172064 | tf_op jit(solution)/shard_map/ppermute | solution.py:1104
  63.0 1.9 %forward.3 = (f32[18,256,128]{2,1,0:T(8,128)S(1)}, s16[560,128]{1,0:T(8,128)(2,1)S(1)}, s16[528,128]{1,0:T(8,128)(2,1)S(1)}, s16[816,128]{1,0:T(8,128)(2,1)S(1)}...) custom-call(s16[672,128]{1,0:T(8,128)(2,1)S(1)} %get-tuple-element.70.refs_0_, ...), custom_call_target="tpu_custom_call" | custom-call | flops 301989888 | bytes 4718592 | tf_op jit(solution)/shard_map/forward/pallas_call | solution.py:633
  64.9 0.1 collective-permute-start.13
  64.9 0.9 collective-permute-start.15
  65.8 4.3 %collective-permute-start.14 = (s16[528,128]{1,0:T(8,128)(2,1)S(1)}, s16[528,128]{1,0:T(8,128)(2,1)S(1)}, u32[]{:S(2)}, u32[]{:S(2)}) collective-permute-start(s16[528,128]{1,0:T(8,128)(2,1)S(1)} %get-tuple-element.76), channel_id=1, source_target_pairs={{0,4},{8,12},{4,0},{12,8},{1,5},{9,13},{5,1},{13,9},{2,6},{10,14},... | collective-permute-start | bytes 405512 | tf_op jit(solution)/shard_map/ppermute | solution.py:1118
  70.1 0.6 collective-permute-done.13.even_ref.refs_1_.refs_0_
  70.7 0.1 pair_messages.3
  70.9 0.8 collective-permute-start.16
  71.7 1.9 %collective-permute-done.14.refs_2_ = s16[528,128]{1,0:T(8,128)(2,1)S(1)} collective-permute-done((s16[528,128]{1,0:T(8,128)(2,1)S(1)}, s16[528,128]{1,0:T(8,128)(2,1)S(1)}, u32[]{:S(2)}, u32[]{:S(2)}) %collective-permute-start.14) | collective-permute-done | bytes 135200 | tf_op jit(solution)/shard_map/ppermute | solution.py:1118
  73.6 4.6 %collective-permute-done.16.refs_6_ = s16[272,128]{1,0:T(8,128)(2,1)S(1)} collective-permute-done((s16[272,128]{1,0:T(8,128)(2,1)S(1)}, s16[272,128]{1,0:T(8,128)(2,1)S(1)}, u32[]{:S(2)}, u32[]{:S(2)}) %collective-permute-start.16) | collective-permute-done | bytes 69664 | tf_op jit(solution)/shard_map/ppermute | solution.py:1120
  78.1 3.0 %inverse.3 = (s16[672,128]{1,0:T(8,128)(2,1)S(1)}, bf16[18,256,128]{2,1,0:T(8,128)(2,1)S(1)}, bf16[18,256,128]{2,1,0:T(8,128)(2,1)S(1)}) custom-call(f32[18,256,128]{2,1,0:T(8,128)S(1)} %get-tuple-element.74.refs_0_, s16[560,128]{1,0:T(8,128)(2,1)S(1)} %collective-permute-done.13.even_ref.refs_1_.refs_0_, ...), custom_call_target="tpu_custom_call" | custom-call | flops 301989888 | bytes 4718592 | tf_op jit(solution)/shard_map/inverse/pallas_call | solution.py:841
  81.1 0.2 collective-permute-start.19
  81.3 0.9 %inverse_rest.3 = (s16[672,128]{1,0:T(8,128)(2,1)S(1)}, s16[672,128]{1,0:T(8,128)(2,1)S(1)}, s16[672,128]{1,0:T(8,128)(2,1)S(1)}) custom-call(bf16[18,256,128]{2,1,0:T(8,128)(2,1)S(1)} %get-tuple-element.80.field_high, bf16[18,256,128]{2,1,0:T(8,128)(2,1)S(1)} %get-tuple-element.81.field_low, bf16[4,48,256]{2,1,0:T(8,128)(2,1)S(1)} %copy-done.5, ...), custom_call_target="tpu_custom_call" | custom-call | flops 301989888 | bytes 4718592 | tf_op jit(solution)/shard_map/inverse_rest/pallas_call | solution.py:865
  82.3 0.1 collective-permute-start.17
  82.4 2.0 %collective-permute-start.18 = (s16[672,128]{1,0:T(8,128)(2,1)S(1)}, s16[672,128]{1,0:T(8,128)(2,1)S(1)}, u32[]{:S(2)}, u32[]{:S(2)}) collective-permute-start(s16[672,128]{1,0:T(8,128)(2,1)S(1)} %get-tuple-element.83), channel_id=1, source_target_pairs={{0,3},{1,2},{2,1},{3,0},{4,7},{5,6},{6,5},{7,4},{8,11},{9,10},{10,... | collective-permute-start | bytes 516104 | tf_op jit(solution)/shard_map/ppermute | solution.py:1104
  84.4 1.0 %near_field.3.refs_8_ = f32[8,128]{1,0:T(8,128)S(1)} custom-call(s32[24]{0:T(128)S(1)} %get-tuple-element.88.place_ref, s32[24]{0:T(128)S(1)} %get-tuple-element.87.target_ref, s16[560,128]{1,0:T(8,128)(2,1)S(1)} %collective-permute-done.13.even_ref.refs_1_.refs_0_, s16[816,128]{1,0:T(8,128)(2,1)S(1)} %collective-permute-done.15.refs_3_.refs_1_, ...), custom_call_target="tpu_custom_call" | custom-call | flops 12582912 | bytes 786432 | tf_op jit(solution)/shard_map/near_field/pallas_call | solution.py:1037
  85.4 2.2 %collective-permute-done.19.refs_1_ = s16[672,128]{1,0:T(8,128)(2,1)S(1)} collective-permute-done((s16[672,128]{1,0:T(8,128)(2,1)S(1)}, s16[672,128]{1,0:T(8,128)(2,1)S(1)}, u32[]{:S(2)}, u32[]{:S(2)}) %collective-permute-start.19) | collective-permute-done | bytes 172064 | tf_op jit(solution)/shard_map/ppermute | solution.py:1104
  87.6 0.5 sample_early.3.refs_2_
  88.1 1.1 %collective-permute-done.18.refs_1_ = s16[672,128]{1,0:T(8,128)(2,1)S(1)} collective-permute-done((s16[672,128]{1,0:T(8,128)(2,1)S(1)}, s16[672,128]{1,0:T(8,128)(2,1)S(1)}, u32[]{:S(2)}, u32[]{:S(2)}) %collective-permute-start.18) | collective-permute-done | bytes 172064 | tf_op jit(solution)/shard_map/ppermute | solution.py:1104
  89.2 3.6 %sample.3 = f32[2,512]{1,0:T(2,128)} custom-call(s32[2,512]{1,0:T(2,128)S(1)} %get-tuple-element.46.place_ref.refs_1_, s16[672,128]{1,0:T(8,128)(2,1)S(1)} %collective-permute-done.17.refs_0_, s16[672,128]{1,0:T(8,128)(2,1)S(1)} %collective-permute-done.18.refs_1_, f32[656,256]{1,0:T(8,128)S(1)} %sample_early.3.refs_2_, bf16[4,128,256]{2,1,0:T(8,128)(2,1)S(1)} %copy-done.7, ...), custom_call_target="tpu_custom_call" | custom-call | flops 169869312 | bytes 4194304 | tf_op jit(solution)/shard_map/sample/pallas_call | solution.py:981
  (30 shorter events, 0.1 us)
Async XLA Ops:
  5.7 10.7 %collective-permute-start.1 = (s16[672,128]{1,0:T(8,128)(2,1)S(1)}, s16[672,128]{1,0:T(8,128)(2,1)S(1)}, u32[]{:S(2)}, u32[]{:S(2)}) collective-permute-start(s16[672,128]{1,0:T(8,128)(2,1)S(1)} %get-tuple-element.51), channel_id=1, source_target_pairs={{0,2},{1,3},{2,0},{3,1},{4,6},{5,7},{6,4},{7,5},{8,10},{9,11},{10,... | collective-permute-start | bytes 516104 | tf_op jit(solution)/shard_map/ppermute | solution.py:1104
  8.7 0.9 %copy-start = (bf16[4,256,128]{2,1,0:T(8,128)(2,1)S(1)}, bf16[4,256,128]{2,1,0:T(8,128)(2,1)}, u32[]{:S(2)}) copy-start(bf16[4,256,128]{2,1,0:T(8,128)(2,1)} %constant.74.clone.refs_2_.high_ref.refs_3_) | copy-start | bytes 786436
  9.6 0.9 %copy-start.2 = (bf16[4,256,128]{2,1,0:T(8,128)(2,1)S(1)}, bf16[4,256,128]{2,1,0:T(8,128)(2,1)}, u32[]{:S(2)}) copy-start(bf16[4,256,128]{2,1,0:T(8,128)(2,1)} %constant.75.clone.refs_3_.low_ref.refs_4_) | copy-start | bytes 786436
  10.6 0.7 copy-start.10
  12.1 4.9 %collective-permute-start = (s16[672,128]{1,0:T(8,128)(2,1)S(1)}, s16[672,128]{1,0:T(8,128)(2,1)S(1)}, u32[]{:S(2)}, u32[]{:S(2)}) collective-permute-start(s16[672,128]{1,0:T(8,128)(2,1)S(1)} %get-tuple-element.50), channel_id=1, source_target_pairs={{0,1},{1,0},{2,3},{3,2},{4,5},{5,4},{6,7},{7,6},{8,9},{9,8},{10,11... | collective-permute-start | bytes 516104 | tf_op jit(solution)/shard_map/ppermute | solution.py:1104
  12.2 6.2 %collective-permute-start.2 = (s16[672,128]{1,0:T(8,128)(2,1)S(1)}, s16[672,128]{1,0:T(8,128)(2,1)S(1)}, u32[]{:S(2)}, u32[]{:S(2)}) collective-permute-start(s16[672,128]{1,0:T(8,128)(2,1)S(1)} %get-tuple-element.52), channel_id=1, source_target_pairs={{0,3},{1,2},{2,1},{3,0},{4,7},{5,6},{6,5},{7,4},{8,11},{9,10},{10,... | collective-permute-start | bytes 516104 | tf_op jit(solution)/shard_map/ppermute | solution.py:1104
  12.4 4.0 %copy-start.9 = (bf16[2,256,240]{2,1,0:T(8,128)(2,1)S(1)}, bf16[2,256,240]{2,1,0:T(8,128)(2,1)}, u32[]{:S(2)}) copy-start(bf16[2,256,240]{2,1,0:T(8,128)(2,1)} %constant.76.clone.refs_2_.refs_5_) | copy-start | bytes 737284
  17.1 17.8 %copy-start.5 = (bf16[4,48,256]{2,1,0:T(8,128)(2,1)S(1)}, bf16[4,48,256]{2,1,0:T(8,128)(2,1)}, u32[]{:S(2)}) copy-start(bf16[4,48,256]{2,1,0:T(8,128)(2,1)} %constant.77.clone.refs_7_.high_ref) | copy-start | bytes 294916
  17.1 17.8 %copy-start.6 = (bf16[4,48,256]{2,1,0:T(8,128)(2,1)S(1)}, bf16[4,48,256]{2,1,0:T(8,128)(2,1)}, u32[]{:S(2)}) copy-start(bf16[4,48,256]{2,1,0:T(8,128)(2,1)} %constant.78.clone.refs_8_.low_ref) | copy-start | bytes 294916
  20.3 6.8 %collective-permute-start.3 = (s16[560,128]{1,0:T(8,128)(2,1)S(1)}, s16[560,128]{1,0:T(8,128)(2,1)S(1)}, u32[]{:S(2)}, u32[]{:S(2)}) collective-permute-start(s16[560,128]{1,0:T(8,128)(2,1)S(1)} %get-tuple-element.55), channel_id=1, source_target_pairs={{0,4},{8,12},{4,0},{12,8},{1,5},{9,13},{5,1},{13,9},{2,6},{10,14},... | collective-permute-start | bytes 430088 | tf_op jit(solution)/shard_map/ppermute | solution.py:1116
  21.9 8.7 %collective-permute-start.5 = (s16[816,128]{1,0:T(8,128)(2,1)S(1)}, s16[816,128]{1,0:T(8,128)(2,1)S(1)}, u32[]{:S(2)}, u32[]{:S(2)}) collective-permute-start(s16[816,128]{1,0:T(8,128)(2,1)S(1)} %get-tuple-element.57), channel_id=1, source_target_pairs={{4,8},{8,4},{5,9},{9,5},{6,10},{10,6},{7,11},{11,7},{20,24},{24,20... | collective-permute-start | bytes 626696 | tf_op jit(solution)/shard_map/ppermute | solution.py:1117
  22.6 8.0 %collective-permute-start.4 = (s16[528,128]{1,0:T(8,128)(2,1)S(1)}, s16[528,128]{1,0:T(8,128)(2,1)S(1)}, u32[]{:S(2)}, u32[]{:S(2)}) collective-permute-start(s16[528,128]{1,0:T(8,128)(2,1)S(1)} %get-tuple-element.56), channel_id=1, source_target_pairs={{0,4},{8,12},{4,0},{12,8},{1,5},{9,13},{5,1},{13,9},{2,6},{10,14},... | collective-permute-start | bytes 405512 | tf_op jit(solution)/shard_map/ppermute | solution.py:1118
  27.1 11.4 %copy-start.13 = (s32[24]{0:T(128)S(1)}, s32[24]{0:T(128)}, u32[]{:S(2)}) copy-start(s32[24]{0:T(128)} %param.21) | copy-start | bytes 292
  27.1 11.4 %copy-start.14 = (s32[24]{0:T(128)S(1)}, s32[24]{0:T(128)}, u32[]{:S(2)}) copy-start(s32[24]{0:T(128)} %param.22) | copy-start | bytes 292
  27.2 7.6 %collective-permute-start.6 = (s16[272,128]{1,0:T(8,128)(2,1)S(1)}, s16[272,128]{1,0:T(8,128)(2,1)S(1)}, u32[]{:S(2)}, u32[]{:S(2)}) collective-permute-start(s16[272,128]{1,0:T(8,128)(2,1)S(1)} %pair_messages.2), channel_id=1, source_target_pairs={{0,8},{4,12},{8,0},{12,4},{1,9},{5,13},{9,1},{13,5},{2,10},{6,14},... | collective-permute-start | bytes 208904 | tf_op jit(solution)/shard_map/ppermute | solution.py:1120
  34.8 6.3 %copy-start.4 = (bf16[24,128,128]{2,1,0:T(8,128)(2,1)S(1)}, bf16[24,128,128]{2,1,0:T(8,128)(2,1)}, u32[]{:S(2)}) copy-start(bf16[24,128,128]{2,1,0:T(8,128)(2,1)} %refs_3_.9) | copy-start | bytes 2359300
  37.8 7.3 %collective-permute-start.9 = (s16[672,128]{1,0:T(8,128)(2,1)S(1)}, s16[672,128]{1,0:T(8,128)(2,1)S(1)}, u32[]{:S(2)}, u32[]{:S(2)}) collective-permute-start(s16[672,128]{1,0:T(8,128)(2,1)S(1)} %get-tuple-element.65), channel_id=1, source_target_pairs={{0,2},{1,3},{2,0},{3,1},{4,6},{5,7},{6,4},{7,5},{8,10},{9,11},{10,... | collective-permute-start | bytes 516104 | tf_op jit(solution)/shard_map/ppermute | solution.py:1104
  39.4 6.2 %collective-permute-start.7 = (s16[672,128]{1,0:T(8,128)(2,1)S(1)}, s16[672,128]{1,0:T(8,128)(2,1)S(1)}, u32[]{:S(2)}, u32[]{:S(2)}) collective-permute-start(s16[672,128]{1,0:T(8,128)(2,1)S(1)} %get-tuple-element.62), channel_id=1, source_target_pairs={{0,1},{1,0},{2,3},{3,2},{4,5},{5,4},{6,7},{7,6},{8,9},{9,8},{10,11... | collective-permute-start | bytes 516104 | tf_op jit(solution)/shard_map/ppermute | solution.py:1104
  39.5 6.7 %collective-permute-start.8 = (s16[672,128]{1,0:T(8,128)(2,1)S(1)}, s16[672,128]{1,0:T(8,128)(2,1)S(1)}, u32[]{:S(2)}, u32[]{:S(2)}) collective-permute-start(s16[672,128]{1,0:T(8,128)(2,1)S(1)} %get-tuple-element.63), channel_id=1, source_target_pairs={{0,3},{1,2},{2,1},{3,0},{4,7},{5,6},{6,5},{7,4},{8,11},{9,10},{10,... | collective-permute-start | bytes 516104 | tf_op jit(solution)/shard_map/ppermute | solution.py:1104
  42.2 3.0 %copy-start.7 = (bf16[4,128,256]{2,1,0:T(8,128)(2,1)S(1)}, bf16[4,128,256]{2,1,0:T(8,128)(2,1)}, u32[]{:S(2)}) copy-start(bf16[4,128,256]{2,1,0:T(8,128)(2,1)} %constant.79.clone.refs_2_.refs_3_) | copy-start | bytes 786436
  42.2 3.0 %copy-start.8 = (bf16[4,128,256]{2,1,0:T(8,128)(2,1)S(1)}, bf16[4,128,256]{2,1,0:T(8,128)(2,1)}, u32[]{:S(2)}) copy-start(bf16[4,128,256]{2,1,0:T(8,128)(2,1)} %constant.80.clone.refs_3_.refs_4_) | copy-start | bytes 786436
  45.1 1.1 %copy-start.11 = (f32[512]{0:T(512)S(1)}, f32[512]{0:T(512)}, u32[]{:S(2)}) copy-start(f32[512]{0:T(512)} %refs_0_.1) | copy-start | bytes 6148
  45.1 1.1 %copy-start.12 = (s32[512]{0:T(512)S(1)}, s32[512]{0:T(512)}, u32[]{:S(2)}) copy-start(s32[512]{0:T(512)} %param.17) | copy-start | bytes 6148
  46.2 2.9 %copy-start.1 = (bf16[4,256,128]{2,1,0:T(8,128)(2,1)S(1)}, bf16[4,256,128]{2,1,0:T(8,128)(2,1)}, u32[]{:S(2)}) copy-start(bf16[4,256,128]{2,1,0:T(8,128)(2,1)} %constant.74.clone.refs_2_.high_ref.refs_3_) | copy-start | bytes 786436
  46.2 2.9 %copy-start.3 = (bf16[4,256,128]{2,1,0:T(8,128)(2,1)S(1)}, bf16[4,256,128]{2,1,0:T(8,128)(2,1)}, u32[]{:S(2)}) copy-start(bf16[4,256,128]{2,1,0:T(8,128)(2,1)} %constant.75.clone.refs_3_.low_ref.refs_4_) | copy-start | bytes 786436
  52.0 7.3 %collective-permute-start.11 = (s16[672,128]{1,0:T(8,128)(2,1)S(1)}, s16[672,128]{1,0:T(8,128)(2,1)S(1)}, u32[]{:S(2)}, u32[]{:S(2)}) collective-permute-start(s16[672,128]{1,0:T(8,128)(2,1)S(1)} %get-tuple-element.72), channel_id=1, source_target_pairs={{0,2},{1,3},{2,0},{3,1},{4,6},{5,7},{6,4},{7,5},{8,10},{9,11},{10,... | collective-permute-start | bytes 516104 | tf_op jit(solution)/shard_map/ppermute | solution.py:1104
  53.9 6.0 %collective-permute-start.10 = (s16[672,128]{1,0:T(8,128)(2,1)S(1)}, s16[672,128]{1,0:T(8,128)(2,1)S(1)}, u32[]{:S(2)}, u32[]{:S(2)}) collective-permute-start(s16[672,128]{1,0:T(8,128)(2,1)S(1)} %get-tuple-element.71), channel_id=1, source_target_pairs={{0,1},{1,0},{2,3},{3,2},{4,5},{5,4},{6,7},{7,6},{8,9},{9,8},{10,11... | collective-permute-start | bytes 516104 | tf_op jit(solution)/shard_map/ppermute | solution.py:1104
  54.1 8.9 %collective-permute-start.12 = (s16[672,128]{1,0:T(8,128)(2,1)S(1)}, s16[672,128]{1,0:T(8,128)(2,1)S(1)}, u32[]{:S(2)}, u32[]{:S(2)}) collective-permute-start(s16[672,128]{1,0:T(8,128)(2,1)S(1)} %get-tuple-element.73), channel_id=1, source_target_pairs={{0,3},{1,2},{2,1},{3,0},{4,7},{5,6},{6,5},{7,4},{8,11},{9,10},{10,... | collective-permute-start | bytes 516104 | tf_op jit(solution)/shard_map/ppermute | solution.py:1104
  64.9 5.9 %collective-permute-start.13 = (s16[560,128]{1,0:T(8,128)(2,1)S(1)}, s16[560,128]{1,0:T(8,128)(2,1)S(1)}, u32[]{:S(2)}, u32[]{:S(2)}) collective-permute-start(s16[560,128]{1,0:T(8,128)(2,1)S(1)} %get-tuple-element.75), channel_id=1, source_target_pairs={{0,4},{8,12},{4,0},{12,8},{1,5},{9,13},{5,1},{13,9},{2,6},{10,14},... | collective-permute-start | bytes 430088 | tf_op jit(solution)/shard_map/ppermute | solution.py:1116
  64.9 8.6 %collective-permute-start.15 = (s16[816,128]{1,0:T(8,128)(2,1)S(1)}, s16[816,128]{1,0:T(8,128)(2,1)S(1)}, u32[]{:S(2)}, u32[]{:S(2)}) collective-permute-start(s16[816,128]{1,0:T(8,128)(2,1)S(1)} %get-tuple-element.77), channel_id=1, source_target_pairs={{4,8},{8,4},{5,9},{9,5},{6,10},{10,6},{7,11},{11,7},{20,24},{24,20... | collective-permute-start | bytes 626696 | tf_op jit(solution)/shard_map/ppermute | solution.py:1117
  65.8 7.8 %collective-permute-start.14 = (s16[528,128]{1,0:T(8,128)(2,1)S(1)}, s16[528,128]{1,0:T(8,128)(2,1)S(1)}, u32[]{:S(2)}, u32[]{:S(2)}) collective-permute-start(s16[528,128]{1,0:T(8,128)(2,1)S(1)} %get-tuple-element.76), channel_id=1, source_target_pairs={{0,4},{8,12},{4,0},{12,8},{1,5},{9,13},{5,1},{13,9},{2,6},{10,14},... | collective-permute-start | bytes 405512 | tf_op jit(solution)/shard_map/ppermute | solution.py:1118
  70.9 7.3 %collective-permute-start.16 = (s16[272,128]{1,0:T(8,128)(2,1)S(1)}, s16[272,128]{1,0:T(8,128)(2,1)S(1)}, u32[]{:S(2)}, u32[]{:S(2)}) collective-permute-start(s16[272,128]{1,0:T(8,128)(2,1)S(1)} %pair_messages.3), channel_id=1, source_target_pairs={{0,8},{4,12},{8,0},{12,4},{1,9},{5,13},{9,1},{13,5},{2,10},{6,14},... | collective-permute-start | bytes 208904 | tf_op jit(solution)/shard_map/ppermute | solution.py:1120
  81.1 6.5 %collective-permute-start.19 = (s16[672,128]{1,0:T(8,128)(2,1)S(1)}, s16[672,128]{1,0:T(8,128)(2,1)S(1)}, u32[]{:S(2)}, u32[]{:S(2)}) collective-permute-start(s16[672,128]{1,0:T(8,128)(2,1)S(1)} %get-tuple-element.85), channel_id=1, source_target_pairs={{0,2},{1,3},{2,0},{3,1},{4,6},{5,7},{6,4},{7,5},{8,10},{9,11},{10,... | collective-permute-start | bytes 516104 | tf_op jit(solution)/shard_map/ppermute | solution.py:1104
  82.3 5.8 %collective-permute-start.17 = (s16[672,128]{1,0:T(8,128)(2,1)S(1)}, s16[672,128]{1,0:T(8,128)(2,1)S(1)}, u32[]{:S(2)}, u32[]{:S(2)}) collective-permute-start(s16[672,128]{1,0:T(8,128)(2,1)S(1)} %get-tuple-element.82), channel_id=1, source_target_pairs={{0,1},{1,0},{2,3},{3,2},{4,5},{5,4},{6,7},{7,6},{8,9},{9,8},{10,11... | collective-permute-start | bytes 516104 | tf_op jit(solution)/shard_map/ppermute | solution.py:1104
  82.4 6.9 %collective-permute-start.18 = (s16[672,128]{1,0:T(8,128)(2,1)S(1)}, s16[672,128]{1,0:T(8,128)(2,1)S(1)}, u32[]{:S(2)}, u32[]{:S(2)}) collective-permute-start(s16[672,128]{1,0:T(8,128)(2,1)S(1)} %get-tuple-element.83), channel_id=1, source_target_pairs={{0,3},{1,2},{2,1},{3,0},{4,7},{5,6},{6,5},{7,4},{8,11},{9,10},{10,... | collective-permute-start | bytes 516104 | tf_op jit(solution)/shard_map/ppermute | solution.py:1104

commit v11 on v10

--- a/solution.py
+++ b/solution.py
@@ -176,34 +176,28 @@
     )
 
 
-def weave(flag, sample_refs, dipole_refs, source_out, sample_out):
+def mixing_matrix():
     place = lax.broadcasted_iota(jnp.int32, (4 * BLOCK, 4 * BLOCK), 0)
     lane = lax.broadcasted_iota(jnp.int32, (4 * BLOCK, 4 * BLOCK), 1)
-    wanted = 4 * (place % BLOCK) + place // BLOCK
-    mixing = jnp.where(lane == wanted, 1.0, 0.0).astype(BF16)
-    stacked = []
-    for tile, (sample_ref, dipole_ref) in enumerate(zip(sample_refs, dipole_refs)):
-        charged = flag[:, tile * BLOCK : (tile + 1) * BLOCK] == 1
-        rows = []
-        for depth in range(4):
-            sample = sample_ref[pl.ds(depth, 16, stride=4), :]
-            dipole = dipole_ref[pl.ds(depth, 16, stride=4), :]
-            rows.append(jnp.concatenate([jnp.where(charged, -sample, dipole), sample], axis=0))
-        stacked.append(jnp.concatenate(rows, axis=1))
-    weights = jnp.concatenate(stacked, axis=0)
+    return jnp.where(lane == 4 * (place % BLOCK) + place // BLOCK, 1.0, 0.0).astype(BF16)
+
+
+def weave(tiles, mixing, out):
+    weights = jnp.concatenate([jnp.concatenate(tile, axis=1) for tile in tiles], axis=0)
     first, rest = split(weights)
     second, third = split(weights - first.astype(F32))
     woven = dot(first, mixing) + (dot(second, mixing) + dot(third, mixing))
-    for tile in range(len(sample_refs)):
-        for which, out in enumerate((source_out, sample_out)):
-            for part in range(BLOCK // GROUP):
-                at = (tile * (BLOCK // GROUP) + part) * 16
-                lanes = slice(part * BLOCK, (part + 1) * BLOCK)
-                for a in range(4):
-                    row = tile * 32 + which * 16 + 4 * a
-                    out[pl.ds(at + 8 * (a // 2) + a % 2, 4, stride=2), :] = woven[
-                        row : row + 4, lanes
-                    ]
+    for tile in range(len(tiles)):
+        for part in range(BLOCK // GROUP):
+            at = (tile * (BLOCK // GROUP) + part) * 16
+            lanes = slice(part * BLOCK, (part + 1) * BLOCK)
+            for a in range(4):
+                row = tile * 16 + 4 * a
+                out[pl.ds(at + 8 * (a // 2) + a % 2, 4, stride=2), :] = woven[row : row + 4, lanes]
+
+
+def by_depth(ref):
+    return [ref[pl.ds(depth, 16, stride=4), :] for depth in range(4)]
 
 
 def pair_rows(x, reach_x, reach_y):
@@ -286,7 +280,7 @@
     vector_ref, *remote = refs[:8]
     refs = refs[8:]
     outs, refs = refs[: len(flips)], refs[len(flips) :]
-    wides, (weight_ref, sample_coeff_ref, places_out), refs = refs[:2], refs[2:5], refs[5:]
+    wides, (weight_ref, places_out), refs = refs[:2], refs[2:4], refs[4:]
     rounded, high, low, stencil, flag, samples, dipoles = refs[:7]
     place_ref, sems, head, total = refs[7:11]
     grids = refs[11:]
@@ -310,6 +304,7 @@
         copy.start()
     for grid in grids:
         grid[...] = jnp.zeros_like(grid)
+    mixing = mixing_matrix()
     copies[0].wait()
     span_x, span_y = reach_x - 4, reach_y - 4
     local_x = stencil[0:1, :] - (lax.axis_index("wide") * span_x - 2)
@@ -321,8 +316,12 @@
     to_scalar.start()
     for copy in copies[1:needed_first]:
         copy.wait()
-    each = lambda values: [values.at[tile] for tile in range(tiles)]
-    weave(flag[...], each(samples), each(dipoles), weight_ref, sample_coeff_ref)
+    sources = []
+    for tile in range(tiles):
+        charged = flag[:, tile * BLOCK : (tile + 1) * BLOCK] == 1
+        pairs = zip(by_depth(samples.at[tile]), by_depth(dipoles.at[tile]))
+        sources.append([jnp.where(charged, -sample, dipole) for sample, dipole in pairs])
+    weave(sources, mixing, weight_ref)
     to_scalar.wait()
     add_panels(reach_y, True, vector_ref, place_ref, weight_ref, grids)
     for copy in copies[needed_first:]:
@@ -379,13 +378,12 @@
         pinned = [pltpu.with_memory_space_constraint(value, pltpu.HBM) for value in operands[1:]]
         operands = [vector] + pinned
         in_specs = [in_smem()] + [pl.BlockSpec(memory_space=pltpu.HBM)] * 7
-        out_shapes += [jax.ShapeDtypeStruct(woven, F32)] * 2
+        out_shapes += [jax.ShapeDtypeStruct(woven, F32)]
         out_shapes += [jax.ShapeDtypeStruct((2, count), jnp.int32)]
+        out_shapes += [jax.ShapeDtypeStruct(rounded.shape, F32)]
+        out_shapes += [jax.ShapeDtypeStruct(values.shape, BF16) for values in table]
         tiled = pltpu.VMEM((blocks, 64, BLOCK), F32)
         work = [
-            pltpu.VMEM(rounded.shape, F32),
-            pltpu.VMEM(table[0].shape, BF16),
-            pltpu.VMEM(table[1].shape, BF16),
             pltpu.VMEM(stencil.shape, jnp.int32),
             pltpu.VMEM((1, count), jnp.int32),
             tiled,
@@ -418,8 +416,8 @@
     send_pieces(outs, flips, head, rounded_ref[...], both, high_ref, low_ref)
 
 
-def spread_rest(vector, both, table, flips):
-    blocks = vector.shape[0] // BLOCK
+def spread_rest(rounded, both, table, flips):
+    blocks = rounded.shape[0]
     top = up_to(2 + 2 * blocks, 16)
     shape = (top + both[0].shape[0], 2 * HALF)
     return pl.pallas_call(
@@ -431,7 +429,7 @@
         compiler_params=params(),
         cost_estimate=cost(2 * shape[0] * 256 * 256 * 3, 4 * shape[0] * 512),
         name="spread_rest",
-    )(vector.reshape(blocks, BLOCK), *both, *table)
+    )(rounded, *both, *table)
 
 
 def lines_kernel(place_ref, coeff_ref, *refs):
@@ -452,6 +450,30 @@
         return carry
 
     lax.fori_loop(0, place_ref.shape[1] // GROUP, body, 0)
+
+
+def sample_lines_kernel(tiles, place_ref, *refs):
+    out_ref, coeff = refs[-2:]
+    weave([by_depth(ref) for ref in refs[:tiles]], mixing_matrix(), coeff)
+    lines_kernel(place_ref, coeff, out_ref)
+
+
+def place_sample_lines(places, sample):
+    count = places.shape[1]
+    blocks = count // BLOCK
+    tile = lambda t: pl.BlockSpec((64, BLOCK), lambda i: (0, t))
+    shape = (count * 16, REGION)
+    return pl.pallas_call(
+        functools.partial(sample_lines_kernel, blocks),
+        grid=(1,),
+        in_specs=[in_smem()] + [tile(t) for t in range(blocks)],
+        out_specs=pl.BlockSpec(shape, lambda i: (0, 0)),
+        out_shape=jax.ShapeDtypeStruct(shape, F32),
+        scratch_shapes=[pltpu.VMEM((count // GROUP * 16, BLOCK), F32)],
+        compiler_params=params(),
+        cost_estimate=cost(16 * count * REGION, 4 * 16 * count * REGION),
+        name="place_sample_lines",
+    )(places, *[sample] * blocks)
 
 
 def place_lines(places, coeff, awaited):
@@ -1092,8 +1114,7 @@
     odd_swap = swaps([(i, i + 1) for i in range(1, x_count - 1, 2)])
     far_flips = list(range(2, x_count, 2))
 
-    first = list(range(pair, y_count, pair))
-    rest = [flip for flip in range(y_count) if flip not in first]
+    first, rest = list(range(pair, y_count)), list(range(pair))
     same_core = list(range(0, y_count, pair))
     other_core = [flip for flip in range(y_count) if flip not in same_core]
 
@@ -1107,8 +1128,8 @@
     def chosen(parts, flips):
         return [parts[flip] for flip in flips]
 
-    def convolve_and_sample(last, vector, sent, both, places, sample_lines, awaited):
-        arrived = turned(sent, spread_rest(vector, both, z_forward, rest))
+    def convolve_and_sample(last, vector, sent, both, table, places, sample_lines, awaited):
+        arrived = turned(sent, spread_rest(vector, both, table, rest))
         early = forward_early(chosen(arrived, same_core), y_forward, reach_x, reach_y)
         spectrum, even_message, layers, odd_message, own, peers, inner = forward(
             arrived, early, y_forward, modes, reach_x, reach_y, blocks, awaited
@@ -1158,20 +1179,27 @@
         return image, near_part
 
     raw = (stencil_base, surface_flag, sample_weights, dipole_weights)
-    *sent, high, low, source_coeff, sample_coeff, places = spread(
+    *sent, wide_high, wide_low, source_coeff, places, vector, high, low = spread(
         density, z_forward, None, raw, reach_x, reach_y, first
     )
-    sample_lines = place_lines(places, sample_coeff, [])
-    first_image, near_part = convolve_and_sample(
-        False, density, sent, (high, low), places, sample_lines, [sample_lines]
+    z_forward = (high, low)
+    sample_lines = place_sample_lines(places, sample_weights)
+    vector, near_part = convolve_and_sample(
+        False,
+        vector,
+        sent,
+        (wide_high, wide_low),
+        z_forward,
+        places,
+        sample_lines,
+        [sample_lines],
     )
-    first_image = first_image.reshape(-1)
     source_lines = place_lines(places, source_coeff, [near_part])
-    *sent, high, low = spread(
-        first_image, z_forward, (places, source_lines), None, reach_x, reach_y, first
+    *sent, wide_high, wide_low = spread(
+        vector.reshape(-1), z_forward, (places, source_lines), None, reach_x, reach_y, first
     )
     both_images, _ = convolve_and_sample(
-        True, first_image, sent, (high, low), places, sample_lines, []
+        True, vector, sent, (wide_high, wide_low), z_forward, places, sample_lines, []
     )
     return both_images
 

time: 93.5 us -> 92.1 us (0.985)
  local copies, waits for them, and re-layouts: 3.71 us -> 2.02 us
    pallas_call x0 -> x1, Pallas kernels: none -> 3.41 us  [place_sample_lines(): pl.pallas_call(functools.partial(sample_lines_kernel, blocks), grid=(1,),...]
    pallas_call x2 -> x1, Pallas kernels: 5.89 us -> 2.95 us  [place_lines(): pl.pallas_call(lines_kernel, in_specs=[in_smem(), whole_vmem()] + [anywhe...]
    unnamed x30 -> x20, local copies, waits for them, and re-layouts: 2.63 us -> 0.94 us
where the time goes in v11:
time: 92.1 us; the launch traced here: 91.9 us
  Pallas kernels  38.6 us (42%)
  starting transfers between devices  26 us (28%)
  waiting for transfers between devices  24.9 us (27%)
  local copies, waits for them, and re-layouts  2.02 us (2%)
    ppermute x12, waiting for transfers between devices, turned(): lax.ppermute(part, Y_AXES, swap_pairs)  12.7 us
    ppermute x12, starting transfers between devices, turned(): lax.ppermute(part, Y_AXES, swap_pairs)  10.1 us
    ppermute x2, starting transfers between devices, convolve_and_sample(): even_layers = lax.ppermute(layers, 'wide', even_swap)  9.13 us
    pallas_call x2, Pallas kernels, spread(): pl.pallas_call(functools.partial(start_kernel if placed is None else spre...  8.52 us
    ppermute x2, waiting for transfers between devices, convolve_and_sample(): lax.ppermute(message, 'wide', [(i, i ^ flip) for i in range(x_count)])  8.37 us
    pallas_call x2, Pallas kernels, sample(): pl.pallas_call(functools.partial(sample_kernel, last, reach_x, reach_y, f...  6.49 us
    pallas_call x2, Pallas kernels, inverse(): pl.pallas_call(functools.partial(inverse_kernel, reach_x, reach_y, flips,...  6.08 us
    pallas_call x2, Pallas kernels, forward(): pl.pallas_call(functools.partial(forward_kernel, reach_x, reach_y, blocks...  3.77 us
  transfers between devices with their start and end apart: 20, of which 11 were waited for; matrix products, arithmetic and copies ran while one was open for 1% of the time, Pallas kernels for 15%

profile of v11, /device:TPU:0, one launch (start us, length us, event | category | flops | bytes accessed | tf_op | source)
XLA Modules:
  0.0 91.9 jit_solution(16616412073116333534)
XLA Ops:
  0.0 5.7 %start.1 = (s16[672,128]{1,0:T(8,128)(2,1)S(1)}, s16[672,128]{1,0:T(8,128)(2,1)S(1)}, bf16[656,256]{1,0:T(8,128)(2,1)S(1)}, bf16[656,256]{1,0:T(8,128)(2,1)S(1)}...) custom-call(f32[512]{0:T(512)} %refs_0_.2, ...), custom_call_target="tpu_custom_call" | custom-call | flops 169869312 | bytes 4194304 | tf_op jit(solution)/shard_map/start/pallas_call | solution.py:397
  5.7 3.0 %collective-permute-start.1 = (s16[672,128]{1,0:T(8,128)(2,1)S(1)}, s16[672,128]{1,0:T(8,128)(2,1)S(1)}, u32[]{:S(2)}, u32[]{:S(2)}) collective-permute-start(s16[672,128]{1,0:T(8,128)(2,1)S(1)} %get-tuple-element.56), channel_id=1, source_target_pairs={{0,2},{1,3},{2,0},{3,1},{4,6},{5,7},{6,4},{7,5},{8,10},{9,11},{10,... | collective-permute-start | bytes 516104 | tf_op jit(solution)/shard_map/ppermute | solution.py:1125
  8.7 0.6 spread_rest.2
  9.3 0.1 collective-permute-start
  9.4 0.1 collective-permute-start.2
  9.5 0.9 copy-done
  10.4 3.4 %place_sample_lines.1.refs_7_.refs_5_ = f32[8192,128]{1,0:T(8,128)S(1)} custom-call(s32[2,512]{1,0:T(2,128)S(1)} %get-tuple-element.48.place_ref.refs_1_, f32[64,512]{1,0:T(8,128)S(1)} %copy-done, f32[64,512]{1,0:T(8,128)S(1)} %copy-done, f32[64,512]{1,0:T(8,128)S(1)} %copy-done, f32[64,512]{1,0:T(8,128)S(1)} %copy-done), custom_call_target="tpu_custom_call" | custom-call | flops 1048576 | bytes 4194304 | tf_op jit(solution)/shard_map/place_sample_lines/pallas_call | solution.py:466
  13.8 1.1 %dynamic-slice_bitcast_fusion.refs_6_.modes_ref.refs_9_ = f32[4,256,128]{2,1,0:T(8,128)S(1)} fusion(f32[4,4,256,128]{3,2,1,0:T(8,128)} %constant.73.clone, s32[]{:T(128)S(6)} %select_n.30), kind=kLoop, calls=%fused_computation | loop fusion | bytes 1048580 | tf_op jit(solution)/shard_map/jit(dynamic_index_in_dim)/squeeze | solution.py:1102
  14.9 0.0 collective-permute-done.1.refs_1_.refs_2_
  14.9 0.7 forward_early.2.refs_4_
  15.6 0.0 copy-start.2
  15.6 0.0 copy-start.3
  15.6 0.0 collective-permute-done.refs_1_
  15.6 0.6 collective-permute-done.2.refs_3_
  16.2 1.9 %forward.2 = (f32[18,256,128]{2,1,0:T(8,128)S(1)}, s16[560,128]{1,0:T(8,128)(2,1)S(1)}, s16[528,128]{1,0:T(8,128)(2,1)S(1)}, s16[816,128]{1,0:T(8,128)(2,1)S(1)}...) custom-call(s16[672,128]{1,0:T(8,128)(2,1)S(1)} %get-tuple-element.54.refs_0_, ...), custom_call_target="tpu_custom_call" | custom-call | flops 301989888 | bytes 4718592 | tf_op jit(solution)/shard_map/forward/pallas_call | solution.py:655
  18.1 1.6 %collective-permute-start.3 = (s16[560,128]{1,0:T(8,128)(2,1)S(1)}, s16[560,128]{1,0:T(8,128)(2,1)S(1)}, u32[]{:S(2)}, u32[]{:S(2)}) collective-permute-start(s16[560,128]{1,0:T(8,128)(2,1)S(1)} %get-tuple-element.59), channel_id=1, source_target_pairs={{0,4},{8,12},{4,0},{12,8},{1,5},{9,13},{5,1},{13,9},{2,6},{10,14},... | collective-permute-start | bytes 430088 | tf_op jit(solution)/shard_map/ppermute | solution.py:1137
  19.7 0.7 collective-permute-start.5
  20.4 4.4 %collective-permute-start.4 = (s16[528,128]{1,0:T(8,128)(2,1)S(1)}, s16[528,128]{1,0:T(8,128)(2,1)S(1)}, u32[]{:S(2)}, u32[]{:S(2)}) collective-permute-start(s16[528,128]{1,0:T(8,128)(2,1)S(1)} %get-tuple-element.60), channel_id=1, source_target_pairs={{0,4},{8,12},{4,0},{12,8},{1,5},{9,13},{5,1},{13,9},{2,6},{10,14},... | collective-permute-start | bytes 405512 | tf_op jit(solution)/shard_map/ppermute | solution.py:1139
  24.8 0.0 collective-permute-done.3.even_ref.refs_1_.refs_0_
  24.8 0.1 pair_messages.2
  24.9 2.3 %collective-permute-start.6 = (s16[272,128]{1,0:T(8,128)(2,1)S(1)}, s16[272,128]{1,0:T(8,128)(2,1)S(1)}, u32[]{:S(2)}, u32[]{:S(2)}) collective-permute-start(s16[272,128]{1,0:T(8,128)(2,1)S(1)} %pair_messages.2), channel_id=1, source_target_pairs={{0,8},{4,12},{8,0},{12,4},{1,9},{5,13},{9,1},{13,5},{2,10},{6,14},... | collective-permute-start | bytes 208904 | tf_op jit(solution)/shard_map/ppermute | solution.py:1141
  27.3 1.4 %collective-permute-done.4.refs_2_ = s16[528,128]{1,0:T(8,128)(2,1)S(1)} collective-permute-done((s16[528,128]{1,0:T(8,128)(2,1)S(1)}, s16[528,128]{1,0:T(8,128)(2,1)S(1)}, u32[]{:S(2)}, u32[]{:S(2)}) %collective-permute-start.4) | collective-permute-done | bytes 135200 | tf_op jit(solution)/shard_map/ppermute | solution.py:1139
  28.7 4.2 %collective-permute-done.6.refs_6_ = s16[272,128]{1,0:T(8,128)(2,1)S(1)} collective-permute-done((s16[272,128]{1,0:T(8,128)(2,1)S(1)}, s16[272,128]{1,0:T(8,128)(2,1)S(1)}, u32[]{:S(2)}, u32[]{:S(2)}) %collective-permute-start.6) | collective-permute-done | bytes 69664 | tf_op jit(solution)/shard_map/ppermute | solution.py:1141
  32.9 3.0 %inverse.2 = (s16[672,128]{1,0:T(8,128)(2,1)S(1)}, s16[672,128]{1,0:T(8,128)(2,1)S(1)}, bf16[18,256,128]{2,1,0:T(8,128)(2,1)S(1)}, bf16[18,256,128]{2,1,0:T(8,128)(2,1)S(1)}) custom-call(f32[18,256,128]{2,1,0:T(8,128)S(1)} %get-tuple-element.58.refs_0_, s16[560,128]{1,0:T(8,128)(2,1)S(1)} %collective-permute-done.3.even_ref.refs_1_.refs_0_, ...), custom_call_target="tpu_custom_call" | custom-call | flops 301989888 | bytes 4718592 | tf_op jit(solution)/shard_map/inverse/pallas_call | solution.py:863
  35.9 1.6 %collective-permute-start.9 = (s16[672,128]{1,0:T(8,128)(2,1)S(1)}, s16[672,128]{1,0:T(8,128)(2,1)S(1)}, u32[]{:S(2)}, u32[]{:S(2)}) collective-permute-start(s16[672,128]{1,0:T(8,128)(2,1)S(1)} %get-tuple-element.69), channel_id=1, source_target_pairs={{0,2},{1,3},{2,0},{3,1},{4,6},{5,7},{6,4},{7,5},{8,10},{9,11},{10,... | collective-permute-start | bytes 516104 | tf_op jit(solution)/shard_map/ppermute | solution.py:1125
  37.5 0.9 inverse_rest.2
  38.4 0.1 collective-permute-start.7
  38.5 0.6 collective-permute-start.8
  39.1 1.0 %near_field.2.refs_8_.refs_0_ = f32[8,128]{1,0:T(8,128)S(1)} custom-call(s32[24]{0:T(128)S(1)} %get-tuple-element.92.place_ref, s32[24]{0:T(128)S(1)} %get-tuple-element.91.target_ref, s16[560,128]{1,0:T(8,128)(2,1)S(1)} %collective-permute-done.3.even_ref.refs_1_.refs_0_, s16[816,128]{1,0:T(8,128)(2,1)S(1)} %collective-permute-done.5.refs_3_.refs_1_, ...), custom_call_target="tpu_custom_call" | custom-call | flops 12582912 | bytes 786432 | tf_op jit(solution)/shard_map/near_field/pallas_call | solution.py:1059
  40.2 0.0 copy-start.5
  40.2 3.0 %place_lines.1.refs_5_ = f32[8192,128]{1,0:T(8,128)S(1)} custom-call(s32[2,512]{1,0:T(2,128)S(1)} %get-tuple-element.48.place_ref.refs_1_, f32[256,128]{1,0:T(8,128)S(1)} %get-tuple-element.71.coeff_ref, f32[8,128]{1,0:T(8,128)S(1)} %near_field.2.refs_8_.refs_0_), custom_call_target="tpu_custom_call" | custom-call | flops 1048576 | bytes 4194304 | tf_op jit(solution)/shard_map/place_lines/pallas_call | solution.py:482
  43.1 0.0 collective-permute-done.9.refs_1_
  43.2 0.5 sample_early.2.refs_2_
  43.6 1.6 %collective-permute-done.8.refs_1_ = s16[672,128]{1,0:T(8,128)(2,1)S(1)} collective-permute-done((s16[672,128]{1,0:T(8,128)(2,1)S(1)}, s16[672,128]{1,0:T(8,128)(2,1)S(1)}, u32[]{:S(2)}, u32[]{:S(2)}) %collective-permute-start.8) | collective-permute-done | bytes 172064 | tf_op jit(solution)/shard_map/ppermute | solution.py:1125
  45.3 2.9 %sample.2.refs_2_.rounded_ref.refs_7_ = f32[4,128]{1,0:T(4,128)S(1)} custom-call(s32[2,512]{1,0:T(2,128)S(1)} %get-tuple-element.48.place_ref.refs_1_, s16[672,128]{1,0:T(8,128)(2,1)S(1)} %collective-permute-done.7.refs_0_, s16[672,128]{1,0:T(8,128)(2,1)S(1)} %collective-permute-done.8.refs_1_, f32[656,256]{1,0:T(8,128)S(1)} %sample_early.2.refs_2_, ...), custom_call_target="tpu_custom_call" | custom-call | flops 169869312 | bytes 4194304 | tf_op jit(solution)/shard_map/sample/pallas_call | solution.py:1003
  48.2 2.8 %spread.1 = (s16[672,128]{1,0:T(8,128)(2,1)S(1)}, s16[672,128]{1,0:T(8,128)(2,1)S(1)}, bf16[656,256]{1,0:T(8,128)(2,1)S(1)}, bf16[656,256]{1,0:T(8,128)(2,1)S(1)}) custom-call(f32[512]{0:T(512)S(1)} %bitcast.6, s32[2,512]{1,0:T(2,128)S(1)} %get-tuple-element.48.place_ref.refs_1_, f32[4,128]{1,0:T(4,128)S(1)} %sample.2.refs_2_.rounded_ref.refs_7_, ...), custom_call_target="tpu_custom_call" | custom-call | flops 169869312 | bytes 4194304 | tf_op jit(solution)/shard_map/spread/pallas_call | solution.py:397
  51.1 1.0 %collective-permute-start.11 = (s16[672,128]{1,0:T(8,128)(2,1)S(1)}, s16[672,128]{1,0:T(8,128)(2,1)S(1)}, u32[]{:S(2)}, u32[]{:S(2)}) collective-permute-start(s16[672,128]{1,0:T(8,128)(2,1)S(1)} %get-tuple-element.76), channel_id=1, source_target_pairs={{0,2},{1,3},{2,0},{3,1},{4,6},{5,7},{6,4},{7,5},{8,10},{9,11},{10,... | collective-permute-start | bytes 516104 | tf_op jit(solution)/shard_map/ppermute | solution.py:1125
  52.0 0.6 spread_rest.3
  52.6 0.7 collective-permute-start.10
  53.3 0.6 collective-permute-start.12
  53.9 4.4 %collective-permute-done.11.refs_1_.refs_2_ = s16[672,128]{1,0:T(8,128)(2,1)S(1)} collective-permute-done((s16[672,128]{1,0:T(8,128)(2,1)S(1)}, s16[672,128]{1,0:T(8,128)(2,1)S(1)}, u32[]{:S(2)}, u32[]{:S(2)}) %collective-permute-start.11) | collective-permute-done | bytes 172064 | tf_op jit(solution)/shard_map/ppermute | solution.py:1125
  58.3 0.7 forward_early.3.refs_4_
  59.0 1.9 %collective-permute-done.12.refs_3_ = s16[672,128]{1,0:T(8,128)(2,1)S(1)} collective-permute-done((s16[672,128]{1,0:T(8,128)(2,1)S(1)}, s16[672,128]{1,0:T(8,128)(2,1)S(1)}, u32[]{:S(2)}, u32[]{:S(2)}) %collective-permute-start.12) | collective-permute-done | bytes 172064 | tf_op jit(solution)/shard_map/ppermute | solution.py:1125
  60.8 1.9 %forward.3 = (f32[18,256,128]{2,1,0:T(8,128)S(1)}, s16[560,128]{1,0:T(8,128)(2,1)S(1)}, s16[528,128]{1,0:T(8,128)(2,1)S(1)}, s16[816,128]{1,0:T(8,128)(2,1)S(1)}...) custom-call(s16[672,128]{1,0:T(8,128)(2,1)S(1)} %get-tuple-element.74.refs_0_, ...), custom_call_target="tpu_custom_call" | custom-call | flops 301989888 | bytes 4718592 | tf_op jit(solution)/shard_map/forward/pallas_call | solution.py:655
  62.7 0.1 collective-permute-start.13
  62.8 0.9 collective-permute-start.15
  63.7 4.7 %collective-permute-start.14 = (s16[528,128]{1,0:T(8,128)(2,1)S(1)}, s16[528,128]{1,0:T(8,128)(2,1)S(1)}, u32[]{:S(2)}, u32[]{:S(2)}) collective-permute-start(s16[528,128]{1,0:T(8,128)(2,1)S(1)} %get-tuple-element.80), channel_id=1, source_target_pairs={{0,4},{8,12},{4,0},{12,8},{1,5},{9,13},{5,1},{13,9},{2,6},{10,14},... | collective-permute-start | bytes 405512 | tf_op jit(solution)/shard_map/ppermute | solution.py:1139
  68.3 0.5 collective-permute-done.13.even_ref.refs_1_.refs_0_
  68.9 0.1 pair_messages.3
  69.0 1.3 %collective-permute-start.16 = (s16[272,128]{1,0:T(8,128)(2,1)S(1)}, s16[272,128]{1,0:T(8,128)(2,1)S(1)}, u32[]{:S(2)}, u32[]{:S(2)}) collective-permute-start(s16[272,128]{1,0:T(8,128)(2,1)S(1)} %pair_messages.3), channel_id=1, source_target_pairs={{0,8},{4,12},{8,0},{12,4},{1,9},{5,13},{9,1},{13,5},{2,10},{6,14},... | collective-permute-start | bytes 208904 | tf_op jit(solution)/shard_map/ppermute | solution.py:1141
  70.3 1.8 %collective-permute-done.14.refs_2_ = s16[528,128]{1,0:T(8,128)(2,1)S(1)} collective-permute-done((s16[528,128]{1,0:T(8,128)(2,1)S(1)}, s16[528,128]{1,0:T(8,128)(2,1)S(1)}, u32[]{:S(2)}, u32[]{:S(2)}) %collective-permute-start.14) | collective-permute-done | bytes 135200 | tf_op jit(solution)/shard_map/ppermute | solution.py:1139
  72.1 0.0 collective-permute-done.15.refs_3_.refs_1_
  72.1 4.2 %collective-permute-done.16.refs_6_ = s16[272,128]{1,0:T(8,128)(2,1)S(1)} collective-permute-done((s16[272,128]{1,0:T(8,128)(2,1)S(1)}, s16[272,128]{1,0:T(8,128)(2,1)S(1)}, u32[]{:S(2)}, u32[]{:S(2)}) %collective-permute-start.16) | collective-permute-done | bytes 69664 | tf_op jit(solution)/shard_map/ppermute | solution.py:1141
  76.3 3.0 %inverse.3 = (s16[672,128]{1,0:T(8,128)(2,1)S(1)}, s16[672,128]{1,0:T(8,128)(2,1)S(1)}, bf16[18,256,128]{2,1,0:T(8,128)(2,1)S(1)}, bf16[18,256,128]{2,1,0:T(8,128)(2,1)S(1)}) custom-call(f32[18,256,128]{2,1,0:T(8,128)S(1)} %get-tuple-element.78.refs_0_, s16[560,128]{1,0:T(8,128)(2,1)S(1)} %collective-permute-done.13.even_ref.refs_1_.refs_0_, ...), custom_call_target="tpu_custom_call" | custom-call | flops 301989888 | bytes 4718592 | tf_op jit(solution)/shard_map/inverse/pallas_call | solution.py:863
  79.4 1.8 %collective-permute-start.19 = (s16[672,128]{1,0:T(8,128)(2,1)S(1)}, s16[672,128]{1,0:T(8,128)(2,1)S(1)}, u32[]{:S(2)}, u32[]{:S(2)}) collective-permute-start(s16[672,128]{1,0:T(8,128)(2,1)S(1)} %get-tuple-element.89), channel_id=1, source_target_pairs={{0,2},{1,3},{2,0},{3,1},{4,6},{5,7},{6,4},{7,5},{8,10},{9,11},{10,... | collective-permute-start | bytes 516104 | tf_op jit(solution)/shard_map/ppermute | solution.py:1125
  81.2 0.9 inverse_rest.3
  82.1 0.1 collective-permute-start.17
  82.2 0.4 collective-permute-start.18
  82.5 1.0 %near_field.3.refs_8_ = f32[8,128]{1,0:T(8,128)S(1)} custom-call(s32[24]{0:T(128)S(1)} %get-tuple-element.92.place_ref, s32[24]{0:T(128)S(1)} %get-tuple-element.91.target_ref, s16[560,128]{1,0:T(8,128)(2,1)S(1)} %collective-permute-done.13.even_ref.refs_1_.refs_0_, s16[816,128]{1,0:T(8,128)(2,1)S(1)} %collective-permute-done.15.refs_3_.refs_1_, ...), custom_call_target="tpu_custom_call" | custom-call | flops 12582912 | bytes 786432 | tf_op jit(solution)/shard_map/near_field/pallas_call | solution.py:1059
  83.6 1.7 %collective-permute-done.19.refs_1_ = s16[672,128]{1,0:T(8,128)(2,1)S(1)} collective-permute-done((s16[672,128]{1,0:T(8,128)(2,1)S(1)}, s16[672,128]{1,0:T(8,128)(2,1)S(1)}, u32[]{:S(2)}, u32[]{:S(2)}) %collective-permute-start.19) | collective-permute-done | bytes 172064 | tf_op jit(solution)/shard_map/ppermute | solution.py:1125
  85.2 0.4 sample_early.3.refs_2_
  85.7 0.0 collective-permute-done.17.refs_0_
  85.7 2.6 %collective-permute-done.18.refs_1_ = s16[672,128]{1,0:T(8,128)(2,1)S(1)} collective-permute-done((s16[672,128]{1,0:T(8,128)(2,1)S(1)}, s16[672,128]{1,0:T(8,128)(2,1)S(1)}, u32[]{:S(2)}, u32[]{:S(2)}) %collective-permute-start.18) | collective-permute-done | bytes 172064 | tf_op jit(solution)/shard_map/ppermute | solution.py:1125
  88.3 3.6 %sample.3 = f32[2,512]{1,0:T(2,128)} custom-call(s32[2,512]{1,0:T(2,128)S(1)} %get-tuple-element.48.place_ref.refs_1_, s16[672,128]{1,0:T(8,128)(2,1)S(1)} %collective-permute-done.17.refs_0_, s16[672,128]{1,0:T(8,128)(2,1)S(1)} %collective-permute-done.18.refs_1_, f32[656,256]{1,0:T(8,128)S(1)} %sample_early.3.refs_2_, bf16[4,128,256]{2,1,0:T(8,128)(2,1)S(1)} %copy-done.4, ...), custom_call_target="tpu_custom_call" | custom-call | flops 169869312 | bytes 4194304 | tf_op jit(solution)/shard_map/sample/pallas_call | solution.py:1003
  (20 shorter events, 0.1 us)
Async XLA Ops:
  5.7 9.2 %collective-permute-start.1 = (s16[672,128]{1,0:T(8,128)(2,1)S(1)}, s16[672,128]{1,0:T(8,128)(2,1)S(1)}, u32[]{:S(2)}, u32[]{:S(2)}) collective-permute-start(s16[672,128]{1,0:T(8,128)(2,1)S(1)} %get-tuple-element.56), channel_id=1, source_target_pairs={{0,2},{1,3},{2,0},{3,1},{4,6},{5,7},{6,4},{7,5},{8,10},{9,11},{10,... | collective-permute-start | bytes 516104 | tf_op jit(solution)/shard_map/ppermute | solution.py:1125
  9.3 6.3 %collective-permute-start = (s16[672,128]{1,0:T(8,128)(2,1)S(1)}, s16[672,128]{1,0:T(8,128)(2,1)S(1)}, u32[]{:S(2)}, u32[]{:S(2)}) collective-permute-start(s16[672,128]{1,0:T(8,128)(2,1)S(1)} %get-tuple-element.55), channel_id=1, source_target_pairs={{0,1},{1,0},{2,3},{3,2},{4,5},{5,4},{6,7},{7,6},{8,9},{9,8},{10,11... | collective-permute-start | bytes 516104 | tf_op jit(solution)/shard_map/ppermute | solution.py:1125
  9.4 6.8 %collective-permute-start.2 = (s16[672,128]{1,0:T(8,128)(2,1)S(1)}, s16[672,128]{1,0:T(8,128)(2,1)S(1)}, u32[]{:S(2)}, u32[]{:S(2)}) collective-permute-start(s16[672,128]{1,0:T(8,128)(2,1)S(1)} %get-tuple-element.57), channel_id=1, source_target_pairs={{0,3},{1,2},{2,1},{3,0},{4,7},{5,6},{6,5},{7,4},{8,11},{9,10},{10,... | collective-permute-start | bytes 516104 | tf_op jit(solution)/shard_map/ppermute | solution.py:1125
  9.5 0.9 copy-start
  10.4 4.5 %copy-start.6 = (bf16[2,256,240]{2,1,0:T(8,128)(2,1)S(1)}, bf16[2,256,240]{2,1,0:T(8,128)(2,1)}, u32[]{:S(2)}) copy-start(bf16[2,256,240]{2,1,0:T(8,128)(2,1)} %constant.76.clone.refs_2_.refs_5_) | copy-start | bytes 737284
  15.6 17.3 %copy-start.2 = (bf16[4,48,256]{2,1,0:T(8,128)(2,1)S(1)}, bf16[4,48,256]{2,1,0:T(8,128)(2,1)}, u32[]{:S(2)}) copy-start(bf16[4,48,256]{2,1,0:T(8,128)(2,1)} %constant.77.clone.refs_7_.high_ref) | copy-start | bytes 294916
  15.6 17.3 %copy-start.3 = (bf16[4,48,256]{2,1,0:T(8,128)(2,1)S(1)}, bf16[4,48,256]{2,1,0:T(8,128)(2,1)}, u32[]{:S(2)}) copy-start(bf16[4,48,256]{2,1,0:T(8,128)(2,1)} %constant.78.clone.refs_8_.low_ref) | copy-start | bytes 294916
  18.1 6.7 %collective-permute-start.3 = (s16[560,128]{1,0:T(8,128)(2,1)S(1)}, s16[560,128]{1,0:T(8,128)(2,1)S(1)}, u32[]{:S(2)}, u32[]{:S(2)}) collective-permute-start(s16[560,128]{1,0:T(8,128)(2,1)S(1)} %get-tuple-element.59), channel_id=1, source_target_pairs={{0,4},{8,12},{4,0},{12,8},{1,5},{9,13},{5,1},{13,9},{2,6},{10,14},... | collective-permute-start | bytes 430088 | tf_op jit(solution)/shard_map/ppermute | solution.py:1137
  19.7 9.0 %collective-permute-start.5 = (s16[816,128]{1,0:T(8,128)(2,1)S(1)}, s16[816,128]{1,0:T(8,128)(2,1)S(1)}, u32[]{:S(2)}, u32[]{:S(2)}) collective-permute-start(s16[816,128]{1,0:T(8,128)(2,1)S(1)} %get-tuple-element.61), channel_id=1, source_target_pairs={{4,8},{8,4},{5,9},{9,5},{6,10},{10,6},{7,11},{11,7},{20,24},{24,20... | collective-permute-start | bytes 626696 | tf_op jit(solution)/shard_map/ppermute | solution.py:1138
  20.4 8.3 %collective-permute-start.4 = (s16[528,128]{1,0:T(8,128)(2,1)S(1)}, s16[528,128]{1,0:T(8,128)(2,1)S(1)}, u32[]{:S(2)}, u32[]{:S(2)}) collective-permute-start(s16[528,128]{1,0:T(8,128)(2,1)S(1)} %get-tuple-element.60), channel_id=1, source_target_pairs={{0,4},{8,12},{4,0},{12,8},{1,5},{9,13},{5,1},{13,9},{2,6},{10,14},... | collective-permute-start | bytes 405512 | tf_op jit(solution)/shard_map/ppermute | solution.py:1139
  24.8 12.7 %copy-start.8 = (s32[24]{0:T(128)S(1)}, s32[24]{0:T(128)}, u32[]{:S(2)}) copy-start(s32[24]{0:T(128)} %param.21) | copy-start | bytes 292
  24.8 12.7 %copy-start.9 = (s32[24]{0:T(128)S(1)}, s32[24]{0:T(128)}, u32[]{:S(2)}) copy-start(s32[24]{0:T(128)} %param.22) | copy-start | bytes 292
  24.9 7.9 %collective-permute-start.6 = (s16[272,128]{1,0:T(8,128)(2,1)S(1)}, s16[272,128]{1,0:T(8,128)(2,1)S(1)}, u32[]{:S(2)}, u32[]{:S(2)}) collective-permute-start(s16[272,128]{1,0:T(8,128)(2,1)S(1)} %pair_messages.2), channel_id=1, source_target_pairs={{0,8},{4,12},{8,0},{12,4},{1,9},{5,13},{9,1},{13,5},{2,10},{6,14},... | collective-permute-start | bytes 208904 | tf_op jit(solution)/shard_map/ppermute | solution.py:1141
  32.9 6.3 %copy-start.1 = (bf16[24,128,128]{2,1,0:T(8,128)(2,1)S(1)}, bf16[24,128,128]{2,1,0:T(8,128)(2,1)}, u32[]{:S(2)}) copy-start(bf16[24,128,128]{2,1,0:T(8,128)(2,1)} %refs_3_.10) | copy-start | bytes 2359300
  35.9 7.2 %collective-permute-start.9 = (s16[672,128]{1,0:T(8,128)(2,1)S(1)}, s16[672,128]{1,0:T(8,128)(2,1)S(1)}, u32[]{:S(2)}, u32[]{:S(2)}) collective-permute-start(s16[672,128]{1,0:T(8,128)(2,1)S(1)} %get-tuple-element.69), channel_id=1, source_target_pairs={{0,2},{1,3},{2,0},{3,1},{4,6},{5,7},{6,4},{7,5},{8,10},{9,11},{10,... | collective-permute-start | bytes 516104 | tf_op jit(solution)/shard_map/ppermute | solution.py:1125
  38.4 5.2 %collective-permute-start.7 = (s16[672,128]{1,0:T(8,128)(2,1)S(1)}, s16[672,128]{1,0:T(8,128)(2,1)S(1)}, u32[]{:S(2)}, u32[]{:S(2)}) collective-permute-start(s16[672,128]{1,0:T(8,128)(2,1)S(1)} %get-tuple-element.66), channel_id=1, source_target_pairs={{0,1},{1,0},{2,3},{3,2},{4,5},{5,4},{6,7},{7,6},{8,9},{9,8},{10,11... | collective-permute-start | bytes 516104 | tf_op jit(solution)/shard_map/ppermute | solution.py:1125
  38.5 6.8 %collective-permute-start.8 = (s16[672,128]{1,0:T(8,128)(2,1)S(1)}, s16[672,128]{1,0:T(8,128)(2,1)S(1)}, u32[]{:S(2)}, u32[]{:S(2)}) collective-permute-start(s16[672,128]{1,0:T(8,128)(2,1)S(1)} %get-tuple-element.67), channel_id=1, source_target_pairs={{0,3},{1,2},{2,1},{3,0},{4,7},{5,6},{6,5},{7,4},{8,11},{9,10},{10,... | collective-permute-start | bytes 516104 | tf_op jit(solution)/shard_map/ppermute | solution.py:1125
  40.2 3.0 %copy-start.4 = (bf16[4,128,256]{2,1,0:T(8,128)(2,1)S(1)}, bf16[4,128,256]{2,1,0:T(8,128)(2,1)}, u32[]{:S(2)}) copy-start(bf16[4,128,256]{2,1,0:T(8,128)(2,1)} %constant.79.clone.refs_2_.refs_3_) | copy-start | bytes 786436
  40.2 3.0 %copy-start.5 = (bf16[4,128,256]{2,1,0:T(8,128)(2,1)S(1)}, bf16[4,128,256]{2,1,0:T(8,128)(2,1)}, u32[]{:S(2)}) copy-start(bf16[4,128,256]{2,1,0:T(8,128)(2,1)} %constant.80.clone.refs_3_.refs_4_) | copy-start | bytes 786436
  43.1 2.1 %copy-start.7 = (s32[512]{0:T(512)S(1)}, s32[512]{0:T(512)}, u32[]{:S(2)}) copy-start(s32[512]{0:T(512)} %param.17) | copy-start | bytes 6148
  51.1 7.3 %collective-permute-start.11 = (s16[672,128]{1,0:T(8,128)(2,1)S(1)}, s16[672,128]{1,0:T(8,128)(2,1)S(1)}, u32[]{:S(2)}, u32[]{:S(2)}) collective-permute-start(s16[672,128]{1,0:T(8,128)(2,1)S(1)} %get-tuple-element.76), channel_id=1, source_target_pairs={{0,2},{1,3},{2,0},{3,1},{4,6},{5,7},{6,4},{7,5},{8,10},{9,11},{10,... | collective-permute-start | bytes 516104 | tf_op jit(solution)/shard_map/ppermute | solution.py:1125
  52.6 6.4 %collective-permute-start.10 = (s16[672,128]{1,0:T(8,128)(2,1)S(1)}, s16[672,128]{1,0:T(8,128)(2,1)S(1)}, u32[]{:S(2)}, u32[]{:S(2)}) collective-permute-start(s16[672,128]{1,0:T(8,128)(2,1)S(1)} %get-tuple-element.75), channel_id=1, source_target_pairs={{0,1},{1,0},{2,3},{3,2},{4,5},{5,4},{6,7},{7,6},{8,9},{9,8},{10,11... | collective-permute-start | bytes 516104 | tf_op jit(solution)/shard_map/ppermute | solution.py:1125
  53.3 7.5 %collective-permute-start.12 = (s16[672,128]{1,0:T(8,128)(2,1)S(1)}, s16[672,128]{1,0:T(8,128)(2,1)S(1)}, u32[]{:S(2)}, u32[]{:S(2)}) collective-permute-start(s16[672,128]{1,0:T(8,128)(2,1)S(1)} %get-tuple-element.77), channel_id=1, source_target_pairs={{0,3},{1,2},{2,1},{3,0},{4,7},{5,6},{6,5},{7,4},{8,11},{9,10},{10,... | collective-permute-start | bytes 516104 | tf_op jit(solution)/shard_map/ppermute | solution.py:1125
  62.7 6.2 %collective-permute-start.13 = (s16[560,128]{1,0:T(8,128)(2,1)S(1)}, s16[560,128]{1,0:T(8,128)(2,1)S(1)}, u32[]{:S(2)}, u32[]{:S(2)}) collective-permute-start(s16[560,128]{1,0:T(8,128)(2,1)S(1)} %get-tuple-element.79), channel_id=1, source_target_pairs={{0,4},{8,12},{4,0},{12,8},{1,5},{9,13},{5,1},{13,9},{2,6},{10,14},... | collective-permute-start | bytes 430088 | tf_op jit(solution)/shard_map/ppermute | solution.py:1137
  62.8 9.3 %collective-permute-start.15 = (s16[816,128]{1,0:T(8,128)(2,1)S(1)}, s16[816,128]{1,0:T(8,128)(2,1)S(1)}, u32[]{:S(2)}, u32[]{:S(2)}) collective-permute-start(s16[816,128]{1,0:T(8,128)(2,1)S(1)} %get-tuple-element.81), channel_id=1, source_target_pairs={{4,8},{8,4},{5,9},{9,5},{6,10},{10,6},{7,11},{11,7},{20,24},{24,20... | collective-permute-start | bytes 626696 | tf_op jit(solution)/shard_map/ppermute | solution.py:1138
  63.7 8.5 %collective-permute-start.14 = (s16[528,128]{1,0:T(8,128)(2,1)S(1)}, s16[528,128]{1,0:T(8,128)(2,1)S(1)}, u32[]{:S(2)}, u32[]{:S(2)}) collective-permute-start(s16[528,128]{1,0:T(8,128)(2,1)S(1)} %get-tuple-element.80), channel_id=1, source_target_pairs={{0,4},{8,12},{4,0},{12,8},{1,5},{9,13},{5,1},{13,9},{2,6},{10,14},... | collective-permute-start | bytes 405512 | tf_op jit(solution)/shard_map/ppermute | solution.py:1139
  69.0 7.3 %collective-permute-start.16 = (s16[272,128]{1,0:T(8,128)(2,1)S(1)}, s16[272,128]{1,0:T(8,128)(2,1)S(1)}, u32[]{:S(2)}, u32[]{:S(2)}) collective-permute-start(s16[272,128]{1,0:T(8,128)(2,1)S(1)} %pair_messages.3), channel_id=1, source_target_pairs={{0,8},{4,12},{8,0},{12,4},{1,9},{5,13},{9,1},{13,5},{2,10},{6,14},... | collective-permute-start | bytes 208904 | tf_op jit(solution)/shard_map/ppermute | solution.py:1141
  79.4 5.9 %collective-permute-start.19 = (s16[672,128]{1,0:T(8,128)(2,1)S(1)}, s16[672,128]{1,0:T(8,128)(2,1)S(1)}, u32[]{:S(2)}, u32[]{:S(2)}) collective-permute-start(s16[672,128]{1,0:T(8,128)(2,1)S(1)} %get-tuple-element.89), channel_id=1, source_target_pairs={{0,2},{1,3},{2,0},{3,1},{4,6},{5,7},{6,4},{7,5},{8,10},{9,11},{10,... | collective-permute-start | bytes 516104 | tf_op jit(solution)/shard_map/ppermute | solution.py:1125
  82.1 3.6 %collective-permute-start.17 = (s16[672,128]{1,0:T(8,128)(2,1)S(1)}, s16[672,128]{1,0:T(8,128)(2,1)S(1)}, u32[]{:S(2)}, u32[]{:S(2)}) collective-permute-start(s16[672,128]{1,0:T(8,128)(2,1)S(1)} %get-tuple-element.86), channel_id=1, source_target_pairs={{0,1},{1,0},{2,3},{3,2},{4,5},{5,4},{6,7},{7,6},{8,9},{9,8},{10,11... | collective-permute-start | bytes 516104 | tf_op jit(solution)/shard_map/ppermute | solution.py:1125
  82.2 6.2 %collective-permute-start.18 = (s16[672,128]{1,0:T(8,128)(2,1)S(1)}, s16[672,128]{1,0:T(8,128)(2,1)S(1)}, u32[]{:S(2)}, u32[]{:S(2)}) collective-permute-start(s16[672,128]{1,0:T(8,128)(2,1)S(1)} %get-tuple-element.87), channel_id=1, source_target_pairs={{0,3},{1,2},{2,1},{3,0},{4,7},{5,6},{6,5},{7,4},{8,11},{9,10},{10,... | collective-permute-start | bytes 516104 | tf_op jit(solution)/shard_map/ppermute | solution.py:1125

commit v12 on v11

--- a/solution.py
+++ b/solution.py
@@ -490,19 +490,32 @@
     )(places, coeff, *awaited)
 
 
-def stack_pieces(parts, reach_x, reach_y, top, opened, stacked):
+def put_edges(opened, reach_x, reach_y, edges, first):
     half = reach_x // 2
-    pitch = up_to(reach_y, 8)
-    tall = len(parts) * pitch
+    low = low_lanes(reach_y)
+    layer = lambda i: opened[i * reach_y : (i + 1) * reach_y, :]
+    for two in range(2):
+        place = slice(first + two * reach_y, first + (two + 1) * reach_y)
+        edges[0, place, :] = jnp.where(low, layer(2 * two), swap(layer(2 * two + 1)))
+        last = half - 4 + 2 * two
+        edges[1, place, :] = jnp.where(low, swap(layer(last)), layer(last + 1))
+
+
+def stack_layers(layers, at, reach_y, stacked):
+    tall = stacked.shape[0] // len(layers)
+    place = at * up_to(reach_y, 8)
+    for i, layer in enumerate(layers):
+        stacked[pl.ds(pl.multiple_of(i * tall + place, 8), reach_y), :] = layer
+
+
+def stack_pieces(parts, reach_x, reach_y, top, opened, stacked, edges, places):
     chip = lax.axis_index("narrow")
-    for flip, part in enumerate(parts):
+    for flip, (part, place) in enumerate(zip(parts, places)):
         first = from_short(part[:top, :])
         opened[...] = from_short(part[top:, :]) * unit(first[0:1], first[1:2])
-        place = (chip ^ flip) * pitch
-        for i in range(half):
-            stacked[pl.ds(pl.multiple_of(i * tall + place, 8), reach_y), :] = opened[
-                i * reach_y : (i + 1) * reach_y, :
-            ]
+        layers = [opened[i * reach_y : (i + 1) * reach_y, :] for i in range(reach_x // 2)]
+        stack_layers(layers, chip ^ flip, reach_y, stacked)
+        put_edges(opened, reach_x, reach_y, edges, place * 2 * reach_y)
 
 
 def transform_pieces(table, stacked, before, spectrum):
@@ -524,10 +537,10 @@
 
 def forward_early_kernel(reach_x, reach_y, chips, *refs):
     parts = refs[:chips]
-    table_ref, spectrum, opened, stacked = refs[chips:]
+    table_ref, spectrum, edges, opened, stacked = refs[chips:]
     top = parts[0].shape[0] - opened.shape[0]
     stacked[...] = jnp.zeros_like(stacked)
-    stack_pieces(parts, reach_x, reach_y, top, opened, stacked)
+    stack_pieces(parts, reach_x, reach_y, top, opened, stacked, edges, range(chips))
     transform_pieces(table_ref[lax.axis_index("pair")], stacked, None, spectrum)
 
 
@@ -545,8 +558,11 @@
     return pl.pallas_call(
         functools.partial(forward_early_kernel, reach_x, reach_y, chips),
         in_specs=[whole_vmem()] * (chips + 1),
-        out_specs=whole_vmem(),
-        out_shape=jax.ShapeDtypeStruct((half, GRID, 2 * HALF), F32),
+        out_specs=[whole_vmem()] * 2,
+        out_shape=[
+            jax.ShapeDtypeStruct((half, GRID, 2 * HALF), F32),
+            jax.ShapeDtypeStruct((2, chips * 2 * reach_y, 2 * HALF), F32),
+        ],
         scratch_shapes=stacking_scratch(chips, reach_x, reach_y),
         compiler_params=params(),
         cost_estimate=cost(EARLY_FLOPS, 4 * half * GRID * 2 * HALF * 2),
@@ -556,10 +572,10 @@
 
 def forward_kernel(reach_x, reach_y, blocks, pieces, awaited, *refs):
     parts = refs[:pieces]
-    early_ref, table_ref, modes_ref = refs[pieces : pieces + 3]
-    refs = refs[: pieces + 3] + refs[pieces + 3 + awaited :]
-    spectrum, even_out, layers_out, odd_out, own_out, peers_out, inner_out, *refs = refs[pieces + 3 :]
-    opened, stacked, slabs, head = refs
+    early_ref, early_edges, table_ref, modes_ref = refs[pieces : pieces + 4]
+    refs = refs[pieces + 4 + awaited :]
+    spectrum, even_out, layers_out, odd_out, own_out, peers_out, inner_out, *refs = refs
+    opened, stacked, edges, slabs, head = refs
     half = reach_x // 2
     pair = lax.axis_size("pair")
     top = parts[0].shape[0] - opened.shape[0]
@@ -572,9 +588,14 @@
         at = 6 + 2 * piece * blocks
         head[at : at + blocks, :] = mantissa
         head[at + blocks : at + 2 * blocks, :] = exponent
+    rows = 2 * reach_y
+    for chip in range(pieces // pair):
+        place = chip * pair * rows
+        edges[:, place : place + rows, :] = early_edges[:, chip * rows : (chip + 1) * rows, :]
     before = early_ref
     for core in range(1, pair):
-        stack_pieces(parts[core::pair], reach_x, reach_y, top, opened, stacked)
+        places = range(core, pieces, pair)
+        stack_pieces(parts[core::pair], reach_x, reach_y, top, opened, stacked, edges, places)
         transform_pieces(table_ref[lax.axis_index("pair") ^ core], stacked, before, spectrum)
         before = spectrum
 
@@ -605,16 +626,11 @@
         inner_out[rows, :] = jnp.where(low, right, left)
         swapped_right, swapped_left = swap(right), swap(left)
         own = jnp.where(low, left + across_half * swapped_left, right + across_half * swapped_right)
+        own_out[rows, :] = own
         made = [
-            jnp.where(low, swap(layers[half - 4]), layers[half - 3]),
-            jnp.where(low, swap(layers[half - 2]), layers[half - 1]),
             jnp.where(low, own, cut_right + across_cut * swapped_right),
-            jnp.where(low, layers[0], swap(layers[1])),
-            jnp.where(low, layers[2], swap(layers[3])),
             jnp.where(low, cut_left + across_cut * swapped_left, own),
-            own,
         ]
-        own_out[rows, :] = own
         for slab, values in enumerate(made):
             slabs[slab, rows, :] = values
         return tuple(
@@ -623,67 +639,71 @@
         )
 
     zero = jnp.zeros((8, 2 * HALF), F32)
-    largest = lax.fori_loop(0, GRID // chunk, body, (zero,) * 7)
-    scales = [fit_scale(jnp.max(value, axis=0, keepdims=True)) for value in largest]
-    head_rows = head.shape[0]
-
-    def send(out, top, which):
-        for place, slab in enumerate(which):
-            exponent, fraction = scales[slab]
-            head[2 * place : 2 * place + 1, :] = exponent
-            head[2 * place + 1 : 2 * place + 2, :] = fraction
-            at = top + place * GRID
-            out[at : at + GRID, :] = quantize(slabs[slab], exponent, fraction)
-        out[:top, :] = to_short(head[:top, :])
-
+    largest = lax.fori_loop(0, GRID // chunk, body, (zero,) * 2)
+    top = head.shape[0]
+    low = low_lanes(GRID // 2)
+    upper, lower = own_out[: GRID // 2, :], own_out[GRID // 2 :, :]
+    packed = [jnp.where(low, swap(upper), lower), jnp.where(low, upper, swap(lower))]
+
+    def send(out, first, parts):
+        place = first
+        for index, (values, most) in enumerate(parts):
+            exponent, fraction = fit_scale(jnp.max(most, axis=0, keepdims=True))
+            head[2 * index : 2 * index + 1, :] = exponent
+            head[2 * index + 1 : 2 * index + 2, :] = fraction
+            out[place : place + values.shape[0], :] = quantize(values, exponent, fraction)
+            place += values.shape[0]
+        out[:first, :] = to_short(head[:first, :])
+
+    with_most = lambda values: (values, jnp.abs(values))
     on_left = lax.axis_index("wide") & 1
-    for side, (even, odd) in enumerate(((0, 3), (3, 0))):
+    for side, (even, odd) in enumerate(((0, 1), (1, 0))):
 
         @pl.when(on_left == side)
         def _():
-            send(even_out, head_rows, (even + 2, 6))
-            send(layers_out, 16, (even, even + 1))
-            send(odd_out, head_rows, (odd + 2, odd, odd + 1))
-
-
-def forward(parts, early, table, modes, reach_x, reach_y, blocks, awaited):
+            send(even_out, top, [(slabs[even], largest[even]), with_most(packed[even])])
+            send(layers_out, 16, [with_most(edges[1 - even])])
+            send(odd_out, top, [(slabs[odd], largest[odd]), with_most(edges[1 - odd])])
+
+
+def forward(parts, early, early_edges, table, modes, reach_x, reach_y, blocks, awaited):
     pieces = len(parts)
     half = reach_x // 2
     lanes = 2 * HALF
     head = up_to(6 + 2 * pieces * blocks, 16)
+    border = pieces * 2 * reach_y
     short = lambda rows: jax.ShapeDtypeStruct((rows, lanes), jnp.int16)
     return pl.pallas_call(
         functools.partial(
             forward_kernel, reach_x, reach_y, blocks, pieces, len(awaited)
         ),
-        in_specs=[whole_vmem()] * (pieces + 3) + [anywhere()] * len(awaited),
+        in_specs=[whole_vmem()] * (pieces + 4) + [anywhere()] * len(awaited),
         out_specs=[whole_vmem()] * 7,
         out_shape=[
             jax.ShapeDtypeStruct((half, GRID, lanes), F32),
-            short(head + 2 * GRID),
-            short(16 + 2 * GRID),
-            short(head + 3 * GRID),
+            short(head + GRID + GRID // 2),
+            short(16 + border),
+            short(head + GRID + border),
             jax.ShapeDtypeStruct((GRID, lanes), F32),
             jax.ShapeDtypeStruct((pieces * blocks, BLOCK), F32),
             jax.ShapeDtypeStruct((GRID, lanes), F32),
         ],
         scratch_shapes=stacking_scratch(pieces // table.shape[0], reach_x, reach_y)
         + [
-            pltpu.VMEM((7, GRID, lanes), F32),
+            pltpu.VMEM((2, border, lanes), F32),
+            pltpu.VMEM((2, GRID, lanes), F32),
             pltpu.VMEM((head, lanes), F32),
         ],
         compiler_params=params(),
         cost_estimate=cost(2 * half * 256 * 256 * 128, 4 * half * GRID * lanes * 2),
         name="forward",
-    )(*parts, early, table, modes, *awaited)
-
-
-def opened_slabs(ref, count, head_rows):
-    first = from_short(ref[:16, :])
-    for slab in range(count):
-        scale = unit(first[2 * slab : 2 * slab + 1], first[2 * slab + 1 : 2 * slab + 2])
-        at = head_rows + slab * GRID
-        yield from_short(ref[at : at + GRID, :]) * scale
+    )(*parts, early, early_edges, table, modes, *awaited)
+
+
+def opened_part(ref, index, first, rows):
+    head = from_short(ref[:16, :])
+    scale = unit(head[2 * index : 2 * index + 1], head[2 * index + 1 : 2 * index + 2])
+    return from_short(ref[first : first + rows, :]) * scale
 
 
 def pair_kernel(reach_x, flips, own_ref, even_ref, modes_ref, *refs):
@@ -693,7 +713,12 @@
     low = low_lanes(GRID)
     log_decay = modes_ref[1]
     own = own_ref[...]
-    _, partner = opened_slabs(even_ref, 2, even_ref.shape[0] - 2 * GRID)
+    top = even_ref.shape[0] - GRID - GRID // 2
+    cut = opened_part(even_ref, 0, top, GRID)
+    packed = opened_part(even_ref, 1, top + GRID, GRID // 2)
+    from_left = jnp.where(low, cut, jnp.concatenate([swap(packed), packed], axis=0))
+    from_right = jnp.where(low, jnp.concatenate([packed, swap(packed)], axis=0), cut)
+    partner = jnp.where((here & 1) == 1, from_left, from_right)
 
     def weight(distances):
         powers = []
@@ -722,6 +747,51 @@
         cost_estimate=cost(16 * GRID * 2 * HALF, 4 * GRID * 2 * HALF * (6 + len(flips))),
         name="pair_messages",
     )(own, from_even, modes)
+
+
+def borders_kernel(reach_y, pieces, layers_ref, odd_ref, table_ref, out_ref, stacked, partial):
+    on_left = (lax.axis_index("wide") & 1) == 1
+    pair = lax.axis_size("pair")
+    rows = pieces * 2 * reach_y
+    even = opened_part(layers_ref, 0, 16, rows)
+    odd = opened_part(odd_ref, 1, odd_ref.shape[0] - rows, rows)
+    left, right = jnp.where(on_left, even, odd), jnp.where(on_left, odd, even)
+    low = low_lanes(rows)
+    both = [jnp.where(low, left, swap(right)), jnp.where(low, swap(left), right)]
+    core = lax.axis_index("pair")
+    chip = lax.axis_index("narrow")
+    stacked[...] = jnp.zeros_like(stacked)
+    before = None
+    for other in range(pair):
+        for flip in range(pieces // pair):
+            first = (flip * pair + other) * 2 * reach_y
+            layers = [
+                values[first + two * reach_y : first + (two + 1) * reach_y]
+                for two in range(2)
+                for values in both
+            ]
+            stack_layers(layers, chip ^ flip, reach_y, stacked)
+        target = out_ref if other == pair - 1 else partial
+        transform_pieces(table_ref[core ^ other], stacked, before, target)
+        before = target
+
+
+def borders(layers, from_odd, table, reach_y, pieces):
+    chips = pieces // table.shape[0]
+    shape = (4, GRID, 2 * HALF)
+    return pl.pallas_call(
+        functools.partial(borders_kernel, reach_y, pieces),
+        in_specs=[whole_vmem()] * 3,
+        out_specs=whole_vmem(),
+        out_shape=jax.ShapeDtypeStruct(shape, F32),
+        scratch_shapes=[
+            pltpu.VMEM((4 * chips * up_to(reach_y, 8), 2 * HALF), F32),
+            pltpu.VMEM(shape, F32),
+        ],
+        compiler_params=params(),
+        cost_estimate=cost(2 * 4 * 256 * 256 * 128, 4 * 6 * GRID * 2 * HALF),
+        name="borders",
+    )(layers, from_odd, table)
 
 
 def send_fields(outs, flips, reach_y, field_high, field_low, high_ref, low_ref, ready, head):
@@ -747,7 +817,7 @@
 
 
 def inverse_kernel(reach_x, reach_y, flips, fars, *refs):
-    spectrum, from_even, even_layers, from_odd, own_ref, inner_ref, *far_refs = refs[: 6 + fars]
+    spectrum, border_ref, from_even, from_odd, own_ref, inner_ref, *far_refs = refs[: 6 + fars]
     refs = refs[6 + fars :]
     high_ref, low_ref, modes_ref = refs[:3]
     outs = refs[3 : 3 + len(flips)]
@@ -755,20 +825,12 @@
     half = reach_x // 2
     span = reach_x - 4
     chunk = 32
-    head_rows = from_even.shape[0] - 2 * GRID
+    head_rows = from_even.shape[0] - GRID - GRID // 2
     on_left = (lax.axis_index("wide") & 1) == 1
-    even_places = (from_even, head_rows, 0), (even_layers, 16, 0), (even_layers, 16, 1)
-    odd_places = tuple((from_odd, head_rows, place) for place in range(3))
-
-    def slab_unit(place):
-        ref, _, at = place
+    moment_units = []
+    for ref in (from_even, from_odd):
         first = from_short(ref[:16, :])
-        return unit(first[2 * at : 2 * at + 1], first[2 * at + 1 : 2 * at + 2])
-
-    both_units = [[slab_unit(place) for place in places] for places in (even_places, odd_places)]
-
-    def sided(even, odd):
-        return jnp.where(on_left, even, odd), jnp.where(on_left, odd, even)
+        moment_units.append(unit(first[0:1], first[1:2]))
 
     far_units = []
     for ref in far_refs:
@@ -789,30 +851,24 @@
         beside = jnp.exp((GRID - reach_x - span) * log_decay)
         layers = [spectrum[i, rows, :] for i in range(half)]
 
-        def slab(which):
-            found = []
-            for places, units in zip((even_places, odd_places), both_units):
-                ref, top, place = places[which]
-                at = pl.multiple_of(top + place * GRID + index * chunk, 16)
-                found.append(from_short(ref[pl.ds(at, chunk), :]) * units[which])
-            return sided(*found)
-
-        left_moments, right_moments = slab(0)
-        head_layers, tail_layers = zip(slab(1), slab(2))
+        at = pl.ds(pl.multiple_of(head_rows + index * chunk, 16), chunk)
+        even, odd = (
+            from_short(ref[at, :]) * scale for ref, scale in zip((from_even, from_odd), moment_units)
+        )
+        left_moments, right_moments = jnp.where(on_left, even, odd), jnp.where(on_left, odd, even)
+        border = [border_ref[i, rows, :] for i in range(4)]
         zero = jnp.zeros_like(decay)
-        from_head = [head_layers[0], swap(head_layers[0]), head_layers[1], swap(head_layers[1])]
-        from_tail = [swap(tail_layers[0]), tail_layers[0], swap(tail_layers[1]), tail_layers[1]]
-        head_sum = from_head[0]
+        head_sum = border[0]
         for i in range(1, 4):
-            head_sum = decay * head_sum + from_head[i]
-        tail_sum = from_tail[3]
+            head_sum = decay * head_sum + border[i]
+        tail_sum = border[3]
         for i in range(2, -1, -1):
-            tail_sum = decay * tail_sum + from_tail[i]
+            tail_sum = decay * tail_sum + border[i]
         for i in range(4):
-            layers[i] = layers[i] + jnp.where(low, from_head[i], zero)
+            layers[i] = layers[i] + jnp.where(low, border[i], zero)
         for i in range(4):
             place = half - 4 + i
-            layers[place] = layers[place] + jnp.where(low, zero, from_tail[i])
+            layers[place] = layers[place] + jnp.where(low, zero, border[i])
         total = own_ref[rows, :] * jnp.exp((GRID - reach_x) * log_decay)
         at = pl.ds(pl.multiple_of(16 + index * chunk, 16), chunk)
         for ref, scale in zip(far_refs, far_units):
@@ -842,18 +898,7 @@
 
 
 def inverse(
-    spectrum,
-    from_even,
-    even_layers,
-    from_odd,
-    own,
-    inner,
-    fars,
-    table,
-    modes,
-    reach_x,
-    reach_y,
-    flips,
+    spectrum, border, from_even, from_odd, own, inner, fars, table, modes, reach_x, reach_y, flips
 ):
     half = reach_x // 2
     lanes = 2 * HALF
@@ -872,7 +917,7 @@
         compiler_params=params(),
         cost_estimate=cost(2 * half * 256 * 256 * 128, 4 * half * GRID * lanes * 2),
         name="inverse",
-    )(spectrum, from_even, even_layers, from_odd, own, inner, *fars, *table, modes)
+    )(spectrum, border, from_even, from_odd, own, inner, *fars, *table, modes)
 
 
 def inverse_rest_kernel(reach_y, flips, field_high, field_low, high_ref, low_ref, *refs):
@@ -1054,7 +1099,7 @@
 
 def near_field(places, targets, from_even, from_odd, peers, tiles, blocks, out_rows, awaited):
     slots = tiles.shape[0]
-    head = from_even.shape[0] - 2 * GRID
+    head = up_to(6 + 2 * peers.shape[0], 16)
     constant = lambda shape: pl.BlockSpec(shape, lambda i: (0,) * len(shape))
     return pl.pallas_call(
         functools.partial(near_kernel, slots, blocks),
@@ -1130,9 +1175,9 @@
 
     def convolve_and_sample(last, vector, sent, both, table, places, sample_lines, awaited):
         arrived = turned(sent, spread_rest(vector, both, table, rest))
-        early = forward_early(chosen(arrived, same_core), y_forward, reach_x, reach_y)
+        early, edges = forward_early(chosen(arrived, same_core), y_forward, reach_x, reach_y)
         spectrum, even_message, layers, odd_message, own, peers, inner = forward(
-            arrived, early, y_forward, modes, reach_x, reach_y, blocks, awaited
+            arrived, early, edges, y_forward, modes, reach_x, reach_y, blocks, awaited
         )
         from_even = lax.ppermute(even_message, "wide", even_swap)
         from_odd = lax.ppermute(odd_message, "wide", odd_swap)
@@ -1145,8 +1190,8 @@
         ]
         *sent, high, low = inverse(
             spectrum,
+            borders(even_layers, from_odd, y_forward, reach_y, y_count),
             from_even,
-            even_layers,
             from_odd,
             own,
             inner,

time: 92.1 us -> 90.2 us (0.979)
  waiting for transfers between devices: 24.9 us -> 22.9 us
    ppermute x2, waiting for transfers between devices: 8.37 us -> 7.15 us  [convolve_and_sample(): lax.ppermute(message, 'wide', [(i, i ^ flip) for i in range(x_count)])]
    ppermute x2, starting transfers between devices: 3.64 us -> 2.62 us  [convolve_and_sample(): lax.ppermute(message, 'wide', [(i, i ^ flip) for i in range(x_count)])]
  transfers between devices with their start and end apart: 20 -> 20, of which waited for: 11 -> 10; matrix products, arithmetic and copies ran while one was open for 1% -> 1% of each run, Pallas kernels for 15% -> 16%
where the time goes in v12:
time: 90.2 us; the launch traced here: 89.9 us
  Pallas kernels  39.5 us (44%)
  starting transfers between devices  25.1 us (28%)
  waiting for transfers between devices  22.9 us (25%)
  local copies, waits for them, and re-layouts  2.02 us (2%)
    ppermute x12, waiting for transfers between devices, turned(): lax.ppermute(part, Y_AXES, swap_pairs)  13.4 us
    ppermute x12, starting transfers between devices, turned(): lax.ppermute(part, Y_AXES, swap_pairs)  10 us
    ppermute x2, starting transfers between devices, convolve_and_sample(): even_layers = lax.ppermute(layers, 'wide', even_swap)  9.2 us
    pallas_call x2, Pallas kernels, spread(): pl.pallas_call(functools.partial(start_kernel if placed is None else spre...  8.52 us
    ppermute x2, waiting for transfers between devices, convolve_and_sample(): lax.ppermute(message, 'wide', [(i, i ^ flip) for i in range(x_count)])  7.15 us
    pallas_call x2, Pallas kernels, sample(): pl.pallas_call(functools.partial(sample_kernel, last, reach_x, reach_y, f...  6.49 us
    pallas_call x2, Pallas kernels, inverse(): pl.pallas_call(functools.partial(inverse_kernel, reach_x, reach_y, flips,...  5.84 us
    pallas_call x2, Pallas kernels, forward(): pl.pallas_call(functools.partial(forward_kernel, reach_x, reach_y, blocks...  3.89 us
  transfers between devices with their start and end apart: 20, of which 10 were waited for; matrix products, arithmetic and copies ran while one was open for 1% of the time, Pallas kernels for 16%

profile of v12, /device:TPU:0, one launch (start us, length us, event | category | flops | bytes accessed | tf_op | source)
XLA Modules:
  0.0 89.9 jit_solution(224979480457380263)
XLA Ops:
  0.0 5.7 %start.1 = (s16[672,128]{1,0:T(8,128)(2,1)S(1)}, s16[672,128]{1,0:T(8,128)(2,1)S(1)}, bf16[656,256]{1,0:T(8,128)(2,1)S(1)}, bf16[656,256]{1,0:T(8,128)(2,1)S(1)}...) custom-call(f32[512]{0:T(512)} %refs_0_.2, ...), custom_call_target="tpu_custom_call" | custom-call | flops 169869312 | bytes 4194304 | tf_op jit(solution)/shard_map/start/pallas_call | solution.py:397
  5.7 3.0 %collective-permute-start.1 = (s16[672,128]{1,0:T(8,128)(2,1)S(1)}, s16[672,128]{1,0:T(8,128)(2,1)S(1)}, u32[]{:S(2)}, u32[]{:S(2)}) collective-permute-start(s16[672,128]{1,0:T(8,128)(2,1)S(1)} %get-tuple-element.60), channel_id=1, source_target_pairs={{0,2},{1,3},{2,0},{3,1},{4,6},{5,7},{6,4},{7,5},{8,10},{9,11},{10,... | collective-permute-start | bytes 516104 | tf_op jit(solution)/shard_map/ppermute | solution.py:1170
  8.7 0.6 spread_rest.2
  9.3 0.1 collective-permute-start
  9.3 0.1 collective-permute-start.2
  9.5 0.9 %copy-done.1 = f32[64,512]{1,0:T(8,128)S(1)} copy-done((f32[64,512]{1,0:T(8,128)S(1)}, f32[64,512]{1,0:T(8,128)}, u32[]{:S(2)}) %copy-start.1) | copy-done | bytes 131096
  10.4 3.4 %place_sample_lines.1.refs_8_.refs_5_ = f32[8192,128]{1,0:T(8,128)S(1)} custom-call(s32[2,512]{1,0:T(2,128)S(1)} %get-tuple-element.52.place_ref.refs_1_, f32[64,512]{1,0:T(8,128)S(1)} %copy-done.1, f32[64,512]{1,0:T(8,128)S(1)} %copy-done.1, f32[64,512]{1,0:T(8,128)S(1)} %copy-done.1, f32[64,512]{1,0:T(8,128)S(1)} %copy-done.1), custom_call_target="tpu_custom_call" | custom-call | flops 1048576 | bytes 4194304 | tf_op jit(solution)/shard_map/place_sample_lines/pallas_call | solution.py:466
  13.8 1.1 %dynamic-slice_bitcast_fusion.refs_7_.modes_ref.refs_9_ = f32[4,256,128]{2,1,0:T(8,128)S(1)} fusion(f32[4,4,256,128]{3,2,1,0:T(8,128)} %constant.73.clone, s32[]{:T(128)S(6)} %select_n.30), kind=kLoop, calls=%fused_computation | loop fusion | bytes 1048580 | tf_op jit(solution)/shard_map/jit(dynamic_index_in_dim)/squeeze | solution.py:1147
  14.9 0.7 forward_early.2
  15.6 0.0 collective-permute-done.refs_1_
  15.6 0.6 collective-permute-done.2.refs_3_
  16.2 2.0 %forward.2 = (f32[18,256,128]{2,1,0:T(8,128)S(1)}, s16[432,128]{1,0:T(8,128)(2,1)S(1)}, s16[304,128]{1,0:T(8,128)(2,1)S(1)}, s16[592,128]{1,0:T(8,128)(2,1)S(1)}...) custom-call(s16[672,128]{1,0:T(8,128)(2,1)S(1)} %get-tuple-element.58.refs_0_, ...), custom_call_target="tpu_custom_call" | custom-call | flops 301989888 | bytes 4718592 | tf_op jit(solution)/shard_map/forward/pallas_call | solution.py:676
  18.1 1.6 %collective-permute-start.5 = (s16[432,128]{1,0:T(8,128)(2,1)S(1)}, s16[432,128]{1,0:T(8,128)(2,1)S(1)}, u32[]{:S(2)}, u32[]{:S(2)}) collective-permute-start(s16[432,128]{1,0:T(8,128)(2,1)S(1)} %get-tuple-element.67), channel_id=1, source_target_pairs={{0,4},{8,12},{4,0},{12,8},{1,5},{9,13},{5,1},{13,9},{2,6},{10,14},... | collective-permute-start | bytes 331784 | tf_op jit(solution)/shard_map/ppermute | solution.py:1182
  19.7 0.7 collective-permute-start.4
  20.4 4.4 %collective-permute-start.3 = (s16[304,128]{1,0:T(8,128)(2,1)S(1)}, s16[304,128]{1,0:T(8,128)(2,1)S(1)}, u32[]{:S(2)}, u32[]{:S(2)}) collective-permute-start(s16[304,128]{1,0:T(8,128)(2,1)S(1)} %get-tuple-element.65), channel_id=1, source_target_pairs={{0,4},{8,12},{4,0},{12,8},{1,5},{9,13},{5,1},{13,9},{2,6},{10,14},... | collective-permute-start | bytes 233480 | tf_op jit(solution)/shard_map/ppermute | solution.py:1184
  24.9 0.0 collective-permute-done.5.even_ref.refs_2_.refs_0_
  24.9 0.2 pair_messages.2
  25.0 0.0 copy-start.8
  25.0 0.0 copy-start.9
  25.1 1.6 %collective-permute-start.6 = (s16[272,128]{1,0:T(8,128)(2,1)S(1)}, s16[272,128]{1,0:T(8,128)(2,1)S(1)}, u32[]{:S(2)}, u32[]{:S(2)}) collective-permute-start(s16[272,128]{1,0:T(8,128)(2,1)S(1)} %pair_messages.2), channel_id=1, source_target_pairs={{0,8},{4,12},{8,0},{12,4},{1,9},{5,13},{9,1},{13,5},{2,10},{6,14},... | collective-permute-start | bytes 208904 | tf_op jit(solution)/shard_map/ppermute | solution.py:1186
  26.7 0.9 collective-permute-done.3.layers_ref
  27.5 0.0 collective-permute-done.4.odd_ref.refs_3_.refs_1_
  27.5 0.5 borders.2.refs_1_
  28.0 3.7 %collective-permute-done.6.refs_6_ = s16[272,128]{1,0:T(8,128)(2,1)S(1)} collective-permute-done((s16[272,128]{1,0:T(8,128)(2,1)S(1)}, s16[272,128]{1,0:T(8,128)(2,1)S(1)}, u32[]{:S(2)}, u32[]{:S(2)}) %collective-permute-start.6) | collective-permute-done | bytes 69664 | tf_op jit(solution)/shard_map/ppermute | solution.py:1186
  31.7 2.9 %inverse.2 = (s16[672,128]{1,0:T(8,128)(2,1)S(1)}, s16[672,128]{1,0:T(8,128)(2,1)S(1)}, bf16[18,256,128]{2,1,0:T(8,128)(2,1)S(1)}, bf16[18,256,128]{2,1,0:T(8,128)(2,1)S(1)}) custom-call(f32[18,256,128]{2,1,0:T(8,128)S(1)} %get-tuple-element.64.refs_0_, f32[4,256,128]{2,1,0:T(8,128)S(1)} %borders.2.refs_1_, ...), custom_call_target="tpu_custom_call" | custom-call | flops 301989888 | bytes 4718592 | tf_op jit(solution)/shard_map/inverse/pallas_call | solution.py:908
  34.6 1.6 %collective-permute-start.9 = (s16[672,128]{1,0:T(8,128)(2,1)S(1)}, s16[672,128]{1,0:T(8,128)(2,1)S(1)}, u32[]{:S(2)}, u32[]{:S(2)}) collective-permute-start(s16[672,128]{1,0:T(8,128)(2,1)S(1)} %get-tuple-element.75), channel_id=1, source_target_pairs={{0,2},{1,3},{2,0},{3,1},{4,6},{5,7},{6,4},{7,5},{8,10},{9,11},{10,... | collective-permute-start | bytes 516104 | tf_op jit(solution)/shard_map/ppermute | solution.py:1170
  36.2 0.9 inverse_rest.2
  37.1 0.1 collective-permute-start.7
  37.2 0.6 collective-permute-start.8
  37.8 1.1 %near_field.2.refs_8_.refs_0_ = f32[8,128]{1,0:T(8,128)S(1)} custom-call(s32[24]{0:T(128)S(1)} %get-tuple-element.100.place_ref, s32[24]{0:T(128)S(1)} %get-tuple-element.99.target_ref, s16[432,128]{1,0:T(8,128)(2,1)S(1)} %collective-permute-done.5.even_ref.refs_2_.refs_0_, s16[592,128]{1,0:T(8,128)(2,1)S(1)} %collective-permute-done.4.odd_ref.refs_3_.refs_1_, ...), custom_call_target="tpu_custom_call" | custom-call | flops 12582912 | bytes 786432 | tf_op jit(solution)/shard_map/near_field/pallas_call | solution.py:1104
  38.9 3.0 %place_lines.1.refs_5_ = f32[8192,128]{1,0:T(8,128)S(1)} custom-call(s32[2,512]{1,0:T(2,128)S(1)} %get-tuple-element.52.place_ref.refs_1_, f32[256,128]{1,0:T(8,128)S(1)} %get-tuple-element.77.coeff_ref, f32[8,128]{1,0:T(8,128)S(1)} %near_field.2.refs_8_.refs_0_), custom_call_target="tpu_custom_call" | custom-call | flops 1048576 | bytes 4194304 | tf_op jit(solution)/shard_map/place_lines/pallas_call | solution.py:482
  41.9 0.0 collective-permute-done.9.refs_1_
  41.9 0.5 sample_early.2.refs_2_
  42.4 0.0 collective-permute-done.7.refs_0_
  42.4 1.6 %collective-permute-done.8.refs_1_ = s16[672,128]{1,0:T(8,128)(2,1)S(1)} collective-permute-done((s16[672,128]{1,0:T(8,128)(2,1)S(1)}, s16[672,128]{1,0:T(8,128)(2,1)S(1)}, u32[]{:S(2)}, u32[]{:S(2)}) %collective-permute-start.8) | collective-permute-done | bytes 172064 | tf_op jit(solution)/shard_map/ppermute | solution.py:1170
  44.0 2.9 %sample.2.refs_2_.rounded_ref.refs_7_ = f32[4,128]{1,0:T(4,128)S(1)} custom-call(s32[2,512]{1,0:T(2,128)S(1)} %get-tuple-element.52.place_ref.refs_1_, s16[672,128]{1,0:T(8,128)(2,1)S(1)} %collective-permute-done.7.refs_0_, s16[672,128]{1,0:T(8,128)(2,1)S(1)} %collective-permute-done.8.refs_1_, f32[656,256]{1,0:T(8,128)S(1)} %sample_early.2.refs_2_, ...), custom_call_target="tpu_custom_call" | custom-call | flops 169869312 | bytes 4194304 | tf_op jit(solution)/shard_map/sample/pallas_call | solution.py:1048
  46.9 2.8 %spread.1 = (s16[672,128]{1,0:T(8,128)(2,1)S(1)}, s16[672,128]{1,0:T(8,128)(2,1)S(1)}, bf16[656,256]{1,0:T(8,128)(2,1)S(1)}, bf16[656,256]{1,0:T(8,128)(2,1)S(1)}) custom-call(f32[512]{0:T(512)S(1)} %bitcast.6, s32[2,512]{1,0:T(2,128)S(1)} %get-tuple-element.52.place_ref.refs_1_, f32[4,128]{1,0:T(4,128)S(1)} %sample.2.refs_2_.rounded_ref.refs_7_, ...), custom_call_target="tpu_custom_call" | custom-call | flops 169869312 | bytes 4194304 | tf_op jit(solution)/shard_map/spread/pallas_call | solution.py:397
  49.8 1.1 %collective-permute-start.11 = (s16[672,128]{1,0:T(8,128)(2,1)S(1)}, s16[672,128]{1,0:T(8,128)(2,1)S(1)}, u32[]{:S(2)}, u32[]{:S(2)}) collective-permute-start(s16[672,128]{1,0:T(8,128)(2,1)S(1)} %get-tuple-element.82), channel_id=1, source_target_pairs={{0,2},{1,3},{2,0},{3,1},{4,6},{5,7},{6,4},{7,5},{8,10},{9,11},{10,... | collective-permute-start | bytes 516104 | tf_op jit(solution)/shard_map/ppermute | solution.py:1170
  50.9 0.6 spread_rest.3
  51.4 0.7 collective-permute-start.10
  52.1 0.5 collective-permute-start.12
  52.6 4.4 %collective-permute-done.11.refs_1_.refs_2_ = s16[672,128]{1,0:T(8,128)(2,1)S(1)} collective-permute-done((s16[672,128]{1,0:T(8,128)(2,1)S(1)}, s16[672,128]{1,0:T(8,128)(2,1)S(1)}, u32[]{:S(2)}, u32[]{:S(2)}) %collective-permute-start.11) | collective-permute-done | bytes 172064 | tf_op jit(solution)/shard_map/ppermute | solution.py:1170
  57.0 0.7 forward_early.3
  57.7 0.0 collective-permute-done.10.refs_1_
  57.7 2.1 %collective-permute-done.12.refs_3_ = s16[672,128]{1,0:T(8,128)(2,1)S(1)} collective-permute-done((s16[672,128]{1,0:T(8,128)(2,1)S(1)}, s16[672,128]{1,0:T(8,128)(2,1)S(1)}, u32[]{:S(2)}, u32[]{:S(2)}) %collective-permute-start.12) | collective-permute-done | bytes 172064 | tf_op jit(solution)/shard_map/ppermute | solution.py:1170
  59.8 1.9 %forward.3 = (f32[18,256,128]{2,1,0:T(8,128)S(1)}, s16[432,128]{1,0:T(8,128)(2,1)S(1)}, s16[304,128]{1,0:T(8,128)(2,1)S(1)}, s16[592,128]{1,0:T(8,128)(2,1)S(1)}...) custom-call(s16[672,128]{1,0:T(8,128)(2,1)S(1)} %get-tuple-element.80.refs_0_, ...), custom_call_target="tpu_custom_call" | custom-call | flops 301989888 | bytes 4718592 | tf_op jit(solution)/shard_map/forward/pallas_call | solution.py:676
  61.7 0.1 collective-permute-start.15
  61.8 0.9 collective-permute-start.14
  62.7 4.8 %collective-permute-start.13 = (s16[304,128]{1,0:T(8,128)(2,1)S(1)}, s16[304,128]{1,0:T(8,128)(2,1)S(1)}, u32[]{:S(2)}, u32[]{:S(2)}) collective-permute-start(s16[304,128]{1,0:T(8,128)(2,1)S(1)} %get-tuple-element.87), channel_id=1, source_target_pairs={{0,4},{8,12},{4,0},{12,8},{1,5},{9,13},{5,1},{13,9},{2,6},{10,14},... | collective-permute-start | bytes 233480 | tf_op jit(solution)/shard_map/ppermute | solution.py:1184
  67.4 0.2 pair_messages.3
  67.6 1.0 %collective-permute-start.16 = (s16[272,128]{1,0:T(8,128)(2,1)S(1)}, s16[272,128]{1,0:T(8,128)(2,1)S(1)}, u32[]{:S(2)}, u32[]{:S(2)}) collective-permute-start(s16[272,128]{1,0:T(8,128)(2,1)S(1)} %pair_messages.3), channel_id=1, source_target_pairs={{0,8},{4,12},{8,0},{12,4},{1,9},{5,13},{9,1},{13,5},{2,10},{6,14},... | collective-permute-start | bytes 208904 | tf_op jit(solution)/shard_map/ppermute | solution.py:1186
  68.6 1.5 %collective-permute-done.13.layers_ref = s16[304,128]{1,0:T(8,128)(2,1)S(1)} collective-permute-done((s16[304,128]{1,0:T(8,128)(2,1)S(1)}, s16[304,128]{1,0:T(8,128)(2,1)S(1)}, u32[]{:S(2)}, u32[]{:S(2)}) %collective-permute-start.13) | collective-permute-done | bytes 77856 | tf_op jit(solution)/shard_map/ppermute | solution.py:1184
  70.1 0.4 borders.3.refs_1_
  70.5 3.4 %collective-permute-done.16.refs_6_ = s16[272,128]{1,0:T(8,128)(2,1)S(1)} collective-permute-done((s16[272,128]{1,0:T(8,128)(2,1)S(1)}, s16[272,128]{1,0:T(8,128)(2,1)S(1)}, u32[]{:S(2)}, u32[]{:S(2)}) %collective-permute-start.16) | collective-permute-done | bytes 69664 | tf_op jit(solution)/shard_map/ppermute | solution.py:1186
  74.0 2.9 %inverse.3 = (s16[672,128]{1,0:T(8,128)(2,1)S(1)}, s16[672,128]{1,0:T(8,128)(2,1)S(1)}, bf16[18,256,128]{2,1,0:T(8,128)(2,1)S(1)}, bf16[18,256,128]{2,1,0:T(8,128)(2,1)S(1)}) custom-call(f32[18,256,128]{2,1,0:T(8,128)S(1)} %get-tuple-element.86.refs_0_, f32[4,256,128]{2,1,0:T(8,128)S(1)} %borders.3.refs_1_, ...), custom_call_target="tpu_custom_call" | custom-call | flops 301989888 | bytes 4718592 | tf_op jit(solution)/shard_map/inverse/pallas_call | solution.py:908
  76.9 1.7 %collective-permute-start.19 = (s16[672,128]{1,0:T(8,128)(2,1)S(1)}, s16[672,128]{1,0:T(8,128)(2,1)S(1)}, u32[]{:S(2)}, u32[]{:S(2)}) collective-permute-start(s16[672,128]{1,0:T(8,128)(2,1)S(1)} %get-tuple-element.97), channel_id=1, source_target_pairs={{0,2},{1,3},{2,0},{3,1},{4,6},{5,7},{6,4},{7,5},{8,10},{9,11},{10,... | collective-permute-start | bytes 516104 | tf_op jit(solution)/shard_map/ppermute | solution.py:1170
  78.6 0.9 inverse_rest.3
  79.5 0.1 collective-permute-start.17
  79.6 0.5 collective-permute-start.18
  80.1 1.0 %near_field.3.refs_8_ = f32[8,128]{1,0:T(8,128)S(1)} custom-call(s32[24]{0:T(128)S(1)} %get-tuple-element.100.place_ref, s32[24]{0:T(128)S(1)} %get-tuple-element.99.target_ref, s16[432,128]{1,0:T(8,128)(2,1)S(1)} %collective-permute-done.15.even_ref.refs_2_.refs_0_, s16[592,128]{1,0:T(8,128)(2,1)S(1)} %collective-permute-done.14.odd_ref.refs_3_.refs_1_, ...), custom_call_target="tpu_custom_call" | custom-call | flops 12582912 | bytes 786432 | tf_op jit(solution)/shard_map/near_field/pallas_call | solution.py:1104
  81.1 2.3 %collective-permute-done.19.refs_1_ = s16[672,128]{1,0:T(8,128)(2,1)S(1)} collective-permute-done((s16[672,128]{1,0:T(8,128)(2,1)S(1)}, s16[672,128]{1,0:T(8,128)(2,1)S(1)}, u32[]{:S(2)}, u32[]{:S(2)}) %collective-permute-start.19) | collective-permute-done | bytes 172064 | tf_op jit(solution)/shard_map/ppermute | solution.py:1170
  83.4 0.4 sample_early.3.refs_2_
  83.9 2.4 %collective-permute-done.18.refs_1_ = s16[672,128]{1,0:T(8,128)(2,1)S(1)} collective-permute-done((s16[672,128]{1,0:T(8,128)(2,1)S(1)}, s16[672,128]{1,0:T(8,128)(2,1)S(1)}, u32[]{:S(2)}, u32[]{:S(2)}) %collective-permute-start.18) | collective-permute-done | bytes 172064 | tf_op jit(solution)/shard_map/ppermute | solution.py:1170
  86.3 3.6 %sample.3 = f32[2,512]{1,0:T(2,128)} custom-call(s32[2,512]{1,0:T(2,128)S(1)} %get-tuple-element.52.place_ref.refs_1_, s16[672,128]{1,0:T(8,128)(2,1)S(1)} %collective-permute-done.17.refs_0_, s16[672,128]{1,0:T(8,128)(2,1)S(1)} %collective-permute-done.18.refs_1_, f32[656,256]{1,0:T(8,128)S(1)} %sample_early.3.refs_2_, bf16[4,128,256]{2,1,0:T(8,128)(2,1)S(1)} %copy-done.5, ...), custom_call_target="tpu_custom_call" | custom-call | flops 169869312 | bytes 4194304 | tf_op jit(solution)/shard_map/sample/pallas_call | solution.py:1048
  (22 shorter events, 0.1 us)
Async XLA Ops:
  5.7 9.2 %collective-permute-start.1 = (s16[672,128]{1,0:T(8,128)(2,1)S(1)}, s16[672,128]{1,0:T(8,128)(2,1)S(1)}, u32[]{:S(2)}, u32[]{:S(2)}) collective-permute-start(s16[672,128]{1,0:T(8,128)(2,1)S(1)} %get-tuple-element.60), channel_id=1, source_target_pairs={{0,2},{1,3},{2,0},{3,1},{4,6},{5,7},{6,4},{7,5},{8,10},{9,11},{10,... | collective-permute-start | bytes 516104 | tf_op jit(solution)/shard_map/ppermute | solution.py:1170
  9.3 6.3 %collective-permute-start = (s16[672,128]{1,0:T(8,128)(2,1)S(1)}, s16[672,128]{1,0:T(8,128)(2,1)S(1)}, u32[]{:S(2)}, u32[]{:S(2)}) collective-permute-start(s16[672,128]{1,0:T(8,128)(2,1)S(1)} %get-tuple-element.59), channel_id=1, source_target_pairs={{0,1},{1,0},{2,3},{3,2},{4,5},{5,4},{6,7},{7,6},{8,9},{9,8},{10,11... | collective-permute-start | bytes 516104 | tf_op jit(solution)/shard_map/ppermute | solution.py:1170
  9.3 6.8 %collective-permute-start.2 = (s16[672,128]{1,0:T(8,128)(2,1)S(1)}, s16[672,128]{1,0:T(8,128)(2,1)S(1)}, u32[]{:S(2)}, u32[]{:S(2)}) collective-permute-start(s16[672,128]{1,0:T(8,128)(2,1)S(1)} %get-tuple-element.61), channel_id=1, source_target_pairs={{0,3},{1,2},{2,1},{3,0},{4,7},{5,6},{6,5},{7,4},{8,11},{9,10},{10,... | collective-permute-start | bytes 516104 | tf_op jit(solution)/shard_map/ppermute | solution.py:1170
  9.5 0.9 %copy-start.1 = (f32[64,512]{1,0:T(8,128)S(1)}, f32[64,512]{1,0:T(8,128)}, u32[]{:S(2)}) copy-start(f32[64,512]{1,0:T(8,128)} %refs_3_.8) | copy-start | bytes 393220
  10.4 4.5 %copy-start = (bf16[2,256,240]{2,1,0:T(8,128)(2,1)S(1)}, bf16[2,256,240]{2,1,0:T(8,128)(2,1)}, u32[]{:S(2)}) copy-start(bf16[2,256,240]{2,1,0:T(8,128)(2,1)} %constant.76.clone.refs_2_.refs_6_.table_ref) | copy-start | bytes 737284
  16.2 15.6 %copy-start.3 = (bf16[4,48,256]{2,1,0:T(8,128)(2,1)S(1)}, bf16[4,48,256]{2,1,0:T(8,128)(2,1)}, u32[]{:S(2)}) copy-start(bf16[4,48,256]{2,1,0:T(8,128)(2,1)} %constant.77.clone.refs_7_.high_ref) | copy-start | bytes 294916
  16.2 15.6 %copy-start.4 = (bf16[4,48,256]{2,1,0:T(8,128)(2,1)S(1)}, bf16[4,48,256]{2,1,0:T(8,128)(2,1)}, u32[]{:S(2)}) copy-start(bf16[4,48,256]{2,1,0:T(8,128)(2,1)} %constant.78.clone.refs_8_.low_ref) | copy-start | bytes 294916
  18.1 6.7 %collective-permute-start.5 = (s16[432,128]{1,0:T(8,128)(2,1)S(1)}, s16[432,128]{1,0:T(8,128)(2,1)S(1)}, u32[]{:S(2)}, u32[]{:S(2)}) collective-permute-start(s16[432,128]{1,0:T(8,128)(2,1)S(1)} %get-tuple-element.67), channel_id=1, source_target_pairs={{0,4},{8,12},{4,0},{12,8},{1,5},{9,13},{5,1},{13,9},{2,6},{10,14},... | collective-permute-start | bytes 331784 | tf_op jit(solution)/shard_map/ppermute | solution.py:1182
  19.7 7.8 %collective-permute-start.4 = (s16[592,128]{1,0:T(8,128)(2,1)S(1)}, s16[592,128]{1,0:T(8,128)(2,1)S(1)}, u32[]{:S(2)}, u32[]{:S(2)}) collective-permute-start(s16[592,128]{1,0:T(8,128)(2,1)S(1)} %get-tuple-element.66), channel_id=1, source_target_pairs={{4,8},{8,4},{5,9},{9,5},{6,10},{10,6},{7,11},{11,7},{20,24},{24,20... | collective-permute-start | bytes 454664 | tf_op jit(solution)/shard_map/ppermute | solution.py:1183
  20.4 7.1 %collective-permute-start.3 = (s16[304,128]{1,0:T(8,128)(2,1)S(1)}, s16[304,128]{1,0:T(8,128)(2,1)S(1)}, u32[]{:S(2)}, u32[]{:S(2)}) collective-permute-start(s16[304,128]{1,0:T(8,128)(2,1)S(1)} %get-tuple-element.65), channel_id=1, source_target_pairs={{0,4},{8,12},{4,0},{12,8},{1,5},{9,13},{5,1},{13,9},{2,6},{10,14},... | collective-permute-start | bytes 233480 | tf_op jit(solution)/shard_map/ppermute | solution.py:1184
  25.0 11.2 %copy-start.8 = (s32[24]{0:T(128)S(1)}, s32[24]{0:T(128)}, u32[]{:S(2)}) copy-start(s32[24]{0:T(128)} %param.21) | copy-start | bytes 292
  25.0 11.2 %copy-start.9 = (s32[24]{0:T(128)S(1)}, s32[24]{0:T(128)}, u32[]{:S(2)}) copy-start(s32[24]{0:T(128)} %param.22) | copy-start | bytes 292
  25.1 6.6 %collective-permute-start.6 = (s16[272,128]{1,0:T(8,128)(2,1)S(1)}, s16[272,128]{1,0:T(8,128)(2,1)S(1)}, u32[]{:S(2)}, u32[]{:S(2)}) collective-permute-start(s16[272,128]{1,0:T(8,128)(2,1)S(1)} %pair_messages.2), channel_id=1, source_target_pairs={{0,8},{4,12},{8,0},{12,4},{1,9},{5,13},{9,1},{13,5},{2,10},{6,14},... | collective-permute-start | bytes 208904 | tf_op jit(solution)/shard_map/ppermute | solution.py:1186
  31.7 6.1 %copy-start.2 = (bf16[24,128,128]{2,1,0:T(8,128)(2,1)S(1)}, bf16[24,128,128]{2,1,0:T(8,128)(2,1)}, u32[]{:S(2)}) copy-start(bf16[24,128,128]{2,1,0:T(8,128)(2,1)} %refs_3_.10) | copy-start | bytes 2359300
  34.6 7.2 %collective-permute-start.9 = (s16[672,128]{1,0:T(8,128)(2,1)S(1)}, s16[672,128]{1,0:T(8,128)(2,1)S(1)}, u32[]{:S(2)}, u32[]{:S(2)}) collective-permute-start(s16[672,128]{1,0:T(8,128)(2,1)S(1)} %get-tuple-element.75), channel_id=1, source_target_pairs={{0,2},{1,3},{2,0},{3,1},{4,6},{5,7},{6,4},{7,5},{8,10},{9,11},{10,... | collective-permute-start | bytes 516104 | tf_op jit(solution)/shard_map/ppermute | solution.py:1170
  37.1 5.2 %collective-permute-start.7 = (s16[672,128]{1,0:T(8,128)(2,1)S(1)}, s16[672,128]{1,0:T(8,128)(2,1)S(1)}, u32[]{:S(2)}, u32[]{:S(2)}) collective-permute-start(s16[672,128]{1,0:T(8,128)(2,1)S(1)} %get-tuple-element.72), channel_id=1, source_target_pairs={{0,1},{1,0},{2,3},{3,2},{4,5},{5,4},{6,7},{7,6},{8,9},{9,8},{10,11... | collective-permute-start | bytes 516104 | tf_op jit(solution)/shard_map/ppermute | solution.py:1170
  37.2 6.8 %collective-permute-start.8 = (s16[672,128]{1,0:T(8,128)(2,1)S(1)}, s16[672,128]{1,0:T(8,128)(2,1)S(1)}, u32[]{:S(2)}, u32[]{:S(2)}) collective-permute-start(s16[672,128]{1,0:T(8,128)(2,1)S(1)} %get-tuple-element.73), channel_id=1, source_target_pairs={{0,3},{1,2},{2,1},{3,0},{4,7},{5,6},{6,5},{7,4},{8,11},{9,10},{10,... | collective-permute-start | bytes 516104 | tf_op jit(solution)/shard_map/ppermute | solution.py:1170
  38.9 3.0 %copy-start.5 = (bf16[4,128,256]{2,1,0:T(8,128)(2,1)S(1)}, bf16[4,128,256]{2,1,0:T(8,128)(2,1)}, u32[]{:S(2)}) copy-start(bf16[4,128,256]{2,1,0:T(8,128)(2,1)} %constant.79.clone.refs_2_.refs_3_) | copy-start | bytes 786436
  38.9 3.0 %copy-start.6 = (bf16[4,128,256]{2,1,0:T(8,128)(2,1)S(1)}, bf16[4,128,256]{2,1,0:T(8,128)(2,1)}, u32[]{:S(2)}) copy-start(bf16[4,128,256]{2,1,0:T(8,128)(2,1)} %constant.80.clone.refs_3_.refs_4_) | copy-start | bytes 786436
  41.9 2.1 %copy-start.7 = (s32[512]{0:T(512)S(1)}, s32[512]{0:T(512)}, u32[]{:S(2)}) copy-start(s32[512]{0:T(512)} %param.17) | copy-start | bytes 6148
  49.8 7.2 %collective-permute-start.11 = (s16[672,128]{1,0:T(8,128)(2,1)S(1)}, s16[672,128]{1,0:T(8,128)(2,1)S(1)}, u32[]{:S(2)}, u32[]{:S(2)}) collective-permute-start(s16[672,128]{1,0:T(8,128)(2,1)S(1)} %get-tuple-element.82), channel_id=1, source_target_pairs={{0,2},{1,3},{2,0},{3,1},{4,6},{5,7},{6,4},{7,5},{8,10},{9,11},{10,... | collective-permute-start | bytes 516104 | tf_op jit(solution)/shard_map/ppermute | solution.py:1170
  51.4 6.2 %collective-permute-start.10 = (s16[672,128]{1,0:T(8,128)(2,1)S(1)}, s16[672,128]{1,0:T(8,128)(2,1)S(1)}, u32[]{:S(2)}, u32[]{:S(2)}) collective-permute-start(s16[672,128]{1,0:T(8,128)(2,1)S(1)} %get-tuple-element.81), channel_id=1, source_target_pairs={{0,1},{1,0},{2,3},{3,2},{4,5},{5,4},{6,7},{7,6},{8,9},{9,8},{10,11... | collective-permute-start | bytes 516104 | tf_op jit(solution)/shard_map/ppermute | solution.py:1170
  52.1 7.7 %collective-permute-start.12 = (s16[672,128]{1,0:T(8,128)(2,1)S(1)}, s16[672,128]{1,0:T(8,128)(2,1)S(1)}, u32[]{:S(2)}, u32[]{:S(2)}) collective-permute-start(s16[672,128]{1,0:T(8,128)(2,1)S(1)} %get-tuple-element.83), channel_id=1, source_target_pairs={{0,3},{1,2},{2,1},{3,0},{4,7},{5,6},{6,5},{7,4},{8,11},{9,10},{10,... | collective-permute-start | bytes 516104 | tf_op jit(solution)/shard_map/ppermute | solution.py:1170
  61.7 5.7 %collective-permute-start.15 = (s16[432,128]{1,0:T(8,128)(2,1)S(1)}, s16[432,128]{1,0:T(8,128)(2,1)S(1)}, u32[]{:S(2)}, u32[]{:S(2)}) collective-permute-start(s16[432,128]{1,0:T(8,128)(2,1)S(1)} %get-tuple-element.89), channel_id=1, source_target_pairs={{0,4},{8,12},{4,0},{12,8},{1,5},{9,13},{5,1},{13,9},{2,6},{10,14},... | collective-permute-start | bytes 331784 | tf_op jit(solution)/shard_map/ppermute | solution.py:1182
  61.8 8.3 %collective-permute-start.14 = (s16[592,128]{1,0:T(8,128)(2,1)S(1)}, s16[592,128]{1,0:T(8,128)(2,1)S(1)}, u32[]{:S(2)}, u32[]{:S(2)}) collective-permute-start(s16[592,128]{1,0:T(8,128)(2,1)S(1)} %get-tuple-element.88), channel_id=1, source_target_pairs={{4,8},{8,4},{5,9},{9,5},{6,10},{10,6},{7,11},{11,7},{20,24},{24,20... | collective-permute-start | bytes 454664 | tf_op jit(solution)/shard_map/ppermute | solution.py:1183
  62.7 7.4 %collective-permute-start.13 = (s16[304,128]{1,0:T(8,128)(2,1)S(1)}, s16[304,128]{1,0:T(8,128)(2,1)S(1)}, u32[]{:S(2)}, u32[]{:S(2)}) collective-permute-start(s16[304,128]{1,0:T(8,128)(2,1)S(1)} %get-tuple-element.87), channel_id=1, source_target_pairs={{0,4},{8,12},{4,0},{12,8},{1,5},{9,13},{5,1},{13,9},{2,6},{10,14},... | collective-permute-start | bytes 233480 | tf_op jit(solution)/shard_map/ppermute | solution.py:1184
  67.6 6.4 %collective-permute-start.16 = (s16[272,128]{1,0:T(8,128)(2,1)S(1)}, s16[272,128]{1,0:T(8,128)(2,1)S(1)}, u32[]{:S(2)}, u32[]{:S(2)}) collective-permute-start(s16[272,128]{1,0:T(8,128)(2,1)S(1)} %pair_messages.3), channel_id=1, source_target_pairs={{0,8},{4,12},{8,0},{12,4},{1,9},{5,13},{9,1},{13,5},{2,10},{6,14},... | collective-permute-start | bytes 208904 | tf_op jit(solution)/shard_map/ppermute | solution.py:1186
  76.9 6.5 %collective-permute-start.19 = (s16[672,128]{1,0:T(8,128)(2,1)S(1)}, s16[672,128]{1,0:T(8,128)(2,1)S(1)}, u32[]{:S(2)}, u32[]{:S(2)}) collective-permute-start(s16[672,128]{1,0:T(8,128)(2,1)S(1)} %get-tuple-element.97), channel_id=1, source_target_pairs={{0,2},{1,3},{2,0},{3,1},{4,6},{5,7},{6,4},{7,5},{8,10},{9,11},{10,... | collective-permute-start | bytes 516104 | tf_op jit(solution)/shard_map/ppermute | solution.py:1170
  79.5 4.4 %collective-permute-start.17 = (s16[672,128]{1,0:T(8,128)(2,1)S(1)}, s16[672,128]{1,0:T(8,128)(2,1)S(1)}, u32[]{:S(2)}, u32[]{:S(2)}) collective-permute-start(s16[672,128]{1,0:T(8,128)(2,1)S(1)} %get-tuple-element.94), channel_id=1, source_target_pairs={{0,1},{1,0},{2,3},{3,2},{4,5},{5,4},{6,7},{7,6},{8,9},{9,8},{10,11... | collective-permute-start | bytes 516104 | tf_op jit(solution)/shard_map/ppermute | solution.py:1170
  79.6 6.7 %collective-permute-start.18 = (s16[672,128]{1,0:T(8,128)(2,1)S(1)}, s16[672,128]{1,0:T(8,128)(2,1)S(1)}, u32[]{:S(2)}, u32[]{:S(2)}) collective-permute-start(s16[672,128]{1,0:T(8,128)(2,1)S(1)} %get-tuple-element.95), channel_id=1, source_target_pairs={{0,3},{1,2},{2,1},{3,0},{4,7},{5,6},{6,5},{7,4},{8,11},{9,10},{10,... | collective-permute-start | bytes 516104 | tf_op jit(solution)/shard_map/ppermute | solution.py:1170

commit v13 on v12

--- a/solution.py
+++ b/solution.py
@@ -277,19 +277,19 @@
 
 
 def start_kernel(reach_x, reach_y, flips, *refs):
-    vector_ref, *remote = refs[:8]
-    refs = refs[8:]
+    vector_ref, *remote = refs[:9]
+    refs = refs[9:]
     outs, refs = refs[: len(flips)], refs[len(flips) :]
     wides, (weight_ref, places_out), refs = refs[:2], refs[2:4], refs[4:]
-    rounded, high, low, stencil, flag, samples, dipoles = refs[:7]
-    place_ref, sems, head, total = refs[7:11]
-    grids = refs[11:]
+    rounded, high, low, modes, samples, stencil, flag, dipoles = refs[:8]
+    place_ref, sems, head, total = refs[8:12]
+    grids = refs[12:]
     tiles = samples.shape[0]
     copies = []
     fetch = lambda source, target: copies.append(
         pltpu.make_async_copy(source, target, sems.at[len(copies)])
     )
-    rounded_in, high_in, low_in, stencil_in, flag_in, sample_in, dipole_in = remote
+    rounded_in, high_in, low_in, stencil_in, flag_in, sample_in, dipole_in, modes_in = remote
     fetch(stencil_in, stencil)
     fetch(flag_in, flag)
     for tile in range(tiles):
@@ -300,6 +300,7 @@
     fetch(rounded_in, rounded)
     fetch(high_in, high)
     fetch(low_in, low)
+    fetch(modes_in.at[y_position()], modes)
     for copy in copies:
         copy.start()
     for grid in grids:
@@ -373,23 +374,23 @@
         pltpu.VMEM((reach_x * reach_y, REGION), F32),
     ] + [pltpu.VMEM((pair_count(reach_x, reach_y), REGION), F32)] * CHAINS
     if placed is None:
-        stencil, flag, sample, dipole = raw
-        operands = [vector, rounded, *table, stencil, flag.reshape(1, -1), sample, dipole]
+        stencil, flag, sample, dipole, modes = raw
+        operands = [vector, rounded, *table, stencil, flag.reshape(1, -1), sample, dipole, modes]
         pinned = [pltpu.with_memory_space_constraint(value, pltpu.HBM) for value in operands[1:]]
         operands = [vector] + pinned
-        in_specs = [in_smem()] + [pl.BlockSpec(memory_space=pltpu.HBM)] * 7
+        in_specs = [in_smem()] + [pl.BlockSpec(memory_space=pltpu.HBM)] * 8
         out_shapes += [jax.ShapeDtypeStruct(woven, F32)]
         out_shapes += [jax.ShapeDtypeStruct((2, count), jnp.int32)]
         out_shapes += [jax.ShapeDtypeStruct(rounded.shape, F32)]
         out_shapes += [jax.ShapeDtypeStruct(values.shape, BF16) for values in table]
-        tiled = pltpu.VMEM((blocks, 64, BLOCK), F32)
+        out_shapes += [jax.ShapeDtypeStruct(modes.shape[1:], F32)]
+        out_shapes += [jax.ShapeDtypeStruct((blocks, 64, BLOCK), F32)]
         work = [
             pltpu.VMEM(stencil.shape, jnp.int32),
             pltpu.VMEM((1, count), jnp.int32),
-            tiled,
-            tiled,
+            pltpu.VMEM((blocks, 64, BLOCK), F32),
             pltpu.SMEM((2, count), jnp.int32),
-            pltpu.SemaphoreType.DMA((6 + 2 * blocks,)),
+            pltpu.SemaphoreType.DMA((7 + 2 * blocks,)),
         ] + work
     else:
         operands = [vector, placed[0], rounded, *table, placed[1]]
@@ -452,28 +453,25 @@
     lax.fori_loop(0, place_ref.shape[1] // GROUP, body, 0)
 
 
-def sample_lines_kernel(tiles, place_ref, *refs):
-    out_ref, coeff = refs[-2:]
-    weave([by_depth(ref) for ref in refs[:tiles]], mixing_matrix(), coeff)
+def sample_lines_kernel(place_ref, sample_ref, out_ref, coeff):
+    tiles = [by_depth(sample_ref.at[tile]) for tile in range(sample_ref.shape[0])]
+    weave(tiles, mixing_matrix(), coeff)
     lines_kernel(place_ref, coeff, out_ref)
 
 
 def place_sample_lines(places, sample):
     count = places.shape[1]
-    blocks = count // BLOCK
-    tile = lambda t: pl.BlockSpec((64, BLOCK), lambda i: (0, t))
     shape = (count * 16, REGION)
     return pl.pallas_call(
-        functools.partial(sample_lines_kernel, blocks),
-        grid=(1,),
-        in_specs=[in_smem()] + [tile(t) for t in range(blocks)],
-        out_specs=pl.BlockSpec(shape, lambda i: (0, 0)),
+        sample_lines_kernel,
+        in_specs=[in_smem(), whole_vmem()],
+        out_specs=whole_vmem(),
         out_shape=jax.ShapeDtypeStruct(shape, F32),
         scratch_shapes=[pltpu.VMEM((count // GROUP * 16, BLOCK), F32)],
         compiler_params=params(),
         cost_estimate=cost(16 * count * REGION, 4 * 16 * count * REGION),
         name="place_sample_lines",
-    )(places, *[sample] * blocks)
+    )(places, sample)
 
 
 def place_lines(places, coeff, awaited):
@@ -490,6 +488,24 @@
     )(places, coeff, *awaited)
 
 
+def open_kernel(part_ref, out_ref):
+    top = part_ref.shape[0] - out_ref.shape[0]
+    first = from_short(part_ref[:top, :])
+    out_ref[...] = from_short(part_ref[top:, :]) * unit(first[0:1], first[1:2])
+
+
+def open_piece(part, rows):
+    return pl.pallas_call(
+        open_kernel,
+        in_specs=[whole_vmem()],
+        out_specs=whole_vmem(),
+        out_shape=jax.ShapeDtypeStruct((rows, 2 * HALF), F32),
+        compiler_params=params(),
+        cost_estimate=cost(EARLY_FLOPS, 6 * rows * 2 * HALF),
+        name="open_piece",
+    )(part)
+
+
 def put_edges(opened, reach_x, reach_y, edges, first):
     half = reach_x // 2
     low = low_lanes(reach_y)
@@ -511,11 +527,15 @@
 def stack_pieces(parts, reach_x, reach_y, top, opened, stacked, edges, places):
     chip = lax.axis_index("narrow")
     for flip, (part, place) in enumerate(zip(parts, places)):
-        first = from_short(part[:top, :])
-        opened[...] = from_short(part[top:, :]) * unit(first[0:1], first[1:2])
-        layers = [opened[i * reach_y : (i + 1) * reach_y, :] for i in range(reach_x // 2)]
+        if part.dtype == F32:
+            values = part
+        else:
+            values = opened
+            first = from_short(part[:top, :])
+            values[...] = from_short(part[top:, :]) * unit(first[0:1], first[1:2])
+        layers = [values[i * reach_y : (i + 1) * reach_y, :] for i in range(reach_x // 2)]
         stack_layers(layers, chip ^ flip, reach_y, stacked)
-        put_edges(opened, reach_x, reach_y, edges, place * 2 * reach_y)
+        put_edges(values, reach_x, reach_y, edges, place * 2 * reach_y)
 
 
 def transform_pieces(table, stacked, before, spectrum):
@@ -570,8 +590,10 @@
     )(*parts, table)
 
 
-def forward_kernel(reach_x, reach_y, blocks, pieces, awaited, *refs):
+def forward_kernel(reach_x, reach_y, blocks, pieces, before_opened, awaited, *refs):
     parts = refs[:pieces]
+    ready = dict(zip(before_opened, refs[pieces:]))
+    refs = refs[:pieces] + refs[pieces + len(before_opened) :]
     early_ref, early_edges, table_ref, modes_ref = refs[pieces : pieces + 4]
     refs = refs[pieces + 4 + awaited :]
     spectrum, even_out, layers_out, odd_out, own_out, peers_out, inner_out, *refs = refs
@@ -595,7 +617,8 @@
     before = early_ref
     for core in range(1, pair):
         places = range(core, pieces, pair)
-        stack_pieces(parts[core::pair], reach_x, reach_y, top, opened, stacked, edges, places)
+        held = [ready.get(flip, parts[flip]) for flip in places]
+        stack_pieces(held, reach_x, reach_y, top, opened, stacked, edges, places)
         transform_pieces(table_ref[lax.axis_index("pair") ^ core], stacked, before, spectrum)
         before = spectrum
 
@@ -666,7 +689,9 @@
             send(odd_out, top, [(slabs[odd], largest[odd]), with_most(edges[1 - odd])])
 
 
-def forward(parts, early, early_edges, table, modes, reach_x, reach_y, blocks, awaited):
+def forward(
+    parts, ready, early, early_edges, table, modes, reach_x, reach_y, blocks, awaited
+):
     pieces = len(parts)
     half = reach_x // 2
     lanes = 2 * HALF
@@ -675,9 +700,9 @@
     short = lambda rows: jax.ShapeDtypeStruct((rows, lanes), jnp.int16)
     return pl.pallas_call(
         functools.partial(
-            forward_kernel, reach_x, reach_y, blocks, pieces, len(awaited)
+            forward_kernel, reach_x, reach_y, blocks, pieces, list(ready), len(awaited)
         ),
-        in_specs=[whole_vmem()] * (pieces + 4) + [anywhere()] * len(awaited),
+        in_specs=[whole_vmem()] * (pieces + len(ready) + 4) + [anywhere()] * len(awaited),
         out_specs=[whole_vmem()] * 7,
         out_shape=[
             jax.ShapeDtypeStruct((half, GRID, lanes), F32),
@@ -697,7 +722,7 @@
         compiler_params=params(),
         cost_estimate=cost(2 * half * 256 * 256 * 128, 4 * half * GRID * lanes * 2),
         name="forward",
-    )(*parts, early, early_edges, table, modes, *awaited)
+    )(*parts, *ready.values(), early, early_edges, table, modes, *awaited)
 
 
 def opened_part(ref, index, first, rows):
@@ -965,8 +990,11 @@
     mine = y_position()
     opened = []
     for part in parts:
-        first = from_short(part[:16, :])
-        opened.append(from_short(part[16:, :]) * unit(first[0:1], first[1:2]))
+        if part.dtype == F32:
+            opened.append(part[...])
+        else:
+            first = from_short(part[:16, :])
+            opened.append(from_short(part[16:, :]) * unit(first[0:1], first[1:2]))
     values = split(jnp.concatenate(opened, axis=1))
     pick = lambda ref: jnp.concatenate([ref[mine ^ flip] for flip in flips], axis=0)
     return dot_three(values, (pick(high_ref), pick(low_ref)))
@@ -1144,7 +1172,6 @@
     blocks = count // BLOCK
 
     z_forward, z_inverse, y_forward, y_inverse, modes = tables(y_count, pair, span_y)
-    modes = lax.dynamic_index_in_dim(jnp.asarray(modes), y_index, 0, keepdims=False)
 
     neighbour = near_source // blocks
     flip = (y_index + neighbour % 3 - 1) ^ y_index
@@ -1173,11 +1200,24 @@
     def chosen(parts, flips):
         return [parts[flip] for flip in flips]
 
-    def convolve_and_sample(last, vector, sent, both, table, places, sample_lines, awaited):
+    def opened(parts):
+        rows = up_to(reach_x * reach_y // 2, 16)
+        return {flip: open_piece(parts[flip], rows) for flip in first if flip in other_core}
+
+    def convolve_and_sample(last, vector, sent, both, table, modes, places, sample_lines, awaited):
         arrived = turned(sent, spread_rest(vector, both, table, rest))
         early, edges = forward_early(chosen(arrived, same_core), y_forward, reach_x, reach_y)
         spectrum, even_message, layers, odd_message, own, peers, inner = forward(
-            arrived, early, edges, y_forward, modes, reach_x, reach_y, blocks, awaited
+            arrived,
+            opened(arrived),
+            early,
+            edges,
+            y_forward,
+            modes,
+            reach_x,
+            reach_y,
+            blocks,
+            awaited,
         )
         from_even = lax.ppermute(even_message, "wide", even_swap)
         from_odd = lax.ppermute(odd_message, "wide", odd_swap)
@@ -1207,10 +1247,11 @@
             sources, targets, from_even, from_odd, peers, near_tiles, blocks, out_rows, then[:1]
         )
         arrived = turned(sent, then)
+        ready = opened(arrived)
         image = sample(
             last,
             places,
-            chosen(arrived, other_core),
+            [ready.get(flip, arrived[flip]) for flip in other_core],
             other_core,
             sample_early(chosen(arrived, same_core), same_core, z_inverse),
             z_inverse,
@@ -1223,18 +1264,19 @@
         )
         return image, near_part
 
-    raw = (stencil_base, surface_flag, sample_weights, dipole_weights)
-    *sent, wide_high, wide_low, source_coeff, places, vector, high, low = spread(
+    raw = (stencil_base, surface_flag, sample_weights, dipole_weights, jnp.asarray(modes))
+    *sent, wide_high, wide_low, source_coeff, places, vector, high, low, modes, samples = spread(
         density, z_forward, None, raw, reach_x, reach_y, first
     )
     z_forward = (high, low)
-    sample_lines = place_sample_lines(places, sample_weights)
+    sample_lines = place_sample_lines(places, samples)
     vector, near_part = convolve_and_sample(
         False,
         vector,
         sent,
         (wide_high, wide_low),
         z_forward,
+        modes,
         places,
         sample_lines,
         [sample_lines],
@@ -1244,7 +1286,7 @@
         vector.reshape(-1), z_forward, (places, source_lines), None, reach_x, reach_y, first
     )
     both_images, _ = convolve_and_sample(
-        True, vector, sent, (wide_high, wide_low), z_forward, places, sample_lines, []
+        True, vector, sent, (wide_high, wide_low), z_forward, modes, places, sample_lines, []
     )
     return both_images
 

time: 90.2 us -> 102 us (1.13); the launches traced: 89.9 us -> 101 us
  local copies, waits for them, and re-layouts: 2.02 us -> 6.04 us
  Pallas kernels: 39.5 us -> 43.4 us
  waiting for transfers between devices: 22.9 us -> 26.7 us
  starting transfers between devices: 25.1 us -> 24 us
    unnamed x20 -> x44, local copies, waits for them, and re-layouts: 0.94 us -> 6.04 us
    ppermute x12, waiting for transfers between devices: 13.4 us -> 18.2 us  [turned(): lax.ppermute(part, Y_AXES, swap_pairs)]
    squeeze x1 -> x0, local copies, waits for them, and re-layouts: 1.08 us -> none  [shards(): lax.dynamic_index_in_dim(jnp.asarray(modes), y_index, 0, keepdims=False)]
    ppermute x2, starting transfers between devices: 2.62 us -> 1.56 us  [convolve_and_sample(): lax.ppermute(message, 'wide', [(i, i ^ flip) for i in range(x_count)])]
    pallas_call x2, Pallas kernels: 5.84 us -> 6.88 us  [inverse(): pl.pallas_call(functools.partial(inverse_kernel, reach_x, reach_y, flips,...]
    pallas_call x1 -> x5, Pallas kernels: 3.41 us -> 3.56 us  [the longest x1 3.41 us: place_sample_lines(): pl.pallas_call(sample_lines_kernel, in_specs=[in_smem(), whole_vmem()], o...]
  transfers between devices with their start and end apart: 20 -> 20, of which waited for: 10 -> 10; matrix products, arithmetic and copies ran while one was open for 1% -> 0% of each run, Pallas kernels for 16% -> 17%
where the time goes in v13:
time: 102 us; the launch traced here: 101 us
  Pallas kernels  43.4 us (43%)
  waiting for transfers between devices  26.7 us (26%)
  starting transfers between devices  24 us (24%)
  local copies, waits for them, and re-layouts  6.04 us (6%)
    ppermute x12, waiting for transfers between devices, turned(): lax.ppermute(part, Y_AXES, swap_pairs)  18.2 us
    ppermute x12, starting transfers between devices, turned(): lax.ppermute(part, Y_AXES, swap_pairs)  9.46 us
    pallas_call x2, Pallas kernels, spread(): pl.pallas_call(functools.partial(start_kernel if placed is None else spre...  8.55 us
    ppermute x2, starting transfers between devices, convolve_and_sample(): even_layers = lax.ppermute(layers, 'wide', even_swap)  8.52 us
    pallas_call x2, Pallas kernels, inverse(): pl.pallas_call(functools.partial(inverse_kernel, reach_x, reach_y, flips,...  6.88 us
    ppermute x2, waiting for transfers between devices, convolve_and_sample(): lax.ppermute(message, 'wide', [(i, i ^ flip) for i in range(x_count)])  6.66 us
    pallas_call x2, Pallas kernels, sample(): pl.pallas_call(functools.partial(sample_kernel, last, reach_x, reach_y, f...  6.49 us
    unnamed x44, local copies, waits for them, and re-layouts  6.04 us
  transfers between devices with their start and end apart: 20, of which 10 were waited for; matrix products, arithmetic and copies ran while one was open for 0% of the time, Pallas kernels for 17%

profile of v13, /device:TPU:0, one launch (start us, length us, event | category | flops | bytes accessed | tf_op | source)
XLA Modules:
  0.0 100.6 jit_solution(5557012051366965863)
XLA Ops:
  0.0 5.7 %start.1 = (s16[672,128]{1,0:T(8,128)(2,1)S(1)}, s16[672,128]{1,0:T(8,128)(2,1)S(1)}, bf16[656,256]{1,0:T(8,128)(2,1)S(1)}, bf16[656,256]{1,0:T(8,128)(2,1)S(1)}...) custom-call(f32[512]{0:T(512)} %refs_0_.1, ...), custom_call_target="tpu_custom_call" | custom-call | flops 169869312 | bytes 4194304 | tf_op jit(solution)/shard_map/start/pallas_call | solution.py:398
  5.7 2.4 %collective-permute-start.2 = (s16[672,128]{1,0:T(8,128)(2,1)S(1)}, s16[672,128]{1,0:T(8,128)(2,1)S(1)}, u32[]{:S(2)}, u32[]{:S(2)}) collective-permute-start(s16[672,128]{1,0:T(8,128)(2,1)S(1)} %get-tuple-element.63), channel_id=1, source_target_pairs={{0,3},{1,2},{2,1},{3,0},{4,7},{5,6},{6,5},{7,4},{8,11},{9,10},{10,... | collective-permute-start | bytes 516104 | tf_op jit(solution)/shard_map/ppermute | solution.py:1197
  8.2 0.6 collective-permute-start.1
  8.8 0.6 spread_rest.2
  9.4 0.1 collective-permute-start
  9.5 3.4 %place_sample_lines.1.refs_9_.refs_5_ = f32[8192,128]{1,0:T(8,128)S(1)} custom-call(s32[2,512]{1,0:T(2,128)S(1)} %get-tuple-element.54.place_ref.refs_1_, f32[4,64,128]{2,1,0:T(8,128)S(1)} %get-tuple-element.67.sample_ref), custom_call_target="tpu_custom_call" | custom-call | flops 1048576 | bytes 4194304 | tf_op jit(solution)/shard_map/place_sample_lines/pallas_call | solution.py:465
  12.9 0.0 collective-permute-done.2.part_ref.refs_3_
  13.0 3.8 %collective-permute-done.1.refs_1_.refs_2_ = s16[672,128]{1,0:T(8,128)(2,1)S(1)} collective-permute-done((s16[672,128]{1,0:T(8,128)(2,1)S(1)}, s16[672,128]{1,0:T(8,128)(2,1)S(1)}, u32[]{:S(2)}, u32[]{:S(2)}) %collective-permute-start.1) | collective-permute-done | bytes 172064 | tf_op jit(solution)/shard_map/ppermute | solution.py:1197
  16.8 0.7 forward_early.2
  17.5 0.0 copy-start.6
  17.5 2.7 %forward.2 = (f32[18,256,128]{2,1,0:T(8,128)S(1)}, s16[432,128]{1,0:T(8,128)(2,1)S(1)}, s16[304,128]{1,0:T(8,128)(2,1)}, s16[592,128]{1,0:T(8,128)(2,1)}, f32[25...) custom-call(s16[672,128]{1,0:T(8,128)(2,1)S(1)} %get-tuple-element.60.refs_0_, ...), custom_call_target="tpu_custom_call" | custom-call | flops 301989888 | bytes 4718592 | tf_op jit(solution)/shard_map/forward/pallas_call | solution.py:701
  20.2 2.4 %collective-permute-start.5 = (s16[432,128]{1,0:T(8,128)(2,1)S(1)}, s16[432,128]{1,0:T(8,128)(2,1)S(1)}, u32[]{:S(2)}, u32[]{:S(2)}) collective-permute-start(s16[432,128]{1,0:T(8,128)(2,1)S(1)} %get-tuple-element.71), channel_id=1, source_target_pairs={{0,4},{8,12},{4,0},{12,8},{1,5},{9,13},{5,1},{13,9},{2,6},{10,14},... | collective-permute-start | bytes 331784 | tf_op jit(solution)/shard_map/ppermute | solution.py:1222
  22.5 1.3 %collective-permute-start.4 = (s16[592,128]{1,0:T(8,128)(2,1)}, s16[592,128]{1,0:T(8,128)(2,1)}, u32[]{:S(2)}, u32[]{:S(2)}) collective-permute-start(s16[592,128]{1,0:T(8,128)(2,1)} %get-tuple-element.70), channel_id=1, source_target_pairs={{4,8},{8,4},{5,9},{9,5},{6,10},{10,6},{7,11},{11,7},{20,24},{24,20... | collective-permute-start | bytes 454664 | tf_op jit(solution)/shard_map/ppermute | solution.py:1223
  23.9 3.8 %collective-permute-start.3 = (s16[304,128]{1,0:T(8,128)(2,1)}, s16[304,128]{1,0:T(8,128)(2,1)}, u32[]{:S(2)}, u32[]{:S(2)}) collective-permute-start(s16[304,128]{1,0:T(8,128)(2,1)} %get-tuple-element.69), channel_id=1, source_target_pairs={{0,4},{8,12},{4,0},{12,8},{1,5},{9,13},{5,1},{13,9},{2,6},{10,14},... | collective-permute-start | bytes 233480 | tf_op jit(solution)/shard_map/ppermute | solution.py:1224
  27.7 0.8 pair_messages.2
  28.5 0.7 copy-done.11
  29.1 0.9 collective-permute-start.6
  30.1 0.3 collective-permute-done.3.layers_ref
  30.4 1.4 %borders.2.refs_1_ = f32[4,256,128]{2,1,0:T(8,128)S(1)} custom-call(s16[304,128]{1,0:T(8,128)(2,1)} %collective-permute-done.3.layers_ref, s16[592,128]{1,0:T(8,128)(2,1)} %collective-permute-done.4.odd_ref.refs_3_.refs_1_, bf16[2,256,240]{2,1,0:T(8,128)(2,1)S(1)} %copy-done.2), custom_call_target="tpu_custom_call" | custom-call | flops 67108864 | bytes 786432 | tf_op jit(solution)/shard_map/borders/pallas_call | solution.py:807
  31.8 3.1 %collective-permute-done.6.refs_6_ = s16[272,128]{1,0:T(8,128)(2,1)} collective-permute-done((s16[272,128]{1,0:T(8,128)(2,1)}, s16[272,128]{1,0:T(8,128)(2,1)}, u32[]{:S(2)}, u32[]{:S(2)}) %collective-permute-start.6) | collective-permute-done | bytes 69664 | tf_op jit(solution)/shard_map/ppermute | solution.py:1226
  34.9 0.9 copy-done.7
  35.8 0.9 copy-done.12
  36.7 0.9 copy-done.14
  37.6 0.9 copy-done.18
  38.5 3.9 %inverse.2 = (s16[672,128]{1,0:T(8,128)(2,1)S(1)}, s16[672,128]{1,0:T(8,128)(2,1)S(1)}, bf16[18,256,128]{2,1,0:T(8,128)(2,1)S(1)}, bf16[18,256,128]{2,1,0:T(8,128)(2,1)S(1)}) custom-call(f32[18,256,128]{2,1,0:T(8,128)S(1)} %get-tuple-element.68.refs_0_, f32[4,256,128]{2,1,0:T(8,128)S(1)} %borders.2.refs_1_, s16[432,128]{1,0:T(8,128)(2,1)S(1)} %copy-done.12, ...), custom_call_target="tpu_custom_call" | custom-call | flops 301989888 | bytes 4718592 | tf_op jit(solution)/shard_map/inverse/pallas_call | solution.py:933
  42.5 0.1 collective-permute-start.8
  42.6 1.6 %collective-permute-start.9 = (s16[672,128]{1,0:T(8,128)(2,1)S(1)}, s16[672,128]{1,0:T(8,128)(2,1)S(1)}, u32[]{:S(2)}, u32[]{:S(2)}) collective-permute-start(s16[672,128]{1,0:T(8,128)(2,1)S(1)} %get-tuple-element.79), channel_id=1, source_target_pairs={{0,2},{1,3},{2,0},{3,1},{4,6},{5,7},{6,4},{7,5},{8,10},{9,11},{10,... | collective-permute-start | bytes 516104 | tf_op jit(solution)/shard_map/ppermute | solution.py:1197
  44.2 0.9 inverse_rest.2
  45.1 0.4 collective-permute-start.7
  45.4 1.2 %near_field.2.refs_8_.refs_0_ = f32[8,128]{1,0:T(8,128)S(1)} custom-call(s32[24]{0:T(128)S(1)} %get-tuple-element.104.place_ref, s32[24]{0:T(128)S(1)} %get-tuple-element.103.target_ref, s16[432,128]{1,0:T(8,128)(2,1)S(1)} %copy-done.12, s16[592,128]{1,0:T(8,128)(2,1)} %collective-permute-done.4.odd_ref.refs_3_.refs_1_, ...), custom_call_target="tpu_custom_call" | custom-call | flops 12582912 | bytes 786432 | tf_op jit(solution)/shard_map/near_field/pallas_call | solution.py:1132
  46.7 3.0 %place_lines.1.refs_5_ = f32[8192,128]{1,0:T(8,128)S(1)} custom-call(s32[2,512]{1,0:T(2,128)S(1)} %get-tuple-element.54.place_ref.refs_1_, f32[256,128]{1,0:T(8,128)S(1)} %copy-done.16, f32[8,128]{1,0:T(8,128)S(1)} %near_field.2.refs_8_.refs_0_), custom_call_target="tpu_custom_call" | custom-call | flops 1048576 | bytes 4194304 | tf_op jit(solution)/shard_map/place_lines/pallas_call | solution.py:480
  49.6 0.0 copy-start.10
  49.7 3.2 %collective-permute-done.9.refs_1_ = s16[672,128]{1,0:T(8,128)(2,1)S(1)} collective-permute-done((s16[672,128]{1,0:T(8,128)(2,1)S(1)}, s16[672,128]{1,0:T(8,128)(2,1)S(1)}, u32[]{:S(2)}, u32[]{:S(2)}) %collective-permute-start.9) | collective-permute-done | bytes 172064 | tf_op jit(solution)/shard_map/ppermute | solution.py:1197
  52.9 0.5 sample_early.2.refs_2_
  53.4 1.7 %copy-done.1 = f32[8192,128]{1,0:T(8,128)S(1)} copy-done((f32[8192,128]{1,0:T(8,128)S(1)}, f32[8192,128]{1,0:T(8,128)}, u32[]{:S(2)}) %copy-start.1) | copy-done | bytes 4194328
  55.1 2.9 %sample.2.refs_2_.rounded_ref.refs_7_ = f32[4,128]{1,0:T(4,128)S(1)} custom-call(s32[2,512]{1,0:T(2,128)S(1)} %get-tuple-element.54.place_ref.refs_1_, s16[672,128]{1,0:T(8,128)(2,1)S(1)} %collective-permute-done.7.refs_0_, f32[656,128]{1,0:T(8,128)S(1)} %open_piece.5.refs_1_, f32[656,256]{1,0:T(8,128)S(1)} %sample_early.2.refs_2_, ...), custom_call_target="tpu_custom_call" | custom-call | flops 169869312 | bytes 4194304 | tf_op jit(solution)/shard_map/sample/pallas_call | solution.py:1076
  58.0 2.8 %spread.1 = (s16[672,128]{1,0:T(8,128)(2,1)S(1)}, s16[672,128]{1,0:T(8,128)(2,1)S(1)}, bf16[656,256]{1,0:T(8,128)(2,1)S(1)}, bf16[656,256]{1,0:T(8,128)(2,1)S(1)}) custom-call(f32[512]{0:T(512)S(1)} %bitcast.4, s32[2,512]{1,0:T(2,128)S(1)} %get-tuple-element.54.place_ref.refs_1_, f32[4,128]{1,0:T(4,128)S(1)} %sample.2.refs_2_.rounded_ref.refs_7_, ...), custom_call_target="tpu_custom_call" | custom-call | flops 169869312 | bytes 4194304 | tf_op jit(solution)/shard_map/spread/pallas_call | solution.py:398
  60.9 0.1 collective-permute-start.12
  60.9 1.7 %collective-permute-start.11 = (s16[672,128]{1,0:T(8,128)(2,1)S(1)}, s16[672,128]{1,0:T(8,128)(2,1)S(1)}, u32[]{:S(2)}, u32[]{:S(2)}) collective-permute-start(s16[672,128]{1,0:T(8,128)(2,1)S(1)} %get-tuple-element.86), channel_id=1, source_target_pairs={{0,2},{1,3},{2,0},{3,1},{4,6},{5,7},{6,4},{7,5},{8,10},{9,11},{10,... | collective-permute-start | bytes 516104 | tf_op jit(solution)/shard_map/ppermute | solution.py:1197
  62.6 0.6 spread_rest.3
  63.2 0.3 collective-permute-start.10
  63.4 4.0 %collective-permute-done.12.part_ref.refs_3_ = s16[672,128]{1,0:T(8,128)(2,1)S(1)} collective-permute-done((s16[672,128]{1,0:T(8,128)(2,1)S(1)}, s16[672,128]{1,0:T(8,128)(2,1)S(1)}, u32[]{:S(2)}, u32[]{:S(2)}) %collective-permute-start.12) | collective-permute-done | bytes 172064 | tf_op jit(solution)/shard_map/ppermute | solution.py:1197
  67.4 3.9 %collective-permute-done.11.refs_1_.refs_2_ = s16[672,128]{1,0:T(8,128)(2,1)S(1)} collective-permute-done((s16[672,128]{1,0:T(8,128)(2,1)S(1)}, s16[672,128]{1,0:T(8,128)(2,1)S(1)}, u32[]{:S(2)}, u32[]{:S(2)}) %collective-permute-start.11) | collective-permute-done | bytes 172064 | tf_op jit(solution)/shard_map/ppermute | solution.py:1197
  71.3 0.7 forward_early.3
  72.0 0.0 copy-start.8
  72.0 2.1 %forward.3 = (f32[18,256,128]{2,1,0:T(8,128)S(1)}, s16[432,128]{1,0:T(8,128)(2,1)S(1)}, s16[304,128]{1,0:T(8,128)(2,1)S(1)}, s16[592,128]{1,0:T(8,128)(2,1)S(1)}...) custom-call(s16[672,128]{1,0:T(8,128)(2,1)S(1)} %get-tuple-element.84.refs_0_, ...), custom_call_target="tpu_custom_call" | custom-call | flops 301989888 | bytes 4718592 | tf_op jit(solution)/shard_map/forward/pallas_call | solution.py:701
  74.1 0.1 collective-permute-start.15
  74.2 0.7 collective-permute-start.14
  74.9 4.7 %collective-permute-start.13 = (s16[304,128]{1,0:T(8,128)(2,1)S(1)}, s16[304,128]{1,0:T(8,128)(2,1)S(1)}, u32[]{:S(2)}, u32[]{:S(2)}) collective-permute-start(s16[304,128]{1,0:T(8,128)(2,1)S(1)} %get-tuple-element.91), channel_id=1, source_target_pairs={{0,4},{8,12},{4,0},{12,8},{1,5},{9,13},{5,1},{13,9},{2,6},{10,14},... | collective-permute-start | bytes 233480 | tf_op jit(solution)/shard_map/ppermute | solution.py:1224
  79.6 0.2 pair_messages.3
  79.8 0.6 collective-permute-start.16
  80.4 1.6 %collective-permute-done.13.layers_ref = s16[304,128]{1,0:T(8,128)(2,1)S(1)} collective-permute-done((s16[304,128]{1,0:T(8,128)(2,1)S(1)}, s16[304,128]{1,0:T(8,128)(2,1)S(1)}, u32[]{:S(2)}, u32[]{:S(2)}) %collective-permute-start.13) | collective-permute-done | bytes 77856 | tf_op jit(solution)/shard_map/ppermute | solution.py:1224
  82.0 0.4 borders.3.refs_1_
  82.4 3.5 %collective-permute-done.16.refs_6_ = s16[272,128]{1,0:T(8,128)(2,1)S(1)} collective-permute-done((s16[272,128]{1,0:T(8,128)(2,1)S(1)}, s16[272,128]{1,0:T(8,128)(2,1)S(1)}, u32[]{:S(2)}, u32[]{:S(2)}) %collective-permute-start.16) | collective-permute-done | bytes 69664 | tf_op jit(solution)/shard_map/ppermute | solution.py:1226
  86.0 2.9 %inverse.3 = (s16[672,128]{1,0:T(8,128)(2,1)S(1)}, s16[672,128]{1,0:T(8,128)(2,1)S(1)}, bf16[18,256,128]{2,1,0:T(8,128)(2,1)S(1)}, bf16[18,256,128]{2,1,0:T(8,128)(2,1)S(1)}) custom-call(f32[18,256,128]{2,1,0:T(8,128)S(1)} %get-tuple-element.90.refs_0_, f32[4,256,128]{2,1,0:T(8,128)S(1)} %borders.3.refs_1_, ...), custom_call_target="tpu_custom_call" | custom-call | flops 301989888 | bytes 4718592 | tf_op jit(solution)/shard_map/inverse/pallas_call | solution.py:933
  88.9 0.1 collective-permute-start.19
  89.0 0.9 inverse_rest.3
  89.9 0.1 collective-permute-start.17
  89.9 2.1 %collective-permute-start.18 = (s16[672,128]{1,0:T(8,128)(2,1)S(1)}, s16[672,128]{1,0:T(8,128)(2,1)S(1)}, u32[]{:S(2)}, u32[]{:S(2)}) collective-permute-start(s16[672,128]{1,0:T(8,128)(2,1)S(1)} %get-tuple-element.99), channel_id=1, source_target_pairs={{0,3},{1,2},{2,1},{3,0},{4,7},{5,6},{6,5},{7,4},{8,11},{9,10},{10,... | collective-permute-start | bytes 516104 | tf_op jit(solution)/shard_map/ppermute | solution.py:1197
  92.1 1.1 %near_field.3.refs_8_ = f32[8,128]{1,0:T(8,128)S(1)} custom-call(s32[24]{0:T(128)S(1)} %get-tuple-element.104.place_ref, s32[24]{0:T(128)S(1)} %get-tuple-element.103.target_ref, s16[432,128]{1,0:T(8,128)(2,1)S(1)} %collective-permute-done.15.even_ref.refs_2_.refs_0_, s16[592,128]{1,0:T(8,128)(2,1)S(1)} %collective-permute-done.14.odd_ref.refs_3_.refs_1_, ...), custom_call_target="tpu_custom_call" | custom-call | flops 12582912 | bytes 786432 | tf_op jit(solution)/shard_map/near_field/pallas_call | solution.py:1132
  93.1 2.8 %collective-permute-done.19.refs_1_ = s16[672,128]{1,0:T(8,128)(2,1)S(1)} collective-permute-done((s16[672,128]{1,0:T(8,128)(2,1)S(1)}, s16[672,128]{1,0:T(8,128)(2,1)S(1)}, u32[]{:S(2)}, u32[]{:S(2)}) %collective-permute-start.19) | collective-permute-done | bytes 172064 | tf_op jit(solution)/shard_map/ppermute | solution.py:1197
  95.9 0.4 sample_early.3.refs_2_
  96.4 0.6 collective-permute-done.18.part_ref
  97.0 3.6 %sample.3 = f32[2,512]{1,0:T(2,128)} custom-call(s32[2,512]{1,0:T(2,128)S(1)} %get-tuple-element.54.place_ref.refs_1_, s16[672,128]{1,0:T(8,128)(2,1)S(1)} %collective-permute-done.17.refs_0_, f32[656,128]{1,0:T(8,128)S(1)} %open_piece.7.refs_1_, f32[656,256]{1,0:T(8,128)S(1)} %sample_early.3.refs_2_, bf16[4,128,256]{2,1,0:T(8,128)(2,1)S(1)} %copy-done.9, ...), custom_call_target="tpu_custom_call" | custom-call | flops 169869312 | bytes 4194304 | tf_op jit(solution)/shard_map/sample/pallas_call | solution.py:1076
  (49 shorter events, 0.3 us)
Async XLA Ops:
  5.7 7.2 %copy-start.4 = (bf16[4,256,128]{2,1,0:T(8,128)(2,1)}, bf16[4,256,128]{2,1,0:T(8,128)(2,1)S(1)}, u32[]{:S(2)}) copy-start(bf16[4,256,128]{2,1,0:T(8,128)(2,1)S(1)} %get-tuple-element.59.low_ref.refs_4_) | copy-start | bytes 786436
  5.7 7.2 %copy-start.15 = (f32[256,128]{1,0:T(8,128)}, f32[256,128]{1,0:T(8,128)S(1)}, u32[]{:S(2)}) copy-start(f32[256,128]{1,0:T(8,128)S(1)} %get-tuple-element.81.coeff_ref) | copy-start | bytes 393220
  5.7 7.2 %collective-permute-start.2 = (s16[672,128]{1,0:T(8,128)(2,1)S(1)}, s16[672,128]{1,0:T(8,128)(2,1)S(1)}, u32[]{:S(2)}, u32[]{:S(2)}) collective-permute-start(s16[672,128]{1,0:T(8,128)(2,1)S(1)} %get-tuple-element.63), channel_id=1, source_target_pairs={{0,3},{1,2},{2,1},{3,0},{4,7},{5,6},{6,5},{7,4},{8,11},{9,10},{10,... | collective-permute-start | bytes 516104 | tf_op jit(solution)/shard_map/ppermute | solution.py:1197
  8.2 8.6 %collective-permute-start.1 = (s16[672,128]{1,0:T(8,128)(2,1)S(1)}, s16[672,128]{1,0:T(8,128)(2,1)S(1)}, u32[]{:S(2)}, u32[]{:S(2)}) collective-permute-start(s16[672,128]{1,0:T(8,128)(2,1)S(1)} %get-tuple-element.62), channel_id=1, source_target_pairs={{0,2},{1,3},{2,0},{3,1},{4,6},{5,7},{6,4},{7,5},{8,10},{9,11},{10,... | collective-permute-start | bytes 516104 | tf_op jit(solution)/shard_map/ppermute | solution.py:1197
  9.4 8.1 %collective-permute-start = (s16[672,128]{1,0:T(8,128)(2,1)S(1)}, s16[672,128]{1,0:T(8,128)(2,1)S(1)}, u32[]{:S(2)}, u32[]{:S(2)}) collective-permute-start(s16[672,128]{1,0:T(8,128)(2,1)S(1)} %get-tuple-element.61), channel_id=1, source_target_pairs={{0,1},{1,0},{2,3},{3,2},{4,5},{5,4},{6,7},{7,6},{8,9},{9,8},{10,11... | collective-permute-start | bytes 516104 | tf_op jit(solution)/shard_map/ppermute | solution.py:1197
  12.9 4.6 %copy-start = (f32[8192,128]{1,0:T(8,128)}, f32[8192,128]{1,0:T(8,128)S(1)}, u32[]{:S(2)}) copy-start(f32[8192,128]{1,0:T(8,128)S(1)} %place_sample_lines.1.refs_9_.refs_5_) | copy-start | bytes 12582916
  12.9 3.9 %copy-start.2 = (bf16[2,256,240]{2,1,0:T(8,128)(2,1)S(1)}, bf16[2,256,240]{2,1,0:T(8,128)(2,1)}, u32[]{:S(2)}) copy-start(bf16[2,256,240]{2,1,0:T(8,128)(2,1)} %constant.72.clone.refs_2_.refs_7_.table_ref) | copy-start | bytes 737284
  17.5 17.4 %copy-start.6 = (bf16[4,48,256]{2,1,0:T(8,128)(2,1)S(1)}, bf16[4,48,256]{2,1,0:T(8,128)(2,1)}, u32[]{:S(2)}) copy-start(bf16[4,48,256]{2,1,0:T(8,128)(2,1)} %constant.73.clone.refs_7_.high_ref) | copy-start | bytes 294916
  20.2 8.3 %copy-start.13 = (f32[256,128]{1,0:T(8,128)}, f32[256,128]{1,0:T(8,128)S(1)}, u32[]{:S(2)}) copy-start(f32[256,128]{1,0:T(8,128)S(1)} %get-tuple-element.72.own_ref.refs_4_) | copy-start | bytes 393220
  20.2 9.9 %copy-start.17 = (f32[256,128]{1,0:T(8,128)}, f32[256,128]{1,0:T(8,128)S(1)}, u32[]{:S(2)}) copy-start(f32[256,128]{1,0:T(8,128)S(1)} %get-tuple-element.73.refs_5_) | copy-start | bytes 393220
  20.2 7.5 %collective-permute-start.5 = (s16[432,128]{1,0:T(8,128)(2,1)S(1)}, s16[432,128]{1,0:T(8,128)(2,1)S(1)}, u32[]{:S(2)}, u32[]{:S(2)}) collective-permute-start(s16[432,128]{1,0:T(8,128)(2,1)S(1)} %get-tuple-element.71), channel_id=1, source_target_pairs={{0,4},{8,12},{4,0},{12,8},{1,5},{9,13},{5,1},{13,9},{2,6},{10,14},... | collective-permute-start | bytes 331784 | tf_op jit(solution)/shard_map/ppermute | solution.py:1222
  22.5 7.8 %collective-permute-start.4 = (s16[592,128]{1,0:T(8,128)(2,1)}, s16[592,128]{1,0:T(8,128)(2,1)}, u32[]{:S(2)}, u32[]{:S(2)}) collective-permute-start(s16[592,128]{1,0:T(8,128)(2,1)} %get-tuple-element.70), channel_id=1, source_target_pairs={{4,8},{8,4},{5,9},{9,5},{6,10},{10,6},{7,11},{11,7},{20,24},{24,20... | collective-permute-start | bytes 454664 | tf_op jit(solution)/shard_map/ppermute | solution.py:1223
  23.9 6.5 %collective-permute-start.3 = (s16[304,128]{1,0:T(8,128)(2,1)}, s16[304,128]{1,0:T(8,128)(2,1)}, u32[]{:S(2)}, u32[]{:S(2)}) collective-permute-start(s16[304,128]{1,0:T(8,128)(2,1)} %get-tuple-element.69), channel_id=1, source_target_pairs={{0,4},{8,12},{4,0},{12,8},{1,5},{9,13},{5,1},{13,9},{2,6},{10,14},... | collective-permute-start | bytes 233480 | tf_op jit(solution)/shard_map/ppermute | solution.py:1224
  28.5 0.7 copy-start.11
  29.1 5.8 %collective-permute-start.6 = (s16[272,128]{1,0:T(8,128)(2,1)}, s16[272,128]{1,0:T(8,128)(2,1)}, u32[]{:S(2)}, u32[]{:S(2)}) collective-permute-start(s16[272,128]{1,0:T(8,128)(2,1)} %pair_messages.2), channel_id=1, source_target_pairs={{0,8},{4,12},{8,0},{12,4},{1,9},{5,13},{9,1},{13,5},{2,10},{6,14},... | collective-permute-start | bytes 208904 | tf_op jit(solution)/shard_map/ppermute | solution.py:1226
  30.1 12.5 %copy-start.20 = (s32[24]{0:T(128)S(1)}, s32[24]{0:T(128)}, u32[]{:S(2)}) copy-start(s32[24]{0:T(128)} %param.21) | copy-start | bytes 292
  30.1 12.5 %copy-start.21 = (s32[24]{0:T(128)S(1)}, s32[24]{0:T(128)}, u32[]{:S(2)}) copy-start(s32[24]{0:T(128)} %param.22) | copy-start | bytes 292
  34.9 0.9 copy-start.7
  35.8 0.9 copy-start.12
  36.7 0.9 copy-start.14
  37.6 0.9 copy-start.18
  38.5 7.0 %copy-start.3 = (bf16[24,128,128]{2,1,0:T(8,128)(2,1)S(1)}, bf16[24,128,128]{2,1,0:T(8,128)(2,1)}, u32[]{:S(2)}) copy-start(bf16[24,128,128]{2,1,0:T(8,128)(2,1)} %refs_3_.8) | copy-start | bytes 2359300
  42.4 4.2 %copy-start.16 = (f32[256,128]{1,0:T(8,128)S(1)}, f32[256,128]{1,0:T(8,128)}, u32[]{:S(2)}) copy-start(f32[256,128]{1,0:T(8,128)} %copy-done.15) | copy-start | bytes 393220
  42.5 7.2 %collective-permute-start.8 = (s16[672,128]{1,0:T(8,128)(2,1)S(1)}, s16[672,128]{1,0:T(8,128)(2,1)S(1)}, u32[]{:S(2)}, u32[]{:S(2)}) collective-permute-start(s16[672,128]{1,0:T(8,128)(2,1)S(1)} %get-tuple-element.77), channel_id=1, source_target_pairs={{0,3},{1,2},{2,1},{3,0},{4,7},{5,6},{6,5},{7,4},{8,11},{9,10},{10,... | collective-permute-start | bytes 516104 | tf_op jit(solution)/shard_map/ppermute | solution.py:1197
  42.6 10.3 %collective-permute-start.9 = (s16[672,128]{1,0:T(8,128)(2,1)S(1)}, s16[672,128]{1,0:T(8,128)(2,1)S(1)}, u32[]{:S(2)}, u32[]{:S(2)}) collective-permute-start(s16[672,128]{1,0:T(8,128)(2,1)S(1)} %get-tuple-element.79), channel_id=1, source_target_pairs={{0,2},{1,3},{2,0},{3,1},{4,6},{5,7},{6,4},{7,5},{8,10},{9,11},{10,... | collective-permute-start | bytes 516104 | tf_op jit(solution)/shard_map/ppermute | solution.py:1197
  45.1 8.3 %collective-permute-start.7 = (s16[672,128]{1,0:T(8,128)(2,1)S(1)}, s16[672,128]{1,0:T(8,128)(2,1)S(1)}, u32[]{:S(2)}, u32[]{:S(2)}) collective-permute-start(s16[672,128]{1,0:T(8,128)(2,1)S(1)} %get-tuple-element.76), channel_id=1, source_target_pairs={{0,1},{1,0},{2,3},{3,2},{4,5},{5,4},{6,7},{7,6},{8,9},{9,8},{10,11... | collective-permute-start | bytes 516104 | tf_op jit(solution)/shard_map/ppermute | solution.py:1197
  49.6 3.3 %copy-start.9 = (bf16[4,128,256]{2,1,0:T(8,128)(2,1)S(1)}, bf16[4,128,256]{2,1,0:T(8,128)(2,1)}, u32[]{:S(2)}) copy-start(bf16[4,128,256]{2,1,0:T(8,128)(2,1)} %constant.75.clone.refs_2_.refs_3_) | copy-start | bytes 786436
  49.6 3.2 %copy-start.10 = (bf16[4,128,256]{2,1,0:T(8,128)(2,1)S(1)}, bf16[4,128,256]{2,1,0:T(8,128)(2,1)}, u32[]{:S(2)}) copy-start(bf16[4,128,256]{2,1,0:T(8,128)(2,1)} %constant.76.clone.refs_3_.refs_4_) | copy-start | bytes 786436
  49.7 3.7 %copy-start.19 = (s32[512]{0:T(512)S(1)}, s32[512]{0:T(512)}, u32[]{:S(2)}) copy-start(s32[512]{0:T(512)} %param.17) | copy-start | bytes 6148
  52.9 2.2 %copy-start.1 = (f32[8192,128]{1,0:T(8,128)S(1)}, f32[8192,128]{1,0:T(8,128)}, u32[]{:S(2)}) copy-start(f32[8192,128]{1,0:T(8,128)} %copy-done) | copy-start | bytes 12582916
  55.1 2.9 %copy-start.5 = (bf16[4,256,128]{2,1,0:T(8,128)(2,1)S(1)}, bf16[4,256,128]{2,1,0:T(8,128)(2,1)}, u32[]{:S(2)}) copy-start(bf16[4,256,128]{2,1,0:T(8,128)(2,1)} %copy-done.4) | copy-start | bytes 786436
  60.9 6.5 %collective-permute-start.12 = (s16[672,128]{1,0:T(8,128)(2,1)S(1)}, s16[672,128]{1,0:T(8,128)(2,1)S(1)}, u32[]{:S(2)}, u32[]{:S(2)}) collective-permute-start(s16[672,128]{1,0:T(8,128)(2,1)S(1)} %get-tuple-element.87), channel_id=1, source_target_pairs={{0,3},{1,2},{2,1},{3,0},{4,7},{5,6},{6,5},{7,4},{8,11},{9,10},{10,... | collective-permute-start | bytes 516104 | tf_op jit(solution)/shard_map/ppermute | solution.py:1197
  60.9 10.3 %collective-permute-start.11 = (s16[672,128]{1,0:T(8,128)(2,1)S(1)}, s16[672,128]{1,0:T(8,128)(2,1)S(1)}, u32[]{:S(2)}, u32[]{:S(2)}) collective-permute-start(s16[672,128]{1,0:T(8,128)(2,1)S(1)} %get-tuple-element.86), channel_id=1, source_target_pairs={{0,2},{1,3},{2,0},{3,1},{4,6},{5,7},{6,4},{7,5},{8,10},{9,11},{10,... | collective-permute-start | bytes 516104 | tf_op jit(solution)/shard_map/ppermute | solution.py:1197
  63.2 8.8 %collective-permute-start.10 = (s16[672,128]{1,0:T(8,128)(2,1)S(1)}, s16[672,128]{1,0:T(8,128)(2,1)S(1)}, u32[]{:S(2)}, u32[]{:S(2)}) collective-permute-start(s16[672,128]{1,0:T(8,128)(2,1)S(1)} %get-tuple-element.85), channel_id=1, source_target_pairs={{0,1},{1,0},{2,3},{3,2},{4,5},{5,4},{6,7},{7,6},{8,9},{9,8},{10,11... | collective-permute-start | bytes 516104 | tf_op jit(solution)/shard_map/ppermute | solution.py:1197
  72.0 14.0 %copy-start.8 = (bf16[4,48,256]{2,1,0:T(8,128)(2,1)S(1)}, bf16[4,48,256]{2,1,0:T(8,128)(2,1)}, u32[]{:S(2)}) copy-start(bf16[4,48,256]{2,1,0:T(8,128)(2,1)} %constant.74.clone.refs_8_.low_ref) | copy-start | bytes 294916
  74.1 5.5 %collective-permute-start.15 = (s16[432,128]{1,0:T(8,128)(2,1)S(1)}, s16[432,128]{1,0:T(8,128)(2,1)S(1)}, u32[]{:S(2)}, u32[]{:S(2)}) collective-permute-start(s16[432,128]{1,0:T(8,128)(2,1)S(1)} %get-tuple-element.93), channel_id=1, source_target_pairs={{0,4},{8,12},{4,0},{12,8},{1,5},{9,13},{5,1},{13,9},{2,6},{10,14},... | collective-permute-start | bytes 331784 | tf_op jit(solution)/shard_map/ppermute | solution.py:1222
  74.2 7.8 %collective-permute-start.14 = (s16[592,128]{1,0:T(8,128)(2,1)S(1)}, s16[592,128]{1,0:T(8,128)(2,1)S(1)}, u32[]{:S(2)}, u32[]{:S(2)}) collective-permute-start(s16[592,128]{1,0:T(8,128)(2,1)S(1)} %get-tuple-element.92), channel_id=1, source_target_pairs={{4,8},{8,4},{5,9},{9,5},{6,10},{10,6},{7,11},{11,7},{20,24},{24,20... | collective-permute-start | bytes 454664 | tf_op jit(solution)/shard_map/ppermute | solution.py:1223
  74.9 7.1 %collective-permute-start.13 = (s16[304,128]{1,0:T(8,128)(2,1)S(1)}, s16[304,128]{1,0:T(8,128)(2,1)S(1)}, u32[]{:S(2)}, u32[]{:S(2)}) collective-permute-start(s16[304,128]{1,0:T(8,128)(2,1)S(1)} %get-tuple-element.91), channel_id=1, source_target_pairs={{0,4},{8,12},{4,0},{12,8},{1,5},{9,13},{5,1},{13,9},{2,6},{10,14},... | collective-permute-start | bytes 233480 | tf_op jit(solution)/shard_map/ppermute | solution.py:1224
  79.8 6.2 %collective-permute-start.16 = (s16[272,128]{1,0:T(8,128)(2,1)S(1)}, s16[272,128]{1,0:T(8,128)(2,1)S(1)}, u32[]{:S(2)}, u32[]{:S(2)}) collective-permute-start(s16[272,128]{1,0:T(8,128)(2,1)S(1)} %pair_messages.3), channel_id=1, source_target_pairs={{0,8},{4,12},{8,0},{12,4},{1,9},{5,13},{9,1},{13,5},{2,10},{6,14},... | collective-permute-start | bytes 208904 | tf_op jit(solution)/shard_map/ppermute | solution.py:1226
  88.9 7.0 %collective-permute-start.19 = (s16[672,128]{1,0:T(8,128)(2,1)S(1)}, s16[672,128]{1,0:T(8,128)(2,1)S(1)}, u32[]{:S(2)}, u32[]{:S(2)}) collective-permute-start(s16[672,128]{1,0:T(8,128)(2,1)S(1)} %get-tuple-element.101), channel_id=1, source_target_pairs={{0,2},{1,3},{2,0},{3,1},{4,6},{5,7},{6,4},{7,5},{8,10},{9,11},{10,... | collective-permute-start | bytes 516104 | tf_op jit(solution)/shard_map/ppermute | solution.py:1197
  89.9 7.1 %collective-permute-start.17 = (s16[672,128]{1,0:T(8,128)(2,1)S(1)}, s16[672,128]{1,0:T(8,128)(2,1)S(1)}, u32[]{:S(2)}, u32[]{:S(2)}) collective-permute-start(s16[672,128]{1,0:T(8,128)(2,1)S(1)} %get-tuple-element.98), channel_id=1, source_target_pairs={{0,1},{1,0},{2,3},{3,2},{4,5},{5,4},{6,7},{7,6},{8,9},{9,8},{10,11... | collective-permute-start | bytes 516104 | tf_op jit(solution)/shard_map/ppermute | solution.py:1197
  89.9 7.0 %collective-permute-start.18 = (s16[672,128]{1,0:T(8,128)(2,1)S(1)}, s16[672,128]{1,0:T(8,128)(2,1)S(1)}, u32[]{:S(2)}, u32[]{:S(2)}) collective-permute-start(s16[672,128]{1,0:T(8,128)(2,1)S(1)} %get-tuple-element.99), channel_id=1, source_target_pairs={{0,3},{1,2},{2,1},{3,0},{4,7},{5,6},{6,5},{7,4},{8,11},{9,10},{10,... | collective-permute-start | bytes 516104 | tf_op jit(solution)/shard_map/ppermute | solution.py:1197

commit v14 on v12

--- a/solution.py
+++ b/solution.py
@@ -332,16 +332,24 @@
 
 
 def spread_kernel(reach_x, reach_y, flips, *refs):
-    vector_ref, place_ref, rounded_ref, high_ref, low_ref, line_ref = refs[:6]
+    vector_in, place_in, rounded_ref, high_ref, low_ref, line_ref = refs[:6]
     refs = refs[6:]
-    outs, wides, (head, total), grids = (
+    outs, wides, (vector_ref, place_ref, sems, head, total), grids = (
         refs[: len(flips)],
         refs[len(flips) : len(flips) + 2],
-        refs[len(flips) + 2 : len(flips) + 4],
-        refs[len(flips) + 4 :],
+        refs[len(flips) + 2 : len(flips) + 7],
+        refs[len(flips) + 7 :],
     )
+    copies = [
+        pltpu.make_async_copy(vector_in, vector_ref, sems.at[0]),
+        pltpu.make_async_copy(place_in, place_ref, sems.at[1]),
+    ]
+    for copy in copies:
+        copy.start()
     for grid in grids:
         grid[...] = jnp.zeros_like(grid)
+    for copy in copies:
+        copy.wait()
     add_panels(reach_y, False, vector_ref, place_ref, line_ref, grids)
     spread_grid(
         reach_x,
@@ -393,7 +401,12 @@
         ] + work
     else:
         operands = [vector, placed[0], rounded, *table, placed[1]]
-        in_specs = [in_smem()] * 2 + [whole_vmem()] * 4
+        in_specs = [anywhere()] * 2 + [whole_vmem()] * 4
+        work = [
+            pltpu.SMEM((count,), F32),
+            pltpu.SMEM((2, count), jnp.int32),
+            pltpu.SemaphoreType.DMA((2,)),
+        ] + work
     return pl.pallas_call(
         functools.partial(
             start_kernel if placed is None else spread_kernel, reach_x, reach_y, flips
@@ -599,7 +612,7 @@
         transform_pieces(table_ref[lax.axis_index("pair") ^ core], stacked, before, spectrum)
         before = spectrum
 
-    chunk = 32
+    chunk = 64
 
     def body(index, largest):
         rows = pl.ds(pl.multiple_of(index * chunk, chunk), chunk)
@@ -824,7 +837,7 @@
     field_high, field_low, ready, head = refs[3 + len(flips) :]
     half = reach_x // 2
     span = reach_x - 4
-    chunk = 32
+    chunk = 64
     head_rows = from_even.shape[0] - GRID - GRID // 2
     on_left = (lax.axis_index("wide") & 1) == 1
     moment_units = []
@@ -990,12 +1003,14 @@
     )(*parts, *table)
 
 
-def sample_kernel(last, reach_x, reach_y, flips, place_ref, *refs):
+def sample_kernel(last, reach_x, reach_y, flips, place_in, *refs):
     parts = refs[: len(flips)]
     early_ref, high_ref, low_ref, line_ref, own_ref, vector_ref, near_ref, out_ref = refs[
         len(flips) : len(flips) + 8
     ]
-    flat, field, sums = refs[len(flips) + 8 :]
+    flat, field, sums, place_ref, sem = refs[len(flips) + 8 :]
+    copy = pltpu.make_async_copy(place_in, place_ref, sem)
+    copy.start()
     half_rows = reach_x * reach_y // 2
     both = early_ref[...] + z_lines(parts, flips, high_ref, low_ref)
     flat[:half_rows, :] = both[:half_rows, :REGION]
@@ -1020,14 +1035,17 @@
             sums[pl.ds(pl.multiple_of(group * GROUP + eight, 8), 8), :] = sum_rows(totals)
         return carry
 
+    copy.wait()
     lax.fori_loop(0, count // GROUP, body, 0)
-    sampled = lax.dot_general(
-        jnp.ones((8, REGION), F32),
-        sums[...],
+    first, rest = split(sums[...])
+    second, third = split(sums[...] - first.astype(F32))
+    across = lambda values: lax.dot_general(
+        jnp.ones((16, REGION), BF16),
+        values,
         (((1,), (1,)), ((), ())),
-        precision=lax.Precision.HIGHEST,
         preferred_element_type=F32,
     )
+    sampled = across(first) + (across(second) + across(third))
     for block in range(count // BLOCK):
         lane = slice(block * BLOCK, (block + 1) * BLOCK)
         row = slice(block, block + 1)
@@ -1047,13 +1065,15 @@
     shape = (2, count) if last else (blocks, BLOCK)
     return pl.pallas_call(
         functools.partial(sample_kernel, last, reach_x, reach_y, flips),
-        in_specs=[in_smem()] + [whole_vmem()] * (len(parts) + 7),
+        in_specs=[anywhere()] + [whole_vmem()] * (len(parts) + 7),
         out_specs=whole_vmem(),
         out_shape=jax.ShapeDtypeStruct(shape, F32),
         scratch_shapes=[
             pltpu.VMEM((reach_x * reach_y, REGION), F32),
             pltpu.VMEM((pair_count(reach_x, reach_y), REGION), F32),
             pltpu.VMEM((count, REGION), F32),
+            pltpu.SMEM((2, count), jnp.int32),
+            pltpu.SemaphoreType.DMA,
         ],
         compiler_params=params(),
         cost_estimate=cost(reach_x * reach_y * 256 * 512, 4 * 16 * count * REGION),

time: 90.2 us -> 86.7 us (0.961)
  Pallas kernels: 39.5 us -> 36 us
    pallas_call x2, Pallas kernels: 6.49 us -> 4.87 us  [sample(): pl.pallas_call(functools.partial(sample_kernel, last, reach_x, reach_y, f...]
    pallas_call x2, Pallas kernels: 5.84 us -> 4.63 us  [inverse(): pl.pallas_call(functools.partial(inverse_kernel, reach_x, reach_y, flips,...]
  transfers between devices with their start and end apart: 20 -> 20, of which waited for: 10 -> 10; matrix products, arithmetic and copies ran while one was open for 1% -> 1% of each run, Pallas kernels for 16% -> 17%
where the time goes in v14:
time: 86.7 us; the launch traced here: 86.4 us
  Pallas kernels  36 us (42%)
  starting transfers between devices  25.2 us (29%)
  waiting for transfers between devices  22.6 us (26%)
  local copies, waits for them, and re-layouts  2.02 us (2%)
    ppermute x12, waiting for transfers between devices, turned(): lax.ppermute(part, Y_AXES, swap_pairs)  13.1 us
    ppermute x12, starting transfers between devices, turned(): lax.ppermute(part, Y_AXES, swap_pairs)  10.1 us
    ppermute x2, starting transfers between devices, convolve_and_sample(): even_layers = lax.ppermute(layers, 'wide', even_swap)  9.31 us
    pallas_call x2, Pallas kernels, spread(): pl.pallas_call(functools.partial(start_kernel if placed is None else spre...  8.35 us
    ppermute x2, waiting for transfers between devices, convolve_and_sample(): lax.ppermute(message, 'wide', [(i, i ^ flip) for i in range(x_count)])  7.5 us
    pallas_call x2, Pallas kernels, sample(): pl.pallas_call(functools.partial(sample_kernel, last, reach_x, reach_y, f...  4.87 us
    pallas_call x2, Pallas kernels, inverse(): pl.pallas_call(functools.partial(inverse_kernel, reach_x, reach_y, flips,...  4.63 us
    pallas_call x1, Pallas kernels, place_sample_lines(): pl.pallas_call(functools.partial(sample_lines_kernel, blocks), grid=(1,),...  3.41 us
  transfers between devices with their start and end apart: 20, of which 10 were waited for; matrix products, arithmetic and copies ran while one was open for 1% of the time, Pallas kernels for 17%

profile of v14, /device:TPU:0, one launch (start us, length us, event | category | flops | bytes accessed | tf_op | source)
XLA Modules:
  0.0 86.4 jit_solution(5586045948638903237)
XLA Ops:
  0.0 5.7 %start.1 = (s16[672,128]{1,0:T(8,128)(2,1)S(1)}, s16[672,128]{1,0:T(8,128)(2,1)S(1)}, bf16[656,256]{1,0:T(8,128)(2,1)S(1)}, bf16[656,256]{1,0:T(8,128)(2,1)S(1)}...) custom-call(f32[512]{0:T(512)} %refs_0_.2, ...), custom_call_target="tpu_custom_call" | custom-call | flops 169869312 | bytes 4194304 | tf_op jit(solution)/shard_map/start/pallas_call | solution.py:410
  5.7 3.0 %collective-permute-start.1 = (s16[672,128]{1,0:T(8,128)(2,1)S(1)}, s16[672,128]{1,0:T(8,128)(2,1)S(1)}, u32[]{:S(2)}, u32[]{:S(2)}) collective-permute-start(s16[672,128]{1,0:T(8,128)(2,1)S(1)} %get-tuple-element.60), channel_id=1, source_target_pairs={{0,2},{1,3},{2,0},{3,1},{4,6},{5,7},{6,4},{7,5},{8,10},{9,11},{10,... | collective-permute-start | bytes 516104 | tf_op jit(solution)/shard_map/ppermute | solution.py:1190
  8.7 0.6 spread_rest.2
  9.3 0.1 collective-permute-start
  9.4 0.1 collective-permute-start.2
  9.5 0.9 %copy-done.1 = f32[64,512]{1,0:T(8,128)S(1)} copy-done((f32[64,512]{1,0:T(8,128)S(1)}, f32[64,512]{1,0:T(8,128)}, u32[]{:S(2)}) %copy-start.1) | copy-done | bytes 131096
  10.4 3.4 %place_sample_lines.1.refs_8_.refs_5_ = f32[8192,128]{1,0:T(8,128)S(1)} custom-call(s32[2,512]{1,0:T(2,128)S(1)} %get-tuple-element.52.place_ref.place_in.refs_1_, f32[64,512]{1,0:T(8,128)S(1)} %copy-done.1, f32[64,512]{1,0:T(8,128)S(1)} %copy-done.1, f32[64,512]{1,0:T(8,128)S(1)} %copy-done.1, f32[64,512]{1,0:T(8,128)S(1)} %copy-done.1), custom_call_target="tpu_custom_call" | custom-call | flops 1048576 | bytes 4194304 | tf_op jit(solution)/shard_map/place_sample_lines/pallas_call | solution.py:479
  13.8 1.1 %dynamic-slice_bitcast_fusion.refs_7_.modes_ref.refs_9_ = f32[4,256,128]{2,1,0:T(8,128)S(1)} fusion(f32[4,4,256,128]{3,2,1,0:T(8,128)} %constant.73.clone, s32[]{:T(128)S(6)} %select_n.30), kind=kLoop, calls=%fused_computation | loop fusion | bytes 1048580 | tf_op jit(solution)/shard_map/jit(dynamic_index_in_dim)/squeeze | solution.py:1167
  14.9 0.0 collective-permute-done.1.refs_1_.refs_2_
  14.9 0.7 forward_early.2
  15.6 0.0 collective-permute-done.refs_1_
  15.6 0.6 collective-permute-done.2.refs_3_
  16.2 1.6 %forward.2 = (f32[18,256,128]{2,1,0:T(8,128)S(1)}, s16[432,128]{1,0:T(8,128)(2,1)S(1)}, s16[304,128]{1,0:T(8,128)(2,1)S(1)}, s16[592,128]{1,0:T(8,128)(2,1)S(1)}...) custom-call(s16[672,128]{1,0:T(8,128)(2,1)S(1)} %get-tuple-element.58.refs_0_, ...), custom_call_target="tpu_custom_call" | custom-call | flops 301989888 | bytes 4718592 | tf_op jit(solution)/shard_map/forward/pallas_call | solution.py:689
  17.8 1.6 %collective-permute-start.5 = (s16[432,128]{1,0:T(8,128)(2,1)S(1)}, s16[432,128]{1,0:T(8,128)(2,1)S(1)}, u32[]{:S(2)}, u32[]{:S(2)}) collective-permute-start(s16[432,128]{1,0:T(8,128)(2,1)S(1)} %get-tuple-element.67), channel_id=1, source_target_pairs={{0,4},{8,12},{4,0},{12,8},{1,5},{9,13},{5,1},{13,9},{2,6},{10,14},... | collective-permute-start | bytes 331784 | tf_op jit(solution)/shard_map/ppermute | solution.py:1202
  19.4 0.7 collective-permute-start.4
  20.1 4.5 %collective-permute-start.3 = (s16[304,128]{1,0:T(8,128)(2,1)S(1)}, s16[304,128]{1,0:T(8,128)(2,1)S(1)}, u32[]{:S(2)}, u32[]{:S(2)}) collective-permute-start(s16[304,128]{1,0:T(8,128)(2,1)S(1)} %get-tuple-element.65), channel_id=1, source_target_pairs={{0,4},{8,12},{4,0},{12,8},{1,5},{9,13},{5,1},{13,9},{2,6},{10,14},... | collective-permute-start | bytes 233480 | tf_op jit(solution)/shard_map/ppermute | solution.py:1204
  24.5 0.0 collective-permute-done.5.even_ref.refs_2_.refs_0_
  24.5 0.2 pair_messages.2
  24.7 0.0 copy-start.8
  24.7 0.0 copy-start.9
  24.7 1.6 %collective-permute-start.6 = (s16[272,128]{1,0:T(8,128)(2,1)S(1)}, s16[272,128]{1,0:T(8,128)(2,1)S(1)}, u32[]{:S(2)}, u32[]{:S(2)}) collective-permute-start(s16[272,128]{1,0:T(8,128)(2,1)S(1)} %pair_messages.2), channel_id=1, source_target_pairs={{0,8},{4,12},{8,0},{12,4},{1,9},{5,13},{9,1},{13,5},{2,10},{6,14},... | collective-permute-start | bytes 208904 | tf_op jit(solution)/shard_map/ppermute | solution.py:1206
  26.3 0.9 %collective-permute-done.3.layers_ref = s16[304,128]{1,0:T(8,128)(2,1)S(1)} collective-permute-done((s16[304,128]{1,0:T(8,128)(2,1)S(1)}, s16[304,128]{1,0:T(8,128)(2,1)S(1)}, u32[]{:S(2)}, u32[]{:S(2)}) %collective-permute-start.3) | collective-permute-done | bytes 77856 | tf_op jit(solution)/shard_map/ppermute | solution.py:1204
  27.2 0.0 collective-permute-done.4.odd_ref.refs_3_.refs_1_
  27.2 0.4 borders.2.refs_1_
  27.7 3.7 %collective-permute-done.6.refs_6_ = s16[272,128]{1,0:T(8,128)(2,1)S(1)} collective-permute-done((s16[272,128]{1,0:T(8,128)(2,1)S(1)}, s16[272,128]{1,0:T(8,128)(2,1)S(1)}, u32[]{:S(2)}, u32[]{:S(2)}) %collective-permute-start.6) | collective-permute-done | bytes 69664 | tf_op jit(solution)/shard_map/ppermute | solution.py:1206
  31.4 2.3 %inverse.2 = (s16[672,128]{1,0:T(8,128)(2,1)S(1)}, s16[672,128]{1,0:T(8,128)(2,1)S(1)}, bf16[18,256,128]{2,1,0:T(8,128)(2,1)S(1)}, bf16[18,256,128]{2,1,0:T(8,128)(2,1)S(1)}) custom-call(f32[18,256,128]{2,1,0:T(8,128)S(1)} %get-tuple-element.64.refs_0_, f32[4,256,128]{2,1,0:T(8,128)S(1)} %borders.2.refs_1_, ...), custom_call_target="tpu_custom_call" | custom-call | flops 301989888 | bytes 4718592 | tf_op jit(solution)/shard_map/inverse/pallas_call | solution.py:921
  33.7 1.6 %collective-permute-start.9 = (s16[672,128]{1,0:T(8,128)(2,1)S(1)}, s16[672,128]{1,0:T(8,128)(2,1)S(1)}, u32[]{:S(2)}, u32[]{:S(2)}) collective-permute-start(s16[672,128]{1,0:T(8,128)(2,1)S(1)} %get-tuple-element.75), channel_id=1, source_target_pairs={{0,2},{1,3},{2,0},{3,1},{4,6},{5,7},{6,4},{7,5},{8,10},{9,11},{10,... | collective-permute-start | bytes 516104 | tf_op jit(solution)/shard_map/ppermute | solution.py:1190
  35.3 0.9 %inverse_rest.2 = (s16[672,128]{1,0:T(8,128)(2,1)S(1)}, s16[672,128]{1,0:T(8,128)(2,1)S(1)}) custom-call(bf16[18,256,128]{2,1,0:T(8,128)(2,1)S(1)} %get-tuple-element.70.field_high, bf16[18,256,128]{2,1,0:T(8,128)(2,1)S(1)} %get-tuple-element.71.field_low, bf16[4,48,256]{2,1,0:T(8,128)(2,1)S(1)} %copy-done.3, bf16[4,48,256]{2,1,0:T(8,128)(2,1)S(1)} %copy-done.4), custom_call_target="tpu_custom_call" | custom-call | flops 301989888 | bytes 4718592 | tf_op jit(solution)/shard_map/inverse_rest/pallas_call | solution.py:945
  36.2 0.1 collective-permute-start.7
  36.3 0.7 collective-permute-start.8
  36.9 1.0 %near_field.2.refs_8_.refs_0_ = f32[8,128]{1,0:T(8,128)S(1)} custom-call(s32[24]{0:T(128)S(1)} %get-tuple-element.100.place_ref, s32[24]{0:T(128)S(1)} %get-tuple-element.99.target_ref, s16[432,128]{1,0:T(8,128)(2,1)S(1)} %collective-permute-done.5.even_ref.refs_2_.refs_0_, s16[592,128]{1,0:T(8,128)(2,1)S(1)} %collective-permute-done.4.odd_ref.refs_3_.refs_1_, ...), custom_call_target="tpu_custom_call" | custom-call | flops 12582912 | bytes 786432 | tf_op jit(solution)/shard_map/near_field/pallas_call | solution.py:1124
  38.0 0.0 copy-start.6
  38.0 3.0 %place_lines.1.refs_5_ = f32[8192,128]{1,0:T(8,128)S(1)} custom-call(s32[2,512]{1,0:T(2,128)S(1)} %get-tuple-element.52.place_ref.place_in.refs_1_, f32[256,128]{1,0:T(8,128)S(1)} %get-tuple-element.77.coeff_ref, f32[8,128]{1,0:T(8,128)S(1)} %near_field.2.refs_8_.refs_0_), custom_call_target="tpu_custom_call" | custom-call | flops 1048576 | bytes 4194304 | tf_op jit(solution)/shard_map/place_lines/pallas_call | solution.py:495
  41.0 0.4 sample_early.2.refs_2_
  41.4 1.6 %collective-permute-done.8.refs_1_ = s16[672,128]{1,0:T(8,128)(2,1)S(1)} collective-permute-done((s16[672,128]{1,0:T(8,128)(2,1)S(1)}, s16[672,128]{1,0:T(8,128)(2,1)S(1)}, u32[]{:S(2)}, u32[]{:S(2)}) %collective-permute-start.8) | collective-permute-done | bytes 172064 | tf_op jit(solution)/shard_map/ppermute | solution.py:1190
  43.1 2.1 %sample.2.refs_2_.rounded_ref.refs_7_ = f32[4,128]{1,0:T(4,128)S(1)} custom-call(s32[2,512]{1,0:T(2,128)S(1)} %get-tuple-element.52.place_ref.place_in.refs_1_, s16[672,128]{1,0:T(8,128)(2,1)S(1)} %collective-permute-done.7.refs_0_, s16[672,128]{1,0:T(8,128)(2,1)S(1)} %collective-permute-done.8.refs_1_, f32[656,256]{1,0:T(8,128)S(1)} %sample_early.2.refs_2_, ...), custom_call_target="tpu_custom_call" | custom-call | flops 169869312 | bytes 4194304 | tf_op jit(solution)/shard_map/sample/pallas_call | solution.py:1066
  45.2 2.7 %spread.1 = (s16[672,128]{1,0:T(8,128)(2,1)S(1)}, s16[672,128]{1,0:T(8,128)(2,1)S(1)}, bf16[656,256]{1,0:T(8,128)(2,1)S(1)}, bf16[656,256]{1,0:T(8,128)(2,1)S(1)}) custom-call(f32[512]{0:T(512)S(1)} %bitcast.6, s32[2,512]{1,0:T(2,128)S(1)} %get-tuple-element.52.place_ref.place_in.refs_1_, f32[4,128]{1,0:T(4,128)S(1)} %sample.2.refs_2_.rounded_ref.refs_7_, ...), custom_call_target="tpu_custom_call" | custom-call | flops 169869312 | bytes 4194304 | tf_op jit(solution)/shard_map/spread/pallas_call | solution.py:410
  47.9 1.1 %collective-permute-start.11 = (s16[672,128]{1,0:T(8,128)(2,1)S(1)}, s16[672,128]{1,0:T(8,128)(2,1)S(1)}, u32[]{:S(2)}, u32[]{:S(2)}) collective-permute-start(s16[672,128]{1,0:T(8,128)(2,1)S(1)} %get-tuple-element.82), channel_id=1, source_target_pairs={{0,2},{1,3},{2,0},{3,1},{4,6},{5,7},{6,4},{7,5},{8,10},{9,11},{10,... | collective-permute-start | bytes 516104 | tf_op jit(solution)/shard_map/ppermute | solution.py:1190
  49.0 0.6 spread_rest.3
  49.5 0.7 collective-permute-start.10
  50.2 0.6 collective-permute-start.12
  50.8 4.4 %collective-permute-done.11.refs_1_.refs_2_ = s16[672,128]{1,0:T(8,128)(2,1)S(1)} collective-permute-done((s16[672,128]{1,0:T(8,128)(2,1)S(1)}, s16[672,128]{1,0:T(8,128)(2,1)S(1)}, u32[]{:S(2)}, u32[]{:S(2)}) %collective-permute-start.11) | collective-permute-done | bytes 172064 | tf_op jit(solution)/shard_map/ppermute | solution.py:1190
  55.2 0.7 forward_early.3
  55.8 1.9 %collective-permute-done.12.refs_3_ = s16[672,128]{1,0:T(8,128)(2,1)S(1)} collective-permute-done((s16[672,128]{1,0:T(8,128)(2,1)S(1)}, s16[672,128]{1,0:T(8,128)(2,1)S(1)}, u32[]{:S(2)}, u32[]{:S(2)}) %collective-permute-start.12) | collective-permute-done | bytes 172064 | tf_op jit(solution)/shard_map/ppermute | solution.py:1190
  57.7 1.8 %forward.3 = (f32[18,256,128]{2,1,0:T(8,128)S(1)}, s16[432,128]{1,0:T(8,128)(2,1)S(1)}, s16[304,128]{1,0:T(8,128)(2,1)S(1)}, s16[592,128]{1,0:T(8,128)(2,1)S(1)}...) custom-call(s16[672,128]{1,0:T(8,128)(2,1)S(1)} %get-tuple-element.80.refs_0_, ...), custom_call_target="tpu_custom_call" | custom-call | flops 301989888 | bytes 4718592 | tf_op jit(solution)/shard_map/forward/pallas_call | solution.py:689
  59.5 0.1 collective-permute-start.15
  59.6 0.7 collective-permute-start.14
  60.3 4.8 %collective-permute-start.13 = (s16[304,128]{1,0:T(8,128)(2,1)S(1)}, s16[304,128]{1,0:T(8,128)(2,1)S(1)}, u32[]{:S(2)}, u32[]{:S(2)}) collective-permute-start(s16[304,128]{1,0:T(8,128)(2,1)S(1)} %get-tuple-element.87), channel_id=1, source_target_pairs={{0,4},{8,12},{4,0},{12,8},{1,5},{9,13},{5,1},{13,9},{2,6},{10,14},... | collective-permute-start | bytes 233480 | tf_op jit(solution)/shard_map/ppermute | solution.py:1204
  65.2 0.2 pair_messages.3
  65.3 1.2 %collective-permute-start.16 = (s16[272,128]{1,0:T(8,128)(2,1)S(1)}, s16[272,128]{1,0:T(8,128)(2,1)S(1)}, u32[]{:S(2)}, u32[]{:S(2)}) collective-permute-start(s16[272,128]{1,0:T(8,128)(2,1)S(1)} %pair_messages.3), channel_id=1, source_target_pairs={{0,8},{4,12},{8,0},{12,4},{1,9},{5,13},{9,1},{13,5},{2,10},{6,14},... | collective-permute-start | bytes 208904 | tf_op jit(solution)/shard_map/ppermute | solution.py:1206
  66.5 1.1 %collective-permute-done.13.layers_ref = s16[304,128]{1,0:T(8,128)(2,1)S(1)} collective-permute-done((s16[304,128]{1,0:T(8,128)(2,1)S(1)}, s16[304,128]{1,0:T(8,128)(2,1)S(1)}, u32[]{:S(2)}, u32[]{:S(2)}) %collective-permute-start.13) | collective-permute-done | bytes 77856 | tf_op jit(solution)/shard_map/ppermute | solution.py:1204
  67.6 0.0 collective-permute-done.14.odd_ref.refs_3_.refs_1_
  67.6 0.5 borders.3.refs_1_
  68.1 3.8 %collective-permute-done.16.refs_6_ = s16[272,128]{1,0:T(8,128)(2,1)S(1)} collective-permute-done((s16[272,128]{1,0:T(8,128)(2,1)S(1)}, s16[272,128]{1,0:T(8,128)(2,1)S(1)}, u32[]{:S(2)}, u32[]{:S(2)}) %collective-permute-start.16) | collective-permute-done | bytes 69664 | tf_op jit(solution)/shard_map/ppermute | solution.py:1206
  71.9 2.3 %inverse.3 = (s16[672,128]{1,0:T(8,128)(2,1)S(1)}, s16[672,128]{1,0:T(8,128)(2,1)S(1)}, bf16[18,256,128]{2,1,0:T(8,128)(2,1)S(1)}, bf16[18,256,128]{2,1,0:T(8,128)(2,1)S(1)}) custom-call(f32[18,256,128]{2,1,0:T(8,128)S(1)} %get-tuple-element.86.refs_0_, f32[4,256,128]{2,1,0:T(8,128)S(1)} %borders.3.refs_1_, ...), custom_call_target="tpu_custom_call" | custom-call | flops 301989888 | bytes 4718592 | tf_op jit(solution)/shard_map/inverse/pallas_call | solution.py:921
  74.2 1.8 %collective-permute-start.19 = (s16[672,128]{1,0:T(8,128)(2,1)S(1)}, s16[672,128]{1,0:T(8,128)(2,1)S(1)}, u32[]{:S(2)}, u32[]{:S(2)}) collective-permute-start(s16[672,128]{1,0:T(8,128)(2,1)S(1)} %get-tuple-element.97), channel_id=1, source_target_pairs={{0,2},{1,3},{2,0},{3,1},{4,6},{5,7},{6,4},{7,5},{8,10},{9,11},{10,... | collective-permute-start | bytes 516104 | tf_op jit(solution)/shard_map/ppermute | solution.py:1190
  76.0 0.9 %inverse_rest.3 = (s16[672,128]{1,0:T(8,128)(2,1)S(1)}, s16[672,128]{1,0:T(8,128)(2,1)S(1)}) custom-call(bf16[18,256,128]{2,1,0:T(8,128)(2,1)S(1)} %get-tuple-element.92.field_high, bf16[18,256,128]{2,1,0:T(8,128)(2,1)S(1)} %get-tuple-element.93.field_low, bf16[4,48,256]{2,1,0:T(8,128)(2,1)S(1)} %copy-done.3, bf16[4,48,256]{2,1,0:T(8,128)(2,1)S(1)} %copy-done.4), custom_call_target="tpu_custom_call" | custom-call | flops 301989888 | bytes 4718592 | tf_op jit(solution)/shard_map/inverse_rest/pallas_call | solution.py:945
  76.9 0.1 collective-permute-start.17
  76.9 0.4 collective-permute-start.18
  77.4 1.0 %near_field.3.refs_8_ = f32[8,128]{1,0:T(8,128)S(1)} custom-call(s32[24]{0:T(128)S(1)} %get-tuple-element.100.place_ref, s32[24]{0:T(128)S(1)} %get-tuple-element.99.target_ref, s16[432,128]{1,0:T(8,128)(2,1)S(1)} %collective-permute-done.15.even_ref.refs_2_.refs_0_, s16[592,128]{1,0:T(8,128)(2,1)S(1)} %collective-permute-done.14.odd_ref.refs_3_.refs_1_, ...), custom_call_target="tpu_custom_call" | custom-call | flops 12582912 | bytes 786432 | tf_op jit(solution)/shard_map/near_field/pallas_call | solution.py:1124
  78.4 2.4 %collective-permute-done.19.refs_1_ = s16[672,128]{1,0:T(8,128)(2,1)S(1)} collective-permute-done((s16[672,128]{1,0:T(8,128)(2,1)S(1)}, s16[672,128]{1,0:T(8,128)(2,1)S(1)}, u32[]{:S(2)}, u32[]{:S(2)}) %collective-permute-start.19) | collective-permute-done | bytes 172064 | tf_op jit(solution)/shard_map/ppermute | solution.py:1190
  80.8 0.4 sample_early.3.refs_2_
  81.2 2.3 %collective-permute-done.18.refs_1_ = s16[672,128]{1,0:T(8,128)(2,1)S(1)} collective-permute-done((s16[672,128]{1,0:T(8,128)(2,1)S(1)}, s16[672,128]{1,0:T(8,128)(2,1)S(1)}, u32[]{:S(2)}, u32[]{:S(2)}) %collective-permute-start.18) | collective-permute-done | bytes 172064 | tf_op jit(solution)/shard_map/ppermute | solution.py:1190
  83.5 2.7 %sample.3 = f32[2,512]{1,0:T(2,128)} custom-call(s32[2,512]{1,0:T(2,128)S(1)} %get-tuple-element.52.place_ref.place_in.refs_1_, s16[672,128]{1,0:T(8,128)(2,1)S(1)} %collective-permute-done.17.refs_0_, s16[672,128]{1,0:T(8,128)(2,1)S(1)} %collective-permute-done.18.refs_1_, f32[656,256]{1,0:T(8,128)S(1)} %sample_early.3.refs_2_, ...), custom_call_target="tpu_custom_call" | custom-call | flops 169869312 | bytes 4194304 | tf_op jit(solution)/shard_map/sample/pallas_call | solution.py:1066
  (22 shorter events, 0.1 us)
Async XLA Ops:
  5.7 9.2 %collective-permute-start.1 = (s16[672,128]{1,0:T(8,128)(2,1)S(1)}, s16[672,128]{1,0:T(8,128)(2,1)S(1)}, u32[]{:S(2)}, u32[]{:S(2)}) collective-permute-start(s16[672,128]{1,0:T(8,128)(2,1)S(1)} %get-tuple-element.60), channel_id=1, source_target_pairs={{0,2},{1,3},{2,0},{3,1},{4,6},{5,7},{6,4},{7,5},{8,10},{9,11},{10,... | collective-permute-start | bytes 516104 | tf_op jit(solution)/shard_map/ppermute | solution.py:1190
  9.3 6.3 %collective-permute-start = (s16[672,128]{1,0:T(8,128)(2,1)S(1)}, s16[672,128]{1,0:T(8,128)(2,1)S(1)}, u32[]{:S(2)}, u32[]{:S(2)}) collective-permute-start(s16[672,128]{1,0:T(8,128)(2,1)S(1)} %get-tuple-element.59), channel_id=1, source_target_pairs={{0,1},{1,0},{2,3},{3,2},{4,5},{5,4},{6,7},{7,6},{8,9},{9,8},{10,11... | collective-permute-start | bytes 516104 | tf_op jit(solution)/shard_map/ppermute | solution.py:1190
  9.4 6.8 %collective-permute-start.2 = (s16[672,128]{1,0:T(8,128)(2,1)S(1)}, s16[672,128]{1,0:T(8,128)(2,1)S(1)}, u32[]{:S(2)}, u32[]{:S(2)}) collective-permute-start(s16[672,128]{1,0:T(8,128)(2,1)S(1)} %get-tuple-element.61), channel_id=1, source_target_pairs={{0,3},{1,2},{2,1},{3,0},{4,7},{5,6},{6,5},{7,4},{8,11},{9,10},{10,... | collective-permute-start | bytes 516104 | tf_op jit(solution)/shard_map/ppermute | solution.py:1190
  9.5 0.9 %copy-start.1 = (f32[64,512]{1,0:T(8,128)S(1)}, f32[64,512]{1,0:T(8,128)}, u32[]{:S(2)}) copy-start(f32[64,512]{1,0:T(8,128)} %refs_3_.8) | copy-start | bytes 393220
  10.4 4.5 %copy-start = (bf16[2,256,240]{2,1,0:T(8,128)(2,1)S(1)}, bf16[2,256,240]{2,1,0:T(8,128)(2,1)}, u32[]{:S(2)}) copy-start(bf16[2,256,240]{2,1,0:T(8,128)(2,1)} %constant.76.clone.refs_2_.refs_6_.table_ref) | copy-start | bytes 737284
  16.2 15.2 %copy-start.3 = (bf16[4,48,256]{2,1,0:T(8,128)(2,1)S(1)}, bf16[4,48,256]{2,1,0:T(8,128)(2,1)}, u32[]{:S(2)}) copy-start(bf16[4,48,256]{2,1,0:T(8,128)(2,1)} %constant.77.clone.refs_7_.high_ref) | copy-start | bytes 294916
  16.2 15.2 %copy-start.4 = (bf16[4,48,256]{2,1,0:T(8,128)(2,1)S(1)}, bf16[4,48,256]{2,1,0:T(8,128)(2,1)}, u32[]{:S(2)}) copy-start(bf16[4,48,256]{2,1,0:T(8,128)(2,1)} %constant.78.clone.refs_8_.low_ref) | copy-start | bytes 294916
  17.8 6.8 %collective-permute-start.5 = (s16[432,128]{1,0:T(8,128)(2,1)S(1)}, s16[432,128]{1,0:T(8,128)(2,1)S(1)}, u32[]{:S(2)}, u32[]{:S(2)}) collective-permute-start(s16[432,128]{1,0:T(8,128)(2,1)S(1)} %get-tuple-element.67), channel_id=1, source_target_pairs={{0,4},{8,12},{4,0},{12,8},{1,5},{9,13},{5,1},{13,9},{2,6},{10,14},... | collective-permute-start | bytes 331784 | tf_op jit(solution)/shard_map/ppermute | solution.py:1202
  19.4 7.8 %collective-permute-start.4 = (s16[592,128]{1,0:T(8,128)(2,1)S(1)}, s16[592,128]{1,0:T(8,128)(2,1)S(1)}, u32[]{:S(2)}, u32[]{:S(2)}) collective-permute-start(s16[592,128]{1,0:T(8,128)(2,1)S(1)} %get-tuple-element.66), channel_id=1, source_target_pairs={{4,8},{8,4},{5,9},{9,5},{6,10},{10,6},{7,11},{11,7},{20,24},{24,20... | collective-permute-start | bytes 454664 | tf_op jit(solution)/shard_map/ppermute | solution.py:1203
  20.1 7.1 %collective-permute-start.3 = (s16[304,128]{1,0:T(8,128)(2,1)S(1)}, s16[304,128]{1,0:T(8,128)(2,1)S(1)}, u32[]{:S(2)}, u32[]{:S(2)}) collective-permute-start(s16[304,128]{1,0:T(8,128)(2,1)S(1)} %get-tuple-element.65), channel_id=1, source_target_pairs={{0,4},{8,12},{4,0},{12,8},{1,5},{9,13},{5,1},{13,9},{2,6},{10,14},... | collective-permute-start | bytes 233480 | tf_op jit(solution)/shard_map/ppermute | solution.py:1204
  24.7 10.6 %copy-start.8 = (s32[24]{0:T(128)S(1)}, s32[24]{0:T(128)}, u32[]{:S(2)}) copy-start(s32[24]{0:T(128)} %param.21) | copy-start | bytes 292
  24.7 10.5 %copy-start.9 = (s32[24]{0:T(128)S(1)}, s32[24]{0:T(128)}, u32[]{:S(2)}) copy-start(s32[24]{0:T(128)} %param.22) | copy-start | bytes 292
  24.7 6.6 %collective-permute-start.6 = (s16[272,128]{1,0:T(8,128)(2,1)S(1)}, s16[272,128]{1,0:T(8,128)(2,1)S(1)}, u32[]{:S(2)}, u32[]{:S(2)}) collective-permute-start(s16[272,128]{1,0:T(8,128)(2,1)S(1)} %pair_messages.2), channel_id=1, source_target_pairs={{0,8},{4,12},{8,0},{12,4},{1,9},{5,13},{9,1},{13,5},{2,10},{6,14},... | collective-permute-start | bytes 208904 | tf_op jit(solution)/shard_map/ppermute | solution.py:1206
  31.4 5.5 %copy-start.2 = (bf16[24,128,128]{2,1,0:T(8,128)(2,1)S(1)}, bf16[24,128,128]{2,1,0:T(8,128)(2,1)}, u32[]{:S(2)}) copy-start(bf16[24,128,128]{2,1,0:T(8,128)(2,1)} %refs_3_.10) | copy-start | bytes 2359300
  33.7 7.2 %collective-permute-start.9 = (s16[672,128]{1,0:T(8,128)(2,1)S(1)}, s16[672,128]{1,0:T(8,128)(2,1)S(1)}, u32[]{:S(2)}, u32[]{:S(2)}) collective-permute-start(s16[672,128]{1,0:T(8,128)(2,1)S(1)} %get-tuple-element.75), channel_id=1, source_target_pairs={{0,2},{1,3},{2,0},{3,1},{4,6},{5,7},{6,4},{7,5},{8,10},{9,11},{10,... | collective-permute-start | bytes 516104 | tf_op jit(solution)/shard_map/ppermute | solution.py:1190
  36.2 5.2 %collective-permute-start.7 = (s16[672,128]{1,0:T(8,128)(2,1)S(1)}, s16[672,128]{1,0:T(8,128)(2,1)S(1)}, u32[]{:S(2)}, u32[]{:S(2)}) collective-permute-start(s16[672,128]{1,0:T(8,128)(2,1)S(1)} %get-tuple-element.72), channel_id=1, source_target_pairs={{0,1},{1,0},{2,3},{3,2},{4,5},{5,4},{6,7},{7,6},{8,9},{9,8},{10,11... | collective-permute-start | bytes 516104 | tf_op jit(solution)/shard_map/ppermute | solution.py:1190
  36.3 6.8 %collective-permute-start.8 = (s16[672,128]{1,0:T(8,128)(2,1)S(1)}, s16[672,128]{1,0:T(8,128)(2,1)S(1)}, u32[]{:S(2)}, u32[]{:S(2)}) collective-permute-start(s16[672,128]{1,0:T(8,128)(2,1)S(1)} %get-tuple-element.73), channel_id=1, source_target_pairs={{0,3},{1,2},{2,1},{3,0},{4,7},{5,6},{6,5},{7,4},{8,11},{9,10},{10,... | collective-permute-start | bytes 516104 | tf_op jit(solution)/shard_map/ppermute | solution.py:1190
  38.0 3.0 %copy-start.5 = (bf16[4,128,256]{2,1,0:T(8,128)(2,1)S(1)}, bf16[4,128,256]{2,1,0:T(8,128)(2,1)}, u32[]{:S(2)}) copy-start(bf16[4,128,256]{2,1,0:T(8,128)(2,1)} %constant.79.clone.refs_2_.refs_3_) | copy-start | bytes 786436
  38.0 3.0 %copy-start.6 = (bf16[4,128,256]{2,1,0:T(8,128)(2,1)S(1)}, bf16[4,128,256]{2,1,0:T(8,128)(2,1)}, u32[]{:S(2)}) copy-start(bf16[4,128,256]{2,1,0:T(8,128)(2,1)} %constant.80.clone.refs_3_.refs_4_) | copy-start | bytes 786436
  40.9 2.1 %copy-start.7 = (s32[512]{0:T(512)S(1)}, s32[512]{0:T(512)}, u32[]{:S(2)}) copy-start(s32[512]{0:T(512)} %param.17) | copy-start | bytes 6148
  47.9 7.3 %collective-permute-start.11 = (s16[672,128]{1,0:T(8,128)(2,1)S(1)}, s16[672,128]{1,0:T(8,128)(2,1)S(1)}, u32[]{:S(2)}, u32[]{:S(2)}) collective-permute-start(s16[672,128]{1,0:T(8,128)(2,1)S(1)} %get-tuple-element.82), channel_id=1, source_target_pairs={{0,2},{1,3},{2,0},{3,1},{4,6},{5,7},{6,4},{7,5},{8,10},{9,11},{10,... | collective-permute-start | bytes 516104 | tf_op jit(solution)/shard_map/ppermute | solution.py:1190
  49.5 6.3 %collective-permute-start.10 = (s16[672,128]{1,0:T(8,128)(2,1)S(1)}, s16[672,128]{1,0:T(8,128)(2,1)S(1)}, u32[]{:S(2)}, u32[]{:S(2)}) collective-permute-start(s16[672,128]{1,0:T(8,128)(2,1)S(1)} %get-tuple-element.81), channel_id=1, source_target_pairs={{0,1},{1,0},{2,3},{3,2},{4,5},{5,4},{6,7},{7,6},{8,9},{9,8},{10,11... | collective-permute-start | bytes 516104 | tf_op jit(solution)/shard_map/ppermute | solution.py:1190
  50.2 7.5 %collective-permute-start.12 = (s16[672,128]{1,0:T(8,128)(2,1)S(1)}, s16[672,128]{1,0:T(8,128)(2,1)S(1)}, u32[]{:S(2)}, u32[]{:S(2)}) collective-permute-start(s16[672,128]{1,0:T(8,128)(2,1)S(1)} %get-tuple-element.83), channel_id=1, source_target_pairs={{0,3},{1,2},{2,1},{3,0},{4,7},{5,6},{6,5},{7,4},{8,11},{9,10},{10,... | collective-permute-start | bytes 516104 | tf_op jit(solution)/shard_map/ppermute | solution.py:1190
  59.5 5.6 %collective-permute-start.15 = (s16[432,128]{1,0:T(8,128)(2,1)S(1)}, s16[432,128]{1,0:T(8,128)(2,1)S(1)}, u32[]{:S(2)}, u32[]{:S(2)}) collective-permute-start(s16[432,128]{1,0:T(8,128)(2,1)S(1)} %get-tuple-element.89), channel_id=1, source_target_pairs={{0,4},{8,12},{4,0},{12,8},{1,5},{9,13},{5,1},{13,9},{2,6},{10,14},... | collective-permute-start | bytes 331784 | tf_op jit(solution)/shard_map/ppermute | solution.py:1202
  59.6 8.0 %collective-permute-start.14 = (s16[592,128]{1,0:T(8,128)(2,1)S(1)}, s16[592,128]{1,0:T(8,128)(2,1)S(1)}, u32[]{:S(2)}, u32[]{:S(2)}) collective-permute-start(s16[592,128]{1,0:T(8,128)(2,1)S(1)} %get-tuple-element.88), channel_id=1, source_target_pairs={{4,8},{8,4},{5,9},{9,5},{6,10},{10,6},{7,11},{11,7},{20,24},{24,20... | collective-permute-start | bytes 454664 | tf_op jit(solution)/shard_map/ppermute | solution.py:1203
  60.3 7.3 %collective-permute-start.13 = (s16[304,128]{1,0:T(8,128)(2,1)S(1)}, s16[304,128]{1,0:T(8,128)(2,1)S(1)}, u32[]{:S(2)}, u32[]{:S(2)}) collective-permute-start(s16[304,128]{1,0:T(8,128)(2,1)S(1)} %get-tuple-element.87), channel_id=1, source_target_pairs={{0,4},{8,12},{4,0},{12,8},{1,5},{9,13},{5,1},{13,9},{2,6},{10,14},... | collective-permute-start | bytes 233480 | tf_op jit(solution)/shard_map/ppermute | solution.py:1204
  65.3 6.5 %collective-permute-start.16 = (s16[272,128]{1,0:T(8,128)(2,1)S(1)}, s16[272,128]{1,0:T(8,128)(2,1)S(1)}, u32[]{:S(2)}, u32[]{:S(2)}) collective-permute-start(s16[272,128]{1,0:T(8,128)(2,1)S(1)} %pair_messages.3), channel_id=1, source_target_pairs={{0,8},{4,12},{8,0},{12,4},{1,9},{5,13},{9,1},{13,5},{2,10},{6,14},... | collective-permute-start | bytes 208904 | tf_op jit(solution)/shard_map/ppermute | solution.py:1206
  74.2 6.6 %collective-permute-start.19 = (s16[672,128]{1,0:T(8,128)(2,1)S(1)}, s16[672,128]{1,0:T(8,128)(2,1)S(1)}, u32[]{:S(2)}, u32[]{:S(2)}) collective-permute-start(s16[672,128]{1,0:T(8,128)(2,1)S(1)} %get-tuple-element.97), channel_id=1, source_target_pairs={{0,2},{1,3},{2,0},{3,1},{4,6},{5,7},{6,4},{7,5},{8,10},{9,11},{10,... | collective-permute-start | bytes 516104 | tf_op jit(solution)/shard_map/ppermute | solution.py:1190
  76.9 4.4 %collective-permute-start.17 = (s16[672,128]{1,0:T(8,128)(2,1)S(1)}, s16[672,128]{1,0:T(8,128)(2,1)S(1)}, u32[]{:S(2)}, u32[]{:S(2)}) collective-permute-start(s16[672,128]{1,0:T(8,128)(2,1)S(1)} %get-tuple-element.94), channel_id=1, source_target_pairs={{0,1},{1,0},{2,3},{3,2},{4,5},{5,4},{6,7},{7,6},{8,9},{9,8},{10,11... | collective-permute-start | bytes 516104 | tf_op jit(solution)/shard_map/ppermute | solution.py:1190
  76.9 6.6 %collective-permute-start.18 = (s16[672,128]{1,0:T(8,128)(2,1)S(1)}, s16[672,128]{1,0:T(8,128)(2,1)S(1)}, u32[]{:S(2)}, u32[]{:S(2)}) collective-permute-start(s16[672,128]{1,0:T(8,128)(2,1)S(1)} %get-tuple-element.95), channel_id=1, source_target_pairs={{0,3},{1,2},{2,1},{3,0},{4,7},{5,6},{6,5},{7,4},{8,11},{9,10},{10,... | collective-permute-start | bytes 516104 | tf_op jit(solution)/shard_map/ppermute | solution.py:1190

commit v15 on v14

--- a/solution.py
+++ b/solution.py
@@ -277,13 +277,13 @@
 
 
 def start_kernel(reach_x, reach_y, flips, *refs):
-    vector_ref, *remote = refs[:8]
+    vector_in, *remote = refs[:8]
     refs = refs[8:]
     outs, refs = refs[: len(flips)], refs[len(flips) :]
     wides, (weight_ref, places_out), refs = refs[:2], refs[2:4], refs[4:]
-    rounded, high, low, stencil, flag, samples, dipoles = refs[:7]
-    place_ref, sems, head, total = refs[7:11]
-    grids = refs[11:]
+    rounded, high, low, stencil, flag, samples, dipoles, vector_ref = refs[:8]
+    place_ref, sems, head, total = refs[8:12]
+    grids = refs[12:]
     tiles = samples.shape[0]
     copies = []
     fetch = lambda source, target: copies.append(
@@ -292,6 +292,7 @@
     rounded_in, high_in, low_in, stencil_in, flag_in, sample_in, dipole_in = remote
     fetch(stencil_in, stencil)
     fetch(flag_in, flag)
+    fetch(vector_in, vector_ref)
     for tile in range(tiles):
         lanes = pl.ds(tile * BLOCK, BLOCK)
         fetch(sample_in.at[:, lanes], samples.at[tile])
@@ -383,9 +384,8 @@
     if placed is None:
         stencil, flag, sample, dipole = raw
         operands = [vector, rounded, *table, stencil, flag.reshape(1, -1), sample, dipole]
-        pinned = [pltpu.with_memory_space_constraint(value, pltpu.HBM) for value in operands[1:]]
-        operands = [vector] + pinned
-        in_specs = [in_smem()] + [pl.BlockSpec(memory_space=pltpu.HBM)] * 7
+        operands = [pltpu.with_memory_space_constraint(value, pltpu.HBM) for value in operands]
+        in_specs = [pl.BlockSpec(memory_space=pltpu.HBM)] * 8
         out_shapes += [jax.ShapeDtypeStruct(woven, F32)]
         out_shapes += [jax.ShapeDtypeStruct((2, count), jnp.int32)]
         out_shapes += [jax.ShapeDtypeStruct(rounded.shape, F32)]
@@ -396,8 +396,9 @@
             pltpu.VMEM((1, count), jnp.int32),
             tiled,
             tiled,
+            pltpu.SMEM((count,), F32),
             pltpu.SMEM((2, count), jnp.int32),
-            pltpu.SemaphoreType.DMA((6 + 2 * blocks,)),
+            pltpu.SemaphoreType.DMA((7 + 2 * blocks,)),
         ] + work
     else:
         operands = [vector, placed[0], rounded, *table, placed[1]]
@@ -612,7 +613,7 @@
         transform_pieces(table_ref[lax.axis_index("pair") ^ core], stacked, before, spectrum)
         before = spectrum
 
-    chunk = 64
+    chunk = 128
 
     def body(index, largest):
         rows = pl.ds(pl.multiple_of(index * chunk, chunk), chunk)
@@ -837,7 +838,7 @@
     field_high, field_low, ready, head = refs[3 + len(flips) :]
     half = reach_x // 2
     span = reach_x - 4
-    chunk = 64
+    chunk = 128
     head_rows = from_even.shape[0] - GRID - GRID // 2
     on_left = (lax.axis_index("wide") & 1) == 1
     moment_units = []

time: 86.7 us -> 85.2 us (0.983)
  Pallas kernels: 36 us -> 34.4 us
where the time goes in v15:
time: 85.2 us; the launch traced here: 85 us
  Pallas kernels  34.4 us (40%)
  starting transfers between devices  24.9 us (29%)
  waiting for transfers between devices  23.1 us (27%)
  local copies, waits for them, and re-layouts  2.02 us (2%)
    ppermute x12, waiting for transfers between devices, turned(): lax.ppermute(part, Y_AXES, swap_pairs)  13.5 us
    ppermute x12, starting transfers between devices, turned(): lax.ppermute(part, Y_AXES, swap_pairs)  10 us
    ppermute x2, starting transfers between devices, convolve_and_sample(): even_layers = lax.ppermute(layers, 'wide', even_swap)  9.03 us
    pallas_call x2, Pallas kernels, spread(): pl.pallas_call(functools.partial(start_kernel if placed is None else spre...  7.69 us
    ppermute x2, waiting for transfers between devices, convolve_and_sample(): lax.ppermute(message, 'wide', [(i, i ^ flip) for i in range(x_count)])  7.04 us
    pallas_call x2, Pallas kernels, sample(): pl.pallas_call(functools.partial(sample_kernel, last, reach_x, reach_y, f...  4.87 us
    pallas_call x2, Pallas kernels, inverse(): pl.pallas_call(functools.partial(inverse_kernel, reach_x, reach_y, flips,...  4.13 us
    pallas_call x1, Pallas kernels, place_sample_lines(): pl.pallas_call(functools.partial(sample_lines_kernel, blocks), grid=(1,),...  3.41 us
  transfers between devices with their start and end apart: 20, of which 10 were waited for; matrix products, arithmetic and copies ran while one was open for 1% of the time, Pallas kernels for 17%

profile of v15, /device:TPU:0, one launch (start us, length us, event | category | flops | bytes accessed | tf_op | source)
XLA Modules:
  0.0 85.0 jit_solution(13547383935027205799)
XLA Ops:
  0.0 5.0 %start.1 = (s16[672,128]{1,0:T(8,128)(2,1)S(1)}, s16[672,128]{1,0:T(8,128)(2,1)S(1)}, bf16[656,256]{1,0:T(8,128)(2,1)S(1)}, bf16[656,256]{1,0:T(8,128)(2,1)S(1)}...) custom-call(f32[512]{0:T(512)} %refs_0_.2, ...), custom_call_target="tpu_custom_call" | custom-call | flops 169869312 | bytes 4194304 | tf_op jit(solution)/shard_map/start/pallas_call | solution.py:411
  5.0 3.0 %collective-permute-start.1 = (s16[672,128]{1,0:T(8,128)(2,1)S(1)}, s16[672,128]{1,0:T(8,128)(2,1)S(1)}, u32[]{:S(2)}, u32[]{:S(2)}) collective-permute-start(s16[672,128]{1,0:T(8,128)(2,1)S(1)} %get-tuple-element.60), channel_id=1, source_target_pairs={{0,2},{1,3},{2,0},{3,1},{4,6},{5,7},{6,4},{7,5},{8,10},{9,11},{10,... | collective-permute-start | bytes 516104 | tf_op jit(solution)/shard_map/ppermute | solution.py:1191
  8.0 0.6 spread_rest.2
  8.6 0.1 collective-permute-start
  8.7 0.1 collective-permute-start.2
  8.8 0.9 %copy-done.1 = f32[64,512]{1,0:T(8,128)S(1)} copy-done((f32[64,512]{1,0:T(8,128)S(1)}, f32[64,512]{1,0:T(8,128)}, u32[]{:S(2)}) %copy-start.1) | copy-done | bytes 131096
  9.7 3.4 %place_sample_lines.1.refs_8_.refs_5_ = f32[8192,128]{1,0:T(8,128)S(1)} custom-call(s32[2,512]{1,0:T(2,128)S(1)} %get-tuple-element.52.place_ref.place_in.refs_1_, f32[64,512]{1,0:T(8,128)S(1)} %copy-done.1, f32[64,512]{1,0:T(8,128)S(1)} %copy-done.1, f32[64,512]{1,0:T(8,128)S(1)} %copy-done.1, f32[64,512]{1,0:T(8,128)S(1)} %copy-done.1), custom_call_target="tpu_custom_call" | custom-call | flops 1048576 | bytes 4194304 | tf_op jit(solution)/shard_map/place_sample_lines/pallas_call | solution.py:480
  13.2 1.1 %dynamic-slice_bitcast_fusion.refs_7_.modes_ref.refs_9_ = f32[4,256,128]{2,1,0:T(8,128)S(1)} fusion(f32[4,4,256,128]{3,2,1,0:T(8,128)} %constant.73.clone, s32[]{:T(128)S(6)} %select_n.30), kind=kLoop, calls=%fused_computation | loop fusion | bytes 1048580 | tf_op jit(solution)/shard_map/jit(dynamic_index_in_dim)/squeeze | solution.py:1168
  14.2 0.0 collective-permute-done.1.refs_1_.refs_2_
  14.3 0.7 forward_early.2
  14.9 0.0 collective-permute-done.refs_1_
  15.0 0.5 collective-permute-done.2.refs_3_
  15.5 1.4 %forward.2 = (f32[18,256,128]{2,1,0:T(8,128)S(1)}, s16[432,128]{1,0:T(8,128)(2,1)S(1)}, s16[304,128]{1,0:T(8,128)(2,1)S(1)}, s16[592,128]{1,0:T(8,128)(2,1)S(1)}...) custom-call(s16[672,128]{1,0:T(8,128)(2,1)S(1)} %get-tuple-element.58.refs_0_, ...), custom_call_target="tpu_custom_call" | custom-call | flops 301989888 | bytes 4718592 | tf_op jit(solution)/shard_map/forward/pallas_call | solution.py:690
  17.0 1.6 %collective-permute-start.5 = (s16[432,128]{1,0:T(8,128)(2,1)S(1)}, s16[432,128]{1,0:T(8,128)(2,1)S(1)}, u32[]{:S(2)}, u32[]{:S(2)}) collective-permute-start(s16[432,128]{1,0:T(8,128)(2,1)S(1)} %get-tuple-element.67), channel_id=1, source_target_pairs={{0,4},{8,12},{4,0},{12,8},{1,5},{9,13},{5,1},{13,9},{2,6},{10,14},... | collective-permute-start | bytes 331784 | tf_op jit(solution)/shard_map/ppermute | solution.py:1203
  18.6 0.8 collective-permute-start.4
  19.4 4.5 %collective-permute-start.3 = (s16[304,128]{1,0:T(8,128)(2,1)S(1)}, s16[304,128]{1,0:T(8,128)(2,1)S(1)}, u32[]{:S(2)}, u32[]{:S(2)}) collective-permute-start(s16[304,128]{1,0:T(8,128)(2,1)S(1)} %get-tuple-element.65), channel_id=1, source_target_pairs={{0,4},{8,12},{4,0},{12,8},{1,5},{9,13},{5,1},{13,9},{2,6},{10,14},... | collective-permute-start | bytes 233480 | tf_op jit(solution)/shard_map/ppermute | solution.py:1205
  23.9 0.0 collective-permute-done.5.even_ref.refs_2_.refs_0_
  23.9 0.2 pair_messages.2
  24.1 0.0 copy-start.8
  24.1 0.0 copy-start.9
  24.1 1.4 %collective-permute-start.6 = (s16[272,128]{1,0:T(8,128)(2,1)S(1)}, s16[272,128]{1,0:T(8,128)(2,1)S(1)}, u32[]{:S(2)}, u32[]{:S(2)}) collective-permute-start(s16[272,128]{1,0:T(8,128)(2,1)S(1)} %pair_messages.2), channel_id=1, source_target_pairs={{0,8},{4,12},{8,0},{12,4},{1,9},{5,13},{9,1},{13,5},{2,10},{6,14},... | collective-permute-start | bytes 208904 | tf_op jit(solution)/shard_map/ppermute | solution.py:1207
  25.5 1.0 %collective-permute-done.3.layers_ref = s16[304,128]{1,0:T(8,128)(2,1)S(1)} collective-permute-done((s16[304,128]{1,0:T(8,128)(2,1)S(1)}, s16[304,128]{1,0:T(8,128)(2,1)S(1)}, u32[]{:S(2)}, u32[]{:S(2)}) %collective-permute-start.3) | collective-permute-done | bytes 77856 | tf_op jit(solution)/shard_map/ppermute | solution.py:1205
  26.6 0.0 collective-permute-done.4.odd_ref.refs_3_.refs_1_
  26.6 0.4 borders.2.refs_1_
  27.0 3.5 %collective-permute-done.6.refs_6_ = s16[272,128]{1,0:T(8,128)(2,1)S(1)} collective-permute-done((s16[272,128]{1,0:T(8,128)(2,1)S(1)}, s16[272,128]{1,0:T(8,128)(2,1)S(1)}, u32[]{:S(2)}, u32[]{:S(2)}) %collective-permute-start.6) | collective-permute-done | bytes 69664 | tf_op jit(solution)/shard_map/ppermute | solution.py:1207
  30.6 2.1 %inverse.2 = (s16[672,128]{1,0:T(8,128)(2,1)S(1)}, s16[672,128]{1,0:T(8,128)(2,1)S(1)}, bf16[18,256,128]{2,1,0:T(8,128)(2,1)S(1)}, bf16[18,256,128]{2,1,0:T(8,128)(2,1)S(1)}) custom-call(f32[18,256,128]{2,1,0:T(8,128)S(1)} %get-tuple-element.64.refs_0_, f32[4,256,128]{2,1,0:T(8,128)S(1)} %borders.2.refs_1_, ...), custom_call_target="tpu_custom_call" | custom-call | flops 301989888 | bytes 4718592 | tf_op jit(solution)/shard_map/inverse/pallas_call | solution.py:922
  32.6 1.6 %collective-permute-start.9 = (s16[672,128]{1,0:T(8,128)(2,1)S(1)}, s16[672,128]{1,0:T(8,128)(2,1)S(1)}, u32[]{:S(2)}, u32[]{:S(2)}) collective-permute-start(s16[672,128]{1,0:T(8,128)(2,1)S(1)} %get-tuple-element.75), channel_id=1, source_target_pairs={{0,2},{1,3},{2,0},{3,1},{4,6},{5,7},{6,4},{7,5},{8,10},{9,11},{10,... | collective-permute-start | bytes 516104 | tf_op jit(solution)/shard_map/ppermute | solution.py:1191
  34.2 0.9 %inverse_rest.2 = (s16[672,128]{1,0:T(8,128)(2,1)S(1)}, s16[672,128]{1,0:T(8,128)(2,1)S(1)}) custom-call(bf16[18,256,128]{2,1,0:T(8,128)(2,1)S(1)} %get-tuple-element.70.field_high, bf16[18,256,128]{2,1,0:T(8,128)(2,1)S(1)} %get-tuple-element.71.field_low, bf16[4,48,256]{2,1,0:T(8,128)(2,1)S(1)} %copy-done.3, bf16[4,48,256]{2,1,0:T(8,128)(2,1)S(1)} %copy-done.4), custom_call_target="tpu_custom_call" | custom-call | flops 301989888 | bytes 4718592 | tf_op jit(solution)/shard_map/inverse_rest/pallas_call | solution.py:946
  35.1 0.1 collective-permute-start.7
  35.2 0.7 collective-permute-start.8
  35.8 1.0 %near_field.2.refs_8_.refs_0_ = f32[8,128]{1,0:T(8,128)S(1)} custom-call(s32[24]{0:T(128)S(1)} %get-tuple-element.100.place_ref, s32[24]{0:T(128)S(1)} %get-tuple-element.99.target_ref, s16[432,128]{1,0:T(8,128)(2,1)S(1)} %collective-permute-done.5.even_ref.refs_2_.refs_0_, s16[592,128]{1,0:T(8,128)(2,1)S(1)} %collective-permute-done.4.odd_ref.refs_3_.refs_1_, ...), custom_call_target="tpu_custom_call" | custom-call | flops 12582912 | bytes 786432 | tf_op jit(solution)/shard_map/near_field/pallas_call | solution.py:1125
  36.9 3.0 %place_lines.1.refs_5_ = f32[8192,128]{1,0:T(8,128)S(1)} custom-call(s32[2,512]{1,0:T(2,128)S(1)} %get-tuple-element.52.place_ref.place_in.refs_1_, f32[256,128]{1,0:T(8,128)S(1)} %get-tuple-element.77.coeff_ref, f32[8,128]{1,0:T(8,128)S(1)} %near_field.2.refs_8_.refs_0_), custom_call_target="tpu_custom_call" | custom-call | flops 1048576 | bytes 4194304 | tf_op jit(solution)/shard_map/place_lines/pallas_call | solution.py:496
  39.9 0.0 collective-permute-done.9.refs_1_
  39.9 0.4 sample_early.2.refs_2_
  40.3 0.0 collective-permute-done.7.refs_0_
  40.4 1.6 %collective-permute-done.8.refs_1_ = s16[672,128]{1,0:T(8,128)(2,1)S(1)} collective-permute-done((s16[672,128]{1,0:T(8,128)(2,1)S(1)}, s16[672,128]{1,0:T(8,128)(2,1)S(1)}, u32[]{:S(2)}, u32[]{:S(2)}) %collective-permute-start.8) | collective-permute-done | bytes 172064 | tf_op jit(solution)/shard_map/ppermute | solution.py:1191
  42.0 2.1 %sample.2.refs_2_.rounded_ref.refs_7_ = f32[4,128]{1,0:T(4,128)S(1)} custom-call(s32[2,512]{1,0:T(2,128)S(1)} %get-tuple-element.52.place_ref.place_in.refs_1_, s16[672,128]{1,0:T(8,128)(2,1)S(1)} %collective-permute-done.7.refs_0_, s16[672,128]{1,0:T(8,128)(2,1)S(1)} %collective-permute-done.8.refs_1_, f32[656,256]{1,0:T(8,128)S(1)} %sample_early.2.refs_2_, ...), custom_call_target="tpu_custom_call" | custom-call | flops 169869312 | bytes 4194304 | tf_op jit(solution)/shard_map/sample/pallas_call | solution.py:1067
  44.1 2.7 %spread.1 = (s16[672,128]{1,0:T(8,128)(2,1)S(1)}, s16[672,128]{1,0:T(8,128)(2,1)S(1)}, bf16[656,256]{1,0:T(8,128)(2,1)S(1)}, bf16[656,256]{1,0:T(8,128)(2,1)S(1)}) custom-call(f32[512]{0:T(512)S(1)} %bitcast.6, s32[2,512]{1,0:T(2,128)S(1)} %get-tuple-element.52.place_ref.place_in.refs_1_, f32[4,128]{1,0:T(4,128)S(1)} %sample.2.refs_2_.rounded_ref.refs_7_, ...), custom_call_target="tpu_custom_call" | custom-call | flops 169869312 | bytes 4194304 | tf_op jit(solution)/shard_map/spread/pallas_call | solution.py:411
  46.8 1.3 %collective-permute-start.11 = (s16[672,128]{1,0:T(8,128)(2,1)S(1)}, s16[672,128]{1,0:T(8,128)(2,1)S(1)}, u32[]{:S(2)}, u32[]{:S(2)}) collective-permute-start(s16[672,128]{1,0:T(8,128)(2,1)S(1)} %get-tuple-element.82), channel_id=1, source_target_pairs={{0,2},{1,3},{2,0},{3,1},{4,6},{5,7},{6,4},{7,5},{8,10},{9,11},{10,... | collective-permute-start | bytes 516104 | tf_op jit(solution)/shard_map/ppermute | solution.py:1191
  48.1 0.6 spread_rest.3
  48.6 0.6 collective-permute-start.10
  49.2 0.4 collective-permute-start.12
  49.6 4.4 %collective-permute-done.11.refs_1_.refs_2_ = s16[672,128]{1,0:T(8,128)(2,1)S(1)} collective-permute-done((s16[672,128]{1,0:T(8,128)(2,1)S(1)}, s16[672,128]{1,0:T(8,128)(2,1)S(1)}, u32[]{:S(2)}, u32[]{:S(2)}) %collective-permute-start.11) | collective-permute-done | bytes 172064 | tf_op jit(solution)/shard_map/ppermute | solution.py:1191
  54.0 0.7 forward_early.3
  54.7 2.2 %collective-permute-done.12.refs_3_ = s16[672,128]{1,0:T(8,128)(2,1)S(1)} collective-permute-done((s16[672,128]{1,0:T(8,128)(2,1)S(1)}, s16[672,128]{1,0:T(8,128)(2,1)S(1)}, u32[]{:S(2)}, u32[]{:S(2)}) %collective-permute-start.12) | collective-permute-done | bytes 172064 | tf_op jit(solution)/shard_map/ppermute | solution.py:1191
  56.9 1.4 %forward.3 = (f32[18,256,128]{2,1,0:T(8,128)S(1)}, s16[432,128]{1,0:T(8,128)(2,1)S(1)}, s16[304,128]{1,0:T(8,128)(2,1)S(1)}, s16[592,128]{1,0:T(8,128)(2,1)S(1)}...) custom-call(s16[672,128]{1,0:T(8,128)(2,1)S(1)} %get-tuple-element.80.refs_0_, ...), custom_call_target="tpu_custom_call" | custom-call | flops 301989888 | bytes 4718592 | tf_op jit(solution)/shard_map/forward/pallas_call | solution.py:690
  58.4 0.1 collective-permute-start.15
  58.5 0.9 %collective-permute-start.14 = (s16[592,128]{1,0:T(8,128)(2,1)S(1)}, s16[592,128]{1,0:T(8,128)(2,1)S(1)}, u32[]{:S(2)}, u32[]{:S(2)}) collective-permute-start(s16[592,128]{1,0:T(8,128)(2,1)S(1)} %get-tuple-element.88), channel_id=1, source_target_pairs={{4,8},{8,4},{5,9},{9,5},{6,10},{10,6},{7,11},{11,7},{20,24},{24,20... | collective-permute-start | bytes 454664 | tf_op jit(solution)/shard_map/ppermute | solution.py:1204
  59.4 4.6 %collective-permute-start.13 = (s16[304,128]{1,0:T(8,128)(2,1)S(1)}, s16[304,128]{1,0:T(8,128)(2,1)S(1)}, u32[]{:S(2)}, u32[]{:S(2)}) collective-permute-start(s16[304,128]{1,0:T(8,128)(2,1)S(1)} %get-tuple-element.87), channel_id=1, source_target_pairs={{0,4},{8,12},{4,0},{12,8},{1,5},{9,13},{5,1},{13,9},{2,6},{10,14},... | collective-permute-start | bytes 233480 | tf_op jit(solution)/shard_map/ppermute | solution.py:1205
  63.9 0.2 pair_messages.3
  64.1 1.0 %collective-permute-start.16 = (s16[272,128]{1,0:T(8,128)(2,1)S(1)}, s16[272,128]{1,0:T(8,128)(2,1)S(1)}, u32[]{:S(2)}, u32[]{:S(2)}) collective-permute-start(s16[272,128]{1,0:T(8,128)(2,1)S(1)} %pair_messages.3), channel_id=1, source_target_pairs={{0,8},{4,12},{8,0},{12,4},{1,9},{5,13},{9,1},{13,5},{2,10},{6,14},... | collective-permute-start | bytes 208904 | tf_op jit(solution)/shard_map/ppermute | solution.py:1207
  65.1 1.5 %collective-permute-done.13.layers_ref = s16[304,128]{1,0:T(8,128)(2,1)S(1)} collective-permute-done((s16[304,128]{1,0:T(8,128)(2,1)S(1)}, s16[304,128]{1,0:T(8,128)(2,1)S(1)}, u32[]{:S(2)}, u32[]{:S(2)}) %collective-permute-start.13) | collective-permute-done | bytes 77856 | tf_op jit(solution)/shard_map/ppermute | solution.py:1205
  66.6 0.4 borders.3.refs_1_
  67.0 3.5 %collective-permute-done.16.refs_6_ = s16[272,128]{1,0:T(8,128)(2,1)S(1)} collective-permute-done((s16[272,128]{1,0:T(8,128)(2,1)S(1)}, s16[272,128]{1,0:T(8,128)(2,1)S(1)}, u32[]{:S(2)}, u32[]{:S(2)}) %collective-permute-start.16) | collective-permute-done | bytes 69664 | tf_op jit(solution)/shard_map/ppermute | solution.py:1207
  70.6 2.1 %inverse.3 = (s16[672,128]{1,0:T(8,128)(2,1)S(1)}, s16[672,128]{1,0:T(8,128)(2,1)S(1)}, bf16[18,256,128]{2,1,0:T(8,128)(2,1)S(1)}, bf16[18,256,128]{2,1,0:T(8,128)(2,1)S(1)}) custom-call(f32[18,256,128]{2,1,0:T(8,128)S(1)} %get-tuple-element.86.refs_0_, f32[4,256,128]{2,1,0:T(8,128)S(1)} %borders.3.refs_1_, ...), custom_call_target="tpu_custom_call" | custom-call | flops 301989888 | bytes 4718592 | tf_op jit(solution)/shard_map/inverse/pallas_call | solution.py:922
  72.6 1.7 %collective-permute-start.19 = (s16[672,128]{1,0:T(8,128)(2,1)S(1)}, s16[672,128]{1,0:T(8,128)(2,1)S(1)}, u32[]{:S(2)}, u32[]{:S(2)}) collective-permute-start(s16[672,128]{1,0:T(8,128)(2,1)S(1)} %get-tuple-element.97), channel_id=1, source_target_pairs={{0,2},{1,3},{2,0},{3,1},{4,6},{5,7},{6,4},{7,5},{8,10},{9,11},{10,... | collective-permute-start | bytes 516104 | tf_op jit(solution)/shard_map/ppermute | solution.py:1191
  74.3 0.9 %inverse_rest.3 = (s16[672,128]{1,0:T(8,128)(2,1)S(1)}, s16[672,128]{1,0:T(8,128)(2,1)S(1)}) custom-call(bf16[18,256,128]{2,1,0:T(8,128)(2,1)S(1)} %get-tuple-element.92.field_high, bf16[18,256,128]{2,1,0:T(8,128)(2,1)S(1)} %get-tuple-element.93.field_low, bf16[4,48,256]{2,1,0:T(8,128)(2,1)S(1)} %copy-done.3, bf16[4,48,256]{2,1,0:T(8,128)(2,1)S(1)} %copy-done.4), custom_call_target="tpu_custom_call" | custom-call | flops 301989888 | bytes 4718592 | tf_op jit(solution)/shard_map/inverse_rest/pallas_call | solution.py:946
  75.2 0.1 collective-permute-start.17
  75.3 0.6 collective-permute-start.18
  75.8 1.0 %near_field.3.refs_8_ = f32[8,128]{1,0:T(8,128)S(1)} custom-call(s32[24]{0:T(128)S(1)} %get-tuple-element.100.place_ref, s32[24]{0:T(128)S(1)} %get-tuple-element.99.target_ref, s16[432,128]{1,0:T(8,128)(2,1)S(1)} %collective-permute-done.15.even_ref.refs_2_.refs_0_, s16[592,128]{1,0:T(8,128)(2,1)S(1)} %collective-permute-done.14.odd_ref.refs_3_.refs_1_, ...), custom_call_target="tpu_custom_call" | custom-call | flops 12582912 | bytes 786432 | tf_op jit(solution)/shard_map/near_field/pallas_call | solution.py:1125
  76.9 2.3 %collective-permute-done.19.refs_1_ = s16[672,128]{1,0:T(8,128)(2,1)S(1)} collective-permute-done((s16[672,128]{1,0:T(8,128)(2,1)S(1)}, s16[672,128]{1,0:T(8,128)(2,1)S(1)}, u32[]{:S(2)}, u32[]{:S(2)}) %collective-permute-start.19) | collective-permute-done | bytes 172064 | tf_op jit(solution)/shard_map/ppermute | solution.py:1191
  79.1 0.4 sample_early.3.refs_2_
  79.6 2.5 %collective-permute-done.18.refs_1_ = s16[672,128]{1,0:T(8,128)(2,1)S(1)} collective-permute-done((s16[672,128]{1,0:T(8,128)(2,1)S(1)}, s16[672,128]{1,0:T(8,128)(2,1)S(1)}, u32[]{:S(2)}, u32[]{:S(2)}) %collective-permute-start.18) | collective-permute-done | bytes 172064 | tf_op jit(solution)/shard_map/ppermute | solution.py:1191
  82.1 2.7 %sample.3 = f32[2,512]{1,0:T(2,128)} custom-call(s32[2,512]{1,0:T(2,128)S(1)} %get-tuple-element.52.place_ref.place_in.refs_1_, s16[672,128]{1,0:T(8,128)(2,1)S(1)} %collective-permute-done.17.refs_0_, s16[672,128]{1,0:T(8,128)(2,1)S(1)} %collective-permute-done.18.refs_1_, f32[656,256]{1,0:T(8,128)S(1)} %sample_early.3.refs_2_, ...), custom_call_target="tpu_custom_call" | custom-call | flops 169869312 | bytes 4194304 | tf_op jit(solution)/shard_map/sample/pallas_call | solution.py:1067
  (22 shorter events, 0.1 us)
Async XLA Ops:
  5.0 9.2 %collective-permute-start.1 = (s16[672,128]{1,0:T(8,128)(2,1)S(1)}, s16[672,128]{1,0:T(8,128)(2,1)S(1)}, u32[]{:S(2)}, u32[]{:S(2)}) collective-permute-start(s16[672,128]{1,0:T(8,128)(2,1)S(1)} %get-tuple-element.60), channel_id=1, source_target_pairs={{0,2},{1,3},{2,0},{3,1},{4,6},{5,7},{6,4},{7,5},{8,10},{9,11},{10,... | collective-permute-start | bytes 516104 | tf_op jit(solution)/shard_map/ppermute | solution.py:1191
  8.6 6.3 %collective-permute-start = (s16[672,128]{1,0:T(8,128)(2,1)S(1)}, s16[672,128]{1,0:T(8,128)(2,1)S(1)}, u32[]{:S(2)}, u32[]{:S(2)}) collective-permute-start(s16[672,128]{1,0:T(8,128)(2,1)S(1)} %get-tuple-element.59), channel_id=1, source_target_pairs={{0,1},{1,0},{2,3},{3,2},{4,5},{5,4},{6,7},{7,6},{8,9},{9,8},{10,11... | collective-permute-start | bytes 516104 | tf_op jit(solution)/shard_map/ppermute | solution.py:1191
  8.7 6.8 %collective-permute-start.2 = (s16[672,128]{1,0:T(8,128)(2,1)S(1)}, s16[672,128]{1,0:T(8,128)(2,1)S(1)}, u32[]{:S(2)}, u32[]{:S(2)}) collective-permute-start(s16[672,128]{1,0:T(8,128)(2,1)S(1)} %get-tuple-element.61), channel_id=1, source_target_pairs={{0,3},{1,2},{2,1},{3,0},{4,7},{5,6},{6,5},{7,4},{8,11},{9,10},{10,... | collective-permute-start | bytes 516104 | tf_op jit(solution)/shard_map/ppermute | solution.py:1191
  8.8 0.9 %copy-start.1 = (f32[64,512]{1,0:T(8,128)S(1)}, f32[64,512]{1,0:T(8,128)}, u32[]{:S(2)}) copy-start(f32[64,512]{1,0:T(8,128)} %refs_3_.8) | copy-start | bytes 393220
  9.7 4.5 %copy-start = (bf16[2,256,240]{2,1,0:T(8,128)(2,1)S(1)}, bf16[2,256,240]{2,1,0:T(8,128)(2,1)}, u32[]{:S(2)}) copy-start(bf16[2,256,240]{2,1,0:T(8,128)(2,1)} %constant.76.clone.refs_2_.refs_6_.table_ref) | copy-start | bytes 737284
  15.5 15.1 %copy-start.3 = (bf16[4,48,256]{2,1,0:T(8,128)(2,1)S(1)}, bf16[4,48,256]{2,1,0:T(8,128)(2,1)}, u32[]{:S(2)}) copy-start(bf16[4,48,256]{2,1,0:T(8,128)(2,1)} %constant.77.clone.refs_7_.high_ref) | copy-start | bytes 294916
  15.5 15.1 %copy-start.4 = (bf16[4,48,256]{2,1,0:T(8,128)(2,1)S(1)}, bf16[4,48,256]{2,1,0:T(8,128)(2,1)}, u32[]{:S(2)}) copy-start(bf16[4,48,256]{2,1,0:T(8,128)(2,1)} %constant.78.clone.refs_8_.low_ref) | copy-start | bytes 294916
  17.0 6.9 %collective-permute-start.5 = (s16[432,128]{1,0:T(8,128)(2,1)S(1)}, s16[432,128]{1,0:T(8,128)(2,1)S(1)}, u32[]{:S(2)}, u32[]{:S(2)}) collective-permute-start(s16[432,128]{1,0:T(8,128)(2,1)S(1)} %get-tuple-element.67), channel_id=1, source_target_pairs={{0,4},{8,12},{4,0},{12,8},{1,5},{9,13},{5,1},{13,9},{2,6},{10,14},... | collective-permute-start | bytes 331784 | tf_op jit(solution)/shard_map/ppermute | solution.py:1203
  18.6 8.0 %collective-permute-start.4 = (s16[592,128]{1,0:T(8,128)(2,1)S(1)}, s16[592,128]{1,0:T(8,128)(2,1)S(1)}, u32[]{:S(2)}, u32[]{:S(2)}) collective-permute-start(s16[592,128]{1,0:T(8,128)(2,1)S(1)} %get-tuple-element.66), channel_id=1, source_target_pairs={{4,8},{8,4},{5,9},{9,5},{6,10},{10,6},{7,11},{11,7},{20,24},{24,20... | collective-permute-start | bytes 454664 | tf_op jit(solution)/shard_map/ppermute | solution.py:1204
  19.4 7.1 %collective-permute-start.3 = (s16[304,128]{1,0:T(8,128)(2,1)S(1)}, s16[304,128]{1,0:T(8,128)(2,1)S(1)}, u32[]{:S(2)}, u32[]{:S(2)}) collective-permute-start(s16[304,128]{1,0:T(8,128)(2,1)S(1)} %get-tuple-element.65), channel_id=1, source_target_pairs={{0,4},{8,12},{4,0},{12,8},{1,5},{9,13},{5,1},{13,9},{2,6},{10,14},... | collective-permute-start | bytes 233480 | tf_op jit(solution)/shard_map/ppermute | solution.py:1205
  24.1 10.1 %copy-start.8 = (s32[24]{0:T(128)S(1)}, s32[24]{0:T(128)}, u32[]{:S(2)}) copy-start(s32[24]{0:T(128)} %param.21) | copy-start | bytes 292
  24.1 10.1 %copy-start.9 = (s32[24]{0:T(128)S(1)}, s32[24]{0:T(128)}, u32[]{:S(2)}) copy-start(s32[24]{0:T(128)} %param.22) | copy-start | bytes 292
  24.1 6.5 %collective-permute-start.6 = (s16[272,128]{1,0:T(8,128)(2,1)S(1)}, s16[272,128]{1,0:T(8,128)(2,1)S(1)}, u32[]{:S(2)}, u32[]{:S(2)}) collective-permute-start(s16[272,128]{1,0:T(8,128)(2,1)S(1)} %pair_messages.2), channel_id=1, source_target_pairs={{0,8},{4,12},{8,0},{12,4},{1,9},{5,13},{9,1},{13,5},{2,10},{6,14},... | collective-permute-start | bytes 208904 | tf_op jit(solution)/shard_map/ppermute | solution.py:1207
  30.6 5.3 %copy-start.2 = (bf16[24,128,128]{2,1,0:T(8,128)(2,1)S(1)}, bf16[24,128,128]{2,1,0:T(8,128)(2,1)}, u32[]{:S(2)}) copy-start(bf16[24,128,128]{2,1,0:T(8,128)(2,1)} %refs_3_.10) | copy-start | bytes 2359300
  32.6 7.2 %collective-permute-start.9 = (s16[672,128]{1,0:T(8,128)(2,1)S(1)}, s16[672,128]{1,0:T(8,128)(2,1)S(1)}, u32[]{:S(2)}, u32[]{:S(2)}) collective-permute-start(s16[672,128]{1,0:T(8,128)(2,1)S(1)} %get-tuple-element.75), channel_id=1, source_target_pairs={{0,2},{1,3},{2,0},{3,1},{4,6},{5,7},{6,4},{7,5},{8,10},{9,11},{10,... | collective-permute-start | bytes 516104 | tf_op jit(solution)/shard_map/ppermute | solution.py:1191
  35.1 5.2 %collective-permute-start.7 = (s16[672,128]{1,0:T(8,128)(2,1)S(1)}, s16[672,128]{1,0:T(8,128)(2,1)S(1)}, u32[]{:S(2)}, u32[]{:S(2)}) collective-permute-start(s16[672,128]{1,0:T(8,128)(2,1)S(1)} %get-tuple-element.72), channel_id=1, source_target_pairs={{0,1},{1,0},{2,3},{3,2},{4,5},{5,4},{6,7},{7,6},{8,9},{9,8},{10,11... | collective-permute-start | bytes 516104 | tf_op jit(solution)/shard_map/ppermute | solution.py:1191
  35.2 6.8 %collective-permute-start.8 = (s16[672,128]{1,0:T(8,128)(2,1)S(1)}, s16[672,128]{1,0:T(8,128)(2,1)S(1)}, u32[]{:S(2)}, u32[]{:S(2)}) collective-permute-start(s16[672,128]{1,0:T(8,128)(2,1)S(1)} %get-tuple-element.73), channel_id=1, source_target_pairs={{0,3},{1,2},{2,1},{3,0},{4,7},{5,6},{6,5},{7,4},{8,11},{9,10},{10,... | collective-permute-start | bytes 516104 | tf_op jit(solution)/shard_map/ppermute | solution.py:1191
  36.9 3.0 %copy-start.5 = (bf16[4,128,256]{2,1,0:T(8,128)(2,1)S(1)}, bf16[4,128,256]{2,1,0:T(8,128)(2,1)}, u32[]{:S(2)}) copy-start(bf16[4,128,256]{2,1,0:T(8,128)(2,1)} %constant.79.clone.refs_2_.refs_3_) | copy-start | bytes 786436
  36.9 3.0 %copy-start.6 = (bf16[4,128,256]{2,1,0:T(8,128)(2,1)S(1)}, bf16[4,128,256]{2,1,0:T(8,128)(2,1)}, u32[]{:S(2)}) copy-start(bf16[4,128,256]{2,1,0:T(8,128)(2,1)} %constant.80.clone.refs_3_.refs_4_) | copy-start | bytes 786436
  39.9 2.1 %copy-start.7 = (s32[512]{0:T(512)S(1)}, s32[512]{0:T(512)}, u32[]{:S(2)}) copy-start(s32[512]{0:T(512)} %param.17) | copy-start | bytes 6148
  46.8 7.2 %collective-permute-start.11 = (s16[672,128]{1,0:T(8,128)(2,1)S(1)}, s16[672,128]{1,0:T(8,128)(2,1)S(1)}, u32[]{:S(2)}, u32[]{:S(2)}) collective-permute-start(s16[672,128]{1,0:T(8,128)(2,1)S(1)} %get-tuple-element.82), channel_id=1, source_target_pairs={{0,2},{1,3},{2,0},{3,1},{4,6},{5,7},{6,4},{7,5},{8,10},{9,11},{10,... | collective-permute-start | bytes 516104 | tf_op jit(solution)/shard_map/ppermute | solution.py:1191
  48.6 6.1 %collective-permute-start.10 = (s16[672,128]{1,0:T(8,128)(2,1)S(1)}, s16[672,128]{1,0:T(8,128)(2,1)S(1)}, u32[]{:S(2)}, u32[]{:S(2)}) collective-permute-start(s16[672,128]{1,0:T(8,128)(2,1)S(1)} %get-tuple-element.81), channel_id=1, source_target_pairs={{0,1},{1,0},{2,3},{3,2},{4,5},{5,4},{6,7},{7,6},{8,9},{9,8},{10,11... | collective-permute-start | bytes 516104 | tf_op jit(solution)/shard_map/ppermute | solution.py:1191
  49.2 7.7 %collective-permute-start.12 = (s16[672,128]{1,0:T(8,128)(2,1)S(1)}, s16[672,128]{1,0:T(8,128)(2,1)S(1)}, u32[]{:S(2)}, u32[]{:S(2)}) collective-permute-start(s16[672,128]{1,0:T(8,128)(2,1)S(1)} %get-tuple-element.83), channel_id=1, source_target_pairs={{0,3},{1,2},{2,1},{3,0},{4,7},{5,6},{6,5},{7,4},{8,11},{9,10},{10,... | collective-permute-start | bytes 516104 | tf_op jit(solution)/shard_map/ppermute | solution.py:1191
  58.4 5.6 %collective-permute-start.15 = (s16[432,128]{1,0:T(8,128)(2,1)S(1)}, s16[432,128]{1,0:T(8,128)(2,1)S(1)}, u32[]{:S(2)}, u32[]{:S(2)}) collective-permute-start(s16[432,128]{1,0:T(8,128)(2,1)S(1)} %get-tuple-element.89), channel_id=1, source_target_pairs={{0,4},{8,12},{4,0},{12,8},{1,5},{9,13},{5,1},{13,9},{2,6},{10,14},... | collective-permute-start | bytes 331784 | tf_op jit(solution)/shard_map/ppermute | solution.py:1203
  58.5 8.1 %collective-permute-start.14 = (s16[592,128]{1,0:T(8,128)(2,1)S(1)}, s16[592,128]{1,0:T(8,128)(2,1)S(1)}, u32[]{:S(2)}, u32[]{:S(2)}) collective-permute-start(s16[592,128]{1,0:T(8,128)(2,1)S(1)} %get-tuple-element.88), channel_id=1, source_target_pairs={{4,8},{8,4},{5,9},{9,5},{6,10},{10,6},{7,11},{11,7},{20,24},{24,20... | collective-permute-start | bytes 454664 | tf_op jit(solution)/shard_map/ppermute | solution.py:1204
  59.4 7.2 %collective-permute-start.13 = (s16[304,128]{1,0:T(8,128)(2,1)S(1)}, s16[304,128]{1,0:T(8,128)(2,1)S(1)}, u32[]{:S(2)}, u32[]{:S(2)}) collective-permute-start(s16[304,128]{1,0:T(8,128)(2,1)S(1)} %get-tuple-element.87), channel_id=1, source_target_pairs={{0,4},{8,12},{4,0},{12,8},{1,5},{9,13},{5,1},{13,9},{2,6},{10,14},... | collective-permute-start | bytes 233480 | tf_op jit(solution)/shard_map/ppermute | solution.py:1205
  64.1 6.4 %collective-permute-start.16 = (s16[272,128]{1,0:T(8,128)(2,1)S(1)}, s16[272,128]{1,0:T(8,128)(2,1)S(1)}, u32[]{:S(2)}, u32[]{:S(2)}) collective-permute-start(s16[272,128]{1,0:T(8,128)(2,1)S(1)} %pair_messages.3), channel_id=1, source_target_pairs={{0,8},{4,12},{8,0},{12,4},{1,9},{5,13},{9,1},{13,5},{2,10},{6,14},... | collective-permute-start | bytes 208904 | tf_op jit(solution)/shard_map/ppermute | solution.py:1207
  72.6 6.5 %collective-permute-start.19 = (s16[672,128]{1,0:T(8,128)(2,1)S(1)}, s16[672,128]{1,0:T(8,128)(2,1)S(1)}, u32[]{:S(2)}, u32[]{:S(2)}) collective-permute-start(s16[672,128]{1,0:T(8,128)(2,1)S(1)} %get-tuple-element.97), channel_id=1, source_target_pairs={{0,2},{1,3},{2,0},{3,1},{4,6},{5,7},{6,4},{7,5},{8,10},{9,11},{10,... | collective-permute-start | bytes 516104 | tf_op jit(solution)/shard_map/ppermute | solution.py:1191
  75.2 4.4 %collective-permute-start.17 = (s16[672,128]{1,0:T(8,128)(2,1)S(1)}, s16[672,128]{1,0:T(8,128)(2,1)S(1)}, u32[]{:S(2)}, u32[]{:S(2)}) collective-permute-start(s16[672,128]{1,0:T(8,128)(2,1)S(1)} %get-tuple-element.94), channel_id=1, source_target_pairs={{0,1},{1,0},{2,3},{3,2},{4,5},{5,4},{6,7},{7,6},{8,9},{9,8},{10,11... | collective-permute-start | bytes 516104 | tf_op jit(solution)/shard_map/ppermute | solution.py:1191
  75.3 6.8 %collective-permute-start.18 = (s16[672,128]{1,0:T(8,128)(2,1)S(1)}, s16[672,128]{1,0:T(8,128)(2,1)S(1)}, u32[]{:S(2)}, u32[]{:S(2)}) collective-permute-start(s16[672,128]{1,0:T(8,128)(2,1)S(1)} %get-tuple-element.95), channel_id=1, source_target_pairs={{0,3},{1,2},{2,1},{3,0},{4,7},{5,6},{6,5},{7,4},{8,11},{9,10},{10,... | collective-permute-start | bytes 516104 | tf_op jit(solution)/shard_map/ppermute | solution.py:1191

commit v16 on v15

--- a/solution.py
+++ b/solution.py
@@ -522,14 +522,24 @@
         stacked[pl.ds(pl.multiple_of(i * tall + place, 8), reach_y), :] = layer
 
 
-def stack_pieces(parts, reach_x, reach_y, top, opened, stacked, edges, places):
+def transform_flips(parts, flips, reach_x, reach_y, table_ref, before, spectrum, edges, scratch):
+    opened, stacked = scratch
+    top = parts[0].shape[0] - opened.shape[0]
+    pair = lax.axis_size("pair")
     chip = lax.axis_index("narrow")
-    for flip, (part, place) in enumerate(zip(parts, places)):
-        first = from_short(part[:top, :])
-        opened[...] = from_short(part[top:, :]) * unit(first[0:1], first[1:2])
-        layers = [opened[i * reach_y : (i + 1) * reach_y, :] for i in range(reach_x // 2)]
-        stack_layers(layers, chip ^ flip, reach_y, stacked)
-        put_edges(opened, reach_x, reach_y, edges, place * 2 * reach_y)
+    for core in range(pair):
+        mine = [(flip, part) for flip, part in zip(flips, parts) if flip % pair == core]
+        if not mine:
+            continue
+        stacked[...] = jnp.zeros_like(stacked)
+        for flip, part in mine:
+            first = from_short(part[:top, :])
+            opened[...] = from_short(part[top:, :]) * unit(first[0:1], first[1:2])
+            layers = [opened[i * reach_y : (i + 1) * reach_y, :] for i in range(reach_x // 2)]
+            stack_layers(layers, chip ^ (flip // pair), reach_y, stacked)
+            put_edges(opened, reach_x, reach_y, edges, flip * 2 * reach_y)
+        transform_pieces(table_ref[lax.axis_index("pair") ^ core], stacked, before, spectrum)
+        before = spectrum
 
 
 def transform_pieces(table, stacked, before, spectrum):
@@ -549,13 +559,11 @@
             spectrum[j] = made if before is None else before[j] + made
 
 
-def forward_early_kernel(reach_x, reach_y, chips, *refs):
-    parts = refs[:chips]
-    table_ref, spectrum, edges, opened, stacked = refs[chips:]
-    top = parts[0].shape[0] - opened.shape[0]
-    stacked[...] = jnp.zeros_like(stacked)
-    stack_pieces(parts, reach_x, reach_y, top, opened, stacked, edges, range(chips))
-    transform_pieces(table_ref[lax.axis_index("pair")], stacked, None, spectrum)
+def forward_early_kernel(reach_x, reach_y, flips, *refs):
+    parts = refs[: len(flips)]
+    table_ref, spectrum, edges, *scratch = refs[len(flips) :]
+    edges[...] = jnp.zeros_like(edges)
+    transform_flips(parts, flips, reach_x, reach_y, table_ref, None, spectrum, edges, scratch)
 
 
 def stacking_scratch(chips, reach_x, reach_y):
@@ -566,34 +574,31 @@
     ]
 
 
-def forward_early(parts, table, reach_x, reach_y):
+def forward_early(parts, flips, pieces, table, reach_x, reach_y):
     half = reach_x // 2
-    chips = len(parts)
     return pl.pallas_call(
-        functools.partial(forward_early_kernel, reach_x, reach_y, chips),
-        in_specs=[whole_vmem()] * (chips + 1),
+        functools.partial(forward_early_kernel, reach_x, reach_y, flips),
+        in_specs=[whole_vmem()] * (len(flips) + 1),
         out_specs=[whole_vmem()] * 2,
         out_shape=[
             jax.ShapeDtypeStruct((half, GRID, 2 * HALF), F32),
-            jax.ShapeDtypeStruct((2, chips * 2 * reach_y, 2 * HALF), F32),
+            jax.ShapeDtypeStruct((2, pieces * 2 * reach_y, 2 * HALF), F32),
         ],
-        scratch_shapes=stacking_scratch(chips, reach_x, reach_y),
+        scratch_shapes=stacking_scratch(pieces // table.shape[0], reach_x, reach_y),
         compiler_params=params(),
         cost_estimate=cost(EARLY_FLOPS, 4 * half * GRID * 2 * HALF * 2),
         name="forward_early",
     )(*parts, table)
 
 
-def forward_kernel(reach_x, reach_y, blocks, pieces, awaited, *refs):
+def forward_kernel(reach_x, reach_y, blocks, pieces, late, awaited, *refs):
     parts = refs[:pieces]
     early_ref, early_edges, table_ref, modes_ref = refs[pieces : pieces + 4]
     refs = refs[pieces + 4 + awaited :]
     spectrum, even_out, layers_out, odd_out, own_out, peers_out, inner_out, *refs = refs
     opened, stacked, edges, slabs, head = refs
     half = reach_x // 2
-    pair = lax.axis_size("pair")
     top = parts[0].shape[0] - opened.shape[0]
-    stacked[...] = jnp.zeros_like(stacked)
     head[...] = jnp.zeros_like(head)
     for piece in range(pieces):
         first = from_short(parts[piece][:top, :])
@@ -602,18 +607,12 @@
         at = 6 + 2 * piece * blocks
         head[at : at + blocks, :] = mantissa
         head[at + blocks : at + 2 * blocks, :] = exponent
-    rows = 2 * reach_y
-    for chip in range(pieces // pair):
-        place = chip * pair * rows
-        edges[:, place : place + rows, :] = early_edges[:, chip * rows : (chip + 1) * rows, :]
-    before = early_ref
-    for core in range(1, pair):
-        places = range(core, pieces, pair)
-        stack_pieces(parts[core::pair], reach_x, reach_y, top, opened, stacked, edges, places)
-        transform_pieces(table_ref[lax.axis_index("pair") ^ core], stacked, before, spectrum)
-        before = spectrum
-
-    chunk = 128
+    edges[...] = early_edges[...]
+    held = [parts[flip] for flip in late]
+    scratch = (opened, stacked)
+    transform_flips(held, late, reach_x, reach_y, table_ref, early_ref, spectrum, edges, scratch)
+
+    chunk = 256
 
     def body(index, largest):
         rows = pl.ds(pl.multiple_of(index * chunk, chunk), chunk)
@@ -680,7 +679,7 @@
             send(odd_out, top, [(slabs[odd], largest[odd]), with_most(edges[1 - odd])])
 
 
-def forward(parts, early, early_edges, table, modes, reach_x, reach_y, blocks, awaited):
+def forward(parts, late, early, early_edges, table, modes, reach_x, reach_y, blocks, awaited):
     pieces = len(parts)
     half = reach_x // 2
     lanes = 2 * HALF
@@ -689,7 +688,7 @@
     short = lambda rows: jax.ShapeDtypeStruct((rows, lanes), jnp.int16)
     return pl.pallas_call(
         functools.partial(
-            forward_kernel, reach_x, reach_y, blocks, pieces, len(awaited)
+            forward_kernel, reach_x, reach_y, blocks, pieces, late, len(awaited)
         ),
         in_specs=[whole_vmem()] * (pieces + 4) + [anywhere()] * len(awaited),
         out_specs=[whole_vmem()] * 7,
@@ -838,7 +837,7 @@
     field_high, field_low, ready, head = refs[3 + len(flips) :]
     half = reach_x // 2
     span = reach_x - 4
-    chunk = 128
+    chunk = 256
     head_rows = from_even.shape[0] - GRID - GRID // 2
     on_left = (lax.axis_index("wide") & 1) == 1
     moment_units = []
@@ -1180,9 +1179,8 @@
     odd_swap = swaps([(i, i + 1) for i in range(1, x_count - 1, 2)])
     far_flips = list(range(2, x_count, 2))
 
-    first, rest = list(range(pair, y_count)), list(range(pair))
-    same_core = list(range(0, y_count, pair))
-    other_core = [flip for flip in range(y_count) if flip not in same_core]
+    first, rest = list(range(1, y_count)), [0]
+    early_flips, late_flips = list(range(y_count - 1)), [y_count - 1]
 
     def turned(sent, then):
         arrived = [None] * y_count
@@ -1196,9 +1194,20 @@
 
     def convolve_and_sample(last, vector, sent, both, table, places, sample_lines, awaited):
         arrived = turned(sent, spread_rest(vector, both, table, rest))
-        early, edges = forward_early(chosen(arrived, same_core), y_forward, reach_x, reach_y)
+        early, edges = forward_early(
+            chosen(arrived, early_flips), early_flips, y_count, y_forward, reach_x, reach_y
+        )
         spectrum, even_message, layers, odd_message, own, peers, inner = forward(
-            arrived, early, edges, y_forward, modes, reach_x, reach_y, blocks, awaited
+            arrived,
+            late_flips,
+            early,
+            edges,
+            y_forward,
+            modes,
+            reach_x,
+            reach_y,
+            blocks,
+            awaited,
         )
         from_even = lax.ppermute(even_message, "wide", even_swap)
         from_odd = lax.ppermute(odd_message, "wide", odd_swap)
@@ -1231,9 +1240,9 @@
         image = sample(
             last,
             places,
-            chosen(arrived, other_core),
-            other_core,
-            sample_early(chosen(arrived, same_core), same_core, z_inverse),
+            chosen(arrived, late_flips),
+            late_flips,
+            sample_early(chosen(arrived, early_flips), early_flips, z_inverse),
             z_inverse,
             sample_lines,
             surface_flag,

time: 85.2 us -> 87.3 us (1.025)
  waiting for transfers between devices: 23.1 us -> 25 us
  Pallas kernels: 34.4 us -> 35.4 us
    ppermute x12, waiting for transfers between devices: 13.5 us -> 15.6 us  [turned(): lax.ppermute(part, Y_AXES, swap_pairs)]
    ppermute x12, starting transfers between devices: 10 us -> 9.03 us  [turned(): lax.ppermute(part, Y_AXES, swap_pairs)]
  transfers between devices with their start and end apart: 20 -> 20, of which waited for: 10 -> 11; matrix products, arithmetic and copies ran while one was open for 1% -> 1% of each run, Pallas kernels for 17% -> 18%
where the time goes in v16:
time: 87.3 us; the launch traced here: 87.1 us
  Pallas kernels  35.4 us (41%)
  waiting for transfers between devices  25 us (29%)
  starting transfers between devices  24.1 us (28%)
  local copies, waits for them, and re-layouts  2.03 us (2%)
    ppermute x12, waiting for transfers between devices, turned(): lax.ppermute(part, Y_AXES, swap_pairs)  15.6 us
    ppermute x2, starting transfers between devices, convolve_and_sample(): even_layers = lax.ppermute(layers, 'wide', even_swap)  9.49 us
    ppermute x12, starting transfers between devices, turned(): lax.ppermute(part, Y_AXES, swap_pairs)  9.03 us
    pallas_call x2, Pallas kernels, spread(): pl.pallas_call(functools.partial(start_kernel if placed is None else spre...  8.3 us
    ppermute x2, waiting for transfers between devices, convolve_and_sample(): lax.ppermute(message, 'wide', [(i, i ^ flip) for i in range(x_count)])  6.75 us
    pallas_call x2, Pallas kernels, sample(): pl.pallas_call(functools.partial(sample_kernel, last, reach_x, reach_y, f...  4.86 us
    pallas_call x2, Pallas kernels, inverse(): pl.pallas_call(functools.partial(inverse_kernel, reach_x, reach_y, flips,...  3.92 us
    pallas_call x1, Pallas kernels, place_sample_lines(): pl.pallas_call(functools.partial(sample_lines_kernel, blocks), grid=(1,),...  3.41 us
  transfers between devices with their start and end apart: 20, of which 11 were waited for; matrix products, arithmetic and copies ran while one was open for 1% of the time, Pallas kernels for 18%

profile of v16, /device:TPU:0, one launch (start us, length us, event | category | flops | bytes accessed | tf_op | source)
XLA Modules:
  0.0 87.1 jit_solution(8009472454517996615)
XLA Ops:
  0.0 5.3 %start.1 = (s16[672,128]{1,0:T(8,128)(2,1)S(1)}, s16[672,128]{1,0:T(8,128)(2,1)S(1)}, s16[672,128]{1,0:T(8,128)(2,1)S(1)}, bf16[656,256]{1,0:T(8,128)(2,1)S(1)},...) custom-call(f32[512]{0:T(512)} %refs_0_.2, ...), custom_call_target="tpu_custom_call" | custom-call | flops 169869312 | bytes 4194304 | tf_op jit(solution)/shard_map/start/pallas_call | solution.py:411
  5.3 0.5 collective-permute-start
  5.9 2.6 %collective-permute-start.1 = (s16[672,128]{1,0:T(8,128)(2,1)S(1)}, s16[672,128]{1,0:T(8,128)(2,1)S(1)}, u32[]{:S(2)}, u32[]{:S(2)}) collective-permute-start(s16[672,128]{1,0:T(8,128)(2,1)S(1)} %get-tuple-element.55), channel_id=1, source_target_pairs={{0,2},{1,3},{2,0},{3,1},{4,6},{5,7},{6,4},{7,5},{8,10},{9,11},{10,... | collective-permute-start | bytes 516104 | tf_op jit(solution)/shard_map/ppermute | solution.py:1189
  8.4 0.1 collective-permute-start.2
  8.5 0.9 %copy-done.1 = f32[64,512]{1,0:T(8,128)S(1)} copy-done((f32[64,512]{1,0:T(8,128)S(1)}, f32[64,512]{1,0:T(8,128)}, u32[]{:S(2)}) %copy-start.1) | copy-done | bytes 131096
  9.4 3.4 %place_sample_lines.1.refs_8_.refs_4_ = f32[8192,128]{1,0:T(8,128)S(1)} custom-call(s32[2,512]{1,0:T(2,128)S(1)} %get-tuple-element.48.place_ref.place_in.refs_1_, f32[64,512]{1,0:T(8,128)S(1)} %copy-done.1, f32[64,512]{1,0:T(8,128)S(1)} %copy-done.1, f32[64,512]{1,0:T(8,128)S(1)} %copy-done.1, f32[64,512]{1,0:T(8,128)S(1)} %copy-done.1), custom_call_target="tpu_custom_call" | custom-call | flops 1048576 | bytes 4194304 | tf_op jit(solution)/shard_map/place_sample_lines/pallas_call | solution.py:480
  12.8 0.5 spread_rest.2.refs_0_
  13.4 1.1 %dynamic-slice_bitcast_fusion.refs_7_.modes_ref.refs_9_ = f32[4,256,128]{2,1,0:T(8,128)S(1)} fusion(f32[4,4,256,128]{3,2,1,0:T(8,128)} %constant.73.clone, s32[]{:T(128)S(6)} %select_n.30), kind=kLoop, calls=%fused_computation | loop fusion | bytes 1048580 | tf_op jit(solution)/shard_map/jit(dynamic_index_in_dim)/squeeze | solution.py:1167
  14.5 0.0 collective-permute-done.1.refs_2_
  14.5 1.1 %forward_early.2 = (f32[18,256,128]{2,1,0:T(8,128)S(1)}, f32[2,288,128]{2,1,0:T(8,128)S(1)}) custom-call(s16[672,128]{1,0:T(8,128)(2,1)S(1)} %spread_rest.2.refs_0_, s16[672,128]{1,0:T(8,128)(2,1)S(1)} %collective-permute-done.refs_1_, s16[672,128]{1,0:T(8,128)(2,1)S(1)} %collective-permute-done.1.refs_2_, bf16[2,256,240]{2,1,0:T(8,128)(2,1)S(1)} %copy-done), custom_call_target="tpu_custom_call" | custom-call | flops 5000000000 | bytes 4718592 | tf_op jit(solution)/shard_map/forward_early/pallas_call | solution.py:579
  15.6 1.3 %collective-permute-done.2.refs_3_ = s16[672,128]{1,0:T(8,128)(2,1)S(1)} collective-permute-done((s16[672,128]{1,0:T(8,128)(2,1)S(1)}, s16[672,128]{1,0:T(8,128)(2,1)S(1)}, u32[]{:S(2)}, u32[]{:S(2)}) %collective-permute-start.2) | collective-permute-done | bytes 172064 | tf_op jit(solution)/shard_map/ppermute | solution.py:1189
  16.8 1.2 %forward.2 = (f32[18,256,128]{2,1,0:T(8,128)S(1)}, s16[432,128]{1,0:T(8,128)(2,1)S(1)}, s16[304,128]{1,0:T(8,128)(2,1)S(1)}, s16[592,128]{1,0:T(8,128)(2,1)S(1)}...) custom-call(s16[672,128]{1,0:T(8,128)(2,1)S(1)} %spread_rest.2.refs_0_, ...), custom_call_target="tpu_custom_call" | custom-call | flops 301989888 | bytes 4718592 | tf_op jit(solution)/shard_map/forward/pallas_call | solution.py:689
  18.1 1.7 %collective-permute-start.5 = (s16[432,128]{1,0:T(8,128)(2,1)S(1)}, s16[432,128]{1,0:T(8,128)(2,1)S(1)}, u32[]{:S(2)}, u32[]{:S(2)}) collective-permute-start(s16[432,128]{1,0:T(8,128)(2,1)S(1)} %get-tuple-element.62), channel_id=1, source_target_pairs={{0,4},{8,12},{4,0},{12,8},{1,5},{9,13},{5,1},{13,9},{2,6},{10,14},... | collective-permute-start | bytes 331784 | tf_op jit(solution)/shard_map/ppermute | solution.py:1212
  19.8 0.8 collective-permute-start.4
  20.7 4.4 %collective-permute-start.3 = (s16[304,128]{1,0:T(8,128)(2,1)S(1)}, s16[304,128]{1,0:T(8,128)(2,1)S(1)}, u32[]{:S(2)}, u32[]{:S(2)}) collective-permute-start(s16[304,128]{1,0:T(8,128)(2,1)S(1)} %get-tuple-element.60), channel_id=1, source_target_pairs={{0,4},{8,12},{4,0},{12,8},{1,5},{9,13},{5,1},{13,9},{2,6},{10,14},... | collective-permute-start | bytes 233480 | tf_op jit(solution)/shard_map/ppermute | solution.py:1214
  25.1 0.0 collective-permute-done.5.even_ref.refs_2_.refs_0_
  25.1 0.2 pair_messages.2
  25.3 0.0 copy-start.8
  25.3 0.0 copy-start.9
  25.3 1.0 %collective-permute-start.6 = (s16[272,128]{1,0:T(8,128)(2,1)S(1)}, s16[272,128]{1,0:T(8,128)(2,1)S(1)}, u32[]{:S(2)}, u32[]{:S(2)}) collective-permute-start(s16[272,128]{1,0:T(8,128)(2,1)S(1)} %pair_messages.2), channel_id=1, source_target_pairs={{0,8},{4,12},{8,0},{12,4},{1,9},{5,13},{9,1},{13,5},{2,10},{6,14},... | collective-permute-start | bytes 208904 | tf_op jit(solution)/shard_map/ppermute | solution.py:1216
  26.3 1.2 %collective-permute-done.3.layers_ref = s16[304,128]{1,0:T(8,128)(2,1)S(1)} collective-permute-done((s16[304,128]{1,0:T(8,128)(2,1)S(1)}, s16[304,128]{1,0:T(8,128)(2,1)S(1)}, u32[]{:S(2)}, u32[]{:S(2)}) %collective-permute-start.3) | collective-permute-done | bytes 77856 | tf_op jit(solution)/shard_map/ppermute | solution.py:1214
  27.5 0.0 collective-permute-done.4.odd_ref.refs_3_.refs_1_
  27.5 0.4 borders.2.refs_1_
  27.9 3.4 %collective-permute-done.6.refs_6_ = s16[272,128]{1,0:T(8,128)(2,1)S(1)} collective-permute-done((s16[272,128]{1,0:T(8,128)(2,1)S(1)}, s16[272,128]{1,0:T(8,128)(2,1)S(1)}, u32[]{:S(2)}, u32[]{:S(2)}) %collective-permute-start.6) | collective-permute-done | bytes 69664 | tf_op jit(solution)/shard_map/ppermute | solution.py:1216
  31.4 1.9 %inverse.2 = (s16[672,128]{1,0:T(8,128)(2,1)S(1)}, s16[672,128]{1,0:T(8,128)(2,1)S(1)}, s16[672,128]{1,0:T(8,128)(2,1)S(1)}, bf16[18,256,128]{2,1,0:T(8,128)(2,1)S(1)}, bf16[18,256,128]{2,1,0:T(8,128)(2,1)S(1)}) custom-call(f32[18,256,128]{2,1,0:T(8,128)S(1)} %get-tuple-element.59.refs_0_, f32[4,256,128]{2,1,0:T(8,128)S(1)} %borders.2.refs_1_, ...), custom_call_target="tpu_custom_call" | custom-call | flops 301989888 | bytes 4718592 | tf_op jit(solution)/shard_map/inverse/pallas_call | solution.py:921
  33.3 0.0 copy-start.2
  33.3 0.1 collective-permute-start.8
  33.4 1.6 %collective-permute-start.9 = (s16[672,128]{1,0:T(8,128)(2,1)S(1)}, s16[672,128]{1,0:T(8,128)(2,1)S(1)}, u32[]{:S(2)}, u32[]{:S(2)}) collective-permute-start(s16[672,128]{1,0:T(8,128)(2,1)S(1)} %get-tuple-element.69), channel_id=1, source_target_pairs={{0,2},{1,3},{2,0},{3,1},{4,6},{5,7},{6,4},{7,5},{8,10},{9,11},{10,... | collective-permute-start | bytes 516104 | tf_op jit(solution)/shard_map/ppermute | solution.py:1189
  35.0 0.4 collective-permute-start.7
  35.4 0.8 inverse_rest.2.refs_0_.refs_4_
  36.2 1.1 %near_field.2.refs_7_.refs_0_ = f32[8,128]{1,0:T(8,128)S(1)} custom-call(s32[24]{0:T(128)S(1)} %get-tuple-element.92.place_ref, s32[24]{0:T(128)S(1)} %get-tuple-element.91.target_ref, s16[432,128]{1,0:T(8,128)(2,1)S(1)} %collective-permute-done.5.even_ref.refs_2_.refs_0_, s16[592,128]{1,0:T(8,128)(2,1)S(1)} %collective-permute-done.4.odd_ref.refs_3_.refs_1_, ...), custom_call_target="tpu_custom_call" | custom-call | flops 12582912 | bytes 786432 | tf_op jit(solution)/shard_map/near_field/pallas_call | solution.py:1124
  37.3 3.0 %place_lines.1.refs_5_ = f32[8192,128]{1,0:T(8,128)S(1)} custom-call(s32[2,512]{1,0:T(2,128)S(1)} %get-tuple-element.48.place_ref.place_in.refs_1_, f32[256,128]{1,0:T(8,128)S(1)} %get-tuple-element.71.coeff_ref, f32[8,128]{1,0:T(8,128)S(1)} %near_field.2.refs_7_.refs_0_), custom_call_target="tpu_custom_call" | custom-call | flops 1048576 | bytes 4194304 | tf_op jit(solution)/shard_map/place_lines/pallas_call | solution.py:496
  40.3 0.4 collective-permute-done.9.refs_2_
  40.7 0.7 sample_early.2.refs_1_
  41.4 2.1 %collective-permute-done.7.refs_0_ = s16[672,128]{1,0:T(8,128)(2,1)S(1)} collective-permute-done((s16[672,128]{1,0:T(8,128)(2,1)S(1)}, s16[672,128]{1,0:T(8,128)(2,1)S(1)}, u32[]{:S(2)}, u32[]{:S(2)}) %collective-permute-start.7) | collective-permute-done | bytes 172064 | tf_op jit(solution)/shard_map/ppermute | solution.py:1189
  43.4 2.1 %sample.2.refs_2_.rounded_ref.refs_6_ = f32[4,128]{1,0:T(4,128)S(1)} custom-call(s32[2,512]{1,0:T(2,128)S(1)} %get-tuple-element.48.place_ref.place_in.refs_1_, s16[672,128]{1,0:T(8,128)(2,1)S(1)} %collective-permute-done.7.refs_0_, f32[656,256]{1,0:T(8,128)S(1)} %sample_early.2.refs_1_, bf16[4,128,256]{2,1,0:T(8,128)(2,1)S(1)} %copy-done.5, ...), custom_call_target="tpu_custom_call" | custom-call | flops 169869312 | bytes 4194304 | tf_op jit(solution)/shard_map/sample/pallas_call | solution.py:1066
  45.6 3.0 %spread.1 = (s16[672,128]{1,0:T(8,128)(2,1)S(1)}, s16[672,128]{1,0:T(8,128)(2,1)S(1)}, s16[672,128]{1,0:T(8,128)(2,1)S(1)}, bf16[656,256]{1,0:T(8,128)(2,1)S(1)}, bf16[656,256]{1,0:T(8,128)(2,1)S(1)}) custom-call(f32[512]{0:T(512)S(1)} %bitcast.6, s32[2,512]{1,0:T(2,128)S(1)} %get-tuple-element.48.place_ref.place_in.refs_1_, ...), custom_call_target="tpu_custom_call" | custom-call | flops 169869312 | bytes 4194304 | tf_op jit(solution)/shard_map/spread/pallas_call | solution.py:411
  48.6 0.3 collective-permute-start.10
  48.9 1.5 %collective-permute-start.11 = (s16[672,128]{1,0:T(8,128)(2,1)S(1)}, s16[672,128]{1,0:T(8,128)(2,1)S(1)}, u32[]{:S(2)}, u32[]{:S(2)}) collective-permute-start(s16[672,128]{1,0:T(8,128)(2,1)S(1)} %get-tuple-element.75), channel_id=1, source_target_pairs={{0,2},{1,3},{2,0},{3,1},{4,6},{5,7},{6,4},{7,5},{8,10},{9,11},{10,... | collective-permute-start | bytes 516104 | tf_op jit(solution)/shard_map/ppermute | solution.py:1189
  50.4 0.1 collective-permute-start.12
  50.5 0.5 spread_rest.3.refs_0_
  51.0 0.0 collective-permute-done.10.refs_1_
  51.0 5.1 %collective-permute-done.11.refs_2_ = s16[672,128]{1,0:T(8,128)(2,1)S(1)} collective-permute-done((s16[672,128]{1,0:T(8,128)(2,1)S(1)}, s16[672,128]{1,0:T(8,128)(2,1)S(1)}, u32[]{:S(2)}, u32[]{:S(2)}) %collective-permute-start.11) | collective-permute-done | bytes 172064 | tf_op jit(solution)/shard_map/ppermute | solution.py:1189
  56.1 1.0 %forward_early.3 = (f32[18,256,128]{2,1,0:T(8,128)S(1)}, f32[2,288,128]{2,1,0:T(8,128)S(1)}) custom-call(s16[672,128]{1,0:T(8,128)(2,1)S(1)} %spread_rest.3.refs_0_, s16[672,128]{1,0:T(8,128)(2,1)S(1)} %collective-permute-done.10.refs_1_, s16[672,128]{1,0:T(8,128)(2,1)S(1)} %collective-permute-done.11.refs_2_, bf16[2,256,240]{2,1,0:T(8,128)(2,1)S(1)} %copy-done), custom_call_target="tpu_custom_call" | custom-call | flops 5000000000 | bytes 4718592 | tf_op jit(solution)/shard_map/forward_early/pallas_call | solution.py:579
  57.2 1.2 %collective-permute-done.12.refs_3_ = s16[672,128]{1,0:T(8,128)(2,1)S(1)} collective-permute-done((s16[672,128]{1,0:T(8,128)(2,1)S(1)}, s16[672,128]{1,0:T(8,128)(2,1)S(1)}, u32[]{:S(2)}, u32[]{:S(2)}) %collective-permute-start.12) | collective-permute-done | bytes 172064 | tf_op jit(solution)/shard_map/ppermute | solution.py:1189
  58.4 1.2 %forward.3 = (f32[18,256,128]{2,1,0:T(8,128)S(1)}, s16[432,128]{1,0:T(8,128)(2,1)S(1)}, s16[304,128]{1,0:T(8,128)(2,1)S(1)}, s16[592,128]{1,0:T(8,128)(2,1)S(1)}...) custom-call(s16[672,128]{1,0:T(8,128)(2,1)S(1)} %spread_rest.3.refs_0_, ...), custom_call_target="tpu_custom_call" | custom-call | flops 301989888 | bytes 4718592 | tf_op jit(solution)/shard_map/forward/pallas_call | solution.py:689
  59.6 0.1 collective-permute-start.15
  59.7 0.9 %collective-permute-start.14 = (s16[592,128]{1,0:T(8,128)(2,1)S(1)}, s16[592,128]{1,0:T(8,128)(2,1)S(1)}, u32[]{:S(2)}, u32[]{:S(2)}) collective-permute-start(s16[592,128]{1,0:T(8,128)(2,1)S(1)} %get-tuple-element.81), channel_id=1, source_target_pairs={{4,8},{8,4},{5,9},{9,5},{6,10},{10,6},{7,11},{11,7},{20,24},{24,20... | collective-permute-start | bytes 454664 | tf_op jit(solution)/shard_map/ppermute | solution.py:1213
  60.6 5.0 %collective-permute-start.13 = (s16[304,128]{1,0:T(8,128)(2,1)S(1)}, s16[304,128]{1,0:T(8,128)(2,1)S(1)}, u32[]{:S(2)}, u32[]{:S(2)}) collective-permute-start(s16[304,128]{1,0:T(8,128)(2,1)S(1)} %get-tuple-element.80), channel_id=1, source_target_pairs={{0,4},{8,12},{4,0},{12,8},{1,5},{9,13},{5,1},{13,9},{2,6},{10,14},... | collective-permute-start | bytes 233480 | tf_op jit(solution)/shard_map/ppermute | solution.py:1214
  65.7 0.2 pair_messages.3
  65.8 1.1 %collective-permute-start.16 = (s16[272,128]{1,0:T(8,128)(2,1)S(1)}, s16[272,128]{1,0:T(8,128)(2,1)S(1)}, u32[]{:S(2)}, u32[]{:S(2)}) collective-permute-start(s16[272,128]{1,0:T(8,128)(2,1)S(1)} %pair_messages.3), channel_id=1, source_target_pairs={{0,8},{4,12},{8,0},{12,4},{1,9},{5,13},{9,1},{13,5},{2,10},{6,14},... | collective-permute-start | bytes 208904 | tf_op jit(solution)/shard_map/ppermute | solution.py:1216
  66.9 1.4 %collective-permute-done.13.layers_ref = s16[304,128]{1,0:T(8,128)(2,1)S(1)} collective-permute-done((s16[304,128]{1,0:T(8,128)(2,1)S(1)}, s16[304,128]{1,0:T(8,128)(2,1)S(1)}, u32[]{:S(2)}, u32[]{:S(2)}) %collective-permute-start.13) | collective-permute-done | bytes 77856 | tf_op jit(solution)/shard_map/ppermute | solution.py:1214
  68.3 0.4 borders.3.refs_1_
  68.8 3.3 %collective-permute-done.16.refs_6_ = s16[272,128]{1,0:T(8,128)(2,1)S(1)} collective-permute-done((s16[272,128]{1,0:T(8,128)(2,1)S(1)}, s16[272,128]{1,0:T(8,128)(2,1)S(1)}, u32[]{:S(2)}, u32[]{:S(2)}) %collective-permute-start.16) | collective-permute-done | bytes 69664 | tf_op jit(solution)/shard_map/ppermute | solution.py:1216
  72.1 2.0 %inverse.3 = (s16[672,128]{1,0:T(8,128)(2,1)S(1)}, s16[672,128]{1,0:T(8,128)(2,1)S(1)}, s16[672,128]{1,0:T(8,128)(2,1)S(1)}, bf16[18,256,128]{2,1,0:T(8,128)(2,1)S(1)}, bf16[18,256,128]{2,1,0:T(8,128)(2,1)S(1)}) custom-call(f32[18,256,128]{2,1,0:T(8,128)S(1)} %get-tuple-element.79.refs_0_, f32[4,256,128]{2,1,0:T(8,128)S(1)} %borders.3.refs_1_, ...), custom_call_target="tpu_custom_call" | custom-call | flops 301989888 | bytes 4718592 | tf_op jit(solution)/shard_map/inverse/pallas_call | solution.py:921
  74.1 0.1 collective-permute-start.18
  74.2 1.6 %collective-permute-start.19 = (s16[672,128]{1,0:T(8,128)(2,1)S(1)}, s16[672,128]{1,0:T(8,128)(2,1)S(1)}, u32[]{:S(2)}, u32[]{:S(2)}) collective-permute-start(s16[672,128]{1,0:T(8,128)(2,1)S(1)} %get-tuple-element.89), channel_id=1, source_target_pairs={{0,2},{1,3},{2,0},{3,1},{4,6},{5,7},{6,4},{7,5},{8,10},{9,11},{10,... | collective-permute-start | bytes 516104 | tf_op jit(solution)/shard_map/ppermute | solution.py:1189
  75.7 0.3 collective-permute-start.17
  76.0 0.8 inverse_rest.3.refs_0_.refs_4_
  76.9 1.1 %near_field.3.refs_7_ = f32[8,128]{1,0:T(8,128)S(1)} custom-call(s32[24]{0:T(128)S(1)} %get-tuple-element.92.place_ref, s32[24]{0:T(128)S(1)} %get-tuple-element.91.target_ref, s16[432,128]{1,0:T(8,128)(2,1)S(1)} %collective-permute-done.15.even_ref.refs_2_.refs_0_, s16[592,128]{1,0:T(8,128)(2,1)S(1)} %collective-permute-done.14.odd_ref.refs_3_.refs_1_, ...), custom_call_target="tpu_custom_call" | custom-call | flops 12582912 | bytes 786432 | tf_op jit(solution)/shard_map/near_field/pallas_call | solution.py:1124
  78.0 3.5 %collective-permute-done.19.refs_2_ = s16[672,128]{1,0:T(8,128)(2,1)S(1)} collective-permute-done((s16[672,128]{1,0:T(8,128)(2,1)S(1)}, s16[672,128]{1,0:T(8,128)(2,1)S(1)}, u32[]{:S(2)}, u32[]{:S(2)}) %collective-permute-start.19) | collective-permute-done | bytes 172064 | tf_op jit(solution)/shard_map/ppermute | solution.py:1189
  81.4 0.7 sample_early.3.refs_1_
  82.1 2.1 %collective-permute-done.17.refs_0_ = s16[672,128]{1,0:T(8,128)(2,1)S(1)} collective-permute-done((s16[672,128]{1,0:T(8,128)(2,1)S(1)}, s16[672,128]{1,0:T(8,128)(2,1)S(1)}, u32[]{:S(2)}, u32[]{:S(2)}) %collective-permute-start.17) | collective-permute-done | bytes 172064 | tf_op jit(solution)/shard_map/ppermute | solution.py:1189
  84.2 2.7 %sample.3 = f32[2,512]{1,0:T(2,128)} custom-call(s32[2,512]{1,0:T(2,128)S(1)} %get-tuple-element.48.place_ref.place_in.refs_1_, s16[672,128]{1,0:T(8,128)(2,1)S(1)} %collective-permute-done.17.refs_0_, f32[656,256]{1,0:T(8,128)S(1)} %sample_early.3.refs_1_, bf16[4,128,256]{2,1,0:T(8,128)(2,1)S(1)} %copy-done.5, bf16[4,128,256]{2,1,0:T(8,128)(2,1)S(1)} %copy-done.6, ...), custom_call_target="tpu_custom_call" | custom-call | flops 169869312 | bytes 4194304 | tf_op jit(solution)/shard_map/sample/pallas_call | solution.py:1066
  (22 shorter events, 0.1 us)
Async XLA Ops:
  5.3 9.1 %collective-permute-start = (s16[672,128]{1,0:T(8,128)(2,1)S(1)}, s16[672,128]{1,0:T(8,128)(2,1)S(1)}, u32[]{:S(2)}, u32[]{:S(2)}) collective-permute-start(s16[672,128]{1,0:T(8,128)(2,1)S(1)} %get-tuple-element.54), channel_id=1, source_target_pairs={{0,1},{1,0},{2,3},{3,2},{4,5},{5,4},{6,7},{7,6},{8,9},{9,8},{10,11... | collective-permute-start | bytes 516104 | tf_op jit(solution)/shard_map/ppermute | solution.py:1189
  5.9 8.6 %collective-permute-start.1 = (s16[672,128]{1,0:T(8,128)(2,1)S(1)}, s16[672,128]{1,0:T(8,128)(2,1)S(1)}, u32[]{:S(2)}, u32[]{:S(2)}) collective-permute-start(s16[672,128]{1,0:T(8,128)(2,1)S(1)} %get-tuple-element.55), channel_id=1, source_target_pairs={{0,2},{1,3},{2,0},{3,1},{4,6},{5,7},{6,4},{7,5},{8,10},{9,11},{10,... | collective-permute-start | bytes 516104 | tf_op jit(solution)/shard_map/ppermute | solution.py:1189
  8.4 8.4 %collective-permute-start.2 = (s16[672,128]{1,0:T(8,128)(2,1)S(1)}, s16[672,128]{1,0:T(8,128)(2,1)S(1)}, u32[]{:S(2)}, u32[]{:S(2)}) collective-permute-start(s16[672,128]{1,0:T(8,128)(2,1)S(1)} %get-tuple-element.56), channel_id=1, source_target_pairs={{0,3},{1,2},{2,1},{3,0},{4,7},{5,6},{6,5},{7,4},{8,11},{9,10},{10,... | collective-permute-start | bytes 516104 | tf_op jit(solution)/shard_map/ppermute | solution.py:1189
  8.5 0.9 %copy-start.1 = (f32[64,512]{1,0:T(8,128)S(1)}, f32[64,512]{1,0:T(8,128)}, u32[]{:S(2)}) copy-start(f32[64,512]{1,0:T(8,128)} %refs_3_.10) | copy-start | bytes 393220
  12.8 1.6 %copy-start = (bf16[2,256,240]{2,1,0:T(8,128)(2,1)S(1)}, bf16[2,256,240]{2,1,0:T(8,128)(2,1)}, u32[]{:S(2)}) copy-start(bf16[2,256,240]{2,1,0:T(8,128)(2,1)} %constant.76.clone.refs_3_.refs_6_.table_ref) | copy-start | bytes 737284
  16.8 14.5 %copy-start.3 = (bf16[4,48,256]{2,1,0:T(8,128)(2,1)S(1)}, bf16[4,48,256]{2,1,0:T(8,128)(2,1)}, u32[]{:S(2)}) copy-start(bf16[4,48,256]{2,1,0:T(8,128)(2,1)} %constant.77.clone.refs_7_.high_ref) | copy-start | bytes 294916
  16.8 14.5 %copy-start.4 = (bf16[4,48,256]{2,1,0:T(8,128)(2,1)S(1)}, bf16[4,48,256]{2,1,0:T(8,128)(2,1)}, u32[]{:S(2)}) copy-start(bf16[4,48,256]{2,1,0:T(8,128)(2,1)} %constant.78.clone.refs_8_.low_ref) | copy-start | bytes 294916
  18.1 7.0 %collective-permute-start.5 = (s16[432,128]{1,0:T(8,128)(2,1)S(1)}, s16[432,128]{1,0:T(8,128)(2,1)S(1)}, u32[]{:S(2)}, u32[]{:S(2)}) collective-permute-start(s16[432,128]{1,0:T(8,128)(2,1)S(1)} %get-tuple-element.62), channel_id=1, source_target_pairs={{0,4},{8,12},{4,0},{12,8},{1,5},{9,13},{5,1},{13,9},{2,6},{10,14},... | collective-permute-start | bytes 331784 | tf_op jit(solution)/shard_map/ppermute | solution.py:1212
  19.8 7.7 %collective-permute-start.4 = (s16[592,128]{1,0:T(8,128)(2,1)S(1)}, s16[592,128]{1,0:T(8,128)(2,1)S(1)}, u32[]{:S(2)}, u32[]{:S(2)}) collective-permute-start(s16[592,128]{1,0:T(8,128)(2,1)S(1)} %get-tuple-element.61), channel_id=1, source_target_pairs={{4,8},{8,4},{5,9},{9,5},{6,10},{10,6},{7,11},{11,7},{20,24},{24,20... | collective-permute-start | bytes 454664 | tf_op jit(solution)/shard_map/ppermute | solution.py:1213
  20.7 6.8 %collective-permute-start.3 = (s16[304,128]{1,0:T(8,128)(2,1)S(1)}, s16[304,128]{1,0:T(8,128)(2,1)S(1)}, u32[]{:S(2)}, u32[]{:S(2)}) collective-permute-start(s16[304,128]{1,0:T(8,128)(2,1)S(1)} %get-tuple-element.60), channel_id=1, source_target_pairs={{0,4},{8,12},{4,0},{12,8},{1,5},{9,13},{5,1},{13,9},{2,6},{10,14},... | collective-permute-start | bytes 233480 | tf_op jit(solution)/shard_map/ppermute | solution.py:1214
  25.3 9.7 %copy-start.8 = (s32[24]{0:T(128)S(1)}, s32[24]{0:T(128)}, u32[]{:S(2)}) copy-start(s32[24]{0:T(128)} %param.21) | copy-start | bytes 292
  25.3 9.7 %copy-start.9 = (s32[24]{0:T(128)S(1)}, s32[24]{0:T(128)}, u32[]{:S(2)}) copy-start(s32[24]{0:T(128)} %param.22) | copy-start | bytes 292
  25.3 6.1 %collective-permute-start.6 = (s16[272,128]{1,0:T(8,128)(2,1)S(1)}, s16[272,128]{1,0:T(8,128)(2,1)S(1)}, u32[]{:S(2)}, u32[]{:S(2)}) collective-permute-start(s16[272,128]{1,0:T(8,128)(2,1)S(1)} %pair_messages.2), channel_id=1, source_target_pairs={{0,8},{4,12},{8,0},{12,4},{1,9},{5,13},{9,1},{13,5},{2,10},{6,14},... | collective-permute-start | bytes 208904 | tf_op jit(solution)/shard_map/ppermute | solution.py:1216
  33.3 2.9 %copy-start.2 = (bf16[24,128,128]{2,1,0:T(8,128)(2,1)S(1)}, bf16[24,128,128]{2,1,0:T(8,128)(2,1)}, u32[]{:S(2)}) copy-start(bf16[24,128,128]{2,1,0:T(8,128)(2,1)} %refs_3_.12) | copy-start | bytes 2359300
  33.3 6.9 %collective-permute-start.8 = (s16[672,128]{1,0:T(8,128)(2,1)S(1)}, s16[672,128]{1,0:T(8,128)(2,1)S(1)}, u32[]{:S(2)}, u32[]{:S(2)}) collective-permute-start(s16[672,128]{1,0:T(8,128)(2,1)S(1)} %get-tuple-element.68), channel_id=1, source_target_pairs={{0,1},{1,0},{2,3},{3,2},{4,5},{5,4},{6,7},{7,6},{8,9},{9,8},{10,11... | collective-permute-start | bytes 516104 | tf_op jit(solution)/shard_map/ppermute | solution.py:1189
  33.4 7.2 %collective-permute-start.9 = (s16[672,128]{1,0:T(8,128)(2,1)S(1)}, s16[672,128]{1,0:T(8,128)(2,1)S(1)}, u32[]{:S(2)}, u32[]{:S(2)}) collective-permute-start(s16[672,128]{1,0:T(8,128)(2,1)S(1)} %get-tuple-element.69), channel_id=1, source_target_pairs={{0,2},{1,3},{2,0},{3,1},{4,6},{5,7},{6,4},{7,5},{8,10},{9,11},{10,... | collective-permute-start | bytes 516104 | tf_op jit(solution)/shard_map/ppermute | solution.py:1189
  35.0 8.4 %collective-permute-start.7 = (s16[672,128]{1,0:T(8,128)(2,1)S(1)}, s16[672,128]{1,0:T(8,128)(2,1)S(1)}, u32[]{:S(2)}, u32[]{:S(2)}) collective-permute-start(s16[672,128]{1,0:T(8,128)(2,1)S(1)} %get-tuple-element.65), channel_id=1, source_target_pairs={{0,3},{1,2},{2,1},{3,0},{4,7},{5,6},{6,5},{7,4},{8,11},{9,10},{10,... | collective-permute-start | bytes 516104 | tf_op jit(solution)/shard_map/ppermute | solution.py:1189
  37.3 3.4 %copy-start.5 = (bf16[4,128,256]{2,1,0:T(8,128)(2,1)S(1)}, bf16[4,128,256]{2,1,0:T(8,128)(2,1)}, u32[]{:S(2)}) copy-start(bf16[4,128,256]{2,1,0:T(8,128)(2,1)} %constant.79.clone.refs_3_.refs_2_) | copy-start | bytes 786436
  37.3 3.4 %copy-start.6 = (bf16[4,128,256]{2,1,0:T(8,128)(2,1)S(1)}, bf16[4,128,256]{2,1,0:T(8,128)(2,1)}, u32[]{:S(2)}) copy-start(bf16[4,128,256]{2,1,0:T(8,128)(2,1)} %constant.80.clone.refs_4_.refs_3_) | copy-start | bytes 786436
  40.3 3.2 %copy-start.7 = (s32[512]{0:T(512)S(1)}, s32[512]{0:T(512)}, u32[]{:S(2)}) copy-start(s32[512]{0:T(512)} %param.17) | copy-start | bytes 6148
  48.6 2.5 %collective-permute-start.10 = (s16[672,128]{1,0:T(8,128)(2,1)S(1)}, s16[672,128]{1,0:T(8,128)(2,1)S(1)}, u32[]{:S(2)}, u32[]{:S(2)}) collective-permute-start(s16[672,128]{1,0:T(8,128)(2,1)S(1)} %get-tuple-element.74), channel_id=1, source_target_pairs={{0,1},{1,0},{2,3},{3,2},{4,5},{5,4},{6,7},{7,6},{8,9},{9,8},{10,11... | collective-permute-start | bytes 516104 | tf_op jit(solution)/shard_map/ppermute | solution.py:1189
  48.9 7.2 %collective-permute-start.11 = (s16[672,128]{1,0:T(8,128)(2,1)S(1)}, s16[672,128]{1,0:T(8,128)(2,1)S(1)}, u32[]{:S(2)}, u32[]{:S(2)}) collective-permute-start(s16[672,128]{1,0:T(8,128)(2,1)S(1)} %get-tuple-element.75), channel_id=1, source_target_pairs={{0,2},{1,3},{2,0},{3,1},{4,6},{5,7},{6,4},{7,5},{8,10},{9,11},{10,... | collective-permute-start | bytes 516104 | tf_op jit(solution)/shard_map/ppermute | solution.py:1189
  50.4 8.0 %collective-permute-start.12 = (s16[672,128]{1,0:T(8,128)(2,1)S(1)}, s16[672,128]{1,0:T(8,128)(2,1)S(1)}, u32[]{:S(2)}, u32[]{:S(2)}) collective-permute-start(s16[672,128]{1,0:T(8,128)(2,1)S(1)} %get-tuple-element.76), channel_id=1, source_target_pairs={{0,3},{1,2},{2,1},{3,0},{4,7},{5,6},{6,5},{7,4},{8,11},{9,10},{10,... | collective-permute-start | bytes 516104 | tf_op jit(solution)/shard_map/ppermute | solution.py:1189
  59.6 6.0 %collective-permute-start.15 = (s16[432,128]{1,0:T(8,128)(2,1)S(1)}, s16[432,128]{1,0:T(8,128)(2,1)S(1)}, u32[]{:S(2)}, u32[]{:S(2)}) collective-permute-start(s16[432,128]{1,0:T(8,128)(2,1)S(1)} %get-tuple-element.82), channel_id=1, source_target_pairs={{0,4},{8,12},{4,0},{12,8},{1,5},{9,13},{5,1},{13,9},{2,6},{10,14},... | collective-permute-start | bytes 331784 | tf_op jit(solution)/shard_map/ppermute | solution.py:1212
  59.7 8.6 %collective-permute-start.14 = (s16[592,128]{1,0:T(8,128)(2,1)S(1)}, s16[592,128]{1,0:T(8,128)(2,1)S(1)}, u32[]{:S(2)}, u32[]{:S(2)}) collective-permute-start(s16[592,128]{1,0:T(8,128)(2,1)S(1)} %get-tuple-element.81), channel_id=1, source_target_pairs={{4,8},{8,4},{5,9},{9,5},{6,10},{10,6},{7,11},{11,7},{20,24},{24,20... | collective-permute-start | bytes 454664 | tf_op jit(solution)/shard_map/ppermute | solution.py:1213
  60.6 7.7 %collective-permute-start.13 = (s16[304,128]{1,0:T(8,128)(2,1)S(1)}, s16[304,128]{1,0:T(8,128)(2,1)S(1)}, u32[]{:S(2)}, u32[]{:S(2)}) collective-permute-start(s16[304,128]{1,0:T(8,128)(2,1)S(1)} %get-tuple-element.80), channel_id=1, source_target_pairs={{0,4},{8,12},{4,0},{12,8},{1,5},{9,13},{5,1},{13,9},{2,6},{10,14},... | collective-permute-start | bytes 233480 | tf_op jit(solution)/shard_map/ppermute | solution.py:1214
  65.8 6.3 %collective-permute-start.16 = (s16[272,128]{1,0:T(8,128)(2,1)S(1)}, s16[272,128]{1,0:T(8,128)(2,1)S(1)}, u32[]{:S(2)}, u32[]{:S(2)}) collective-permute-start(s16[272,128]{1,0:T(8,128)(2,1)S(1)} %pair_messages.3), channel_id=1, source_target_pairs={{0,8},{4,12},{8,0},{12,4},{1,9},{5,13},{9,1},{13,5},{2,10},{6,14},... | collective-permute-start | bytes 208904 | tf_op jit(solution)/shard_map/ppermute | solution.py:1216
  74.1 3.9 %collective-permute-start.18 = (s16[672,128]{1,0:T(8,128)(2,1)S(1)}, s16[672,128]{1,0:T(8,128)(2,1)S(1)}, u32[]{:S(2)}, u32[]{:S(2)}) collective-permute-start(s16[672,128]{1,0:T(8,128)(2,1)S(1)} %get-tuple-element.88), channel_id=1, source_target_pairs={{0,1},{1,0},{2,3},{3,2},{4,5},{5,4},{6,7},{7,6},{8,9},{9,8},{10,11... | collective-permute-start | bytes 516104 | tf_op jit(solution)/shard_map/ppermute | solution.py:1189
  74.2 7.2 %collective-permute-start.19 = (s16[672,128]{1,0:T(8,128)(2,1)S(1)}, s16[672,128]{1,0:T(8,128)(2,1)S(1)}, u32[]{:S(2)}, u32[]{:S(2)}) collective-permute-start(s16[672,128]{1,0:T(8,128)(2,1)S(1)} %get-tuple-element.89), channel_id=1, source_target_pairs={{0,2},{1,3},{2,0},{3,1},{4,6},{5,7},{6,4},{7,5},{8,10},{9,11},{10,... | collective-permute-start | bytes 516104 | tf_op jit(solution)/shard_map/ppermute | solution.py:1189
  75.7 8.5 %collective-permute-start.17 = (s16[672,128]{1,0:T(8,128)(2,1)S(1)}, s16[672,128]{1,0:T(8,128)(2,1)S(1)}, u32[]{:S(2)}, u32[]{:S(2)}) collective-permute-start(s16[672,128]{1,0:T(8,128)(2,1)S(1)} %get-tuple-element.85), channel_id=1, source_target_pairs={{0,3},{1,2},{2,1},{3,0},{4,7},{5,6},{6,5},{7,4},{8,11},{9,10},{10,... | collective-permute-start | bytes 516104 | tf_op jit(solution)/shard_map/ppermute | solution.py:1189

commit v17 on v15

--- a/solution.py
+++ b/solution.py
@@ -613,7 +613,7 @@
         transform_pieces(table_ref[lax.axis_index("pair") ^ core], stacked, before, spectrum)
         before = spectrum
 
-    chunk = 128
+    chunk = 256
 
     def body(index, largest):
         rows = pl.ds(pl.multiple_of(index * chunk, chunk), chunk)
@@ -763,12 +763,55 @@
     )(own, from_even, modes)
 
 
-def borders_kernel(reach_y, pieces, layers_ref, odd_ref, table_ref, out_ref, stacked, partial):
+def odd_kernel(odd_ref, moments_out, edges_out):
+    rows = edges_out.shape[0]
+    first = odd_ref.shape[0] - rows - GRID
+    moments_out[...] = opened_part(odd_ref, 0, first, GRID)
+    edges_out[...] = opened_part(odd_ref, 1, first + GRID, rows)
+
+
+def open_odd(from_odd, border):
+    lanes = 2 * HALF
+    return pl.pallas_call(
+        odd_kernel,
+        in_specs=[whole_vmem()],
+        out_specs=[whole_vmem()] * 2,
+        out_shape=[
+            jax.ShapeDtypeStruct((GRID, lanes), F32),
+            jax.ShapeDtypeStruct((border, lanes), F32),
+        ],
+        compiler_params=params(),
+        cost_estimate=cost(4 * GRID * lanes, 6 * (GRID + border) * lanes),
+        name="open_odd",
+    )(from_odd)
+
+
+def far_kernel(fars, *refs):
+    total = opened_part(refs[0], 0, 16, GRID)
+    for ref in refs[1:fars]:
+        total = total + opened_part(ref, 0, 16, GRID)
+    refs[-1][...] = total
+
+
+def far_moments(fars, awaited):
+    return pl.pallas_call(
+        functools.partial(far_kernel, len(fars)),
+        in_specs=[whole_vmem()] * len(fars) + [anywhere()] * len(awaited),
+        out_specs=whole_vmem(),
+        out_shape=jax.ShapeDtypeStruct((GRID, 2 * HALF), F32),
+        compiler_params=params(),
+        cost_estimate=cost(EARLY_FLOPS, 2 * GRID * 2 * HALF * (2 + len(fars))),
+        name="far_moments",
+    )(*fars, *awaited)
+
+
+def borders_kernel(reach_y, pieces, layers_ref, edges_ref, table_ref, *refs):
+    out_ref, stacked, partial = refs[-3:]
     on_left = (lax.axis_index("wide") & 1) == 1
     pair = lax.axis_size("pair")
     rows = pieces * 2 * reach_y
     even = opened_part(layers_ref, 0, 16, rows)
-    odd = opened_part(odd_ref, 1, odd_ref.shape[0] - rows, rows)
+    odd = edges_ref[...]
     left, right = jnp.where(on_left, even, odd), jnp.where(on_left, odd, even)
     low = low_lanes(rows)
     both = [jnp.where(low, left, swap(right)), jnp.where(low, swap(left), right)]
@@ -790,12 +833,12 @@
         before = target
 
 
-def borders(layers, from_odd, table, reach_y, pieces):
+def borders(layers, odd_edges, table, reach_y, pieces, awaited):
     chips = pieces // table.shape[0]
     shape = (4, GRID, 2 * HALF)
     return pl.pallas_call(
         functools.partial(borders_kernel, reach_y, pieces),
-        in_specs=[whole_vmem()] * 3,
+        in_specs=[whole_vmem()] * 3 + [anywhere()] * len(awaited),
         out_specs=whole_vmem(),
         out_shape=jax.ShapeDtypeStruct(shape, F32),
         scratch_shapes=[
@@ -805,7 +848,7 @@
         compiler_params=params(),
         cost_estimate=cost(2 * 4 * 256 * 256 * 128, 4 * 6 * GRID * 2 * HALF),
         name="borders",
-    )(layers, from_odd, table)
+    )(layers, odd_edges, table, *awaited)
 
 
 def send_fields(outs, flips, reach_y, field_high, field_low, high_ref, low_ref, ready, head):
@@ -830,26 +873,19 @@
         send_piece(out, head, ready[piece])
 
 
-def inverse_kernel(reach_x, reach_y, flips, fars, *refs):
-    spectrum, border_ref, from_even, from_odd, own_ref, inner_ref, *far_refs = refs[: 6 + fars]
-    refs = refs[6 + fars :]
+def inverse_kernel(reach_x, reach_y, flips, *refs):
+    spectrum, border_ref, from_even, odd_ref, own_ref, inner_ref, far_ref = refs[:7]
+    refs = refs[7:]
     high_ref, low_ref, modes_ref = refs[:3]
     outs = refs[3 : 3 + len(flips)]
     field_high, field_low, ready, head = refs[3 + len(flips) :]
     half = reach_x // 2
     span = reach_x - 4
-    chunk = 128
+    chunk = 256
     head_rows = from_even.shape[0] - GRID - GRID // 2
     on_left = (lax.axis_index("wide") & 1) == 1
-    moment_units = []
-    for ref in (from_even, from_odd):
-        first = from_short(ref[:16, :])
-        moment_units.append(unit(first[0:1], first[1:2]))
-
-    far_units = []
-    for ref in far_refs:
-        first = from_short(ref[:16, :])
-        far_units.append(unit(first[0:1], first[1:2]))
+    first = from_short(from_even[:16, :])
+    even_unit = unit(first[0:1], first[1:2])
 
     def body(index, carry):
         first = pl.multiple_of(index * chunk, chunk)
@@ -866,9 +902,7 @@
         layers = [spectrum[i, rows, :] for i in range(half)]
 
         at = pl.ds(pl.multiple_of(head_rows + index * chunk, 16), chunk)
-        even, odd = (
-            from_short(ref[at, :]) * scale for ref, scale in zip((from_even, from_odd), moment_units)
-        )
+        even, odd = from_short(from_even[at, :]) * even_unit, odd_ref[rows, :]
         left_moments, right_moments = jnp.where(on_left, even, odd), jnp.where(on_left, odd, even)
         border = [border_ref[i, rows, :] for i in range(4)]
         zero = jnp.zeros_like(decay)
@@ -884,9 +918,7 @@
             place = half - 4 + i
             layers[place] = layers[place] + jnp.where(low, zero, border[i])
         total = own_ref[rows, :] * jnp.exp((GRID - reach_x) * log_decay)
-        at = pl.ds(pl.multiple_of(16 + index * chunk, 16), chunk)
-        for ref, scale in zip(far_refs, far_units):
-            total = total + from_short(ref[at, :]) * scale
+        total = total + far_ref[rows, :]
         one = jnp.ones_like(decay)
         total = total + left_moments * jnp.where(low, beside, one)
         total = total + right_moments * jnp.where(low, one, beside)
@@ -912,7 +944,7 @@
 
 
 def inverse(
-    spectrum, border, from_even, from_odd, own, inner, fars, table, modes, reach_x, reach_y, flips
+    spectrum, border, from_even, odd, own, inner, far, table, modes, reach_x, reach_y, flips
 ):
     half = reach_x // 2
     lanes = 2 * HALF
@@ -920,8 +952,8 @@
     shapes = [jax.ShapeDtypeStruct((16 + body, lanes), jnp.int16)] * len(flips)
     shapes += [jax.ShapeDtypeStruct((half, GRID, lanes), BF16)] * 2
     return pl.pallas_call(
-        functools.partial(inverse_kernel, reach_x, reach_y, flips, len(fars)),
-        in_specs=[whole_vmem()] * (9 + len(fars)),
+        functools.partial(inverse_kernel, reach_x, reach_y, flips),
+        in_specs=[whole_vmem()] * 10,
         out_specs=[whole_vmem()] * len(shapes),
         out_shape=shapes,
         scratch_shapes=[
@@ -931,7 +963,7 @@
         compiler_params=params(),
         cost_estimate=cost(2 * half * 256 * 256 * 128, 4 * half * GRID * lanes * 2),
         name="inverse",
-    )(spectrum, border, from_even, from_odd, own, inner, *fars, *table, modes)
+    )(spectrum, border, from_even, odd, own, inner, far, *table, modes)
 
 
 def inverse_rest_kernel(reach_y, flips, field_high, field_low, high_ref, low_ref, *refs):
@@ -1209,14 +1241,16 @@
                 far_flips, pair_messages(own, from_even, modes, reach_x, far_flips)
             )
         ]
+        odd_moments, odd_edges = open_odd(from_odd, y_count * 2 * reach_y)
+        far = far_moments(fars, [odd_moments]) if fars else jnp.zeros_like(own)
         *sent, high, low = inverse(
             spectrum,
-            borders(even_layers, from_odd, y_forward, reach_y, y_count),
+            borders(even_layers, odd_edges, y_forward, reach_y, y_count, [far]),
             from_even,
-            from_odd,
+            odd_moments,
             own,
             inner,
-            fars,
+            far,
             y_inverse,
             modes,
             reach_x,

time: 85.2 us -> 85.9 us (level)
  waiting for transfers between devices: 23.1 us -> 27.8 us
  starting transfers between devices: 24.9 us -> 21.2 us
    ppermute x2, waiting for transfers between devices: 0.01 us -> 7.55 us  [convolve_and_sample(): from_even = lax.ppermute(even_message, 'wide', even_swap)]
    ppermute x2, starting transfers between devices: 9.03 us -> 3.33 us  [convolve_and_sample(): even_layers = lax.ppermute(layers, 'wide', even_swap)]
    ppermute x2, waiting for transfers between devices: 2.51 us -> 0.52 us  [convolve_and_sample(): even_layers = lax.ppermute(layers, 'wide', even_swap)]
    ppermute x2, starting transfers between devices: 2.43 us -> 4.28 us  [convolve_and_sample(): lax.ppermute(message, 'wide', [(i, i ^ flip) for i in range(x_count)])]
    ppermute x12, waiting for transfers between devices: 13.5 us -> 12.6 us  [turned(): lax.ppermute(part, Y_AXES, swap_pairs)]
    pallas_call x2 -> x6, Pallas kernels: 4.13 us -> 3.92 us  [the longest x2 3.8 us: inverse(): pl.pallas_call(functools.partial(inverse_kernel, reach_x, reach_y, flips)...]
  transfers between devices with their start and end apart: 20 -> 20, of which waited for: 10 -> 12; matrix products, arithmetic and copies ran while one was open for 1% -> 1% of each run, Pallas kernels for 17% -> 16%
where the time goes in v17:
time: 85.9 us; the launch traced here: 85.6 us
  Pallas kernels  33.9 us (39%)
  waiting for transfers between devices  27.8 us (32%)
  starting transfers between devices  21.2 us (25%)
  local copies, waits for them, and re-layouts  2.18 us (3%)
    ppermute x12, waiting for transfers between devices, turned(): lax.ppermute(part, Y_AXES, swap_pairs)  12.6 us
    ppermute x12, starting transfers between devices, turned(): lax.ppermute(part, Y_AXES, swap_pairs)  10.1 us
    pallas_call x2, Pallas kernels, spread(): pl.pallas_call(functools.partial(start_kernel if placed is None else spre...  7.69 us
    ppermute x2, waiting for transfers between devices, convolve_and_sample(): from_even = lax.ppermute(even_message, 'wide', even_swap)  7.55 us
    ppermute x2, waiting for transfers between devices, convolve_and_sample(): lax.ppermute(message, 'wide', [(i, i ^ flip) for i in range(x_count)])  7.15 us
    pallas_call x2, Pallas kernels, sample(): pl.pallas_call(functools.partial(sample_kernel, last, reach_x, reach_y, f...  4.87 us
    ppermute x2, starting transfers between devices, convolve_and_sample(): lax.ppermute(message, 'wide', [(i, i ^ flip) for i in range(x_count)])  4.28 us
    pallas_call x2, Pallas kernels, inverse(): pl.pallas_call(functools.partial(inverse_kernel, reach_x, reach_y, flips)...  3.8 us
  transfers between devices with their start and end apart: 20, of which 12 were waited for; matrix products, arithmetic and copies ran while one was open for 1% of the time, Pallas kernels for 16%

profile of v17, /device:TPU:0, one launch (start us, length us, event | category | flops | bytes accessed | tf_op | source)
XLA Modules:
  0.0 85.6 jit_solution(18105026589571952199)
XLA Ops:
  0.0 5.0 %start.1 = (s16[672,128]{1,0:T(8,128)(2,1)S(1)}, s16[672,128]{1,0:T(8,128)(2,1)S(1)}, bf16[656,256]{1,0:T(8,128)(2,1)S(1)}, bf16[656,256]{1,0:T(8,128)(2,1)S(1)}...) custom-call(f32[512]{0:T(512)} %refs_0_.2, ...), custom_call_target="tpu_custom_call" | custom-call | flops 169869312 | bytes 4194304 | tf_op jit(solution)/shard_map/start/pallas_call | solution.py:411
  5.0 3.0 %collective-permute-start.1 = (s16[672,128]{1,0:T(8,128)(2,1)S(1)}, s16[672,128]{1,0:T(8,128)(2,1)S(1)}, u32[]{:S(2)}, u32[]{:S(2)}) collective-permute-start(s16[672,128]{1,0:T(8,128)(2,1)S(1)} %get-tuple-element.64), channel_id=1, source_target_pairs={{0,2},{1,3},{2,0},{3,1},{4,6},{5,7},{6,4},{7,5},{8,10},{9,11},{10,... | collective-permute-start | bytes 516104 | tf_op jit(solution)/shard_map/ppermute | solution.py:1223
  8.0 0.6 spread_rest.2
  8.6 0.1 collective-permute-start
  8.7 0.1 collective-permute-start.2
  8.8 0.9 %copy-done.1 = f32[64,512]{1,0:T(8,128)S(1)} copy-done((f32[64,512]{1,0:T(8,128)S(1)}, f32[64,512]{1,0:T(8,128)}, u32[]{:S(2)}) %copy-start.1) | copy-done | bytes 131096
  9.7 3.4 %place_sample_lines.1.refs_8_.refs_5_ = f32[8192,128]{1,0:T(8,128)S(1)} custom-call(s32[2,512]{1,0:T(2,128)S(1)} %get-tuple-element.56.place_ref.place_in.refs_1_, f32[64,512]{1,0:T(8,128)S(1)} %copy-done.1, f32[64,512]{1,0:T(8,128)S(1)} %copy-done.1, f32[64,512]{1,0:T(8,128)S(1)} %copy-done.1, f32[64,512]{1,0:T(8,128)S(1)} %copy-done.1), custom_call_target="tpu_custom_call" | custom-call | flops 1048576 | bytes 4194304 | tf_op jit(solution)/shard_map/place_sample_lines/pallas_call | solution.py:480
  13.2 1.1 %dynamic-slice_bitcast_fusion.refs_7_.modes_ref.refs_9_ = f32[4,256,128]{2,1,0:T(8,128)S(1)} fusion(f32[4,4,256,128]{3,2,1,0:T(8,128)} %constant.73.clone, s32[]{:T(128)S(6)} %select_n.30), kind=kLoop, calls=%fused_computation | loop fusion | bytes 1048580 | tf_op jit(solution)/shard_map/jit(dynamic_index_in_dim)/squeeze | solution.py:1200
  14.3 0.7 forward_early.2
  14.9 0.6 collective-permute-done.2.refs_3_
  15.5 1.3 %forward.2 = (f32[18,256,128]{2,1,0:T(8,128)S(1)}, s16[432,128]{1,0:T(8,128)(2,1)S(1)}, s16[304,128]{1,0:T(8,128)(2,1)S(1)}, s16[592,128]{1,0:T(8,128)(2,1)S(1)}...) custom-call(s16[672,128]{1,0:T(8,128)(2,1)S(1)} %get-tuple-element.62.refs_0_, ...), custom_call_target="tpu_custom_call" | custom-call | flops 301989888 | bytes 4718592 | tf_op jit(solution)/shard_map/forward/pallas_call | solution.py:690
  16.8 1.7 %collective-permute-start.5 = (s16[432,128]{1,0:T(8,128)(2,1)S(1)}, s16[432,128]{1,0:T(8,128)(2,1)S(1)}, u32[]{:S(2)}, u32[]{:S(2)}) collective-permute-start(s16[432,128]{1,0:T(8,128)(2,1)S(1)} %get-tuple-element.73), channel_id=1, source_target_pairs={{0,4},{8,12},{4,0},{12,8},{1,5},{9,13},{5,1},{13,9},{2,6},{10,14},... | collective-permute-start | bytes 331784 | tf_op jit(solution)/shard_map/ppermute | solution.py:1235
  18.5 0.8 collective-permute-start.4
  19.3 3.1 %collective-permute-done.5.even_ref.refs_2_.refs_0_ = s16[432,128]{1,0:T(8,128)(2,1)S(1)} collective-permute-done((s16[432,128]{1,0:T(8,128)(2,1)S(1)}, s16[432,128]{1,0:T(8,128)(2,1)S(1)}, u32[]{:S(2)}, u32[]{:S(2)}) %collective-permute-start.5) | collective-permute-done | bytes 110624 | tf_op jit(solution)/shard_map/ppermute | solution.py:1235
  22.4 0.2 pair_messages.2
  22.5 2.8 %collective-permute-start.6 = (s16[272,128]{1,0:T(8,128)(2,1)S(1)}, s16[272,128]{1,0:T(8,128)(2,1)S(1)}, u32[]{:S(2)}, u32[]{:S(2)}) collective-permute-start(s16[272,128]{1,0:T(8,128)(2,1)S(1)} %pair_messages.2), channel_id=1, source_target_pairs={{0,8},{4,12},{8,0},{12,4},{1,9},{5,13},{9,1},{13,5},{2,10},{6,14},... | collective-permute-start | bytes 208904 | tf_op jit(solution)/shard_map/ppermute | solution.py:1239
  25.3 1.6 %collective-permute-start.3 = (s16[304,128]{1,0:T(8,128)(2,1)S(1)}, s16[304,128]{1,0:T(8,128)(2,1)S(1)}, u32[]{:S(2)}, u32[]{:S(2)}) collective-permute-start(s16[304,128]{1,0:T(8,128)(2,1)S(1)} %get-tuple-element.69), channel_id=1, source_target_pairs={{0,4},{8,12},{4,0},{12,8},{1,5},{9,13},{5,1},{13,9},{2,6},{10,14},... | collective-permute-start | bytes 233480 | tf_op jit(solution)/shard_map/ppermute | solution.py:1237
  26.9 0.0 collective-permute-done.4.odd_ref.refs_1_
  27.0 3.6 %collective-permute-done.6.refs_0_ = s16[272,128]{1,0:T(8,128)(2,1)S(1)} collective-permute-done((s16[272,128]{1,0:T(8,128)(2,1)S(1)}, s16[272,128]{1,0:T(8,128)(2,1)S(1)}, u32[]{:S(2)}, u32[]{:S(2)}) %collective-permute-start.6) | collective-permute-done | bytes 69664 | tf_op jit(solution)/shard_map/ppermute | solution.py:1239
  30.6 0.3 collective-permute-done.3.layers_ref
  30.8 0.4 borders.2.refs_1_
  31.3 0.0 copy-start.8
  31.3 0.0 copy-start.9
  31.3 0.1 copy-done.3
  31.4 0.0 copy-done.4
  31.5 1.9 %inverse.2 = (s16[672,128]{1,0:T(8,128)(2,1)S(1)}, s16[672,128]{1,0:T(8,128)(2,1)S(1)}, bf16[18,256,128]{2,1,0:T(8,128)(2,1)S(1)}, bf16[18,256,128]{2,1,0:T(8,128)(2,1)S(1)}) custom-call(f32[18,256,128]{2,1,0:T(8,128)S(1)} %get-tuple-element.68.refs_0_, f32[4,256,128]{2,1,0:T(8,128)S(1)} %borders.2.refs_1_, ...), custom_call_target="tpu_custom_call" | custom-call | flops 301989888 | bytes 4718592 | tf_op jit(solution)/shard_map/inverse/pallas_call | solution.py:954
  33.4 1.6 %collective-permute-start.9 = (s16[672,128]{1,0:T(8,128)(2,1)S(1)}, s16[672,128]{1,0:T(8,128)(2,1)S(1)}, u32[]{:S(2)}, u32[]{:S(2)}) collective-permute-start(s16[672,128]{1,0:T(8,128)(2,1)S(1)} %get-tuple-element.81), channel_id=1, source_target_pairs={{0,2},{1,3},{2,0},{3,1},{4,6},{5,7},{6,4},{7,5},{8,10},{9,11},{10,... | collective-permute-start | bytes 516104 | tf_op jit(solution)/shard_map/ppermute | solution.py:1223
  35.0 0.9 %inverse_rest.2 = (s16[672,128]{1,0:T(8,128)(2,1)S(1)}, s16[672,128]{1,0:T(8,128)(2,1)S(1)}) custom-call(bf16[18,256,128]{2,1,0:T(8,128)(2,1)S(1)} %get-tuple-element.76.field_high, bf16[18,256,128]{2,1,0:T(8,128)(2,1)S(1)} %get-tuple-element.77.field_low, bf16[4,48,256]{2,1,0:T(8,128)(2,1)S(1)} %copy-done.3, bf16[4,48,256]{2,1,0:T(8,128)(2,1)S(1)} %copy-done.4), custom_call_target="tpu_custom_call" | custom-call | flops 301989888 | bytes 4718592 | tf_op jit(solution)/shard_map/inverse_rest/pallas_call | solution.py:978
  35.8 0.1 collective-permute-start.7
  35.9 0.7 collective-permute-start.8
  36.6 1.0 %near_field.2.refs_8_.refs_0_ = f32[8,128]{1,0:T(8,128)S(1)} custom-call(s32[24]{0:T(128)S(1)} %get-tuple-element.108.place_ref, s32[24]{0:T(128)S(1)} %get-tuple-element.107.target_ref, s16[432,128]{1,0:T(8,128)(2,1)S(1)} %collective-permute-done.5.even_ref.refs_2_.refs_0_, s16[592,128]{1,0:T(8,128)(2,1)S(1)} %collective-permute-done.4.odd_ref.refs_1_, ...), custom_call_target="tpu_custom_call" | custom-call | flops 12582912 | bytes 786432 | tf_op jit(solution)/shard_map/near_field/pallas_call | solution.py:1157
  37.6 0.0 copy-start.6
  37.6 3.0 %place_lines.1.refs_5_ = f32[8192,128]{1,0:T(8,128)S(1)} custom-call(s32[2,512]{1,0:T(2,128)S(1)} %get-tuple-element.56.place_ref.place_in.refs_1_, f32[256,128]{1,0:T(8,128)S(1)} %get-tuple-element.83.coeff_ref, f32[8,128]{1,0:T(8,128)S(1)} %near_field.2.refs_8_.refs_0_), custom_call_target="tpu_custom_call" | custom-call | flops 1048576 | bytes 4194304 | tf_op jit(solution)/shard_map/place_lines/pallas_call | solution.py:496
  40.6 0.4 sample_early.2.refs_2_
  41.1 1.6 %collective-permute-done.8.refs_1_ = s16[672,128]{1,0:T(8,128)(2,1)S(1)} collective-permute-done((s16[672,128]{1,0:T(8,128)(2,1)S(1)}, s16[672,128]{1,0:T(8,128)(2,1)S(1)}, u32[]{:S(2)}, u32[]{:S(2)}) %collective-permute-start.8) | collective-permute-done | bytes 172064 | tf_op jit(solution)/shard_map/ppermute | solution.py:1223
  42.7 2.1 %sample.2.refs_2_.rounded_ref.refs_7_ = f32[4,128]{1,0:T(4,128)S(1)} custom-call(s32[2,512]{1,0:T(2,128)S(1)} %get-tuple-element.56.place_ref.place_in.refs_1_, s16[672,128]{1,0:T(8,128)(2,1)S(1)} %collective-permute-done.7.refs_0_, s16[672,128]{1,0:T(8,128)(2,1)S(1)} %collective-permute-done.8.refs_1_, f32[656,256]{1,0:T(8,128)S(1)} %sample_early.2.refs_2_, ...), custom_call_target="tpu_custom_call" | custom-call | flops 169869312 | bytes 4194304 | tf_op jit(solution)/shard_map/sample/pallas_call | solution.py:1099
  44.9 2.7 %spread.1 = (s16[672,128]{1,0:T(8,128)(2,1)S(1)}, s16[672,128]{1,0:T(8,128)(2,1)S(1)}, bf16[656,256]{1,0:T(8,128)(2,1)S(1)}, bf16[656,256]{1,0:T(8,128)(2,1)S(1)}) custom-call(f32[512]{0:T(512)S(1)} %bitcast.6, s32[2,512]{1,0:T(2,128)S(1)} %get-tuple-element.56.place_ref.place_in.refs_1_, f32[4,128]{1,0:T(4,128)S(1)} %sample.2.refs_2_.rounded_ref.refs_7_, ...), custom_call_target="tpu_custom_call" | custom-call | flops 169869312 | bytes 4194304 | tf_op jit(solution)/shard_map/spread/pallas_call | solution.py:411
  47.5 0.7 collective-permute-start.11
  48.2 0.6 spread_rest.3
  48.8 0.9 %collective-permute-start.10 = (s16[672,128]{1,0:T(8,128)(2,1)S(1)}, s16[672,128]{1,0:T(8,128)(2,1)S(1)}, u32[]{:S(2)}, u32[]{:S(2)}) collective-permute-start(s16[672,128]{1,0:T(8,128)(2,1)S(1)} %get-tuple-element.87), channel_id=1, source_target_pairs={{0,1},{1,0},{2,3},{3,2},{4,5},{5,4},{6,7},{7,6},{8,9},{9,8},{10,11... | collective-permute-start | bytes 516104 | tf_op jit(solution)/shard_map/ppermute | solution.py:1223
  49.7 0.7 collective-permute-start.12
  50.4 4.4 %collective-permute-done.11.refs_1_.refs_2_ = s16[672,128]{1,0:T(8,128)(2,1)S(1)} collective-permute-done((s16[672,128]{1,0:T(8,128)(2,1)S(1)}, s16[672,128]{1,0:T(8,128)(2,1)S(1)}, u32[]{:S(2)}, u32[]{:S(2)}) %collective-permute-start.11) | collective-permute-done | bytes 172064 | tf_op jit(solution)/shard_map/ppermute | solution.py:1223
  54.8 0.7 forward_early.3
  55.5 1.5 %collective-permute-done.12.refs_3_ = s16[672,128]{1,0:T(8,128)(2,1)S(1)} collective-permute-done((s16[672,128]{1,0:T(8,128)(2,1)S(1)}, s16[672,128]{1,0:T(8,128)(2,1)S(1)}, u32[]{:S(2)}, u32[]{:S(2)}) %collective-permute-start.12) | collective-permute-done | bytes 172064 | tf_op jit(solution)/shard_map/ppermute | solution.py:1223
  57.0 1.3 %forward.3 = (f32[18,256,128]{2,1,0:T(8,128)S(1)}, s16[432,128]{1,0:T(8,128)(2,1)S(1)}, s16[304,128]{1,0:T(8,128)(2,1)S(1)}, s16[592,128]{1,0:T(8,128)(2,1)S(1)}...) custom-call(s16[672,128]{1,0:T(8,128)(2,1)S(1)} %get-tuple-element.86.refs_0_, ...), custom_call_target="tpu_custom_call" | custom-call | flops 301989888 | bytes 4718592 | tf_op jit(solution)/shard_map/forward/pallas_call | solution.py:690
  58.4 0.2 collective-permute-start.15
  58.6 0.9 %collective-permute-start.14 = (s16[592,128]{1,0:T(8,128)(2,1)S(1)}, s16[592,128]{1,0:T(8,128)(2,1)S(1)}, u32[]{:S(2)}, u32[]{:S(2)}) collective-permute-start(s16[592,128]{1,0:T(8,128)(2,1)S(1)} %get-tuple-element.94), channel_id=1, source_target_pairs={{4,8},{8,4},{5,9},{9,5},{6,10},{10,6},{7,11},{11,7},{20,24},{24,20... | collective-permute-start | bytes 454664 | tf_op jit(solution)/shard_map/ppermute | solution.py:1236
  59.4 4.5 %collective-permute-done.15.even_ref.refs_2_.refs_0_ = s16[432,128]{1,0:T(8,128)(2,1)S(1)} collective-permute-done((s16[432,128]{1,0:T(8,128)(2,1)S(1)}, s16[432,128]{1,0:T(8,128)(2,1)S(1)}, u32[]{:S(2)}, u32[]{:S(2)}) %collective-permute-start.15) | collective-permute-done | bytes 110624 | tf_op jit(solution)/shard_map/ppermute | solution.py:1235
  63.9 0.2 pair_messages.3
  64.1 1.5 %collective-permute-start.16 = (s16[272,128]{1,0:T(8,128)(2,1)S(1)}, s16[272,128]{1,0:T(8,128)(2,1)S(1)}, u32[]{:S(2)}, u32[]{:S(2)}) collective-permute-start(s16[272,128]{1,0:T(8,128)(2,1)S(1)} %pair_messages.3), channel_id=1, source_target_pairs={{0,8},{4,12},{8,0},{12,4},{1,9},{5,13},{9,1},{13,5},{2,10},{6,14},... | collective-permute-start | bytes 208904 | tf_op jit(solution)/shard_map/ppermute | solution.py:1239
  65.6 1.7 %collective-permute-start.13 = (s16[304,128]{1,0:T(8,128)(2,1)S(1)}, s16[304,128]{1,0:T(8,128)(2,1)S(1)}, u32[]{:S(2)}, u32[]{:S(2)}) collective-permute-start(s16[304,128]{1,0:T(8,128)(2,1)S(1)} %get-tuple-element.93), channel_id=1, source_target_pairs={{0,4},{8,12},{4,0},{12,8},{1,5},{9,13},{5,1},{13,9},{2,6},{10,14},... | collective-permute-start | bytes 233480 | tf_op jit(solution)/shard_map/ppermute | solution.py:1237
  67.4 3.6 %collective-permute-done.16.refs_0_ = s16[272,128]{1,0:T(8,128)(2,1)S(1)} collective-permute-done((s16[272,128]{1,0:T(8,128)(2,1)S(1)}, s16[272,128]{1,0:T(8,128)(2,1)S(1)}, u32[]{:S(2)}, u32[]{:S(2)}) %collective-permute-start.16) | collective-permute-done | bytes 69664 | tf_op jit(solution)/shard_map/ppermute | solution.py:1239
  71.0 0.2 collective-permute-done.13.layers_ref
  71.3 0.4 borders.3.refs_1_
  71.7 1.9 %inverse.3 = (s16[672,128]{1,0:T(8,128)(2,1)S(1)}, s16[672,128]{1,0:T(8,128)(2,1)S(1)}, bf16[18,256,128]{2,1,0:T(8,128)(2,1)S(1)}, bf16[18,256,128]{2,1,0:T(8,128)(2,1)S(1)}) custom-call(f32[18,256,128]{2,1,0:T(8,128)S(1)} %get-tuple-element.92.refs_0_, f32[4,256,128]{2,1,0:T(8,128)S(1)} %borders.3.refs_1_, ...), custom_call_target="tpu_custom_call" | custom-call | flops 301989888 | bytes 4718592 | tf_op jit(solution)/shard_map/inverse/pallas_call | solution.py:954
  73.6 1.3 %collective-permute-start.19 = (s16[672,128]{1,0:T(8,128)(2,1)S(1)}, s16[672,128]{1,0:T(8,128)(2,1)S(1)}, u32[]{:S(2)}, u32[]{:S(2)}) collective-permute-start(s16[672,128]{1,0:T(8,128)(2,1)S(1)} %get-tuple-element.105), channel_id=1, source_target_pairs={{0,2},{1,3},{2,0},{3,1},{4,6},{5,7},{6,4},{7,5},{8,10},{9,11},{10,... | collective-permute-start | bytes 516104 | tf_op jit(solution)/shard_map/ppermute | solution.py:1223
  75.0 0.9 %inverse_rest.3 = (s16[672,128]{1,0:T(8,128)(2,1)S(1)}, s16[672,128]{1,0:T(8,128)(2,1)S(1)}) custom-call(bf16[18,256,128]{2,1,0:T(8,128)(2,1)S(1)} %get-tuple-element.100.field_high, bf16[18,256,128]{2,1,0:T(8,128)(2,1)S(1)} %get-tuple-element.101.field_low, bf16[4,48,256]{2,1,0:T(8,128)(2,1)S(1)} %copy-done.3, bf16[4,48,256]{2,1,0:T(8,128)(2,1)S(1)} %copy-done.4), custom_call_target="tpu_custom_call" | custom-call | flops 301989888 | bytes 4718592 | tf_op jit(solution)/shard_map/inverse_rest/pallas_call | solution.py:978
  75.8 0.1 collective-permute-start.17
  75.9 0.9 %collective-permute-start.18 = (s16[672,128]{1,0:T(8,128)(2,1)S(1)}, s16[672,128]{1,0:T(8,128)(2,1)S(1)}, u32[]{:S(2)}, u32[]{:S(2)}) collective-permute-start(s16[672,128]{1,0:T(8,128)(2,1)S(1)} %get-tuple-element.103), channel_id=1, source_target_pairs={{0,3},{1,2},{2,1},{3,0},{4,7},{5,6},{6,5},{7,4},{8,11},{9,10},{10,... | collective-permute-start | bytes 516104 | tf_op jit(solution)/shard_map/ppermute | solution.py:1223
  76.8 1.0 %near_field.3.refs_8_ = f32[8,128]{1,0:T(8,128)S(1)} custom-call(s32[24]{0:T(128)S(1)} %get-tuple-element.108.place_ref, s32[24]{0:T(128)S(1)} %get-tuple-element.107.target_ref, s16[432,128]{1,0:T(8,128)(2,1)S(1)} %collective-permute-done.15.even_ref.refs_2_.refs_0_, s16[592,128]{1,0:T(8,128)(2,1)S(1)} %collective-permute-done.14.odd_ref.refs_1_, ...), custom_call_target="tpu_custom_call" | custom-call | flops 12582912 | bytes 786432 | tf_op jit(solution)/shard_map/near_field/pallas_call | solution.py:1157
  77.8 1.8 %collective-permute-done.19.refs_1_ = s16[672,128]{1,0:T(8,128)(2,1)S(1)} collective-permute-done((s16[672,128]{1,0:T(8,128)(2,1)S(1)}, s16[672,128]{1,0:T(8,128)(2,1)S(1)}, u32[]{:S(2)}, u32[]{:S(2)}) %collective-permute-start.19) | collective-permute-done | bytes 172064 | tf_op jit(solution)/shard_map/ppermute | solution.py:1223
  79.7 0.4 sample_early.3.refs_2_
  80.1 2.6 %collective-permute-done.18.refs_1_ = s16[672,128]{1,0:T(8,128)(2,1)S(1)} collective-permute-done((s16[672,128]{1,0:T(8,128)(2,1)S(1)}, s16[672,128]{1,0:T(8,128)(2,1)S(1)}, u32[]{:S(2)}, u32[]{:S(2)}) %collective-permute-start.18) | collective-permute-done | bytes 172064 | tf_op jit(solution)/shard_map/ppermute | solution.py:1223
  82.7 2.7 %sample.3 = f32[2,512]{1,0:T(2,128)} custom-call(s32[2,512]{1,0:T(2,128)S(1)} %get-tuple-element.56.place_ref.place_in.refs_1_, s16[672,128]{1,0:T(8,128)(2,1)S(1)} %collective-permute-done.17.refs_0_, s16[672,128]{1,0:T(8,128)(2,1)S(1)} %collective-permute-done.18.refs_1_, f32[656,256]{1,0:T(8,128)S(1)} %sample_early.3.refs_2_, ...), custom_call_target="tpu_custom_call" | custom-call | flops 169869312 | bytes 4194304 | tf_op jit(solution)/shard_map/sample/pallas_call | solution.py:1099
  (26 shorter events, 0.2 us)
Async XLA Ops:
  5.0 9.2 %collective-permute-start.1 = (s16[672,128]{1,0:T(8,128)(2,1)S(1)}, s16[672,128]{1,0:T(8,128)(2,1)S(1)}, u32[]{:S(2)}, u32[]{:S(2)}) collective-permute-start(s16[672,128]{1,0:T(8,128)(2,1)S(1)} %get-tuple-element.64), channel_id=1, source_target_pairs={{0,2},{1,3},{2,0},{3,1},{4,6},{5,7},{6,4},{7,5},{8,10},{9,11},{10,... | collective-permute-start | bytes 516104 | tf_op jit(solution)/shard_map/ppermute | solution.py:1223
  8.6 6.3 %collective-permute-start = (s16[672,128]{1,0:T(8,128)(2,1)S(1)}, s16[672,128]{1,0:T(8,128)(2,1)S(1)}, u32[]{:S(2)}, u32[]{:S(2)}) collective-permute-start(s16[672,128]{1,0:T(8,128)(2,1)S(1)} %get-tuple-element.63), channel_id=1, source_target_pairs={{0,1},{1,0},{2,3},{3,2},{4,5},{5,4},{6,7},{7,6},{8,9},{9,8},{10,11... | collective-permute-start | bytes 516104 | tf_op jit(solution)/shard_map/ppermute | solution.py:1223
  8.7 6.8 %collective-permute-start.2 = (s16[672,128]{1,0:T(8,128)(2,1)S(1)}, s16[672,128]{1,0:T(8,128)(2,1)S(1)}, u32[]{:S(2)}, u32[]{:S(2)}) collective-permute-start(s16[672,128]{1,0:T(8,128)(2,1)S(1)} %get-tuple-element.65), channel_id=1, source_target_pairs={{0,3},{1,2},{2,1},{3,0},{4,7},{5,6},{6,5},{7,4},{8,11},{9,10},{10,... | collective-permute-start | bytes 516104 | tf_op jit(solution)/shard_map/ppermute | solution.py:1223
  8.8 0.9 %copy-start.1 = (f32[64,512]{1,0:T(8,128)S(1)}, f32[64,512]{1,0:T(8,128)}, u32[]{:S(2)}) copy-start(f32[64,512]{1,0:T(8,128)} %refs_3_.8) | copy-start | bytes 393220
  9.7 4.5 %copy-start = (bf16[2,256,240]{2,1,0:T(8,128)(2,1)S(1)}, bf16[2,256,240]{2,1,0:T(8,128)(2,1)}, u32[]{:S(2)}) copy-start(bf16[2,256,240]{2,1,0:T(8,128)(2,1)} %constant.76.clone.refs_2_.refs_6_.table_ref) | copy-start | bytes 737284
  16.8 5.6 %collective-permute-start.5 = (s16[432,128]{1,0:T(8,128)(2,1)S(1)}, s16[432,128]{1,0:T(8,128)(2,1)S(1)}, u32[]{:S(2)}, u32[]{:S(2)}) collective-permute-start(s16[432,128]{1,0:T(8,128)(2,1)S(1)} %get-tuple-element.73), channel_id=1, source_target_pairs={{0,4},{8,12},{4,0},{12,8},{1,5},{9,13},{5,1},{13,9},{2,6},{10,14},... | collective-permute-start | bytes 331784 | tf_op jit(solution)/shard_map/ppermute | solution.py:1235
  18.5 8.5 %collective-permute-start.4 = (s16[592,128]{1,0:T(8,128)(2,1)S(1)}, s16[592,128]{1,0:T(8,128)(2,1)S(1)}, u32[]{:S(2)}, u32[]{:S(2)}) collective-permute-start(s16[592,128]{1,0:T(8,128)(2,1)S(1)} %get-tuple-element.70), channel_id=1, source_target_pairs={{4,8},{8,4},{5,9},{9,5},{6,10},{10,6},{7,11},{11,7},{20,24},{24,20... | collective-permute-start | bytes 454664 | tf_op jit(solution)/shard_map/ppermute | solution.py:1236
  22.5 8.0 %collective-permute-start.6 = (s16[272,128]{1,0:T(8,128)(2,1)S(1)}, s16[272,128]{1,0:T(8,128)(2,1)S(1)}, u32[]{:S(2)}, u32[]{:S(2)}) collective-permute-start(s16[272,128]{1,0:T(8,128)(2,1)S(1)} %pair_messages.2), channel_id=1, source_target_pairs={{0,8},{4,12},{8,0},{12,4},{1,9},{5,13},{9,1},{13,5},{2,10},{6,14},... | collective-permute-start | bytes 208904 | tf_op jit(solution)/shard_map/ppermute | solution.py:1239
  25.3 5.5 %collective-permute-start.3 = (s16[304,128]{1,0:T(8,128)(2,1)S(1)}, s16[304,128]{1,0:T(8,128)(2,1)S(1)}, u32[]{:S(2)}, u32[]{:S(2)}) collective-permute-start(s16[304,128]{1,0:T(8,128)(2,1)S(1)} %get-tuple-element.69), channel_id=1, source_target_pairs={{0,4},{8,12},{4,0},{12,8},{1,5},{9,13},{5,1},{13,9},{2,6},{10,14},... | collective-permute-start | bytes 233480 | tf_op jit(solution)/shard_map/ppermute | solution.py:1237
  30.5 0.9 %copy-start.3 = (bf16[4,48,256]{2,1,0:T(8,128)(2,1)S(1)}, bf16[4,48,256]{2,1,0:T(8,128)(2,1)}, u32[]{:S(2)}) copy-start(bf16[4,48,256]{2,1,0:T(8,128)(2,1)} %constant.77.clone.refs_7_.high_ref) | copy-start | bytes 294916
  30.5 0.9 %copy-start.4 = (bf16[4,48,256]{2,1,0:T(8,128)(2,1)S(1)}, bf16[4,48,256]{2,1,0:T(8,128)(2,1)}, u32[]{:S(2)}) copy-start(bf16[4,48,256]{2,1,0:T(8,128)(2,1)} %constant.78.clone.refs_8_.low_ref) | copy-start | bytes 294916
  31.3 3.7 %copy-start.8 = (s32[24]{0:T(128)S(1)}, s32[24]{0:T(128)}, u32[]{:S(2)}) copy-start(s32[24]{0:T(128)} %param.21) | copy-start | bytes 292
  31.3 3.6 %copy-start.9 = (s32[24]{0:T(128)S(1)}, s32[24]{0:T(128)}, u32[]{:S(2)}) copy-start(s32[24]{0:T(128)} %param.22) | copy-start | bytes 292
  31.5 5.1 %copy-start.2 = (bf16[24,128,128]{2,1,0:T(8,128)(2,1)S(1)}, bf16[24,128,128]{2,1,0:T(8,128)(2,1)}, u32[]{:S(2)}) copy-start(bf16[24,128,128]{2,1,0:T(8,128)(2,1)} %refs_3_.10) | copy-start | bytes 2359300
  33.4 7.2 %collective-permute-start.9 = (s16[672,128]{1,0:T(8,128)(2,1)S(1)}, s16[672,128]{1,0:T(8,128)(2,1)S(1)}, u32[]{:S(2)}, u32[]{:S(2)}) collective-permute-start(s16[672,128]{1,0:T(8,128)(2,1)S(1)} %get-tuple-element.81), channel_id=1, source_target_pairs={{0,2},{1,3},{2,0},{3,1},{4,6},{5,7},{6,4},{7,5},{8,10},{9,11},{10,... | collective-permute-start | bytes 516104 | tf_op jit(solution)/shard_map/ppermute | solution.py:1223
  35.8 5.2 %collective-permute-start.7 = (s16[672,128]{1,0:T(8,128)(2,1)S(1)}, s16[672,128]{1,0:T(8,128)(2,1)S(1)}, u32[]{:S(2)}, u32[]{:S(2)}) collective-permute-start(s16[672,128]{1,0:T(8,128)(2,1)S(1)} %get-tuple-element.78), channel_id=1, source_target_pairs={{0,1},{1,0},{2,3},{3,2},{4,5},{5,4},{6,7},{7,6},{8,9},{9,8},{10,11... | collective-permute-start | bytes 516104 | tf_op jit(solution)/shard_map/ppermute | solution.py:1223
  35.9 6.8 %collective-permute-start.8 = (s16[672,128]{1,0:T(8,128)(2,1)S(1)}, s16[672,128]{1,0:T(8,128)(2,1)S(1)}, u32[]{:S(2)}, u32[]{:S(2)}) collective-permute-start(s16[672,128]{1,0:T(8,128)(2,1)S(1)} %get-tuple-element.79), channel_id=1, source_target_pairs={{0,3},{1,2},{2,1},{3,0},{4,7},{5,6},{6,5},{7,4},{8,11},{9,10},{10,... | collective-permute-start | bytes 516104 | tf_op jit(solution)/shard_map/ppermute | solution.py:1223
  37.6 3.0 %copy-start.5 = (bf16[4,128,256]{2,1,0:T(8,128)(2,1)S(1)}, bf16[4,128,256]{2,1,0:T(8,128)(2,1)}, u32[]{:S(2)}) copy-start(bf16[4,128,256]{2,1,0:T(8,128)(2,1)} %constant.79.clone.refs_2_.refs_3_) | copy-start | bytes 786436
  37.6 3.0 %copy-start.6 = (bf16[4,128,256]{2,1,0:T(8,128)(2,1)S(1)}, bf16[4,128,256]{2,1,0:T(8,128)(2,1)}, u32[]{:S(2)}) copy-start(bf16[4,128,256]{2,1,0:T(8,128)(2,1)} %constant.80.clone.refs_3_.refs_4_) | copy-start | bytes 786436
  40.6 2.1 %copy-start.7 = (s32[512]{0:T(512)S(1)}, s32[512]{0:T(512)}, u32[]{:S(2)}) copy-start(s32[512]{0:T(512)} %param.17) | copy-start | bytes 6148
  47.5 7.3 %collective-permute-start.11 = (s16[672,128]{1,0:T(8,128)(2,1)S(1)}, s16[672,128]{1,0:T(8,128)(2,1)S(1)}, u32[]{:S(2)}, u32[]{:S(2)}) collective-permute-start(s16[672,128]{1,0:T(8,128)(2,1)S(1)} %get-tuple-element.88), channel_id=1, source_target_pairs={{0,2},{1,3},{2,0},{3,1},{4,6},{5,7},{6,4},{7,5},{8,10},{9,11},{10,... | collective-permute-start | bytes 516104 | tf_op jit(solution)/shard_map/ppermute | solution.py:1223
  48.8 6.7 %collective-permute-start.10 = (s16[672,128]{1,0:T(8,128)(2,1)S(1)}, s16[672,128]{1,0:T(8,128)(2,1)S(1)}, u32[]{:S(2)}, u32[]{:S(2)}) collective-permute-start(s16[672,128]{1,0:T(8,128)(2,1)S(1)} %get-tuple-element.87), channel_id=1, source_target_pairs={{0,1},{1,0},{2,3},{3,2},{4,5},{5,4},{6,7},{7,6},{8,9},{9,8},{10,11... | collective-permute-start | bytes 516104 | tf_op jit(solution)/shard_map/ppermute | solution.py:1223
  49.7 7.4 %collective-permute-start.12 = (s16[672,128]{1,0:T(8,128)(2,1)S(1)}, s16[672,128]{1,0:T(8,128)(2,1)S(1)}, u32[]{:S(2)}, u32[]{:S(2)}) collective-permute-start(s16[672,128]{1,0:T(8,128)(2,1)S(1)} %get-tuple-element.89), channel_id=1, source_target_pairs={{0,3},{1,2},{2,1},{3,0},{4,7},{5,6},{6,5},{7,4},{8,11},{9,10},{10,... | collective-permute-start | bytes 516104 | tf_op jit(solution)/shard_map/ppermute | solution.py:1223
  58.4 5.6 %collective-permute-start.15 = (s16[432,128]{1,0:T(8,128)(2,1)S(1)}, s16[432,128]{1,0:T(8,128)(2,1)S(1)}, u32[]{:S(2)}, u32[]{:S(2)}) collective-permute-start(s16[432,128]{1,0:T(8,128)(2,1)S(1)} %get-tuple-element.97), channel_id=1, source_target_pairs={{0,4},{8,12},{4,0},{12,8},{1,5},{9,13},{5,1},{13,9},{2,6},{10,14},... | collective-permute-start | bytes 331784 | tf_op jit(solution)/shard_map/ppermute | solution.py:1235
  58.6 8.8 %collective-permute-start.14 = (s16[592,128]{1,0:T(8,128)(2,1)S(1)}, s16[592,128]{1,0:T(8,128)(2,1)S(1)}, u32[]{:S(2)}, u32[]{:S(2)}) collective-permute-start(s16[592,128]{1,0:T(8,128)(2,1)S(1)} %get-tuple-element.94), channel_id=1, source_target_pairs={{4,8},{8,4},{5,9},{9,5},{6,10},{10,6},{7,11},{11,7},{20,24},{24,20... | collective-permute-start | bytes 454664 | tf_op jit(solution)/shard_map/ppermute | solution.py:1236
  64.1 6.9 %collective-permute-start.16 = (s16[272,128]{1,0:T(8,128)(2,1)S(1)}, s16[272,128]{1,0:T(8,128)(2,1)S(1)}, u32[]{:S(2)}, u32[]{:S(2)}) collective-permute-start(s16[272,128]{1,0:T(8,128)(2,1)S(1)} %pair_messages.3), channel_id=1, source_target_pairs={{0,8},{4,12},{8,0},{12,4},{1,9},{5,13},{9,1},{13,5},{2,10},{6,14},... | collective-permute-start | bytes 208904 | tf_op jit(solution)/shard_map/ppermute | solution.py:1239
  65.6 5.7 %collective-permute-start.13 = (s16[304,128]{1,0:T(8,128)(2,1)S(1)}, s16[304,128]{1,0:T(8,128)(2,1)S(1)}, u32[]{:S(2)}, u32[]{:S(2)}) collective-permute-start(s16[304,128]{1,0:T(8,128)(2,1)S(1)} %get-tuple-element.93), channel_id=1, source_target_pairs={{0,4},{8,12},{4,0},{12,8},{1,5},{9,13},{5,1},{13,9},{2,6},{10,14},... | collective-permute-start | bytes 233480 | tf_op jit(solution)/shard_map/ppermute | solution.py:1237
  73.6 6.1 %collective-permute-start.19 = (s16[672,128]{1,0:T(8,128)(2,1)S(1)}, s16[672,128]{1,0:T(8,128)(2,1)S(1)}, u32[]{:S(2)}, u32[]{:S(2)}) collective-permute-start(s16[672,128]{1,0:T(8,128)(2,1)S(1)} %get-tuple-element.105), channel_id=1, source_target_pairs={{0,2},{1,3},{2,0},{3,1},{4,6},{5,7},{6,4},{7,5},{8,10},{9,11},{10,... | collective-permute-start | bytes 516104 | tf_op jit(solution)/shard_map/ppermute | solution.py:1223
  75.8 4.3 %collective-permute-start.17 = (s16[672,128]{1,0:T(8,128)(2,1)S(1)}, s16[672,128]{1,0:T(8,128)(2,1)S(1)}, u32[]{:S(2)}, u32[]{:S(2)}) collective-permute-start(s16[672,128]{1,0:T(8,128)(2,1)S(1)} %get-tuple-element.102), channel_id=1, source_target_pairs={{0,1},{1,0},{2,3},{3,2},{4,5},{5,4},{6,7},{7,6},{8,9},{9,8},{10,11... | collective-permute-start | bytes 516104 | tf_op jit(solution)/shard_map/ppermute | solution.py:1223
  75.9 6.8 %collective-permute-start.18 = (s16[672,128]{1,0:T(8,128)(2,1)S(1)}, s16[672,128]{1,0:T(8,128)(2,1)S(1)}, u32[]{:S(2)}, u32[]{:S(2)}) collective-permute-start(s16[672,128]{1,0:T(8,128)(2,1)S(1)} %get-tuple-element.103), channel_id=1, source_target_pairs={{0,3},{1,2},{2,1},{3,0},{4,7},{5,6},{6,5},{7,4},{8,11},{9,10},{10,... | collective-permute-start | bytes 516104 | tf_op jit(solution)/shard_map/ppermute | solution.py:1223

commit v18 on v15

--- a/solution.py
+++ b/solution.py
@@ -16,6 +16,7 @@
 KERNEL_GAIN = 4.0
 SCREEN = 1.0 / 1024.0
 LN2 = math.log(2.0)
+ROUNDING = 1.5 * 2.0**23
 Y_AXES = ("narrow", "pair")
 ALL_AXES = ("wide", "narrow", "pair")
 F32 = jnp.float32
@@ -96,7 +97,8 @@
 
 
 def quantize(values, exponent, fraction):
-    return to_short(jnp.round(values * (32767.0 / full_scale(exponent, fraction))))
+    scaled = values * (32767.0 / full_scale(exponent, fraction))
+    return to_short((scaled + ROUNDING) - ROUNDING)
 
 
 def unit(exponent, fraction):
@@ -613,7 +615,7 @@
         transform_pieces(table_ref[lax.axis_index("pair") ^ core], stacked, before, spectrum)
         before = spectrum
 
-    chunk = 128
+    chunk = 256
 
     def body(index, largest):
         rows = pl.ds(pl.multiple_of(index * chunk, chunk), chunk)
@@ -675,8 +677,8 @@
 
         @pl.when(on_left == side)
         def _():
-            send(even_out, top, [(slabs[even], largest[even]), with_most(packed[even])])
-            send(layers_out, 16, [with_most(edges[1 - even])])
+            send(even_out, 16, [(slabs[even], largest[even]), with_most(packed[even])])
+            send(layers_out, top, [with_most(edges[1 - even])])
             send(odd_out, top, [(slabs[odd], largest[odd]), with_most(edges[1 - odd])])
 
 
@@ -695,8 +697,8 @@
         out_specs=[whole_vmem()] * 7,
         out_shape=[
             jax.ShapeDtypeStruct((half, GRID, lanes), F32),
-            short(head + GRID + GRID // 2),
-            short(16 + border),
+            short(16 + GRID + GRID // 2),
+            short(head + border),
             short(head + GRID + border),
             jax.ShapeDtypeStruct((GRID, lanes), F32),
             jax.ShapeDtypeStruct((pieces * blocks, BLOCK), F32),
@@ -767,7 +769,7 @@
     on_left = (lax.axis_index("wide") & 1) == 1
     pair = lax.axis_size("pair")
     rows = pieces * 2 * reach_y
-    even = opened_part(layers_ref, 0, 16, rows)
+    even = opened_part(layers_ref, 0, layers_ref.shape[0] - rows, rows)
     odd = opened_part(odd_ref, 1, odd_ref.shape[0] - rows, rows)
     left, right = jnp.where(on_left, even, odd), jnp.where(on_left, odd, even)
     low = low_lanes(rows)
@@ -838,8 +840,9 @@
     field_high, field_low, ready, head = refs[3 + len(flips) :]
     half = reach_x // 2
     span = reach_x - 4
-    chunk = 128
-    head_rows = from_even.shape[0] - GRID - GRID // 2
+    chunk = 256
+    border_rows = lax.axis_size("narrow") * lax.axis_size("pair") * 2 * reach_y
+    tops = from_even.shape[0] - GRID - GRID // 2, from_odd.shape[0] - GRID - border_rows
     on_left = (lax.axis_index("wide") & 1) == 1
     moment_units = []
     for ref in (from_even, from_odd):
@@ -865,9 +868,9 @@
         beside = jnp.exp((GRID - reach_x - span) * log_decay)
         layers = [spectrum[i, rows, :] for i in range(half)]
 
-        at = pl.ds(pl.multiple_of(head_rows + index * chunk, 16), chunk)
         even, odd = (
-            from_short(ref[at, :]) * scale for ref, scale in zip((from_even, from_odd), moment_units)
+            from_short(ref[pl.ds(pl.multiple_of(top + index * chunk, 16), chunk), :]) * scale
+            for ref, top, scale in zip((from_even, from_odd), tops, moment_units)
         )
         left_moments, right_moments = jnp.where(on_left, even, odd), jnp.where(on_left, odd, even)
         border = [border_ref[i, rows, :] for i in range(4)]
@@ -1225,7 +1228,7 @@
         )
         then = inverse_rest((high, low), y_inverse, reach_y, rest)
         near_part = near_field(
-            sources, targets, from_even, from_odd, peers, near_tiles, blocks, out_rows, then[:1]
+            sources, targets, even_layers, from_odd, peers, near_tiles, blocks, out_rows, then[:1]
         )
         arrived = turned(sent, then)
         image = sample(

time: 85.2 us -> 84.8 us (level)
  transfers between devices with their start and end apart: 20 -> 20, of which waited for: 10 -> 10; matrix products, arithmetic and copies ran while one was open for 1% -> 1% of each run, Pallas kernels for 17% -> 18%
where the time goes in v18:
time: 84.8 us; the launch traced here: 84.6 us
  Pallas kernels  34.7 us (41%)
  starting transfers between devices  24.5 us (29%)
  waiting for transfers between devices  22.9 us (27%)
  local copies, waits for them, and re-layouts  2.02 us (2%)
    ppermute x12, waiting for transfers between devices, turned(): lax.ppermute(part, Y_AXES, swap_pairs)  12.8 us
    ppermute x12, starting transfers between devices, turned(): lax.ppermute(part, Y_AXES, swap_pairs)  10.1 us
    ppermute x2, starting transfers between devices, convolve_and_sample(): even_layers = lax.ppermute(layers, 'wide', even_swap)  8.87 us
    pallas_call x2, Pallas kernels, spread(): pl.pallas_call(functools.partial(start_kernel if placed is None else spre...  7.86 us
    ppermute x2, waiting for transfers between devices, convolve_and_sample(): lax.ppermute(message, 'wide', [(i, i ^ flip) for i in range(x_count)])  7.1 us
    pallas_call x2, Pallas kernels, sample(): pl.pallas_call(functools.partial(sample_kernel, last, reach_x, reach_y, f...  4.87 us
    pallas_call x2, Pallas kernels, inverse(): pl.pallas_call(functools.partial(inverse_kernel, reach_x, reach_y, flips,...  4.02 us
    pallas_call x1, Pallas kernels, place_sample_lines(): pl.pallas_call(functools.partial(sample_lines_kernel, blocks), grid=(1,),...  3.41 us
  transfers between devices with their start and end apart: 20, of which 10 were waited for; matrix products, arithmetic and copies ran while one was open for 1% of the time, Pallas kernels for 18%

profile of v18, /device:TPU:0, one launch (start us, length us, event | category | flops | bytes accessed | tf_op | source)
XLA Modules:
  0.0 84.6 jit_solution(13267018956750447567)
XLA Ops:
  0.0 5.1 %start.1 = (s16[672,128]{1,0:T(8,128)(2,1)S(1)}, s16[672,128]{1,0:T(8,128)(2,1)S(1)}, bf16[656,256]{1,0:T(8,128)(2,1)S(1)}, bf16[656,256]{1,0:T(8,128)(2,1)S(1)}...) custom-call(f32[512]{0:T(512)} %refs_0_.2, ...), custom_call_target="tpu_custom_call" | custom-call | flops 169869312 | bytes 4194304 | tf_op jit(solution)/shard_map/start/pallas_call | solution.py:413
  5.1 3.0 %collective-permute-start.1 = (s16[672,128]{1,0:T(8,128)(2,1)S(1)}, s16[672,128]{1,0:T(8,128)(2,1)S(1)}, u32[]{:S(2)}, u32[]{:S(2)}) collective-permute-start(s16[672,128]{1,0:T(8,128)(2,1)S(1)} %get-tuple-element.60), channel_id=1, source_target_pairs={{0,2},{1,3},{2,0},{3,1},{4,6},{5,7},{6,4},{7,5},{8,10},{9,11},{10,... | collective-permute-start | bytes 516104 | tf_op jit(solution)/shard_map/ppermute | solution.py:1194
  8.1 0.6 spread_rest.2
  8.8 0.1 collective-permute-start
  8.9 0.1 collective-permute-start.2
  9.0 0.9 %copy-done.1 = f32[64,512]{1,0:T(8,128)S(1)} copy-done((f32[64,512]{1,0:T(8,128)S(1)}, f32[64,512]{1,0:T(8,128)}, u32[]{:S(2)}) %copy-start.1) | copy-done | bytes 131096
  9.9 3.4 %place_sample_lines.1.refs_8_.refs_5_ = f32[8192,128]{1,0:T(8,128)S(1)} custom-call(s32[2,512]{1,0:T(2,128)S(1)} %get-tuple-element.52.place_ref.place_in.refs_1_, f32[64,512]{1,0:T(8,128)S(1)} %copy-done.1, f32[64,512]{1,0:T(8,128)S(1)} %copy-done.1, f32[64,512]{1,0:T(8,128)S(1)} %copy-done.1, f32[64,512]{1,0:T(8,128)S(1)} %copy-done.1), custom_call_target="tpu_custom_call" | custom-call | flops 1048576 | bytes 4194304 | tf_op jit(solution)/shard_map/place_sample_lines/pallas_call | solution.py:482
  13.3 1.1 %dynamic-slice_bitcast_fusion.refs_7_.modes_ref.refs_9_ = f32[4,256,128]{2,1,0:T(8,128)S(1)} fusion(f32[4,4,256,128]{3,2,1,0:T(8,128)} %constant.73.clone, s32[]{:T(128)S(6)} %select_n.30), kind=kLoop, calls=%fused_computation | loop fusion | bytes 1048580 | tf_op jit(solution)/shard_map/jit(dynamic_index_in_dim)/squeeze | solution.py:1171
  14.4 0.0 collective-permute-done.1.refs_1_.refs_2_
  14.4 0.7 forward_early.2
  15.1 0.0 collective-permute-done.refs_1_
  15.1 0.6 collective-permute-done.2.refs_3_
  15.7 1.4 %forward.2 = (f32[18,256,128]{2,1,0:T(8,128)S(1)}, s16[400,128]{1,0:T(8,128)(2,1)S(1)}, s16[336,128]{1,0:T(8,128)(2,1)S(1)}, s16[592,128]{1,0:T(8,128)(2,1)S(1)}...) custom-call(s16[672,128]{1,0:T(8,128)(2,1)S(1)} %get-tuple-element.58.refs_0_, ...), custom_call_target="tpu_custom_call" | custom-call | flops 301989888 | bytes 4718592 | tf_op jit(solution)/shard_map/forward/pallas_call | solution.py:692
  17.1 1.6 %collective-permute-start.5 = (s16[400,128]{1,0:T(8,128)(2,1)S(1)}, s16[400,128]{1,0:T(8,128)(2,1)S(1)}, u32[]{:S(2)}, u32[]{:S(2)}) collective-permute-start(s16[400,128]{1,0:T(8,128)(2,1)S(1)} %get-tuple-element.67), channel_id=1, source_target_pairs={{0,4},{8,12},{4,0},{12,8},{1,5},{9,13},{5,1},{13,9},{2,6},{10,14},... | collective-permute-start | bytes 307208 | tf_op jit(solution)/shard_map/ppermute | solution.py:1206
  18.7 0.8 collective-permute-start.4
  19.6 4.4 %collective-permute-start.3 = (s16[336,128]{1,0:T(8,128)(2,1)S(1)}, s16[336,128]{1,0:T(8,128)(2,1)S(1)}, u32[]{:S(2)}, u32[]{:S(2)}) collective-permute-start(s16[336,128]{1,0:T(8,128)(2,1)S(1)} %get-tuple-element.65), channel_id=1, source_target_pairs={{0,4},{8,12},{4,0},{12,8},{1,5},{9,13},{5,1},{13,9},{2,6},{10,14},... | collective-permute-start | bytes 258056 | tf_op jit(solution)/shard_map/ppermute | solution.py:1208
  24.0 0.0 collective-permute-done.5.even_ref.refs_2_
  24.0 0.2 pair_messages.2
  24.2 0.0 copy-start.8
  24.2 0.0 copy-start.9
  24.2 1.2 %collective-permute-start.6 = (s16[272,128]{1,0:T(8,128)(2,1)S(1)}, s16[272,128]{1,0:T(8,128)(2,1)S(1)}, u32[]{:S(2)}, u32[]{:S(2)}) collective-permute-start(s16[272,128]{1,0:T(8,128)(2,1)S(1)} %pair_messages.2), channel_id=1, source_target_pairs={{0,8},{4,12},{8,0},{12,4},{1,9},{5,13},{9,1},{13,5},{2,10},{6,14},... | collective-permute-start | bytes 208904 | tf_op jit(solution)/shard_map/ppermute | solution.py:1210
  25.4 1.4 %collective-permute-done.3.layers_ref.refs_0_ = s16[336,128]{1,0:T(8,128)(2,1)S(1)} collective-permute-done((s16[336,128]{1,0:T(8,128)(2,1)S(1)}, s16[336,128]{1,0:T(8,128)(2,1)S(1)}, u32[]{:S(2)}, u32[]{:S(2)}) %collective-permute-start.3) | collective-permute-done | bytes 86048 | tf_op jit(solution)/shard_map/ppermute | solution.py:1208
  26.7 0.0 collective-permute-done.4.odd_ref.refs_3_.refs_1_
  26.7 0.4 borders.2.refs_1_
  27.2 3.4 %collective-permute-done.6.refs_6_ = s16[272,128]{1,0:T(8,128)(2,1)S(1)} collective-permute-done((s16[272,128]{1,0:T(8,128)(2,1)S(1)}, s16[272,128]{1,0:T(8,128)(2,1)S(1)}, u32[]{:S(2)}, u32[]{:S(2)}) %collective-permute-start.6) | collective-permute-done | bytes 69664 | tf_op jit(solution)/shard_map/ppermute | solution.py:1210
  30.6 2.0 %inverse.2 = (s16[672,128]{1,0:T(8,128)(2,1)S(1)}, s16[672,128]{1,0:T(8,128)(2,1)S(1)}, bf16[18,256,128]{2,1,0:T(8,128)(2,1)S(1)}, bf16[18,256,128]{2,1,0:T(8,128)(2,1)S(1)}) custom-call(f32[18,256,128]{2,1,0:T(8,128)S(1)} %get-tuple-element.64.refs_0_, f32[4,256,128]{2,1,0:T(8,128)S(1)} %borders.2.refs_1_, ...), custom_call_target="tpu_custom_call" | custom-call | flops 301989888 | bytes 4718592 | tf_op jit(solution)/shard_map/inverse/pallas_call | solution.py:925
  32.6 1.6 %collective-permute-start.9 = (s16[672,128]{1,0:T(8,128)(2,1)S(1)}, s16[672,128]{1,0:T(8,128)(2,1)S(1)}, u32[]{:S(2)}, u32[]{:S(2)}) collective-permute-start(s16[672,128]{1,0:T(8,128)(2,1)S(1)} %get-tuple-element.75), channel_id=1, source_target_pairs={{0,2},{1,3},{2,0},{3,1},{4,6},{5,7},{6,4},{7,5},{8,10},{9,11},{10,... | collective-permute-start | bytes 516104 | tf_op jit(solution)/shard_map/ppermute | solution.py:1194
  34.2 1.0 %inverse_rest.2 = (s16[672,128]{1,0:T(8,128)(2,1)S(1)}, s16[672,128]{1,0:T(8,128)(2,1)S(1)}) custom-call(bf16[18,256,128]{2,1,0:T(8,128)(2,1)S(1)} %get-tuple-element.70.field_high, bf16[18,256,128]{2,1,0:T(8,128)(2,1)S(1)} %get-tuple-element.71.field_low, bf16[4,48,256]{2,1,0:T(8,128)(2,1)S(1)} %copy-done.3, bf16[4,48,256]{2,1,0:T(8,128)(2,1)S(1)} %copy-done.4), custom_call_target="tpu_custom_call" | custom-call | flops 301989888 | bytes 4718592 | tf_op jit(solution)/shard_map/inverse_rest/pallas_call | solution.py:949
  35.2 0.1 collective-permute-start.7
  35.2 0.7 collective-permute-start.8
  35.9 1.0 %near_field.2.refs_8_.refs_0_ = f32[8,128]{1,0:T(8,128)S(1)} custom-call(s32[24]{0:T(128)S(1)} %get-tuple-element.100.place_ref, s32[24]{0:T(128)S(1)} %get-tuple-element.99.target_ref, s16[336,128]{1,0:T(8,128)(2,1)S(1)} %collective-permute-done.3.layers_ref.refs_0_, s16[592,128]{1,0:T(8,128)(2,1)S(1)} %collective-permute-done.4.odd_ref.refs_3_.refs_1_, ...), custom_call_target="tpu_custom_call" | custom-call | flops 12582912 | bytes 786432 | tf_op jit(solution)/shard_map/near_field/pallas_call | solution.py:1128
  37.0 3.0 %place_lines.1.refs_5_ = f32[8192,128]{1,0:T(8,128)S(1)} custom-call(s32[2,512]{1,0:T(2,128)S(1)} %get-tuple-element.52.place_ref.place_in.refs_1_, f32[256,128]{1,0:T(8,128)S(1)} %get-tuple-element.77.coeff_ref, f32[8,128]{1,0:T(8,128)S(1)} %near_field.2.refs_8_.refs_0_), custom_call_target="tpu_custom_call" | custom-call | flops 1048576 | bytes 4194304 | tf_op jit(solution)/shard_map/place_lines/pallas_call | solution.py:498
  39.9 0.0 collective-permute-done.9.refs_1_
  40.0 0.4 sample_early.2.refs_2_
  40.4 1.6 %collective-permute-done.8.refs_1_ = s16[672,128]{1,0:T(8,128)(2,1)S(1)} collective-permute-done((s16[672,128]{1,0:T(8,128)(2,1)S(1)}, s16[672,128]{1,0:T(8,128)(2,1)S(1)}, u32[]{:S(2)}, u32[]{:S(2)}) %collective-permute-start.8) | collective-permute-done | bytes 172064 | tf_op jit(solution)/shard_map/ppermute | solution.py:1194
  42.0 2.1 %sample.2.refs_2_.rounded_ref.refs_7_ = f32[4,128]{1,0:T(4,128)S(1)} custom-call(s32[2,512]{1,0:T(2,128)S(1)} %get-tuple-element.52.place_ref.place_in.refs_1_, s16[672,128]{1,0:T(8,128)(2,1)S(1)} %collective-permute-done.7.refs_0_, s16[672,128]{1,0:T(8,128)(2,1)S(1)} %collective-permute-done.8.refs_1_, f32[656,256]{1,0:T(8,128)S(1)} %sample_early.2.refs_2_, ...), custom_call_target="tpu_custom_call" | custom-call | flops 169869312 | bytes 4194304 | tf_op jit(solution)/shard_map/sample/pallas_call | solution.py:1070
  44.2 2.7 %spread.1 = (s16[672,128]{1,0:T(8,128)(2,1)S(1)}, s16[672,128]{1,0:T(8,128)(2,1)S(1)}, bf16[656,256]{1,0:T(8,128)(2,1)S(1)}, bf16[656,256]{1,0:T(8,128)(2,1)S(1)}) custom-call(f32[512]{0:T(512)S(1)} %bitcast.6, s32[2,512]{1,0:T(2,128)S(1)} %get-tuple-element.52.place_ref.place_in.refs_1_, f32[4,128]{1,0:T(4,128)S(1)} %sample.2.refs_2_.rounded_ref.refs_7_, ...), custom_call_target="tpu_custom_call" | custom-call | flops 169869312 | bytes 4194304 | tf_op jit(solution)/shard_map/spread/pallas_call | solution.py:413
  46.9 1.1 %collective-permute-start.11 = (s16[672,128]{1,0:T(8,128)(2,1)S(1)}, s16[672,128]{1,0:T(8,128)(2,1)S(1)}, u32[]{:S(2)}, u32[]{:S(2)}) collective-permute-start(s16[672,128]{1,0:T(8,128)(2,1)S(1)} %get-tuple-element.82), channel_id=1, source_target_pairs={{0,2},{1,3},{2,0},{3,1},{4,6},{5,7},{6,4},{7,5},{8,10},{9,11},{10,... | collective-permute-start | bytes 516104 | tf_op jit(solution)/shard_map/ppermute | solution.py:1194
  48.1 0.6 spread_rest.3
  48.7 0.6 collective-permute-start.10
  49.3 0.6 collective-permute-start.12
  49.9 4.3 %collective-permute-done.11.refs_1_.refs_2_ = s16[672,128]{1,0:T(8,128)(2,1)S(1)} collective-permute-done((s16[672,128]{1,0:T(8,128)(2,1)S(1)}, s16[672,128]{1,0:T(8,128)(2,1)S(1)}, u32[]{:S(2)}, u32[]{:S(2)}) %collective-permute-start.11) | collective-permute-done | bytes 172064 | tf_op jit(solution)/shard_map/ppermute | solution.py:1194
  54.2 0.7 forward_early.3
  54.9 1.9 %collective-permute-done.12.refs_3_ = s16[672,128]{1,0:T(8,128)(2,1)S(1)} collective-permute-done((s16[672,128]{1,0:T(8,128)(2,1)S(1)}, s16[672,128]{1,0:T(8,128)(2,1)S(1)}, u32[]{:S(2)}, u32[]{:S(2)}) %collective-permute-start.12) | collective-permute-done | bytes 172064 | tf_op jit(solution)/shard_map/ppermute | solution.py:1194
  56.8 1.4 %forward.3 = (f32[18,256,128]{2,1,0:T(8,128)S(1)}, s16[400,128]{1,0:T(8,128)(2,1)S(1)}, s16[336,128]{1,0:T(8,128)(2,1)S(1)}, s16[592,128]{1,0:T(8,128)(2,1)S(1)}...) custom-call(s16[672,128]{1,0:T(8,128)(2,1)S(1)} %get-tuple-element.80.refs_0_, ...), custom_call_target="tpu_custom_call" | custom-call | flops 301989888 | bytes 4718592 | tf_op jit(solution)/shard_map/forward/pallas_call | solution.py:692
  58.2 0.1 collective-permute-start.15
  58.3 0.9 %collective-permute-start.14 = (s16[592,128]{1,0:T(8,128)(2,1)S(1)}, s16[592,128]{1,0:T(8,128)(2,1)S(1)}, u32[]{:S(2)}, u32[]{:S(2)}) collective-permute-start(s16[592,128]{1,0:T(8,128)(2,1)S(1)} %get-tuple-element.88), channel_id=1, source_target_pairs={{4,8},{8,4},{5,9},{9,5},{6,10},{10,6},{7,11},{11,7},{20,24},{24,20... | collective-permute-start | bytes 454664 | tf_op jit(solution)/shard_map/ppermute | solution.py:1207
  59.2 4.4 %collective-permute-start.13 = (s16[336,128]{1,0:T(8,128)(2,1)S(1)}, s16[336,128]{1,0:T(8,128)(2,1)S(1)}, u32[]{:S(2)}, u32[]{:S(2)}) collective-permute-start(s16[336,128]{1,0:T(8,128)(2,1)S(1)} %get-tuple-element.87), channel_id=1, source_target_pairs={{0,4},{8,12},{4,0},{12,8},{1,5},{9,13},{5,1},{13,9},{2,6},{10,14},... | collective-permute-start | bytes 258056 | tf_op jit(solution)/shard_map/ppermute | solution.py:1208
  63.6 0.0 collective-permute-done.15.even_ref.refs_2_
  63.6 0.2 pair_messages.3
  63.8 1.0 %collective-permute-start.16 = (s16[272,128]{1,0:T(8,128)(2,1)S(1)}, s16[272,128]{1,0:T(8,128)(2,1)S(1)}, u32[]{:S(2)}, u32[]{:S(2)}) collective-permute-start(s16[272,128]{1,0:T(8,128)(2,1)S(1)} %pair_messages.3), channel_id=1, source_target_pairs={{0,8},{4,12},{8,0},{12,4},{1,9},{5,13},{9,1},{13,5},{2,10},{6,14},... | collective-permute-start | bytes 208904 | tf_op jit(solution)/shard_map/ppermute | solution.py:1210
  64.7 1.6 %collective-permute-done.13.layers_ref.refs_0_ = s16[336,128]{1,0:T(8,128)(2,1)S(1)} collective-permute-done((s16[336,128]{1,0:T(8,128)(2,1)S(1)}, s16[336,128]{1,0:T(8,128)(2,1)S(1)}, u32[]{:S(2)}, u32[]{:S(2)}) %collective-permute-start.13) | collective-permute-done | bytes 86048 | tf_op jit(solution)/shard_map/ppermute | solution.py:1208
  66.3 0.4 borders.3.refs_1_
  66.8 3.7 %collective-permute-done.16.refs_6_ = s16[272,128]{1,0:T(8,128)(2,1)S(1)} collective-permute-done((s16[272,128]{1,0:T(8,128)(2,1)S(1)}, s16[272,128]{1,0:T(8,128)(2,1)S(1)}, u32[]{:S(2)}, u32[]{:S(2)}) %collective-permute-start.16) | collective-permute-done | bytes 69664 | tf_op jit(solution)/shard_map/ppermute | solution.py:1210
  70.5 2.0 %inverse.3 = (s16[672,128]{1,0:T(8,128)(2,1)S(1)}, s16[672,128]{1,0:T(8,128)(2,1)S(1)}, bf16[18,256,128]{2,1,0:T(8,128)(2,1)S(1)}, bf16[18,256,128]{2,1,0:T(8,128)(2,1)S(1)}) custom-call(f32[18,256,128]{2,1,0:T(8,128)S(1)} %get-tuple-element.86.refs_0_, f32[4,256,128]{2,1,0:T(8,128)S(1)} %borders.3.refs_1_, ...), custom_call_target="tpu_custom_call" | custom-call | flops 301989888 | bytes 4718592 | tf_op jit(solution)/shard_map/inverse/pallas_call | solution.py:925
  72.5 1.7 %collective-permute-start.19 = (s16[672,128]{1,0:T(8,128)(2,1)S(1)}, s16[672,128]{1,0:T(8,128)(2,1)S(1)}, u32[]{:S(2)}, u32[]{:S(2)}) collective-permute-start(s16[672,128]{1,0:T(8,128)(2,1)S(1)} %get-tuple-element.97), channel_id=1, source_target_pairs={{0,2},{1,3},{2,0},{3,1},{4,6},{5,7},{6,4},{7,5},{8,10},{9,11},{10,... | collective-permute-start | bytes 516104 | tf_op jit(solution)/shard_map/ppermute | solution.py:1194
  74.2 1.0 %inverse_rest.3 = (s16[672,128]{1,0:T(8,128)(2,1)S(1)}, s16[672,128]{1,0:T(8,128)(2,1)S(1)}) custom-call(bf16[18,256,128]{2,1,0:T(8,128)(2,1)S(1)} %get-tuple-element.92.field_high, bf16[18,256,128]{2,1,0:T(8,128)(2,1)S(1)} %get-tuple-element.93.field_low, bf16[4,48,256]{2,1,0:T(8,128)(2,1)S(1)} %copy-done.3, bf16[4,48,256]{2,1,0:T(8,128)(2,1)S(1)} %copy-done.4), custom_call_target="tpu_custom_call" | custom-call | flops 301989888 | bytes 4718592 | tf_op jit(solution)/shard_map/inverse_rest/pallas_call | solution.py:949
  75.2 0.1 collective-permute-start.17
  75.3 0.5 collective-permute-start.18
  75.8 1.0 %near_field.3.refs_8_ = f32[8,128]{1,0:T(8,128)S(1)} custom-call(s32[24]{0:T(128)S(1)} %get-tuple-element.100.place_ref, s32[24]{0:T(128)S(1)} %get-tuple-element.99.target_ref, s16[336,128]{1,0:T(8,128)(2,1)S(1)} %collective-permute-done.13.layers_ref.refs_0_, s16[592,128]{1,0:T(8,128)(2,1)S(1)} %collective-permute-done.14.odd_ref.refs_3_.refs_1_, ...), custom_call_target="tpu_custom_call" | custom-call | flops 12582912 | bytes 786432 | tf_op jit(solution)/shard_map/near_field/pallas_call | solution.py:1128
  76.9 2.2 %collective-permute-done.19.refs_1_ = s16[672,128]{1,0:T(8,128)(2,1)S(1)} collective-permute-done((s16[672,128]{1,0:T(8,128)(2,1)S(1)}, s16[672,128]{1,0:T(8,128)(2,1)S(1)}, u32[]{:S(2)}, u32[]{:S(2)}) %collective-permute-start.19) | collective-permute-done | bytes 172064 | tf_op jit(solution)/shard_map/ppermute | solution.py:1194
  79.0 0.4 sample_early.3.refs_2_
  79.5 2.2 %collective-permute-done.18.refs_1_ = s16[672,128]{1,0:T(8,128)(2,1)S(1)} collective-permute-done((s16[672,128]{1,0:T(8,128)(2,1)S(1)}, s16[672,128]{1,0:T(8,128)(2,1)S(1)}, u32[]{:S(2)}, u32[]{:S(2)}) %collective-permute-start.18) | collective-permute-done | bytes 172064 | tf_op jit(solution)/shard_map/ppermute | solution.py:1194
  81.7 2.7 %sample.3 = f32[2,512]{1,0:T(2,128)} custom-call(s32[2,512]{1,0:T(2,128)S(1)} %get-tuple-element.52.place_ref.place_in.refs_1_, s16[672,128]{1,0:T(8,128)(2,1)S(1)} %collective-permute-done.17.refs_0_, s16[672,128]{1,0:T(8,128)(2,1)S(1)} %collective-permute-done.18.refs_1_, f32[656,256]{1,0:T(8,128)S(1)} %sample_early.3.refs_2_, ...), custom_call_target="tpu_custom_call" | custom-call | flops 169869312 | bytes 4194304 | tf_op jit(solution)/shard_map/sample/pallas_call | solution.py:1070
  (22 shorter events, 0.1 us)
Async XLA Ops:
  5.1 9.3 %collective-permute-start.1 = (s16[672,128]{1,0:T(8,128)(2,1)S(1)}, s16[672,128]{1,0:T(8,128)(2,1)S(1)}, u32[]{:S(2)}, u32[]{:S(2)}) collective-permute-start(s16[672,128]{1,0:T(8,128)(2,1)S(1)} %get-tuple-element.60), channel_id=1, source_target_pairs={{0,2},{1,3},{2,0},{3,1},{4,6},{5,7},{6,4},{7,5},{8,10},{9,11},{10,... | collective-permute-start | bytes 516104 | tf_op jit(solution)/shard_map/ppermute | solution.py:1194
  8.8 6.3 %collective-permute-start = (s16[672,128]{1,0:T(8,128)(2,1)S(1)}, s16[672,128]{1,0:T(8,128)(2,1)S(1)}, u32[]{:S(2)}, u32[]{:S(2)}) collective-permute-start(s16[672,128]{1,0:T(8,128)(2,1)S(1)} %get-tuple-element.59), channel_id=1, source_target_pairs={{0,1},{1,0},{2,3},{3,2},{4,5},{5,4},{6,7},{7,6},{8,9},{9,8},{10,11... | collective-permute-start | bytes 516104 | tf_op jit(solution)/shard_map/ppermute | solution.py:1194
  8.9 6.8 %collective-permute-start.2 = (s16[672,128]{1,0:T(8,128)(2,1)S(1)}, s16[672,128]{1,0:T(8,128)(2,1)S(1)}, u32[]{:S(2)}, u32[]{:S(2)}) collective-permute-start(s16[672,128]{1,0:T(8,128)(2,1)S(1)} %get-tuple-element.61), channel_id=1, source_target_pairs={{0,3},{1,2},{2,1},{3,0},{4,7},{5,6},{6,5},{7,4},{8,11},{9,10},{10,... | collective-permute-start | bytes 516104 | tf_op jit(solution)/shard_map/ppermute | solution.py:1194
  9.0 0.9 %copy-start.1 = (f32[64,512]{1,0:T(8,128)S(1)}, f32[64,512]{1,0:T(8,128)}, u32[]{:S(2)}) copy-start(f32[64,512]{1,0:T(8,128)} %refs_3_.8) | copy-start | bytes 393220
  9.9 4.5 %copy-start = (bf16[2,256,240]{2,1,0:T(8,128)(2,1)S(1)}, bf16[2,256,240]{2,1,0:T(8,128)(2,1)}, u32[]{:S(2)}) copy-start(bf16[2,256,240]{2,1,0:T(8,128)(2,1)} %constant.76.clone.refs_2_.refs_6_.table_ref) | copy-start | bytes 737284
  15.7 14.9 %copy-start.3 = (bf16[4,48,256]{2,1,0:T(8,128)(2,1)S(1)}, bf16[4,48,256]{2,1,0:T(8,128)(2,1)}, u32[]{:S(2)}) copy-start(bf16[4,48,256]{2,1,0:T(8,128)(2,1)} %constant.77.clone.refs_7_.high_ref) | copy-start | bytes 294916
  15.7 14.9 %copy-start.4 = (bf16[4,48,256]{2,1,0:T(8,128)(2,1)S(1)}, bf16[4,48,256]{2,1,0:T(8,128)(2,1)}, u32[]{:S(2)}) copy-start(bf16[4,48,256]{2,1,0:T(8,128)(2,1)} %constant.78.clone.refs_8_.low_ref) | copy-start | bytes 294916
  17.1 6.9 %collective-permute-start.5 = (s16[400,128]{1,0:T(8,128)(2,1)S(1)}, s16[400,128]{1,0:T(8,128)(2,1)S(1)}, u32[]{:S(2)}, u32[]{:S(2)}) collective-permute-start(s16[400,128]{1,0:T(8,128)(2,1)S(1)} %get-tuple-element.67), channel_id=1, source_target_pairs={{0,4},{8,12},{4,0},{12,8},{1,5},{9,13},{5,1},{13,9},{2,6},{10,14},... | collective-permute-start | bytes 307208 | tf_op jit(solution)/shard_map/ppermute | solution.py:1206
  18.7 8.0 %collective-permute-start.4 = (s16[592,128]{1,0:T(8,128)(2,1)S(1)}, s16[592,128]{1,0:T(8,128)(2,1)S(1)}, u32[]{:S(2)}, u32[]{:S(2)}) collective-permute-start(s16[592,128]{1,0:T(8,128)(2,1)S(1)} %get-tuple-element.66), channel_id=1, source_target_pairs={{4,8},{8,4},{5,9},{9,5},{6,10},{10,6},{7,11},{11,7},{20,24},{24,20... | collective-permute-start | bytes 454664 | tf_op jit(solution)/shard_map/ppermute | solution.py:1207
  19.6 7.2 %collective-permute-start.3 = (s16[336,128]{1,0:T(8,128)(2,1)S(1)}, s16[336,128]{1,0:T(8,128)(2,1)S(1)}, u32[]{:S(2)}, u32[]{:S(2)}) collective-permute-start(s16[336,128]{1,0:T(8,128)(2,1)S(1)} %get-tuple-element.65), channel_id=1, source_target_pairs={{0,4},{8,12},{4,0},{12,8},{1,5},{9,13},{5,1},{13,9},{2,6},{10,14},... | collective-permute-start | bytes 258056 | tf_op jit(solution)/shard_map/ppermute | solution.py:1208
  24.2 10.0 %copy-start.8 = (s32[24]{0:T(128)S(1)}, s32[24]{0:T(128)}, u32[]{:S(2)}) copy-start(s32[24]{0:T(128)} %param.21) | copy-start | bytes 292
  24.2 10.0 %copy-start.9 = (s32[24]{0:T(128)S(1)}, s32[24]{0:T(128)}, u32[]{:S(2)}) copy-start(s32[24]{0:T(128)} %param.22) | copy-start | bytes 292
  24.2 6.4 %collective-permute-start.6 = (s16[272,128]{1,0:T(8,128)(2,1)S(1)}, s16[272,128]{1,0:T(8,128)(2,1)S(1)}, u32[]{:S(2)}, u32[]{:S(2)}) collective-permute-start(s16[272,128]{1,0:T(8,128)(2,1)S(1)} %pair_messages.2), channel_id=1, source_target_pairs={{0,8},{4,12},{8,0},{12,4},{1,9},{5,13},{9,1},{13,5},{2,10},{6,14},... | collective-permute-start | bytes 208904 | tf_op jit(solution)/shard_map/ppermute | solution.py:1210
  30.6 5.3 %copy-start.2 = (bf16[24,128,128]{2,1,0:T(8,128)(2,1)S(1)}, bf16[24,128,128]{2,1,0:T(8,128)(2,1)}, u32[]{:S(2)}) copy-start(bf16[24,128,128]{2,1,0:T(8,128)(2,1)} %refs_3_.10) | copy-start | bytes 2359300
  32.6 7.3 %collective-permute-start.9 = (s16[672,128]{1,0:T(8,128)(2,1)S(1)}, s16[672,128]{1,0:T(8,128)(2,1)S(1)}, u32[]{:S(2)}, u32[]{:S(2)}) collective-permute-start(s16[672,128]{1,0:T(8,128)(2,1)S(1)} %get-tuple-element.75), channel_id=1, source_target_pairs={{0,2},{1,3},{2,0},{3,1},{4,6},{5,7},{6,4},{7,5},{8,10},{9,11},{10,... | collective-permute-start | bytes 516104 | tf_op jit(solution)/shard_map/ppermute | solution.py:1194
  35.2 5.2 %collective-permute-start.7 = (s16[672,128]{1,0:T(8,128)(2,1)S(1)}, s16[672,128]{1,0:T(8,128)(2,1)S(1)}, u32[]{:S(2)}, u32[]{:S(2)}) collective-permute-start(s16[672,128]{1,0:T(8,128)(2,1)S(1)} %get-tuple-element.72), channel_id=1, source_target_pairs={{0,1},{1,0},{2,3},{3,2},{4,5},{5,4},{6,7},{7,6},{8,9},{9,8},{10,11... | collective-permute-start | bytes 516104 | tf_op jit(solution)/shard_map/ppermute | solution.py:1194
  35.2 6.8 %collective-permute-start.8 = (s16[672,128]{1,0:T(8,128)(2,1)S(1)}, s16[672,128]{1,0:T(8,128)(2,1)S(1)}, u32[]{:S(2)}, u32[]{:S(2)}) collective-permute-start(s16[672,128]{1,0:T(8,128)(2,1)S(1)} %get-tuple-element.73), channel_id=1, source_target_pairs={{0,3},{1,2},{2,1},{3,0},{4,7},{5,6},{6,5},{7,4},{8,11},{9,10},{10,... | collective-permute-start | bytes 516104 | tf_op jit(solution)/shard_map/ppermute | solution.py:1194
  36.9 3.0 %copy-start.5 = (bf16[4,128,256]{2,1,0:T(8,128)(2,1)S(1)}, bf16[4,128,256]{2,1,0:T(8,128)(2,1)}, u32[]{:S(2)}) copy-start(bf16[4,128,256]{2,1,0:T(8,128)(2,1)} %constant.79.clone.refs_2_.refs_3_) | copy-start | bytes 786436
  36.9 3.0 %copy-start.6 = (bf16[4,128,256]{2,1,0:T(8,128)(2,1)S(1)}, bf16[4,128,256]{2,1,0:T(8,128)(2,1)}, u32[]{:S(2)}) copy-start(bf16[4,128,256]{2,1,0:T(8,128)(2,1)} %constant.80.clone.refs_3_.refs_4_) | copy-start | bytes 786436
  39.9 2.1 %copy-start.7 = (s32[512]{0:T(512)S(1)}, s32[512]{0:T(512)}, u32[]{:S(2)}) copy-start(s32[512]{0:T(512)} %param.17) | copy-start | bytes 6148
  46.9 7.3 %collective-permute-start.11 = (s16[672,128]{1,0:T(8,128)(2,1)S(1)}, s16[672,128]{1,0:T(8,128)(2,1)S(1)}, u32[]{:S(2)}, u32[]{:S(2)}) collective-permute-start(s16[672,128]{1,0:T(8,128)(2,1)S(1)} %get-tuple-element.82), channel_id=1, source_target_pairs={{0,2},{1,3},{2,0},{3,1},{4,6},{5,7},{6,4},{7,5},{8,10},{9,11},{10,... | collective-permute-start | bytes 516104 | tf_op jit(solution)/shard_map/ppermute | solution.py:1194
  48.7 6.2 %collective-permute-start.10 = (s16[672,128]{1,0:T(8,128)(2,1)S(1)}, s16[672,128]{1,0:T(8,128)(2,1)S(1)}, u32[]{:S(2)}, u32[]{:S(2)}) collective-permute-start(s16[672,128]{1,0:T(8,128)(2,1)S(1)} %get-tuple-element.81), channel_id=1, source_target_pairs={{0,1},{1,0},{2,3},{3,2},{4,5},{5,4},{6,7},{7,6},{8,9},{9,8},{10,11... | collective-permute-start | bytes 516104 | tf_op jit(solution)/shard_map/ppermute | solution.py:1194
  49.3 7.5 %collective-permute-start.12 = (s16[672,128]{1,0:T(8,128)(2,1)S(1)}, s16[672,128]{1,0:T(8,128)(2,1)S(1)}, u32[]{:S(2)}, u32[]{:S(2)}) collective-permute-start(s16[672,128]{1,0:T(8,128)(2,1)S(1)} %get-tuple-element.83), channel_id=1, source_target_pairs={{0,3},{1,2},{2,1},{3,0},{4,7},{5,6},{6,5},{7,4},{8,11},{9,10},{10,... | collective-permute-start | bytes 516104 | tf_op jit(solution)/shard_map/ppermute | solution.py:1194
  58.2 5.4 %collective-permute-start.15 = (s16[400,128]{1,0:T(8,128)(2,1)S(1)}, s16[400,128]{1,0:T(8,128)(2,1)S(1)}, u32[]{:S(2)}, u32[]{:S(2)}) collective-permute-start(s16[400,128]{1,0:T(8,128)(2,1)S(1)} %get-tuple-element.89), channel_id=1, source_target_pairs={{0,4},{8,12},{4,0},{12,8},{1,5},{9,13},{5,1},{13,9},{2,6},{10,14},... | collective-permute-start | bytes 307208 | tf_op jit(solution)/shard_map/ppermute | solution.py:1206
  58.3 8.1 %collective-permute-start.14 = (s16[592,128]{1,0:T(8,128)(2,1)S(1)}, s16[592,128]{1,0:T(8,128)(2,1)S(1)}, u32[]{:S(2)}, u32[]{:S(2)}) collective-permute-start(s16[592,128]{1,0:T(8,128)(2,1)S(1)} %get-tuple-element.88), channel_id=1, source_target_pairs={{4,8},{8,4},{5,9},{9,5},{6,10},{10,6},{7,11},{11,7},{20,24},{24,20... | collective-permute-start | bytes 454664 | tf_op jit(solution)/shard_map/ppermute | solution.py:1207
  59.2 7.2 %collective-permute-start.13 = (s16[336,128]{1,0:T(8,128)(2,1)S(1)}, s16[336,128]{1,0:T(8,128)(2,1)S(1)}, u32[]{:S(2)}, u32[]{:S(2)}) collective-permute-start(s16[336,128]{1,0:T(8,128)(2,1)S(1)} %get-tuple-element.87), channel_id=1, source_target_pairs={{0,4},{8,12},{4,0},{12,8},{1,5},{9,13},{5,1},{13,9},{2,6},{10,14},... | collective-permute-start | bytes 258056 | tf_op jit(solution)/shard_map/ppermute | solution.py:1208
  63.8 6.7 %collective-permute-start.16 = (s16[272,128]{1,0:T(8,128)(2,1)S(1)}, s16[272,128]{1,0:T(8,128)(2,1)S(1)}, u32[]{:S(2)}, u32[]{:S(2)}) collective-permute-start(s16[272,128]{1,0:T(8,128)(2,1)S(1)} %pair_messages.3), channel_id=1, source_target_pairs={{0,8},{4,12},{8,0},{12,4},{1,9},{5,13},{9,1},{13,5},{2,10},{6,14},... | collective-permute-start | bytes 208904 | tf_op jit(solution)/shard_map/ppermute | solution.py:1210
  72.5 6.5 %collective-permute-start.19 = (s16[672,128]{1,0:T(8,128)(2,1)S(1)}, s16[672,128]{1,0:T(8,128)(2,1)S(1)}, u32[]{:S(2)}, u32[]{:S(2)}) collective-permute-start(s16[672,128]{1,0:T(8,128)(2,1)S(1)} %get-tuple-element.97), channel_id=1, source_target_pairs={{0,2},{1,3},{2,0},{3,1},{4,6},{5,7},{6,4},{7,5},{8,10},{9,11},{10,... | collective-permute-start | bytes 516104 | tf_op jit(solution)/shard_map/ppermute | solution.py:1194
  75.2 4.2 %collective-permute-start.17 = (s16[672,128]{1,0:T(8,128)(2,1)S(1)}, s16[672,128]{1,0:T(8,128)(2,1)S(1)}, u32[]{:S(2)}, u32[]{:S(2)}) collective-permute-start(s16[672,128]{1,0:T(8,128)(2,1)S(1)} %get-tuple-element.94), channel_id=1, source_target_pairs={{0,1},{1,0},{2,3},{3,2},{4,5},{5,4},{6,7},{7,6},{8,9},{9,8},{10,11... | collective-permute-start | bytes 516104 | tf_op jit(solution)/shard_map/ppermute | solution.py:1194
  75.3 6.4 %collective-permute-start.18 = (s16[672,128]{1,0:T(8,128)(2,1)S(1)}, s16[672,128]{1,0:T(8,128)(2,1)S(1)}, u32[]{:S(2)}, u32[]{:S(2)}) collective-permute-start(s16[672,128]{1,0:T(8,128)(2,1)S(1)} %get-tuple-element.95), channel_id=1, source_target_pairs={{0,3},{1,2},{2,1},{3,0},{4,7},{5,6},{6,5},{7,4},{8,11},{9,10},{10,... | collective-permute-start | bytes 516104 | tf_op jit(solution)/shard_map/ppermute | solution.py:1194

commit v19 on v18

--- a/solution.py
+++ b/solution.py
@@ -16,7 +16,6 @@
 KERNEL_GAIN = 4.0
 SCREEN = 1.0 / 1024.0
 LN2 = math.log(2.0)
-ROUNDING = 1.5 * 2.0**23
 Y_AXES = ("narrow", "pair")
 ALL_AXES = ("wide", "narrow", "pair")
 F32 = jnp.float32
@@ -97,8 +96,7 @@
 
 
 def quantize(values, exponent, fraction):
-    scaled = values * (32767.0 / full_scale(exponent, fraction))
-    return to_short((scaled + ROUNDING) - ROUNDING)
+    return to_short(jnp.round(values * (32767.0 / full_scale(exponent, fraction))))
 
 
 def unit(exponent, fraction):
@@ -1183,13 +1181,13 @@
     odd_swap = swaps([(i, i + 1) for i in range(1, x_count - 1, 2)])
     far_flips = list(range(2, x_count, 2))
 
-    first, rest = list(range(pair, y_count)), list(range(pair))
+    first, inside, local = list(range(pair, y_count)), list(range(1, pair)), [0]
     same_core = list(range(0, y_count, pair))
     other_core = [flip for flip in range(y_count) if flip not in same_core]
 
     def turned(sent, then):
         arrived = [None] * y_count
-        for flip, part in zip(first + rest, list(sent) + list(then)):
+        for flip, part in zip(first + inside + local, list(sent) + list(then)):
             swap_pairs = [(i, i ^ flip) for i in range(y_count)]
             arrived[flip] = part if flip == 0 else lax.ppermute(part, Y_AXES, swap_pairs)
         return arrived
@@ -1198,7 +1196,8 @@
         return [parts[flip] for flip in flips]
 
     def convolve_and_sample(last, vector, sent, both, table, places, sample_lines, awaited):
-        arrived = turned(sent, spread_rest(vector, both, table, rest))
+        then = [part for flips in (inside, local) for part in spread_rest(vector, both, table, flips)]
+        arrived = turned(sent, then)
         early, edges = forward_early(chosen(arrived, same_core), y_forward, reach_x, reach_y)
         spectrum, even_message, layers, odd_message, own, peers, inner = forward(
             arrived, early, edges, y_forward, modes, reach_x, reach_y, blocks, awaited
@@ -1226,7 +1225,11 @@
             reach_y,
             first,
         )
-        then = inverse_rest((high, low), y_inverse, reach_y, rest)
+        then = [
+            part
+            for flips in (inside, local)
+            for part in inverse_rest((high, low), y_inverse, reach_y, flips)
+        ]
         near_part = near_field(
             sources, targets, even_layers, from_odd, peers, near_tiles, blocks, out_rows, then[:1]
         )

time: 84.8 us -> 83.8 us (0.988)
  waiting for transfers between devices: 22.9 us -> 20.2 us
  Pallas kernels: 34.7 us -> 36.3 us
    ppermute x12, waiting for transfers between devices: 12.8 us -> 9.86 us  [turned(): lax.ppermute(part, Y_AXES, swap_pairs)]
    pallas_call x2 -> x4, Pallas kernels: 1.95 us -> 3.41 us  [inverse_rest(): pl.pallas_call(functools.partial(inverse_rest_kernel, reach_y, flips), in...]
    pallas_call x2 -> x4, Pallas kernels: 1.29 us -> 2.07 us  [spread_rest(): pl.pallas_call(functools.partial(spread_rest_kernel, flips), in_specs=[wh...]
  transfers between devices with their start and end apart: 20 -> 20, of which waited for: 10 -> 9; matrix products, arithmetic and copies ran while one was open for 1% -> 1% of each run, Pallas kernels for 18% -> 21%
where the time goes in v19:
time: 83.8 us; the launch traced here: 83.6 us
  Pallas kernels  36.3 us (43%)
  starting transfers between devices  24.4 us (29%)
  waiting for transfers between devices  20.2 us (24%)
  local copies, waits for them, and re-layouts  2.16 us (3%)
    ppermute x12, starting transfers between devices, turned(): lax.ppermute(part, Y_AXES, swap_pairs)  10.1 us
    ppermute x12, waiting for transfers between devices, turned(): lax.ppermute(part, Y_AXES, swap_pairs)  9.86 us
    ppermute x2, starting transfers between devices, convolve_and_sample(): even_layers = lax.ppermute(layers, 'wide', even_swap)  8.82 us
    pallas_call x2, Pallas kernels, spread(): pl.pallas_call(functools.partial(start_kernel if placed is None else spre...  7.69 us
    ppermute x2, waiting for transfers between devices, convolve_and_sample(): lax.ppermute(message, 'wide', [(i, i ^ flip) for i in range(x_count)])  7.19 us
    pallas_call x2, Pallas kernels, sample(): pl.pallas_call(functools.partial(sample_kernel, last, reach_x, reach_y, f...  4.87 us
    pallas_call x2, Pallas kernels, inverse(): pl.pallas_call(functools.partial(inverse_kernel, reach_x, reach_y, flips,...  3.8 us
    pallas_call x1, Pallas kernels, place_sample_lines(): pl.pallas_call(functools.partial(sample_lines_kernel, blocks), grid=(1,),...  3.41 us
  transfers between devices with their start and end apart: 20, of which 9 were waited for; matrix products, arithmetic and copies ran while one was open for 1% of the time, Pallas kernels for 21%

profile of v19, /device:TPU:0, one launch (start us, length us, event | category | flops | bytes accessed | tf_op | source)
XLA Modules:
  0.0 83.6 jit_solution(12000787685769834258)
XLA Ops:
  0.0 5.0 %start.1 = (s16[672,128]{1,0:T(8,128)(2,1)S(1)}, s16[672,128]{1,0:T(8,128)(2,1)S(1)}, bf16[656,256]{1,0:T(8,128)(2,1)S(1)}, bf16[656,256]{1,0:T(8,128)(2,1)S(1)}...) custom-call(f32[512]{0:T(512)} %refs_0_.2, ...), custom_call_target="tpu_custom_call" | custom-call | flops 169869312 | bytes 4194304 | tf_op jit(solution)/shard_map/start/pallas_call | solution.py:411
  5.0 3.0 %collective-permute-start.1 = (s16[672,128]{1,0:T(8,128)(2,1)S(1)}, s16[672,128]{1,0:T(8,128)(2,1)S(1)}, u32[]{:S(2)}, u32[]{:S(2)}) collective-permute-start(s16[672,128]{1,0:T(8,128)(2,1)S(1)} %get-tuple-element.50), channel_id=1, source_target_pairs={{0,2},{1,3},{2,0},{3,1},{4,6},{5,7},{6,4},{7,5},{8,10},{9,11},{10,... | collective-permute-start | bytes 516104 | tf_op jit(solution)/shard_map/ppermute | solution.py:1192
  8.0 0.5 spread_rest.5
  8.6 0.1 collective-permute-start
  8.7 0.1 collective-permute-start.2
  8.8 0.9 %copy-done.3 = f32[64,512]{1,0:T(8,128)S(1)} copy-done((f32[64,512]{1,0:T(8,128)S(1)}, f32[64,512]{1,0:T(8,128)}, u32[]{:S(2)}) %copy-start.3) | copy-done | bytes 131096
  9.7 3.4 %place_sample_lines.1.refs_8_.refs_5_ = f32[8192,128]{1,0:T(8,128)S(1)} custom-call(s32[2,512]{1,0:T(2,128)S(1)} %get-tuple-element.44.place_ref.place_in.refs_1_, f32[64,512]{1,0:T(8,128)S(1)} %copy-done.3, f32[64,512]{1,0:T(8,128)S(1)} %copy-done.3, f32[64,512]{1,0:T(8,128)S(1)} %copy-done.3, f32[64,512]{1,0:T(8,128)S(1)} %copy-done.3), custom_call_target="tpu_custom_call" | custom-call | flops 1048576 | bytes 4194304 | tf_op jit(solution)/shard_map/place_sample_lines/pallas_call | solution.py:480
  13.1 0.5 spread_rest.4.refs_0_
  13.6 1.1 %dynamic-slice_bitcast_fusion.refs_7_.modes_ref.refs_9_ = f32[4,256,128]{2,1,0:T(8,128)S(1)} fusion(f32[4,4,256,128]{3,2,1,0:T(8,128)} %constant.73.clone, s32[]{:T(128)S(6)} %select_n.30), kind=kLoop, calls=%fused_computation | loop fusion | bytes 1048580 | tf_op jit(solution)/shard_map/jit(dynamic_index_in_dim)/squeeze | solution.py:1169
  14.8 0.7 forward_early.2
  15.4 0.0 collective-permute-done.2.refs_3_
  15.5 0.0 copy-start.2
  15.5 1.2 %forward.2 = (f32[18,256,128]{2,1,0:T(8,128)S(1)}, s16[400,128]{1,0:T(8,128)(2,1)S(1)}, s16[336,128]{1,0:T(8,128)(2,1)S(1)}, s16[592,128]{1,0:T(8,128)(2,1)S(1)}...) custom-call(s16[672,128]{1,0:T(8,128)(2,1)S(1)} %spread_rest.4.refs_0_, ...), custom_call_target="tpu_custom_call" | custom-call | flops 301989888 | bytes 4718592 | tf_op jit(solution)/shard_map/forward/pallas_call | solution.py:690
  16.7 2.2 %collective-permute-start.5 = (s16[400,128]{1,0:T(8,128)(2,1)S(1)}, s16[400,128]{1,0:T(8,128)(2,1)S(1)}, u32[]{:S(2)}, u32[]{:S(2)}) collective-permute-start(s16[400,128]{1,0:T(8,128)(2,1)S(1)} %get-tuple-element.57), channel_id=1, source_target_pairs={{0,4},{8,12},{4,0},{12,8},{1,5},{9,13},{5,1},{13,9},{2,6},{10,14},... | collective-permute-start | bytes 307208 | tf_op jit(solution)/shard_map/ppermute | solution.py:1205
  18.8 0.8 %collective-permute-start.4 = (s16[592,128]{1,0:T(8,128)(2,1)S(1)}, s16[592,128]{1,0:T(8,128)(2,1)S(1)}, u32[]{:S(2)}, u32[]{:S(2)}) collective-permute-start(s16[592,128]{1,0:T(8,128)(2,1)S(1)} %get-tuple-element.56), channel_id=1, source_target_pairs={{4,8},{8,4},{5,9},{9,5},{6,10},{10,6},{7,11},{11,7},{20,24},{24,20... | collective-permute-start | bytes 454664 | tf_op jit(solution)/shard_map/ppermute | solution.py:1206
  19.7 4.5 %collective-permute-start.3 = (s16[336,128]{1,0:T(8,128)(2,1)S(1)}, s16[336,128]{1,0:T(8,128)(2,1)S(1)}, u32[]{:S(2)}, u32[]{:S(2)}) collective-permute-start(s16[336,128]{1,0:T(8,128)(2,1)S(1)} %get-tuple-element.55), channel_id=1, source_target_pairs={{0,4},{8,12},{4,0},{12,8},{1,5},{9,13},{5,1},{13,9},{2,6},{10,14},... | collective-permute-start | bytes 258056 | tf_op jit(solution)/shard_map/ppermute | solution.py:1207
  24.2 0.2 pair_messages.2
  24.4 0.7 collective-permute-start.6
  25.1 1.5 %collective-permute-done.3.layers_ref.refs_0_ = s16[336,128]{1,0:T(8,128)(2,1)S(1)} collective-permute-done((s16[336,128]{1,0:T(8,128)(2,1)S(1)}, s16[336,128]{1,0:T(8,128)(2,1)S(1)}, u32[]{:S(2)}, u32[]{:S(2)}) %collective-permute-start.3) | collective-permute-done | bytes 86048 | tf_op jit(solution)/shard_map/ppermute | solution.py:1207
  26.6 0.4 borders.2.refs_1_
  27.1 3.2 %collective-permute-done.6.refs_6_ = s16[272,128]{1,0:T(8,128)(2,1)S(1)} collective-permute-done((s16[272,128]{1,0:T(8,128)(2,1)S(1)}, s16[272,128]{1,0:T(8,128)(2,1)S(1)}, u32[]{:S(2)}, u32[]{:S(2)}) %collective-permute-start.6) | collective-permute-done | bytes 69664 | tf_op jit(solution)/shard_map/ppermute | solution.py:1209
  30.3 1.9 %inverse.2 = (s16[672,128]{1,0:T(8,128)(2,1)S(1)}, s16[672,128]{1,0:T(8,128)(2,1)S(1)}, bf16[18,256,128]{2,1,0:T(8,128)(2,1)S(1)}, bf16[18,256,128]{2,1,0:T(8,128)(2,1)S(1)}) custom-call(f32[18,256,128]{2,1,0:T(8,128)S(1)} %get-tuple-element.54.refs_0_, f32[4,256,128]{2,1,0:T(8,128)S(1)} %borders.2.refs_1_, ...), custom_call_target="tpu_custom_call" | custom-call | flops 301989888 | bytes 4718592 | tf_op jit(solution)/shard_map/inverse/pallas_call | solution.py:923
  32.2 1.6 %collective-permute-start.9 = (s16[672,128]{1,0:T(8,128)(2,1)S(1)}, s16[672,128]{1,0:T(8,128)(2,1)S(1)}, u32[]{:S(2)}, u32[]{:S(2)}) collective-permute-start(s16[672,128]{1,0:T(8,128)(2,1)S(1)} %get-tuple-element.63), channel_id=1, source_target_pairs={{0,2},{1,3},{2,0},{3,1},{4,6},{5,7},{6,4},{7,5},{8,10},{9,11},{10,... | collective-permute-start | bytes 516104 | tf_op jit(solution)/shard_map/ppermute | solution.py:1192
  33.8 0.8 %inverse_rest.4.refs_4_ = s16[672,128]{1,0:T(8,128)(2,1)S(1)} custom-call(bf16[18,256,128]{2,1,0:T(8,128)(2,1)S(1)} %get-tuple-element.60.field_high, bf16[18,256,128]{2,1,0:T(8,128)(2,1)S(1)} %get-tuple-element.61.field_low, bf16[4,48,256]{2,1,0:T(8,128)(2,1)S(1)} %copy-done.1, bf16[4,48,256]{2,1,0:T(8,128)(2,1)S(1)} %copy-done.2), custom_call_target="tpu_custom_call" | custom-call | flops 301989888 | bytes 4718592 | tf_op jit(solution)/shard_map/inverse_rest/pallas_call | solution.py:947
  34.7 0.1 collective-permute-start.7
  34.8 0.7 collective-permute-start.8
  35.4 1.0 %near_field.2.refs_8_.refs_0_ = f32[8,128]{1,0:T(8,128)S(1)} custom-call(s32[24]{0:T(128)S(1)} %get-tuple-element.84.place_ref, s32[24]{0:T(128)S(1)} %get-tuple-element.83.target_ref, s16[336,128]{1,0:T(8,128)(2,1)S(1)} %collective-permute-done.3.layers_ref.refs_0_, s16[592,128]{1,0:T(8,128)(2,1)S(1)} %collective-permute-done.4.odd_ref.refs_3_.refs_1_, ...), custom_call_target="tpu_custom_call" | custom-call | flops 12582912 | bytes 786432 | tf_op jit(solution)/shard_map/near_field/pallas_call | solution.py:1126
  36.5 3.0 %place_lines.1.refs_5_ = f32[8192,128]{1,0:T(8,128)S(1)} custom-call(s32[2,512]{1,0:T(2,128)S(1)} %get-tuple-element.44.place_ref.place_in.refs_1_, f32[256,128]{1,0:T(8,128)S(1)} %get-tuple-element.65.coeff_ref, f32[8,128]{1,0:T(8,128)S(1)} %near_field.2.refs_8_.refs_0_), custom_call_target="tpu_custom_call" | custom-call | flops 1048576 | bytes 4194304 | tf_op jit(solution)/shard_map/place_lines/pallas_call | solution.py:496
  39.4 0.0 copy-start.6
  39.4 0.8 %inverse_rest.5.refs_0_ = s16[672,128]{1,0:T(8,128)(2,1)S(1)} custom-call(bf16[18,256,128]{2,1,0:T(8,128)(2,1)S(1)} %get-tuple-element.60.field_high, bf16[18,256,128]{2,1,0:T(8,128)(2,1)S(1)} %get-tuple-element.61.field_low, bf16[4,48,256]{2,1,0:T(8,128)(2,1)S(1)} %copy-done.1, bf16[4,48,256]{2,1,0:T(8,128)(2,1)S(1)} %copy-done.2), custom_call_target="tpu_custom_call" | custom-call | flops 301989888 | bytes 4718592 | tf_op jit(solution)/shard_map/inverse_rest/pallas_call | solution.py:947
  40.3 0.1 copy-done.5
  40.4 0.1 copy-done.6
  40.5 0.5 sample_early.2.refs_2_
  40.9 0.6 collective-permute-done.8.refs_1_
  41.6 2.1 %sample.2.refs_2_.rounded_ref.refs_7_ = f32[4,128]{1,0:T(4,128)S(1)} custom-call(s32[2,512]{1,0:T(2,128)S(1)} %get-tuple-element.44.place_ref.place_in.refs_1_, s16[672,128]{1,0:T(8,128)(2,1)S(1)} %collective-permute-done.7.refs_0_, s16[672,128]{1,0:T(8,128)(2,1)S(1)} %collective-permute-done.8.refs_1_, f32[656,256]{1,0:T(8,128)S(1)} %sample_early.2.refs_2_, ...), custom_call_target="tpu_custom_call" | custom-call | flops 169869312 | bytes 4194304 | tf_op jit(solution)/shard_map/sample/pallas_call | solution.py:1068
  43.7 2.7 %spread.1 = (s16[672,128]{1,0:T(8,128)(2,1)S(1)}, s16[672,128]{1,0:T(8,128)(2,1)S(1)}, bf16[656,256]{1,0:T(8,128)(2,1)S(1)}, bf16[656,256]{1,0:T(8,128)(2,1)S(1)}) custom-call(f32[512]{0:T(512)S(1)} %bitcast.6, s32[2,512]{1,0:T(2,128)S(1)} %get-tuple-element.44.place_ref.place_in.refs_1_, f32[4,128]{1,0:T(4,128)S(1)} %sample.2.refs_2_.rounded_ref.refs_7_, ...), custom_call_target="tpu_custom_call" | custom-call | flops 169869312 | bytes 4194304 | tf_op jit(solution)/shard_map/spread/pallas_call | solution.py:411
  46.4 1.0 %collective-permute-start.11 = (s16[672,128]{1,0:T(8,128)(2,1)S(1)}, s16[672,128]{1,0:T(8,128)(2,1)S(1)}, u32[]{:S(2)}, u32[]{:S(2)}) collective-permute-start(s16[672,128]{1,0:T(8,128)(2,1)S(1)} %get-tuple-element.68), channel_id=1, source_target_pairs={{0,2},{1,3},{2,0},{3,1},{4,6},{5,7},{6,4},{7,5},{8,10},{9,11},{10,... | collective-permute-start | bytes 516104 | tf_op jit(solution)/shard_map/ppermute | solution.py:1192
  47.4 0.5 spread_rest.7
  47.9 0.7 collective-permute-start.10
  48.6 0.6 collective-permute-start.12
  49.2 0.5 spread_rest.6.refs_0_
  49.7 3.9 %collective-permute-done.11.refs_1_.refs_2_ = s16[672,128]{1,0:T(8,128)(2,1)S(1)} collective-permute-done((s16[672,128]{1,0:T(8,128)(2,1)S(1)}, s16[672,128]{1,0:T(8,128)(2,1)S(1)}, u32[]{:S(2)}, u32[]{:S(2)}) %collective-permute-start.11) | collective-permute-done | bytes 172064 | tf_op jit(solution)/shard_map/ppermute | solution.py:1192
  53.7 0.7 forward_early.3
  54.3 1.9 %collective-permute-done.12.refs_3_ = s16[672,128]{1,0:T(8,128)(2,1)S(1)} collective-permute-done((s16[672,128]{1,0:T(8,128)(2,1)S(1)}, s16[672,128]{1,0:T(8,128)(2,1)S(1)}, u32[]{:S(2)}, u32[]{:S(2)}) %collective-permute-start.12) | collective-permute-done | bytes 172064 | tf_op jit(solution)/shard_map/ppermute | solution.py:1192
  56.2 1.3 %forward.3 = (f32[18,256,128]{2,1,0:T(8,128)S(1)}, s16[400,128]{1,0:T(8,128)(2,1)S(1)}, s16[336,128]{1,0:T(8,128)(2,1)S(1)}, s16[592,128]{1,0:T(8,128)(2,1)S(1)}...) custom-call(s16[672,128]{1,0:T(8,128)(2,1)S(1)} %spread_rest.6.refs_0_, ...), custom_call_target="tpu_custom_call" | custom-call | flops 301989888 | bytes 4718592 | tf_op jit(solution)/shard_map/forward/pallas_call | solution.py:690
  57.6 0.1 collective-permute-start.15
  57.6 0.9 %collective-permute-start.14 = (s16[592,128]{1,0:T(8,128)(2,1)S(1)}, s16[592,128]{1,0:T(8,128)(2,1)S(1)}, u32[]{:S(2)}, u32[]{:S(2)}) collective-permute-start(s16[592,128]{1,0:T(8,128)(2,1)S(1)} %get-tuple-element.74), channel_id=1, source_target_pairs={{4,8},{8,4},{5,9},{9,5},{6,10},{10,6},{7,11},{11,7},{20,24},{24,20... | collective-permute-start | bytes 454664 | tf_op jit(solution)/shard_map/ppermute | solution.py:1206
  58.5 4.3 %collective-permute-start.13 = (s16[336,128]{1,0:T(8,128)(2,1)S(1)}, s16[336,128]{1,0:T(8,128)(2,1)S(1)}, u32[]{:S(2)}, u32[]{:S(2)}) collective-permute-start(s16[336,128]{1,0:T(8,128)(2,1)S(1)} %get-tuple-element.73), channel_id=1, source_target_pairs={{0,4},{8,12},{4,0},{12,8},{1,5},{9,13},{5,1},{13,9},{2,6},{10,14},... | collective-permute-start | bytes 258056 | tf_op jit(solution)/shard_map/ppermute | solution.py:1207
  62.9 0.2 pair_messages.3
  63.1 0.8 collective-permute-start.16
  63.9 1.6 %collective-permute-done.13.layers_ref.refs_0_ = s16[336,128]{1,0:T(8,128)(2,1)S(1)} collective-permute-done((s16[336,128]{1,0:T(8,128)(2,1)S(1)}, s16[336,128]{1,0:T(8,128)(2,1)S(1)}, u32[]{:S(2)}, u32[]{:S(2)}) %collective-permute-start.13) | collective-permute-done | bytes 86048 | tf_op jit(solution)/shard_map/ppermute | solution.py:1207
  65.5 0.4 borders.3.refs_1_
  65.9 3.9 %collective-permute-done.16.refs_6_ = s16[272,128]{1,0:T(8,128)(2,1)S(1)} collective-permute-done((s16[272,128]{1,0:T(8,128)(2,1)S(1)}, s16[272,128]{1,0:T(8,128)(2,1)S(1)}, u32[]{:S(2)}, u32[]{:S(2)}) %collective-permute-start.16) | collective-permute-done | bytes 69664 | tf_op jit(solution)/shard_map/ppermute | solution.py:1209
  69.9 1.9 %inverse.3 = (s16[672,128]{1,0:T(8,128)(2,1)S(1)}, s16[672,128]{1,0:T(8,128)(2,1)S(1)}, bf16[18,256,128]{2,1,0:T(8,128)(2,1)S(1)}, bf16[18,256,128]{2,1,0:T(8,128)(2,1)S(1)}) custom-call(f32[18,256,128]{2,1,0:T(8,128)S(1)} %get-tuple-element.72.refs_0_, f32[4,256,128]{2,1,0:T(8,128)S(1)} %borders.3.refs_1_, ...), custom_call_target="tpu_custom_call" | custom-call | flops 301989888 | bytes 4718592 | tf_op jit(solution)/shard_map/inverse/pallas_call | solution.py:923
  71.8 1.8 %collective-permute-start.19 = (s16[672,128]{1,0:T(8,128)(2,1)S(1)}, s16[672,128]{1,0:T(8,128)(2,1)S(1)}, u32[]{:S(2)}, u32[]{:S(2)}) collective-permute-start(s16[672,128]{1,0:T(8,128)(2,1)S(1)} %get-tuple-element.81), channel_id=1, source_target_pairs={{0,2},{1,3},{2,0},{3,1},{4,6},{5,7},{6,4},{7,5},{8,10},{9,11},{10,... | collective-permute-start | bytes 516104 | tf_op jit(solution)/shard_map/ppermute | solution.py:1192
  73.6 0.8 %inverse_rest.6.refs_4_ = s16[672,128]{1,0:T(8,128)(2,1)S(1)} custom-call(bf16[18,256,128]{2,1,0:T(8,128)(2,1)S(1)} %get-tuple-element.78.field_high, bf16[18,256,128]{2,1,0:T(8,128)(2,1)S(1)} %get-tuple-element.79.field_low, bf16[4,48,256]{2,1,0:T(8,128)(2,1)S(1)} %copy-done.1, bf16[4,48,256]{2,1,0:T(8,128)(2,1)S(1)} %copy-done.2), custom_call_target="tpu_custom_call" | custom-call | flops 301989888 | bytes 4718592 | tf_op jit(solution)/shard_map/inverse_rest/pallas_call | solution.py:947
  74.5 0.1 collective-permute-start.17
  74.5 0.4 collective-permute-start.18
  74.9 1.0 %near_field.3.refs_8_ = f32[8,128]{1,0:T(8,128)S(1)} custom-call(s32[24]{0:T(128)S(1)} %get-tuple-element.84.place_ref, s32[24]{0:T(128)S(1)} %get-tuple-element.83.target_ref, s16[336,128]{1,0:T(8,128)(2,1)S(1)} %collective-permute-done.13.layers_ref.refs_0_, s16[592,128]{1,0:T(8,128)(2,1)S(1)} %collective-permute-done.14.odd_ref.refs_3_.refs_1_, ...), custom_call_target="tpu_custom_call" | custom-call | flops 12582912 | bytes 786432 | tf_op jit(solution)/shard_map/near_field/pallas_call | solution.py:1126
  76.0 0.9 %inverse_rest.7.refs_0_ = s16[672,128]{1,0:T(8,128)(2,1)S(1)} custom-call(bf16[18,256,128]{2,1,0:T(8,128)(2,1)S(1)} %get-tuple-element.78.field_high, bf16[18,256,128]{2,1,0:T(8,128)(2,1)S(1)} %get-tuple-element.79.field_low, bf16[4,48,256]{2,1,0:T(8,128)(2,1)S(1)} %copy-done.1, bf16[4,48,256]{2,1,0:T(8,128)(2,1)S(1)} %copy-done.2), custom_call_target="tpu_custom_call" | custom-call | flops 301989888 | bytes 4718592 | tf_op jit(solution)/shard_map/inverse_rest/pallas_call | solution.py:947
  76.9 0.8 collective-permute-done.19.refs_1_
  77.7 0.4 sample_early.3.refs_2_
  78.1 2.6 %collective-permute-done.18.refs_1_ = s16[672,128]{1,0:T(8,128)(2,1)S(1)} collective-permute-done((s16[672,128]{1,0:T(8,128)(2,1)S(1)}, s16[672,128]{1,0:T(8,128)(2,1)S(1)}, u32[]{:S(2)}, u32[]{:S(2)}) %collective-permute-start.18) | collective-permute-done | bytes 172064 | tf_op jit(solution)/shard_map/ppermute | solution.py:1192
  80.7 2.7 %sample.3 = f32[2,512]{1,0:T(2,128)} custom-call(s32[2,512]{1,0:T(2,128)S(1)} %get-tuple-element.44.place_ref.place_in.refs_1_, s16[672,128]{1,0:T(8,128)(2,1)S(1)} %collective-permute-done.17.refs_0_, s16[672,128]{1,0:T(8,128)(2,1)S(1)} %collective-permute-done.18.refs_1_, f32[656,256]{1,0:T(8,128)S(1)} %sample_early.3.refs_2_, ...), custom_call_target="tpu_custom_call" | custom-call | flops 169869312 | bytes 4194304 | tf_op jit(solution)/shard_map/sample/pallas_call | solution.py:1068
  (26 shorter events, 0.1 us)
Async XLA Ops:
  5.0 9.7 %collective-permute-start.1 = (s16[672,128]{1,0:T(8,128)(2,1)S(1)}, s16[672,128]{1,0:T(8,128)(2,1)S(1)}, u32[]{:S(2)}, u32[]{:S(2)}) collective-permute-start(s16[672,128]{1,0:T(8,128)(2,1)S(1)} %get-tuple-element.50), channel_id=1, source_target_pairs={{0,2},{1,3},{2,0},{3,1},{4,6},{5,7},{6,4},{7,5},{8,10},{9,11},{10,... | collective-permute-start | bytes 516104 | tf_op jit(solution)/shard_map/ppermute | solution.py:1192
  8.6 6.9 %collective-permute-start = (s16[672,128]{1,0:T(8,128)(2,1)S(1)}, s16[672,128]{1,0:T(8,128)(2,1)S(1)}, u32[]{:S(2)}, u32[]{:S(2)}) collective-permute-start(s16[672,128]{1,0:T(8,128)(2,1)S(1)} %spread_rest.5), channel_id=1, source_target_pairs={{0,1},{1,0},{2,3},{3,2},{4,5},{5,4},{6,7},{7,6},{8,9},{9,8},{10,11... | collective-permute-start | bytes 516104 | tf_op jit(solution)/shard_map/ppermute | solution.py:1192
  8.7 6.8 %collective-permute-start.2 = (s16[672,128]{1,0:T(8,128)(2,1)S(1)}, s16[672,128]{1,0:T(8,128)(2,1)S(1)}, u32[]{:S(2)}, u32[]{:S(2)}) collective-permute-start(s16[672,128]{1,0:T(8,128)(2,1)S(1)} %get-tuple-element.51), channel_id=1, source_target_pairs={{0,3},{1,2},{2,1},{3,0},{4,7},{5,6},{6,5},{7,4},{8,11},{9,10},{10,... | collective-permute-start | bytes 516104 | tf_op jit(solution)/shard_map/ppermute | solution.py:1192
  8.8 0.9 %copy-start.3 = (f32[64,512]{1,0:T(8,128)S(1)}, f32[64,512]{1,0:T(8,128)}, u32[]{:S(2)}) copy-start(f32[64,512]{1,0:T(8,128)} %refs_3_.8) | copy-start | bytes 393220
  13.1 1.6 %copy-start = (bf16[2,256,240]{2,1,0:T(8,128)(2,1)S(1)}, bf16[2,256,240]{2,1,0:T(8,128)(2,1)}, u32[]{:S(2)}) copy-start(bf16[2,256,240]{2,1,0:T(8,128)(2,1)} %constant.76.clone.refs_2_.refs_6_.table_ref) | copy-start | bytes 737284
  15.5 14.9 %copy-start.1 = (bf16[4,48,256]{2,1,0:T(8,128)(2,1)S(1)}, bf16[4,48,256]{2,1,0:T(8,128)(2,1)}, u32[]{:S(2)}) copy-start(bf16[4,48,256]{2,1,0:T(8,128)(2,1)} %constant.77.clone.refs_7_.high_ref) | copy-start | bytes 294916
  15.5 14.9 %copy-start.2 = (bf16[4,48,256]{2,1,0:T(8,128)(2,1)S(1)}, bf16[4,48,256]{2,1,0:T(8,128)(2,1)}, u32[]{:S(2)}) copy-start(bf16[4,48,256]{2,1,0:T(8,128)(2,1)} %constant.78.clone.refs_8_.low_ref) | copy-start | bytes 294916
  16.7 7.5 %collective-permute-start.5 = (s16[400,128]{1,0:T(8,128)(2,1)S(1)}, s16[400,128]{1,0:T(8,128)(2,1)S(1)}, u32[]{:S(2)}, u32[]{:S(2)}) collective-permute-start(s16[400,128]{1,0:T(8,128)(2,1)S(1)} %get-tuple-element.57), channel_id=1, source_target_pairs={{0,4},{8,12},{4,0},{12,8},{1,5},{9,13},{5,1},{13,9},{2,6},{10,14},... | collective-permute-start | bytes 307208 | tf_op jit(solution)/shard_map/ppermute | solution.py:1205
  18.8 7.8 %collective-permute-start.4 = (s16[592,128]{1,0:T(8,128)(2,1)S(1)}, s16[592,128]{1,0:T(8,128)(2,1)S(1)}, u32[]{:S(2)}, u32[]{:S(2)}) collective-permute-start(s16[592,128]{1,0:T(8,128)(2,1)S(1)} %get-tuple-element.56), channel_id=1, source_target_pairs={{4,8},{8,4},{5,9},{9,5},{6,10},{10,6},{7,11},{11,7},{20,24},{24,20... | collective-permute-start | bytes 454664 | tf_op jit(solution)/shard_map/ppermute | solution.py:1206
  19.7 6.9 %collective-permute-start.3 = (s16[336,128]{1,0:T(8,128)(2,1)S(1)}, s16[336,128]{1,0:T(8,128)(2,1)S(1)}, u32[]{:S(2)}, u32[]{:S(2)}) collective-permute-start(s16[336,128]{1,0:T(8,128)(2,1)S(1)} %get-tuple-element.55), channel_id=1, source_target_pairs={{0,4},{8,12},{4,0},{12,8},{1,5},{9,13},{5,1},{13,9},{2,6},{10,14},... | collective-permute-start | bytes 258056 | tf_op jit(solution)/shard_map/ppermute | solution.py:1207
  24.3 9.5 %copy-start.8 = (s32[24]{0:T(128)S(1)}, s32[24]{0:T(128)}, u32[]{:S(2)}) copy-start(s32[24]{0:T(128)} %param.21) | copy-start | bytes 292
  24.4 9.5 %copy-start.9 = (s32[24]{0:T(128)S(1)}, s32[24]{0:T(128)}, u32[]{:S(2)}) copy-start(s32[24]{0:T(128)} %param.22) | copy-start | bytes 292
  24.4 6.0 %collective-permute-start.6 = (s16[272,128]{1,0:T(8,128)(2,1)S(1)}, s16[272,128]{1,0:T(8,128)(2,1)S(1)}, u32[]{:S(2)}, u32[]{:S(2)}) collective-permute-start(s16[272,128]{1,0:T(8,128)(2,1)S(1)} %pair_messages.2), channel_id=1, source_target_pairs={{0,8},{4,12},{8,0},{12,4},{1,9},{5,13},{9,1},{13,5},{2,10},{6,14},... | collective-permute-start | bytes 208904 | tf_op jit(solution)/shard_map/ppermute | solution.py:1209
  32.2 3.2 %copy-start.4 = (bf16[24,128,128]{2,1,0:T(8,128)(2,1)S(1)}, bf16[24,128,128]{2,1,0:T(8,128)(2,1)}, u32[]{:S(2)}) copy-start(bf16[24,128,128]{2,1,0:T(8,128)(2,1)} %refs_3_.10) | copy-start | bytes 2359300
  32.2 8.1 %collective-permute-start.9 = (s16[672,128]{1,0:T(8,128)(2,1)S(1)}, s16[672,128]{1,0:T(8,128)(2,1)S(1)}, u32[]{:S(2)}, u32[]{:S(2)}) collective-permute-start(s16[672,128]{1,0:T(8,128)(2,1)S(1)} %get-tuple-element.63), channel_id=1, source_target_pairs={{0,2},{1,3},{2,0},{3,1},{4,6},{5,7},{6,4},{7,5},{8,10},{9,11},{10,... | collective-permute-start | bytes 516104 | tf_op jit(solution)/shard_map/ppermute | solution.py:1192
  34.7 6.2 %collective-permute-start.7 = (s16[672,128]{1,0:T(8,128)(2,1)S(1)}, s16[672,128]{1,0:T(8,128)(2,1)S(1)}, u32[]{:S(2)}, u32[]{:S(2)}) collective-permute-start(s16[672,128]{1,0:T(8,128)(2,1)S(1)} %inverse_rest.4.refs_4_), channel_id=1, source_target_pairs={{0,1},{1,0},{2,3},{3,2},{4,5},{5,4},{6,7},{7,6},{8,9},{9,8},{10,11... | collective-permute-start | bytes 516104 | tf_op jit(solution)/shard_map/ppermute | solution.py:1192
  34.8 6.8 %collective-permute-start.8 = (s16[672,128]{1,0:T(8,128)(2,1)S(1)}, s16[672,128]{1,0:T(8,128)(2,1)S(1)}, u32[]{:S(2)}, u32[]{:S(2)}) collective-permute-start(s16[672,128]{1,0:T(8,128)(2,1)S(1)} %get-tuple-element.62), channel_id=1, source_target_pairs={{0,3},{1,2},{2,1},{3,0},{4,7},{5,6},{6,5},{7,4},{8,11},{9,10},{10,... | collective-permute-start | bytes 516104 | tf_op jit(solution)/shard_map/ppermute | solution.py:1192
  39.4 1.0 %copy-start.5 = (bf16[4,128,256]{2,1,0:T(8,128)(2,1)S(1)}, bf16[4,128,256]{2,1,0:T(8,128)(2,1)}, u32[]{:S(2)}) copy-start(bf16[4,128,256]{2,1,0:T(8,128)(2,1)} %constant.79.clone.refs_2_.refs_3_) | copy-start | bytes 786436
  39.4 1.0 %copy-start.6 = (bf16[4,128,256]{2,1,0:T(8,128)(2,1)S(1)}, bf16[4,128,256]{2,1,0:T(8,128)(2,1)}, u32[]{:S(2)}) copy-start(bf16[4,128,256]{2,1,0:T(8,128)(2,1)} %constant.80.clone.refs_3_.refs_4_) | copy-start | bytes 786436
  40.3 1.3 %copy-start.7 = (s32[512]{0:T(512)S(1)}, s32[512]{0:T(512)}, u32[]{:S(2)}) copy-start(s32[512]{0:T(512)} %param.17) | copy-start | bytes 6148
  46.4 7.3 %collective-permute-start.11 = (s16[672,128]{1,0:T(8,128)(2,1)S(1)}, s16[672,128]{1,0:T(8,128)(2,1)S(1)}, u32[]{:S(2)}, u32[]{:S(2)}) collective-permute-start(s16[672,128]{1,0:T(8,128)(2,1)S(1)} %get-tuple-element.68), channel_id=1, source_target_pairs={{0,2},{1,3},{2,0},{3,1},{4,6},{5,7},{6,4},{7,5},{8,10},{9,11},{10,... | collective-permute-start | bytes 516104 | tf_op jit(solution)/shard_map/ppermute | solution.py:1192
  47.9 6.4 %collective-permute-start.10 = (s16[672,128]{1,0:T(8,128)(2,1)S(1)}, s16[672,128]{1,0:T(8,128)(2,1)S(1)}, u32[]{:S(2)}, u32[]{:S(2)}) collective-permute-start(s16[672,128]{1,0:T(8,128)(2,1)S(1)} %spread_rest.7), channel_id=1, source_target_pairs={{0,1},{1,0},{2,3},{3,2},{4,5},{5,4},{6,7},{7,6},{8,9},{9,8},{10,11... | collective-permute-start | bytes 516104 | tf_op jit(solution)/shard_map/ppermute | solution.py:1192
  48.6 7.6 %collective-permute-start.12 = (s16[672,128]{1,0:T(8,128)(2,1)S(1)}, s16[672,128]{1,0:T(8,128)(2,1)S(1)}, u32[]{:S(2)}, u32[]{:S(2)}) collective-permute-start(s16[672,128]{1,0:T(8,128)(2,1)S(1)} %get-tuple-element.69), channel_id=1, source_target_pairs={{0,3},{1,2},{2,1},{3,0},{4,7},{5,6},{6,5},{7,4},{8,11},{9,10},{10,... | collective-permute-start | bytes 516104 | tf_op jit(solution)/shard_map/ppermute | solution.py:1192
  57.6 5.3 %collective-permute-start.15 = (s16[400,128]{1,0:T(8,128)(2,1)S(1)}, s16[400,128]{1,0:T(8,128)(2,1)S(1)}, u32[]{:S(2)}, u32[]{:S(2)}) collective-permute-start(s16[400,128]{1,0:T(8,128)(2,1)S(1)} %get-tuple-element.75), channel_id=1, source_target_pairs={{0,4},{8,12},{4,0},{12,8},{1,5},{9,13},{5,1},{13,9},{2,6},{10,14},... | collective-permute-start | bytes 307208 | tf_op jit(solution)/shard_map/ppermute | solution.py:1205
  57.6 7.9 %collective-permute-start.14 = (s16[592,128]{1,0:T(8,128)(2,1)S(1)}, s16[592,128]{1,0:T(8,128)(2,1)S(1)}, u32[]{:S(2)}, u32[]{:S(2)}) collective-permute-start(s16[592,128]{1,0:T(8,128)(2,1)S(1)} %get-tuple-element.74), channel_id=1, source_target_pairs={{4,8},{8,4},{5,9},{9,5},{6,10},{10,6},{7,11},{11,7},{20,24},{24,20... | collective-permute-start | bytes 454664 | tf_op jit(solution)/shard_map/ppermute | solution.py:1206
  58.5 7.0 %collective-permute-start.13 = (s16[336,128]{1,0:T(8,128)(2,1)S(1)}, s16[336,128]{1,0:T(8,128)(2,1)S(1)}, u32[]{:S(2)}, u32[]{:S(2)}) collective-permute-start(s16[336,128]{1,0:T(8,128)(2,1)S(1)} %get-tuple-element.73), channel_id=1, source_target_pairs={{0,4},{8,12},{4,0},{12,8},{1,5},{9,13},{5,1},{13,9},{2,6},{10,14},... | collective-permute-start | bytes 258056 | tf_op jit(solution)/shard_map/ppermute | solution.py:1207
  63.1 6.8 %collective-permute-start.16 = (s16[272,128]{1,0:T(8,128)(2,1)S(1)}, s16[272,128]{1,0:T(8,128)(2,1)S(1)}, u32[]{:S(2)}, u32[]{:S(2)}) collective-permute-start(s16[272,128]{1,0:T(8,128)(2,1)S(1)} %pair_messages.3), channel_id=1, source_target_pairs={{0,8},{4,12},{8,0},{12,4},{1,9},{5,13},{9,1},{13,5},{2,10},{6,14},... | collective-permute-start | bytes 208904 | tf_op jit(solution)/shard_map/ppermute | solution.py:1209
  71.8 5.9 %collective-permute-start.19 = (s16[672,128]{1,0:T(8,128)(2,1)S(1)}, s16[672,128]{1,0:T(8,128)(2,1)S(1)}, u32[]{:S(2)}, u32[]{:S(2)}) collective-permute-start(s16[672,128]{1,0:T(8,128)(2,1)S(1)} %get-tuple-element.81), channel_id=1, source_target_pairs={{0,2},{1,3},{2,0},{3,1},{4,6},{5,7},{6,4},{7,5},{8,10},{9,11},{10,... | collective-permute-start | bytes 516104 | tf_op jit(solution)/shard_map/ppermute | solution.py:1192
  74.5 3.7 %collective-permute-start.17 = (s16[672,128]{1,0:T(8,128)(2,1)S(1)}, s16[672,128]{1,0:T(8,128)(2,1)S(1)}, u32[]{:S(2)}, u32[]{:S(2)}) collective-permute-start(s16[672,128]{1,0:T(8,128)(2,1)S(1)} %inverse_rest.6.refs_4_), channel_id=1, source_target_pairs={{0,1},{1,0},{2,3},{3,2},{4,5},{5,4},{6,7},{7,6},{8,9},{9,8},{10,11... | collective-permute-start | bytes 516104 | tf_op jit(solution)/shard_map/ppermute | solution.py:1192
  74.5 6.2 %collective-permute-start.18 = (s16[672,128]{1,0:T(8,128)(2,1)S(1)}, s16[672,128]{1,0:T(8,128)(2,1)S(1)}, u32[]{:S(2)}, u32[]{:S(2)}) collective-permute-start(s16[672,128]{1,0:T(8,128)(2,1)S(1)} %get-tuple-element.80), channel_id=1, source_target_pairs={{0,3},{1,2},{2,1},{3,0},{4,7},{5,6},{6,5},{7,4},{8,11},{9,10},{10,... | collective-permute-start | bytes 516104 | tf_op jit(solution)/shard_map/ppermute | solution.py:1192

commit v20 on v19

--- a/solution.py
+++ b/solution.py
@@ -16,6 +16,7 @@
 KERNEL_GAIN = 4.0
 SCREEN = 1.0 / 1024.0
 LN2 = math.log(2.0)
+SPARE = 16
 Y_AXES = ("narrow", "pair")
 ALL_AXES = ("wide", "narrow", "pair")
 F32 = jnp.float32
@@ -164,9 +165,7 @@
     root = np.sqrt(shift * (shift + 4.0))
     decay = 2.0 / (2.0 + shift + root)
     log_decay = np.log(decay)
-    ring = 1.0 / (1.0 - np.exp(GRID * log_decay))
-    gain = KERNEL_GAIN / root
-    modes = np.stack([decay, log_decay, ring, gain], axis=1).astype(np.float32)
+    modes = np.stack([decay, log_decay], axis=1).astype(np.float32)
     return (
         halves(z_forward),
         halves(z_inverse),
@@ -208,7 +207,7 @@
 
 
 def pair_count(reach_x, reach_y):
-    return (2 * reach_x - 2) * reach_y
+    return (2 * reach_x - 2) * reach_y + SPARE
 
 
 def in_window(lanes, depth):
@@ -266,7 +265,7 @@
         ]
         total[x * reach_y : (x + 1) * reach_y, :] = sum(parts[1:], parts[0])
     half = reach_x * reach_y // 2
-    both = jnp.concatenate([total[:half, :], total[half:, :]], axis=1)
+    both = jnp.concatenate([total[:half, :], total[half : 2 * half, :]], axis=1)
     extra = wides[0].shape[0] - half
     if extra:
         both = jnp.concatenate([both, jnp.zeros((extra, 2 * REGION), F32)], axis=0)
@@ -295,8 +294,8 @@
     fetch(vector_in, vector_ref)
     for tile in range(tiles):
         lanes = pl.ds(tile * BLOCK, BLOCK)
-        fetch(sample_in.at[:, lanes], samples.at[tile])
-        fetch(dipole_in.at[:, lanes], dipoles.at[tile])
+        fetch(sample_in.at[:, lanes], samples.at[tile, pl.ds(0, 64)])
+        fetch(dipole_in.at[:, lanes], dipoles.at[tile, pl.ds(0, 64)])
     needed_first = len(copies)
     fetch(rounded_in, rounded)
     fetch(high_in, high)
@@ -373,13 +372,13 @@
     top = up_to(2 + 2 * blocks, 16)
     lanes = 2 * HALF
     body = up_to(half, 16)
-    woven = (count // GROUP * 16, BLOCK)
+    woven = (count // GROUP * 16 + SPARE, BLOCK)
     out_shapes = [jax.ShapeDtypeStruct((top + body, lanes), jnp.int16)] * len(flips)
     out_shapes += [jax.ShapeDtypeStruct((body, 2 * REGION), BF16)] * 2
     rounded = vector.reshape(blocks, BLOCK)
     work = [
         pltpu.VMEM((top, lanes), F32),
-        pltpu.VMEM((reach_x * reach_y, REGION), F32),
+        pltpu.VMEM((reach_x * reach_y + SPARE, REGION), F32),
     ] + [pltpu.VMEM((pair_count(reach_x, reach_y), REGION), F32)] * CHAINS
     if placed is None:
         stencil, flag, sample, dipole = raw
@@ -390,7 +389,7 @@
         out_shapes += [jax.ShapeDtypeStruct((2, count), jnp.int32)]
         out_shapes += [jax.ShapeDtypeStruct(rounded.shape, F32)]
         out_shapes += [jax.ShapeDtypeStruct(values.shape, BF16) for values in table]
-        tiled = pltpu.VMEM((blocks, 64, BLOCK), F32)
+        tiled = pltpu.VMEM((blocks, 64 + SPARE, BLOCK), F32)
         work = [
             pltpu.VMEM(stencil.shape, jnp.int32),
             pltpu.VMEM((1, count), jnp.int32),
@@ -467,8 +466,10 @@
 
 
 def sample_lines_kernel(tiles, place_ref, *refs):
-    out_ref, coeff = refs[-2:]
-    weave([by_depth(ref) for ref in refs[:tiles]], mixing_matrix(), coeff)
+    out_ref, coeff, held = refs[-3:]
+    for tile, ref in enumerate(refs[:tiles]):
+        held[tile, :64, :] = ref[...]
+    weave([by_depth(held.at[tile]) for tile in range(tiles)], mixing_matrix(), coeff)
     lines_kernel(place_ref, coeff, out_ref)
 
 
@@ -483,7 +484,10 @@
         in_specs=[in_smem()] + [tile(t) for t in range(blocks)],
         out_specs=pl.BlockSpec(shape, lambda i: (0, 0)),
         out_shape=jax.ShapeDtypeStruct(shape, F32),
-        scratch_shapes=[pltpu.VMEM((count // GROUP * 16, BLOCK), F32)],
+        scratch_shapes=[
+            pltpu.VMEM((count // GROUP * 16 + SPARE, BLOCK), F32),
+            pltpu.VMEM((blocks, 64 + SPARE, BLOCK), F32),
+        ],
         compiler_params=params(),
         cost_estimate=cost(16 * count * REGION, 4 * 16 * count * REGION),
         name="place_sample_lines",
@@ -575,7 +579,7 @@
         out_specs=[whole_vmem()] * 2,
         out_shape=[
             jax.ShapeDtypeStruct((half, GRID, 2 * HALF), F32),
-            jax.ShapeDtypeStruct((2, chips * 2 * reach_y, 2 * HALF), F32),
+            jax.ShapeDtypeStruct((2, chips * 2 * reach_y + SPARE, 2 * HALF), F32),
         ],
         scratch_shapes=stacking_scratch(chips, reach_x, reach_y),
         compiler_params=params(),
@@ -670,14 +674,15 @@
         out[:first, :] = to_short(head[:first, :])
 
     with_most = lambda values: (values, jnp.abs(values))
+    border = pieces * 2 * reach_y
     on_left = lax.axis_index("wide") & 1
     for side, (even, odd) in enumerate(((0, 1), (1, 0))):
 
         @pl.when(on_left == side)
         def _():
             send(even_out, 16, [(slabs[even], largest[even]), with_most(packed[even])])
-            send(layers_out, top, [with_most(edges[1 - even])])
-            send(odd_out, top, [(slabs[odd], largest[odd]), with_most(edges[1 - odd])])
+            send(layers_out, top, [with_most(edges[1 - even, :border, :])])
+            send(odd_out, top, [(slabs[odd], largest[odd]), with_most(edges[1 - odd, :border, :])])
 
 
 def forward(parts, early, early_edges, table, modes, reach_x, reach_y, blocks, awaited):
@@ -704,7 +709,7 @@
         ],
         scratch_shapes=stacking_scratch(pieces // table.shape[0], reach_x, reach_y)
         + [
-            pltpu.VMEM((2, border, lanes), F32),
+            pltpu.VMEM((2, border + SPARE, lanes), F32),
             pltpu.VMEM((2, GRID, lanes), F32),
             pltpu.VMEM((head, lanes), F32),
         ],
@@ -858,8 +863,8 @@
         low = low_lanes(chunk)
         decay = modes_ref[0, rows, :]
         log_decay = modes_ref[1, rows, :]
-        ring = modes_ref[2, rows, :]
-        gain = modes_ref[3, rows, :]
+        ring = 1.0 / (1.0 - jnp.exp(GRID * log_decay))
+        gain = KERNEL_GAIN * decay / ((1.0 - decay) * (1.0 + decay))
         across_half = jnp.exp(half * log_decay)
         across_cut = jnp.exp((half - 4) * log_decay)
         around = jnp.exp((GRID - 4) * log_decay)
@@ -1016,7 +1021,7 @@
     half_rows = reach_x * reach_y // 2
     both = early_ref[...] + z_lines(parts, flips, high_ref, low_ref)
     flat[:half_rows, :] = both[:half_rows, :REGION]
-    flat[half_rows:, :] = both[:half_rows, REGION:]
+    flat[half_rows : 2 * half_rows, :] = both[:half_rows, REGION:]
     for x in range(reach_x):
         layer = flat[x * reach_y : (x + 1) * reach_y, :]
         for row in pair_rows(x, reach_x, reach_y):
@@ -1071,7 +1076,7 @@
         out_specs=whole_vmem(),
         out_shape=jax.ShapeDtypeStruct(shape, F32),
         scratch_shapes=[
-            pltpu.VMEM((reach_x * reach_y, REGION), F32),
+            pltpu.VMEM((reach_x * reach_y + SPARE, REGION), F32),
             pltpu.VMEM((pair_count(reach_x, reach_y), REGION), F32),
             pltpu.VMEM((count, REGION), F32),
             pltpu.SMEM((2, count), jnp.int32),
@@ -1137,7 +1142,7 @@
         + [anywhere()] * len(awaited),
         out_specs=constant((out_rows, BLOCK)),
         out_shape=jax.ShapeDtypeStruct((out_rows, BLOCK), F32),
-        scratch_shapes=[pltpu.VMEM((3 * peers.shape[0], BLOCK), F32)],
+        scratch_shapes=[pltpu.VMEM((3 * peers.shape[0] + SPARE, BLOCK), F32)],
         compiler_params=params(),
         cost_estimate=cost(2 * slots * 16 * BLOCK * BLOCK, 2 * slots * BLOCK * BLOCK),
         name="near_field",

time: 83.8 us -> 84.1 us (level)
  transfers between devices with their start and end apart: 20 -> 20, of which waited for: 9 -> 10; matrix products, arithmetic and copies ran while one was open for 1% -> 1% of each run, Pallas kernels for 21% -> 21%
where the time goes in v20:
time: 84.1 us; the launch traced here: 83.9 us
  Pallas kernels  36.5 us (43%)
  starting transfers between devices  24.2 us (29%)
  waiting for transfers between devices  20.7 us (25%)
  local copies, waits for them, and re-layouts  2.05 us (2%)
    ppermute x12, waiting for transfers between devices, turned(): lax.ppermute(part, Y_AXES, swap_pairs)  10.2 us
    ppermute x12, starting transfers between devices, turned(): lax.ppermute(part, Y_AXES, swap_pairs)  10 us
    ppermute x2, starting transfers between devices, convolve_and_sample(): even_layers = lax.ppermute(layers, 'wide', even_swap)  8.61 us
    pallas_call x2, Pallas kernels, spread(): pl.pallas_call(functools.partial(start_kernel if placed is None else spre...  7.7 us
    ppermute x2, waiting for transfers between devices, convolve_and_sample(): lax.ppermute(message, 'wide', [(i, i ^ flip) for i in range(x_count)])  7.39 us
    pallas_call x2, Pallas kernels, sample(): pl.pallas_call(functools.partial(sample_kernel, last, reach_x, reach_y, f...  4.87 us
    pallas_call x2, Pallas kernels, inverse(): pl.pallas_call(functools.partial(inverse_kernel, reach_x, reach_y, flips,...  3.91 us
    pallas_call x4, Pallas kernels, inverse_rest(): pl.pallas_call(functools.partial(inverse_rest_kernel, reach_y, flips), in...  3.41 us
  transfers between devices with their start and end apart: 20, of which 10 were waited for; matrix products, arithmetic and copies ran while one was open for 1% of the time, Pallas kernels for 21%

profile of v20, /device:TPU:0, one launch (start us, length us, event | category | flops | bytes accessed | tf_op | source)
XLA Modules:
  0.0 83.9 jit_solution(7656807445064434714)
XLA Ops:
  0.0 5.0 %start.1 = (s16[672,128]{1,0:T(8,128)(2,1)S(1)}, s16[672,128]{1,0:T(8,128)(2,1)S(1)}, bf16[656,256]{1,0:T(8,128)(2,1)S(1)}, bf16[656,256]{1,0:T(8,128)(2,1)S(1)}...) custom-call(f32[512]{0:T(512)} %refs_0_.2, ...), custom_call_target="tpu_custom_call" | custom-call | flops 169869312 | bytes 4194304 | tf_op jit(solution)/shard_map/start/pallas_call | solution.py:410
  5.0 3.0 %collective-permute-start.1 = (s16[672,128]{1,0:T(8,128)(2,1)S(1)}, s16[672,128]{1,0:T(8,128)(2,1)S(1)}, u32[]{:S(2)}, u32[]{:S(2)}) collective-permute-start(s16[672,128]{1,0:T(8,128)(2,1)S(1)} %get-tuple-element.50), channel_id=1, source_target_pairs={{0,2},{1,3},{2,0},{3,1},{4,6},{5,7},{6,4},{7,5},{8,10},{9,11},{10,... | collective-permute-start | bytes 516104 | tf_op jit(solution)/shard_map/ppermute | solution.py:1197
  8.1 0.5 spread_rest.5
  8.6 0.1 collective-permute-start
  8.7 0.1 collective-permute-start.2
  8.8 0.9 %copy-done.3 = f32[64,512]{1,0:T(8,128)S(1)} copy-done((f32[64,512]{1,0:T(8,128)S(1)}, f32[64,512]{1,0:T(8,128)}, u32[]{:S(2)}) %copy-start.3) | copy-done | bytes 131096
  9.7 3.4 %place_sample_lines.1.refs_8_.refs_5_ = f32[8192,128]{1,0:T(8,128)S(1)} custom-call(s32[2,512]{1,0:T(2,128)S(1)} %get-tuple-element.44.place_ref.place_in.refs_1_, f32[64,512]{1,0:T(8,128)S(1)} %copy-done.3, f32[64,512]{1,0:T(8,128)S(1)} %copy-done.3, f32[64,512]{1,0:T(8,128)S(1)} %copy-done.3, f32[64,512]{1,0:T(8,128)S(1)} %copy-done.3), custom_call_target="tpu_custom_call" | custom-call | flops 1048576 | bytes 4194304 | tf_op jit(solution)/shard_map/place_sample_lines/pallas_call | solution.py:481
  13.1 0.5 spread_rest.4.refs_0_
  13.6 1.0 %dynamic-slice_bitcast_fusion.refs_7_.modes_ref.refs_9_ = f32[2,256,128]{2,1,0:T(8,128)S(1)} fusion(f32[4,2,256,128]{3,2,1,0:T(8,128)} %constant.73.clone, s32[]{:T(128)S(6)} %select_n.30), kind=kLoop, calls=%fused_computation | loop fusion | bytes 524292 | tf_op jit(solution)/shard_map/jit(dynamic_index_in_dim)/squeeze | solution.py:1174
  14.6 0.7 forward_early.2
  15.3 0.1 collective-permute-done.2.refs_3_
  15.5 1.3 %forward.2 = (f32[18,256,128]{2,1,0:T(8,128)S(1)}, s16[400,128]{1,0:T(8,128)(2,1)S(1)}, s16[336,128]{1,0:T(8,128)(2,1)S(1)}, s16[592,128]{1,0:T(8,128)(2,1)S(1)}...) custom-call(s16[672,128]{1,0:T(8,128)(2,1)S(1)} %spread_rest.4.refs_0_, ...), custom_call_target="tpu_custom_call" | custom-call | flops 301989888 | bytes 4718592 | tf_op jit(solution)/shard_map/forward/pallas_call | solution.py:695
  16.8 2.1 %collective-permute-start.5 = (s16[400,128]{1,0:T(8,128)(2,1)S(1)}, s16[400,128]{1,0:T(8,128)(2,1)S(1)}, u32[]{:S(2)}, u32[]{:S(2)}) collective-permute-start(s16[400,128]{1,0:T(8,128)(2,1)S(1)} %get-tuple-element.57), channel_id=1, source_target_pairs={{0,4},{8,12},{4,0},{12,8},{1,5},{9,13},{5,1},{13,9},{2,6},{10,14},... | collective-permute-start | bytes 307208 | tf_op jit(solution)/shard_map/ppermute | solution.py:1210
  18.8 0.8 %collective-permute-start.4 = (s16[592,128]{1,0:T(8,128)(2,1)S(1)}, s16[592,128]{1,0:T(8,128)(2,1)S(1)}, u32[]{:S(2)}, u32[]{:S(2)}) collective-permute-start(s16[592,128]{1,0:T(8,128)(2,1)S(1)} %get-tuple-element.56), channel_id=1, source_target_pairs={{4,8},{8,4},{5,9},{9,5},{6,10},{10,6},{7,11},{11,7},{20,24},{24,20... | collective-permute-start | bytes 454664 | tf_op jit(solution)/shard_map/ppermute | solution.py:1211
  19.7 4.5 %collective-permute-start.3 = (s16[336,128]{1,0:T(8,128)(2,1)S(1)}, s16[336,128]{1,0:T(8,128)(2,1)S(1)}, u32[]{:S(2)}, u32[]{:S(2)}) collective-permute-start(s16[336,128]{1,0:T(8,128)(2,1)S(1)} %get-tuple-element.55), channel_id=1, source_target_pairs={{0,4},{8,12},{4,0},{12,8},{1,5},{9,13},{5,1},{13,9},{2,6},{10,14},... | collective-permute-start | bytes 258056 | tf_op jit(solution)/shard_map/ppermute | solution.py:1212
  24.2 0.2 pair_messages.2
  24.3 0.0 copy-start.8
  24.4 0.9 %collective-permute-start.6 = (s16[272,128]{1,0:T(8,128)(2,1)S(1)}, s16[272,128]{1,0:T(8,128)(2,1)S(1)}, u32[]{:S(2)}, u32[]{:S(2)}) collective-permute-start(s16[272,128]{1,0:T(8,128)(2,1)S(1)} %pair_messages.2), channel_id=1, source_target_pairs={{0,8},{4,12},{8,0},{12,4},{1,9},{5,13},{9,1},{13,5},{2,10},{6,14},... | collective-permute-start | bytes 208904 | tf_op jit(solution)/shard_map/ppermute | solution.py:1214
  25.2 1.4 %collective-permute-done.3.layers_ref.refs_0_ = s16[336,128]{1,0:T(8,128)(2,1)S(1)} collective-permute-done((s16[336,128]{1,0:T(8,128)(2,1)S(1)}, s16[336,128]{1,0:T(8,128)(2,1)S(1)}, u32[]{:S(2)}, u32[]{:S(2)}) %collective-permute-start.3) | collective-permute-done | bytes 86048 | tf_op jit(solution)/shard_map/ppermute | solution.py:1212
  26.6 0.5 borders.2.refs_1_
  27.1 3.4 %collective-permute-done.6.refs_6_ = s16[272,128]{1,0:T(8,128)(2,1)S(1)} collective-permute-done((s16[272,128]{1,0:T(8,128)(2,1)S(1)}, s16[272,128]{1,0:T(8,128)(2,1)S(1)}, u32[]{:S(2)}, u32[]{:S(2)}) %collective-permute-start.6) | collective-permute-done | bytes 69664 | tf_op jit(solution)/shard_map/ppermute | solution.py:1214
  30.4 2.0 %inverse.2 = (s16[672,128]{1,0:T(8,128)(2,1)S(1)}, s16[672,128]{1,0:T(8,128)(2,1)S(1)}, bf16[18,256,128]{2,1,0:T(8,128)(2,1)S(1)}, bf16[18,256,128]{2,1,0:T(8,128)(2,1)S(1)}) custom-call(f32[18,256,128]{2,1,0:T(8,128)S(1)} %get-tuple-element.54.refs_0_, f32[4,256,128]{2,1,0:T(8,128)S(1)} %borders.2.refs_1_, ...), custom_call_target="tpu_custom_call" | custom-call | flops 301989888 | bytes 4718592 | tf_op jit(solution)/shard_map/inverse/pallas_call | solution.py:928
  32.4 1.6 %collective-permute-start.9 = (s16[672,128]{1,0:T(8,128)(2,1)S(1)}, s16[672,128]{1,0:T(8,128)(2,1)S(1)}, u32[]{:S(2)}, u32[]{:S(2)}) collective-permute-start(s16[672,128]{1,0:T(8,128)(2,1)S(1)} %get-tuple-element.63), channel_id=1, source_target_pairs={{0,2},{1,3},{2,0},{3,1},{4,6},{5,7},{6,4},{7,5},{8,10},{9,11},{10,... | collective-permute-start | bytes 516104 | tf_op jit(solution)/shard_map/ppermute | solution.py:1197
  34.0 0.8 %inverse_rest.4.refs_4_ = s16[672,128]{1,0:T(8,128)(2,1)S(1)} custom-call(bf16[18,256,128]{2,1,0:T(8,128)(2,1)S(1)} %get-tuple-element.60.field_high, bf16[18,256,128]{2,1,0:T(8,128)(2,1)S(1)} %get-tuple-element.61.field_low, bf16[4,48,256]{2,1,0:T(8,128)(2,1)S(1)} %copy-done.1, bf16[4,48,256]{2,1,0:T(8,128)(2,1)S(1)} %copy-done.2), custom_call_target="tpu_custom_call" | custom-call | flops 301989888 | bytes 4718592 | tf_op jit(solution)/shard_map/inverse_rest/pallas_call | solution.py:952
  34.9 0.1 collective-permute-start.7
  34.9 0.7 collective-permute-start.8
  35.6 1.0 %near_field.2.refs_8_.refs_0_ = f32[8,128]{1,0:T(8,128)S(1)} custom-call(s32[24]{0:T(128)S(1)} %get-tuple-element.84.place_ref, s32[24]{0:T(128)S(1)} %get-tuple-element.83.target_ref, s16[336,128]{1,0:T(8,128)(2,1)S(1)} %collective-permute-done.3.layers_ref.refs_0_, s16[592,128]{1,0:T(8,128)(2,1)S(1)} %collective-permute-done.4.odd_ref.refs_3_.refs_1_, ...), custom_call_target="tpu_custom_call" | custom-call | flops 12582912 | bytes 786432 | tf_op jit(solution)/shard_map/near_field/pallas_call | solution.py:1131
  36.6 3.0 %place_lines.1.refs_5_ = f32[8192,128]{1,0:T(8,128)S(1)} custom-call(s32[2,512]{1,0:T(2,128)S(1)} %get-tuple-element.44.place_ref.place_in.refs_1_, f32[272,128]{1,0:T(8,128)S(1)} %get-tuple-element.65.coeff_ref, f32[8,128]{1,0:T(8,128)S(1)} %near_field.2.refs_8_.refs_0_), custom_call_target="tpu_custom_call" | custom-call | flops 1048576 | bytes 4194304 | tf_op jit(solution)/shard_map/place_lines/pallas_call | solution.py:500
  39.6 0.0 copy-start.6
  39.6 0.8 %inverse_rest.5.refs_0_ = s16[672,128]{1,0:T(8,128)(2,1)S(1)} custom-call(bf16[18,256,128]{2,1,0:T(8,128)(2,1)S(1)} %get-tuple-element.60.field_high, bf16[18,256,128]{2,1,0:T(8,128)(2,1)S(1)} %get-tuple-element.61.field_low, bf16[4,48,256]{2,1,0:T(8,128)(2,1)S(1)} %copy-done.1, bf16[4,48,256]{2,1,0:T(8,128)(2,1)S(1)} %copy-done.2), custom_call_target="tpu_custom_call" | custom-call | flops 301989888 | bytes 4718592 | tf_op jit(solution)/shard_map/inverse_rest/pallas_call | solution.py:952
  40.5 0.0 copy-done.5
  40.6 0.1 copy-done.6
  40.6 0.4 sample_early.2.refs_2_
  41.1 0.6 collective-permute-done.8.refs_1_
  41.7 2.1 %sample.2.refs_2_.rounded_ref.refs_7_ = f32[4,128]{1,0:T(4,128)S(1)} custom-call(s32[2,512]{1,0:T(2,128)S(1)} %get-tuple-element.44.place_ref.place_in.refs_1_, s16[672,128]{1,0:T(8,128)(2,1)S(1)} %collective-permute-done.7.refs_0_, s16[672,128]{1,0:T(8,128)(2,1)S(1)} %collective-permute-done.8.refs_1_, f32[656,256]{1,0:T(8,128)S(1)} %sample_early.2.refs_2_, ...), custom_call_target="tpu_custom_call" | custom-call | flops 169869312 | bytes 4194304 | tf_op jit(solution)/shard_map/sample/pallas_call | solution.py:1073
  43.9 2.7 %spread.1 = (s16[672,128]{1,0:T(8,128)(2,1)S(1)}, s16[672,128]{1,0:T(8,128)(2,1)S(1)}, bf16[656,256]{1,0:T(8,128)(2,1)S(1)}, bf16[656,256]{1,0:T(8,128)(2,1)S(1)}) custom-call(f32[512]{0:T(512)S(1)} %bitcast.6, s32[2,512]{1,0:T(2,128)S(1)} %get-tuple-element.44.place_ref.place_in.refs_1_, f32[4,128]{1,0:T(4,128)S(1)} %sample.2.refs_2_.rounded_ref.refs_7_, ...), custom_call_target="tpu_custom_call" | custom-call | flops 169869312 | bytes 4194304 | tf_op jit(solution)/shard_map/spread/pallas_call | solution.py:410
  46.6 1.2 %collective-permute-start.11 = (s16[672,128]{1,0:T(8,128)(2,1)S(1)}, s16[672,128]{1,0:T(8,128)(2,1)S(1)}, u32[]{:S(2)}, u32[]{:S(2)}) collective-permute-start(s16[672,128]{1,0:T(8,128)(2,1)S(1)} %get-tuple-element.68), channel_id=1, source_target_pairs={{0,2},{1,3},{2,0},{3,1},{4,6},{5,7},{6,4},{7,5},{8,10},{9,11},{10,... | collective-permute-start | bytes 516104 | tf_op jit(solution)/shard_map/ppermute | solution.py:1197
  47.7 0.5 spread_rest.7
  48.3 0.6 collective-permute-start.10
  48.9 0.5 collective-permute-start.12
  49.4 0.5 spread_rest.6.refs_0_
  49.9 3.9 %collective-permute-done.11.refs_1_.refs_2_ = s16[672,128]{1,0:T(8,128)(2,1)S(1)} collective-permute-done((s16[672,128]{1,0:T(8,128)(2,1)S(1)}, s16[672,128]{1,0:T(8,128)(2,1)S(1)}, u32[]{:S(2)}, u32[]{:S(2)}) %collective-permute-start.11) | collective-permute-done | bytes 172064 | tf_op jit(solution)/shard_map/ppermute | solution.py:1197
  53.8 0.7 forward_early.3
  54.5 2.1 %collective-permute-done.12.refs_3_ = s16[672,128]{1,0:T(8,128)(2,1)S(1)} collective-permute-done((s16[672,128]{1,0:T(8,128)(2,1)S(1)}, s16[672,128]{1,0:T(8,128)(2,1)S(1)}, u32[]{:S(2)}, u32[]{:S(2)}) %collective-permute-start.12) | collective-permute-done | bytes 172064 | tf_op jit(solution)/shard_map/ppermute | solution.py:1197
  56.6 1.2 %forward.3 = (f32[18,256,128]{2,1,0:T(8,128)S(1)}, s16[400,128]{1,0:T(8,128)(2,1)S(1)}, s16[336,128]{1,0:T(8,128)(2,1)S(1)}, s16[592,128]{1,0:T(8,128)(2,1)S(1)}...) custom-call(s16[672,128]{1,0:T(8,128)(2,1)S(1)} %spread_rest.6.refs_0_, ...), custom_call_target="tpu_custom_call" | custom-call | flops 301989888 | bytes 4718592 | tf_op jit(solution)/shard_map/forward/pallas_call | solution.py:695
  57.9 0.1 collective-permute-start.15
  57.9 0.9 %collective-permute-start.14 = (s16[592,128]{1,0:T(8,128)(2,1)S(1)}, s16[592,128]{1,0:T(8,128)(2,1)S(1)}, u32[]{:S(2)}, u32[]{:S(2)}) collective-permute-start(s16[592,128]{1,0:T(8,128)(2,1)S(1)} %get-tuple-element.74), channel_id=1, source_target_pairs={{4,8},{8,4},{5,9},{9,5},{6,10},{10,6},{7,11},{11,7},{20,24},{24,20... | collective-permute-start | bytes 454664 | tf_op jit(solution)/shard_map/ppermute | solution.py:1211
  58.8 4.2 %collective-permute-start.13 = (s16[336,128]{1,0:T(8,128)(2,1)S(1)}, s16[336,128]{1,0:T(8,128)(2,1)S(1)}, u32[]{:S(2)}, u32[]{:S(2)}) collective-permute-start(s16[336,128]{1,0:T(8,128)(2,1)S(1)} %get-tuple-element.73), channel_id=1, source_target_pairs={{0,4},{8,12},{4,0},{12,8},{1,5},{9,13},{5,1},{13,9},{2,6},{10,14},... | collective-permute-start | bytes 258056 | tf_op jit(solution)/shard_map/ppermute | solution.py:1212
  63.0 0.2 pair_messages.3
  63.2 0.8 collective-permute-start.16
  64.0 1.6 %collective-permute-done.13.layers_ref.refs_0_ = s16[336,128]{1,0:T(8,128)(2,1)S(1)} collective-permute-done((s16[336,128]{1,0:T(8,128)(2,1)S(1)}, s16[336,128]{1,0:T(8,128)(2,1)S(1)}, u32[]{:S(2)}, u32[]{:S(2)}) %collective-permute-start.13) | collective-permute-done | bytes 86048 | tf_op jit(solution)/shard_map/ppermute | solution.py:1212
  65.6 0.5 borders.3.refs_1_
  66.0 4.0 %collective-permute-done.16.refs_6_ = s16[272,128]{1,0:T(8,128)(2,1)S(1)} collective-permute-done((s16[272,128]{1,0:T(8,128)(2,1)S(1)}, s16[272,128]{1,0:T(8,128)(2,1)S(1)}, u32[]{:S(2)}, u32[]{:S(2)}) %collective-permute-start.16) | collective-permute-done | bytes 69664 | tf_op jit(solution)/shard_map/ppermute | solution.py:1214
  70.1 2.0 %inverse.3 = (s16[672,128]{1,0:T(8,128)(2,1)S(1)}, s16[672,128]{1,0:T(8,128)(2,1)S(1)}, bf16[18,256,128]{2,1,0:T(8,128)(2,1)S(1)}, bf16[18,256,128]{2,1,0:T(8,128)(2,1)S(1)}) custom-call(f32[18,256,128]{2,1,0:T(8,128)S(1)} %get-tuple-element.72.refs_0_, f32[4,256,128]{2,1,0:T(8,128)S(1)} %borders.3.refs_1_, ...), custom_call_target="tpu_custom_call" | custom-call | flops 301989888 | bytes 4718592 | tf_op jit(solution)/shard_map/inverse/pallas_call | solution.py:928
  72.0 1.7 %collective-permute-start.19 = (s16[672,128]{1,0:T(8,128)(2,1)S(1)}, s16[672,128]{1,0:T(8,128)(2,1)S(1)}, u32[]{:S(2)}, u32[]{:S(2)}) collective-permute-start(s16[672,128]{1,0:T(8,128)(2,1)S(1)} %get-tuple-element.81), channel_id=1, source_target_pairs={{0,2},{1,3},{2,0},{3,1},{4,6},{5,7},{6,4},{7,5},{8,10},{9,11},{10,... | collective-permute-start | bytes 516104 | tf_op jit(solution)/shard_map/ppermute | solution.py:1197
  73.8 0.8 %inverse_rest.6.refs_4_ = s16[672,128]{1,0:T(8,128)(2,1)S(1)} custom-call(bf16[18,256,128]{2,1,0:T(8,128)(2,1)S(1)} %get-tuple-element.78.field_high, bf16[18,256,128]{2,1,0:T(8,128)(2,1)S(1)} %get-tuple-element.79.field_low, bf16[4,48,256]{2,1,0:T(8,128)(2,1)S(1)} %copy-done.1, bf16[4,48,256]{2,1,0:T(8,128)(2,1)S(1)} %copy-done.2), custom_call_target="tpu_custom_call" | custom-call | flops 301989888 | bytes 4718592 | tf_op jit(solution)/shard_map/inverse_rest/pallas_call | solution.py:952
  74.6 0.1 collective-permute-start.17
  74.7 0.5 collective-permute-start.18
  75.2 1.0 %near_field.3.refs_8_ = f32[8,128]{1,0:T(8,128)S(1)} custom-call(s32[24]{0:T(128)S(1)} %get-tuple-element.84.place_ref, s32[24]{0:T(128)S(1)} %get-tuple-element.83.target_ref, s16[336,128]{1,0:T(8,128)(2,1)S(1)} %collective-permute-done.13.layers_ref.refs_0_, s16[592,128]{1,0:T(8,128)(2,1)S(1)} %collective-permute-done.14.odd_ref.refs_3_.refs_1_, ...), custom_call_target="tpu_custom_call" | custom-call | flops 12582912 | bytes 786432 | tf_op jit(solution)/shard_map/near_field/pallas_call | solution.py:1131
  76.2 0.9 %inverse_rest.7.refs_0_ = s16[672,128]{1,0:T(8,128)(2,1)S(1)} custom-call(bf16[18,256,128]{2,1,0:T(8,128)(2,1)S(1)} %get-tuple-element.78.field_high, bf16[18,256,128]{2,1,0:T(8,128)(2,1)S(1)} %get-tuple-element.79.field_low, bf16[4,48,256]{2,1,0:T(8,128)(2,1)S(1)} %copy-done.1, bf16[4,48,256]{2,1,0:T(8,128)(2,1)S(1)} %copy-done.2), custom_call_target="tpu_custom_call" | custom-call | flops 301989888 | bytes 4718592 | tf_op jit(solution)/shard_map/inverse_rest/pallas_call | solution.py:952
  77.1 0.7 collective-permute-done.19.refs_1_
  77.8 0.4 sample_early.3.refs_2_
  78.3 2.7 %collective-permute-done.18.refs_1_ = s16[672,128]{1,0:T(8,128)(2,1)S(1)} collective-permute-done((s16[672,128]{1,0:T(8,128)(2,1)S(1)}, s16[672,128]{1,0:T(8,128)(2,1)S(1)}, u32[]{:S(2)}, u32[]{:S(2)}) %collective-permute-start.18) | collective-permute-done | bytes 172064 | tf_op jit(solution)/shard_map/ppermute | solution.py:1197
  81.0 2.7 %sample.3 = f32[2,512]{1,0:T(2,128)} custom-call(s32[2,512]{1,0:T(2,128)S(1)} %get-tuple-element.44.place_ref.place_in.refs_1_, s16[672,128]{1,0:T(8,128)(2,1)S(1)} %collective-permute-done.17.refs_0_, s16[672,128]{1,0:T(8,128)(2,1)S(1)} %collective-permute-done.18.refs_1_, f32[656,256]{1,0:T(8,128)S(1)} %sample_early.3.refs_2_, ...), custom_call_target="tpu_custom_call" | custom-call | flops 169869312 | bytes 4194304 | tf_op jit(solution)/shard_map/sample/pallas_call | solution.py:1073
  (26 shorter events, 0.1 us)
Async XLA Ops:
  5.0 9.6 %collective-permute-start.1 = (s16[672,128]{1,0:T(8,128)(2,1)S(1)}, s16[672,128]{1,0:T(8,128)(2,1)S(1)}, u32[]{:S(2)}, u32[]{:S(2)}) collective-permute-start(s16[672,128]{1,0:T(8,128)(2,1)S(1)} %get-tuple-element.50), channel_id=1, source_target_pairs={{0,2},{1,3},{2,0},{3,1},{4,6},{5,7},{6,4},{7,5},{8,10},{9,11},{10,... | collective-permute-start | bytes 516104 | tf_op jit(solution)/shard_map/ppermute | solution.py:1197
  8.6 6.8 %collective-permute-start = (s16[672,128]{1,0:T(8,128)(2,1)S(1)}, s16[672,128]{1,0:T(8,128)(2,1)S(1)}, u32[]{:S(2)}, u32[]{:S(2)}) collective-permute-start(s16[672,128]{1,0:T(8,128)(2,1)S(1)} %spread_rest.5), channel_id=1, source_target_pairs={{0,1},{1,0},{2,3},{3,2},{4,5},{5,4},{6,7},{7,6},{8,9},{9,8},{10,11... | collective-permute-start | bytes 516104 | tf_op jit(solution)/shard_map/ppermute | solution.py:1197
  8.7 6.8 %collective-permute-start.2 = (s16[672,128]{1,0:T(8,128)(2,1)S(1)}, s16[672,128]{1,0:T(8,128)(2,1)S(1)}, u32[]{:S(2)}, u32[]{:S(2)}) collective-permute-start(s16[672,128]{1,0:T(8,128)(2,1)S(1)} %get-tuple-element.51), channel_id=1, source_target_pairs={{0,3},{1,2},{2,1},{3,0},{4,7},{5,6},{6,5},{7,4},{8,11},{9,10},{10,... | collective-permute-start | bytes 516104 | tf_op jit(solution)/shard_map/ppermute | solution.py:1197
  8.8 0.9 %copy-start.3 = (f32[64,512]{1,0:T(8,128)S(1)}, f32[64,512]{1,0:T(8,128)}, u32[]{:S(2)}) copy-start(f32[64,512]{1,0:T(8,128)} %refs_3_.8) | copy-start | bytes 393220
  9.7 4.9 %copy-start = (bf16[2,256,240]{2,1,0:T(8,128)(2,1)S(1)}, bf16[2,256,240]{2,1,0:T(8,128)(2,1)}, u32[]{:S(2)}) copy-start(bf16[2,256,240]{2,1,0:T(8,128)(2,1)} %constant.76.clone.refs_2_.refs_6_.table_ref) | copy-start | bytes 737284
  15.5 15.0 %copy-start.1 = (bf16[4,48,256]{2,1,0:T(8,128)(2,1)S(1)}, bf16[4,48,256]{2,1,0:T(8,128)(2,1)}, u32[]{:S(2)}) copy-start(bf16[4,48,256]{2,1,0:T(8,128)(2,1)} %constant.77.clone.refs_7_.high_ref) | copy-start | bytes 294916
  15.5 15.0 %copy-start.2 = (bf16[4,48,256]{2,1,0:T(8,128)(2,1)S(1)}, bf16[4,48,256]{2,1,0:T(8,128)(2,1)}, u32[]{:S(2)}) copy-start(bf16[4,48,256]{2,1,0:T(8,128)(2,1)} %constant.78.clone.refs_8_.low_ref) | copy-start | bytes 294916
  16.8 7.4 %collective-permute-start.5 = (s16[400,128]{1,0:T(8,128)(2,1)S(1)}, s16[400,128]{1,0:T(8,128)(2,1)S(1)}, u32[]{:S(2)}, u32[]{:S(2)}) collective-permute-start(s16[400,128]{1,0:T(8,128)(2,1)S(1)} %get-tuple-element.57), channel_id=1, source_target_pairs={{0,4},{8,12},{4,0},{12,8},{1,5},{9,13},{5,1},{13,9},{2,6},{10,14},... | collective-permute-start | bytes 307208 | tf_op jit(solution)/shard_map/ppermute | solution.py:1210
  18.8 7.8 %collective-permute-start.4 = (s16[592,128]{1,0:T(8,128)(2,1)S(1)}, s16[592,128]{1,0:T(8,128)(2,1)S(1)}, u32[]{:S(2)}, u32[]{:S(2)}) collective-permute-start(s16[592,128]{1,0:T(8,128)(2,1)S(1)} %get-tuple-element.56), channel_id=1, source_target_pairs={{4,8},{8,4},{5,9},{9,5},{6,10},{10,6},{7,11},{11,7},{20,24},{24,20... | collective-permute-start | bytes 454664 | tf_op jit(solution)/shard_map/ppermute | solution.py:1211
  19.7 6.9 %collective-permute-start.3 = (s16[336,128]{1,0:T(8,128)(2,1)S(1)}, s16[336,128]{1,0:T(8,128)(2,1)S(1)}, u32[]{:S(2)}, u32[]{:S(2)}) collective-permute-start(s16[336,128]{1,0:T(8,128)(2,1)S(1)} %get-tuple-element.55), channel_id=1, source_target_pairs={{0,4},{8,12},{4,0},{12,8},{1,5},{9,13},{5,1},{13,9},{2,6},{10,14},... | collective-permute-start | bytes 258056 | tf_op jit(solution)/shard_map/ppermute | solution.py:1212
  24.3 9.6 %copy-start.8 = (s32[24]{0:T(128)S(1)}, s32[24]{0:T(128)}, u32[]{:S(2)}) copy-start(s32[24]{0:T(128)} %param.21) | copy-start | bytes 292
  24.3 9.6 %copy-start.9 = (s32[24]{0:T(128)S(1)}, s32[24]{0:T(128)}, u32[]{:S(2)}) copy-start(s32[24]{0:T(128)} %param.22) | copy-start | bytes 292
  24.4 6.1 %collective-permute-start.6 = (s16[272,128]{1,0:T(8,128)(2,1)S(1)}, s16[272,128]{1,0:T(8,128)(2,1)S(1)}, u32[]{:S(2)}, u32[]{:S(2)}) collective-permute-start(s16[272,128]{1,0:T(8,128)(2,1)S(1)} %pair_messages.2), channel_id=1, source_target_pairs={{0,8},{4,12},{8,0},{12,4},{1,9},{5,13},{9,1},{13,5},{2,10},{6,14},... | collective-permute-start | bytes 208904 | tf_op jit(solution)/shard_map/ppermute | solution.py:1214
  30.4 5.1 %copy-start.4 = (bf16[24,128,128]{2,1,0:T(8,128)(2,1)S(1)}, bf16[24,128,128]{2,1,0:T(8,128)(2,1)}, u32[]{:S(2)}) copy-start(bf16[24,128,128]{2,1,0:T(8,128)(2,1)} %refs_3_.10) | copy-start | bytes 2359300
  32.4 8.1 %collective-permute-start.9 = (s16[672,128]{1,0:T(8,128)(2,1)S(1)}, s16[672,128]{1,0:T(8,128)(2,1)S(1)}, u32[]{:S(2)}, u32[]{:S(2)}) collective-permute-start(s16[672,128]{1,0:T(8,128)(2,1)S(1)} %get-tuple-element.63), channel_id=1, source_target_pairs={{0,2},{1,3},{2,0},{3,1},{4,6},{5,7},{6,4},{7,5},{8,10},{9,11},{10,... | collective-permute-start | bytes 516104 | tf_op jit(solution)/shard_map/ppermute | solution.py:1197
  34.9 6.2 %collective-permute-start.7 = (s16[672,128]{1,0:T(8,128)(2,1)S(1)}, s16[672,128]{1,0:T(8,128)(2,1)S(1)}, u32[]{:S(2)}, u32[]{:S(2)}) collective-permute-start(s16[672,128]{1,0:T(8,128)(2,1)S(1)} %inverse_rest.4.refs_4_), channel_id=1, source_target_pairs={{0,1},{1,0},{2,3},{3,2},{4,5},{5,4},{6,7},{7,6},{8,9},{9,8},{10,11... | collective-permute-start | bytes 516104 | tf_op jit(solution)/shard_map/ppermute | solution.py:1197
  34.9 6.8 %collective-permute-start.8 = (s16[672,128]{1,0:T(8,128)(2,1)S(1)}, s16[672,128]{1,0:T(8,128)(2,1)S(1)}, u32[]{:S(2)}, u32[]{:S(2)}) collective-permute-start(s16[672,128]{1,0:T(8,128)(2,1)S(1)} %get-tuple-element.62), channel_id=1, source_target_pairs={{0,3},{1,2},{2,1},{3,0},{4,7},{5,6},{6,5},{7,4},{8,11},{9,10},{10,... | collective-permute-start | bytes 516104 | tf_op jit(solution)/shard_map/ppermute | solution.py:1197
  39.6 1.0 %copy-start.5 = (bf16[4,128,256]{2,1,0:T(8,128)(2,1)S(1)}, bf16[4,128,256]{2,1,0:T(8,128)(2,1)}, u32[]{:S(2)}) copy-start(bf16[4,128,256]{2,1,0:T(8,128)(2,1)} %constant.79.clone.refs_2_.refs_3_) | copy-start | bytes 786436
  39.6 1.0 %copy-start.6 = (bf16[4,128,256]{2,1,0:T(8,128)(2,1)S(1)}, bf16[4,128,256]{2,1,0:T(8,128)(2,1)}, u32[]{:S(2)}) copy-start(bf16[4,128,256]{2,1,0:T(8,128)(2,1)} %constant.80.clone.refs_3_.refs_4_) | copy-start | bytes 786436
  40.5 1.3 %copy-start.7 = (s32[512]{0:T(512)S(1)}, s32[512]{0:T(512)}, u32[]{:S(2)}) copy-start(s32[512]{0:T(512)} %param.17) | copy-start | bytes 6148
  46.6 7.2 %collective-permute-start.11 = (s16[672,128]{1,0:T(8,128)(2,1)S(1)}, s16[672,128]{1,0:T(8,128)(2,1)S(1)}, u32[]{:S(2)}, u32[]{:S(2)}) collective-permute-start(s16[672,128]{1,0:T(8,128)(2,1)S(1)} %get-tuple-element.68), channel_id=1, source_target_pairs={{0,2},{1,3},{2,0},{3,1},{4,6},{5,7},{6,4},{7,5},{8,10},{9,11},{10,... | collective-permute-start | bytes 516104 | tf_op jit(solution)/shard_map/ppermute | solution.py:1197
  48.3 6.2 %collective-permute-start.10 = (s16[672,128]{1,0:T(8,128)(2,1)S(1)}, s16[672,128]{1,0:T(8,128)(2,1)S(1)}, u32[]{:S(2)}, u32[]{:S(2)}) collective-permute-start(s16[672,128]{1,0:T(8,128)(2,1)S(1)} %spread_rest.7), channel_id=1, source_target_pairs={{0,1},{1,0},{2,3},{3,2},{4,5},{5,4},{6,7},{7,6},{8,9},{9,8},{10,11... | collective-permute-start | bytes 516104 | tf_op jit(solution)/shard_map/ppermute | solution.py:1197
  48.9 7.7 %collective-permute-start.12 = (s16[672,128]{1,0:T(8,128)(2,1)S(1)}, s16[672,128]{1,0:T(8,128)(2,1)S(1)}, u32[]{:S(2)}, u32[]{:S(2)}) collective-permute-start(s16[672,128]{1,0:T(8,128)(2,1)S(1)} %get-tuple-element.69), channel_id=1, source_target_pairs={{0,3},{1,2},{2,1},{3,0},{4,7},{5,6},{6,5},{7,4},{8,11},{9,10},{10,... | collective-permute-start | bytes 516104 | tf_op jit(solution)/shard_map/ppermute | solution.py:1197
  57.9 5.1 %collective-permute-start.15 = (s16[400,128]{1,0:T(8,128)(2,1)S(1)}, s16[400,128]{1,0:T(8,128)(2,1)S(1)}, u32[]{:S(2)}, u32[]{:S(2)}) collective-permute-start(s16[400,128]{1,0:T(8,128)(2,1)S(1)} %get-tuple-element.75), channel_id=1, source_target_pairs={{0,4},{8,12},{4,0},{12,8},{1,5},{9,13},{5,1},{13,9},{2,6},{10,14},... | collective-permute-start | bytes 307208 | tf_op jit(solution)/shard_map/ppermute | solution.py:1210
  57.9 7.6 %collective-permute-start.14 = (s16[592,128]{1,0:T(8,128)(2,1)S(1)}, s16[592,128]{1,0:T(8,128)(2,1)S(1)}, u32[]{:S(2)}, u32[]{:S(2)}) collective-permute-start(s16[592,128]{1,0:T(8,128)(2,1)S(1)} %get-tuple-element.74), channel_id=1, source_target_pairs={{4,8},{8,4},{5,9},{9,5},{6,10},{10,6},{7,11},{11,7},{20,24},{24,20... | collective-permute-start | bytes 454664 | tf_op jit(solution)/shard_map/ppermute | solution.py:1211
  58.8 6.7 %collective-permute-start.13 = (s16[336,128]{1,0:T(8,128)(2,1)S(1)}, s16[336,128]{1,0:T(8,128)(2,1)S(1)}, u32[]{:S(2)}, u32[]{:S(2)}) collective-permute-start(s16[336,128]{1,0:T(8,128)(2,1)S(1)} %get-tuple-element.73), channel_id=1, source_target_pairs={{0,4},{8,12},{4,0},{12,8},{1,5},{9,13},{5,1},{13,9},{2,6},{10,14},... | collective-permute-start | bytes 258056 | tf_op jit(solution)/shard_map/ppermute | solution.py:1212
  63.2 6.9 %collective-permute-start.16 = (s16[272,128]{1,0:T(8,128)(2,1)S(1)}, s16[272,128]{1,0:T(8,128)(2,1)S(1)}, u32[]{:S(2)}, u32[]{:S(2)}) collective-permute-start(s16[272,128]{1,0:T(8,128)(2,1)S(1)} %pair_messages.3), channel_id=1, source_target_pairs={{0,8},{4,12},{8,0},{12,4},{1,9},{5,13},{9,1},{13,5},{2,10},{6,14},... | collective-permute-start | bytes 208904 | tf_op jit(solution)/shard_map/ppermute | solution.py:1214
  72.0 5.8 %collective-permute-start.19 = (s16[672,128]{1,0:T(8,128)(2,1)S(1)}, s16[672,128]{1,0:T(8,128)(2,1)S(1)}, u32[]{:S(2)}, u32[]{:S(2)}) collective-permute-start(s16[672,128]{1,0:T(8,128)(2,1)S(1)} %get-tuple-element.81), channel_id=1, source_target_pairs={{0,2},{1,3},{2,0},{3,1},{4,6},{5,7},{6,4},{7,5},{8,10},{9,11},{10,... | collective-permute-start | bytes 516104 | tf_op jit(solution)/shard_map/ppermute | solution.py:1197
  74.6 3.6 %collective-permute-start.17 = (s16[672,128]{1,0:T(8,128)(2,1)S(1)}, s16[672,128]{1,0:T(8,128)(2,1)S(1)}, u32[]{:S(2)}, u32[]{:S(2)}) collective-permute-start(s16[672,128]{1,0:T(8,128)(2,1)S(1)} %inverse_rest.6.refs_4_), channel_id=1, source_target_pairs={{0,1},{1,0},{2,3},{3,2},{4,5},{5,4},{6,7},{7,6},{8,9},{9,8},{10,11... | collective-permute-start | bytes 516104 | tf_op jit(solution)/shard_map/ppermute | solution.py:1197
  74.7 6.3 %collective-permute-start.18 = (s16[672,128]{1,0:T(8,128)(2,1)S(1)}, s16[672,128]{1,0:T(8,128)(2,1)S(1)}, u32[]{:S(2)}, u32[]{:S(2)}) collective-permute-start(s16[672,128]{1,0:T(8,128)(2,1)S(1)} %get-tuple-element.80), channel_id=1, source_target_pairs={{0,3},{1,2},{2,1},{3,0},{4,7},{5,6},{6,5},{7,4},{8,11},{9,10},{10,... | collective-permute-start | bytes 516104 | tf_op jit(solution)/shard_map/ppermute | solution.py:1197

commit v21 on v20

--- a/solution.py
+++ b/solution.py
@@ -622,8 +622,8 @@
     def body(index, largest):
         rows = pl.ds(pl.multiple_of(index * chunk, chunk), chunk)
         low = low_lanes(chunk)
-        decay = modes_ref[0, rows, :]
-        log_decay = modes_ref[1, rows, :]
+        decay = modes_ref[y_position(), 0, rows, :]
+        log_decay = modes_ref[y_position(), 1, rows, :]
         across_half = jnp.exp(half * log_decay)
         across_cut = jnp.exp((half - 4) * log_decay)
         layers = [spectrum[i, rows, :] for i in range(half)]
@@ -730,7 +730,7 @@
     span = reach_x - 4
     here = lax.axis_index("wide")
     low = low_lanes(GRID)
-    log_decay = modes_ref[1]
+    log_decay = modes_ref[y_position(), 1]
     own = own_ref[...]
     top = even_ref.shape[0] - GRID - GRID // 2
     cut = opened_part(even_ref, 0, top, GRID)
@@ -861,8 +861,8 @@
         first = pl.multiple_of(index * chunk, chunk)
         rows = pl.ds(first, chunk)
         low = low_lanes(chunk)
-        decay = modes_ref[0, rows, :]
-        log_decay = modes_ref[1, rows, :]
+        decay = modes_ref[y_position(), 0, rows, :]
+        log_decay = modes_ref[y_position(), 1, rows, :]
         ring = 1.0 / (1.0 - jnp.exp(GRID * log_decay))
         gain = KERNEL_GAIN * decay / ((1.0 - decay) * (1.0 + decay))
         across_half = jnp.exp(half * log_decay)
@@ -1171,7 +1171,6 @@
     blocks = count // BLOCK
 
     z_forward, z_inverse, y_forward, y_inverse, modes = tables(y_count, pair, span_y)
-    modes = lax.dynamic_index_in_dim(jnp.asarray(modes), y_index, 0, keepdims=False)
 
     neighbour = near_source // blocks
     flip = (y_index + neighbour % 3 - 1) ^ y_index

time: 84.1 us -> 88.3 us (1.050)
  local copies, waits for them, and re-layouts: 2.05 us -> 5.48 us
  starting transfers between devices: 24.2 us -> 25.1 us
    unnamed x20 -> x30, local copies, waits for them, and re-layouts: 1.07 us -> 5.48 us
    squeeze x1 -> x0, local copies, waits for them, and re-layouts: 0.98 us -> none  [shards(): lax.dynamic_index_in_dim(jnp.asarray(modes), y_index, 0, keepdims=False)]
    ppermute x2, waiting for transfers between devices: 7.39 us -> 6.43 us  [convolve_and_sample(): lax.ppermute(message, 'wide', [(i, i ^ flip) for i in range(x_count)])]
    ppermute x2, starting transfers between devices: 8.61 us -> 9.51 us  [convolve_and_sample(): even_layers = lax.ppermute(layers, 'wide', even_swap)]
  transfers between devices with their start and end apart: 20 -> 20, of which waited for: 10 -> 10; matrix products, arithmetic and copies ran while one was open for 1% -> 0% of each run, Pallas kernels for 21% -> 20%
where the time goes in v21:
time: 88.3 us; the launch traced here: 88 us
  Pallas kernels  36.3 us (41%)
  starting transfers between devices  25.1 us (28%)
  waiting for transfers between devices  20.5 us (23%)
  local copies, waits for them, and re-layouts  5.48 us (6%)
    ppermute x12, waiting for transfers between devices, turned(): lax.ppermute(part, Y_AXES, swap_pairs)  10.7 us
    ppermute x12, starting transfers between devices, turned(): lax.ppermute(part, Y_AXES, swap_pairs)  10 us
    ppermute x2, starting transfers between devices, convolve_and_sample(): even_layers = lax.ppermute(layers, 'wide', even_swap)  9.51 us
    pallas_call x2, Pallas kernels, spread(): pl.pallas_call(functools.partial(start_kernel if placed is None else spre...  7.7 us
    ppermute x2, waiting for transfers between devices, convolve_and_sample(): lax.ppermute(message, 'wide', [(i, i ^ flip) for i in range(x_count)])  6.43 us
    unnamed x30, local copies, waits for them, and re-layouts  5.48 us
    pallas_call x2, Pallas kernels, sample(): pl.pallas_call(functools.partial(sample_kernel, last, reach_x, reach_y, f...  4.87 us
    pallas_call x2, Pallas kernels, inverse(): pl.pallas_call(functools.partial(inverse_kernel, reach_x, reach_y, flips,...  3.9 us
  transfers between devices with their start and end apart: 20, of which 10 were waited for; matrix products, arithmetic and copies ran while one was open for 0% of the time, Pallas kernels for 20%

profile of v21, /device:TPU:0, one launch (start us, length us, event | category | flops | bytes accessed | tf_op | source)
XLA Modules:
  0.0 88.0 jit_solution(5906080434223138390)
XLA Ops:
  0.0 5.0 %start.1 = (s16[672,128]{1,0:T(8,128)(2,1)S(1)}, s16[672,128]{1,0:T(8,128)(2,1)S(1)}, bf16[656,256]{1,0:T(8,128)(2,1)S(1)}, bf16[656,256]{1,0:T(8,128)(2,1)S(1)}...) custom-call(f32[512]{0:T(512)} %refs_0_.2, ...), custom_call_target="tpu_custom_call" | custom-call | flops 169869312 | bytes 4194304 | tf_op jit(solution)/shard_map/start/pallas_call | solution.py:410
  5.0 3.0 %collective-permute-start.1 = (s16[672,128]{1,0:T(8,128)(2,1)S(1)}, s16[672,128]{1,0:T(8,128)(2,1)S(1)}, u32[]{:S(2)}, u32[]{:S(2)}) collective-permute-start(s16[672,128]{1,0:T(8,128)(2,1)S(1)} %get-tuple-element.50), channel_id=1, source_target_pairs={{0,2},{1,3},{2,0},{3,1},{4,6},{5,7},{6,4},{7,5},{8,10},{9,11},{10,... | collective-permute-start | bytes 516104 | tf_op jit(solution)/shard_map/ppermute | solution.py:1196
  8.1 0.5 spread_rest.5
  8.6 0.1 collective-permute-start
  8.7 0.1 collective-permute-start.2
  8.8 0.9 %copy-done.6 = f32[64,512]{1,0:T(8,128)S(1)} copy-done((f32[64,512]{1,0:T(8,128)S(1)}, f32[64,512]{1,0:T(8,128)}, u32[]{:S(2)}) %copy-start.6) | copy-done | bytes 131096
  9.7 3.4 %place_sample_lines.1.refs_8_.refs_5_ = f32[8192,128]{1,0:T(8,128)S(1)} custom-call(s32[2,512]{1,0:T(2,128)S(1)} %get-tuple-element.44.place_ref.place_in.refs_1_, f32[64,512]{1,0:T(8,128)S(1)} %copy-done.6, f32[64,512]{1,0:T(8,128)S(1)} %copy-done.6, f32[64,512]{1,0:T(8,128)S(1)} %copy-done.6, f32[64,512]{1,0:T(8,128)S(1)} %copy-done.6), custom_call_target="tpu_custom_call" | custom-call | flops 1048576 | bytes 4194304 | tf_op jit(solution)/shard_map/place_sample_lines/pallas_call | solution.py:481
  13.1 0.5 spread_rest.4.refs_0_
  13.7 0.7 forward_early.2
  14.3 1.1 %collective-permute-done.2.refs_3_ = s16[672,128]{1,0:T(8,128)(2,1)S(1)} collective-permute-done((s16[672,128]{1,0:T(8,128)(2,1)S(1)}, s16[672,128]{1,0:T(8,128)(2,1)S(1)}, u32[]{:S(2)}, u32[]{:S(2)}) %collective-permute-start.2) | collective-permute-done | bytes 172064 | tf_op jit(solution)/shard_map/ppermute | solution.py:1196
  15.5 0.2 copy-done.2
  15.7 1.2 %forward.2 = (f32[18,256,128]{2,1,0:T(8,128)S(1)}, s16[400,128]{1,0:T(8,128)(2,1)S(1)}, s16[336,128]{1,0:T(8,128)(2,1)S(1)}, s16[592,128]{1,0:T(8,128)(2,1)S(1)}...) custom-call(s16[672,128]{1,0:T(8,128)(2,1)S(1)} %spread_rest.4.refs_0_, ...), custom_call_target="tpu_custom_call" | custom-call | flops 301989888 | bytes 4718592 | tf_op jit(solution)/shard_map/forward/pallas_call | solution.py:695
  16.9 1.4 %copy-done.8 = f32[18,256,128]{2,1,0:T(8,128)} copy-done((f32[18,256,128]{2,1,0:T(8,128)}, f32[18,256,128]{2,1,0:T(8,128)S(1)}, u32[]{:S(2)}) %copy-start.8) | copy-done | bytes 2359320
  18.3 2.1 %collective-permute-start.5 = (s16[400,128]{1,0:T(8,128)(2,1)S(1)}, s16[400,128]{1,0:T(8,128)(2,1)S(1)}, u32[]{:S(2)}, u32[]{:S(2)}) collective-permute-start(s16[400,128]{1,0:T(8,128)(2,1)S(1)} %get-tuple-element.57), channel_id=1, source_target_pairs={{0,4},{8,12},{4,0},{12,8},{1,5},{9,13},{5,1},{13,9},{2,6},{10,14},... | collective-permute-start | bytes 307208 | tf_op jit(solution)/shard_map/ppermute | solution.py:1209
  20.4 0.8 collective-permute-start.4
  21.2 4.5 %collective-permute-start.3 = (s16[336,128]{1,0:T(8,128)(2,1)S(1)}, s16[336,128]{1,0:T(8,128)(2,1)S(1)}, u32[]{:S(2)}, u32[]{:S(2)}) collective-permute-start(s16[336,128]{1,0:T(8,128)(2,1)S(1)} %get-tuple-element.55), channel_id=1, source_target_pairs={{0,4},{8,12},{4,0},{12,8},{1,5},{9,13},{5,1},{13,9},{2,6},{10,14},... | collective-permute-start | bytes 258056 | tf_op jit(solution)/shard_map/ppermute | solution.py:1211
  25.7 0.2 pair_messages.2
  25.9 0.6 collective-permute-start.6
  26.5 1.7 %collective-permute-done.3.layers_ref.refs_0_ = s16[336,128]{1,0:T(8,128)(2,1)S(1)} collective-permute-done((s16[336,128]{1,0:T(8,128)(2,1)S(1)}, s16[336,128]{1,0:T(8,128)(2,1)S(1)}, u32[]{:S(2)}, u32[]{:S(2)}) %collective-permute-start.3) | collective-permute-done | bytes 86048 | tf_op jit(solution)/shard_map/ppermute | solution.py:1211
  28.2 0.4 borders.2.refs_1_
  28.6 3.1 %collective-permute-done.6.refs_6_ = s16[272,128]{1,0:T(8,128)(2,1)S(1)} collective-permute-done((s16[272,128]{1,0:T(8,128)(2,1)S(1)}, s16[272,128]{1,0:T(8,128)(2,1)S(1)}, u32[]{:S(2)}, u32[]{:S(2)}) %collective-permute-start.6) | collective-permute-done | bytes 69664 | tf_op jit(solution)/shard_map/ppermute | solution.py:1213
  31.8 1.7 %copy-done.9 = f32[18,256,128]{2,1,0:T(8,128)S(1)} copy-done((f32[18,256,128]{2,1,0:T(8,128)S(1)}, f32[18,256,128]{2,1,0:T(8,128)}, u32[]{:S(2)}) %copy-start.9) | copy-done | bytes 2359320
  33.4 1.9 %inverse.2 = (s16[672,128]{1,0:T(8,128)(2,1)S(1)}, s16[672,128]{1,0:T(8,128)(2,1)S(1)}, bf16[18,256,128]{2,1,0:T(8,128)(2,1)S(1)}, bf16[18,256,128]{2,1,0:T(8,128)(2,1)S(1)}) custom-call(f32[18,256,128]{2,1,0:T(8,128)S(1)} %copy-done.9, f32[4,256,128]{2,1,0:T(8,128)S(1)} %borders.2.refs_1_, s16[400,128]{1,0:T(8,128)(2,1)S(1)} %collective-permute-done.5.even_ref.refs_2_, ...), custom_call_target="tpu_custom_call" | custom-call | flops 301989888 | bytes 4718592 | tf_op jit(solution)/shard_map/inverse/pallas_call | solution.py:928
  35.4 1.6 %collective-permute-start.9 = (s16[672,128]{1,0:T(8,128)(2,1)S(1)}, s16[672,128]{1,0:T(8,128)(2,1)S(1)}, u32[]{:S(2)}, u32[]{:S(2)}) collective-permute-start(s16[672,128]{1,0:T(8,128)(2,1)S(1)} %get-tuple-element.63), channel_id=1, source_target_pairs={{0,2},{1,3},{2,0},{3,1},{4,6},{5,7},{6,4},{7,5},{8,10},{9,11},{10,... | collective-permute-start | bytes 516104 | tf_op jit(solution)/shard_map/ppermute | solution.py:1196
  37.0 0.8 inverse_rest.4.refs_4_
  37.8 0.1 collective-permute-start.7
  37.9 0.7 collective-permute-start.8
  38.6 1.0 %near_field.2.refs_8_.refs_0_ = f32[8,128]{1,0:T(8,128)S(1)} custom-call(s32[24]{0:T(128)S(1)} %get-tuple-element.84.place_ref, s32[24]{0:T(128)S(1)} %get-tuple-element.83.target_ref, s16[336,128]{1,0:T(8,128)(2,1)S(1)} %collective-permute-done.3.layers_ref.refs_0_, s16[592,128]{1,0:T(8,128)(2,1)S(1)} %collective-permute-done.4.odd_ref.refs_3_.refs_1_, ...), custom_call_target="tpu_custom_call" | custom-call | flops 12582912 | bytes 786432 | tf_op jit(solution)/shard_map/near_field/pallas_call | solution.py:1131
  39.6 3.0 %place_lines.1.refs_5_ = f32[8192,128]{1,0:T(8,128)S(1)} custom-call(s32[2,512]{1,0:T(2,128)S(1)} %get-tuple-element.44.place_ref.place_in.refs_1_, f32[272,128]{1,0:T(8,128)S(1)} %get-tuple-element.65.coeff_ref, f32[8,128]{1,0:T(8,128)S(1)} %near_field.2.refs_8_.refs_0_), custom_call_target="tpu_custom_call" | custom-call | flops 1048576 | bytes 4194304 | tf_op jit(solution)/shard_map/place_lines/pallas_call | solution.py:500
  42.6 0.8 inverse_rest.5.refs_0_
  43.5 0.1 copy-done.11
  43.6 0.4 sample_early.2.refs_2_
  44.1 0.6 collective-permute-done.8.refs_1_
  44.7 1.1 %copy-done.1 = f32[8192,128]{1,0:T(8,128)S(1)} copy-done((f32[8192,128]{1,0:T(8,128)S(1)}, f32[8192,128]{1,0:T(8,128)}, u32[]{:S(2)}) %copy-start.1) | copy-done | bytes 4194328
  45.8 2.1 %sample.2.refs_2_.rounded_ref.refs_7_ = f32[4,128]{1,0:T(4,128)S(1)} custom-call(s32[2,512]{1,0:T(2,128)S(1)} %get-tuple-element.44.place_ref.place_in.refs_1_, s16[672,128]{1,0:T(8,128)(2,1)S(1)} %collective-permute-done.7.refs_0_, s16[672,128]{1,0:T(8,128)(2,1)S(1)} %collective-permute-done.8.refs_1_, f32[656,256]{1,0:T(8,128)S(1)} %sample_early.2.refs_2_, ...), custom_call_target="tpu_custom_call" | custom-call | flops 169869312 | bytes 4194304 | tf_op jit(solution)/shard_map/sample/pallas_call | solution.py:1073
  48.0 2.7 %spread.1 = (s16[672,128]{1,0:T(8,128)(2,1)S(1)}, s16[672,128]{1,0:T(8,128)(2,1)S(1)}, bf16[656,256]{1,0:T(8,128)(2,1)S(1)}, bf16[656,256]{1,0:T(8,128)(2,1)S(1)}) custom-call(f32[512]{0:T(512)S(1)} %bitcast.4, s32[2,512]{1,0:T(2,128)S(1)} %get-tuple-element.44.place_ref.place_in.refs_1_, f32[4,128]{1,0:T(4,128)S(1)} %sample.2.refs_2_.rounded_ref.refs_7_, ...), custom_call_target="tpu_custom_call" | custom-call | flops 169869312 | bytes 4194304 | tf_op jit(solution)/shard_map/spread/pallas_call | solution.py:410
  50.6 1.6 %collective-permute-start.11 = (s16[672,128]{1,0:T(8,128)(2,1)S(1)}, s16[672,128]{1,0:T(8,128)(2,1)S(1)}, u32[]{:S(2)}, u32[]{:S(2)}) collective-permute-start(s16[672,128]{1,0:T(8,128)(2,1)S(1)} %get-tuple-element.68), channel_id=1, source_target_pairs={{0,2},{1,3},{2,0},{3,1},{4,6},{5,7},{6,4},{7,5},{8,10},{9,11},{10,... | collective-permute-start | bytes 516104 | tf_op jit(solution)/shard_map/ppermute | solution.py:1196
  52.2 0.5 spread_rest.7
  52.7 0.1 collective-permute-start.10
  52.8 0.7 collective-permute-start.12
  53.4 0.5 spread_rest.6.refs_0_
  54.0 4.0 %collective-permute-done.11.refs_1_.refs_2_ = s16[672,128]{1,0:T(8,128)(2,1)S(1)} collective-permute-done((s16[672,128]{1,0:T(8,128)(2,1)S(1)}, s16[672,128]{1,0:T(8,128)(2,1)S(1)}, u32[]{:S(2)}, u32[]{:S(2)}) %collective-permute-start.11) | collective-permute-done | bytes 172064 | tf_op jit(solution)/shard_map/ppermute | solution.py:1196
  57.9 0.7 forward_early.3
  58.6 1.2 %collective-permute-done.12.refs_3_ = s16[672,128]{1,0:T(8,128)(2,1)S(1)} collective-permute-done((s16[672,128]{1,0:T(8,128)(2,1)S(1)}, s16[672,128]{1,0:T(8,128)(2,1)S(1)}, u32[]{:S(2)}, u32[]{:S(2)}) %collective-permute-start.12) | collective-permute-done | bytes 172064 | tf_op jit(solution)/shard_map/ppermute | solution.py:1196
  59.8 1.3 %forward.3 = (f32[18,256,128]{2,1,0:T(8,128)S(1)}, s16[400,128]{1,0:T(8,128)(2,1)S(1)}, s16[336,128]{1,0:T(8,128)(2,1)S(1)}, s16[592,128]{1,0:T(8,128)(2,1)S(1)}...) custom-call(s16[672,128]{1,0:T(8,128)(2,1)S(1)} %spread_rest.6.refs_0_, ...), custom_call_target="tpu_custom_call" | custom-call | flops 301989888 | bytes 4718592 | tf_op jit(solution)/shard_map/forward/pallas_call | solution.py:695
  61.1 0.1 collective-permute-start.15
  61.2 0.9 %collective-permute-start.14 = (s16[592,128]{1,0:T(8,128)(2,1)S(1)}, s16[592,128]{1,0:T(8,128)(2,1)S(1)}, u32[]{:S(2)}, u32[]{:S(2)}) collective-permute-start(s16[592,128]{1,0:T(8,128)(2,1)S(1)} %get-tuple-element.74), channel_id=1, source_target_pairs={{4,8},{8,4},{5,9},{9,5},{6,10},{10,6},{7,11},{11,7},{20,24},{24,20... | collective-permute-start | bytes 454664 | tf_op jit(solution)/shard_map/ppermute | solution.py:1210
  62.1 5.0 %collective-permute-start.13 = (s16[336,128]{1,0:T(8,128)(2,1)S(1)}, s16[336,128]{1,0:T(8,128)(2,1)S(1)}, u32[]{:S(2)}, u32[]{:S(2)}) collective-permute-start(s16[336,128]{1,0:T(8,128)(2,1)S(1)} %get-tuple-element.73), channel_id=1, source_target_pairs={{0,4},{8,12},{4,0},{12,8},{1,5},{9,13},{5,1},{13,9},{2,6},{10,14},... | collective-permute-start | bytes 258056 | tf_op jit(solution)/shard_map/ppermute | solution.py:1211
  67.1 0.2 pair_messages.3
  67.3 1.1 %collective-permute-start.16 = (s16[272,128]{1,0:T(8,128)(2,1)S(1)}, s16[272,128]{1,0:T(8,128)(2,1)S(1)}, u32[]{:S(2)}, u32[]{:S(2)}) collective-permute-start(s16[272,128]{1,0:T(8,128)(2,1)S(1)} %pair_messages.3), channel_id=1, source_target_pairs={{0,8},{4,12},{8,0},{12,4},{1,9},{5,13},{9,1},{13,5},{2,10},{6,14},... | collective-permute-start | bytes 208904 | tf_op jit(solution)/shard_map/ppermute | solution.py:1213
  68.4 1.6 %collective-permute-done.13.layers_ref.refs_0_ = s16[336,128]{1,0:T(8,128)(2,1)S(1)} collective-permute-done((s16[336,128]{1,0:T(8,128)(2,1)S(1)}, s16[336,128]{1,0:T(8,128)(2,1)S(1)}, u32[]{:S(2)}, u32[]{:S(2)}) %collective-permute-start.13) | collective-permute-done | bytes 86048 | tf_op jit(solution)/shard_map/ppermute | solution.py:1211
  70.0 0.4 borders.3.refs_1_
  70.5 3.3 %collective-permute-done.16.refs_6_ = s16[272,128]{1,0:T(8,128)(2,1)S(1)} collective-permute-done((s16[272,128]{1,0:T(8,128)(2,1)S(1)}, s16[272,128]{1,0:T(8,128)(2,1)S(1)}, u32[]{:S(2)}, u32[]{:S(2)}) %collective-permute-start.16) | collective-permute-done | bytes 69664 | tf_op jit(solution)/shard_map/ppermute | solution.py:1213
  73.8 2.0 %inverse.3 = (s16[672,128]{1,0:T(8,128)(2,1)S(1)}, s16[672,128]{1,0:T(8,128)(2,1)S(1)}, bf16[18,256,128]{2,1,0:T(8,128)(2,1)S(1)}, bf16[18,256,128]{2,1,0:T(8,128)(2,1)S(1)}) custom-call(f32[18,256,128]{2,1,0:T(8,128)S(1)} %get-tuple-element.72.refs_0_, f32[4,256,128]{2,1,0:T(8,128)S(1)} %borders.3.refs_1_, ...), custom_call_target="tpu_custom_call" | custom-call | flops 301989888 | bytes 4718592 | tf_op jit(solution)/shard_map/inverse/pallas_call | solution.py:928
  75.8 1.6 %collective-permute-start.19 = (s16[672,128]{1,0:T(8,128)(2,1)S(1)}, s16[672,128]{1,0:T(8,128)(2,1)S(1)}, u32[]{:S(2)}, u32[]{:S(2)}) collective-permute-start(s16[672,128]{1,0:T(8,128)(2,1)S(1)} %get-tuple-element.81), channel_id=1, source_target_pairs={{0,2},{1,3},{2,0},{3,1},{4,6},{5,7},{6,4},{7,5},{8,10},{9,11},{10,... | collective-permute-start | bytes 516104 | tf_op jit(solution)/shard_map/ppermute | solution.py:1196
  77.3 0.8 inverse_rest.6.refs_4_
  78.2 0.1 collective-permute-start.17
  78.3 0.6 collective-permute-start.18
  78.9 1.0 %near_field.3.refs_8_ = f32[8,128]{1,0:T(8,128)S(1)} custom-call(s32[24]{0:T(128)S(1)} %get-tuple-element.84.place_ref, s32[24]{0:T(128)S(1)} %get-tuple-element.83.target_ref, s16[336,128]{1,0:T(8,128)(2,1)S(1)} %collective-permute-done.13.layers_ref.refs_0_, s16[592,128]{1,0:T(8,128)(2,1)S(1)} %collective-permute-done.14.odd_ref.refs_3_.refs_1_, ...), custom_call_target="tpu_custom_call" | custom-call | flops 12582912 | bytes 786432 | tf_op jit(solution)/shard_map/near_field/pallas_call | solution.py:1131
  79.9 0.9 inverse_rest.7.refs_0_
  80.8 2.0 %collective-permute-done.19.refs_1_ = s16[672,128]{1,0:T(8,128)(2,1)S(1)} collective-permute-done((s16[672,128]{1,0:T(8,128)(2,1)S(1)}, s16[672,128]{1,0:T(8,128)(2,1)S(1)}, u32[]{:S(2)}, u32[]{:S(2)}) %collective-permute-start.19) | collective-permute-done | bytes 172064 | tf_op jit(solution)/shard_map/ppermute | solution.py:1196
  82.8 0.4 sample_early.3.refs_2_
  83.2 1.8 %collective-permute-done.18.refs_1_ = s16[672,128]{1,0:T(8,128)(2,1)S(1)} collective-permute-done((s16[672,128]{1,0:T(8,128)(2,1)S(1)}, s16[672,128]{1,0:T(8,128)(2,1)S(1)}, u32[]{:S(2)}, u32[]{:S(2)}) %collective-permute-start.18) | collective-permute-done | bytes 172064 | tf_op jit(solution)/shard_map/ppermute | solution.py:1196
  85.1 2.7 %sample.3 = f32[2,512]{1,0:T(2,128)} custom-call(s32[2,512]{1,0:T(2,128)S(1)} %get-tuple-element.44.place_ref.place_in.refs_1_, s16[672,128]{1,0:T(8,128)(2,1)S(1)} %collective-permute-done.17.refs_0_, s16[672,128]{1,0:T(8,128)(2,1)S(1)} %collective-permute-done.18.refs_1_, f32[656,256]{1,0:T(8,128)S(1)} %sample_early.3.refs_2_, ...), custom_call_target="tpu_custom_call" | custom-call | flops 169869312 | bytes 4194304 | tf_op jit(solution)/shard_map/sample/pallas_call | solution.py:1073
  (35 shorter events, 0.2 us)
Async XLA Ops:
  5.0 8.6 %collective-permute-start.1 = (s16[672,128]{1,0:T(8,128)(2,1)S(1)}, s16[672,128]{1,0:T(8,128)(2,1)S(1)}, u32[]{:S(2)}, u32[]{:S(2)}) collective-permute-start(s16[672,128]{1,0:T(8,128)(2,1)S(1)} %get-tuple-element.50), channel_id=1, source_target_pairs={{0,2},{1,3},{2,0},{3,1},{4,6},{5,7},{6,4},{7,5},{8,10},{9,11},{10,... | collective-permute-start | bytes 516104 | tf_op jit(solution)/shard_map/ppermute | solution.py:1196
  8.6 5.8 %collective-permute-start = (s16[672,128]{1,0:T(8,128)(2,1)S(1)}, s16[672,128]{1,0:T(8,128)(2,1)S(1)}, u32[]{:S(2)}, u32[]{:S(2)}) collective-permute-start(s16[672,128]{1,0:T(8,128)(2,1)S(1)} %spread_rest.5), channel_id=1, source_target_pairs={{0,1},{1,0},{2,3},{3,2},{4,5},{5,4},{6,7},{7,6},{8,9},{9,8},{10,11... | collective-permute-start | bytes 516104 | tf_op jit(solution)/shard_map/ppermute | solution.py:1196
  8.7 6.8 %collective-permute-start.2 = (s16[672,128]{1,0:T(8,128)(2,1)S(1)}, s16[672,128]{1,0:T(8,128)(2,1)S(1)}, u32[]{:S(2)}, u32[]{:S(2)}) collective-permute-start(s16[672,128]{1,0:T(8,128)(2,1)S(1)} %get-tuple-element.51), channel_id=1, source_target_pairs={{0,3},{1,2},{2,1},{3,0},{4,7},{5,6},{6,5},{7,4},{8,11},{9,10},{10,... | collective-permute-start | bytes 516104 | tf_op jit(solution)/shard_map/ppermute | solution.py:1196
  8.8 0.9 %copy-start.6 = (f32[64,512]{1,0:T(8,128)S(1)}, f32[64,512]{1,0:T(8,128)}, u32[]{:S(2)}) copy-start(f32[64,512]{1,0:T(8,128)} %refs_3_.8) | copy-start | bytes 393220
  9.7 4.0 %copy-start.3 = (bf16[2,256,240]{2,1,0:T(8,128)(2,1)S(1)}, bf16[2,256,240]{2,1,0:T(8,128)(2,1)}, u32[]{:S(2)}) copy-start(bf16[2,256,240]{2,1,0:T(8,128)(2,1)} %constant.71.clone.refs_2_.refs_6_.table_ref) | copy-start | bytes 737284
  13.1 2.4 %copy-start = (f32[8192,128]{1,0:T(8,128)}, f32[8192,128]{1,0:T(8,128)S(1)}, u32[]{:S(2)}) copy-start(f32[8192,128]{1,0:T(8,128)S(1)} %place_sample_lines.1.refs_8_.refs_5_) | copy-start | bytes 12582916
  13.6 2.0 %copy-start.2 = (f32[4,2,256,128]{3,2,1,0:T(8,128)S(1)}, f32[4,2,256,128]{3,2,1,0:T(8,128)}, u32[]{:S(2)}) copy-start(f32[4,2,256,128]{3,2,1,0:T(8,128)} %constant.72.clone.refs_7_.modes_ref.refs_9_) | copy-start | bytes 3145732
  16.9 1.4 %copy-start.8 = (f32[18,256,128]{2,1,0:T(8,128)}, f32[18,256,128]{2,1,0:T(8,128)S(1)}, u32[]{:S(2)}) copy-start(f32[18,256,128]{2,1,0:T(8,128)S(1)} %get-tuple-element.54.refs_0_) | copy-start | bytes 7077892
  18.3 13.5 %copy-start.4 = (bf16[4,48,256]{2,1,0:T(8,128)(2,1)S(1)}, bf16[4,48,256]{2,1,0:T(8,128)(2,1)}, u32[]{:S(2)}) copy-start(bf16[4,48,256]{2,1,0:T(8,128)(2,1)} %constant.73.clone.refs_7_.high_ref) | copy-start | bytes 294916
  18.3 13.5 %copy-start.5 = (bf16[4,48,256]{2,1,0:T(8,128)(2,1)S(1)}, bf16[4,48,256]{2,1,0:T(8,128)(2,1)}, u32[]{:S(2)}) copy-start(bf16[4,48,256]{2,1,0:T(8,128)(2,1)} %constant.74.clone.refs_8_.low_ref) | copy-start | bytes 294916
  18.3 7.4 %collective-permute-start.5 = (s16[400,128]{1,0:T(8,128)(2,1)S(1)}, s16[400,128]{1,0:T(8,128)(2,1)S(1)}, u32[]{:S(2)}, u32[]{:S(2)}) collective-permute-start(s16[400,128]{1,0:T(8,128)(2,1)S(1)} %get-tuple-element.57), channel_id=1, source_target_pairs={{0,4},{8,12},{4,0},{12,8},{1,5},{9,13},{5,1},{13,9},{2,6},{10,14},... | collective-permute-start | bytes 307208 | tf_op jit(solution)/shard_map/ppermute | solution.py:1209
  20.4 7.8 %collective-permute-start.4 = (s16[592,128]{1,0:T(8,128)(2,1)S(1)}, s16[592,128]{1,0:T(8,128)(2,1)S(1)}, u32[]{:S(2)}, u32[]{:S(2)}) collective-permute-start(s16[592,128]{1,0:T(8,128)(2,1)S(1)} %get-tuple-element.56), channel_id=1, source_target_pairs={{4,8},{8,4},{5,9},{9,5},{6,10},{10,6},{7,11},{11,7},{20,24},{24,20... | collective-permute-start | bytes 454664 | tf_op jit(solution)/shard_map/ppermute | solution.py:1210
  21.2 6.9 %collective-permute-start.3 = (s16[336,128]{1,0:T(8,128)(2,1)S(1)}, s16[336,128]{1,0:T(8,128)(2,1)S(1)}, u32[]{:S(2)}, u32[]{:S(2)}) collective-permute-start(s16[336,128]{1,0:T(8,128)(2,1)S(1)} %get-tuple-element.55), channel_id=1, source_target_pairs={{0,4},{8,12},{4,0},{12,8},{1,5},{9,13},{5,1},{13,9},{2,6},{10,14},... | collective-permute-start | bytes 258056 | tf_op jit(solution)/shard_map/ppermute | solution.py:1211
  25.9 5.9 %collective-permute-start.6 = (s16[272,128]{1,0:T(8,128)(2,1)S(1)}, s16[272,128]{1,0:T(8,128)(2,1)S(1)}, u32[]{:S(2)}, u32[]{:S(2)}) collective-permute-start(s16[272,128]{1,0:T(8,128)(2,1)S(1)} %pair_messages.2), channel_id=1, source_target_pairs={{0,8},{4,12},{8,0},{12,4},{1,9},{5,13},{9,1},{13,5},{2,10},{6,14},... | collective-permute-start | bytes 208904 | tf_op jit(solution)/shard_map/ppermute | solution.py:1213
  31.7 5.2 %copy-start.13 = (s32[24]{0:T(128)S(1)}, s32[24]{0:T(128)}, u32[]{:S(2)}) copy-start(s32[24]{0:T(128)} %param.21) | copy-start | bytes 292
  31.7 5.2 %copy-start.14 = (s32[24]{0:T(128)S(1)}, s32[24]{0:T(128)}, u32[]{:S(2)}) copy-start(s32[24]{0:T(128)} %param.22) | copy-start | bytes 292
  31.8 1.7 %copy-start.9 = (f32[18,256,128]{2,1,0:T(8,128)S(1)}, f32[18,256,128]{2,1,0:T(8,128)}, u32[]{:S(2)}) copy-start(f32[18,256,128]{2,1,0:T(8,128)} %copy-done.8) | copy-start | bytes 7077892
  35.4 3.2 %copy-start.7 = (bf16[24,128,128]{2,1,0:T(8,128)(2,1)S(1)}, bf16[24,128,128]{2,1,0:T(8,128)(2,1)}, u32[]{:S(2)}) copy-start(bf16[24,128,128]{2,1,0:T(8,128)(2,1)} %refs_3_.10) | copy-start | bytes 2359300
  35.4 8.1 %collective-permute-start.9 = (s16[672,128]{1,0:T(8,128)(2,1)S(1)}, s16[672,128]{1,0:T(8,128)(2,1)S(1)}, u32[]{:S(2)}, u32[]{:S(2)}) collective-permute-start(s16[672,128]{1,0:T(8,128)(2,1)S(1)} %get-tuple-element.63), channel_id=1, source_target_pairs={{0,2},{1,3},{2,0},{3,1},{4,6},{5,7},{6,4},{7,5},{8,10},{9,11},{10,... | collective-permute-start | bytes 516104 | tf_op jit(solution)/shard_map/ppermute | solution.py:1196
  37.8 6.2 %collective-permute-start.7 = (s16[672,128]{1,0:T(8,128)(2,1)S(1)}, s16[672,128]{1,0:T(8,128)(2,1)S(1)}, u32[]{:S(2)}, u32[]{:S(2)}) collective-permute-start(s16[672,128]{1,0:T(8,128)(2,1)S(1)} %inverse_rest.4.refs_4_), channel_id=1, source_target_pairs={{0,1},{1,0},{2,3},{3,2},{4,5},{5,4},{6,7},{7,6},{8,9},{9,8},{10,11... | collective-permute-start | bytes 516104 | tf_op jit(solution)/shard_map/ppermute | solution.py:1196
  37.9 6.8 %collective-permute-start.8 = (s16[672,128]{1,0:T(8,128)(2,1)S(1)}, s16[672,128]{1,0:T(8,128)(2,1)S(1)}, u32[]{:S(2)}, u32[]{:S(2)}) collective-permute-start(s16[672,128]{1,0:T(8,128)(2,1)S(1)} %get-tuple-element.62), channel_id=1, source_target_pairs={{0,3},{1,2},{2,1},{3,0},{4,7},{5,6},{6,5},{7,4},{8,11},{9,10},{10,... | collective-permute-start | bytes 516104 | tf_op jit(solution)/shard_map/ppermute | solution.py:1196
  42.6 1.0 %copy-start.10 = (bf16[4,128,256]{2,1,0:T(8,128)(2,1)S(1)}, bf16[4,128,256]{2,1,0:T(8,128)(2,1)}, u32[]{:S(2)}) copy-start(bf16[4,128,256]{2,1,0:T(8,128)(2,1)} %constant.75.clone.refs_2_.refs_3_) | copy-start | bytes 786436
  42.6 1.0 %copy-start.11 = (bf16[4,128,256]{2,1,0:T(8,128)(2,1)S(1)}, bf16[4,128,256]{2,1,0:T(8,128)(2,1)}, u32[]{:S(2)}) copy-start(bf16[4,128,256]{2,1,0:T(8,128)(2,1)} %constant.76.clone.refs_3_.refs_4_) | copy-start | bytes 786436
  43.5 1.3 %copy-start.12 = (s32[512]{0:T(512)S(1)}, s32[512]{0:T(512)}, u32[]{:S(2)}) copy-start(s32[512]{0:T(512)} %param.17) | copy-start | bytes 6148
  43.6 2.2 %copy-start.1 = (f32[8192,128]{1,0:T(8,128)S(1)}, f32[8192,128]{1,0:T(8,128)}, u32[]{:S(2)}) copy-start(f32[8192,128]{1,0:T(8,128)} %copy-done) | copy-start | bytes 12582916
  50.6 7.3 %collective-permute-start.11 = (s16[672,128]{1,0:T(8,128)(2,1)S(1)}, s16[672,128]{1,0:T(8,128)(2,1)S(1)}, u32[]{:S(2)}, u32[]{:S(2)}) collective-permute-start(s16[672,128]{1,0:T(8,128)(2,1)S(1)} %get-tuple-element.68), channel_id=1, source_target_pairs={{0,2},{1,3},{2,0},{3,1},{4,6},{5,7},{6,4},{7,5},{8,10},{9,11},{10,... | collective-permute-start | bytes 516104 | tf_op jit(solution)/shard_map/ppermute | solution.py:1196
  52.7 5.9 %collective-permute-start.10 = (s16[672,128]{1,0:T(8,128)(2,1)S(1)}, s16[672,128]{1,0:T(8,128)(2,1)S(1)}, u32[]{:S(2)}, u32[]{:S(2)}) collective-permute-start(s16[672,128]{1,0:T(8,128)(2,1)S(1)} %spread_rest.7), channel_id=1, source_target_pairs={{0,1},{1,0},{2,3},{3,2},{4,5},{5,4},{6,7},{7,6},{8,9},{9,8},{10,11... | collective-permute-start | bytes 516104 | tf_op jit(solution)/shard_map/ppermute | solution.py:1196
  52.8 7.1 %collective-permute-start.12 = (s16[672,128]{1,0:T(8,128)(2,1)S(1)}, s16[672,128]{1,0:T(8,128)(2,1)S(1)}, u32[]{:S(2)}, u32[]{:S(2)}) collective-permute-start(s16[672,128]{1,0:T(8,128)(2,1)S(1)} %get-tuple-element.69), channel_id=1, source_target_pairs={{0,3},{1,2},{2,1},{3,0},{4,7},{5,6},{6,5},{7,4},{8,11},{9,10},{10,... | collective-permute-start | bytes 516104 | tf_op jit(solution)/shard_map/ppermute | solution.py:1196
  61.1 6.0 %collective-permute-start.15 = (s16[400,128]{1,0:T(8,128)(2,1)S(1)}, s16[400,128]{1,0:T(8,128)(2,1)S(1)}, u32[]{:S(2)}, u32[]{:S(2)}) collective-permute-start(s16[400,128]{1,0:T(8,128)(2,1)S(1)} %get-tuple-element.75), channel_id=1, source_target_pairs={{0,4},{8,12},{4,0},{12,8},{1,5},{9,13},{5,1},{13,9},{2,6},{10,14},... | collective-permute-start | bytes 307208 | tf_op jit(solution)/shard_map/ppermute | solution.py:1209
  61.2 8.8 %collective-permute-start.14 = (s16[592,128]{1,0:T(8,128)(2,1)S(1)}, s16[592,128]{1,0:T(8,128)(2,1)S(1)}, u32[]{:S(2)}, u32[]{:S(2)}) collective-permute-start(s16[592,128]{1,0:T(8,128)(2,1)S(1)} %get-tuple-element.74), channel_id=1, source_target_pairs={{4,8},{8,4},{5,9},{9,5},{6,10},{10,6},{7,11},{11,7},{20,24},{24,20... | collective-permute-start | bytes 454664 | tf_op jit(solution)/shard_map/ppermute | solution.py:1210
  62.1 7.9 %collective-permute-start.13 = (s16[336,128]{1,0:T(8,128)(2,1)S(1)}, s16[336,128]{1,0:T(8,128)(2,1)S(1)}, u32[]{:S(2)}, u32[]{:S(2)}) collective-permute-start(s16[336,128]{1,0:T(8,128)(2,1)S(1)} %get-tuple-element.73), channel_id=1, source_target_pairs={{0,4},{8,12},{4,0},{12,8},{1,5},{9,13},{5,1},{13,9},{2,6},{10,14},... | collective-permute-start | bytes 258056 | tf_op jit(solution)/shard_map/ppermute | solution.py:1211
  67.3 6.5 %collective-permute-start.16 = (s16[272,128]{1,0:T(8,128)(2,1)S(1)}, s16[272,128]{1,0:T(8,128)(2,1)S(1)}, u32[]{:S(2)}, u32[]{:S(2)}) collective-permute-start(s16[272,128]{1,0:T(8,128)(2,1)S(1)} %pair_messages.3), channel_id=1, source_target_pairs={{0,8},{4,12},{8,0},{12,4},{1,9},{5,13},{9,1},{13,5},{2,10},{6,14},... | collective-permute-start | bytes 208904 | tf_op jit(solution)/shard_map/ppermute | solution.py:1213
  75.8 7.0 %collective-permute-start.19 = (s16[672,128]{1,0:T(8,128)(2,1)S(1)}, s16[672,128]{1,0:T(8,128)(2,1)S(1)}, u32[]{:S(2)}, u32[]{:S(2)}) collective-permute-start(s16[672,128]{1,0:T(8,128)(2,1)S(1)} %get-tuple-element.81), channel_id=1, source_target_pairs={{0,2},{1,3},{2,0},{3,1},{4,6},{5,7},{6,4},{7,5},{8,10},{9,11},{10,... | collective-permute-start | bytes 516104 | tf_op jit(solution)/shard_map/ppermute | solution.py:1196
  78.2 5.1 %collective-permute-start.17 = (s16[672,128]{1,0:T(8,128)(2,1)S(1)}, s16[672,128]{1,0:T(8,128)(2,1)S(1)}, u32[]{:S(2)}, u32[]{:S(2)}) collective-permute-start(s16[672,128]{1,0:T(8,128)(2,1)S(1)} %inverse_rest.6.refs_4_), channel_id=1, source_target_pairs={{0,1},{1,0},{2,3},{3,2},{4,5},{5,4},{6,7},{7,6},{8,9},{9,8},{10,11... | collective-permute-start | bytes 516104 | tf_op jit(solution)/shard_map/ppermute | solution.py:1196
  78.3 6.8 %collective-permute-start.18 = (s16[672,128]{1,0:T(8,128)(2,1)S(1)}, s16[672,128]{1,0:T(8,128)(2,1)S(1)}, u32[]{:S(2)}, u32[]{:S(2)}) collective-permute-start(s16[672,128]{1,0:T(8,128)(2,1)S(1)} %get-tuple-element.80), channel_id=1, source_target_pairs={{0,3},{1,2},{2,1},{3,0},{4,7},{5,6},{6,5},{7,4},{8,11},{9,10},{10,... | collective-permute-start | bytes 516104 | tf_op jit(solution)/shard_map/ppermute | solution.py:1196

commit v22 on v20

--- a/solution.py
+++ b/solution.py
@@ -165,7 +165,9 @@
     root = np.sqrt(shift * (shift + 4.0))
     decay = 2.0 / (2.0 + shift + root)
     log_decay = np.log(decay)
-    modes = np.stack([decay, log_decay], axis=1).astype(np.float32)
+    ring = 1.0 / (1.0 - np.exp(GRID * log_decay))
+    gain = KERNEL_GAIN / root
+    modes = np.stack([decay, log_decay, ring, gain], axis=1).astype(np.float32)
     return (
         halves(z_forward),
         halves(z_inverse),
@@ -863,8 +865,8 @@
         low = low_lanes(chunk)
         decay = modes_ref[0, rows, :]
         log_decay = modes_ref[1, rows, :]
-        ring = 1.0 / (1.0 - jnp.exp(GRID * log_decay))
-        gain = KERNEL_GAIN * decay / ((1.0 - decay) * (1.0 + decay))
+        ring = modes_ref[2, rows, :]
+        gain = modes_ref[3, rows, :]
         across_half = jnp.exp(half * log_decay)
         across_cut = jnp.exp((half - 4) * log_decay)
         around = jnp.exp((GRID - 4) * log_decay)

time: 84.1 us -> 83.9 us (level)
  transfers between devices with their start and end apart: 20 -> 20, of which waited for: 10 -> 9; matrix products, arithmetic and copies ran while one was open for 1% -> 1% of each run, Pallas kernels for 21% -> 21%
where the time goes in v22:
time: 83.9 us; the launch traced here: 83.7 us
  Pallas kernels  36.3 us (43%)
  starting transfers between devices  24.4 us (29%)
  waiting for transfers between devices  20.2 us (24%)
  local copies, waits for them, and re-layouts  2.16 us (3%)
    ppermute x12, starting transfers between devices, turned(): lax.ppermute(part, Y_AXES, swap_pairs)  10.1 us
    ppermute x12, waiting for transfers between devices, turned(): lax.ppermute(part, Y_AXES, swap_pairs)  9.87 us
    ppermute x2, starting transfers between devices, convolve_and_sample(): even_layers = lax.ppermute(layers, 'wide', even_swap)  8.86 us
    pallas_call x2, Pallas kernels, spread(): pl.pallas_call(functools.partial(start_kernel if placed is None else spre...  7.7 us
    ppermute x2, waiting for transfers between devices, convolve_and_sample(): lax.ppermute(message, 'wide', [(i, i ^ flip) for i in range(x_count)])  7.17 us
    pallas_call x2, Pallas kernels, sample(): pl.pallas_call(functools.partial(sample_kernel, last, reach_x, reach_y, f...  4.87 us
    pallas_call x2, Pallas kernels, inverse(): pl.pallas_call(functools.partial(inverse_kernel, reach_x, reach_y, flips,...  3.81 us
    pallas_call x4, Pallas kernels, inverse_rest(): pl.pallas_call(functools.partial(inverse_rest_kernel, reach_y, flips), in...  3.41 us
  transfers between devices with their start and end apart: 20, of which 9 were waited for; matrix products, arithmetic and copies ran while one was open for 1% of the time, Pallas kernels for 21%

profile of v22, /device:TPU:0, one launch (start us, length us, event | category | flops | bytes accessed | tf_op | source)
XLA Modules:
  0.0 83.7 jit_solution(3757265180527954799)
XLA Ops:
  0.0 5.0 %start.1 = (s16[672,128]{1,0:T(8,128)(2,1)S(1)}, s16[672,128]{1,0:T(8,128)(2,1)S(1)}, bf16[656,256]{1,0:T(8,128)(2,1)S(1)}, bf16[656,256]{1,0:T(8,128)(2,1)S(1)}...) custom-call(f32[512]{0:T(512)} %refs_0_.2, ...), custom_call_target="tpu_custom_call" | custom-call | flops 169869312 | bytes 4194304 | tf_op jit(solution)/shard_map/start/pallas_call | solution.py:412
  5.0 3.0 %collective-permute-start.1 = (s16[672,128]{1,0:T(8,128)(2,1)S(1)}, s16[672,128]{1,0:T(8,128)(2,1)S(1)}, u32[]{:S(2)}, u32[]{:S(2)}) collective-permute-start(s16[672,128]{1,0:T(8,128)(2,1)S(1)} %get-tuple-element.50), channel_id=1, source_target_pairs={{0,2},{1,3},{2,0},{3,1},{4,6},{5,7},{6,4},{7,5},{8,10},{9,11},{10,... | collective-permute-start | bytes 516104 | tf_op jit(solution)/shard_map/ppermute | solution.py:1199
  8.1 0.5 spread_rest.5
  8.6 0.1 collective-permute-start
  8.7 0.1 collective-permute-start.2
  8.8 0.9 %copy-done.3 = f32[64,512]{1,0:T(8,128)S(1)} copy-done((f32[64,512]{1,0:T(8,128)S(1)}, f32[64,512]{1,0:T(8,128)}, u32[]{:S(2)}) %copy-start.3) | copy-done | bytes 131096
  9.7 3.4 %place_sample_lines.1.refs_8_.refs_5_ = f32[8192,128]{1,0:T(8,128)S(1)} custom-call(s32[2,512]{1,0:T(2,128)S(1)} %get-tuple-element.44.place_ref.place_in.refs_1_, f32[64,512]{1,0:T(8,128)S(1)} %copy-done.3, f32[64,512]{1,0:T(8,128)S(1)} %copy-done.3, f32[64,512]{1,0:T(8,128)S(1)} %copy-done.3, f32[64,512]{1,0:T(8,128)S(1)} %copy-done.3), custom_call_target="tpu_custom_call" | custom-call | flops 1048576 | bytes 4194304 | tf_op jit(solution)/shard_map/place_sample_lines/pallas_call | solution.py:483
  13.1 0.5 spread_rest.4.refs_0_
  13.6 1.1 %dynamic-slice_bitcast_fusion.refs_7_.modes_ref.refs_9_ = f32[4,256,128]{2,1,0:T(8,128)S(1)} fusion(f32[4,4,256,128]{3,2,1,0:T(8,128)} %constant.73.clone, s32[]{:T(128)S(6)} %select_n.30), kind=kLoop, calls=%fused_computation | loop fusion | bytes 1048580 | tf_op jit(solution)/shard_map/jit(dynamic_index_in_dim)/squeeze | solution.py:1176
  14.8 0.7 forward_early.2
  15.4 0.0 collective-permute-done.2.refs_3_
  15.5 1.2 %forward.2 = (f32[18,256,128]{2,1,0:T(8,128)S(1)}, s16[400,128]{1,0:T(8,128)(2,1)S(1)}, s16[336,128]{1,0:T(8,128)(2,1)S(1)}, s16[592,128]{1,0:T(8,128)(2,1)S(1)}...) custom-call(s16[672,128]{1,0:T(8,128)(2,1)S(1)} %spread_rest.4.refs_0_, ...), custom_call_target="tpu_custom_call" | custom-call | flops 301989888 | bytes 4718592 | tf_op jit(solution)/shard_map/forward/pallas_call | solution.py:697
  16.7 2.2 %collective-permute-start.5 = (s16[400,128]{1,0:T(8,128)(2,1)S(1)}, s16[400,128]{1,0:T(8,128)(2,1)S(1)}, u32[]{:S(2)}, u32[]{:S(2)}) collective-permute-start(s16[400,128]{1,0:T(8,128)(2,1)S(1)} %get-tuple-element.57), channel_id=1, source_target_pairs={{0,4},{8,12},{4,0},{12,8},{1,5},{9,13},{5,1},{13,9},{2,6},{10,14},... | collective-permute-start | bytes 307208 | tf_op jit(solution)/shard_map/ppermute | solution.py:1212
  18.9 0.8 %collective-permute-start.4 = (s16[592,128]{1,0:T(8,128)(2,1)S(1)}, s16[592,128]{1,0:T(8,128)(2,1)S(1)}, u32[]{:S(2)}, u32[]{:S(2)}) collective-permute-start(s16[592,128]{1,0:T(8,128)(2,1)S(1)} %get-tuple-element.56), channel_id=1, source_target_pairs={{4,8},{8,4},{5,9},{9,5},{6,10},{10,6},{7,11},{11,7},{20,24},{24,20... | collective-permute-start | bytes 454664 | tf_op jit(solution)/shard_map/ppermute | solution.py:1213
  19.7 4.5 %collective-permute-start.3 = (s16[336,128]{1,0:T(8,128)(2,1)S(1)}, s16[336,128]{1,0:T(8,128)(2,1)S(1)}, u32[]{:S(2)}, u32[]{:S(2)}) collective-permute-start(s16[336,128]{1,0:T(8,128)(2,1)S(1)} %get-tuple-element.55), channel_id=1, source_target_pairs={{0,4},{8,12},{4,0},{12,8},{1,5},{9,13},{5,1},{13,9},{2,6},{10,14},... | collective-permute-start | bytes 258056 | tf_op jit(solution)/shard_map/ppermute | solution.py:1214
  24.2 0.2 pair_messages.2
  24.4 0.0 copy-start.8
  24.4 0.7 collective-permute-start.6
  25.1 1.5 %collective-permute-done.3.layers_ref.refs_0_ = s16[336,128]{1,0:T(8,128)(2,1)S(1)} collective-permute-done((s16[336,128]{1,0:T(8,128)(2,1)S(1)}, s16[336,128]{1,0:T(8,128)(2,1)S(1)}, u32[]{:S(2)}, u32[]{:S(2)}) %collective-permute-start.3) | collective-permute-done | bytes 86048 | tf_op jit(solution)/shard_map/ppermute | solution.py:1214
  26.6 0.5 borders.2.refs_1_
  27.1 3.2 %collective-permute-done.6.refs_6_ = s16[272,128]{1,0:T(8,128)(2,1)S(1)} collective-permute-done((s16[272,128]{1,0:T(8,128)(2,1)S(1)}, s16[272,128]{1,0:T(8,128)(2,1)S(1)}, u32[]{:S(2)}, u32[]{:S(2)}) %collective-permute-start.6) | collective-permute-done | bytes 69664 | tf_op jit(solution)/shard_map/ppermute | solution.py:1216
  30.3 1.9 %inverse.2 = (s16[672,128]{1,0:T(8,128)(2,1)S(1)}, s16[672,128]{1,0:T(8,128)(2,1)S(1)}, bf16[18,256,128]{2,1,0:T(8,128)(2,1)S(1)}, bf16[18,256,128]{2,1,0:T(8,128)(2,1)S(1)}) custom-call(f32[18,256,128]{2,1,0:T(8,128)S(1)} %get-tuple-element.54.refs_0_, f32[4,256,128]{2,1,0:T(8,128)S(1)} %borders.2.refs_1_, ...), custom_call_target="tpu_custom_call" | custom-call | flops 301989888 | bytes 4718592 | tf_op jit(solution)/shard_map/inverse/pallas_call | solution.py:930
  32.3 1.6 %collective-permute-start.9 = (s16[672,128]{1,0:T(8,128)(2,1)S(1)}, s16[672,128]{1,0:T(8,128)(2,1)S(1)}, u32[]{:S(2)}, u32[]{:S(2)}) collective-permute-start(s16[672,128]{1,0:T(8,128)(2,1)S(1)} %get-tuple-element.63), channel_id=1, source_target_pairs={{0,2},{1,3},{2,0},{3,1},{4,6},{5,7},{6,4},{7,5},{8,10},{9,11},{10,... | collective-permute-start | bytes 516104 | tf_op jit(solution)/shard_map/ppermute | solution.py:1199
  33.8 0.8 %inverse_rest.4.refs_4_ = s16[672,128]{1,0:T(8,128)(2,1)S(1)} custom-call(bf16[18,256,128]{2,1,0:T(8,128)(2,1)S(1)} %get-tuple-element.60.field_high, bf16[18,256,128]{2,1,0:T(8,128)(2,1)S(1)} %get-tuple-element.61.field_low, bf16[4,48,256]{2,1,0:T(8,128)(2,1)S(1)} %copy-done.1, bf16[4,48,256]{2,1,0:T(8,128)(2,1)S(1)} %copy-done.2), custom_call_target="tpu_custom_call" | custom-call | flops 301989888 | bytes 4718592 | tf_op jit(solution)/shard_map/inverse_rest/pallas_call | solution.py:954
  34.7 0.1 collective-permute-start.7
  34.8 0.6 collective-permute-start.8
  35.4 1.0 %near_field.2.refs_8_.refs_0_ = f32[8,128]{1,0:T(8,128)S(1)} custom-call(s32[24]{0:T(128)S(1)} %get-tuple-element.84.place_ref, s32[24]{0:T(128)S(1)} %get-tuple-element.83.target_ref, s16[336,128]{1,0:T(8,128)(2,1)S(1)} %collective-permute-done.3.layers_ref.refs_0_, s16[592,128]{1,0:T(8,128)(2,1)S(1)} %collective-permute-done.4.odd_ref.refs_3_.refs_1_, ...), custom_call_target="tpu_custom_call" | custom-call | flops 12582912 | bytes 786432 | tf_op jit(solution)/shard_map/near_field/pallas_call | solution.py:1133
  36.5 3.0 %place_lines.1.refs_5_ = f32[8192,128]{1,0:T(8,128)S(1)} custom-call(s32[2,512]{1,0:T(2,128)S(1)} %get-tuple-element.44.place_ref.place_in.refs_1_, f32[272,128]{1,0:T(8,128)S(1)} %get-tuple-element.65.coeff_ref, f32[8,128]{1,0:T(8,128)S(1)} %near_field.2.refs_8_.refs_0_), custom_call_target="tpu_custom_call" | custom-call | flops 1048576 | bytes 4194304 | tf_op jit(solution)/shard_map/place_lines/pallas_call | solution.py:502
  39.5 0.0 copy-start.6
  39.5 0.8 %inverse_rest.5.refs_0_ = s16[672,128]{1,0:T(8,128)(2,1)S(1)} custom-call(bf16[18,256,128]{2,1,0:T(8,128)(2,1)S(1)} %get-tuple-element.60.field_high, bf16[18,256,128]{2,1,0:T(8,128)(2,1)S(1)} %get-tuple-element.61.field_low, bf16[4,48,256]{2,1,0:T(8,128)(2,1)S(1)} %copy-done.1, bf16[4,48,256]{2,1,0:T(8,128)(2,1)S(1)} %copy-done.2), custom_call_target="tpu_custom_call" | custom-call | flops 301989888 | bytes 4718592 | tf_op jit(solution)/shard_map/inverse_rest/pallas_call | solution.py:954
  40.3 0.0 copy-done.5
  40.4 0.1 copy-done.6
  40.5 0.5 sample_early.2.refs_2_
  40.9 0.6 collective-permute-done.8.refs_1_
  41.6 2.1 %sample.2.refs_2_.rounded_ref.refs_7_ = f32[4,128]{1,0:T(4,128)S(1)} custom-call(s32[2,512]{1,0:T(2,128)S(1)} %get-tuple-element.44.place_ref.place_in.refs_1_, s16[672,128]{1,0:T(8,128)(2,1)S(1)} %collective-permute-done.7.refs_0_, s16[672,128]{1,0:T(8,128)(2,1)S(1)} %collective-permute-done.8.refs_1_, f32[656,256]{1,0:T(8,128)S(1)} %sample_early.2.refs_2_, ...), custom_call_target="tpu_custom_call" | custom-call | flops 169869312 | bytes 4194304 | tf_op jit(solution)/shard_map/sample/pallas_call | solution.py:1075
  43.7 2.7 %spread.1 = (s16[672,128]{1,0:T(8,128)(2,1)S(1)}, s16[672,128]{1,0:T(8,128)(2,1)S(1)}, bf16[656,256]{1,0:T(8,128)(2,1)S(1)}, bf16[656,256]{1,0:T(8,128)(2,1)S(1)}) custom-call(f32[512]{0:T(512)S(1)} %bitcast.6, s32[2,512]{1,0:T(2,128)S(1)} %get-tuple-element.44.place_ref.place_in.refs_1_, f32[4,128]{1,0:T(4,128)S(1)} %sample.2.refs_2_.rounded_ref.refs_7_, ...), custom_call_target="tpu_custom_call" | custom-call | flops 169869312 | bytes 4194304 | tf_op jit(solution)/shard_map/spread/pallas_call | solution.py:412
  46.4 1.0 %collective-permute-start.11 = (s16[672,128]{1,0:T(8,128)(2,1)S(1)}, s16[672,128]{1,0:T(8,128)(2,1)S(1)}, u32[]{:S(2)}, u32[]{:S(2)}) collective-permute-start(s16[672,128]{1,0:T(8,128)(2,1)S(1)} %get-tuple-element.68), channel_id=1, source_target_pairs={{0,2},{1,3},{2,0},{3,1},{4,6},{5,7},{6,4},{7,5},{8,10},{9,11},{10,... | collective-permute-start | bytes 516104 | tf_op jit(solution)/shard_map/ppermute | solution.py:1199
  47.4 0.5 spread_rest.7
  48.0 0.7 collective-permute-start.10
  48.7 0.6 collective-permute-start.12
  49.2 0.5 spread_rest.6.refs_0_
  49.8 3.9 %collective-permute-done.11.refs_1_.refs_2_ = s16[672,128]{1,0:T(8,128)(2,1)S(1)} collective-permute-done((s16[672,128]{1,0:T(8,128)(2,1)S(1)}, s16[672,128]{1,0:T(8,128)(2,1)S(1)}, u32[]{:S(2)}, u32[]{:S(2)}) %collective-permute-start.11) | collective-permute-done | bytes 172064 | tf_op jit(solution)/shard_map/ppermute | solution.py:1199
  53.7 0.7 forward_early.3
  54.4 1.9 %collective-permute-done.12.refs_3_ = s16[672,128]{1,0:T(8,128)(2,1)S(1)} collective-permute-done((s16[672,128]{1,0:T(8,128)(2,1)S(1)}, s16[672,128]{1,0:T(8,128)(2,1)S(1)}, u32[]{:S(2)}, u32[]{:S(2)}) %collective-permute-start.12) | collective-permute-done | bytes 172064 | tf_op jit(solution)/shard_map/ppermute | solution.py:1199
  56.3 1.3 %forward.3 = (f32[18,256,128]{2,1,0:T(8,128)S(1)}, s16[400,128]{1,0:T(8,128)(2,1)S(1)}, s16[336,128]{1,0:T(8,128)(2,1)S(1)}, s16[592,128]{1,0:T(8,128)(2,1)S(1)}...) custom-call(s16[672,128]{1,0:T(8,128)(2,1)S(1)} %spread_rest.6.refs_0_, ...), custom_call_target="tpu_custom_call" | custom-call | flops 301989888 | bytes 4718592 | tf_op jit(solution)/shard_map/forward/pallas_call | solution.py:697
  57.6 0.1 collective-permute-start.15
  57.6 0.9 %collective-permute-start.14 = (s16[592,128]{1,0:T(8,128)(2,1)S(1)}, s16[592,128]{1,0:T(8,128)(2,1)S(1)}, u32[]{:S(2)}, u32[]{:S(2)}) collective-permute-start(s16[592,128]{1,0:T(8,128)(2,1)S(1)} %get-tuple-element.74), channel_id=1, source_target_pairs={{4,8},{8,4},{5,9},{9,5},{6,10},{10,6},{7,11},{11,7},{20,24},{24,20... | collective-permute-start | bytes 454664 | tf_op jit(solution)/shard_map/ppermute | solution.py:1213
  58.5 4.4 %collective-permute-start.13 = (s16[336,128]{1,0:T(8,128)(2,1)S(1)}, s16[336,128]{1,0:T(8,128)(2,1)S(1)}, u32[]{:S(2)}, u32[]{:S(2)}) collective-permute-start(s16[336,128]{1,0:T(8,128)(2,1)S(1)} %get-tuple-element.73), channel_id=1, source_target_pairs={{0,4},{8,12},{4,0},{12,8},{1,5},{9,13},{5,1},{13,9},{2,6},{10,14},... | collective-permute-start | bytes 258056 | tf_op jit(solution)/shard_map/ppermute | solution.py:1214
  62.9 0.2 pair_messages.3
  63.1 0.8 collective-permute-start.16
  63.9 1.6 %collective-permute-done.13.layers_ref.refs_0_ = s16[336,128]{1,0:T(8,128)(2,1)S(1)} collective-permute-done((s16[336,128]{1,0:T(8,128)(2,1)S(1)}, s16[336,128]{1,0:T(8,128)(2,1)S(1)}, u32[]{:S(2)}, u32[]{:S(2)}) %collective-permute-start.13) | collective-permute-done | bytes 86048 | tf_op jit(solution)/shard_map/ppermute | solution.py:1214
  65.5 0.5 borders.3.refs_1_
  66.0 3.9 %collective-permute-done.16.refs_6_ = s16[272,128]{1,0:T(8,128)(2,1)S(1)} collective-permute-done((s16[272,128]{1,0:T(8,128)(2,1)S(1)}, s16[272,128]{1,0:T(8,128)(2,1)S(1)}, u32[]{:S(2)}, u32[]{:S(2)}) %collective-permute-start.16) | collective-permute-done | bytes 69664 | tf_op jit(solution)/shard_map/ppermute | solution.py:1216
  69.9 1.9 %inverse.3 = (s16[672,128]{1,0:T(8,128)(2,1)S(1)}, s16[672,128]{1,0:T(8,128)(2,1)S(1)}, bf16[18,256,128]{2,1,0:T(8,128)(2,1)S(1)}, bf16[18,256,128]{2,1,0:T(8,128)(2,1)S(1)}) custom-call(f32[18,256,128]{2,1,0:T(8,128)S(1)} %get-tuple-element.72.refs_0_, f32[4,256,128]{2,1,0:T(8,128)S(1)} %borders.3.refs_1_, ...), custom_call_target="tpu_custom_call" | custom-call | flops 301989888 | bytes 4718592 | tf_op jit(solution)/shard_map/inverse/pallas_call | solution.py:930
  71.8 1.8 %collective-permute-start.19 = (s16[672,128]{1,0:T(8,128)(2,1)S(1)}, s16[672,128]{1,0:T(8,128)(2,1)S(1)}, u32[]{:S(2)}, u32[]{:S(2)}) collective-permute-start(s16[672,128]{1,0:T(8,128)(2,1)S(1)} %get-tuple-element.81), channel_id=1, source_target_pairs={{0,2},{1,3},{2,0},{3,1},{4,6},{5,7},{6,4},{7,5},{8,10},{9,11},{10,... | collective-permute-start | bytes 516104 | tf_op jit(solution)/shard_map/ppermute | solution.py:1199
  73.7 0.8 %inverse_rest.6.refs_4_ = s16[672,128]{1,0:T(8,128)(2,1)S(1)} custom-call(bf16[18,256,128]{2,1,0:T(8,128)(2,1)S(1)} %get-tuple-element.78.field_high, bf16[18,256,128]{2,1,0:T(8,128)(2,1)S(1)} %get-tuple-element.79.field_low, bf16[4,48,256]{2,1,0:T(8,128)(2,1)S(1)} %copy-done.1, bf16[4,48,256]{2,1,0:T(8,128)(2,1)S(1)} %copy-done.2), custom_call_target="tpu_custom_call" | custom-call | flops 301989888 | bytes 4718592 | tf_op jit(solution)/shard_map/inverse_rest/pallas_call | solution.py:954
  74.5 0.1 collective-permute-start.17
  74.6 0.4 collective-permute-start.18
  75.0 1.0 %near_field.3.refs_8_ = f32[8,128]{1,0:T(8,128)S(1)} custom-call(s32[24]{0:T(128)S(1)} %get-tuple-element.84.place_ref, s32[24]{0:T(128)S(1)} %get-tuple-element.83.target_ref, s16[336,128]{1,0:T(8,128)(2,1)S(1)} %collective-permute-done.13.layers_ref.refs_0_, s16[592,128]{1,0:T(8,128)(2,1)S(1)} %collective-permute-done.14.odd_ref.refs_3_.refs_1_, ...), custom_call_target="tpu_custom_call" | custom-call | flops 12582912 | bytes 786432 | tf_op jit(solution)/shard_map/near_field/pallas_call | solution.py:1133
  76.0 0.9 %inverse_rest.7.refs_0_ = s16[672,128]{1,0:T(8,128)(2,1)S(1)} custom-call(bf16[18,256,128]{2,1,0:T(8,128)(2,1)S(1)} %get-tuple-element.78.field_high, bf16[18,256,128]{2,1,0:T(8,128)(2,1)S(1)} %get-tuple-element.79.field_low, bf16[4,48,256]{2,1,0:T(8,128)(2,1)S(1)} %copy-done.1, bf16[4,48,256]{2,1,0:T(8,128)(2,1)S(1)} %copy-done.2), custom_call_target="tpu_custom_call" | custom-call | flops 301989888 | bytes 4718592 | tf_op jit(solution)/shard_map/inverse_rest/pallas_call | solution.py:954
  76.9 0.8 collective-permute-done.19.refs_1_
  77.7 0.4 sample_early.3.refs_2_
  78.2 2.6 %collective-permute-done.18.refs_1_ = s16[672,128]{1,0:T(8,128)(2,1)S(1)} collective-permute-done((s16[672,128]{1,0:T(8,128)(2,1)S(1)}, s16[672,128]{1,0:T(8,128)(2,1)S(1)}, u32[]{:S(2)}, u32[]{:S(2)}) %collective-permute-start.18) | collective-permute-done | bytes 172064 | tf_op jit(solution)/shard_map/ppermute | solution.py:1199
  80.8 2.7 %sample.3 = f32[2,512]{1,0:T(2,128)} custom-call(s32[2,512]{1,0:T(2,128)S(1)} %get-tuple-element.44.place_ref.place_in.refs_1_, s16[672,128]{1,0:T(8,128)(2,1)S(1)} %collective-permute-done.17.refs_0_, s16[672,128]{1,0:T(8,128)(2,1)S(1)} %collective-permute-done.18.refs_1_, f32[656,256]{1,0:T(8,128)S(1)} %sample_early.3.refs_2_, ...), custom_call_target="tpu_custom_call" | custom-call | flops 169869312 | bytes 4194304 | tf_op jit(solution)/shard_map/sample/pallas_call | solution.py:1075
  (26 shorter events, 0.1 us)
Async XLA Ops:
  5.0 9.7 %collective-permute-start.1 = (s16[672,128]{1,0:T(8,128)(2,1)S(1)}, s16[672,128]{1,0:T(8,128)(2,1)S(1)}, u32[]{:S(2)}, u32[]{:S(2)}) collective-permute-start(s16[672,128]{1,0:T(8,128)(2,1)S(1)} %get-tuple-element.50), channel_id=1, source_target_pairs={{0,2},{1,3},{2,0},{3,1},{4,6},{5,7},{6,4},{7,5},{8,10},{9,11},{10,... | collective-permute-start | bytes 516104 | tf_op jit(solution)/shard_map/ppermute | solution.py:1199
  8.6 6.8 %collective-permute-start = (s16[672,128]{1,0:T(8,128)(2,1)S(1)}, s16[672,128]{1,0:T(8,128)(2,1)S(1)}, u32[]{:S(2)}, u32[]{:S(2)}) collective-permute-start(s16[672,128]{1,0:T(8,128)(2,1)S(1)} %spread_rest.5), channel_id=1, source_target_pairs={{0,1},{1,0},{2,3},{3,2},{4,5},{5,4},{6,7},{7,6},{8,9},{9,8},{10,11... | collective-permute-start | bytes 516104 | tf_op jit(solution)/shard_map/ppermute | solution.py:1199
  8.7 6.8 %collective-permute-start.2 = (s16[672,128]{1,0:T(8,128)(2,1)S(1)}, s16[672,128]{1,0:T(8,128)(2,1)S(1)}, u32[]{:S(2)}, u32[]{:S(2)}) collective-permute-start(s16[672,128]{1,0:T(8,128)(2,1)S(1)} %get-tuple-element.51), channel_id=1, source_target_pairs={{0,3},{1,2},{2,1},{3,0},{4,7},{5,6},{6,5},{7,4},{8,11},{9,10},{10,... | collective-permute-start | bytes 516104 | tf_op jit(solution)/shard_map/ppermute | solution.py:1199
  8.8 0.9 %copy-start.3 = (f32[64,512]{1,0:T(8,128)S(1)}, f32[64,512]{1,0:T(8,128)}, u32[]{:S(2)}) copy-start(f32[64,512]{1,0:T(8,128)} %refs_3_.8) | copy-start | bytes 393220
  13.1 1.6 %copy-start = (bf16[2,256,240]{2,1,0:T(8,128)(2,1)S(1)}, bf16[2,256,240]{2,1,0:T(8,128)(2,1)}, u32[]{:S(2)}) copy-start(bf16[2,256,240]{2,1,0:T(8,128)(2,1)} %constant.76.clone.refs_2_.refs_6_.table_ref) | copy-start | bytes 737284
  15.5 14.9 %copy-start.1 = (bf16[4,48,256]{2,1,0:T(8,128)(2,1)S(1)}, bf16[4,48,256]{2,1,0:T(8,128)(2,1)}, u32[]{:S(2)}) copy-start(bf16[4,48,256]{2,1,0:T(8,128)(2,1)} %constant.77.clone.refs_7_.high_ref) | copy-start | bytes 294916
  15.5 14.9 %copy-start.2 = (bf16[4,48,256]{2,1,0:T(8,128)(2,1)S(1)}, bf16[4,48,256]{2,1,0:T(8,128)(2,1)}, u32[]{:S(2)}) copy-start(bf16[4,48,256]{2,1,0:T(8,128)(2,1)} %constant.78.clone.refs_8_.low_ref) | copy-start | bytes 294916
  16.7 7.5 %collective-permute-start.5 = (s16[400,128]{1,0:T(8,128)(2,1)S(1)}, s16[400,128]{1,0:T(8,128)(2,1)S(1)}, u32[]{:S(2)}, u32[]{:S(2)}) collective-permute-start(s16[400,128]{1,0:T(8,128)(2,1)S(1)} %get-tuple-element.57), channel_id=1, source_target_pairs={{0,4},{8,12},{4,0},{12,8},{1,5},{9,13},{5,1},{13,9},{2,6},{10,14},... | collective-permute-start | bytes 307208 | tf_op jit(solution)/shard_map/ppermute | solution.py:1212
  18.9 7.8 %collective-permute-start.4 = (s16[592,128]{1,0:T(8,128)(2,1)S(1)}, s16[592,128]{1,0:T(8,128)(2,1)S(1)}, u32[]{:S(2)}, u32[]{:S(2)}) collective-permute-start(s16[592,128]{1,0:T(8,128)(2,1)S(1)} %get-tuple-element.56), channel_id=1, source_target_pairs={{4,8},{8,4},{5,9},{9,5},{6,10},{10,6},{7,11},{11,7},{20,24},{24,20... | collective-permute-start | bytes 454664 | tf_op jit(solution)/shard_map/ppermute | solution.py:1213
  19.7 6.9 %collective-permute-start.3 = (s16[336,128]{1,0:T(8,128)(2,1)S(1)}, s16[336,128]{1,0:T(8,128)(2,1)S(1)}, u32[]{:S(2)}, u32[]{:S(2)}) collective-permute-start(s16[336,128]{1,0:T(8,128)(2,1)S(1)} %get-tuple-element.55), channel_id=1, source_target_pairs={{0,4},{8,12},{4,0},{12,8},{1,5},{9,13},{5,1},{13,9},{2,6},{10,14},... | collective-permute-start | bytes 258056 | tf_op jit(solution)/shard_map/ppermute | solution.py:1214
  24.4 9.5 %copy-start.8 = (s32[24]{0:T(128)S(1)}, s32[24]{0:T(128)}, u32[]{:S(2)}) copy-start(s32[24]{0:T(128)} %param.21) | copy-start | bytes 292
  24.4 9.5 %copy-start.9 = (s32[24]{0:T(128)S(1)}, s32[24]{0:T(128)}, u32[]{:S(2)}) copy-start(s32[24]{0:T(128)} %param.22) | copy-start | bytes 292
  24.4 6.0 %collective-permute-start.6 = (s16[272,128]{1,0:T(8,128)(2,1)S(1)}, s16[272,128]{1,0:T(8,128)(2,1)S(1)}, u32[]{:S(2)}, u32[]{:S(2)}) collective-permute-start(s16[272,128]{1,0:T(8,128)(2,1)S(1)} %pair_messages.2), channel_id=1, source_target_pairs={{0,8},{4,12},{8,0},{12,4},{1,9},{5,13},{9,1},{13,5},{2,10},{6,14},... | collective-permute-start | bytes 208904 | tf_op jit(solution)/shard_map/ppermute | solution.py:1216
  32.2 3.2 %copy-start.4 = (bf16[24,128,128]{2,1,0:T(8,128)(2,1)S(1)}, bf16[24,128,128]{2,1,0:T(8,128)(2,1)}, u32[]{:S(2)}) copy-start(bf16[24,128,128]{2,1,0:T(8,128)(2,1)} %refs_3_.10) | copy-start | bytes 2359300
  32.3 8.1 %collective-permute-start.9 = (s16[672,128]{1,0:T(8,128)(2,1)S(1)}, s16[672,128]{1,0:T(8,128)(2,1)S(1)}, u32[]{:S(2)}, u32[]{:S(2)}) collective-permute-start(s16[672,128]{1,0:T(8,128)(2,1)S(1)} %get-tuple-element.63), channel_id=1, source_target_pairs={{0,2},{1,3},{2,0},{3,1},{4,6},{5,7},{6,4},{7,5},{8,10},{9,11},{10,... | collective-permute-start | bytes 516104 | tf_op jit(solution)/shard_map/ppermute | solution.py:1199
  34.7 6.2 %collective-permute-start.7 = (s16[672,128]{1,0:T(8,128)(2,1)S(1)}, s16[672,128]{1,0:T(8,128)(2,1)S(1)}, u32[]{:S(2)}, u32[]{:S(2)}) collective-permute-start(s16[672,128]{1,0:T(8,128)(2,1)S(1)} %inverse_rest.4.refs_4_), channel_id=1, source_target_pairs={{0,1},{1,0},{2,3},{3,2},{4,5},{5,4},{6,7},{7,6},{8,9},{9,8},{10,11... | collective-permute-start | bytes 516104 | tf_op jit(solution)/shard_map/ppermute | solution.py:1199
  34.8 6.8 %collective-permute-start.8 = (s16[672,128]{1,0:T(8,128)(2,1)S(1)}, s16[672,128]{1,0:T(8,128)(2,1)S(1)}, u32[]{:S(2)}, u32[]{:S(2)}) collective-permute-start(s16[672,128]{1,0:T(8,128)(2,1)S(1)} %get-tuple-element.62), channel_id=1, source_target_pairs={{0,3},{1,2},{2,1},{3,0},{4,7},{5,6},{6,5},{7,4},{8,11},{9,10},{10,... | collective-permute-start | bytes 516104 | tf_op jit(solution)/shard_map/ppermute | solution.py:1199
  39.4 1.0 %copy-start.5 = (bf16[4,128,256]{2,1,0:T(8,128)(2,1)S(1)}, bf16[4,128,256]{2,1,0:T(8,128)(2,1)}, u32[]{:S(2)}) copy-start(bf16[4,128,256]{2,1,0:T(8,128)(2,1)} %constant.79.clone.refs_2_.refs_3_) | copy-start | bytes 786436
  39.5 1.0 %copy-start.6 = (bf16[4,128,256]{2,1,0:T(8,128)(2,1)S(1)}, bf16[4,128,256]{2,1,0:T(8,128)(2,1)}, u32[]{:S(2)}) copy-start(bf16[4,128,256]{2,1,0:T(8,128)(2,1)} %constant.80.clone.refs_3_.refs_4_) | copy-start | bytes 786436
  40.3 1.3 %copy-start.7 = (s32[512]{0:T(512)S(1)}, s32[512]{0:T(512)}, u32[]{:S(2)}) copy-start(s32[512]{0:T(512)} %param.17) | copy-start | bytes 6148
  46.4 7.3 %collective-permute-start.11 = (s16[672,128]{1,0:T(8,128)(2,1)S(1)}, s16[672,128]{1,0:T(8,128)(2,1)S(1)}, u32[]{:S(2)}, u32[]{:S(2)}) collective-permute-start(s16[672,128]{1,0:T(8,128)(2,1)S(1)} %get-tuple-element.68), channel_id=1, source_target_pairs={{0,2},{1,3},{2,0},{3,1},{4,6},{5,7},{6,4},{7,5},{8,10},{9,11},{10,... | collective-permute-start | bytes 516104 | tf_op jit(solution)/shard_map/ppermute | solution.py:1199
  48.0 6.4 %collective-permute-start.10 = (s16[672,128]{1,0:T(8,128)(2,1)S(1)}, s16[672,128]{1,0:T(8,128)(2,1)S(1)}, u32[]{:S(2)}, u32[]{:S(2)}) collective-permute-start(s16[672,128]{1,0:T(8,128)(2,1)S(1)} %spread_rest.7), channel_id=1, source_target_pairs={{0,1},{1,0},{2,3},{3,2},{4,5},{5,4},{6,7},{7,6},{8,9},{9,8},{10,11... | collective-permute-start | bytes 516104 | tf_op jit(solution)/shard_map/ppermute | solution.py:1199
  48.7 7.6 %collective-permute-start.12 = (s16[672,128]{1,0:T(8,128)(2,1)S(1)}, s16[672,128]{1,0:T(8,128)(2,1)S(1)}, u32[]{:S(2)}, u32[]{:S(2)}) collective-permute-start(s16[672,128]{1,0:T(8,128)(2,1)S(1)} %get-tuple-element.69), channel_id=1, source_target_pairs={{0,3},{1,2},{2,1},{3,0},{4,7},{5,6},{6,5},{7,4},{8,11},{9,10},{10,... | collective-permute-start | bytes 516104 | tf_op jit(solution)/shard_map/ppermute | solution.py:1199
  57.6 5.4 %collective-permute-start.15 = (s16[400,128]{1,0:T(8,128)(2,1)S(1)}, s16[400,128]{1,0:T(8,128)(2,1)S(1)}, u32[]{:S(2)}, u32[]{:S(2)}) collective-permute-start(s16[400,128]{1,0:T(8,128)(2,1)S(1)} %get-tuple-element.75), channel_id=1, source_target_pairs={{0,4},{8,12},{4,0},{12,8},{1,5},{9,13},{5,1},{13,9},{2,6},{10,14},... | collective-permute-start | bytes 307208 | tf_op jit(solution)/shard_map/ppermute | solution.py:1212
  57.6 7.9 %collective-permute-start.14 = (s16[592,128]{1,0:T(8,128)(2,1)S(1)}, s16[592,128]{1,0:T(8,128)(2,1)S(1)}, u32[]{:S(2)}, u32[]{:S(2)}) collective-permute-start(s16[592,128]{1,0:T(8,128)(2,1)S(1)} %get-tuple-element.74), channel_id=1, source_target_pairs={{4,8},{8,4},{5,9},{9,5},{6,10},{10,6},{7,11},{11,7},{20,24},{24,20... | collective-permute-start | bytes 454664 | tf_op jit(solution)/shard_map/ppermute | solution.py:1213
  58.5 7.0 %collective-permute-start.13 = (s16[336,128]{1,0:T(8,128)(2,1)S(1)}, s16[336,128]{1,0:T(8,128)(2,1)S(1)}, u32[]{:S(2)}, u32[]{:S(2)}) collective-permute-start(s16[336,128]{1,0:T(8,128)(2,1)S(1)} %get-tuple-element.73), channel_id=1, source_target_pairs={{0,4},{8,12},{4,0},{12,8},{1,5},{9,13},{5,1},{13,9},{2,6},{10,14},... | collective-permute-start | bytes 258056 | tf_op jit(solution)/shard_map/ppermute | solution.py:1214
  63.1 6.8 %collective-permute-start.16 = (s16[272,128]{1,0:T(8,128)(2,1)S(1)}, s16[272,128]{1,0:T(8,128)(2,1)S(1)}, u32[]{:S(2)}, u32[]{:S(2)}) collective-permute-start(s16[272,128]{1,0:T(8,128)(2,1)S(1)} %pair_messages.3), channel_id=1, source_target_pairs={{0,8},{4,12},{8,0},{12,4},{1,9},{5,13},{9,1},{13,5},{2,10},{6,14},... | collective-permute-start | bytes 208904 | tf_op jit(solution)/shard_map/ppermute | solution.py:1216
  71.8 5.9 %collective-permute-start.19 = (s16[672,128]{1,0:T(8,128)(2,1)S(1)}, s16[672,128]{1,0:T(8,128)(2,1)S(1)}, u32[]{:S(2)}, u32[]{:S(2)}) collective-permute-start(s16[672,128]{1,0:T(8,128)(2,1)S(1)} %get-tuple-element.81), channel_id=1, source_target_pairs={{0,2},{1,3},{2,0},{3,1},{4,6},{5,7},{6,4},{7,5},{8,10},{9,11},{10,... | collective-permute-start | bytes 516104 | tf_op jit(solution)/shard_map/ppermute | solution.py:1199
  74.5 3.7 %collective-permute-start.17 = (s16[672,128]{1,0:T(8,128)(2,1)S(1)}, s16[672,128]{1,0:T(8,128)(2,1)S(1)}, u32[]{:S(2)}, u32[]{:S(2)}) collective-permute-start(s16[672,128]{1,0:T(8,128)(2,1)S(1)} %inverse_rest.6.refs_4_), channel_id=1, source_target_pairs={{0,1},{1,0},{2,3},{3,2},{4,5},{5,4},{6,7},{7,6},{8,9},{9,8},{10,11... | collective-permute-start | bytes 516104 | tf_op jit(solution)/shard_map/ppermute | solution.py:1199
  74.6 6.2 %collective-permute-start.18 = (s16[672,128]{1,0:T(8,128)(2,1)S(1)}, s16[672,128]{1,0:T(8,128)(2,1)S(1)}, u32[]{:S(2)}, u32[]{:S(2)}) collective-permute-start(s16[672,128]{1,0:T(8,128)(2,1)S(1)} %get-tuple-element.80), channel_id=1, source_target_pairs={{0,3},{1,2},{2,1},{3,0},{4,7},{5,6},{6,5},{7,4},{8,11},{9,10},{10,... | collective-permute-start | bytes 516104 | tf_op jit(solution)/shard_map/ppermute | solution.py:1199

commit v23 on v22

--- a/solution.py
+++ b/solution.py
@@ -25,7 +25,7 @@
 START_LIMIT = VMEM_LIMIT
 EARLY_FLOPS = 5 * 10**9
 GROUP = 32
-CHAINS = 2
+CHAINS = 1
 
 
 def cas(angles):

time: 83.9 us -> 85.7 us (1.021)
  Pallas kernels: 36.3 us -> 38.2 us
    pallas_call x2, Pallas kernels: 7.7 us -> 9.52 us  [spread(): pl.pallas_call(functools.partial(start_kernel if placed is None else spre...]
  transfers between devices with their start and end apart: 20 -> 20, of which waited for: 9 -> 9; matrix products, arithmetic and copies ran while one was open for 1% -> 1% of each run, Pallas kernels for 21% -> 20%
where the time goes in v23:
time: 85.7 us; the launch traced here: 85.5 us
  Pallas kernels  38.2 us (45%)
  starting transfers between devices  24.4 us (28%)
  waiting for transfers between devices  20.2 us (24%)
  local copies, waits for them, and re-layouts  2.17 us (3%)
    ppermute x12, starting transfers between devices, turned(): lax.ppermute(part, Y_AXES, swap_pairs)  10.1 us
    ppermute x12, waiting for transfers between devices, turned(): lax.ppermute(part, Y_AXES, swap_pairs)  9.86 us
    pallas_call x2, Pallas kernels, spread(): pl.pallas_call(functools.partial(start_kernel if placed is None else spre...  9.52 us
    ppermute x2, starting transfers between devices, convolve_and_sample(): even_layers = lax.ppermute(layers, 'wide', even_swap)  8.81 us
    ppermute x2, waiting for transfers between devices, convolve_and_sample(): lax.ppermute(message, 'wide', [(i, i ^ flip) for i in range(x_count)])  7.19 us
    pallas_call x2, Pallas kernels, sample(): pl.pallas_call(functools.partial(sample_kernel, last, reach_x, reach_y, f...  4.87 us
    pallas_call x2, Pallas kernels, inverse(): pl.pallas_call(functools.partial(inverse_kernel, reach_x, reach_y, flips,...  3.81 us
    pallas_call x4, Pallas kernels, inverse_rest(): pl.pallas_call(functools.partial(inverse_rest_kernel, reach_y, flips), in...  3.41 us
  transfers between devices with their start and end apart: 20, of which 9 were waited for; matrix products, arithmetic and copies ran while one was open for 1% of the time, Pallas kernels for 20%

profile of v23, /device:TPU:0, one launch (start us, length us, event | category | flops | bytes accessed | tf_op | source)
XLA Modules:
  0.0 85.5 jit_solution(12235267734842364176)
XLA Ops:
  0.0 5.7 %start.1 = (s16[672,128]{1,0:T(8,128)(2,1)S(1)}, s16[672,128]{1,0:T(8,128)(2,1)S(1)}, bf16[656,256]{1,0:T(8,128)(2,1)S(1)}, bf16[656,256]{1,0:T(8,128)(2,1)S(1)}...) custom-call(f32[512]{0:T(512)} %refs_0_.2, ...), custom_call_target="tpu_custom_call" | custom-call | flops 169869312 | bytes 4194304 | tf_op jit(solution)/shard_map/start/pallas_call | solution.py:412
  5.7 3.0 %collective-permute-start.1 = (s16[672,128]{1,0:T(8,128)(2,1)S(1)}, s16[672,128]{1,0:T(8,128)(2,1)S(1)}, u32[]{:S(2)}, u32[]{:S(2)}) collective-permute-start(s16[672,128]{1,0:T(8,128)(2,1)S(1)} %get-tuple-element.50), channel_id=1, source_target_pairs={{0,2},{1,3},{2,0},{3,1},{4,6},{5,7},{6,4},{7,5},{8,10},{9,11},{10,... | collective-permute-start | bytes 516104 | tf_op jit(solution)/shard_map/ppermute | solution.py:1199
  8.7 0.5 spread_rest.5
  9.2 0.1 collective-permute-start
  9.3 0.1 collective-permute-start.2
  9.4 0.9 %copy-done.3 = f32[64,512]{1,0:T(8,128)S(1)} copy-done((f32[64,512]{1,0:T(8,128)S(1)}, f32[64,512]{1,0:T(8,128)}, u32[]{:S(2)}) %copy-start.3) | copy-done | bytes 131096
  10.4 3.4 %place_sample_lines.1.refs_8_.refs_5_ = f32[8192,128]{1,0:T(8,128)S(1)} custom-call(s32[2,512]{1,0:T(2,128)S(1)} %get-tuple-element.44.place_ref.place_in.refs_1_, f32[64,512]{1,0:T(8,128)S(1)} %copy-done.3, f32[64,512]{1,0:T(8,128)S(1)} %copy-done.3, f32[64,512]{1,0:T(8,128)S(1)} %copy-done.3, f32[64,512]{1,0:T(8,128)S(1)} %copy-done.3), custom_call_target="tpu_custom_call" | custom-call | flops 1048576 | bytes 4194304 | tf_op jit(solution)/shard_map/place_sample_lines/pallas_call | solution.py:483
  13.8 0.5 spread_rest.4.refs_0_
  14.3 1.1 %dynamic-slice_bitcast_fusion.refs_7_.modes_ref.refs_9_ = f32[4,256,128]{2,1,0:T(8,128)S(1)} fusion(f32[4,4,256,128]{3,2,1,0:T(8,128)} %constant.73.clone, s32[]{:T(128)S(6)} %select_n.30), kind=kLoop, calls=%fused_computation | loop fusion | bytes 1048580 | tf_op jit(solution)/shard_map/jit(dynamic_index_in_dim)/squeeze | solution.py:1176
  15.4 0.7 forward_early.2
  16.1 0.0 collective-permute-done.2.refs_3_
  16.1 0.0 copy-start.1
  16.1 1.2 %forward.2 = (f32[18,256,128]{2,1,0:T(8,128)S(1)}, s16[400,128]{1,0:T(8,128)(2,1)S(1)}, s16[336,128]{1,0:T(8,128)(2,1)S(1)}, s16[592,128]{1,0:T(8,128)(2,1)S(1)}...) custom-call(s16[672,128]{1,0:T(8,128)(2,1)S(1)} %spread_rest.4.refs_0_, ...), custom_call_target="tpu_custom_call" | custom-call | flops 301989888 | bytes 4718592 | tf_op jit(solution)/shard_map/forward/pallas_call | solution.py:697
  17.4 2.2 %collective-permute-start.5 = (s16[400,128]{1,0:T(8,128)(2,1)S(1)}, s16[400,128]{1,0:T(8,128)(2,1)S(1)}, u32[]{:S(2)}, u32[]{:S(2)}) collective-permute-start(s16[400,128]{1,0:T(8,128)(2,1)S(1)} %get-tuple-element.57), channel_id=1, source_target_pairs={{0,4},{8,12},{4,0},{12,8},{1,5},{9,13},{5,1},{13,9},{2,6},{10,14},... | collective-permute-start | bytes 307208 | tf_op jit(solution)/shard_map/ppermute | solution.py:1212
  19.5 0.8 collective-permute-start.4
  20.4 4.4 %collective-permute-start.3 = (s16[336,128]{1,0:T(8,128)(2,1)S(1)}, s16[336,128]{1,0:T(8,128)(2,1)S(1)}, u32[]{:S(2)}, u32[]{:S(2)}) collective-permute-start(s16[336,128]{1,0:T(8,128)(2,1)S(1)} %get-tuple-element.55), channel_id=1, source_target_pairs={{0,4},{8,12},{4,0},{12,8},{1,5},{9,13},{5,1},{13,9},{2,6},{10,14},... | collective-permute-start | bytes 258056 | tf_op jit(solution)/shard_map/ppermute | solution.py:1214
  24.8 0.2 pair_messages.2
  25.0 0.7 collective-permute-start.6
  25.8 1.5 %collective-permute-done.3.layers_ref.refs_0_ = s16[336,128]{1,0:T(8,128)(2,1)S(1)} collective-permute-done((s16[336,128]{1,0:T(8,128)(2,1)S(1)}, s16[336,128]{1,0:T(8,128)(2,1)S(1)}, u32[]{:S(2)}, u32[]{:S(2)}) %collective-permute-start.3) | collective-permute-done | bytes 86048 | tf_op jit(solution)/shard_map/ppermute | solution.py:1214
  27.3 0.4 borders.2.refs_1_
  27.7 3.2 %collective-permute-done.6.refs_6_ = s16[272,128]{1,0:T(8,128)(2,1)S(1)} collective-permute-done((s16[272,128]{1,0:T(8,128)(2,1)S(1)}, s16[272,128]{1,0:T(8,128)(2,1)S(1)}, u32[]{:S(2)}, u32[]{:S(2)}) %collective-permute-start.6) | collective-permute-done | bytes 69664 | tf_op jit(solution)/shard_map/ppermute | solution.py:1216
  31.0 1.9 %inverse.2 = (s16[672,128]{1,0:T(8,128)(2,1)S(1)}, s16[672,128]{1,0:T(8,128)(2,1)S(1)}, bf16[18,256,128]{2,1,0:T(8,128)(2,1)S(1)}, bf16[18,256,128]{2,1,0:T(8,128)(2,1)S(1)}) custom-call(f32[18,256,128]{2,1,0:T(8,128)S(1)} %get-tuple-element.54.refs_0_, f32[4,256,128]{2,1,0:T(8,128)S(1)} %borders.2.refs_1_, ...), custom_call_target="tpu_custom_call" | custom-call | flops 301989888 | bytes 4718592 | tf_op jit(solution)/shard_map/inverse/pallas_call | solution.py:930
  32.9 1.6 %collective-permute-start.9 = (s16[672,128]{1,0:T(8,128)(2,1)S(1)}, s16[672,128]{1,0:T(8,128)(2,1)S(1)}, u32[]{:S(2)}, u32[]{:S(2)}) collective-permute-start(s16[672,128]{1,0:T(8,128)(2,1)S(1)} %get-tuple-element.63), channel_id=1, source_target_pairs={{0,2},{1,3},{2,0},{3,1},{4,6},{5,7},{6,4},{7,5},{8,10},{9,11},{10,... | collective-permute-start | bytes 516104 | tf_op jit(solution)/shard_map/ppermute | solution.py:1199
  34.5 0.8 inverse_rest.4.refs_4_
  35.4 0.1 collective-permute-start.7
  35.4 0.6 collective-permute-start.8
  36.1 1.1 %near_field.2.refs_8_.refs_0_ = f32[8,128]{1,0:T(8,128)S(1)} custom-call(s32[24]{0:T(128)S(1)} %get-tuple-element.84.place_ref, s32[24]{0:T(128)S(1)} %get-tuple-element.83.target_ref, s16[336,128]{1,0:T(8,128)(2,1)S(1)} %collective-permute-done.3.layers_ref.refs_0_, s16[592,128]{1,0:T(8,128)(2,1)S(1)} %collective-permute-done.4.odd_ref.refs_3_.refs_1_, ...), custom_call_target="tpu_custom_call" | custom-call | flops 12582912 | bytes 786432 | tf_op jit(solution)/shard_map/near_field/pallas_call | solution.py:1133
  37.1 3.0 %place_lines.1.refs_5_ = f32[8192,128]{1,0:T(8,128)S(1)} custom-call(s32[2,512]{1,0:T(2,128)S(1)} %get-tuple-element.44.place_ref.place_in.refs_1_, f32[272,128]{1,0:T(8,128)S(1)} %get-tuple-element.65.coeff_ref, f32[8,128]{1,0:T(8,128)S(1)} %near_field.2.refs_8_.refs_0_), custom_call_target="tpu_custom_call" | custom-call | flops 1048576 | bytes 4194304 | tf_op jit(solution)/shard_map/place_lines/pallas_call | solution.py:502
  40.1 0.0 copy-start.6
  40.1 0.8 inverse_rest.5.refs_0_
  41.0 0.0 copy-done.5
  41.1 0.1 copy-done.6
  41.1 0.4 sample_early.2.refs_2_
  41.6 0.6 collective-permute-done.8.refs_1_
  42.2 2.1 %sample.2.refs_2_.rounded_ref.refs_7_ = f32[4,128]{1,0:T(4,128)S(1)} custom-call(s32[2,512]{1,0:T(2,128)S(1)} %get-tuple-element.44.place_ref.place_in.refs_1_, s16[672,128]{1,0:T(8,128)(2,1)S(1)} %collective-permute-done.7.refs_0_, s16[672,128]{1,0:T(8,128)(2,1)S(1)} %collective-permute-done.8.refs_1_, f32[656,256]{1,0:T(8,128)S(1)} %sample_early.2.refs_2_, ...), custom_call_target="tpu_custom_call" | custom-call | flops 169869312 | bytes 4194304 | tf_op jit(solution)/shard_map/sample/pallas_call | solution.py:1075
  44.4 3.8 %spread.1 = (s16[672,128]{1,0:T(8,128)(2,1)S(1)}, s16[672,128]{1,0:T(8,128)(2,1)S(1)}, bf16[656,256]{1,0:T(8,128)(2,1)S(1)}, bf16[656,256]{1,0:T(8,128)(2,1)S(1)}) custom-call(f32[512]{0:T(512)S(1)} %bitcast.6, s32[2,512]{1,0:T(2,128)S(1)} %get-tuple-element.44.place_ref.place_in.refs_1_, f32[4,128]{1,0:T(4,128)S(1)} %sample.2.refs_2_.rounded_ref.refs_7_, ...), custom_call_target="tpu_custom_call" | custom-call | flops 169869312 | bytes 4194304 | tf_op jit(solution)/shard_map/spread/pallas_call | solution.py:412
  48.2 1.0 %collective-permute-start.11 = (s16[672,128]{1,0:T(8,128)(2,1)S(1)}, s16[672,128]{1,0:T(8,128)(2,1)S(1)}, u32[]{:S(2)}, u32[]{:S(2)}) collective-permute-start(s16[672,128]{1,0:T(8,128)(2,1)S(1)} %get-tuple-element.68), channel_id=1, source_target_pairs={{0,2},{1,3},{2,0},{3,1},{4,6},{5,7},{6,4},{7,5},{8,10},{9,11},{10,... | collective-permute-start | bytes 516104 | tf_op jit(solution)/shard_map/ppermute | solution.py:1199
  49.2 0.5 spread_rest.7
  49.8 0.7 collective-permute-start.10
  50.5 0.6 collective-permute-start.12
  51.0 0.5 spread_rest.6.refs_0_
  51.6 3.9 %collective-permute-done.11.refs_1_.refs_2_ = s16[672,128]{1,0:T(8,128)(2,1)S(1)} collective-permute-done((s16[672,128]{1,0:T(8,128)(2,1)S(1)}, s16[672,128]{1,0:T(8,128)(2,1)S(1)}, u32[]{:S(2)}, u32[]{:S(2)}) %collective-permute-start.11) | collective-permute-done | bytes 172064 | tf_op jit(solution)/shard_map/ppermute | solution.py:1199
  55.5 0.7 forward_early.3
  56.2 1.9 %collective-permute-done.12.refs_3_ = s16[672,128]{1,0:T(8,128)(2,1)S(1)} collective-permute-done((s16[672,128]{1,0:T(8,128)(2,1)S(1)}, s16[672,128]{1,0:T(8,128)(2,1)S(1)}, u32[]{:S(2)}, u32[]{:S(2)}) %collective-permute-start.12) | collective-permute-done | bytes 172064 | tf_op jit(solution)/shard_map/ppermute | solution.py:1199
  58.1 1.3 %forward.3 = (f32[18,256,128]{2,1,0:T(8,128)S(1)}, s16[400,128]{1,0:T(8,128)(2,1)S(1)}, s16[336,128]{1,0:T(8,128)(2,1)S(1)}, s16[592,128]{1,0:T(8,128)(2,1)S(1)}...) custom-call(s16[672,128]{1,0:T(8,128)(2,1)S(1)} %spread_rest.6.refs_0_, ...), custom_call_target="tpu_custom_call" | custom-call | flops 301989888 | bytes 4718592 | tf_op jit(solution)/shard_map/forward/pallas_call | solution.py:697
  59.4 0.1 collective-permute-start.15
  59.5 0.9 %collective-permute-start.14 = (s16[592,128]{1,0:T(8,128)(2,1)S(1)}, s16[592,128]{1,0:T(8,128)(2,1)S(1)}, u32[]{:S(2)}, u32[]{:S(2)}) collective-permute-start(s16[592,128]{1,0:T(8,128)(2,1)S(1)} %get-tuple-element.74), channel_id=1, source_target_pairs={{4,8},{8,4},{5,9},{9,5},{6,10},{10,6},{7,11},{11,7},{20,24},{24,20... | collective-permute-start | bytes 454664 | tf_op jit(solution)/shard_map/ppermute | solution.py:1213
  60.4 4.4 %collective-permute-start.13 = (s16[336,128]{1,0:T(8,128)(2,1)S(1)}, s16[336,128]{1,0:T(8,128)(2,1)S(1)}, u32[]{:S(2)}, u32[]{:S(2)}) collective-permute-start(s16[336,128]{1,0:T(8,128)(2,1)S(1)} %get-tuple-element.73), channel_id=1, source_target_pairs={{0,4},{8,12},{4,0},{12,8},{1,5},{9,13},{5,1},{13,9},{2,6},{10,14},... | collective-permute-start | bytes 258056 | tf_op jit(solution)/shard_map/ppermute | solution.py:1214
  64.7 0.2 pair_messages.3
  64.9 0.8 collective-permute-start.16
  65.7 1.6 %collective-permute-done.13.layers_ref.refs_0_ = s16[336,128]{1,0:T(8,128)(2,1)S(1)} collective-permute-done((s16[336,128]{1,0:T(8,128)(2,1)S(1)}, s16[336,128]{1,0:T(8,128)(2,1)S(1)}, u32[]{:S(2)}, u32[]{:S(2)}) %collective-permute-start.13) | collective-permute-done | bytes 86048 | tf_op jit(solution)/shard_map/ppermute | solution.py:1214
  67.3 0.4 borders.3.refs_1_
  67.8 3.9 %collective-permute-done.16.refs_6_ = s16[272,128]{1,0:T(8,128)(2,1)S(1)} collective-permute-done((s16[272,128]{1,0:T(8,128)(2,1)S(1)}, s16[272,128]{1,0:T(8,128)(2,1)S(1)}, u32[]{:S(2)}, u32[]{:S(2)}) %collective-permute-start.16) | collective-permute-done | bytes 69664 | tf_op jit(solution)/shard_map/ppermute | solution.py:1216
  71.7 1.9 %inverse.3 = (s16[672,128]{1,0:T(8,128)(2,1)S(1)}, s16[672,128]{1,0:T(8,128)(2,1)S(1)}, bf16[18,256,128]{2,1,0:T(8,128)(2,1)S(1)}, bf16[18,256,128]{2,1,0:T(8,128)(2,1)S(1)}) custom-call(f32[18,256,128]{2,1,0:T(8,128)S(1)} %get-tuple-element.72.refs_0_, f32[4,256,128]{2,1,0:T(8,128)S(1)} %borders.3.refs_1_, ...), custom_call_target="tpu_custom_call" | custom-call | flops 301989888 | bytes 4718592 | tf_op jit(solution)/shard_map/inverse/pallas_call | solution.py:930
  73.6 1.8 %collective-permute-start.19 = (s16[672,128]{1,0:T(8,128)(2,1)S(1)}, s16[672,128]{1,0:T(8,128)(2,1)S(1)}, u32[]{:S(2)}, u32[]{:S(2)}) collective-permute-start(s16[672,128]{1,0:T(8,128)(2,1)S(1)} %get-tuple-element.81), channel_id=1, source_target_pairs={{0,2},{1,3},{2,0},{3,1},{4,6},{5,7},{6,4},{7,5},{8,10},{9,11},{10,... | collective-permute-start | bytes 516104 | tf_op jit(solution)/shard_map/ppermute | solution.py:1199
  75.4 0.8 inverse_rest.6.refs_4_
  76.3 0.1 collective-permute-start.17
  76.4 0.4 collective-permute-start.18
  76.8 1.1 %near_field.3.refs_8_ = f32[8,128]{1,0:T(8,128)S(1)} custom-call(s32[24]{0:T(128)S(1)} %get-tuple-element.84.place_ref, s32[24]{0:T(128)S(1)} %get-tuple-element.83.target_ref, s16[336,128]{1,0:T(8,128)(2,1)S(1)} %collective-permute-done.13.layers_ref.refs_0_, s16[592,128]{1,0:T(8,128)(2,1)S(1)} %collective-permute-done.14.odd_ref.refs_3_.refs_1_, ...), custom_call_target="tpu_custom_call" | custom-call | flops 12582912 | bytes 786432 | tf_op jit(solution)/shard_map/near_field/pallas_call | solution.py:1133
  77.8 0.9 %inverse_rest.7.refs_0_ = s16[672,128]{1,0:T(8,128)(2,1)S(1)} custom-call(bf16[18,256,128]{2,1,0:T(8,128)(2,1)S(1)} %get-tuple-element.78.field_high, bf16[18,256,128]{2,1,0:T(8,128)(2,1)S(1)} %get-tuple-element.79.field_low, bf16[4,48,256]{2,1,0:T(8,128)(2,1)S(1)} %copy-done.1, bf16[4,48,256]{2,1,0:T(8,128)(2,1)S(1)} %copy-done.2), custom_call_target="tpu_custom_call" | custom-call | flops 301989888 | bytes 4718592 | tf_op jit(solution)/shard_map/inverse_rest/pallas_call | solution.py:954
  78.7 0.8 collective-permute-done.19.refs_1_
  79.5 0.4 sample_early.3.refs_2_
  80.0 2.6 %collective-permute-done.18.refs_1_ = s16[672,128]{1,0:T(8,128)(2,1)S(1)} collective-permute-done((s16[672,128]{1,0:T(8,128)(2,1)S(1)}, s16[672,128]{1,0:T(8,128)(2,1)S(1)}, u32[]{:S(2)}, u32[]{:S(2)}) %collective-permute-start.18) | collective-permute-done | bytes 172064 | tf_op jit(solution)/shard_map/ppermute | solution.py:1199
  82.5 2.7 %sample.3 = f32[2,512]{1,0:T(2,128)} custom-call(s32[2,512]{1,0:T(2,128)S(1)} %get-tuple-element.44.place_ref.place_in.refs_1_, s16[672,128]{1,0:T(8,128)(2,1)S(1)} %collective-permute-done.17.refs_0_, s16[672,128]{1,0:T(8,128)(2,1)S(1)} %collective-permute-done.18.refs_1_, f32[656,256]{1,0:T(8,128)S(1)} %sample_early.3.refs_2_, ...), custom_call_target="tpu_custom_call" | custom-call | flops 169869312 | bytes 4194304 | tf_op jit(solution)/shard_map/sample/pallas_call | solution.py:1075
  (26 shorter events, 0.1 us)
Async XLA Ops:
  5.7 9.7 %collective-permute-start.1 = (s16[672,128]{1,0:T(8,128)(2,1)S(1)}, s16[672,128]{1,0:T(8,128)(2,1)S(1)}, u32[]{:S(2)}, u32[]{:S(2)}) collective-permute-start(s16[672,128]{1,0:T(8,128)(2,1)S(1)} %get-tuple-element.50), channel_id=1, source_target_pairs={{0,2},{1,3},{2,0},{3,1},{4,6},{5,7},{6,4},{7,5},{8,10},{9,11},{10,... | collective-permute-start | bytes 516104 | tf_op jit(solution)/shard_map/ppermute | solution.py:1199
  9.2 6.9 %collective-permute-start = (s16[672,128]{1,0:T(8,128)(2,1)S(1)}, s16[672,128]{1,0:T(8,128)(2,1)S(1)}, u32[]{:S(2)}, u32[]{:S(2)}) collective-permute-start(s16[672,128]{1,0:T(8,128)(2,1)S(1)} %spread_rest.5), channel_id=1, source_target_pairs={{0,1},{1,0},{2,3},{3,2},{4,5},{5,4},{6,7},{7,6},{8,9},{9,8},{10,11... | collective-permute-start | bytes 516104 | tf_op jit(solution)/shard_map/ppermute | solution.py:1199
  9.3 6.8 %collective-permute-start.2 = (s16[672,128]{1,0:T(8,128)(2,1)S(1)}, s16[672,128]{1,0:T(8,128)(2,1)S(1)}, u32[]{:S(2)}, u32[]{:S(2)}) collective-permute-start(s16[672,128]{1,0:T(8,128)(2,1)S(1)} %get-tuple-element.51), channel_id=1, source_target_pairs={{0,3},{1,2},{2,1},{3,0},{4,7},{5,6},{6,5},{7,4},{8,11},{9,10},{10,... | collective-permute-start | bytes 516104 | tf_op jit(solution)/shard_map/ppermute | solution.py:1199
  9.4 0.9 %copy-start.3 = (f32[64,512]{1,0:T(8,128)S(1)}, f32[64,512]{1,0:T(8,128)}, u32[]{:S(2)}) copy-start(f32[64,512]{1,0:T(8,128)} %refs_3_.8) | copy-start | bytes 393220
  13.8 1.6 %copy-start = (bf16[2,256,240]{2,1,0:T(8,128)(2,1)S(1)}, bf16[2,256,240]{2,1,0:T(8,128)(2,1)}, u32[]{:S(2)}) copy-start(bf16[2,256,240]{2,1,0:T(8,128)(2,1)} %constant.76.clone.refs_2_.refs_6_.table_ref) | copy-start | bytes 737284
  16.1 14.9 %copy-start.1 = (bf16[4,48,256]{2,1,0:T(8,128)(2,1)S(1)}, bf16[4,48,256]{2,1,0:T(8,128)(2,1)}, u32[]{:S(2)}) copy-start(bf16[4,48,256]{2,1,0:T(8,128)(2,1)} %constant.77.clone.refs_7_.high_ref) | copy-start | bytes 294916
  16.1 14.9 %copy-start.2 = (bf16[4,48,256]{2,1,0:T(8,128)(2,1)S(1)}, bf16[4,48,256]{2,1,0:T(8,128)(2,1)}, u32[]{:S(2)}) copy-start(bf16[4,48,256]{2,1,0:T(8,128)(2,1)} %constant.78.clone.refs_8_.low_ref) | copy-start | bytes 294916
  17.4 7.5 %collective-permute-start.5 = (s16[400,128]{1,0:T(8,128)(2,1)S(1)}, s16[400,128]{1,0:T(8,128)(2,1)S(1)}, u32[]{:S(2)}, u32[]{:S(2)}) collective-permute-start(s16[400,128]{1,0:T(8,128)(2,1)S(1)} %get-tuple-element.57), channel_id=1, source_target_pairs={{0,4},{8,12},{4,0},{12,8},{1,5},{9,13},{5,1},{13,9},{2,6},{10,14},... | collective-permute-start | bytes 307208 | tf_op jit(solution)/shard_map/ppermute | solution.py:1212
  19.5 7.8 %collective-permute-start.4 = (s16[592,128]{1,0:T(8,128)(2,1)S(1)}, s16[592,128]{1,0:T(8,128)(2,1)S(1)}, u32[]{:S(2)}, u32[]{:S(2)}) collective-permute-start(s16[592,128]{1,0:T(8,128)(2,1)S(1)} %get-tuple-element.56), channel_id=1, source_target_pairs={{4,8},{8,4},{5,9},{9,5},{6,10},{10,6},{7,11},{11,7},{20,24},{24,20... | collective-permute-start | bytes 454664 | tf_op jit(solution)/shard_map/ppermute | solution.py:1213
  20.4 6.9 %collective-permute-start.3 = (s16[336,128]{1,0:T(8,128)(2,1)S(1)}, s16[336,128]{1,0:T(8,128)(2,1)S(1)}, u32[]{:S(2)}, u32[]{:S(2)}) collective-permute-start(s16[336,128]{1,0:T(8,128)(2,1)S(1)} %get-tuple-element.55), channel_id=1, source_target_pairs={{0,4},{8,12},{4,0},{12,8},{1,5},{9,13},{5,1},{13,9},{2,6},{10,14},... | collective-permute-start | bytes 258056 | tf_op jit(solution)/shard_map/ppermute | solution.py:1214
  25.0 9.5 %copy-start.8 = (s32[24]{0:T(128)S(1)}, s32[24]{0:T(128)}, u32[]{:S(2)}) copy-start(s32[24]{0:T(128)} %param.21) | copy-start | bytes 292
  25.0 9.5 %copy-start.9 = (s32[24]{0:T(128)S(1)}, s32[24]{0:T(128)}, u32[]{:S(2)}) copy-start(s32[24]{0:T(128)} %param.22) | copy-start | bytes 292
  25.0 6.0 %collective-permute-start.6 = (s16[272,128]{1,0:T(8,128)(2,1)S(1)}, s16[272,128]{1,0:T(8,128)(2,1)S(1)}, u32[]{:S(2)}, u32[]{:S(2)}) collective-permute-start(s16[272,128]{1,0:T(8,128)(2,1)S(1)} %pair_messages.2), channel_id=1, source_target_pairs={{0,8},{4,12},{8,0},{12,4},{1,9},{5,13},{9,1},{13,5},{2,10},{6,14},... | collective-permute-start | bytes 208904 | tf_op jit(solution)/shard_map/ppermute | solution.py:1216
  32.9 3.2 %copy-start.4 = (bf16[24,128,128]{2,1,0:T(8,128)(2,1)S(1)}, bf16[24,128,128]{2,1,0:T(8,128)(2,1)}, u32[]{:S(2)}) copy-start(bf16[24,128,128]{2,1,0:T(8,128)(2,1)} %refs_3_.10) | copy-start | bytes 2359300
  32.9 8.1 %collective-permute-start.9 = (s16[672,128]{1,0:T(8,128)(2,1)S(1)}, s16[672,128]{1,0:T(8,128)(2,1)S(1)}, u32[]{:S(2)}, u32[]{:S(2)}) collective-permute-start(s16[672,128]{1,0:T(8,128)(2,1)S(1)} %get-tuple-element.63), channel_id=1, source_target_pairs={{0,2},{1,3},{2,0},{3,1},{4,6},{5,7},{6,4},{7,5},{8,10},{9,11},{10,... | collective-permute-start | bytes 516104 | tf_op jit(solution)/shard_map/ppermute | solution.py:1199
  35.4 6.2 %collective-permute-start.7 = (s16[672,128]{1,0:T(8,128)(2,1)S(1)}, s16[672,128]{1,0:T(8,128)(2,1)S(1)}, u32[]{:S(2)}, u32[]{:S(2)}) collective-permute-start(s16[672,128]{1,0:T(8,128)(2,1)S(1)} %inverse_rest.4.refs_4_), channel_id=1, source_target_pairs={{0,1},{1,0},{2,3},{3,2},{4,5},{5,4},{6,7},{7,6},{8,9},{9,8},{10,11... | collective-permute-start | bytes 516104 | tf_op jit(solution)/shard_map/ppermute | solution.py:1199
  35.4 6.8 %collective-permute-start.8 = (s16[672,128]{1,0:T(8,128)(2,1)S(1)}, s16[672,128]{1,0:T(8,128)(2,1)S(1)}, u32[]{:S(2)}, u32[]{:S(2)}) collective-permute-start(s16[672,128]{1,0:T(8,128)(2,1)S(1)} %get-tuple-element.62), channel_id=1, source_target_pairs={{0,3},{1,2},{2,1},{3,0},{4,7},{5,6},{6,5},{7,4},{8,11},{9,10},{10,... | collective-permute-start | bytes 516104 | tf_op jit(solution)/shard_map/ppermute | solution.py:1199
  40.1 1.0 %copy-start.5 = (bf16[4,128,256]{2,1,0:T(8,128)(2,1)S(1)}, bf16[4,128,256]{2,1,0:T(8,128)(2,1)}, u32[]{:S(2)}) copy-start(bf16[4,128,256]{2,1,0:T(8,128)(2,1)} %constant.79.clone.refs_2_.refs_3_) | copy-start | bytes 786436
  40.1 1.0 %copy-start.6 = (bf16[4,128,256]{2,1,0:T(8,128)(2,1)S(1)}, bf16[4,128,256]{2,1,0:T(8,128)(2,1)}, u32[]{:S(2)}) copy-start(bf16[4,128,256]{2,1,0:T(8,128)(2,1)} %constant.80.clone.refs_3_.refs_4_) | copy-start | bytes 786436
  41.0 1.3 %copy-start.7 = (s32[512]{0:T(512)S(1)}, s32[512]{0:T(512)}, u32[]{:S(2)}) copy-start(s32[512]{0:T(512)} %param.17) | copy-start | bytes 6148
  48.2 7.3 %collective-permute-start.11 = (s16[672,128]{1,0:T(8,128)(2,1)S(1)}, s16[672,128]{1,0:T(8,128)(2,1)S(1)}, u32[]{:S(2)}, u32[]{:S(2)}) collective-permute-start(s16[672,128]{1,0:T(8,128)(2,1)S(1)} %get-tuple-element.68), channel_id=1, source_target_pairs={{0,2},{1,3},{2,0},{3,1},{4,6},{5,7},{6,4},{7,5},{8,10},{9,11},{10,... | collective-permute-start | bytes 516104 | tf_op jit(solution)/shard_map/ppermute | solution.py:1199
  49.8 6.4 %collective-permute-start.10 = (s16[672,128]{1,0:T(8,128)(2,1)S(1)}, s16[672,128]{1,0:T(8,128)(2,1)S(1)}, u32[]{:S(2)}, u32[]{:S(2)}) collective-permute-start(s16[672,128]{1,0:T(8,128)(2,1)S(1)} %spread_rest.7), channel_id=1, source_target_pairs={{0,1},{1,0},{2,3},{3,2},{4,5},{5,4},{6,7},{7,6},{8,9},{9,8},{10,11... | collective-permute-start | bytes 516104 | tf_op jit(solution)/shard_map/ppermute | solution.py:1199
  50.5 7.6 %collective-permute-start.12 = (s16[672,128]{1,0:T(8,128)(2,1)S(1)}, s16[672,128]{1,0:T(8,128)(2,1)S(1)}, u32[]{:S(2)}, u32[]{:S(2)}) collective-permute-start(s16[672,128]{1,0:T(8,128)(2,1)S(1)} %get-tuple-element.69), channel_id=1, source_target_pairs={{0,3},{1,2},{2,1},{3,0},{4,7},{5,6},{6,5},{7,4},{8,11},{9,10},{10,... | collective-permute-start | bytes 516104 | tf_op jit(solution)/shard_map/ppermute | solution.py:1199
  59.4 5.3 %collective-permute-start.15 = (s16[400,128]{1,0:T(8,128)(2,1)S(1)}, s16[400,128]{1,0:T(8,128)(2,1)S(1)}, u32[]{:S(2)}, u32[]{:S(2)}) collective-permute-start(s16[400,128]{1,0:T(8,128)(2,1)S(1)} %get-tuple-element.75), channel_id=1, source_target_pairs={{0,4},{8,12},{4,0},{12,8},{1,5},{9,13},{5,1},{13,9},{2,6},{10,14},... | collective-permute-start | bytes 307208 | tf_op jit(solution)/shard_map/ppermute | solution.py:1212
  59.5 7.9 %collective-permute-start.14 = (s16[592,128]{1,0:T(8,128)(2,1)S(1)}, s16[592,128]{1,0:T(8,128)(2,1)S(1)}, u32[]{:S(2)}, u32[]{:S(2)}) collective-permute-start(s16[592,128]{1,0:T(8,128)(2,1)S(1)} %get-tuple-element.74), channel_id=1, source_target_pairs={{4,8},{8,4},{5,9},{9,5},{6,10},{10,6},{7,11},{11,7},{20,24},{24,20... | collective-permute-start | bytes 454664 | tf_op jit(solution)/shard_map/ppermute | solution.py:1213
  60.4 7.0 %collective-permute-start.13 = (s16[336,128]{1,0:T(8,128)(2,1)S(1)}, s16[336,128]{1,0:T(8,128)(2,1)S(1)}, u32[]{:S(2)}, u32[]{:S(2)}) collective-permute-start(s16[336,128]{1,0:T(8,128)(2,1)S(1)} %get-tuple-element.73), channel_id=1, source_target_pairs={{0,4},{8,12},{4,0},{12,8},{1,5},{9,13},{5,1},{13,9},{2,6},{10,14},... | collective-permute-start | bytes 258056 | tf_op jit(solution)/shard_map/ppermute | solution.py:1214
  64.9 6.8 %collective-permute-start.16 = (s16[272,128]{1,0:T(8,128)(2,1)S(1)}, s16[272,128]{1,0:T(8,128)(2,1)S(1)}, u32[]{:S(2)}, u32[]{:S(2)}) collective-permute-start(s16[272,128]{1,0:T(8,128)(2,1)S(1)} %pair_messages.3), channel_id=1, source_target_pairs={{0,8},{4,12},{8,0},{12,4},{1,9},{5,13},{9,1},{13,5},{2,10},{6,14},... | collective-permute-start | bytes 208904 | tf_op jit(solution)/shard_map/ppermute | solution.py:1216
  73.6 5.9 %collective-permute-start.19 = (s16[672,128]{1,0:T(8,128)(2,1)S(1)}, s16[672,128]{1,0:T(8,128)(2,1)S(1)}, u32[]{:S(2)}, u32[]{:S(2)}) collective-permute-start(s16[672,128]{1,0:T(8,128)(2,1)S(1)} %get-tuple-element.81), channel_id=1, source_target_pairs={{0,2},{1,3},{2,0},{3,1},{4,6},{5,7},{6,4},{7,5},{8,10},{9,11},{10,... | collective-permute-start | bytes 516104 | tf_op jit(solution)/shard_map/ppermute | solution.py:1199
  76.3 3.7 %collective-permute-start.17 = (s16[672,128]{1,0:T(8,128)(2,1)S(1)}, s16[672,128]{1,0:T(8,128)(2,1)S(1)}, u32[]{:S(2)}, u32[]{:S(2)}) collective-permute-start(s16[672,128]{1,0:T(8,128)(2,1)S(1)} %inverse_rest.6.refs_4_), channel_id=1, source_target_pairs={{0,1},{1,0},{2,3},{3,2},{4,5},{5,4},{6,7},{7,6},{8,9},{9,8},{10,11... | collective-permute-start | bytes 516104 | tf_op jit(solution)/shard_map/ppermute | solution.py:1199
  76.4 6.2 %collective-permute-start.18 = (s16[672,128]{1,0:T(8,128)(2,1)S(1)}, s16[672,128]{1,0:T(8,128)(2,1)S(1)}, u32[]{:S(2)}, u32[]{:S(2)}) collective-permute-start(s16[672,128]{1,0:T(8,128)(2,1)S(1)} %get-tuple-element.80), channel_id=1, source_target_pairs={{0,3},{1,2},{2,1},{3,0},{4,7},{5,6},{6,5},{7,4},{8,11},{9,10},{10,... | collective-permute-start | bytes 516104 | tf_op jit(solution)/shard_map/ppermute | solution.py:1199

commit v24 on v22

--- a/solution.py
+++ b/solution.py
@@ -21,7 +21,7 @@
 ALL_AXES = ("wide", "narrow", "pair")
 F32 = jnp.float32
 BF16 = jnp.bfloat16
-VMEM_LIMIT = 24 * 1024 * 1024
+VMEM_LIMIT = 20 * 1024 * 1024
 START_LIMIT = VMEM_LIMIT
 EARLY_FLOPS = 5 * 10**9
 GROUP = 32

time: 83.9 us -> 83.9 us (level)
  no operation moved by 1% of the time
where the time goes in v24:
time: 83.9 us; the launch traced here: 83.7 us
  Pallas kernels  36.3 us (43%)
  starting transfers between devices  24.4 us (29%)
  waiting for transfers between devices  20.2 us (24%)
  local copies, waits for them, and re-layouts  2.16 us (3%)
    ppermute x12, starting transfers between devices, turned(): lax.ppermute(part, Y_AXES, swap_pairs)  10.1 us
    ppermute x12, waiting for transfers between devices, turned(): lax.ppermute(part, Y_AXES, swap_pairs)  9.88 us
    ppermute x2, starting transfers between devices, convolve_and_sample(): even_layers = lax.ppermute(layers, 'wide', even_swap)  8.8 us
    pallas_call x2, Pallas kernels, spread(): pl.pallas_call(functools.partial(start_kernel if placed is None else spre...  7.7 us
    ppermute x2, waiting for transfers between devices, convolve_and_sample(): lax.ppermute(message, 'wide', [(i, i ^ flip) for i in range(x_count)])  7.18 us
    pallas_call x2, Pallas kernels, sample(): pl.pallas_call(functools.partial(sample_kernel, last, reach_x, reach_y, f...  4.87 us
    pallas_call x2, Pallas kernels, inverse(): pl.pallas_call(functools.partial(inverse_kernel, reach_x, reach_y, flips,...  3.8 us
    pallas_call x1, Pallas kernels, place_sample_lines(): pl.pallas_call(functools.partial(sample_lines_kernel, blocks), grid=(1,),...  3.41 us
  transfers between devices with their start and end apart: 20, of which 9 were waited for; matrix products, arithmetic and copies ran while one was open for 1% of the time, Pallas kernels for 21%

profile of v24, /device:TPU:0, one launch (start us, length us, event | category | flops | bytes accessed | tf_op | source)
XLA Modules:
  0.0 83.7 jit_solution(9978012073780842988)
XLA Ops:
  0.0 5.0 %start.1 = (s16[672,128]{1,0:T(8,128)(2,1)S(1)}, s16[672,128]{1,0:T(8,128)(2,1)S(1)}, bf16[656,256]{1,0:T(8,128)(2,1)S(1)}, bf16[656,256]{1,0:T(8,128)(2,1)S(1)}...) custom-call(f32[512]{0:T(512)} %refs_0_.2, ...), custom_call_target="tpu_custom_call" | custom-call | flops 169869312 | bytes 4194304 | tf_op jit(solution)/shard_map/start/pallas_call | solution.py:412
  5.0 3.0 %collective-permute-start.1 = (s16[672,128]{1,0:T(8,128)(2,1)S(1)}, s16[672,128]{1,0:T(8,128)(2,1)S(1)}, u32[]{:S(2)}, u32[]{:S(2)}) collective-permute-start(s16[672,128]{1,0:T(8,128)(2,1)S(1)} %get-tuple-element.50), channel_id=1, source_target_pairs={{0,2},{1,3},{2,0},{3,1},{4,6},{5,7},{6,4},{7,5},{8,10},{9,11},{10,... | collective-permute-start | bytes 516104 | tf_op jit(solution)/shard_map/ppermute | solution.py:1199
  8.1 0.5 spread_rest.5
  8.6 0.1 collective-permute-start
  8.7 0.1 collective-permute-start.2
  8.8 0.9 %copy-done.3 = f32[64,512]{1,0:T(8,128)S(1)} copy-done((f32[64,512]{1,0:T(8,128)S(1)}, f32[64,512]{1,0:T(8,128)}, u32[]{:S(2)}) %copy-start.3) | copy-done | bytes 131096
  9.7 3.4 %place_sample_lines.1.refs_8_.refs_5_ = f32[8192,128]{1,0:T(8,128)S(1)} custom-call(s32[2,512]{1,0:T(2,128)S(1)} %get-tuple-element.44.place_ref.place_in.refs_1_, f32[64,512]{1,0:T(8,128)S(1)} %copy-done.3, f32[64,512]{1,0:T(8,128)S(1)} %copy-done.3, f32[64,512]{1,0:T(8,128)S(1)} %copy-done.3, f32[64,512]{1,0:T(8,128)S(1)} %copy-done.3), custom_call_target="tpu_custom_call" | custom-call | flops 1048576 | bytes 4194304 | tf_op jit(solution)/shard_map/place_sample_lines/pallas_call | solution.py:483
  13.1 0.5 spread_rest.4.refs_0_
  13.6 1.1 %dynamic-slice_bitcast_fusion.refs_7_.modes_ref.refs_9_ = f32[4,256,128]{2,1,0:T(8,128)S(1)} fusion(f32[4,4,256,128]{3,2,1,0:T(8,128)} %constant.73.clone, s32[]{:T(128)S(6)} %select_n.30), kind=kLoop, calls=%fused_computation | loop fusion | bytes 1048580 | tf_op jit(solution)/shard_map/jit(dynamic_index_in_dim)/squeeze | solution.py:1176
  14.8 0.7 forward_early.2
  15.4 0.0 collective-permute-done.2.refs_3_
  15.5 1.2 %forward.2 = (f32[18,256,128]{2,1,0:T(8,128)S(1)}, s16[400,128]{1,0:T(8,128)(2,1)S(1)}, s16[336,128]{1,0:T(8,128)(2,1)S(1)}, s16[592,128]{1,0:T(8,128)(2,1)S(1)}...) custom-call(s16[672,128]{1,0:T(8,128)(2,1)S(1)} %spread_rest.4.refs_0_, ...), custom_call_target="tpu_custom_call" | custom-call | flops 301989888 | bytes 4718592 | tf_op jit(solution)/shard_map/forward/pallas_call | solution.py:697
  16.7 2.2 %collective-permute-start.5 = (s16[400,128]{1,0:T(8,128)(2,1)S(1)}, s16[400,128]{1,0:T(8,128)(2,1)S(1)}, u32[]{:S(2)}, u32[]{:S(2)}) collective-permute-start(s16[400,128]{1,0:T(8,128)(2,1)S(1)} %get-tuple-element.57), channel_id=1, source_target_pairs={{0,4},{8,12},{4,0},{12,8},{1,5},{9,13},{5,1},{13,9},{2,6},{10,14},... | collective-permute-start | bytes 307208 | tf_op jit(solution)/shard_map/ppermute | solution.py:1212
  18.9 0.8 %collective-permute-start.4 = (s16[592,128]{1,0:T(8,128)(2,1)S(1)}, s16[592,128]{1,0:T(8,128)(2,1)S(1)}, u32[]{:S(2)}, u32[]{:S(2)}) collective-permute-start(s16[592,128]{1,0:T(8,128)(2,1)S(1)} %get-tuple-element.56), channel_id=1, source_target_pairs={{4,8},{8,4},{5,9},{9,5},{6,10},{10,6},{7,11},{11,7},{20,24},{24,20... | collective-permute-start | bytes 454664 | tf_op jit(solution)/shard_map/ppermute | solution.py:1213
  19.7 4.5 %collective-permute-start.3 = (s16[336,128]{1,0:T(8,128)(2,1)S(1)}, s16[336,128]{1,0:T(8,128)(2,1)S(1)}, u32[]{:S(2)}, u32[]{:S(2)}) collective-permute-start(s16[336,128]{1,0:T(8,128)(2,1)S(1)} %get-tuple-element.55), channel_id=1, source_target_pairs={{0,4},{8,12},{4,0},{12,8},{1,5},{9,13},{5,1},{13,9},{2,6},{10,14},... | collective-permute-start | bytes 258056 | tf_op jit(solution)/shard_map/ppermute | solution.py:1214
  24.2 0.2 pair_messages.2
  24.4 0.0 copy-start.9
  24.4 0.7 collective-permute-start.6
  25.1 1.5 %collective-permute-done.3.layers_ref.refs_0_ = s16[336,128]{1,0:T(8,128)(2,1)S(1)} collective-permute-done((s16[336,128]{1,0:T(8,128)(2,1)S(1)}, s16[336,128]{1,0:T(8,128)(2,1)S(1)}, u32[]{:S(2)}, u32[]{:S(2)}) %collective-permute-start.3) | collective-permute-done | bytes 86048 | tf_op jit(solution)/shard_map/ppermute | solution.py:1214
  26.6 0.4 borders.2.refs_1_
  27.1 3.2 %collective-permute-done.6.refs_6_ = s16[272,128]{1,0:T(8,128)(2,1)S(1)} collective-permute-done((s16[272,128]{1,0:T(8,128)(2,1)S(1)}, s16[272,128]{1,0:T(8,128)(2,1)S(1)}, u32[]{:S(2)}, u32[]{:S(2)}) %collective-permute-start.6) | collective-permute-done | bytes 69664 | tf_op jit(solution)/shard_map/ppermute | solution.py:1216
  30.3 1.9 %inverse.2 = (s16[672,128]{1,0:T(8,128)(2,1)S(1)}, s16[672,128]{1,0:T(8,128)(2,1)S(1)}, bf16[18,256,128]{2,1,0:T(8,128)(2,1)S(1)}, bf16[18,256,128]{2,1,0:T(8,128)(2,1)S(1)}) custom-call(f32[18,256,128]{2,1,0:T(8,128)S(1)} %get-tuple-element.54.refs_0_, f32[4,256,128]{2,1,0:T(8,128)S(1)} %borders.2.refs_1_, ...), custom_call_target="tpu_custom_call" | custom-call | flops 301989888 | bytes 4718592 | tf_op jit(solution)/shard_map/inverse/pallas_call | solution.py:930
  32.3 1.6 %collective-permute-start.9 = (s16[672,128]{1,0:T(8,128)(2,1)S(1)}, s16[672,128]{1,0:T(8,128)(2,1)S(1)}, u32[]{:S(2)}, u32[]{:S(2)}) collective-permute-start(s16[672,128]{1,0:T(8,128)(2,1)S(1)} %get-tuple-element.63), channel_id=1, source_target_pairs={{0,2},{1,3},{2,0},{3,1},{4,6},{5,7},{6,4},{7,5},{8,10},{9,11},{10,... | collective-permute-start | bytes 516104 | tf_op jit(solution)/shard_map/ppermute | solution.py:1199
  33.8 0.8 %inverse_rest.4.refs_4_ = s16[672,128]{1,0:T(8,128)(2,1)S(1)} custom-call(bf16[18,256,128]{2,1,0:T(8,128)(2,1)S(1)} %get-tuple-element.60.field_high, bf16[18,256,128]{2,1,0:T(8,128)(2,1)S(1)} %get-tuple-element.61.field_low, bf16[4,48,256]{2,1,0:T(8,128)(2,1)S(1)} %copy-done.1, bf16[4,48,256]{2,1,0:T(8,128)(2,1)S(1)} %copy-done.2), custom_call_target="tpu_custom_call" | custom-call | flops 301989888 | bytes 4718592 | tf_op jit(solution)/shard_map/inverse_rest/pallas_call | solution.py:954
  34.7 0.1 collective-permute-start.7
  34.8 0.6 collective-permute-start.8
  35.4 1.0 %near_field.2.refs_8_.refs_0_ = f32[8,128]{1,0:T(8,128)S(1)} custom-call(s32[24]{0:T(128)S(1)} %get-tuple-element.84.place_ref, s32[24]{0:T(128)S(1)} %get-tuple-element.83.target_ref, s16[336,128]{1,0:T(8,128)(2,1)S(1)} %collective-permute-done.3.layers_ref.refs_0_, s16[592,128]{1,0:T(8,128)(2,1)S(1)} %collective-permute-done.4.odd_ref.refs_3_.refs_1_, ...), custom_call_target="tpu_custom_call" | custom-call | flops 12582912 | bytes 786432 | tf_op jit(solution)/shard_map/near_field/pallas_call | solution.py:1133
  36.5 3.0 %place_lines.1.refs_5_ = f32[8192,128]{1,0:T(8,128)S(1)} custom-call(s32[2,512]{1,0:T(2,128)S(1)} %get-tuple-element.44.place_ref.place_in.refs_1_, f32[272,128]{1,0:T(8,128)S(1)} %get-tuple-element.65.coeff_ref, f32[8,128]{1,0:T(8,128)S(1)} %near_field.2.refs_8_.refs_0_), custom_call_target="tpu_custom_call" | custom-call | flops 1048576 | bytes 4194304 | tf_op jit(solution)/shard_map/place_lines/pallas_call | solution.py:502
  39.4 0.0 copy-start.6
  39.5 0.8 %inverse_rest.5.refs_0_ = s16[672,128]{1,0:T(8,128)(2,1)S(1)} custom-call(bf16[18,256,128]{2,1,0:T(8,128)(2,1)S(1)} %get-tuple-element.60.field_high, bf16[18,256,128]{2,1,0:T(8,128)(2,1)S(1)} %get-tuple-element.61.field_low, bf16[4,48,256]{2,1,0:T(8,128)(2,1)S(1)} %copy-done.1, bf16[4,48,256]{2,1,0:T(8,128)(2,1)S(1)} %copy-done.2), custom_call_target="tpu_custom_call" | custom-call | flops 301989888 | bytes 4718592 | tf_op jit(solution)/shard_map/inverse_rest/pallas_call | solution.py:954
  40.3 0.1 copy-done.5
  40.4 0.1 copy-done.6
  40.5 0.4 sample_early.2.refs_2_
  40.9 0.6 collective-permute-done.8.refs_1_
  41.6 2.1 %sample.2.refs_2_.rounded_ref.refs_7_ = f32[4,128]{1,0:T(4,128)S(1)} custom-call(s32[2,512]{1,0:T(2,128)S(1)} %get-tuple-element.44.place_ref.place_in.refs_1_, s16[672,128]{1,0:T(8,128)(2,1)S(1)} %collective-permute-done.7.refs_0_, s16[672,128]{1,0:T(8,128)(2,1)S(1)} %collective-permute-done.8.refs_1_, f32[656,256]{1,0:T(8,128)S(1)} %sample_early.2.refs_2_, ...), custom_call_target="tpu_custom_call" | custom-call | flops 169869312 | bytes 4194304 | tf_op jit(solution)/shard_map/sample/pallas_call | solution.py:1075
  43.7 2.7 %spread.1 = (s16[672,128]{1,0:T(8,128)(2,1)S(1)}, s16[672,128]{1,0:T(8,128)(2,1)S(1)}, bf16[656,256]{1,0:T(8,128)(2,1)S(1)}, bf16[656,256]{1,0:T(8,128)(2,1)S(1)}) custom-call(f32[512]{0:T(512)S(1)} %bitcast.6, s32[2,512]{1,0:T(2,128)S(1)} %get-tuple-element.44.place_ref.place_in.refs_1_, f32[4,128]{1,0:T(4,128)S(1)} %sample.2.refs_2_.rounded_ref.refs_7_, ...), custom_call_target="tpu_custom_call" | custom-call | flops 169869312 | bytes 4194304 | tf_op jit(solution)/shard_map/spread/pallas_call | solution.py:412
  46.4 1.0 %collective-permute-start.11 = (s16[672,128]{1,0:T(8,128)(2,1)S(1)}, s16[672,128]{1,0:T(8,128)(2,1)S(1)}, u32[]{:S(2)}, u32[]{:S(2)}) collective-permute-start(s16[672,128]{1,0:T(8,128)(2,1)S(1)} %get-tuple-element.68), channel_id=1, source_target_pairs={{0,2},{1,3},{2,0},{3,1},{4,6},{5,7},{6,4},{7,5},{8,10},{9,11},{10,... | collective-permute-start | bytes 516104 | tf_op jit(solution)/shard_map/ppermute | solution.py:1199
  47.4 0.5 spread_rest.7
  47.9 0.7 collective-permute-start.10
  48.7 0.6 collective-permute-start.12
  49.2 0.5 spread_rest.6.refs_0_
  49.8 3.9 %collective-permute-done.11.refs_1_.refs_2_ = s16[672,128]{1,0:T(8,128)(2,1)S(1)} collective-permute-done((s16[672,128]{1,0:T(8,128)(2,1)S(1)}, s16[672,128]{1,0:T(8,128)(2,1)S(1)}, u32[]{:S(2)}, u32[]{:S(2)}) %collective-permute-start.11) | collective-permute-done | bytes 172064 | tf_op jit(solution)/shard_map/ppermute | solution.py:1199
  53.7 0.7 forward_early.3
  54.4 1.9 %collective-permute-done.12.refs_3_ = s16[672,128]{1,0:T(8,128)(2,1)S(1)} collective-permute-done((s16[672,128]{1,0:T(8,128)(2,1)S(1)}, s16[672,128]{1,0:T(8,128)(2,1)S(1)}, u32[]{:S(2)}, u32[]{:S(2)}) %collective-permute-start.12) | collective-permute-done | bytes 172064 | tf_op jit(solution)/shard_map/ppermute | solution.py:1199
  56.3 1.3 %forward.3 = (f32[18,256,128]{2,1,0:T(8,128)S(1)}, s16[400,128]{1,0:T(8,128)(2,1)S(1)}, s16[336,128]{1,0:T(8,128)(2,1)S(1)}, s16[592,128]{1,0:T(8,128)(2,1)S(1)}...) custom-call(s16[672,128]{1,0:T(8,128)(2,1)S(1)} %spread_rest.6.refs_0_, ...), custom_call_target="tpu_custom_call" | custom-call | flops 301989888 | bytes 4718592 | tf_op jit(solution)/shard_map/forward/pallas_call | solution.py:697
  57.6 0.1 collective-permute-start.15
  57.6 0.9 %collective-permute-start.14 = (s16[592,128]{1,0:T(8,128)(2,1)S(1)}, s16[592,128]{1,0:T(8,128)(2,1)S(1)}, u32[]{:S(2)}, u32[]{:S(2)}) collective-permute-start(s16[592,128]{1,0:T(8,128)(2,1)S(1)} %get-tuple-element.74), channel_id=1, source_target_pairs={{4,8},{8,4},{5,9},{9,5},{6,10},{10,6},{7,11},{11,7},{20,24},{24,20... | collective-permute-start | bytes 454664 | tf_op jit(solution)/shard_map/ppermute | solution.py:1213
  58.5 4.3 %collective-permute-start.13 = (s16[336,128]{1,0:T(8,128)(2,1)S(1)}, s16[336,128]{1,0:T(8,128)(2,1)S(1)}, u32[]{:S(2)}, u32[]{:S(2)}) collective-permute-start(s16[336,128]{1,0:T(8,128)(2,1)S(1)} %get-tuple-element.73), channel_id=1, source_target_pairs={{0,4},{8,12},{4,0},{12,8},{1,5},{9,13},{5,1},{13,9},{2,6},{10,14},... | collective-permute-start | bytes 258056 | tf_op jit(solution)/shard_map/ppermute | solution.py:1214
  62.9 0.2 pair_messages.3
  63.1 0.8 collective-permute-start.16
  63.9 1.6 %collective-permute-done.13.layers_ref.refs_0_ = s16[336,128]{1,0:T(8,128)(2,1)S(1)} collective-permute-done((s16[336,128]{1,0:T(8,128)(2,1)S(1)}, s16[336,128]{1,0:T(8,128)(2,1)S(1)}, u32[]{:S(2)}, u32[]{:S(2)}) %collective-permute-start.13) | collective-permute-done | bytes 86048 | tf_op jit(solution)/shard_map/ppermute | solution.py:1214
  65.5 0.5 borders.3.refs_1_
  66.0 3.9 %collective-permute-done.16.refs_6_ = s16[272,128]{1,0:T(8,128)(2,1)S(1)} collective-permute-done((s16[272,128]{1,0:T(8,128)(2,1)S(1)}, s16[272,128]{1,0:T(8,128)(2,1)S(1)}, u32[]{:S(2)}, u32[]{:S(2)}) %collective-permute-start.16) | collective-permute-done | bytes 69664 | tf_op jit(solution)/shard_map/ppermute | solution.py:1216
  69.9 1.9 %inverse.3 = (s16[672,128]{1,0:T(8,128)(2,1)S(1)}, s16[672,128]{1,0:T(8,128)(2,1)S(1)}, bf16[18,256,128]{2,1,0:T(8,128)(2,1)S(1)}, bf16[18,256,128]{2,1,0:T(8,128)(2,1)S(1)}) custom-call(f32[18,256,128]{2,1,0:T(8,128)S(1)} %get-tuple-element.72.refs_0_, f32[4,256,128]{2,1,0:T(8,128)S(1)} %borders.3.refs_1_, ...), custom_call_target="tpu_custom_call" | custom-call | flops 301989888 | bytes 4718592 | tf_op jit(solution)/shard_map/inverse/pallas_call | solution.py:930
  71.8 1.8 %collective-permute-start.19 = (s16[672,128]{1,0:T(8,128)(2,1)S(1)}, s16[672,128]{1,0:T(8,128)(2,1)S(1)}, u32[]{:S(2)}, u32[]{:S(2)}) collective-permute-start(s16[672,128]{1,0:T(8,128)(2,1)S(1)} %get-tuple-element.81), channel_id=1, source_target_pairs={{0,2},{1,3},{2,0},{3,1},{4,6},{5,7},{6,4},{7,5},{8,10},{9,11},{10,... | collective-permute-start | bytes 516104 | tf_op jit(solution)/shard_map/ppermute | solution.py:1199
  73.6 0.8 %inverse_rest.6.refs_4_ = s16[672,128]{1,0:T(8,128)(2,1)S(1)} custom-call(bf16[18,256,128]{2,1,0:T(8,128)(2,1)S(1)} %get-tuple-element.78.field_high, bf16[18,256,128]{2,1,0:T(8,128)(2,1)S(1)} %get-tuple-element.79.field_low, bf16[4,48,256]{2,1,0:T(8,128)(2,1)S(1)} %copy-done.1, bf16[4,48,256]{2,1,0:T(8,128)(2,1)S(1)} %copy-done.2), custom_call_target="tpu_custom_call" | custom-call | flops 301989888 | bytes 4718592 | tf_op jit(solution)/shard_map/inverse_rest/pallas_call | solution.py:954
  74.5 0.1 collective-permute-start.17
  74.6 0.4 collective-permute-start.18
  75.0 1.0 %near_field.3.refs_8_ = f32[8,128]{1,0:T(8,128)S(1)} custom-call(s32[24]{0:T(128)S(1)} %get-tuple-element.84.place_ref, s32[24]{0:T(128)S(1)} %get-tuple-element.83.target_ref, s16[336,128]{1,0:T(8,128)(2,1)S(1)} %collective-permute-done.13.layers_ref.refs_0_, s16[592,128]{1,0:T(8,128)(2,1)S(1)} %collective-permute-done.14.odd_ref.refs_3_.refs_1_, ...), custom_call_target="tpu_custom_call" | custom-call | flops 12582912 | bytes 786432 | tf_op jit(solution)/shard_map/near_field/pallas_call | solution.py:1133
  76.0 0.9 %inverse_rest.7.refs_0_ = s16[672,128]{1,0:T(8,128)(2,1)S(1)} custom-call(bf16[18,256,128]{2,1,0:T(8,128)(2,1)S(1)} %get-tuple-element.78.field_high, bf16[18,256,128]{2,1,0:T(8,128)(2,1)S(1)} %get-tuple-element.79.field_low, bf16[4,48,256]{2,1,0:T(8,128)(2,1)S(1)} %copy-done.1, bf16[4,48,256]{2,1,0:T(8,128)(2,1)S(1)} %copy-done.2), custom_call_target="tpu_custom_call" | custom-call | flops 301989888 | bytes 4718592 | tf_op jit(solution)/shard_map/inverse_rest/pallas_call | solution.py:954
  76.9 0.8 collective-permute-done.19.refs_1_
  77.7 0.4 sample_early.3.refs_2_
  78.2 2.6 %collective-permute-done.18.refs_1_ = s16[672,128]{1,0:T(8,128)(2,1)S(1)} collective-permute-done((s16[672,128]{1,0:T(8,128)(2,1)S(1)}, s16[672,128]{1,0:T(8,128)(2,1)S(1)}, u32[]{:S(2)}, u32[]{:S(2)}) %collective-permute-start.18) | collective-permute-done | bytes 172064 | tf_op jit(solution)/shard_map/ppermute | solution.py:1199
  80.7 2.7 %sample.3 = f32[2,512]{1,0:T(2,128)} custom-call(s32[2,512]{1,0:T(2,128)S(1)} %get-tuple-element.44.place_ref.place_in.refs_1_, s16[672,128]{1,0:T(8,128)(2,1)S(1)} %collective-permute-done.17.refs_0_, s16[672,128]{1,0:T(8,128)(2,1)S(1)} %collective-permute-done.18.refs_1_, f32[656,256]{1,0:T(8,128)S(1)} %sample_early.3.refs_2_, ...), custom_call_target="tpu_custom_call" | custom-call | flops 169869312 | bytes 4194304 | tf_op jit(solution)/shard_map/sample/pallas_call | solution.py:1075
  (26 shorter events, 0.1 us)
Async XLA Ops:
  5.0 9.7 %collective-permute-start.1 = (s16[672,128]{1,0:T(8,128)(2,1)S(1)}, s16[672,128]{1,0:T(8,128)(2,1)S(1)}, u32[]{:S(2)}, u32[]{:S(2)}) collective-permute-start(s16[672,128]{1,0:T(8,128)(2,1)S(1)} %get-tuple-element.50), channel_id=1, source_target_pairs={{0,2},{1,3},{2,0},{3,1},{4,6},{5,7},{6,4},{7,5},{8,10},{9,11},{10,... | collective-permute-start | bytes 516104 | tf_op jit(solution)/shard_map/ppermute | solution.py:1199
  8.6 6.8 %collective-permute-start = (s16[672,128]{1,0:T(8,128)(2,1)S(1)}, s16[672,128]{1,0:T(8,128)(2,1)S(1)}, u32[]{:S(2)}, u32[]{:S(2)}) collective-permute-start(s16[672,128]{1,0:T(8,128)(2,1)S(1)} %spread_rest.5), channel_id=1, source_target_pairs={{0,1},{1,0},{2,3},{3,2},{4,5},{5,4},{6,7},{7,6},{8,9},{9,8},{10,11... | collective-permute-start | bytes 516104 | tf_op jit(solution)/shard_map/ppermute | solution.py:1199
  8.7 6.8 %collective-permute-start.2 = (s16[672,128]{1,0:T(8,128)(2,1)S(1)}, s16[672,128]{1,0:T(8,128)(2,1)S(1)}, u32[]{:S(2)}, u32[]{:S(2)}) collective-permute-start(s16[672,128]{1,0:T(8,128)(2,1)S(1)} %get-tuple-element.51), channel_id=1, source_target_pairs={{0,3},{1,2},{2,1},{3,0},{4,7},{5,6},{6,5},{7,4},{8,11},{9,10},{10,... | collective-permute-start | bytes 516104 | tf_op jit(solution)/shard_map/ppermute | solution.py:1199
  8.8 0.9 %copy-start.3 = (f32[64,512]{1,0:T(8,128)S(1)}, f32[64,512]{1,0:T(8,128)}, u32[]{:S(2)}) copy-start(f32[64,512]{1,0:T(8,128)} %refs_3_.8) | copy-start | bytes 393220
  13.1 1.6 %copy-start = (bf16[2,256,240]{2,1,0:T(8,128)(2,1)S(1)}, bf16[2,256,240]{2,1,0:T(8,128)(2,1)}, u32[]{:S(2)}) copy-start(bf16[2,256,240]{2,1,0:T(8,128)(2,1)} %constant.76.clone.refs_2_.refs_6_.table_ref) | copy-start | bytes 737284
  15.5 14.9 %copy-start.1 = (bf16[4,48,256]{2,1,0:T(8,128)(2,1)S(1)}, bf16[4,48,256]{2,1,0:T(8,128)(2,1)}, u32[]{:S(2)}) copy-start(bf16[4,48,256]{2,1,0:T(8,128)(2,1)} %constant.77.clone.refs_7_.high_ref) | copy-start | bytes 294916
  15.5 14.9 %copy-start.2 = (bf16[4,48,256]{2,1,0:T(8,128)(2,1)S(1)}, bf16[4,48,256]{2,1,0:T(8,128)(2,1)}, u32[]{:S(2)}) copy-start(bf16[4,48,256]{2,1,0:T(8,128)(2,1)} %constant.78.clone.refs_8_.low_ref) | copy-start | bytes 294916
  16.7 7.5 %collective-permute-start.5 = (s16[400,128]{1,0:T(8,128)(2,1)S(1)}, s16[400,128]{1,0:T(8,128)(2,1)S(1)}, u32[]{:S(2)}, u32[]{:S(2)}) collective-permute-start(s16[400,128]{1,0:T(8,128)(2,1)S(1)} %get-tuple-element.57), channel_id=1, source_target_pairs={{0,4},{8,12},{4,0},{12,8},{1,5},{9,13},{5,1},{13,9},{2,6},{10,14},... | collective-permute-start | bytes 307208 | tf_op jit(solution)/shard_map/ppermute | solution.py:1212
  18.9 7.8 %collective-permute-start.4 = (s16[592,128]{1,0:T(8,128)(2,1)S(1)}, s16[592,128]{1,0:T(8,128)(2,1)S(1)}, u32[]{:S(2)}, u32[]{:S(2)}) collective-permute-start(s16[592,128]{1,0:T(8,128)(2,1)S(1)} %get-tuple-element.56), channel_id=1, source_target_pairs={{4,8},{8,4},{5,9},{9,5},{6,10},{10,6},{7,11},{11,7},{20,24},{24,20... | collective-permute-start | bytes 454664 | tf_op jit(solution)/shard_map/ppermute | solution.py:1213
  19.7 6.9 %collective-permute-start.3 = (s16[336,128]{1,0:T(8,128)(2,1)S(1)}, s16[336,128]{1,0:T(8,128)(2,1)S(1)}, u32[]{:S(2)}, u32[]{:S(2)}) collective-permute-start(s16[336,128]{1,0:T(8,128)(2,1)S(1)} %get-tuple-element.55), channel_id=1, source_target_pairs={{0,4},{8,12},{4,0},{12,8},{1,5},{9,13},{5,1},{13,9},{2,6},{10,14},... | collective-permute-start | bytes 258056 | tf_op jit(solution)/shard_map/ppermute | solution.py:1214
  24.4 9.5 %copy-start.8 = (s32[24]{0:T(128)S(1)}, s32[24]{0:T(128)}, u32[]{:S(2)}) copy-start(s32[24]{0:T(128)} %param.21) | copy-start | bytes 292
  24.4 9.4 %copy-start.9 = (s32[24]{0:T(128)S(1)}, s32[24]{0:T(128)}, u32[]{:S(2)}) copy-start(s32[24]{0:T(128)} %param.22) | copy-start | bytes 292
  24.4 6.0 %collective-permute-start.6 = (s16[272,128]{1,0:T(8,128)(2,1)S(1)}, s16[272,128]{1,0:T(8,128)(2,1)S(1)}, u32[]{:S(2)}, u32[]{:S(2)}) collective-permute-start(s16[272,128]{1,0:T(8,128)(2,1)S(1)} %pair_messages.2), channel_id=1, source_target_pairs={{0,8},{4,12},{8,0},{12,4},{1,9},{5,13},{9,1},{13,5},{2,10},{6,14},... | collective-permute-start | bytes 208904 | tf_op jit(solution)/shard_map/ppermute | solution.py:1216
  32.2 3.2 %copy-start.4 = (bf16[24,128,128]{2,1,0:T(8,128)(2,1)S(1)}, bf16[24,128,128]{2,1,0:T(8,128)(2,1)}, u32[]{:S(2)}) copy-start(bf16[24,128,128]{2,1,0:T(8,128)(2,1)} %refs_3_.10) | copy-start | bytes 2359300
  32.3 8.1 %collective-permute-start.9 = (s16[672,128]{1,0:T(8,128)(2,1)S(1)}, s16[672,128]{1,0:T(8,128)(2,1)S(1)}, u32[]{:S(2)}, u32[]{:S(2)}) collective-permute-start(s16[672,128]{1,0:T(8,128)(2,1)S(1)} %get-tuple-element.63), channel_id=1, source_target_pairs={{0,2},{1,3},{2,0},{3,1},{4,6},{5,7},{6,4},{7,5},{8,10},{9,11},{10,... | collective-permute-start | bytes 516104 | tf_op jit(solution)/shard_map/ppermute | solution.py:1199
  34.7 6.2 %collective-permute-start.7 = (s16[672,128]{1,0:T(8,128)(2,1)S(1)}, s16[672,128]{1,0:T(8,128)(2,1)S(1)}, u32[]{:S(2)}, u32[]{:S(2)}) collective-permute-start(s16[672,128]{1,0:T(8,128)(2,1)S(1)} %inverse_rest.4.refs_4_), channel_id=1, source_target_pairs={{0,1},{1,0},{2,3},{3,2},{4,5},{5,4},{6,7},{7,6},{8,9},{9,8},{10,11... | collective-permute-start | bytes 516104 | tf_op jit(solution)/shard_map/ppermute | solution.py:1199
  34.8 6.8 %collective-permute-start.8 = (s16[672,128]{1,0:T(8,128)(2,1)S(1)}, s16[672,128]{1,0:T(8,128)(2,1)S(1)}, u32[]{:S(2)}, u32[]{:S(2)}) collective-permute-start(s16[672,128]{1,0:T(8,128)(2,1)S(1)} %get-tuple-element.62), channel_id=1, source_target_pairs={{0,3},{1,2},{2,1},{3,0},{4,7},{5,6},{6,5},{7,4},{8,11},{9,10},{10,... | collective-permute-start | bytes 516104 | tf_op jit(solution)/shard_map/ppermute | solution.py:1199
  39.4 1.0 %copy-start.5 = (bf16[4,128,256]{2,1,0:T(8,128)(2,1)S(1)}, bf16[4,128,256]{2,1,0:T(8,128)(2,1)}, u32[]{:S(2)}) copy-start(bf16[4,128,256]{2,1,0:T(8,128)(2,1)} %constant.79.clone.refs_2_.refs_3_) | copy-start | bytes 786436
  39.4 1.0 %copy-start.6 = (bf16[4,128,256]{2,1,0:T(8,128)(2,1)S(1)}, bf16[4,128,256]{2,1,0:T(8,128)(2,1)}, u32[]{:S(2)}) copy-start(bf16[4,128,256]{2,1,0:T(8,128)(2,1)} %constant.80.clone.refs_3_.refs_4_) | copy-start | bytes 786436
  40.3 1.3 %copy-start.7 = (s32[512]{0:T(512)S(1)}, s32[512]{0:T(512)}, u32[]{:S(2)}) copy-start(s32[512]{0:T(512)} %param.17) | copy-start | bytes 6148
  46.4 7.3 %collective-permute-start.11 = (s16[672,128]{1,0:T(8,128)(2,1)S(1)}, s16[672,128]{1,0:T(8,128)(2,1)S(1)}, u32[]{:S(2)}, u32[]{:S(2)}) collective-permute-start(s16[672,128]{1,0:T(8,128)(2,1)S(1)} %get-tuple-element.68), channel_id=1, source_target_pairs={{0,2},{1,3},{2,0},{3,1},{4,6},{5,7},{6,4},{7,5},{8,10},{9,11},{10,... | collective-permute-start | bytes 516104 | tf_op jit(solution)/shard_map/ppermute | solution.py:1199
  47.9 6.4 %collective-permute-start.10 = (s16[672,128]{1,0:T(8,128)(2,1)S(1)}, s16[672,128]{1,0:T(8,128)(2,1)S(1)}, u32[]{:S(2)}, u32[]{:S(2)}) collective-permute-start(s16[672,128]{1,0:T(8,128)(2,1)S(1)} %spread_rest.7), channel_id=1, source_target_pairs={{0,1},{1,0},{2,3},{3,2},{4,5},{5,4},{6,7},{7,6},{8,9},{9,8},{10,11... | collective-permute-start | bytes 516104 | tf_op jit(solution)/shard_map/ppermute | solution.py:1199
  48.7 7.6 %collective-permute-start.12 = (s16[672,128]{1,0:T(8,128)(2,1)S(1)}, s16[672,128]{1,0:T(8,128)(2,1)S(1)}, u32[]{:S(2)}, u32[]{:S(2)}) collective-permute-start(s16[672,128]{1,0:T(8,128)(2,1)S(1)} %get-tuple-element.69), channel_id=1, source_target_pairs={{0,3},{1,2},{2,1},{3,0},{4,7},{5,6},{6,5},{7,4},{8,11},{9,10},{10,... | collective-permute-start | bytes 516104 | tf_op jit(solution)/shard_map/ppermute | solution.py:1199
  57.6 5.3 %collective-permute-start.15 = (s16[400,128]{1,0:T(8,128)(2,1)S(1)}, s16[400,128]{1,0:T(8,128)(2,1)S(1)}, u32[]{:S(2)}, u32[]{:S(2)}) collective-permute-start(s16[400,128]{1,0:T(8,128)(2,1)S(1)} %get-tuple-element.75), channel_id=1, source_target_pairs={{0,4},{8,12},{4,0},{12,8},{1,5},{9,13},{5,1},{13,9},{2,6},{10,14},... | collective-permute-start | bytes 307208 | tf_op jit(solution)/shard_map/ppermute | solution.py:1212
  57.6 7.8 %collective-permute-start.14 = (s16[592,128]{1,0:T(8,128)(2,1)S(1)}, s16[592,128]{1,0:T(8,128)(2,1)S(1)}, u32[]{:S(2)}, u32[]{:S(2)}) collective-permute-start(s16[592,128]{1,0:T(8,128)(2,1)S(1)} %get-tuple-element.74), channel_id=1, source_target_pairs={{4,8},{8,4},{5,9},{9,5},{6,10},{10,6},{7,11},{11,7},{20,24},{24,20... | collective-permute-start | bytes 454664 | tf_op jit(solution)/shard_map/ppermute | solution.py:1213
  58.5 6.9 %collective-permute-start.13 = (s16[336,128]{1,0:T(8,128)(2,1)S(1)}, s16[336,128]{1,0:T(8,128)(2,1)S(1)}, u32[]{:S(2)}, u32[]{:S(2)}) collective-permute-start(s16[336,128]{1,0:T(8,128)(2,1)S(1)} %get-tuple-element.73), channel_id=1, source_target_pairs={{0,4},{8,12},{4,0},{12,8},{1,5},{9,13},{5,1},{13,9},{2,6},{10,14},... | collective-permute-start | bytes 258056 | tf_op jit(solution)/shard_map/ppermute | solution.py:1214
  63.1 6.8 %collective-permute-start.16 = (s16[272,128]{1,0:T(8,128)(2,1)S(1)}, s16[272,128]{1,0:T(8,128)(2,1)S(1)}, u32[]{:S(2)}, u32[]{:S(2)}) collective-permute-start(s16[272,128]{1,0:T(8,128)(2,1)S(1)} %pair_messages.3), channel_id=1, source_target_pairs={{0,8},{4,12},{8,0},{12,4},{1,9},{5,13},{9,1},{13,5},{2,10},{6,14},... | collective-permute-start | bytes 208904 | tf_op jit(solution)/shard_map/ppermute | solution.py:1216
  71.8 5.9 %collective-permute-start.19 = (s16[672,128]{1,0:T(8,128)(2,1)S(1)}, s16[672,128]{1,0:T(8,128)(2,1)S(1)}, u32[]{:S(2)}, u32[]{:S(2)}) collective-permute-start(s16[672,128]{1,0:T(8,128)(2,1)S(1)} %get-tuple-element.81), channel_id=1, source_target_pairs={{0,2},{1,3},{2,0},{3,1},{4,6},{5,7},{6,4},{7,5},{8,10},{9,11},{10,... | collective-permute-start | bytes 516104 | tf_op jit(solution)/shard_map/ppermute | solution.py:1199
  74.5 3.7 %collective-permute-start.17 = (s16[672,128]{1,0:T(8,128)(2,1)S(1)}, s16[672,128]{1,0:T(8,128)(2,1)S(1)}, u32[]{:S(2)}, u32[]{:S(2)}) collective-permute-start(s16[672,128]{1,0:T(8,128)(2,1)S(1)} %inverse_rest.6.refs_4_), channel_id=1, source_target_pairs={{0,1},{1,0},{2,3},{3,2},{4,5},{5,4},{6,7},{7,6},{8,9},{9,8},{10,11... | collective-permute-start | bytes 516104 | tf_op jit(solution)/shard_map/ppermute | solution.py:1199
  74.6 6.2 %collective-permute-start.18 = (s16[672,128]{1,0:T(8,128)(2,1)S(1)}, s16[672,128]{1,0:T(8,128)(2,1)S(1)}, u32[]{:S(2)}, u32[]{:S(2)}) collective-permute-start(s16[672,128]{1,0:T(8,128)(2,1)S(1)} %get-tuple-element.80), channel_id=1, source_target_pairs={{0,3},{1,2},{2,1},{3,0},{4,7},{5,6},{6,5},{7,4},{8,11},{9,10},{10,... | collective-permute-start | bytes 516104 | tf_op jit(solution)/shard_map/ppermute | solution.py:1199
